TPU v7x, 32 devices: a whole 2x2x4 slice. The times are simulated.
32 devices in a mesh: tile: 16 (over z, y, core), ch: 2 (over x).
Axes of the slice: x: 2, y: 2, z: 4, core: 2. Of those that a mesh axis runs over, the one named last changes fastest.
Arguments:
- features: bfloat16 [16, 32, 32, 384], P('tile', None, None, 'ch'), may hold values from -6 to 6
- weight: bfloat16 [3, 3, 384, 384], replicated, may hold values from -0.109375 to 0.109375
- cotangent: bfloat16 [16, 32, 32, 384], P('tile', None, None, 'ch'), may hold values from -6 to 6
- edge_tiles: int32 [16, 4], replicated, may hold values from 0 to 15, as said below
- edge_turns: int32 [16, 4], replicated, may hold values from 0 to 3
- corner_tiles: int32 [16, 4], replicated, may hold values from 0 to 15, as said below
- corner_turns: int32 [16, 4], replicated, may hold values from 0 to 3
Outputs:
- output: bfloat16 [16, 32, 32, 384], P('tile', None, None, 'ch')
- grad_features: bfloat16 [16, 32, 32, 384], P('tile', None, None, 'ch')
- grad_weight: float32 [3, 3, 384, 384], P(None, None, 'ch')
Inputs may be any that keep to these rules, and one draw needn't show every extreme that they name: (edge_tiles[t, e] - t) mod 16 lies in 1 .. 4 or in 12 .. 15; both distances 4 and -4 occur. (corner_tiles[t, c] - t) mod 16 lies in 1 .. 4 or in 12 .. 15; both distances 4 and -4 occur.
All inputs are finite; a program needn't handle non-finite values.
Results may differ from a plain program's by a relative error of at most 0.0029.
Values may be sent and summed in bfloat16 or wider, within the bound.
No kernel may reach another device: no remote copies, remote signals or barrier semaphores. Data moves between devices by JAX's collectives and lax.ppermute only.
A program may use at most 64 MiB of HBM per device.

v0:
```python
import math

import jax
import jax.numpy as jnp
import numpy as np
from jax import lax
from jax.sharding import PartitionSpec as P

SPAN = 4


def shifted(shard, axis, by):
    peers = lax.axis_size(axis)
    return lax.ppermute(shard, axis, [(i, (i + by) % peers) for i in range(peers)])


def turn_tables():
    labels = [[3 * row + col for col in range(3)] for row in range(3)]

    def turn_once(block):
        return [[block[col][2 - row] for col in range(3)] for row in range(3)]

    def sides_of(block):
        return [
            list(block[0]),
            [block[row][2] for row in range(3)],
            list(block[2]),
            [block[row][0] for row in range(3)],
        ]

    def corners_of(block):
        return [block[0][0], block[0][2], block[2][2], block[2][0]]

    base_sides = sides_of(labels)
    base_corners = corners_of(labels)
    edge_table = np.zeros((4, 4), np.int32)
    corner_table = np.zeros((4, 4), np.int32)
    for border in range(4):
        turned = labels
        for quarter in range(4):
            wanted = sides_of(turned)[(border + 2) % 4]
            for side_index in range(4):
                if base_sides[side_index] == wanted:
                    edge_table[border, quarter] = side_index
                if base_sides[side_index][::-1] == wanted:
                    edge_table[border, quarter] = side_index + 4
            corner_cell = corners_of(turned)[(border + 2) % 4]
            for corner_index in range(4):
                if base_corners[corner_index] == corner_cell:
                    corner_table[border, quarter] = corner_index
            turned = turn_once(turned)
    return (edge_table, corner_table)


def body(features, weight, cotangent, edge_tiles, edge_turns, corner_tiles, corner_turns):
    edge_table, corner_table = turn_tables()
    tile_count = lax.axis_size("tile")
    own_tile = lax.axis_index("tile")
    field = features[0]
    side_len = field.shape[0]
    chan_part = field.shape[2]
    chan_count = weight.shape[3]
    chan_start = lax.axis_index("ch") * chan_part
    rows = side_len * side_len
    offsets = list(range(-SPAN, 0)) + list(range(1, SPAN + 1))
    border_ids = jnp.arange(4)
    own_edges = edge_tiles[own_tile]
    own_corner_tiles = corner_tiles[own_tile]
    edge_slots = jnp.asarray(edge_table)[border_ids, edge_turns[own_tile]]
    corner_slots = jnp.asarray(corner_table)[border_ids, corner_turns[own_tile]]

    def position(target):
        wrapped = jnp.mod(target - own_tile, tile_count)
        signed = jnp.where(wrapped > tile_count // 2, wrapped - tile_count, wrapped)
        return jnp.where(signed < 0, signed + SPAN, signed + SPAN - 1)

    sides = jnp.stack([field[0], field[:, -1], field[-1], field[:, 0]])
    corners = jnp.stack([field[0, 0], field[0, -1], field[-1, -1], field[-1, 0]])
    got_sides = []
    got_corners = []
    for offset in offsets:
        near_sides, near_corners = shifted((sides, corners), "tile", -offset)
        got_sides.append(near_sides)
        got_corners.append(near_corners)
    all_sides = jnp.stack(got_sides)
    all_corners = jnp.stack(got_corners)
    edge_source = position(own_edges)
    corner_source = position(own_corner_tiles)
    halos = all_sides[edge_source, edge_slots % 4]
    halos = jnp.where((edge_slots >= 4)[:, None, None], halos[:, ::-1], halos)
    corner_halos = all_corners[corner_source, corner_slots]
    padded = jnp.pad(field, ((1, 1), (1, 1), (0, 0)))
    padded = padded.at[0, 1:-1].set(halos[0]).at[1:-1, -1].set(halos[1])
    padded = padded.at[-1, 1:-1].set(halos[2]).at[1:-1, 0].set(halos[3])
    padded = padded.at[0, 0].set(corner_halos[0]).at[0, -1].set(corner_halos[1])
    padded = padded.at[-1, -1].set(corner_halos[2]).at[-1, 0].set(corner_halos[3])
    taps = [(row_off, col_off) for row_off in range(3) for col_off in range(3)]
    blocks = [
        lax.dynamic_slice_in_dim(weight[row_off, col_off], chan_start, chan_part, 0)
        for row_off, col_off in taps
    ]
    windows = [
        padded[row_off : row_off + side_len, col_off : col_off + side_len].reshape(rows, chan_part)
        for row_off, col_off in taps
    ]
    partial_out = jnp.zeros((rows, chan_count), jnp.float32)
    for tap_index in range(9):
        partial_out = partial_out + jnp.dot(
            windows[tap_index], blocks[tap_index], preferred_element_type=jnp.float32
        )
    output = lax.psum_scatter(partial_out, "ch", scatter_dimension=1, tiled=True)
    output = output.astype(jnp.bfloat16).reshape(1, side_len, side_len, chan_part)
    cot_full = lax.all_gather(cotangent[0], "ch", axis=2, tiled=True).reshape(rows, chan_count)
    grad_padded = jnp.zeros(padded.shape, jnp.float32)
    grads = []
    for tap_index in range(9):
        row_off, col_off = taps[tap_index]
        back = lax.dot_general(
            cot_full,
            blocks[tap_index],
            (((1,), (1,)), ((), ())),
            preferred_element_type=jnp.float32,
        )
        grad_padded = grad_padded.at[
            row_off : row_off + side_len, col_off : col_off + side_len
        ].add(back.reshape(side_len, side_len, chan_part))
        grads.append(
            lax.dot_general(
                windows[tap_index],
                cot_full,
                (((0,), (0,)), ((), ())),
                preferred_element_type=jnp.float32,
            )
        )
    local_grad = jnp.stack(grads).reshape(3, 3, chan_part, chan_count)
    grad_weight = lax.psum(local_grad, "tile") * (1.0 / math.sqrt(tile_count * rows))
    pieces = jnp.stack(
        [grad_padded[0, 1:-1], grad_padded[1:-1, -1], grad_padded[-1, 1:-1], grad_padded[1:-1, 0]]
    ).astype(jnp.bfloat16)
    corner_pieces = jnp.stack(
        [grad_padded[0, 0], grad_padded[0, -1], grad_padded[-1, -1], grad_padded[-1, 0]]
    ).astype(jnp.bfloat16)
    slot_ids = jnp.arange(8)
    collected = jnp.zeros((8, side_len, chan_part), jnp.float32)
    corner_sums = jnp.zeros((4, chan_part), jnp.float32)
    for offset in offsets:
        got_pieces, got_corners = shifted((pieces, corner_pieces), "tile", offset)
        source = jnp.mod(own_tile - offset, tile_count)
        src_slots = jnp.asarray(edge_table)[border_ids, edge_turns[source]]
        src_corner_slots = jnp.asarray(corner_table)[border_ids, corner_turns[source]]
        edge_mine = edge_tiles[source] == own_tile
        corner_mine = corner_tiles[source] == own_tile
        hits = (edge_mine[:, None] & (src_slots[:, None] == slot_ids[None, :])).astype(jnp.bfloat16)
        corner_hits = (
            corner_mine[:, None] & (src_corner_slots[:, None] == border_ids[None, :])
        ).astype(jnp.bfloat16)
        collected = collected + jnp.einsum(
            "bk,bjc->kjc", hits, got_pieces, preferred_element_type=jnp.float32
        )
        corner_sums = corner_sums + jnp.einsum(
            "bk,bc->kc", corner_hits, got_corners, preferred_element_type=jnp.float32
        )
    side_sums = collected[:4] + collected[4:, ::-1]
    interior = grad_padded[1:-1, 1:-1]
    interior = interior.at[0].add(side_sums[0]).at[:, -1].add(side_sums[1])
    interior = interior.at[-1].add(side_sums[2]).at[:, 0].add(side_sums[3])
    interior = interior.at[0, 0].add(corner_sums[0]).at[0, -1].add(corner_sums[1])
    interior = interior.at[-1, -1].add(corner_sums[2]).at[-1, 0].add(corner_sums[3])
    grad_features = interior.astype(jnp.bfloat16)[None]
    return (output, grad_features, grad_weight)


def solution(mesh):
    return jax.shard_map(
        body,
        mesh=mesh,
        in_specs=(
            P("tile", None, None, "ch"),
            P(),
            P("tile", None, None, "ch"),
            P(),
            P(),
            P(),
            P(),
        ),
        out_specs=(
            P("tile", None, None, "ch"),
            P("tile", None, None, "ch"),
            P(None, None, "ch", None),
        ),
        check_vma=False,
    )
```

profile of v0, /device:TPU:0, one launch (start us, length us, event | category | flops | bytes accessed | tf_op | source)
XLA Modules:
  0.0 408.1 jit_solution(2801948686387362433)
XLA Ops:
  10.5 3.0 collective-permute-start
  17.0 3.1 fusion.331
  21.5 38.0 %all-gather = bf16[1,32,32,384]{2,1,0,3:T(8,128)(2,1)} all-gather(bf16[1,32,32,192]{2,1,0,3:T(8,128)(2,1)S(1)} %copy.111), channel_id=2, replica_groups=mesh['tile'=16,'ch'=2] {'ch'}, dimensions={3}, use_global_device_ids=true | all-gather | bytes 1179648 | tf_op jit(solution)/shard_map/all_gather | solution.py:113
  59.5 4.5 %copy.112 = bf16[1,32,32,384]{3,2,1,0:T(8,128)(2,1)S(1)} copy(bf16[1,32,32,384]{2,1,0,3:T(8,128)(2,1)} %all-gather) | data formatting | bytes 1572864 | tf_op jit(solution)/shard_map/all_gather | solution.py:113
  70.1 2.8 copy_add_fusion
  73.0 6.2 %scatter-add.59 = f32[34,34,192]{2,0,1:T(8,128)S(1)} dynamic-update-slice(f32[34,34,192]{2,0,1:T(8,128)S(1)} %scatter-add.56, f32[32,32,192]{2,0,1:T(8,128)} %copy_add_fusion, s32[]{:T(128)} %bitcast.14, s32[]{:T(128)} %bitcast.15, s32[]{:T(128)} %constant.803.clone.1) | dynamic-update-slice | bytes 1572868 | tf_op jit(solution)/shard_map/scatter-add | solution.py:126
  80.0 3.7 add_select_fusion
  83.7 6.3 %scatter-add.60 = f32[34,34,192]{2,0,1:T(8,128)S(1)} dynamic-update-slice(f32[34,34,192]{2,0,1:T(8,128)S(1)} %scatter-add.59, f32[32,32,192]{2,0,1:T(8,128)} %add_select_fusion, s32[]{:T(128)} %bitcast.63, s32[]{:T(128)} %bitcast.64, s32[]{:T(128)} %constant.803.clone.1) | dynamic-update-slice | bytes 1572868 | tf_op jit(solution)/shard_map/scatter-add | solution.py:126
  92.6 2.2 convolution_bitcast_fusion.4
  96.3 2.9 slice_add_fusion.5
  99.2 4.9 %scatter-add.61 = f32[34,34,192]{2,0,1:T(8,128)S(1)} dynamic-update-slice(f32[34,34,192]{2,0,1:T(8,128)S(1)} %scatter-add.60, f32[32,32,192]{2,0,1:T(8,128)} %slice_add_fusion.5, s32[]{:T(128)} %constant.810.clone.1, s32[]{:T(128)} %constant.803.clone.1, s32[]{:T(128)} %constant.803.clone.1) | dynamic-update-slice | bytes 1572868 | tf_op jit(solution)/shard_map/scatter-add | solution.py:126
  104.1 1.7 slice_add_fusion.4
  105.8 4.9 %scatter-add.64 = f32[34,34,192]{2,0,1:T(8,128)S(1)} dynamic-update-slice(f32[34,34,192]{2,0,1:T(8,128)S(1)} %scatter-add.61, f32[32,32,192]{2,0,1:T(8,128)} %slice_add_fusion.4, s32[]{:T(128)} %constant.810.clone.1, s32[]{:T(128)} %constant.810.clone.1, s32[]{:T(128)} %constant.803.clone.1) | dynamic-update-slice | bytes 1572868 | tf_op jit(solution)/shard_map/scatter-add | solution.py:126
  113.4 2.2 convolution_bitcast_fusion.2
  117.1 2.9 slice_add_fusion.3
  120.0 4.9 %scatter-add.65 = f32[34,34,192]{2,0,1:T(8,128)S(1)} dynamic-update-slice(f32[34,34,192]{2,0,1:T(8,128)S(1)} %scatter-add.64, f32[32,32,192]{2,0,1:T(8,128)} %slice_add_fusion.3, s32[]{:T(128)} %constant.810.clone.1, s32[]{:T(128)} %constant.818.clone.1, s32[]{:T(128)} %constant.803.clone.1) | dynamic-update-slice | bytes 1572868 | tf_op jit(solution)/shard_map/scatter-add | solution.py:126
  126.6 5.1 %scatter-add.66 = f32[34,34,192]{2,0,1:T(8,128)S(1)} dynamic-update-slice(f32[34,34,192]{2,0,1:T(8,128)S(1)} %scatter-add.65, f32[32,32,192]{2,0,1:T(8,128)} %slice_add_fusion.2, s32[]{:T(128)} %constant.818.clone.1, s32[]{:T(128)} %constant.803.clone.1, s32[]{:T(128)} %constant.803.clone.1) | dynamic-update-slice | bytes 1572868 | tf_op jit(solution)/shard_map/scatter-add | solution.py:126
  136.2 4.9 %scatter-add.69 = f32[34,34,192]{2,0,1:T(8,128)S(1)} dynamic-update-slice(f32[34,34,192]{2,0,1:T(8,128)S(1)} %scatter-add.66, f32[32,32,192]{2,0,1:T(8,128)} %slice_add_fusion.1, s32[]{:T(128)} %constant.818.clone.1, s32[]{:T(128)} %constant.810.clone.1, s32[]{:T(128)} %constant.803.clone.1) | dynamic-update-slice | bytes 1572868 | tf_op jit(solution)/shard_map/scatter-add | solution.py:126
  142.9 1.9 slice_add_fusion
  144.8 1.9 scatter-add.70
  156.9 2.8 copy.139
  179.0 3.8 collective-permute-done.30
  184.0 5.4 %collective-permute-done.29 = bf16[4,192]{1,0:T(4,128)(2,1)S(1)} collective-permute-done((bf16[4,192]{1,0:T(4,128)(2,1)}, bf16[4,192]{1,0:T(4,128)(2,1)S(1)}, u32[]{:S(2)}, u32[]{:S(2)}) %collective-permute-start.29) | collective-permute-done | bytes 1568 | tf_op jit(solution)/shard_map/ppermute | solution.py:14
  189.6 5.7 %collective-permute-done.28 = bf16[4,192]{1,0:T(4,128)(2,1)S(1)} collective-permute-done((bf16[4,192]{1,0:T(4,128)(2,1)}, bf16[4,192]{1,0:T(4,128)(2,1)S(1)}, u32[]{:S(2)}, u32[]{:S(2)}) %collective-permute-start.28) | collective-permute-done | bytes 1568 | tf_op jit(solution)/shard_map/ppermute | solution.py:14
  197.0 3.5 collective-permute-done.26
  200.6 2.1 collective-permute-start.25
  205.7 4.5 %collective-permute-done.8 = bf16[4,192]{1,0:T(4,128)(2,1)S(1)} collective-permute-done((bf16[4,192]{1,0:T(4,128)(2,1)S(1)}, bf16[4,192]{1,0:T(4,128)(2,1)S(1)}, u32[]{:S(2)}, u32[]{:S(2)}) %collective-permute-start.8) | collective-permute-done | bytes 1568 | tf_op jit(solution)/shard_map/ppermute | solution.py:14
  210.1 2.7 collective-permute-start.9
  212.8 2.1 collective-permute-done.9
  214.9 3.9 collective-permute-start.10
  218.8 2.4 collective-permute-done.10
  221.2 5.7 %collective-permute-done.11 = bf16[4,192]{1,0:T(4,128)(2,1)S(1)} collective-permute-done((bf16[4,192]{1,0:T(4,128)(2,1)S(1)}, bf16[4,192]{1,0:T(4,128)(2,1)S(1)}, u32[]{:S(2)}, u32[]{:S(2)}) %collective-permute-start.11) | collective-permute-done | bytes 1568 | tf_op jit(solution)/shard_map/ppermute | solution.py:14
  228.3 3.6 collective-permute-done.13
  231.8 2.1 collective-permute-start.14
  235.2 4.4 %collective-permute-start.15 = (bf16[4,192]{1,0:T(4,128)(2,1)S(1)}, bf16[4,192]{1,0:T(4,128)(2,1)S(1)}, u32[]{:S(2)}, u32[]{:S(2)}) collective-permute-start(bf16[4,192]{1,0:T(4,128)(2,1)S(1)} %pad_maximum_fusion.2), channel_id=1, source_target_pairs={{0,24},{2,26},{4,28},{6,30},{8,0},{10,2},{12,4},{14,6},{16,8},{18,... | collective-permute-start | bytes 4616 | tf_op jit(solution)/shard_map/ppermute | solution.py:14
  240.9 4.1 collective-permute-start.24
  246.5 4.8 %collective-permute-start.4 = (bf16[4,32,192]{2,1,0:T(8,128)(2,1)}, bf16[4,32,192]{2,1,0:T(8,128)(2,1)S(1)}, u32[]{:S(2)}, u32[]{:S(2)}) collective-permute-start(bf16[4,32,192]{2,1,0:T(8,128)(2,1)} %pad_maximum_fusion), channel_id=1, source_target_pairs={{0,30},{2,0},{4,2},{6,4},{8,6},{10,8},{12,10},{14,12},{16,14},{18,... | collective-permute-start | bytes 147464 | tf_op jit(solution)/shard_map/ppermute | solution.py:14
  256.6 2.0 collective-permute-start.23
  262.0 2.9 collective-permute-start.21
  266.1 4.4 %collective-permute-start.19 = (bf16[4,32,192]{2,0,1:T(4,128)(2,1)S(1)}, bf16[4,32,192]{2,0,1:T(4,128)(2,1)}, u32[]{:S(2)}, u32[]{:S(2)}) collective-permute-start(bf16[4,32,192]{2,0,1:T(4,128)(2,1)S(1)} %pad_maximum_fusion.1), channel_id=1, source_target_pairs={{0,30},{2,0},{4,2},{6,4},{8,6},{10,8},{12,10},{14,12},{16,14},{18,... | collective-permute-start | bytes 147464 | tf_op jit(solution)/shard_map/ppermute | solution.py:14
  275.1 2.0 broadcast_select_fusion.2
  286.0 1.7 fusion.42
  295.8 1.7 fusion.54
  299.3 1.9 add_add_fusion
  308.6 2.3 collective-permute-done.16
  311.9 1.7 broadcast_select_fusion.1
  315.8 79.3 %all-reduce.4.cloned.1.call-done = f32[3,3,192,384]{3,2,1,0:T(8,128)} async-done(((f32[3,3,192,384]{3,2,1,0:T(8,128)}), f32[3,3,192,384]{3,2,1,0:T(8,128)}) %all-reduce.4.cloned.1.call-update) | async-done | bytes 2654224 | tf_op jit(solution)/shard_map/psum | solution.py:136
  395.0 3.4 broadcast_multiply_fusion
  (321 shorter events, 116.6 us)
Async XLA Ops:
  8.0 387.0 %all-reduce.4.cloned.1.call-start = ((), (), s32[]{:S(2)}) async-start(), calls=%async_computation.2 | async-start | bytes 5308416 | tf_op jit(solution)/shard_map/psum | solution.py:136
  10.5 241.7 %collective-permute-start = (bf16[4,32,192]{2,1,0:T(8,128)(2,1)}, bf16[4,32,192]{2,1,0:T(8,128)(2,1)}, u32[]{:S(2)}, u32[]{:S(2)}) collective-permute-start(bf16[4,32,192]{2,1,0:T(8,128)(2,1)} %pad_maximum_fusion), channel_id=1, source_target_pairs={{0,8},{2,10},{4,12},{6,14},{8,16},{10,18},{12,20},{14,22},{16,24},... | collective-permute-start | bytes 147464 | tf_op jit(solution)/shard_map/ppermute | solution.py:14
  13.5 240.2 %collective-permute-start.1 = (bf16[4,32,192]{2,1,0:T(8,128)(2,1)}, bf16[4,32,192]{2,1,0:T(8,128)(2,1)}, u32[]{:S(2)}, u32[]{:S(2)}) collective-permute-start(bf16[4,32,192]{2,1,0:T(8,128)(2,1)} %pad_maximum_fusion), channel_id=1, source_target_pairs={{0,6},{2,8},{4,10},{6,12},{8,14},{10,16},{12,18},{14,20},{16,22},{... | collective-permute-start | bytes 147464 | tf_op jit(solution)/shard_map/ppermute | solution.py:14
  14.2 241.0 %collective-permute-start.2 = (bf16[4,32,192]{2,1,0:T(8,128)(2,1)}, bf16[4,32,192]{2,1,0:T(8,128)(2,1)}, u32[]{:S(2)}, u32[]{:S(2)}) collective-permute-start(bf16[4,32,192]{2,1,0:T(8,128)(2,1)} %pad_maximum_fusion), channel_id=1, source_target_pairs={{0,4},{2,6},{4,8},{6,10},{8,12},{10,14},{12,16},{14,18},{16,20},{1... | collective-permute-start | bytes 147464 | tf_op jit(solution)/shard_map/ppermute | solution.py:14
  15.7 240.9 %collective-permute-start.3 = (bf16[4,32,192]{2,1,0:T(8,128)(2,1)}, bf16[4,32,192]{2,1,0:T(8,128)(2,1)}, u32[]{:S(2)}, u32[]{:S(2)}) collective-permute-start(bf16[4,32,192]{2,1,0:T(8,128)(2,1)} %pad_maximum_fusion), channel_id=1, source_target_pairs={{0,2},{2,4},{4,6},{6,8},{8,10},{10,12},{12,14},{14,16},{16,18},{18... | collective-permute-start | bytes 147464 | tf_op jit(solution)/shard_map/ppermute | solution.py:14
  20.1 43.9 %copy-start.14 = (bf16[1,1,384,384]{3,2,1,0:T(8,128)(2,1)}, bf16[1,1,384,384]{3,2,1,0:T(8,128)(2,1)S(1)}, u32[]{:S(2)}) copy-start(bf16[1,1,384,384]{3,2,1,0:T(8,128)(2,1)S(1)} %get-tuple-element.347) | copy-start | bytes 884740
  20.1 45.3 %copy-start.13 = (bf16[1,1,384,384]{3,2,1,0:T(8,128)(2,1)}, bf16[1,1,384,384]{3,2,1,0:T(8,128)(2,1)S(1)}, u32[]{:S(2)}) copy-start(bf16[1,1,384,384]{3,2,1,0:T(8,128)(2,1)S(1)} %get-tuple-element.346) | copy-start | bytes 884740
  20.1 121.0 %copy-start.11 = (bf16[1,1,384,384]{3,2,1,0:T(8,128)(2,1)}, bf16[1,1,384,384]{3,2,1,0:T(8,128)(2,1)S(1)}, u32[]{:S(2)}) copy-start(bf16[1,1,384,384]{3,2,1,0:T(8,128)(2,1)S(1)} %get-tuple-element.340) | copy-start | bytes 884740
  73.0 6.2 %copy-start.48 = (s32[3]{0:T(128)S(1)}, s32[3]{0:T(128)}, u32[]{:S(2)}) copy-start(s32[3]{0:T(128)} %constant.819.clone.1) | copy-start | bytes 40
  73.0 7.0 %copy-start.8 = (f32[1024,192]{1,0:T(8,128)S(1)}, f32[1024,192]{1,0:T(8,128)}, u32[]{:S(2)}) copy-start(f32[1024,192]{1,0:T(8,128)} %copy.117) | copy-start | bytes 2359300
  147.6 5.9 %copy-start.23 = (bf16[1,32,32,192]{3,2,1,0:T(8,128)(2,1)S(1)}, bf16[1,32,32,192]{3,2,1,0:T(8,128)(2,1)}, u32[]{:S(2)}) copy-start(bf16[1,32,32,192]{3,2,1,0:T(8,128)(2,1)} %param.59) | copy-start | bytes 1179652
  148.2 29.5 %collective-permute-start.31 = (bf16[4,192]{1,0:T(4,128)(2,1)}, bf16[4,192]{1,0:T(4,128)(2,1)}, u32[]{:S(2)}, u32[]{:S(2)}) collective-permute-start(bf16[4,192]{1,0:T(4,128)(2,1)} %pad_maximum_fusion.3), channel_id=1, source_target_pairs={{0,8},{2,10},{4,12},{6,14},{8,16},{10,18},{12,20},{14,22},{16,24},... | collective-permute-start | bytes 4616 | tf_op jit(solution)/shard_map/ppermute | solution.py:14
  162.1 7.1 %copy-start = (s32[4,4]{1,0:T(4,128)S(1)}, s32[4,4]{1,0:T(4,128)}, u32[]{:S(2)}) copy-start(s32[4,4]{1,0:T(4,128)} %constant.828.clone) | copy-start | bytes 196
  164.5 6.7 %copy-start.46 = (s32[3]{0:T(128)S(1)}, s32[3]{0:T(128)}, u32[]{:S(2)}) copy-start(s32[3]{0:T(128)} %constant.825.clone.1) | copy-start | bytes 40
  177.8 5.1 %collective-permute-start.30 = (bf16[4,192]{1,0:T(4,128)(2,1)}, bf16[4,192]{1,0:T(4,128)(2,1)S(1)}, u32[]{:S(2)}, u32[]{:S(2)}) collective-permute-start(bf16[4,192]{1,0:T(4,128)(2,1)} %pad_maximum_fusion.3), channel_id=1, source_target_pairs={{0,6},{2,8},{4,10},{6,12},{8,14},{10,16},{12,18},{14,20},{16,22},{... | collective-permute-start | bytes 4616 | tf_op jit(solution)/shard_map/ppermute | solution.py:14
  182.9 6.5 %collective-permute-start.29 = (bf16[4,192]{1,0:T(4,128)(2,1)}, bf16[4,192]{1,0:T(4,128)(2,1)S(1)}, u32[]{:S(2)}, u32[]{:S(2)}) collective-permute-start(bf16[4,192]{1,0:T(4,128)(2,1)} %pad_maximum_fusion.3), channel_id=1, source_target_pairs={{0,4},{2,6},{4,8},{6,10},{8,12},{10,14},{12,16},{14,18},{16,20},{1... | collective-permute-start | bytes 4616 | tf_op jit(solution)/shard_map/ppermute | solution.py:14
  189.3 5.9 %collective-permute-start.28 = (bf16[4,192]{1,0:T(4,128)(2,1)}, bf16[4,192]{1,0:T(4,128)(2,1)S(1)}, u32[]{:S(2)}, u32[]{:S(2)}) collective-permute-start(bf16[4,192]{1,0:T(4,128)(2,1)} %pad_maximum_fusion.3), channel_id=1, source_target_pairs={{0,2},{2,4},{4,6},{6,8},{8,10},{10,12},{12,14},{14,16},{16,18},{18... | collective-permute-start | bytes 4616 | tf_op jit(solution)/shard_map/ppermute | solution.py:14
  195.3 1.5 collective-permute-start.27
  196.8 3.8 collective-permute-start.26
  200.6 3.6 collective-permute-start.25
  204.2 6.0 %collective-permute-start.8 = (bf16[4,192]{1,0:T(4,128)(2,1)S(1)}, bf16[4,192]{1,0:T(4,128)(2,1)S(1)}, u32[]{:S(2)}, u32[]{:S(2)}) collective-permute-start(bf16[4,192]{1,0:T(4,128)(2,1)S(1)} %pad_maximum_fusion.2), channel_id=1, source_target_pairs={{0,8},{2,10},{4,12},{6,14},{8,16},{10,18},{12,20},{14,22},{16,24},... | collective-permute-start | bytes 4616 | tf_op jit(solution)/shard_map/ppermute | solution.py:14
  210.1 4.8 %collective-permute-start.9 = (bf16[4,192]{1,0:T(4,128)(2,1)S(1)}, bf16[4,192]{1,0:T(4,128)(2,1)S(1)}, u32[]{:S(2)}, u32[]{:S(2)}) collective-permute-start(bf16[4,192]{1,0:T(4,128)(2,1)S(1)} %pad_maximum_fusion.2), channel_id=1, source_target_pairs={{0,6},{2,8},{4,10},{6,12},{8,14},{10,16},{12,18},{14,20},{16,22},{... | collective-permute-start | bytes 4616 | tf_op jit(solution)/shard_map/ppermute | solution.py:14
  214.9 6.3 %collective-permute-start.10 = (bf16[4,192]{1,0:T(4,128)(2,1)S(1)}, bf16[4,192]{1,0:T(4,128)(2,1)S(1)}, u32[]{:S(2)}, u32[]{:S(2)}) collective-permute-start(bf16[4,192]{1,0:T(4,128)(2,1)S(1)} %pad_maximum_fusion.2), channel_id=1, source_target_pairs={{0,4},{2,6},{4,8},{6,10},{8,12},{10,14},{12,16},{14,18},{16,20},{1... | collective-permute-start | bytes 4616 | tf_op jit(solution)/shard_map/ppermute | solution.py:14
  221.2 5.7 %collective-permute-start.11 = (bf16[4,192]{1,0:T(4,128)(2,1)S(1)}, bf16[4,192]{1,0:T(4,128)(2,1)S(1)}, u32[]{:S(2)}, u32[]{:S(2)}) collective-permute-start(bf16[4,192]{1,0:T(4,128)(2,1)S(1)} %pad_maximum_fusion.2), channel_id=1, source_target_pairs={{0,2},{2,4},{4,6},{6,8},{8,10},{10,12},{12,14},{14,16},{16,18},{18... | collective-permute-start | bytes 4616 | tf_op jit(solution)/shard_map/ppermute | solution.py:14
  226.9 1.3 collective-permute-start.12
  228.2 3.6 collective-permute-start.13
  231.8 3.4 collective-permute-start.14
  235.2 5.7 %collective-permute-start.15 = (bf16[4,192]{1,0:T(4,128)(2,1)S(1)}, bf16[4,192]{1,0:T(4,128)(2,1)S(1)}, u32[]{:S(2)}, u32[]{:S(2)}) collective-permute-start(bf16[4,192]{1,0:T(4,128)(2,1)S(1)} %pad_maximum_fusion.2), channel_id=1, source_target_pairs={{0,24},{2,26},{4,28},{6,30},{8,0},{10,2},{12,4},{14,6},{16,8},{18,... | collective-permute-start | bytes 4616 | tf_op jit(solution)/shard_map/ppermute | solution.py:14
  240.9 5.6 %collective-permute-start.24 = (bf16[4,192]{1,0:T(4,128)(2,1)}, bf16[4,192]{1,0:T(4,128)(2,1)S(1)}, u32[]{:S(2)}, u32[]{:S(2)}) collective-permute-start(bf16[4,192]{1,0:T(4,128)(2,1)} %pad_maximum_fusion.3), channel_id=1, source_target_pairs={{0,24},{2,26},{4,28},{6,30},{8,0},{10,2},{12,4},{14,6},{16,8},{18,... | collective-permute-start | bytes 4616 | tf_op jit(solution)/shard_map/ppermute | solution.py:14
  246.5 13.6 %collective-permute-start.4 = (bf16[4,32,192]{2,1,0:T(8,128)(2,1)}, bf16[4,32,192]{2,1,0:T(8,128)(2,1)S(1)}, u32[]{:S(2)}, u32[]{:S(2)}) collective-permute-start(bf16[4,32,192]{2,1,0:T(8,128)(2,1)} %pad_maximum_fusion), channel_id=1, source_target_pairs={{0,30},{2,0},{4,2},{6,4},{8,6},{10,8},{12,10},{14,12},{16,14},{18,... | collective-permute-start | bytes 147464 | tf_op jit(solution)/shard_map/ppermute | solution.py:14
  252.1 9.8 %collective-permute-start.5 = (bf16[4,32,192]{2,1,0:T(8,128)(2,1)}, bf16[4,32,192]{2,1,0:T(8,128)(2,1)S(1)}, u32[]{:S(2)}, u32[]{:S(2)}) collective-permute-start(bf16[4,32,192]{2,1,0:T(8,128)(2,1)} %pad_maximum_fusion), channel_id=1, source_target_pairs={{0,28},{2,30},{4,0},{6,2},{8,4},{10,6},{12,8},{14,10},{16,12},{18,... | collective-permute-start | bytes 147464 | tf_op jit(solution)/shard_map/ppermute | solution.py:14
  253.7 11.8 %collective-permute-start.6 = (bf16[4,32,192]{2,1,0:T(8,128)(2,1)}, bf16[4,32,192]{2,1,0:T(8,128)(2,1)S(1)}, u32[]{:S(2)}, u32[]{:S(2)}) collective-permute-start(bf16[4,32,192]{2,1,0:T(8,128)(2,1)} %pad_maximum_fusion), channel_id=1, source_target_pairs={{0,26},{2,28},{4,30},{6,0},{8,2},{10,4},{12,6},{14,8},{16,10},{18,... | collective-permute-start | bytes 147464 | tf_op jit(solution)/shard_map/ppermute | solution.py:14
  255.2 11.0 %collective-permute-start.7 = (bf16[4,32,192]{2,1,0:T(8,128)(2,1)}, bf16[4,32,192]{2,1,0:T(8,128)(2,1)S(1)}, u32[]{:S(2)}, u32[]{:S(2)}) collective-permute-start(bf16[4,32,192]{2,1,0:T(8,128)(2,1)} %pad_maximum_fusion), channel_id=1, source_target_pairs={{0,24},{2,26},{4,28},{6,30},{8,0},{10,2},{12,4},{14,6},{16,8},{18,... | collective-permute-start | bytes 147464 | tf_op jit(solution)/shard_map/ppermute | solution.py:14
  256.6 44.7 %collective-permute-start.23 = (bf16[4,32,192]{2,0,1:T(4,128)(2,1)S(1)}, bf16[4,32,192]{2,0,1:T(4,128)(2,1)}, u32[]{:S(2)}, u32[]{:S(2)}) collective-permute-start(bf16[4,32,192]{2,0,1:T(4,128)(2,1)S(1)} %pad_maximum_fusion.1), channel_id=1, source_target_pairs={{0,8},{2,10},{4,12},{6,14},{8,16},{10,18},{12,20},{14,22},{16,24},... | collective-permute-start | bytes 147464 | tf_op jit(solution)/shard_map/ppermute | solution.py:14
  260.1 42.8 %collective-permute-start.22 = (bf16[4,32,192]{2,0,1:T(4,128)(2,1)S(1)}, bf16[4,32,192]{2,0,1:T(4,128)(2,1)}, u32[]{:S(2)}, u32[]{:S(2)}) collective-permute-start(bf16[4,32,192]{2,0,1:T(4,128)(2,1)S(1)} %pad_maximum_fusion.1), channel_id=1, source_target_pairs={{0,6},{2,8},{4,10},{6,12},{8,14},{10,16},{12,18},{14,20},{16,22},{... | collective-permute-start | bytes 147464 | tf_op jit(solution)/shard_map/ppermute | solution.py:14
  262.0 42.2 %collective-permute-start.21 = (bf16[4,32,192]{2,0,1:T(4,128)(2,1)S(1)}, bf16[4,32,192]{2,0,1:T(4,128)(2,1)}, u32[]{:S(2)}, u32[]{:S(2)}) collective-permute-start(bf16[4,32,192]{2,0,1:T(4,128)(2,1)S(1)} %pad_maximum_fusion.1), channel_id=1, source_target_pairs={{0,4},{2,6},{4,8},{6,10},{8,12},{10,14},{12,16},{14,18},{16,20},{1... | collective-permute-start | bytes 147464 | tf_op jit(solution)/shard_map/ppermute | solution.py:14
  265.5 40.1 %collective-permute-start.20 = (bf16[4,32,192]{2,0,1:T(4,128)(2,1)S(1)}, bf16[4,32,192]{2,0,1:T(4,128)(2,1)}, u32[]{:S(2)}, u32[]{:S(2)}) collective-permute-start(bf16[4,32,192]{2,0,1:T(4,128)(2,1)S(1)} %pad_maximum_fusion.1), channel_id=1, source_target_pairs={{0,2},{2,4},{4,6},{6,8},{8,10},{10,12},{12,14},{14,16},{16,18},{18... | collective-permute-start | bytes 147464 | tf_op jit(solution)/shard_map/ppermute | solution.py:14
  266.1 40.6 %collective-permute-start.19 = (bf16[4,32,192]{2,0,1:T(4,128)(2,1)S(1)}, bf16[4,32,192]{2,0,1:T(4,128)(2,1)}, u32[]{:S(2)}, u32[]{:S(2)}) collective-permute-start(bf16[4,32,192]{2,0,1:T(4,128)(2,1)S(1)} %pad_maximum_fusion.1), channel_id=1, source_target_pairs={{0,30},{2,0},{4,2},{6,4},{8,6},{10,8},{12,10},{14,12},{16,14},{18,... | collective-permute-start | bytes 147464 | tf_op jit(solution)/shard_map/ppermute | solution.py:14
  294.1 104.4 %reduce-scatter.2.cloned.1.call-start = ((), (), s32[]{:S(2)}) async-start(), calls=%async_computation.1 | async-start | bytes 2359296 | tf_op jit(solution)/shard_map/reduce_scatter | solution.py:111
  301.2 6.7 %copy-start.31 = (s32[4]{0:T(128)S(1)}, s32[4]{0:T(128)}, u32[]{:S(2)}) copy-start(s32[4]{0:T(128)} %gather_fusion.6) | copy-start | bytes 52
  301.2 6.7 %copy-start.38 = (pred[4]{0:T(512)(128)(4,1)S(1)}, pred[4]{0:T(512)(128)(4,1)}, u32[]{:S(2)}) copy-start(pred[4]{0:T(512)(128)(4,1)} %get-tuple-element.327) | copy-start | bytes 16
  301.3 7.0 %copy-start.30 = (s32[4]{0:T(128)S(1)}, s32[4]{0:T(128)}, u32[]{:S(2)}) copy-start(s32[4]{0:T(128)} %gather_fusion.5) | copy-start | bytes 52
  301.3 7.0 %copy-start.37 = (pred[4]{0:T(512)(128)(4,1)S(1)}, pred[4]{0:T(512)(128)(4,1)}, u32[]{:S(2)}) copy-start(pred[4]{0:T(512)(128)(4,1)} %get-tuple-element.328) | copy-start | bytes 16
  301.3 9.6 %copy-start.44 = (s32[4]{0:T(128)S(1)}, s32[4]{0:T(128)}, u32[]{:S(2)}) copy-start(s32[4]{0:T(128)} %gather_fusion.4) | copy-start | bytes 52
  301.3 9.6 %copy-start.45 = (pred[4]{0:T(512)(128)(4,1)S(1)}, pred[4]{0:T(512)(128)(4,1)}, u32[]{:S(2)}) copy-start(pred[4]{0:T(512)(128)(4,1)} %get-tuple-element.323) | copy-start | bytes 16
  301.3 6.6 %collective-permute-start.18 = (bf16[4,32,192]{2,0,1:T(4,128)(2,1)S(1)}, bf16[4,32,192]{2,0,1:T(4,128)(2,1)S(1)}, u32[]{:S(2)}, u32[]{:S(2)}) collective-permute-start(bf16[4,32,192]{2,0,1:T(4,128)(2,1)S(1)} %pad_maximum_fusion.1), channel_id=1, source_target_pairs={{0,28},{2,30},{4,0},{6,2},{8,4},{10,6},{12,8},{14,10},{16,12},{18,... | collective-permute-start | bytes 147464 | tf_op jit(solution)/shard_map/ppermute | solution.py:14
  303.0 5.3 %collective-permute-start.17 = (bf16[4,32,192]{2,0,1:T(4,128)(2,1)S(1)}, bf16[4,32,192]{2,0,1:T(4,128)(2,1)S(1)}, u32[]{:S(2)}, u32[]{:S(2)}) collective-permute-start(bf16[4,32,192]{2,0,1:T(4,128)(2,1)S(1)} %pad_maximum_fusion.1), channel_id=1, source_target_pairs={{0,26},{2,28},{4,30},{6,0},{8,2},{10,4},{12,6},{14,8},{16,10},{18,... | collective-permute-start | bytes 147464 | tf_op jit(solution)/shard_map/ppermute | solution.py:14
  304.2 6.7 %collective-permute-start.16 = (bf16[4,32,192]{2,0,1:T(4,128)(2,1)S(1)}, bf16[4,32,192]{2,0,1:T(4,128)(2,1)S(1)}, u32[]{:S(2)}, u32[]{:S(2)}) collective-permute-start(bf16[4,32,192]{2,0,1:T(4,128)(2,1)S(1)} %pad_maximum_fusion.1), channel_id=1, source_target_pairs={{0,24},{2,26},{4,28},{6,30},{8,0},{10,2},{12,4},{14,6},{16,8},{18,... | collective-permute-start | bytes 147464 | tf_op jit(solution)/shard_map/ppermute | solution.py:14
  (35 other events, 103.2 us)
Sparse Core Ops, SparseCore 0:
  294.2 100.7 all-reduce.3
Sparse Core Ops, SparseCore 1:
  301.4 23.1 reduce-scatter.1
where the time goes:
time: 410 us; the launch traced here: 408 us
  waiting for transfers between devices  126 us (31%)
  local copies, waits for them, and re-layouts  110 us (27%)
  starting transfers between devices  44.9 us (11%)
  matrix products  38.7 us (9%)
  blocking collectives  38 us (9%)
  other arithmetic  34.1 us (8%)
  between operations  16.8 us (4%)
    psum x1, waiting for transfers between devices, body(): lax.psum(local_grad, 'tile') * (1.0 / math.sqrt(tile_count * rows))  79.3 us
    ppermute x32, waiting for transfers between devices, shifted(): lax.ppermute(shard, axis, [(i, (i + by) % peers) for i in range(peers)])  46.4 us
    ppermute x32, starting transfers between devices, shifted(): lax.ppermute(shard, axis, [(i, (i + by) % peers) for i in range(peers)])  44.8 us
    scatter-add x9, local copies, waits for them, and re-layouts, body(): grad_padded = grad_padded.at[row_off:row_off + side_len, col_off:col_off...  39.4 us
    all_gather x1, blocking collectives, body(): lax.all_gather(cotangent[0], 'ch', axis=2, tiled=True)  38 us
    unnamed x115, local copies, waits for them, and re-layouts  16.1 us
    add x7, other arithmetic, body(): grad_padded = grad_padded.at[row_off:row_off + side_len, col_off:col_off...  15.5 us
    dot_general x9, matrix products, body(): jnp.dot(windows[tap_index], blocks[tap_index], preferred_element_type=jnp...  14.9 us
  transfers between devices with their start and end apart: 34, of which 17 were waited for; matrix products, arithmetic and copies ran while one was open for 43% of the time, Pallas kernels for 0%

commit v1 on v0

v1 whole, which is shorter than its diff:
```python
import math

import jax
import jax.numpy as jnp
import numpy as np
from jax import lax
from jax.sharding import PartitionSpec as P

SPAN = 4


def turn_tables():
    labels = [[3 * row + col for col in range(3)] for row in range(3)]

    def turn_once(block):
        return [[block[col][2 - row] for col in range(3)] for row in range(3)]

    def sides_of(block):
        return [
            list(block[0]),
            [block[row][2] for row in range(3)],
            list(block[2]),
            [block[row][0] for row in range(3)],
        ]

    def corners_of(block):
        return [block[0][0], block[0][2], block[2][2], block[2][0]]

    base_sides = sides_of(labels)
    base_corners = corners_of(labels)
    edge_table = np.zeros((4, 4), np.int32)
    corner_table = np.zeros((4, 4), np.int32)
    for border in range(4):
        turned = labels
        for quarter in range(4):
            wanted = sides_of(turned)[(border + 2) % 4]
            for side_index in range(4):
                if base_sides[side_index] == wanted:
                    edge_table[border, quarter] = side_index
                if base_sides[side_index][::-1] == wanted:
                    edge_table[border, quarter] = side_index + 4
            corner_cell = corners_of(turned)[(border + 2) % 4]
            for corner_index in range(4):
                if base_corners[corner_index] == corner_cell:
                    corner_table[border, quarter] = corner_index
            turned = turn_once(turned)
    return (edge_table, corner_table)


def moved(value, axis, pairs):
    return lax.ppermute(value, axis, pairs)


def by_offset(value, offset, count):
    return moved(value, "tile", [(i, (i + offset) % count) for i in range(count)])


def by_mask(value, mask, count):
    return moved(value, "tile", [(i, i ^ mask) for i in range(count)])


def mask_stages(count):
    bits = [1 << b for b in range(count.bit_length() - 1)]
    stages = [bits[:1]]
    rest = bits[1:]
    while rest:
        stages.append(rest[:2])
        rest = rest[2:]
    return stages


def group_masks(bits):
    masks = [0]
    for bit in bits:
        masks = masks + [m + bit for m in masks]
    return masks


def sum_over_tiles(partial, own_tile, count):
    stages = mask_stages(count)
    held = partial
    for index, bits in enumerate(stages):
        masks = group_masks(bits)
        part = held.shape[0] // len(masks)
        base = (own_tile // bits[0]) % len(masks)
        kind = jnp.float32 if index == 0 else jnp.bfloat16

        def piece(mask):
            return lax.dynamic_slice_in_dim(held, (base ^ (mask // bits[0])) * part, part, 0)

        got = [by_mask(piece(mask).astype(kind), mask, count) for mask in masks[1:]]
        total = piece(0)
        for value in got:
            total = total + value.astype(jnp.float32)
        held = total
    held = held.astype(jnp.bfloat16)
    for bits in stages[::-1]:
        masks = group_masks(bits)
        part = held.shape[0]
        base = (own_tile // bits[0]) % len(masks)
        got = [held] + [by_mask(held, mask, count) for mask in masks[1:]]
        whole = jnp.zeros((part * len(masks), held.shape[1]), held.dtype)
        for mask, value in zip(masks, got):
            whole = lax.dynamic_update_slice_in_dim(
                whole, value, (base ^ (mask // bits[0])) * part, 0
            )
        held = whole
    return held


def body(features, weight, cotangent, edge_tiles, edge_turns, corner_tiles, corner_turns):
    edge_table, corner_table = turn_tables()
    count = lax.axis_size("tile")
    own_tile = lax.axis_index("tile")
    own_ch = lax.axis_index("ch")
    field = features[0]
    side = field.shape[0]
    part = field.shape[2]
    chans = weight.shape[3]
    rows = side * side
    start = own_ch * part
    offsets = list(range(-SPAN, 0)) + list(range(1, SPAN + 1))
    others = [(0, 1), (1, 0)]
    cells = jnp.arange(side)

    cot_own = cotangent[0].reshape(rows, part)
    cot_other = moved(cot_own, "ch", others)

    sides = jnp.concatenate([field[0], field[:, -1], field[-1], field[:, 0]], axis=0)
    near = jnp.concatenate([by_offset(sides, -offset, count) for offset in offsets], axis=0)

    def position(target):
        wrapped = jnp.mod(target - own_tile, count)
        signed = jnp.where(wrapped > count // 2, wrapped - count, wrapped)
        return jnp.where(signed < 0, signed + SPAN, signed + SPAN - 1)

    edge_slot_all = jnp.asarray(edge_table)[jnp.arange(4)[None, :], edge_turns]
    corner_slot_all = jnp.asarray(corner_table)[jnp.arange(4)[None, :], corner_turns]
    corner_cell = jnp.asarray([0, side - 1, 3 * side - 1, 2 * side])

    def side_cell(slots):
        along = jnp.where((slots >= 4)[..., None], side - 1 - cells, cells)
        return (slots % 4)[..., None] * side + along

    edge_from = position(edge_tiles[own_tile])[:, None] * (4 * side) + side_cell(edge_slot_all[own_tile])
    corner_from = position(corner_tiles[own_tile]) * (4 * side) + corner_cell[corner_slot_all[own_tile]]
    wanted = jnp.concatenate([edge_from.reshape(-1), corner_from])
    pick = (wanted[:, None] == jnp.arange(8 * 4 * side)[None, :]).astype(jnp.bfloat16)
    halos = jnp.dot(pick, near, preferred_element_type=jnp.float32).astype(jnp.bfloat16)
    top, right, bottom, left = [halos[e * side : (e + 1) * side] for e in range(4)]
    corners = [halos[4 * side + c : 4 * side + c + 1] for c in range(4)]
    tall = jnp.concatenate([top[None], field, bottom[None]], axis=0)
    west = jnp.concatenate([corners[0], left, corners[3]], axis=0)[:, None]
    east = jnp.concatenate([corners[1], right, corners[2]], axis=0)[:, None]
    shifted = [
        jnp.concatenate([west, tall[:, :-1]], axis=1),
        tall,
        jnp.concatenate([tall[:, 1:], east], axis=1),
    ]
    flat = (side + 2) * side
    columns = jnp.concatenate([s.reshape(flat, part) for s in shifted], axis=1)

    def both(own, other):
        return jnp.where(
            own_ch == 0,
            jnp.concatenate([own, other], axis=-1),
            jnp.concatenate([other, own], axis=-1),
        )

    cot_full = both(cot_own, cot_other)

    grads = [
        lax.dot_general(
            columns[a * side : a * side + rows],
            cot_full,
            (((0,), (0,)), ((), ())),
            preferred_element_type=jnp.float32,
        )
        for a in range(3)
    ]
    chunk = -(-9 * part // (16 * count)) * 16
    padding = jnp.zeros((chunk * count - 9 * part, chans), jnp.float32)
    local_grad = jnp.concatenate(grads + [padding], axis=0) * (1.0 / math.sqrt(count * rows))
    grad_weight = sum_over_tiles(local_grad, own_tile, count)[: 9 * part]
    grad_weight = grad_weight.astype(jnp.float32).reshape(3, 3, part, chans)

    weight_back = lax.dynamic_slice_in_dim(weight, start, part, 2)
    zeros = jnp.zeros((2 * side, chans), jnp.bfloat16)
    cot_tall = jnp.concatenate([zeros, cot_full, zeros], axis=0)
    cot_rows = jnp.concatenate([cot_tall[(2 - a) * side : (2 - a) * side + flat] for a in range(3)], axis=1)
    backs = []
    for b in range(3):
        taps = jnp.concatenate([weight_back[a, b] for a in range(3)], axis=1)
        back = lax.dot_general(
            cot_rows, taps, (((1,), (1,)), ((), ())), preferred_element_type=jnp.float32
        )
        backs.append(back.reshape(side + 2, side, part))
    blank = jnp.zeros((side + 2, 1, part), jnp.float32)
    inner = (
        jnp.concatenate([backs[0][:, 1:], blank], axis=1)
        + backs[1]
        + jnp.concatenate([blank, backs[2][:, :-1]], axis=1)
    )
    west_back, east_back = backs[0][:, 0], backs[2][:, -1]
    pieces = jnp.concatenate(
        [
            inner[0],
            east_back[1:-1],
            inner[-1],
            west_back[1:-1],
            west_back[:1],
            east_back[:1],
            east_back[-1:],
            west_back[-1:],
            jnp.zeros((4, part), jnp.float32),
        ],
        axis=0,
    ).astype(jnp.bfloat16)
    inner = inner[1:-1]
    got = jnp.concatenate([by_offset(pieces, offset, count) for offset in offsets], axis=0)
    sources = jnp.mod(own_tile - jnp.asarray(offsets), count)
    edge_to = jnp.where(
        (edge_tiles[sources] == own_tile)[..., None], side_cell(edge_slot_all[sources]), -1
    ).reshape(8, 4 * side)
    corner_to = jnp.where(
        corner_tiles[sources] == own_tile, corner_cell[corner_slot_all[sources]], -1
    )
    target = jnp.concatenate([edge_to, corner_to, jnp.full((8, 4), -1)], axis=1).reshape(-1)
    place = (jnp.arange(4 * side)[:, None] == target[None, :]).astype(jnp.bfloat16)
    sums = jnp.dot(place, got, preferred_element_type=jnp.float32)
    inner = inner.at[0].add(sums[:side]).at[:, -1].add(sums[side : 2 * side])
    inner = inner.at[-1].add(sums[2 * side : 3 * side]).at[:, 0].add(sums[3 * side :])
    grad_features = inner.astype(jnp.bfloat16)[None]

    field_other = moved(jnp.concatenate([field.reshape(rows, part), halos], axis=0), "ch", others)
    other_field = field_other[:rows].reshape(side, side, part)
    other_halos = field_other[rows:]

    def columns_of(field, halos):
        top, right, bottom, left = [halos[e * side : (e + 1) * side] for e in range(4)]
        corners = [halos[4 * side + c : 4 * side + c + 1] for c in range(4)]
        tall = jnp.concatenate([top[None], field, bottom[None]], axis=0)
        west = jnp.concatenate([corners[0], left, corners[3]], axis=0)[:, None]
        east = jnp.concatenate([corners[1], right, corners[2]], axis=0)[:, None]
        return [
            jnp.concatenate([west, tall[:, :-1]], axis=1).reshape(flat, part),
            tall.reshape(flat, part),
            jnp.concatenate([tall[:, 1:], east], axis=1).reshape(flat, part),
        ]

    others_columns = columns_of(other_field, other_halos)
    weight_out = lax.dynamic_slice_in_dim(weight, start, part, 3)
    weight_own = lax.dynamic_slice_in_dim(weight_out, start, part, 2)
    weight_other = lax.dynamic_slice_in_dim(weight_out, part - start, part, 2)
    output = jnp.zeros((rows, part), jnp.float32)
    for a in range(3):
        for b in range(3):
            output = output + jnp.dot(
                columns[a * side : a * side + rows, b * part : (b + 1) * part],
                weight_own[a, b],
                preferred_element_type=jnp.float32,
            )
            output = output + jnp.dot(
                others_columns[b][a * side : a * side + rows],
                weight_other[a, b],
                preferred_element_type=jnp.float32,
            )
    output = output.astype(jnp.bfloat16).reshape(1, side, side, part)
    return (output, grad_features, grad_weight)


def solution(mesh):
    return jax.shard_map(
        body,
        mesh=mesh,
        in_specs=(
            P("tile", None, None, "ch"),
            P(),
            P("tile", None, None, "ch"),
            P(),
            P(),
            P(),
            P(),
        ),
        out_specs=(
            P("tile", None, None, "ch"),
            P("tile", None, None, "ch"),
            P(None, None, "ch", None),
        ),
        check_vma=False,
    )
```

time: 410 us -> 224 us (0.55)
  waiting for transfers between devices: 126 us -> 28.9 us
  blocking collectives: 38 us -> 0 us
  matrix products: 38.7 us -> 18.8 us
  between operations: 16.8 us -> 2.17 us
  starting transfers between devices: 44.9 us -> 33.3 us
  local copies, waits for them, and re-layouts: 110 us -> 101 us
    psum x1 -> x0, waiting for transfers between devices: 79.3 us -> none  [body(): lax.psum(local_grad, 'tile') * (1.0 / math.sqrt(tile_count * rows))]
    all_gather x1 -> x0, blocking collectives: 38 us -> none  [body(): lax.all_gather(cotangent[0], 'ch', axis=2, tiled=True)]
    dot_general x43 -> x26, matrix products: 38.7 us -> 18.8 us  [the longest x9 6.03 us: body(): jnp.dot(others_columns[b][a * side:a * side + rows], weight_other[a, b],...]
    ppermute x32 -> x28, waiting for transfers between devices: 46.4 us -> 28.9 us  [moved(): return lax.ppermute(value, axis, pairs)]
    gather x20 -> x12, local copies, waits for them, and re-layouts: 18 us -> 5.66 us  [the longest x2 0.96 us: body(): edge_slot_all = jnp.asarray(edge_table)[jnp.arange(4)[None, :], edge_turns]]
    concatenate x20 -> x16, other arithmetic: 0.18 us -> 12.1 us  [the longest x1 2.4 us: columns_of(): jnp.concatenate([west, tall[:, :-1]], axis=1).reshape(flat, part)]
    ppermute x32 -> x28, starting transfers between devices: 44.8 us -> 33.3 us  [moved(): return lax.ppermute(value, axis, pairs)]
    dot_general x9 -> x0, local copies, waits for them, and re-layouts: 11.3 us -> none  [body(): lax.dot_general(cot_full, blocks[tap_index], (((1,), (1,)), ((), ())), pr...]
  transfers between devices with their start and end apart: 34 -> 28, of which waited for: 17 -> 11; matrix products, arithmetic and copies ran while one was open for 43% -> 66% of each run, Pallas kernels for 0% -> 0%
where the time goes in v1:
time: 224 us; the launch traced here: 220 us
  local copies, waits for them, and re-layouts  101 us (45%)
  other arithmetic  35.6 us (16%)
  starting transfers between devices  33.3 us (15%)
  waiting for transfers between devices  28.9 us (13%)
  matrix products  18.8 us (8%)
    ppermute x28, starting transfers between devices, moved(): return lax.ppermute(value, axis, pairs)  33.3 us
    ppermute x28, waiting for transfers between devices, moved(): return lax.ppermute(value, axis, pairs)  28.9 us
    unnamed x115, local copies, waits for them, and re-layouts  23.2 us
    scatter-add x1, local copies, waits for them, and re-layouts, body(): inner.at[-1].add(sums[2 * side:3 * side]).at[:, 0].add(sums[3 * side:])  18.1 us
    scatter-add x1, local copies, waits for them, and re-layouts, body(): inner = inner.at[0].add(sums[:side]).at[:, -1].add(sums[side:2 * side])  14.7 us
    slice x8, local copies, waits for them, and re-layouts, body(): columns[a * side:a * side + rows, b * part:(b + 1) * part]  9.32 us
    another operation x3, local copies, waits for them, and re-layouts  7.58 us
    dot_general x9, matrix products, body(): jnp.dot(others_columns[b][a * side:a * side + rows], weight_other[a, b],...  6.03 us
  transfers between devices with their start and end apart: 28, of which 11 were waited for; matrix products, arithmetic and copies ran while one was open for 66% of the time, Pallas kernels for 0%

profile of v1, /device:TPU:0, one launch (start us, length us, event | category | flops | bytes accessed | tf_op | source)
XLA Modules:
  0.0 219.8 jit_solution(14079560763299718686)
XLA Ops:
  2.7 3.1 %collective-permute-start = (bf16[128,192]{1,0:T(8,128)(2,1)S(1)}, bf16[128,192]{1,0:T(8,128)(2,1)}, u32[]{:S(2)}, u32[]{:S(2)}) collective-permute-start(bf16[128,192]{1,0:T(8,128)(2,1)S(1)} %pad_maximum_fusion.14), channel_id=1, source_target_pairs={{0,8},{2,10},{4,12},{6,14},{8,16},{10,18},{12,20},{14,22},{16,24},... | collective-permute-start | bytes 147464 | tf_op jit(solution)/shard_map/ppermute | solution.py:51
  6.5 1.5 collective-permute-start.2
  8.8 3.7 %collective-permute-start.4 = (bf16[128,192]{1,0:T(8,128)(2,1)S(1)}, bf16[128,192]{1,0:T(8,128)(2,1)}, u32[]{:S(2)}, u32[]{:S(2)}) collective-permute-start(bf16[128,192]{1,0:T(8,128)(2,1)S(1)} %pad_maximum_fusion.14), channel_id=1, source_target_pairs={{0,30},{2,0},{4,2},{6,4},{8,6},{10,8},{12,10},{14,12},{16,14},{18,... | collective-permute-start | bytes 147464 | tf_op jit(solution)/shard_map/ppermute | solution.py:51
  27.1 1.5 collective-permute-start.9
  31.1 1.5 pad_maximum_fusion.10
  37.8 1.4 fusion.48
  42.8 2.2 copy.272
  45.0 2.2 copy.273
  52.0 1.6 pad_maximum_fusion.2
  53.6 1.8 maximum_select_fusion
  58.8 2.5 %copy.322 = f32[34,31,192]{0,2,1:T(8,128)} copy(f32[34,31,192]{2,1,0:T(8,128)S(1)} %bitcast.219) | data formatting | bytes 1618944
  61.3 1.9 fusion.30
  63.2 2.2 copy.288
  65.4 3.3 %copy.321 = f32[34,31,192]{0,2,1:T(8,128)} copy(f32[34,31,192]{2,1,0:T(8,128)} %slice.631) | data formatting | bytes 1618944
  68.7 5.4 %fusion.92 = (bf16[34,32,192]{0,2,1:T(8,128)(2,1)S(1)}, f32[34,32,192]{0,2,1:T(8,128)}) fusion(f32[34,31,192]{0,2,1:T(8,128)} %copy.322, f32[34,32,192]{0,2,1:T(8,128)S(1)} %copy.288, f32[34,31,192]{0,2,1:T(8,128)} %copy.321), kind=kLoop, calls=%fused_computation.272 | loop fusion | flops 626688 | bytes 3707904 | tf_op jit(solution)/shard_map/convert.25
  74.0 1.8 slice_reduce_fusion
  75.9 2.4 %collective-permute-start.10 = (bf16[136,192]{1,0:T(8,128)(2,1)S(1)}, bf16[136,192]{1,0:T(8,128)(2,1)S(1)}, u32[]{:S(2)}, u32[]{:S(2)}) collective-permute-start(bf16[136,192]{1,0:T(8,128)(2,1)S(1)} %concatenate.149), channel_id=1, source_target_pairs={{0,24},{2,26},{4,28},{6,30},{8,0},{10,2},{12,4},{14,6},{16,8},{18,... | collective-permute-start | bytes 156680 | tf_op jit(solution)/shard_map/ppermute | solution.py:51
  79.5 1.8 collective-permute-start.13
  85.3 1.8 copy-done.3
  88.5 2.5 %collective-permute-start.16 = (bf16[136,192]{1,0:T(8,128)(2,1)S(1)}, bf16[136,192]{1,0:T(8,128)(2,1)S(1)}, u32[]{:S(2)}, u32[]{:S(2)}) collective-permute-start(bf16[136,192]{1,0:T(8,128)(2,1)S(1)} %concatenate.149), channel_id=1, source_target_pairs={{0,6},{2,8},{4,10},{6,12},{8,14},{10,16},{12,18},{14,20},{16,22},{... | collective-permute-start | bytes 156680 | tf_op jit(solution)/shard_map/ppermute | solution.py:51
  91.0 1.5 collective-permute-start.17
  92.5 2.2 collective-permute-done.14
  97.6 3.9 %copy.296 = f32[1,32,192]{0,2,1:T(8,128)} copy(f32[1,32,192]{1,2,0:T(8,128)S(1)} %get-tuple-element.130) | data formatting | bytes 49152 | tf_op jit(solution)/shard_map/reshape.85
  101.5 5.4 %slice_add_fusion.1 = f32[1,32,192]{0,2,1:T(8,128)} fusion(f32[1,32,192]{0,2,1:T(8,128)} %copy.296, f32[34,32,192]{0,2,1:T(8,128)} %get-tuple-element.80), kind=kLoop, calls=%fused_computation.13 | loop fusion | flops 6144 | bytes 73728 | tf_op jit(solution)/shard_map/add | solution.py:231
  106.9 14.7 %scatter-add.14 = f32[32,32,192]{0,2,1:T(8,128)S(1)} dynamic-update-slice(f32[32,32,192]{0,2,1:T(8,128)S(1)} %slice.633, f32[1,32,192]{0,2,1:T(8,128)} %slice_add_fusion.1, s32[]{:T(128)} %constant.303.clone.1, s32[]{:T(128)} %constant.303.clone.1, s32[]{:T(128)} %constant.303.clone.1) | dynamic-update-slice | bytes 49156 | tf_op jit(solution)/shard_map/scatter-add | solution.py:231
  121.7 3.6 %copy.298 = f32[1,32,192]{0,2,1:T(8,128)} copy(f32[1,32,192]{1,2,0:T(8,128)S(1)} %get-tuple-element.129) | data formatting | bytes 49152 | tf_op jit(solution)/shard_map/reshape.103
  125.4 4.4 %slice_add_fusion = f32[1,32,192]{0,2,1:T(8,128)} fusion(f32[1,32,192]{0,2,1:T(8,128)} %copy.298, f32[32,32,192]{0,2,1:T(8,128)S(1)} %fusion.47), kind=kLoop, calls=%fused_computation.12 | loop fusion | flops 6144 | bytes 73728 | tf_op jit(solution)/shard_map/add | solution.py:232
  129.8 18.1 %scatter-add.16 = f32[32,32,192]{0,2,1:T(8,128)S(1)} dynamic-update-slice(f32[32,32,192]{0,2,1:T(8,128)S(1)} %fusion.47, f32[1,32,192]{0,2,1:T(8,128)} %slice_add_fusion, s32[]{:T(128)} %constant.312.clone.1, s32[]{:T(128)} %constant.303.clone.1, s32[]{:T(128)} %constant.303.clone.1) | dynamic-update-slice | bytes 49156 | tf_op jit(solution)/shard_map/scatter-add | solution.py:232
  147.9 1.4 convert_bitcast_fusion
  149.3 2.9 %copy.302 = bf16[1,32,32,192]{3,2,1,0:T(8,128)(2,1)} copy(bf16[1,32,32,192]{1,3,2,0:T(8,128)(2,1)} %convert_bitcast_fusion) | data formatting | bytes 786432
  152.3 1.7 fusion.96
  158.0 1.7 fusion.95
  159.7 1.5 copy.314
  162.0 1.5 copy.312
  165.9 2.4 %pad_maximum_fusion.11 = (bf16[32,32,192]{2,1,0:T(8,128)(2,1)S(1)}, bf16[32,32,192]{2,1,0:T(8,128)(2,1)S(1)}, bf16[32,32,192]{2,1,0:T(8,128)(2,1)S(1)}) fusion(bf16[34,31,192]{2,1,0:T(8,128)(2,1)} %get-tuple-element.112, bf16[34,1,192]{2,1,0:T(2,128)(2,1)} %copy.270), kind=kLoop, calls=%fused_computation.83 | loop fusion | flops 2359296 | bytes 1597440 | tf_op jit(solution)/shard_map/concatenate | solution.py:246
  173.1 1.5 fusion.10
  174.7 1.5 dynamic-slice_add_fusion
  177.3 3.0 %collective-permute-start.20 = (bf16[224,384]{1,0:T(8,128)(2,1)S(1)}, bf16[224,384]{1,0:T(8,128)(2,1)S(1)}, u32[]{:S(2)}, u32[]{:S(2)}) collective-permute-start(bf16[224,384]{1,0:T(8,128)(2,1)S(1)} %get-tuple-element.92), channel_id=1, source_target_pairs={{0,8},{2,10},{4,12},{6,14},{8,0},{10,2},{12,4},{14,6},{16,24},{18,... | collective-permute-start | bytes 516104 | tf_op jit(solution)/shard_map/ppermute | solution.py:51
  180.8 3.6 %collective-permute-done.21 = bf16[224,384]{1,0:T(8,128)(2,1)S(1)} collective-permute-done((bf16[224,384]{1,0:T(8,128)(2,1)S(1)}, bf16[224,384]{1,0:T(8,128)(2,1)S(1)}, u32[]{:S(2)}, u32[]{:S(2)}) %collective-permute-start.21) | collective-permute-done | bytes 172064 | tf_op jit(solution)/shard_map/ppermute | solution.py:51
  184.4 2.8 %collective-permute-done.20 = bf16[224,384]{1,0:T(8,128)(2,1)S(1)} collective-permute-done((bf16[224,384]{1,0:T(8,128)(2,1)S(1)}, bf16[224,384]{1,0:T(8,128)(2,1)S(1)}, u32[]{:S(2)}, u32[]{:S(2)}) %collective-permute-start.20) | collective-permute-done | bytes 172064 | tf_op jit(solution)/shard_map/ppermute | solution.py:51
  189.5 4.7 %collective-permute-done.22 = bf16[112,384]{1,0:T(8,128)(2,1)S(1)} collective-permute-done((bf16[112,384]{1,0:T(8,128)(2,1)S(1)}, bf16[112,384]{1,0:T(8,128)(2,1)S(1)}, u32[]{:S(2)}, u32[]{:S(2)}) %collective-permute-start.22) | collective-permute-done | bytes 86048 | tf_op jit(solution)/shard_map/ppermute | solution.py:51
  195.1 5.2 %collective-permute-done.23 = bf16[112,384]{1,0:T(8,128)(2,1)S(1)} collective-permute-done((bf16[112,384]{1,0:T(8,128)(2,1)S(1)}, bf16[112,384]{1,0:T(8,128)(2,1)S(1)}, u32[]{:S(2)}, u32[]{:S(2)}) %collective-permute-start.23) | collective-permute-done | bytes 86048 | tf_op jit(solution)/shard_map/ppermute | solution.py:51
  201.6 2.8 %collective-permute-start.26 = (bf16[224,384]{1,0:T(8,128)(2,1)S(1)}, bf16[224,384]{1,0:T(8,128)(2,1)S(1)}, u32[]{:S(2)}, u32[]{:S(2)}) collective-permute-start(bf16[224,384]{1,0:T(8,128)(2,1)S(1)} %constant_dynamic-update-slice_fusion.22), channel_id=1, source_target_pairs={{0,12},{2,14},{4,8},{6,10},{8,4},{10,6},{12,0},{14,2},{16,28},{18,... | collective-permute-start | bytes 516104 | tf_op jit(solution)/shard_map/ppermute | solution.py:51
  204.6 1.9 collective-permute-done.24
  206.5 2.4 %collective-permute-done.25 = bf16[224,384]{1,0:T(8,128)(2,1)S(1)} collective-permute-done((bf16[224,384]{1,0:T(8,128)(2,1)S(1)}, bf16[224,384]{1,0:T(8,128)(2,1)S(1)}, u32[]{:S(2)}, u32[]{:S(2)}) %collective-permute-start.25) | collective-permute-done | bytes 172064 | tf_op jit(solution)/shard_map/ppermute | solution.py:51
  209.0 2.9 %collective-permute-done.26 = bf16[224,384]{1,0:T(8,128)(2,1)S(1)} collective-permute-done((bf16[224,384]{1,0:T(8,128)(2,1)S(1)}, bf16[224,384]{1,0:T(8,128)(2,1)S(1)}, u32[]{:S(2)}, u32[]{:S(2)}) %collective-permute-start.26) | collective-permute-done | bytes 172064 | tf_op jit(solution)/shard_map/ppermute | solution.py:51
  214.2 2.0 copy.284
  217.8 1.7 convert.36
  (296 shorter events, 68.7 us)
Async XLA Ops:
  0.6 12.7 %copy-start.2 = (s32[4,4]{1,0:T(4,128)S(1)}, s32[4,4]{1,0:T(4,128)}, u32[]{:S(2)}) copy-start(s32[4,4]{1,0:T(4,128)} %constant.327.clone) | copy-start | bytes 196
  2.7 20.0 %collective-permute-start = (bf16[128,192]{1,0:T(8,128)(2,1)S(1)}, bf16[128,192]{1,0:T(8,128)(2,1)}, u32[]{:S(2)}, u32[]{:S(2)}) collective-permute-start(bf16[128,192]{1,0:T(8,128)(2,1)S(1)} %pad_maximum_fusion.14), channel_id=1, source_target_pairs={{0,8},{2,10},{4,12},{6,14},{8,16},{10,18},{12,20},{14,22},{16,24},... | collective-permute-start | bytes 147464 | tf_op jit(solution)/shard_map/ppermute | solution.py:51
  5.8 18.3 %collective-permute-start.1 = (bf16[128,192]{1,0:T(8,128)(2,1)S(1)}, bf16[128,192]{1,0:T(8,128)(2,1)}, u32[]{:S(2)}, u32[]{:S(2)}) collective-permute-start(bf16[128,192]{1,0:T(8,128)(2,1)S(1)} %pad_maximum_fusion.14), channel_id=1, source_target_pairs={{0,6},{2,8},{4,10},{6,12},{8,14},{10,16},{12,18},{14,20},{16,22},{... | collective-permute-start | bytes 147464 | tf_op jit(solution)/shard_map/ppermute | solution.py:51
  6.5 18.5 %collective-permute-start.2 = (bf16[128,192]{1,0:T(8,128)(2,1)S(1)}, bf16[128,192]{1,0:T(8,128)(2,1)}, u32[]{:S(2)}, u32[]{:S(2)}) collective-permute-start(bf16[128,192]{1,0:T(8,128)(2,1)S(1)} %pad_maximum_fusion.14), channel_id=1, source_target_pairs={{0,4},{2,6},{4,8},{6,10},{8,12},{10,14},{12,16},{14,18},{16,20},{1... | collective-permute-start | bytes 147464 | tf_op jit(solution)/shard_map/ppermute | solution.py:51
  8.0 19.1 %collective-permute-start.3 = (bf16[128,192]{1,0:T(8,128)(2,1)S(1)}, bf16[128,192]{1,0:T(8,128)(2,1)}, u32[]{:S(2)}, u32[]{:S(2)}) collective-permute-start(bf16[128,192]{1,0:T(8,128)(2,1)S(1)} %pad_maximum_fusion.14), channel_id=1, source_target_pairs={{0,2},{2,4},{4,6},{6,8},{8,10},{10,12},{12,14},{14,16},{16,18},{18... | collective-permute-start | bytes 147464 | tf_op jit(solution)/shard_map/ppermute | solution.py:51
  8.8 20.7 %collective-permute-start.4 = (bf16[128,192]{1,0:T(8,128)(2,1)S(1)}, bf16[128,192]{1,0:T(8,128)(2,1)}, u32[]{:S(2)}, u32[]{:S(2)}) collective-permute-start(bf16[128,192]{1,0:T(8,128)(2,1)S(1)} %pad_maximum_fusion.14), channel_id=1, source_target_pairs={{0,30},{2,0},{4,2},{6,4},{8,6},{10,8},{12,10},{14,12},{16,14},{18,... | collective-permute-start | bytes 147464 | tf_op jit(solution)/shard_map/ppermute | solution.py:51
  15.9 5.5 %copy-start.8 = (bf16[3,3,384,384]{3,2,1,0:T(8,128)(2,1)S(1)}, bf16[3,3,384,384]{3,2,1,0:T(8,128)(2,1)}, u32[]{:S(2)}) copy-start(bf16[3,3,384,384]{3,2,1,0:T(8,128)(2,1)} %param.20) | copy-start | bytes 7962628
  22.7 7.6 %collective-permute-start.5 = (bf16[128,192]{1,0:T(8,128)(2,1)S(1)}, bf16[128,192]{1,0:T(8,128)(2,1)S(1)}, u32[]{:S(2)}, u32[]{:S(2)}) collective-permute-start(bf16[128,192]{1,0:T(8,128)(2,1)S(1)} %pad_maximum_fusion.14), channel_id=1, source_target_pairs={{0,28},{2,30},{4,0},{6,2},{8,4},{10,6},{12,8},{14,10},{16,12},{18,... | collective-permute-start | bytes 147464 | tf_op jit(solution)/shard_map/ppermute | solution.py:51
  24.1 6.2 %collective-permute-start.6 = (bf16[128,192]{1,0:T(8,128)(2,1)S(1)}, bf16[128,192]{1,0:T(8,128)(2,1)S(1)}, u32[]{:S(2)}, u32[]{:S(2)}) collective-permute-start(bf16[128,192]{1,0:T(8,128)(2,1)S(1)} %pad_maximum_fusion.14), channel_id=1, source_target_pairs={{0,26},{2,28},{4,30},{6,0},{8,2},{10,4},{12,6},{14,8},{16,10},{18,... | collective-permute-start | bytes 147464 | tf_op jit(solution)/shard_map/ppermute | solution.py:51
  25.0 5.4 %collective-permute-start.7 = (bf16[128,192]{1,0:T(8,128)(2,1)S(1)}, bf16[128,192]{1,0:T(8,128)(2,1)S(1)}, u32[]{:S(2)}, u32[]{:S(2)}) collective-permute-start(bf16[128,192]{1,0:T(8,128)(2,1)S(1)} %pad_maximum_fusion.14), channel_id=1, source_target_pairs={{0,24},{2,26},{4,28},{6,30},{8,0},{10,2},{12,4},{14,6},{16,8},{18,... | collective-permute-start | bytes 147464 | tf_op jit(solution)/shard_map/ppermute | solution.py:51
  27.1 26.5 %collective-permute-start.9 = (bf16[1024,192]{1,0:T(8,128)(2,1)}, bf16[1024,192]{1,0:T(8,128)(2,1)}, u32[]{:S(2)}, u32[]{:S(2)}) collective-permute-start(bf16[1024,192]{1,0:T(8,128)(2,1)} %bitcast.243), channel_id=1, source_target_pairs={{0,1},{1,0},{2,3},{3,2},{4,5},{5,4},{6,7},{7,6},{8,9},{9,8},{10,11... | collective-permute-start | bytes 1179656 | tf_op jit(solution)/shard_map/ppermute | solution.py:51
  36.2 4.4 %copy-start.6 = (bf16[1,32,32,192]{3,2,1,0:T(8,128)(2,1)S(1)}, bf16[1,32,32,192]{3,2,1,0:T(8,128)(2,1)}, u32[]{:S(2)}) copy-start(bf16[1,32,32,192]{3,2,1,0:T(8,128)(2,1)} %param.19) | copy-start | bytes 1179652
  40.5 6.6 %copy-start.21 = (bf16[32,32,192]{2,0,1:T(8,128)(2,1)S(1)}, bf16[32,32,192]{2,0,1:T(8,128)(2,1)}, u32[]{:S(2)}) copy-start(bf16[32,32,192]{2,0,1:T(8,128)(2,1)} %get-tuple-element.98) | copy-start | bytes 1179652
  40.5 7.7 %copy-start.20 = (bf16[32,32,192]{2,0,1:T(8,128)(2,1)S(1)}, bf16[32,32,192]{2,0,1:T(8,128)(2,1)}, u32[]{:S(2)}) copy-start(bf16[32,32,192]{2,0,1:T(8,128)(2,1)} %get-tuple-element.96) | copy-start | bytes 1179652
  40.6 8.7 %copy-start.18 = (bf16[32,32,192]{2,0,1:T(8,128)(2,1)S(1)}, bf16[32,32,192]{2,0,1:T(8,128)(2,1)}, u32[]{:S(2)}) copy-start(bf16[32,32,192]{2,0,1:T(8,128)(2,1)} %get-tuple-element.115) | copy-start | bytes 1179652
  41.7 8.8 %copy-start.19 = (bf16[32,32,192]{2,0,1:T(8,128)(2,1)S(1)}, bf16[32,32,192]{2,0,1:T(8,128)(2,1)}, u32[]{:S(2)}) copy-start(bf16[32,32,192]{2,0,1:T(8,128)(2,1)} %get-tuple-element.93) | copy-start | bytes 1179652
  41.7 110.6 %collective-permute-start.8 = (bf16[1156,192]{0,1:T(8,128)(2,1)}, bf16[1156,192]{0,1:T(8,128)(2,1)}, u32[]{:S(2)}, u32[]{:S(2)}) collective-permute-start(bf16[1156,192]{0,1:T(8,128)(2,1)} %copy.263), channel_id=1, source_target_pairs={{0,1},{1,0},{2,3},{3,2},{4,5},{5,4},{6,7},{7,6},{8,9},{9,8},{10,11... | collective-permute-start | bytes 1331720 | tf_op jit(solution)/shard_map/ppermute | solution.py:51
  45.0 6.6 %copy-start.12 = (bf16[34,32,192]{2,0,1:T(8,128)(2,1)S(1)}, bf16[34,32,192]{2,0,1:T(8,128)(2,1)}, u32[]{:S(2)}) copy-start(bf16[34,32,192]{2,0,1:T(8,128)(2,1)} %pad_maximum_fusion.4) | copy-start | bytes 1253380
  51.9 3.5 %copy-start.36 = (bf16[192,384]{1,0:T(8,128)(2,1)S(1)}, bf16[192,384]{1,0:T(8,128)(2,1)}, u32[]{:S(2)}) copy-start(bf16[192,384]{1,0:T(8,128)(2,1)} %get-tuple-element.81) | copy-start | bytes 442372
  52.0 3.5 %copy-start.37 = (bf16[192,384]{1,0:T(8,128)(2,1)S(1)}, bf16[192,384]{1,0:T(8,128)(2,1)}, u32[]{:S(2)}) copy-start(bf16[192,384]{1,0:T(8,128)(2,1)} %get-tuple-element.87) | copy-start | bytes 442372
  55.4 5.9 %copy-start.28 = (bf16[1024,384]{1,0:T(8,128)(2,1)}, bf16[1024,384]{1,0:T(8,128)(2,1)S(1)}, u32[]{:S(2)}) copy-start(bf16[1024,384]{1,0:T(8,128)(2,1)S(1)} %maximum_select_fusion) | copy-start | bytes 2359300
  74.0 7.3 %copy-start.27 = (bf16[1088,576]{1,0:T(8,128)(2,1)S(1)}, bf16[1088,576]{1,0:T(8,128)(2,1)}, u32[]{:S(2)}) copy-start(bf16[1088,576]{1,0:T(8,128)(2,1)} %pad_maximum_fusion.2) | copy-start | bytes 3760132
  74.0 7.3 %copy-start.29 = (bf16[1024,384]{1,0:T(8,128)(2,1)S(1)}, bf16[1024,384]{1,0:T(8,128)(2,1)}, u32[]{:S(2)}) copy-start(bf16[1024,384]{1,0:T(8,128)(2,1)} %copy-done.28) | copy-start | bytes 2359300
  75.9 12.2 %collective-permute-start.10 = (bf16[136,192]{1,0:T(8,128)(2,1)S(1)}, bf16[136,192]{1,0:T(8,128)(2,1)S(1)}, u32[]{:S(2)}, u32[]{:S(2)}) collective-permute-start(bf16[136,192]{1,0:T(8,128)(2,1)S(1)} %concatenate.149), channel_id=1, source_target_pairs={{0,24},{2,26},{4,28},{6,30},{8,0},{10,2},{12,4},{14,6},{16,8},{18,... | collective-permute-start | bytes 156680 | tf_op jit(solution)/shard_map/ppermute | solution.py:51
  78.3 9.9 %collective-permute-start.11 = (bf16[136,192]{1,0:T(8,128)(2,1)S(1)}, bf16[136,192]{1,0:T(8,128)(2,1)S(1)}, u32[]{:S(2)}, u32[]{:S(2)}) collective-permute-start(bf16[136,192]{1,0:T(8,128)(2,1)S(1)} %concatenate.149), channel_id=1, source_target_pairs={{0,26},{2,28},{4,30},{6,0},{8,2},{10,4},{12,6},{14,8},{16,10},{18,... | collective-permute-start | bytes 156680 | tf_op jit(solution)/shard_map/ppermute | solution.py:51
  79.0 9.4 %collective-permute-start.12 = (bf16[136,192]{1,0:T(8,128)(2,1)S(1)}, bf16[136,192]{1,0:T(8,128)(2,1)S(1)}, u32[]{:S(2)}, u32[]{:S(2)}) collective-permute-start(bf16[136,192]{1,0:T(8,128)(2,1)S(1)} %concatenate.149), channel_id=1, source_target_pairs={{0,28},{2,30},{4,0},{6,2},{8,4},{10,6},{12,8},{14,10},{16,12},{18,... | collective-permute-start | bytes 156680 | tf_op jit(solution)/shard_map/ppermute | solution.py:51
  79.5 11.5 %collective-permute-start.13 = (bf16[136,192]{1,0:T(8,128)(2,1)S(1)}, bf16[136,192]{1,0:T(8,128)(2,1)S(1)}, u32[]{:S(2)}, u32[]{:S(2)}) collective-permute-start(bf16[136,192]{1,0:T(8,128)(2,1)S(1)} %concatenate.149), channel_id=1, source_target_pairs={{0,30},{2,0},{4,2},{6,4},{8,6},{10,8},{12,10},{14,12},{16,14},{18,... | collective-permute-start | bytes 156680 | tf_op jit(solution)/shard_map/ppermute | solution.py:51
  84.1 3.9 %copy-start.4 = (f32[1792,384]{1,0:T(8,128)}, f32[1792,384]{1,0:T(8,128)S(1)}, u32[]{:S(2)}) copy-start(f32[1792,384]{1,0:T(8,128)S(1)} %maximum_multiply_fusion) | copy-start | bytes 8257540
  88.1 6.6 %collective-permute-start.14 = (bf16[136,192]{1,0:T(8,128)(2,1)S(1)}, bf16[136,192]{1,0:T(8,128)(2,1)S(1)}, u32[]{:S(2)}, u32[]{:S(2)}) collective-permute-start(bf16[136,192]{1,0:T(8,128)(2,1)S(1)} %concatenate.149), channel_id=1, source_target_pairs={{0,2},{2,4},{4,6},{6,8},{8,10},{10,12},{12,14},{14,16},{16,18},{18... | collective-permute-start | bytes 156680 | tf_op jit(solution)/shard_map/ppermute | solution.py:51
  88.1 7.8 %collective-permute-start.15 = (bf16[136,192]{1,0:T(8,128)(2,1)S(1)}, bf16[136,192]{1,0:T(8,128)(2,1)S(1)}, u32[]{:S(2)}, u32[]{:S(2)}) collective-permute-start(bf16[136,192]{1,0:T(8,128)(2,1)S(1)} %concatenate.149), channel_id=1, source_target_pairs={{0,4},{2,6},{4,8},{6,10},{8,12},{10,14},{12,16},{14,18},{16,20},{1... | collective-permute-start | bytes 156680 | tf_op jit(solution)/shard_map/ppermute | solution.py:51
  88.5 7.4 %collective-permute-start.16 = (bf16[136,192]{1,0:T(8,128)(2,1)S(1)}, bf16[136,192]{1,0:T(8,128)(2,1)S(1)}, u32[]{:S(2)}, u32[]{:S(2)}) collective-permute-start(bf16[136,192]{1,0:T(8,128)(2,1)S(1)} %concatenate.149), channel_id=1, source_target_pairs={{0,6},{2,8},{4,10},{6,12},{8,14},{10,16},{12,18},{14,20},{16,22},{... | collective-permute-start | bytes 156680 | tf_op jit(solution)/shard_map/ppermute | solution.py:51
  91.0 6.2 %collective-permute-start.17 = (bf16[136,192]{1,0:T(8,128)(2,1)S(1)}, bf16[136,192]{1,0:T(8,128)(2,1)S(1)}, u32[]{:S(2)}, u32[]{:S(2)}) collective-permute-start(bf16[136,192]{1,0:T(8,128)(2,1)S(1)} %concatenate.149), channel_id=1, source_target_pairs={{0,8},{2,10},{4,12},{6,14},{8,16},{10,18},{12,20},{14,22},{16,24},... | collective-permute-start | bytes 156680 | tf_op jit(solution)/shard_map/ppermute | solution.py:51
  94.6 80.0 %collective-permute-start.18 = (f32[896,384]{1,0:T(8,128)}, f32[896,384]{1,0:T(8,128)}, u32[]{:S(2)}, u32[]{:S(2)}) collective-permute-start(f32[896,384]{1,0:T(8,128)} %constant_dynamic-slice_fusion), channel_id=1, source_target_pairs={{0,2},{2,0},{4,6},{6,4},{8,10},{10,8},{12,14},{14,12},{16,18},{18,... | collective-permute-start | bytes 4128776 | tf_op jit(solution)/shard_map/ppermute | solution.py:51
  156.7 11.7 %copy-start.9 = (bf16[3,3,384,384]{3,2,1,0:T(8,128)(2,1)S(1)}, bf16[3,3,384,384]{3,2,1,0:T(8,128)(2,1)}, u32[]{:S(2)}) copy-start(bf16[3,3,384,384]{3,2,1,0:T(8,128)(2,1)} %param.20) | copy-start | bytes 7962628
  156.7 11.7 %copy-start.11 = (f32[1024,192]{0,1:T(8,128)S(1)}, f32[1024,192]{0,1:T(8,128)}, u32[]{:S(2)}) copy-start(f32[1024,192]{0,1:T(8,128)} %fusion.49) | copy-start | bytes 2359300
  176.1 12.9 %copy-start.23 = (bf16[32,32,192]{2,1,0:T(8,128)(2,1)S(1)}, bf16[32,32,192]{2,1,0:T(8,128)(2,1)}, u32[]{:S(2)}) copy-start(bf16[32,32,192]{2,1,0:T(8,128)(2,1)} %copy.280) | copy-start | bytes 1179652
  176.2 8.2 %collective-permute-start.21 = (bf16[224,384]{1,0:T(8,128)(2,1)S(1)}, bf16[224,384]{1,0:T(8,128)(2,1)S(1)}, u32[]{:S(2)}, u32[]{:S(2)}) collective-permute-start(bf16[224,384]{1,0:T(8,128)(2,1)S(1)} %get-tuple-element.91), channel_id=1, source_target_pairs={{0,12},{2,14},{4,8},{6,10},{8,4},{10,6},{12,0},{14,2},{16,28},{18,... | collective-permute-start | bytes 516104 | tf_op jit(solution)/shard_map/ppermute | solution.py:51
  177.3 9.9 %collective-permute-start.20 = (bf16[224,384]{1,0:T(8,128)(2,1)S(1)}, bf16[224,384]{1,0:T(8,128)(2,1)S(1)}, u32[]{:S(2)}, u32[]{:S(2)}) collective-permute-start(bf16[224,384]{1,0:T(8,128)(2,1)S(1)} %get-tuple-element.92), channel_id=1, source_target_pairs={{0,8},{2,10},{4,12},{6,14},{8,0},{10,2},{12,4},{14,6},{16,24},{18,... | collective-permute-start | bytes 516104 | tf_op jit(solution)/shard_map/ppermute | solution.py:51
  180.3 7.5 %collective-permute-start.19 = (bf16[224,384]{1,0:T(8,128)(2,1)S(1)}, bf16[224,384]{1,0:T(8,128)(2,1)S(1)}, u32[]{:S(2)}, u32[]{:S(2)}) collective-permute-start(bf16[224,384]{1,0:T(8,128)(2,1)S(1)} %get-tuple-element.90), channel_id=1, source_target_pairs={{0,4},{2,6},{4,0},{6,2},{8,12},{10,14},{12,8},{14,10},{16,20},{18,... | collective-permute-start | bytes 516104 | tf_op jit(solution)/shard_map/ppermute | solution.py:51
  187.9 13.2 %copy-start.17 = (bf16[32,32,192]{2,1,0:T(8,128)(2,1)S(1)}, bf16[32,32,192]{2,1,0:T(8,128)(2,1)}, u32[]{:S(2)}) copy-start(bf16[32,32,192]{2,1,0:T(8,128)(2,1)} %copy.282) | copy-start | bytes 1179652
  187.9 6.3 %collective-permute-start.22 = (bf16[112,384]{1,0:T(8,128)(2,1)S(1)}, bf16[112,384]{1,0:T(8,128)(2,1)S(1)}, u32[]{:S(2)}, u32[]{:S(2)}) collective-permute-start(bf16[112,384]{1,0:T(8,128)(2,1)S(1)} %dynamic-slice_convert_fusion.3), channel_id=1, source_target_pairs={{0,16},{2,18},{4,20},{6,22},{8,24},{10,26},{12,28},{14,30},{16,0},... | collective-permute-start | bytes 258056 | tf_op jit(solution)/shard_map/ppermute | solution.py:51
  194.3 6.0 %collective-permute-start.23 = (bf16[112,384]{1,0:T(8,128)(2,1)S(1)}, bf16[112,384]{1,0:T(8,128)(2,1)S(1)}, u32[]{:S(2)}, u32[]{:S(2)}) collective-permute-start(bf16[112,384]{1,0:T(8,128)(2,1)S(1)} %get-tuple-element.78), channel_id=1, source_target_pairs={{0,16},{2,18},{4,20},{6,22},{8,24},{10,26},{12,28},{14,30},{16,0},... | collective-permute-start | bytes 258056 | tf_op jit(solution)/shard_map/ppermute | solution.py:51
  195.1 16.9 %copy-start.15 = (bf16[32,32,192]{2,1,0:T(8,128)(2,1)S(1)}, bf16[32,32,192]{2,1,0:T(8,128)(2,1)}, u32[]{:S(2)}) copy-start(bf16[32,32,192]{2,1,0:T(8,128)(2,1)} %get-tuple-element.113) | copy-start | bytes 1179652
  200.4 6.1 %collective-permute-start.24 = (bf16[224,384]{1,0:T(8,128)(2,1)S(1)}, bf16[224,384]{1,0:T(8,128)(2,1)S(1)}, u32[]{:S(2)}, u32[]{:S(2)}) collective-permute-start(bf16[224,384]{1,0:T(8,128)(2,1)S(1)} %constant_dynamic-update-slice_fusion.22), channel_id=1, source_target_pairs={{0,4},{2,6},{4,0},{6,2},{8,12},{10,14},{12,8},{14,10},{16,20},{18,... | collective-permute-start | bytes 516104 | tf_op jit(solution)/shard_map/ppermute | solution.py:51
  201.6 11.0 %copy-start.22 = (bf16[32,32,192]{2,1,0:T(8,128)(2,1)S(1)}, bf16[32,32,192]{2,1,0:T(8,128)(2,1)}, u32[]{:S(2)}) copy-start(bf16[32,32,192]{2,1,0:T(8,128)(2,1)} %copy.283) | copy-start | bytes 1179652
  201.6 7.4 %collective-permute-start.25 = (bf16[224,384]{1,0:T(8,128)(2,1)S(1)}, bf16[224,384]{1,0:T(8,128)(2,1)S(1)}, u32[]{:S(2)}, u32[]{:S(2)}) collective-permute-start(bf16[224,384]{1,0:T(8,128)(2,1)S(1)} %constant_dynamic-update-slice_fusion.22), channel_id=1, source_target_pairs={{0,8},{2,10},{4,12},{6,14},{8,0},{10,2},{12,4},{14,6},{16,24},{18,... | collective-permute-start | bytes 516104 | tf_op jit(solution)/shard_map/ppermute | solution.py:51
  201.6 10.3 %collective-permute-start.26 = (bf16[224,384]{1,0:T(8,128)(2,1)S(1)}, bf16[224,384]{1,0:T(8,128)(2,1)S(1)}, u32[]{:S(2)}, u32[]{:S(2)}) collective-permute-start(bf16[224,384]{1,0:T(8,128)(2,1)S(1)} %constant_dynamic-update-slice_fusion.22), channel_id=1, source_target_pairs={{0,12},{2,14},{4,8},{6,10},{8,4},{10,6},{12,0},{14,2},{16,28},{18,... | collective-permute-start | bytes 516104 | tf_op jit(solution)/shard_map/ppermute | solution.py:51
  211.9 4.5 %collective-permute-start.27 = (bf16[896,384]{1,0:T(8,128)(2,1)S(1)}, bf16[896,384]{1,0:T(8,128)(2,1)}, u32[]{:S(2)}, u32[]{:S(2)}) collective-permute-start(bf16[896,384]{1,0:T(8,128)(2,1)S(1)} %constant_dynamic-update-slice_fusion.18), channel_id=1, source_target_pairs={{0,2},{2,0},{4,6},{6,4},{8,10},{10,8},{12,14},{14,12},{16,18},{18,... | collective-permute-start | bytes 2064392 | tf_op jit(solution)/shard_map/ppermute | solution.py:51
  (22 other events, 39.3 us)

commit v2 on v0

v2 whole, which is shorter than its diff:
```python
import functools
import math

import jax
import jax.numpy as jnp
import numpy as np
from jax import lax
from jax.experimental import pallas as pl
from jax.experimental.pallas import tpu as pltpu
from jax.sharding import PartitionSpec as P

SPAN = 4
OFFSETS = list(range(-SPAN, 0)) + list(range(1, SPAN + 1))
EXTRA = 16


def turn_tables():
    labels = [[3 * row + col for col in range(3)] for row in range(3)]

    def turn_once(block):
        return [[block[col][2 - row] for col in range(3)] for row in range(3)]

    def sides_of(block):
        return [
            list(block[0]),
            [block[row][2] for row in range(3)],
            list(block[2]),
            [block[row][0] for row in range(3)],
        ]

    def corners_of(block):
        return [block[0][0], block[0][2], block[2][2], block[2][0]]

    base_sides = sides_of(labels)
    base_corners = corners_of(labels)
    edge_table = np.zeros((4, 4), np.int32)
    corner_table = np.zeros((4, 4), np.int32)
    for border in range(4):
        turned = labels
        for quarter in range(4):
            wanted = sides_of(turned)[(border + 2) % 4]
            for side_index in range(4):
                if base_sides[side_index] == wanted:
                    edge_table[border, quarter] = side_index
                if base_sides[side_index][::-1] == wanted:
                    edge_table[border, quarter] = side_index + 4
            corner_cell = corners_of(turned)[(border + 2) % 4]
            for corner_index in range(4):
                if base_corners[corner_index] == corner_cell:
                    corner_table[border, quarter] = corner_index
            turned = turn_once(turned)
    return np.concatenate([edge_table, corner_table], axis=0)


def by_offset(value, offset, count):
    return lax.ppermute(value, "tile", [(i, (i + offset) % count) for i in range(count)])


def by_mask(value, mask, count):
    return lax.ppermute(value, "tile", [(i, i ^ mask) for i in range(count)])


def mask_stages(count):
    bits = [1 << b for b in range(count.bit_length() - 1)]
    stages = [bits[:1]]
    rest = bits[1:]
    while rest:
        stages.append(rest[:2])
        rest = rest[2:]
    return stages


def group_masks(bits):
    masks = [0]
    for bit in bits:
        masks = masks + [m + bit for m in masks]
    return masks


def slot_of_mask(mask, count):
    place = 0
    for bits in mask_stages(count):
        size = 1 << len(bits)
        place = place * size + (mask // bits[0]) % size
    return place


def corner_spot(slot, side):
    return jnp.where(
        slot == 0, 0, jnp.where(slot == 1, side - 1, jnp.where(slot == 2, 3 * side - 1, 2 * side))
    )


def vmem(shape, dtype):
    return jax.ShapeDtypeStruct(shape, dtype)


def call(kernel, outs, args, smem=(), scratch=(), flops=0):
    in_specs = [
        pl.BlockSpec(memory_space=pltpu.SMEM if i in smem else pltpu.VMEM) for i in range(len(args))
    ]
    size = sum(math.prod(x.shape) * x.dtype.itemsize for x in list(args) + list(outs))
    return pl.pallas_call(
        kernel,
        out_shape=tuple(outs),
        in_specs=in_specs,
        out_specs=tuple(pl.BlockSpec(memory_space=pltpu.VMEM) for _ in outs),
        scratch_shapes=list(scratch),
        compiler_params=pltpu.CompilerParams(vmem_limit_bytes=40 * 1024 * 1024),
        cost_estimate=pl.CostEstimate(flops=flops, bytes_accessed=size, transcendentals=0),
    )(*args)


def sides_kernel(side, field_ref, sides_ref):
    sides_ref[0:side, :] = field_ref[0]
    sides_ref[side : 2 * side, :] = field_ref[:, side - 1, :]
    sides_ref[2 * side : 3 * side, :] = field_ref[side - 1]
    sides_ref[3 * side : 4 * side, :] = field_ref[:, 0, :]


def shifted_columns(side, part, field_ref, halos, out_ref):
    rows = side * side
    flat = rows + 2 * side
    tall = jnp.concatenate(
        [
            halos[0:side].astype(jnp.float32),
            field_ref[...].reshape(rows, part).astype(jnp.float32),
            halos[2 * side : 3 * side].astype(jnp.float32),
        ],
        axis=0,
    )
    edge = halos.astype(jnp.float32)
    corner = [edge[4 * side + c : 4 * side + c + 1] for c in range(4)]
    east = jnp.concatenate([corner[1], edge[side : 2 * side], corner[2]], axis=0)
    west = jnp.concatenate([corner[0], edge[3 * side : 4 * side], corner[3]], axis=0)
    spread = lambda col: jnp.broadcast_to(col[:, None, :], (side + 2, side, part)).reshape(flat, part)
    column = lax.broadcasted_iota(jnp.int32, (flat, part), 0) % side
    out_ref[0] = jnp.where(column == 0, spread(west), pltpu.roll(tall, 1, 0)).astype(jnp.bfloat16)
    out_ref[1] = tall.astype(jnp.bfloat16)
    out_ref[2] = jnp.where(column == side - 1, spread(east), pltpu.roll(tall, flat - 1, 0)).astype(
        jnp.bfloat16
    )


def halo_kernel(side, part, tables_ref, et_ref, eu_ref, ct_ref, cu_ref, *refs):
    near_refs, halos_ref = refs[: len(OFFSETS)], refs[len(OFFSETS)]
    count = lax.axis_size("tile")
    own = lax.axis_index("tile")

    def base(target):
        wrapped = lax.rem(target - own + count, count)
        signed = jnp.where(wrapped > count // 2, wrapped - count, wrapped)
        return jnp.where(signed < 0, signed + SPAN, signed + SPAN - 1) * (4 * side)

    row = lax.broadcasted_iota(jnp.int32, (4 * side + EXTRA, 1), 0)
    wanted = jnp.full((4 * side + EXTRA, 1), -1, jnp.int32)
    for e in range(4):
        slot = tables_ref[e, eu_ref[own, e]]
        start = base(et_ref[own, e]) + lax.rem(slot, 4) * side
        along = row - e * side
        along = jnp.where(slot >= 4, side - 1 - along, along)
        wanted = jnp.where((row >= e * side) & (row < (e + 1) * side), start + along, wanted)
        corner = tables_ref[4 + e, cu_ref[own, e]]
        spot = base(ct_ref[own, e]) + corner_spot(corner, side)
        wanted = jnp.where(row == 4 * side + e, spot, wanted)
    near = jnp.concatenate([ref[...] for ref in near_refs], axis=0)
    lane = lax.broadcasted_iota(jnp.int32, (4 * side + EXTRA, near.shape[0]), 1)
    pick = jnp.where(lane == wanted, 1.0, 0.0).astype(jnp.bfloat16)
    halos_ref[...] = jnp.dot(pick, near, preferred_element_type=jnp.float32).astype(jnp.bfloat16)


def grad_weight_kernel(side, part, chunk, scale, field_ref, halos_ref, cot_ref, out_ref, cols, total):
    rows = side * side
    chans = cot_ref.shape[1]
    count = lax.axis_size("tile")
    own = lax.axis_index("tile")
    shifted_columns(side, part, field_ref, halos_ref[...], cols)
    cot = cot_ref[...]
    for a in range(3):
        for b in range(3):
            tap = 3 * a + b
            total[tap * part : (tap + 1) * part, :] = (
                lax.dot_general(
                    cols[b, a * side : a * side + rows, :],
                    cot,
                    (((0,), (0,)), ((), ())),
                    preferred_element_type=jnp.float32,
                )
                * scale
            )
    total[9 * part :, :] = jnp.zeros((chunk * count - 9 * part, chans), jnp.float32)
    for mask in range(count):
        to = slot_of_mask(mask, count) * chunk
        start = pl.multiple_of((own ^ mask) * chunk, 16)
        out_ref[to : to + chunk, :] = total[pl.ds(start, chunk), :]


def unfold_kernel(part, chunk, mine_ref, other_ref, out_ref):
    count = lax.axis_size("tile")
    own = lax.axis_index("tile")
    half = mine_ref.shape[0] // chunk
    whole = 9 * part
    core = lax.rem(own, 2)
    for block in range(count):
        size = min(chunk, whole - block * chunk)
        if size <= 0:
            continue
        mask = own ^ block
        place = 0
        for bits in mask_stages(count)[1:]:
            span = 1 << len(bits)
            place = place * span + lax.rem(mask // bits[0], span)
        start = pl.multiple_of(place * chunk, 16)
        mine = mine_ref[pl.ds(start, size), :]
        other = other_ref[pl.ds(start, size), :]
        value = jnp.where(core == block % 2, mine.astype(jnp.float32), other.astype(jnp.float32))
        out_ref[block * chunk : block * chunk + size, :] = value


def both_kernel(own_ref, other_ref, out_ref):
    part = own_ref.shape[1]

    @pl.when(lax.axis_index("ch") == 0)
    def _():
        out_ref[:, 0:part] = own_ref[...]
        out_ref[:, part:] = other_ref[...]

    @pl.when(lax.axis_index("ch") != 0)
    def _():
        out_ref[:, 0:part] = other_ref[...]
        out_ref[:, part:] = own_ref[...]


def back_kernel(side, part, cot_ref, weight_ref, inner_ref, pieces_ref, tall):
    rows = side * side
    flat = rows + 2 * side
    start = pl.multiple_of(lax.axis_index("ch") * part, 16)
    chans = cot_ref.shape[1]
    blank = jnp.zeros((2 * side, chans), jnp.bfloat16)
    tall[0 : 2 * side, :] = blank
    tall[2 * side : 2 * side + rows, :] = cot_ref[...]
    tall[2 * side + rows :, :] = blank
    backs = []
    for b in range(3):
        back = jnp.zeros((flat, part), jnp.float32)
        for a in range(3):
            back = back + lax.dot_general(
                tall[(2 - a) * side : (2 - a) * side + flat, :],
                weight_ref[3 * a + b, pl.ds(start, part), :],
                (((1,), (1,)), ((), ())),
                preferred_element_type=jnp.float32,
            )
        backs.append(back)
    column = lax.broadcasted_iota(jnp.int32, (flat, part), 0) % side
    inner = (
        jnp.where(column == side - 1, 0.0, pltpu.roll(backs[0], flat - 1, 0))
        + backs[1]
        + jnp.where(column == 0, 0.0, pltpu.roll(backs[2], 1, 0))
    )
    inner_ref[...] = inner[side : side + rows]
    west = backs[0].reshape(side + 2, side, part)[:, 0, :]
    east = backs[2].reshape(side + 2, side, part)[:, side - 1, :]
    pieces_ref[...] = jnp.concatenate(
        [
            inner[0:side],
            east[1 : side + 1],
            inner[side + rows :],
            west[1 : side + 1],
            west[0:1],
            east[0:1],
            east[side + 1 :],
            west[side + 1 :],
            jnp.zeros((EXTRA - 4, part), jnp.float32),
        ],
        axis=0,
    ).astype(jnp.bfloat16)


def add_halo_kernel(side, part, tables_ref, et_ref, eu_ref, ct_ref, cu_ref, inner_ref, *refs):
    got_refs, out_ref = refs[: len(OFFSETS)], refs[len(OFFSETS)]
    count = lax.axis_size("tile")
    own = lax.axis_index("tile")
    block = 4 * side + EXTRA
    total = len(OFFSETS) * block
    lane = lax.broadcasted_iota(jnp.int32, (1, total), 1)
    target = jnp.full((1, total), -1, jnp.int32)
    for index, offset in enumerate(OFFSETS):
        source = lax.rem(own - offset + count, count)
        for e in range(4):
            first = index * block + e * side
            slot = tables_ref[e, eu_ref[source, e]]
            along = lane - first
            along = jnp.where(slot >= 4, side - 1 - along, along)
            hit = (lane >= first) & (lane < first + side) & (et_ref[source, e] == own)
            target = jnp.where(hit, lax.rem(slot, 4) * side + along, target)
            spot = corner_spot(tables_ref[4 + e, cu_ref[source, e]], side)
            hit = (lane == index * block + 4 * side + e) & (ct_ref[source, e] == own)
            target = jnp.where(hit, spot, target)
    row = lax.broadcasted_iota(jnp.int32, (4 * side, total), 0)
    place = jnp.where(row == target, 1.0, 0.0).astype(jnp.bfloat16)
    got = jnp.concatenate([ref[...] for ref in got_refs], axis=0)
    sums = jnp.dot(place, got, preferred_element_type=jnp.float32)
    rows = side * side
    spread = lambda col: jnp.broadcast_to(col[:, None, :], (side, side, part)).reshape(rows, part)
    column = lax.broadcasted_iota(jnp.int32, (rows, part), 0) % side
    inner = inner_ref[...]
    inner = inner + jnp.where(column == side - 1, spread(sums[side : 2 * side]), 0.0)
    inner = inner + jnp.where(column == 0, spread(sums[3 * side :]), 0.0)
    ends = jnp.concatenate(
        [
            inner[0:side] + sums[0:side],
            inner[side : rows - side],
            inner[rows - side :] + sums[2 * side : 3 * side],
        ],
        axis=0,
    )
    out_ref[...] = ends.astype(jnp.bfloat16)


def output_kernel(side, part, field_ref, halos_ref, other_ref, weight_ref, out_ref, cols, other_cols):
    rows = side * side
    ch = lax.axis_index("ch")
    start = pl.multiple_of(ch * part, 16)
    other = pl.multiple_of((1 - ch) * part, 16)
    chans = weight_ref.shape[2]
    wide = -(-part // 128) * 128
    lanes = pl.multiple_of(ch * (chans - wide), 128)
    shifted_columns(side, part, field_ref, halos_ref[...], cols)
    shifted_columns(side, part, other_ref.at[0:rows], other_ref[rows:, :], other_cols)
    total = jnp.zeros((rows, wide), jnp.float32)
    for a in range(3):
        for b in range(3):
            for ref, first in ((cols, start), (other_cols, other)):
                total = total + jnp.dot(
                    ref[b, a * side : a * side + rows, :],
                    weight_ref[3 * a + b, pl.ds(first, part), pl.ds(lanes, wide)],
                    preferred_element_type=jnp.float32,
                )
    result = jnp.where(ch == 0, total[:, :part], total[:, wide - part :])
    out_ref[...] = result.astype(jnp.bfloat16)


def sum_over_tiles(partial, own_tile, count):
    stages = mask_stages(count)
    held = partial
    for index, bits in enumerate(stages):
        masks = group_masks(bits)
        part = held.shape[0] // len(masks)
        kind = jnp.float32 if index == 0 else jnp.bfloat16
        pieces = [held[i * part : (i + 1) * part] for i in range(len(masks))]
        got = [by_mask(p.astype(kind), m, count) for p, m in zip(pieces[1:], masks[1:])]
        held = pieces[0]
        for value in got:
            held = held + value.astype(jnp.float32)
    held = held.astype(jnp.bfloat16)
    for bits in stages[:0:-1]:
        masks = group_masks(bits)
        held = jnp.concatenate([held] + [by_mask(held, m, count) for m in masks[1:]], axis=0)
    return held, by_mask(held, 1, count)


def body(features, weight, cotangent, edge_tiles, edge_turns, corner_tiles, corner_turns):
    tables = jnp.asarray(turn_tables())
    count = lax.axis_size("tile")
    own_tile = lax.axis_index("tile")
    field = features[0]
    side, part = field.shape[0], field.shape[2]
    chans = weight.shape[3]
    rows = side * side
    flat = rows + 2 * side
    taps = weight.reshape(9, chans, chans)
    others = [(0, 1), (1, 0)]
    smalls = (tables, edge_tiles, edge_turns, corner_tiles, corner_turns)

    cot_own = cotangent[0].reshape(rows, part)
    cot_other = lax.ppermute(cot_own, "ch", others)
    (sides,) = call(functools.partial(sides_kernel, side), [vmem((4 * side, part), jnp.bfloat16)], [field])
    near = [by_offset(sides, -offset, count) for offset in OFFSETS]
    (cot_full,) = call(both_kernel, [vmem((rows, chans), jnp.bfloat16)], [cot_own, cot_other])

    (halos,) = call(
        functools.partial(halo_kernel, side, part),
        [vmem((4 * side + EXTRA, part), jnp.bfloat16)],
        [*smalls, *near],
        smem=range(5),
    )
    chunk = -(-9 * part // (16 * count)) * 16
    (local,) = call(
        functools.partial(grad_weight_kernel, side, part, chunk, 1.0 / math.sqrt(count * rows)),
        [vmem((chunk * count, chans), jnp.float32)],
        [field, halos, cot_full],
        scratch=[
            pltpu.VMEM((3, flat, part), jnp.bfloat16),
            pltpu.VMEM((chunk * count, chans), jnp.float32),
        ],
        flops=2 * rows * 9 * part * chans,
    )
    mine, other = sum_over_tiles(local, own_tile, count)
    (grad_weight,) = call(
        functools.partial(unfold_kernel, part, chunk),
        [vmem((9 * part, chans), jnp.float32)],
        [mine, other],
    )

    inner, pieces = call(
        functools.partial(back_kernel, side, part),
        [vmem((rows, part), jnp.float32), vmem((4 * side + EXTRA, part), jnp.bfloat16)],
        [cot_full, taps],
        scratch=[pltpu.VMEM((rows + 4 * side, chans), jnp.bfloat16)],
        flops=2 * rows * 9 * part * chans,
    )
    got = [by_offset(pieces, offset, count) for offset in OFFSETS]
    (grad_features,) = call(
        functools.partial(add_halo_kernel, side, part),
        [vmem((rows, part), jnp.bfloat16)],
        [*smalls, inner, *got],
        smem=range(5),
    )

    packet = jnp.concatenate([field.reshape(rows, part), halos], axis=0)
    (output,) = call(
        functools.partial(output_kernel, side, part),
        [vmem((rows, part), jnp.bfloat16)],
        [field, halos, lax.ppermute(packet, "ch", others), taps],
        scratch=[pltpu.VMEM((3, flat, part), jnp.bfloat16)] * 2,
        flops=2 * rows * 9 * part * chans,
    )
    shape = (1, side, side, part)
    return (
        output.reshape(shape),
        grad_features.reshape(shape),
        grad_weight.reshape(3, 3, part, chans),
    )


def solution(mesh):
    return jax.shard_map(
        body,
        mesh=mesh,
        in_specs=(
            P("tile", None, None, "ch"),
            P(),
            P("tile", None, None, "ch"),
            P(),
            P(),
            P(),
            P(),
        ),
        out_specs=(
            P("tile", None, None, "ch"),
            P("tile", None, None, "ch"),
            P(None, None, "ch", None),
        ),
        check_vma=False,
    )
```

time: 410 us -> 98.8 us (0.24)
  local copies, waits for them, and re-layouts: 110 us -> 9.76 us
  waiting for transfers between devices: 126 us -> 40.1 us
  matrix products: 38.7 us -> 0 us
  blocking collectives: 38 us -> 0 us
  other arithmetic: 34.1 us -> 0.43 us
  between operations: 16.8 us -> 0.82 us
  Pallas kernels: 0 us -> 14.8 us
  starting transfers between devices: 44.9 us -> 32.5 us
    psum x1 -> x0, waiting for transfers between devices: 79.3 us -> none  [body(): lax.psum(local_grad, 'tile') * (1.0 / math.sqrt(tile_count * rows))]
    scatter-add x16 -> x0, local copies, waits for them, and re-layouts: 41 us -> none  [the longest x9 39.4 us: body(): grad_padded = grad_padded.at[row_off:row_off + side_len, col_off:col_off...]
    dot_general x43 -> x0, matrix products: 38.7 us -> none  [the longest x9 14.9 us: body(): jnp.dot(windows[tap_index], blocks[tap_index], preferred_element_type=jnp...]
    all_gather x1 -> x0, blocking collectives: 38 us -> none  [body(): lax.all_gather(cotangent[0], 'ch', axis=2, tiled=True)]
    gather x20 -> x0, local copies, waits for them, and re-layouts: 18 us -> none  [the longest x8 9.33 us: body(): src_slots = jnp.asarray(edge_table)[border_ids, edge_turns[source]]]
    add x13 -> x1, other arithmetic: 15.7 us -> 0.08 us  [sum_over_tiles(): held = held + value.astype(jnp.float32)]
    pallas_call x0 -> x8, Pallas kernels: none -> 14.8 us  [call(): pl.pallas_call(kernel, out_shape=tuple(outs), in_specs=in_specs, out_spec...]
    ppermute x32 -> x28, starting transfers between devices: 44.8 us -> 32.5 us  [the longest x16 19.1 us: by_offset(): lax.ppermute(value, 'tile', [(i, (i + offset) % count) for i in range(cou...]
  transfers between devices with their start and end apart: 34 -> 28, of which waited for: 17 -> 18; matrix products, arithmetic and copies ran while one was open for 43% -> 5% of each run, Pallas kernels for 0% -> 11%
where the time goes in v2:
time: 98.8 us; the launch traced here: 98.5 us
  waiting for transfers between devices  40.1 us (41%)
  starting transfers between devices  32.5 us (33%)
  Pallas kernels  14.8 us (15%)
  local copies, waits for them, and re-layouts  9.76 us (10%)
    ppermute x10, waiting for transfers between devices, by_mask(): return lax.ppermute(value, 'tile', [(i, i ^ mask) for i in range(count)])  25.9 us
    ppermute x16, starting transfers between devices, by_offset(): lax.ppermute(value, 'tile', [(i, (i + offset) % count) for i in range(cou...  19.1 us
    pallas_call x8, Pallas kernels, call(): pl.pallas_call(kernel, out_shape=tuple(outs), in_specs=in_specs, out_spec...  14.8 us
    ppermute x16, waiting for transfers between devices, by_offset(): lax.ppermute(value, 'tile', [(i, (i + offset) % count) for i in range(cou...  14.2 us
    ppermute x10, starting transfers between devices, by_mask(): return lax.ppermute(value, 'tile', [(i, i ^ mask) for i in range(count)])  9.88 us
    unnamed x21, local copies, waits for them, and re-layouts  8.34 us
    ppermute x1, starting transfers between devices, body(): cot_other = lax.ppermute(cot_own, 'ch', others)  3 us
  transfers between devices with their start and end apart: 28, of which 18 were waited for; matrix products, arithmetic and copies ran while one was open for 5% of the time, Pallas kernels for 11%

profile of v2, /device:TPU:0, one launch (start us, length us, event | category | flops | bytes accessed | tf_op | source)
XLA Modules:
  0.0 98.5 jit_solution(5204797578285079037)
XLA Ops:
  0.6 3.0 %collective-permute-start.9 = (bf16[1024,192]{1,0:T(8,128)(2,1)}, bf16[1024,192]{1,0:T(8,128)(2,1)S(1)}, u32[]{:S(2)}, u32[]{:S(2)}) collective-permute-start(bf16[1024,192]{1,0:T(8,128)(2,1)} %bitcast.11), channel_id=1, source_target_pairs={{0,1},{1,0},{2,3},{3,2},{4,5},{5,4},{6,7},{7,6},{8,9},{9,8},{10,11... | collective-permute-start | bytes 1179656 | tf_op jit(solution)/shard_map/ppermute | solution.py:376
  3.6 1.0 %copy-done = bf16[1,32,32,192]{3,2,1,0:T(8,128)(2,1)S(1)} copy-done((bf16[1,32,32,192]{3,2,1,0:T(8,128)(2,1)S(1)}, bf16[1,32,32,192]{3,2,1,0:T(8,128)(2,1)}, u32[]{:S(2)}) %copy-start) | copy-done | bytes 393240
  4.7 1.6 %collective-permute-start = (bf16[128,192]{1,0:T(8,128)(2,1)S(1)}, bf16[128,192]{1,0:T(8,128)(2,1)S(1)}, u32[]{:S(2)}, u32[]{:S(2)}) collective-permute-start(bf16[128,192]{1,0:T(8,128)(2,1)S(1)} %shard_map.103), channel_id=1, source_target_pairs={{0,8},{2,10},{4,12},{6,14},{8,16},{10,18},{12,20},{14,22},{16,24},... | collective-permute-start | bytes 147464 | tf_op jit(solution)/shard_map/ppermute | solution.py:56
  6.8 1.5 %collective-permute-start.2 = (bf16[128,192]{1,0:T(8,128)(2,1)S(1)}, bf16[128,192]{1,0:T(8,128)(2,1)S(1)}, u32[]{:S(2)}, u32[]{:S(2)}) collective-permute-start(bf16[128,192]{1,0:T(8,128)(2,1)S(1)} %shard_map.103), channel_id=1, source_target_pairs={{0,4},{2,6},{4,8},{6,10},{8,12},{10,14},{12,16},{14,18},{16,20},{1... | collective-permute-start | bytes 147464 | tf_op jit(solution)/shard_map/ppermute | solution.py:56
  8.3 1.0 %collective-permute-start.3 = (bf16[128,192]{1,0:T(8,128)(2,1)S(1)}, bf16[128,192]{1,0:T(8,128)(2,1)S(1)}, u32[]{:S(2)}, u32[]{:S(2)}) collective-permute-start(bf16[128,192]{1,0:T(8,128)(2,1)S(1)} %shard_map.103), channel_id=1, source_target_pairs={{0,2},{2,4},{4,6},{6,8},{8,10},{10,12},{12,14},{14,16},{16,18},{18... | collective-permute-start | bytes 147464 | tf_op jit(solution)/shard_map/ppermute | solution.py:56
  9.3 1.6 %collective-permute-done.refs_0_ = bf16[128,192]{1,0:T(8,128)(2,1)S(1)} collective-permute-done((bf16[128,192]{1,0:T(8,128)(2,1)S(1)}, bf16[128,192]{1,0:T(8,128)(2,1)S(1)}, u32[]{:S(2)}, u32[]{:S(2)}) %collective-permute-start) | collective-permute-done | bytes 49184 | tf_op jit(solution)/shard_map/ppermute | solution.py:56
  10.9 1.9 %collective-permute-start.4 = (bf16[128,192]{1,0:T(8,128)(2,1)S(1)}, bf16[128,192]{1,0:T(8,128)(2,1)S(1)}, u32[]{:S(2)}, u32[]{:S(2)}) collective-permute-start(bf16[128,192]{1,0:T(8,128)(2,1)S(1)} %shard_map.103), channel_id=1, source_target_pairs={{0,30},{2,0},{4,2},{6,4},{8,6},{10,8},{12,10},{14,12},{16,14},{18,... | collective-permute-start | bytes 147464 | tf_op jit(solution)/shard_map/ppermute | solution.py:56
  12.7 1.4 %collective-permute-start.5 = (bf16[128,192]{1,0:T(8,128)(2,1)S(1)}, bf16[128,192]{1,0:T(8,128)(2,1)S(1)}, u32[]{:S(2)}, u32[]{:S(2)}) collective-permute-start(bf16[128,192]{1,0:T(8,128)(2,1)S(1)} %shard_map.103), channel_id=1, source_target_pairs={{0,28},{2,30},{4,0},{6,2},{8,4},{10,6},{12,8},{14,10},{16,12},{18,... | collective-permute-start | bytes 147464 | tf_op jit(solution)/shard_map/ppermute | solution.py:56
  14.5 0.8 collective-permute-start.6
  15.4 1.4 %collective-permute-start.7 = (bf16[128,192]{1,0:T(8,128)(2,1)S(1)}, bf16[128,192]{1,0:T(8,128)(2,1)S(1)}, u32[]{:S(2)}, u32[]{:S(2)}) collective-permute-start(bf16[128,192]{1,0:T(8,128)(2,1)S(1)} %shard_map.103), channel_id=1, source_target_pairs={{0,24},{2,26},{4,28},{6,30},{8,0},{10,2},{12,4},{14,6},{16,8},{18,... | collective-permute-start | bytes 147464 | tf_op jit(solution)/shard_map/ppermute | solution.py:56
  16.8 0.8 copy.30.et_ref
  17.6 0.8 copy.31.eu_ref
  18.4 0.8 copy.32.ct_ref
  19.1 0.8 copy.33.cu_ref
  19.9 0.6 collective-permute-done.7.refs_7_
  20.5 0.7 copy-done.3
  21.2 1.4 %shard_map.104.halos_ref = bf16[144,192]{1,0:T(8,128)(2,1)S(1)} custom-call(s32[8,4]{1,0:T(8,128)S(1)} %copy-done.3, s32[16,4]{1,0:T(8,128)S(1)} %copy.30.et_ref, s32[16,4]{1,0:T(8,128)S(1)} %copy.31.eu_ref, s32[16,4]{1,0:T(8,128)S(1)} %copy.32.ct_ref, s32[16,4]{1,0:T(8,128)S(1)} %copy.33.cu_ref, bf16[128,192]{1,0:T(8,128)(2,1)S(1)} %collective-permute-done.refs_0_, ...), custom_call_target="tpu_custom_call" | custom-call | bytes 449664 | tf_op jit(solution)/shard_map/pallas_call | solution.py:103
  22.8 2.5 %shard_map.109 = f32[1792,384]{1,0:T(8,128)S(1)} custom-call(bf16[32,32,192]{2,1,0:T(8,128)(2,1)S(1)} %bitcast.8, bf16[144,192]{1,0:T(8,128)(2,1)S(1)} %shard_map.104.halos_ref, bf16[1024,384]{1,0:T(8,128)(2,1)S(1)} %shard_map.106.cot_ref), custom_call_target="tpu_custom_call" | custom-call | flops 1358954496 | bytes 3987456 | tf_op jit(solution)/shard_map/pallas_call | solution.py:103
  25.5 3.1 %collective-permute-done.18 = f32[896,384]{1,0:T(8,128)S(1)} collective-permute-done((f32[896,384]{1,0:T(8,128)S(1)}, f32[896,384]{1,0:T(8,128)S(1)}, u32[]{:S(2)}, u32[]{:S(2)}) %collective-permute-start.18) | collective-permute-done | bytes 1376288 | tf_op jit(solution)/shard_map/ppermute | solution.py:60
  28.9 1.0 collective-permute-start.19
  29.8 0.7 collective-permute-start.20
  30.6 1.9 %collective-permute-start.21 = (bf16[224,384]{1,0:T(8,128)(2,1)S(1)}, bf16[224,384]{1,0:T(8,128)(2,1)S(1)}, u32[]{:S(2)}, u32[]{:S(2)}) collective-permute-start(bf16[224,384]{1,0:T(8,128)(2,1)S(1)} %get-tuple-element.12), channel_id=1, source_target_pairs={{0,12},{2,14},{4,8},{6,10},{8,4},{10,6},{12,0},{14,2},{16,28},{18,... | collective-permute-start | bytes 516104 | tf_op jit(solution)/shard_map/ppermute | solution.py:60
  32.4 2.9 %collective-permute-done.19 = bf16[224,384]{1,0:T(8,128)(2,1)S(1)} collective-permute-done((bf16[224,384]{1,0:T(8,128)(2,1)S(1)}, bf16[224,384]{1,0:T(8,128)(2,1)S(1)}, u32[]{:S(2)}, u32[]{:S(2)}) %collective-permute-start.19) | collective-permute-done | bytes 172064 | tf_op jit(solution)/shard_map/ppermute | solution.py:60
  35.4 1.7 %collective-permute-done.20 = bf16[224,384]{1,0:T(8,128)(2,1)S(1)} collective-permute-done((bf16[224,384]{1,0:T(8,128)(2,1)S(1)}, bf16[224,384]{1,0:T(8,128)(2,1)S(1)}, u32[]{:S(2)}, u32[]{:S(2)}) %collective-permute-start.20) | collective-permute-done | bytes 172064 | tf_op jit(solution)/shard_map/ppermute | solution.py:60
  37.1 3.2 %collective-permute-done.21 = bf16[224,384]{1,0:T(8,128)(2,1)S(1)} collective-permute-done((bf16[224,384]{1,0:T(8,128)(2,1)S(1)}, bf16[224,384]{1,0:T(8,128)(2,1)S(1)}, u32[]{:S(2)}, u32[]{:S(2)}) %collective-permute-start.21) | collective-permute-done | bytes 172064 | tf_op jit(solution)/shard_map/ppermute | solution.py:60
  40.3 1.7 %collective-permute-start.22 = (bf16[112,384]{1,0:T(8,128)(2,1)S(1)}, bf16[112,384]{1,0:T(8,128)(2,1)S(1)}, u32[]{:S(2)}, u32[]{:S(2)}) collective-permute-start(bf16[112,384]{1,0:T(8,128)(2,1)S(1)} %slice.54), channel_id=1, source_target_pairs={{0,16},{2,18},{4,20},{6,22},{8,24},{10,26},{12,28},{14,30},{16,0},... | collective-permute-start | bytes 258056 | tf_op jit(solution)/shard_map/ppermute | solution.py:60
  42.0 4.6 %collective-permute-done.22 = bf16[112,384]{1,0:T(8,128)(2,1)S(1)} collective-permute-done((bf16[112,384]{1,0:T(8,128)(2,1)S(1)}, bf16[112,384]{1,0:T(8,128)(2,1)S(1)}, u32[]{:S(2)}, u32[]{:S(2)}) %collective-permute-start.22) | collective-permute-done | bytes 86048 | tf_op jit(solution)/shard_map/ppermute | solution.py:60
  46.6 1.0 collective-permute-start.23
  47.6 5.3 %collective-permute-done.23 = bf16[112,384]{1,0:T(8,128)(2,1)S(1)} collective-permute-done((bf16[112,384]{1,0:T(8,128)(2,1)S(1)}, bf16[112,384]{1,0:T(8,128)(2,1)S(1)}, u32[]{:S(2)}, u32[]{:S(2)}) %collective-permute-start.23) | collective-permute-done | bytes 86048 | tf_op jit(solution)/shard_map/ppermute | solution.py:60
  52.9 1.0 %collective-permute-start.24 = (bf16[224,384]{1,0:T(8,128)(2,1)S(1)}, bf16[224,384]{1,0:T(8,128)(2,1)S(1)}, u32[]{:S(2)}, u32[]{:S(2)}) collective-permute-start(bf16[224,384]{1,0:T(8,128)(2,1)S(1)} %pad_maximum_fusion.1), channel_id=1, source_target_pairs={{0,4},{2,6},{4,0},{6,2},{8,12},{10,14},{12,8},{14,10},{16,20},{18,... | collective-permute-start | bytes 516104 | tf_op jit(solution)/shard_map/ppermute | solution.py:60
  53.9 2.6 %collective-permute-start.26 = (bf16[224,384]{1,0:T(8,128)(2,1)S(1)}, bf16[224,384]{1,0:T(8,128)(2,1)S(1)}, u32[]{:S(2)}, u32[]{:S(2)}) collective-permute-start(bf16[224,384]{1,0:T(8,128)(2,1)S(1)} %pad_maximum_fusion.1), channel_id=1, source_target_pairs={{0,12},{2,14},{4,8},{6,10},{8,4},{10,6},{12,0},{14,2},{16,28},{18,... | collective-permute-start | bytes 516104 | tf_op jit(solution)/shard_map/ppermute | solution.py:60
  56.5 2.3 %collective-permute-done.24 = bf16[224,384]{1,0:T(8,128)(2,1)S(1)} collective-permute-done((bf16[224,384]{1,0:T(8,128)(2,1)S(1)}, bf16[224,384]{1,0:T(8,128)(2,1)S(1)}, u32[]{:S(2)}, u32[]{:S(2)}) %collective-permute-start.24) | collective-permute-done | bytes 172064 | tf_op jit(solution)/shard_map/ppermute | solution.py:60
  59.3 2.3 %collective-permute-done.26 = bf16[224,384]{1,0:T(8,128)(2,1)S(1)} collective-permute-done((bf16[224,384]{1,0:T(8,128)(2,1)S(1)}, bf16[224,384]{1,0:T(8,128)(2,1)S(1)}, u32[]{:S(2)}, u32[]{:S(2)}) %collective-permute-start.26) | collective-permute-done | bytes 172064 | tf_op jit(solution)/shard_map/ppermute | solution.py:60
  61.9 1.0 %copy.34 = bf16[1168,192]{0,1:T(8,128)(2,1)} copy(bf16[1168,192]{1,0:T(8,128)(2,1)S(1)} %pad_maximum_fusion) | data formatting | bytes 897024 | tf_op jit(solution)/shard_map/concatenate | solution.py:420
  63.4 1.7 %copy-done.5 = bf16[3,3,384,384]{3,2,1,0:T(8,128)(2,1)S(1)} copy-done((bf16[3,3,384,384]{3,2,1,0:T(8,128)(2,1)S(1)}, bf16[3,3,384,384]{3,2,1,0:T(8,128)(2,1)}, u32[]{:S(2)}) %copy-start.5) | copy-done | bytes 2654232
  65.2 2.8 %shard_map.107 = (f32[1024,192]{1,0:T(8,128)S(1)}, bf16[144,192]{1,0:T(8,128)(2,1)S(1)}) custom-call(bf16[1024,384]{1,0:T(8,128)(2,1)S(1)} %shard_map.106.cot_ref, bf16[9,384,384]{2,1,0:T(8,128)(2,1)S(1)} %bitcast.13), custom_call_target="tpu_custom_call" | custom-call | flops 1358954496 | bytes 4282368 | tf_op jit(solution)/shard_map/pallas_call | solution.py:103
  68.0 2.2 %collective-permute-start.10 = (bf16[144,192]{1,0:T(8,128)(2,1)S(1)}, bf16[144,192]{1,0:T(8,128)(2,1)S(1)}, u32[]{:S(2)}, u32[]{:S(2)}) collective-permute-start(bf16[144,192]{1,0:T(8,128)(2,1)S(1)} %get-tuple-element.6), channel_id=1, source_target_pairs={{0,24},{2,26},{4,28},{6,30},{8,0},{10,2},{12,4},{14,6},{16,8},{18,... | collective-permute-start | bytes 165896 | tf_op jit(solution)/shard_map/ppermute | solution.py:56
  70.2 1.4 %collective-permute-start.12 = (bf16[144,192]{1,0:T(8,128)(2,1)S(1)}, bf16[144,192]{1,0:T(8,128)(2,1)S(1)}, u32[]{:S(2)}, u32[]{:S(2)}) collective-permute-start(bf16[144,192]{1,0:T(8,128)(2,1)S(1)} %get-tuple-element.6), channel_id=1, source_target_pairs={{0,28},{2,30},{4,0},{6,2},{8,4},{10,6},{12,8},{14,10},{16,12},{18,... | collective-permute-start | bytes 165896 | tf_op jit(solution)/shard_map/ppermute | solution.py:56
  71.6 1.0 %collective-permute-done.10.refs_0_ = bf16[144,192]{1,0:T(8,128)(2,1)S(1)} collective-permute-done((bf16[144,192]{1,0:T(8,128)(2,1)S(1)}, bf16[144,192]{1,0:T(8,128)(2,1)S(1)}, u32[]{:S(2)}, u32[]{:S(2)}) %collective-permute-start.10) | collective-permute-done | bytes 55328 | tf_op jit(solution)/shard_map/ppermute | solution.py:56
  72.6 3.2 %collective-permute-start.13 = (bf16[144,192]{1,0:T(8,128)(2,1)S(1)}, bf16[144,192]{1,0:T(8,128)(2,1)S(1)}, u32[]{:S(2)}, u32[]{:S(2)}) collective-permute-start(bf16[144,192]{1,0:T(8,128)(2,1)S(1)} %get-tuple-element.6), channel_id=1, source_target_pairs={{0,30},{2,0},{4,2},{6,4},{8,6},{10,8},{12,10},{14,12},{16,14},{18,... | collective-permute-start | bytes 165896 | tf_op jit(solution)/shard_map/ppermute | solution.py:56
  75.8 1.9 %collective-permute-start.15 = (bf16[144,192]{1,0:T(8,128)(2,1)S(1)}, bf16[144,192]{1,0:T(8,128)(2,1)S(1)}, u32[]{:S(2)}, u32[]{:S(2)}) collective-permute-start(bf16[144,192]{1,0:T(8,128)(2,1)S(1)} %get-tuple-element.6), channel_id=1, source_target_pairs={{0,4},{2,6},{4,8},{6,10},{8,12},{10,14},{12,16},{14,18},{16,20},{1... | collective-permute-start | bytes 165896 | tf_op jit(solution)/shard_map/ppermute | solution.py:56
  78.1 4.3 %collective-permute-done.14.refs_4_ = bf16[144,192]{1,0:T(8,128)(2,1)S(1)} collective-permute-done((bf16[144,192]{1,0:T(8,128)(2,1)S(1)}, bf16[144,192]{1,0:T(8,128)(2,1)S(1)}, u32[]{:S(2)}, u32[]{:S(2)}) %collective-permute-start.14) | collective-permute-done | bytes 55328 | tf_op jit(solution)/shard_map/ppermute | solution.py:56
  82.4 1.2 %collective-permute-done.15.refs_5_ = bf16[144,192]{1,0:T(8,128)(2,1)S(1)} collective-permute-done((bf16[144,192]{1,0:T(8,128)(2,1)S(1)}, bf16[144,192]{1,0:T(8,128)(2,1)S(1)}, u32[]{:S(2)}, u32[]{:S(2)}) %collective-permute-start.15) | collective-permute-done | bytes 55328 | tf_op jit(solution)/shard_map/ppermute | solution.py:56
  83.6 5.0 %collective-permute-done.17.refs_7_ = bf16[144,192]{1,0:T(8,128)(2,1)S(1)} collective-permute-done((bf16[144,192]{1,0:T(8,128)(2,1)S(1)}, bf16[144,192]{1,0:T(8,128)(2,1)S(1)}, u32[]{:S(2)}, u32[]{:S(2)}) %collective-permute-start.17) | collective-permute-done | bytes 55328 | tf_op jit(solution)/shard_map/ppermute | solution.py:56
  88.6 2.6 %shard_map.108 = bf16[1024,192]{1,0:T(8,128)(2,1)} custom-call(s32[8,4]{1,0:T(8,128)S(1)} %copy-done.4, s32[16,4]{1,0:T(8,128)S(1)} %copy.30.et_ref, s32[16,4]{1,0:T(8,128)S(1)} %copy.31.eu_ref, s32[16,4]{1,0:T(8,128)S(1)} %copy.32.ct_ref, s32[16,4]{1,0:T(8,128)S(1)} %copy.33.cu_ref, f32[1024,192]{1,0:T(8,128)S(1)} %get-tuple-element.5.inner_ref, ...), custom_call_target="tpu_custom_call" | custom-call | bytes 1623168 | tf_op jit(solution)/shard_map/pallas_call | solution.py:103
  91.4 1.7 %copy-done.6 = bf16[3,3,384,384]{3,2,1,0:T(8,128)(2,1)S(1)} copy-done((bf16[3,3,384,384]{3,2,1,0:T(8,128)(2,1)S(1)}, bf16[3,3,384,384]{3,2,1,0:T(8,128)(2,1)}, u32[]{:S(2)}) %copy-start.6) | copy-done | bytes 2654232
  93.2 3.5 %shard_map.105 = bf16[1024,192]{1,0:T(8,128)(2,1)} custom-call(bf16[32,32,192]{2,1,0:T(8,128)(2,1)S(1)} %bitcast.10, bf16[144,192]{1,0:T(8,128)(2,1)S(1)} %shard_map.104.halos_ref, bf16[1168,192]{1,0:T(8,128)(2,1)S(1)} %copy.35.other_ref, bf16[9,384,384]{2,1,0:T(8,128)(2,1)S(1)} %bitcast.14), custom_call_target="tpu_custom_call" | custom-call | flops 1358954496 | bytes 3944448 | tf_op jit(solution)/shard_map/pallas_call | solution.py:103
  96.7 1.8 %shard_map.110 = f32[1728,384]{1,0:T(8,128)} custom-call(bf16[896,384]{1,0:T(8,128)(2,1)S(1)} %constant_dynamic-update-slice_fusion.mine_ref, bf16[896,384]{1,0:T(8,128)(2,1)S(1)} %collective-permute-done.27.other_ref), custom_call_target="tpu_custom_call" | custom-call | bytes 4030464 | tf_op jit(solution)/shard_map/pallas_call | solution.py:103
  (48 shorter events, 3.8 us)
Async XLA Ops:
  0.6 22.0 %collective-permute-start.9 = (bf16[1024,192]{1,0:T(8,128)(2,1)}, bf16[1024,192]{1,0:T(8,128)(2,1)S(1)}, u32[]{:S(2)}, u32[]{:S(2)}) collective-permute-start(bf16[1024,192]{1,0:T(8,128)(2,1)} %bitcast.11), channel_id=1, source_target_pairs={{0,1},{1,0},{2,3},{3,2},{4,5},{5,4},{6,7},{7,6},{8,9},{9,8},{10,11... | collective-permute-start | bytes 1179656 | tf_op jit(solution)/shard_map/ppermute | solution.py:376
  3.6 1.0 %copy-start = (bf16[1,32,32,192]{3,2,1,0:T(8,128)(2,1)S(1)}, bf16[1,32,32,192]{3,2,1,0:T(8,128)(2,1)}, u32[]{:S(2)}) copy-start(bf16[1,32,32,192]{3,2,1,0:T(8,128)(2,1)} %param.8) | copy-start | bytes 1179652
  4.7 17.9 %copy-start.2 = (bf16[1,32,32,192]{3,2,1,0:T(8,128)(2,1)S(1)}, bf16[1,32,32,192]{3,2,1,0:T(8,128)(2,1)}, u32[]{:S(2)}) copy-start(bf16[1,32,32,192]{3,2,1,0:T(8,128)(2,1)} %param.10) | copy-start | bytes 1179652
  4.7 18.1 %copy-start.1 = (bf16[1,32,32,192]{3,2,1,0:T(8,128)(2,1)S(1)}, bf16[1,32,32,192]{3,2,1,0:T(8,128)(2,1)}, u32[]{:S(2)}) copy-start(bf16[1,32,32,192]{3,2,1,0:T(8,128)(2,1)} %param.8) | copy-start | bytes 1179652
  4.7 6.1 %collective-permute-start = (bf16[128,192]{1,0:T(8,128)(2,1)S(1)}, bf16[128,192]{1,0:T(8,128)(2,1)S(1)}, u32[]{:S(2)}, u32[]{:S(2)}) collective-permute-start(bf16[128,192]{1,0:T(8,128)(2,1)S(1)} %shard_map.103), channel_id=1, source_target_pairs={{0,8},{2,10},{4,12},{6,14},{8,16},{10,18},{12,20},{14,22},{16,24},... | collective-permute-start | bytes 147464 | tf_op jit(solution)/shard_map/ppermute | solution.py:56
  6.4 6.4 %collective-permute-start.1 = (bf16[128,192]{1,0:T(8,128)(2,1)S(1)}, bf16[128,192]{1,0:T(8,128)(2,1)S(1)}, u32[]{:S(2)}, u32[]{:S(2)}) collective-permute-start(bf16[128,192]{1,0:T(8,128)(2,1)S(1)} %shard_map.103), channel_id=1, source_target_pairs={{0,6},{2,8},{4,10},{6,12},{8,14},{10,16},{12,18},{14,20},{16,22},{... | collective-permute-start | bytes 147464 | tf_op jit(solution)/shard_map/ppermute | solution.py:56
  6.8 7.7 %collective-permute-start.2 = (bf16[128,192]{1,0:T(8,128)(2,1)S(1)}, bf16[128,192]{1,0:T(8,128)(2,1)S(1)}, u32[]{:S(2)}, u32[]{:S(2)}) collective-permute-start(bf16[128,192]{1,0:T(8,128)(2,1)S(1)} %shard_map.103), channel_id=1, source_target_pairs={{0,4},{2,6},{4,8},{6,10},{8,12},{10,14},{12,16},{14,18},{16,20},{1... | collective-permute-start | bytes 147464 | tf_op jit(solution)/shard_map/ppermute | solution.py:56
  8.3 7.1 %collective-permute-start.3 = (bf16[128,192]{1,0:T(8,128)(2,1)S(1)}, bf16[128,192]{1,0:T(8,128)(2,1)S(1)}, u32[]{:S(2)}, u32[]{:S(2)}) collective-permute-start(bf16[128,192]{1,0:T(8,128)(2,1)S(1)} %shard_map.103), channel_id=1, source_target_pairs={{0,2},{2,4},{4,6},{6,8},{8,10},{10,12},{12,14},{14,16},{16,18},{18... | collective-permute-start | bytes 147464 | tf_op jit(solution)/shard_map/ppermute | solution.py:56
  10.9 9.0 %collective-permute-start.4 = (bf16[128,192]{1,0:T(8,128)(2,1)S(1)}, bf16[128,192]{1,0:T(8,128)(2,1)S(1)}, u32[]{:S(2)}, u32[]{:S(2)}) collective-permute-start(bf16[128,192]{1,0:T(8,128)(2,1)S(1)} %shard_map.103), channel_id=1, source_target_pairs={{0,30},{2,0},{4,2},{6,4},{8,6},{10,8},{12,10},{14,12},{16,14},{18,... | collective-permute-start | bytes 147464 | tf_op jit(solution)/shard_map/ppermute | solution.py:56
  12.7 7.1 %collective-permute-start.5 = (bf16[128,192]{1,0:T(8,128)(2,1)S(1)}, bf16[128,192]{1,0:T(8,128)(2,1)S(1)}, u32[]{:S(2)}, u32[]{:S(2)}) collective-permute-start(bf16[128,192]{1,0:T(8,128)(2,1)S(1)} %shard_map.103), channel_id=1, source_target_pairs={{0,28},{2,30},{4,0},{6,2},{8,4},{10,6},{12,8},{14,10},{16,12},{18,... | collective-permute-start | bytes 147464 | tf_op jit(solution)/shard_map/ppermute | solution.py:56
  14.5 5.4 %collective-permute-start.6 = (bf16[128,192]{1,0:T(8,128)(2,1)S(1)}, bf16[128,192]{1,0:T(8,128)(2,1)S(1)}, u32[]{:S(2)}, u32[]{:S(2)}) collective-permute-start(bf16[128,192]{1,0:T(8,128)(2,1)S(1)} %shard_map.103), channel_id=1, source_target_pairs={{0,26},{2,28},{4,30},{6,0},{8,2},{10,4},{12,6},{14,8},{16,10},{18,... | collective-permute-start | bytes 147464 | tf_op jit(solution)/shard_map/ppermute | solution.py:56
  15.4 5.1 %collective-permute-start.7 = (bf16[128,192]{1,0:T(8,128)(2,1)S(1)}, bf16[128,192]{1,0:T(8,128)(2,1)S(1)}, u32[]{:S(2)}, u32[]{:S(2)}) collective-permute-start(bf16[128,192]{1,0:T(8,128)(2,1)S(1)} %shard_map.103), channel_id=1, source_target_pairs={{0,24},{2,26},{4,28},{6,30},{8,0},{10,2},{12,4},{14,6},{16,8},{18,... | collective-permute-start | bytes 147464 | tf_op jit(solution)/shard_map/ppermute | solution.py:56
  20.5 0.7 copy-start.3
  25.4 3.2 %collective-permute-start.18 = (f32[896,384]{1,0:T(8,128)S(1)}, f32[896,384]{1,0:T(8,128)S(1)}, u32[]{:S(2)}, u32[]{:S(2)}) collective-permute-start(f32[896,384]{1,0:T(8,128)S(1)} %slice.37), channel_id=1, source_target_pairs={{0,2},{2,0},{4,6},{6,4},{8,10},{10,8},{12,14},{14,12},{16,18},{18,... | collective-permute-start | bytes 4128776 | tf_op jit(solution)/shard_map/ppermute | solution.py:60
  28.9 6.5 %collective-permute-start.19 = (bf16[224,384]{1,0:T(8,128)(2,1)S(1)}, bf16[224,384]{1,0:T(8,128)(2,1)S(1)}, u32[]{:S(2)}, u32[]{:S(2)}) collective-permute-start(bf16[224,384]{1,0:T(8,128)(2,1)S(1)} %get-tuple-element.11), channel_id=1, source_target_pairs={{0,4},{2,6},{4,0},{6,2},{8,12},{10,14},{12,8},{14,10},{16,20},{18,... | collective-permute-start | bytes 516104 | tf_op jit(solution)/shard_map/ppermute | solution.py:60
  29.8 7.2 %collective-permute-start.20 = (bf16[224,384]{1,0:T(8,128)(2,1)S(1)}, bf16[224,384]{1,0:T(8,128)(2,1)S(1)}, u32[]{:S(2)}, u32[]{:S(2)}) collective-permute-start(bf16[224,384]{1,0:T(8,128)(2,1)S(1)} %get-tuple-element.13), channel_id=1, source_target_pairs={{0,8},{2,10},{4,12},{6,14},{8,0},{10,2},{12,4},{14,6},{16,24},{18,... | collective-permute-start | bytes 516104 | tf_op jit(solution)/shard_map/ppermute | solution.py:60
  30.6 9.7 %collective-permute-start.21 = (bf16[224,384]{1,0:T(8,128)(2,1)S(1)}, bf16[224,384]{1,0:T(8,128)(2,1)S(1)}, u32[]{:S(2)}, u32[]{:S(2)}) collective-permute-start(bf16[224,384]{1,0:T(8,128)(2,1)S(1)} %get-tuple-element.12), channel_id=1, source_target_pairs={{0,12},{2,14},{4,8},{6,10},{8,4},{10,6},{12,0},{14,2},{16,28},{18,... | collective-permute-start | bytes 516104 | tf_op jit(solution)/shard_map/ppermute | solution.py:60
  40.3 6.2 %collective-permute-start.22 = (bf16[112,384]{1,0:T(8,128)(2,1)S(1)}, bf16[112,384]{1,0:T(8,128)(2,1)S(1)}, u32[]{:S(2)}, u32[]{:S(2)}) collective-permute-start(bf16[112,384]{1,0:T(8,128)(2,1)S(1)} %slice.54), channel_id=1, source_target_pairs={{0,16},{2,18},{4,20},{6,22},{8,24},{10,26},{12,28},{14,30},{16,0},... | collective-permute-start | bytes 258056 | tf_op jit(solution)/shard_map/ppermute | solution.py:60
  46.6 6.3 %collective-permute-start.23 = (bf16[112,384]{1,0:T(8,128)(2,1)S(1)}, bf16[112,384]{1,0:T(8,128)(2,1)S(1)}, u32[]{:S(2)}, u32[]{:S(2)}) collective-permute-start(bf16[112,384]{1,0:T(8,128)(2,1)S(1)} %get-tuple-element.8), channel_id=1, source_target_pairs={{0,16},{2,18},{4,20},{6,22},{8,24},{10,26},{12,28},{14,30},{16,0},... | collective-permute-start | bytes 258056 | tf_op jit(solution)/shard_map/ppermute | solution.py:60
  52.9 5.8 %collective-permute-start.24 = (bf16[224,384]{1,0:T(8,128)(2,1)S(1)}, bf16[224,384]{1,0:T(8,128)(2,1)S(1)}, u32[]{:S(2)}, u32[]{:S(2)}) collective-permute-start(bf16[224,384]{1,0:T(8,128)(2,1)S(1)} %pad_maximum_fusion.1), channel_id=1, source_target_pairs={{0,4},{2,6},{4,0},{6,2},{8,12},{10,14},{12,8},{14,10},{16,20},{18,... | collective-permute-start | bytes 516104 | tf_op jit(solution)/shard_map/ppermute | solution.py:60
  53.9 5.4 %collective-permute-start.25 = (bf16[224,384]{1,0:T(8,128)(2,1)S(1)}, bf16[224,384]{1,0:T(8,128)(2,1)S(1)}, u32[]{:S(2)}, u32[]{:S(2)}) collective-permute-start(bf16[224,384]{1,0:T(8,128)(2,1)S(1)} %pad_maximum_fusion.1), channel_id=1, source_target_pairs={{0,8},{2,10},{4,12},{6,14},{8,0},{10,2},{12,4},{14,6},{16,24},{18,... | collective-permute-start | bytes 516104 | tf_op jit(solution)/shard_map/ppermute | solution.py:60
  53.9 7.8 %collective-permute-start.26 = (bf16[224,384]{1,0:T(8,128)(2,1)S(1)}, bf16[224,384]{1,0:T(8,128)(2,1)S(1)}, u32[]{:S(2)}, u32[]{:S(2)}) collective-permute-start(bf16[224,384]{1,0:T(8,128)(2,1)S(1)} %pad_maximum_fusion.1), channel_id=1, source_target_pairs={{0,12},{2,14},{4,8},{6,10},{8,4},{10,6},{12,0},{14,2},{16,28},{18,... | collective-permute-start | bytes 516104 | tf_op jit(solution)/shard_map/ppermute | solution.py:60
  61.7 35.0 %collective-permute-start.27 = (bf16[896,384]{1,0:T(8,128)(2,1)S(1)}, bf16[896,384]{1,0:T(8,128)(2,1)S(1)}, u32[]{:S(2)}, u32[]{:S(2)}) collective-permute-start(bf16[896,384]{1,0:T(8,128)(2,1)S(1)} %constant_dynamic-update-slice_fusion.mine_ref), channel_id=1, source_target_pairs={{0,2},{2,0},{4,6},{6,4},{8,10},{10,8},{12,14},{14,12},{16,18},{18,... | collective-permute-start | bytes 2064392 | tf_op jit(solution)/shard_map/ppermute | solution.py:60
  62.9 28.3 %collective-permute-start.8 = (bf16[1168,192]{0,1:T(8,128)(2,1)}, bf16[1168,192]{0,1:T(8,128)(2,1)S(1)}, u32[]{:S(2)}, u32[]{:S(2)}) collective-permute-start(bf16[1168,192]{0,1:T(8,128)(2,1)} %copy.34), channel_id=1, source_target_pairs={{0,1},{1,0},{2,3},{3,2},{4,5},{5,4},{6,7},{7,6},{8,9},{9,8},{10,11... | collective-permute-start | bytes 1345544 | tf_op jit(solution)/shard_map/ppermute | solution.py:424
  63.4 1.7 %copy-start.5 = (bf16[3,3,384,384]{3,2,1,0:T(8,128)(2,1)S(1)}, bf16[3,3,384,384]{3,2,1,0:T(8,128)(2,1)}, u32[]{:S(2)}) copy-start(bf16[3,3,384,384]{3,2,1,0:T(8,128)(2,1)} %param.9) | copy-start | bytes 7962628
  65.2 23.4 %copy-start.4 = (s32[8,4]{1,0:T(8,128)S(1)}, s32[8,4]{1,0:T(8,128)}, u32[]{:S(2)}) copy-start(s32[8,4]{1,0:T(8,128)} %constant.2.clone.tables_ref) | copy-start | bytes 388
  68.0 4.6 %collective-permute-start.10 = (bf16[144,192]{1,0:T(8,128)(2,1)S(1)}, bf16[144,192]{1,0:T(8,128)(2,1)S(1)}, u32[]{:S(2)}, u32[]{:S(2)}) collective-permute-start(bf16[144,192]{1,0:T(8,128)(2,1)S(1)} %get-tuple-element.6), channel_id=1, source_target_pairs={{0,24},{2,26},{4,28},{6,30},{8,0},{10,2},{12,4},{14,6},{16,8},{18,... | collective-permute-start | bytes 165896 | tf_op jit(solution)/shard_map/ppermute | solution.py:56
  70.2 5.6 %collective-permute-start.11 = (bf16[144,192]{1,0:T(8,128)(2,1)S(1)}, bf16[144,192]{1,0:T(8,128)(2,1)S(1)}, u32[]{:S(2)}, u32[]{:S(2)}) collective-permute-start(bf16[144,192]{1,0:T(8,128)(2,1)S(1)} %get-tuple-element.6), channel_id=1, source_target_pairs={{0,26},{2,28},{4,30},{6,0},{8,2},{10,4},{12,6},{14,8},{16,10},{18,... | collective-permute-start | bytes 165896 | tf_op jit(solution)/shard_map/ppermute | solution.py:56
  70.2 5.6 %collective-permute-start.12 = (bf16[144,192]{1,0:T(8,128)(2,1)S(1)}, bf16[144,192]{1,0:T(8,128)(2,1)S(1)}, u32[]{:S(2)}, u32[]{:S(2)}) collective-permute-start(bf16[144,192]{1,0:T(8,128)(2,1)S(1)} %get-tuple-element.6), channel_id=1, source_target_pairs={{0,28},{2,30},{4,0},{6,2},{8,4},{10,6},{12,8},{14,10},{16,12},{18,... | collective-permute-start | bytes 165896 | tf_op jit(solution)/shard_map/ppermute | solution.py:56
  72.6 5.1 %collective-permute-start.13 = (bf16[144,192]{1,0:T(8,128)(2,1)S(1)}, bf16[144,192]{1,0:T(8,128)(2,1)S(1)}, u32[]{:S(2)}, u32[]{:S(2)}) collective-permute-start(bf16[144,192]{1,0:T(8,128)(2,1)S(1)} %get-tuple-element.6), channel_id=1, source_target_pairs={{0,30},{2,0},{4,2},{6,4},{8,6},{10,8},{12,10},{14,12},{16,14},{18,... | collective-permute-start | bytes 165896 | tf_op jit(solution)/shard_map/ppermute | solution.py:56
  75.7 6.7 %collective-permute-start.14 = (bf16[144,192]{1,0:T(8,128)(2,1)S(1)}, bf16[144,192]{1,0:T(8,128)(2,1)S(1)}, u32[]{:S(2)}, u32[]{:S(2)}) collective-permute-start(bf16[144,192]{1,0:T(8,128)(2,1)S(1)} %get-tuple-element.6), channel_id=1, source_target_pairs={{0,2},{2,4},{4,6},{6,8},{8,10},{10,12},{12,14},{14,16},{16,18},{18... | collective-permute-start | bytes 165896 | tf_op jit(solution)/shard_map/ppermute | solution.py:56
  75.8 7.8 %collective-permute-start.15 = (bf16[144,192]{1,0:T(8,128)(2,1)S(1)}, bf16[144,192]{1,0:T(8,128)(2,1)S(1)}, u32[]{:S(2)}, u32[]{:S(2)}) collective-permute-start(bf16[144,192]{1,0:T(8,128)(2,1)S(1)} %get-tuple-element.6), channel_id=1, source_target_pairs={{0,4},{2,6},{4,8},{6,10},{8,12},{10,14},{12,16},{14,18},{16,20},{1... | collective-permute-start | bytes 165896 | tf_op jit(solution)/shard_map/ppermute | solution.py:56
  77.7 5.9 %collective-permute-start.16 = (bf16[144,192]{1,0:T(8,128)(2,1)S(1)}, bf16[144,192]{1,0:T(8,128)(2,1)S(1)}, u32[]{:S(2)}, u32[]{:S(2)}) collective-permute-start(bf16[144,192]{1,0:T(8,128)(2,1)S(1)} %get-tuple-element.6), channel_id=1, source_target_pairs={{0,6},{2,8},{4,10},{6,12},{8,14},{10,16},{12,18},{14,20},{16,22},{... | collective-permute-start | bytes 165896 | tf_op jit(solution)/shard_map/ppermute | solution.py:56
  82.4 6.2 %collective-permute-start.17 = (bf16[144,192]{1,0:T(8,128)(2,1)S(1)}, bf16[144,192]{1,0:T(8,128)(2,1)S(1)}, u32[]{:S(2)}, u32[]{:S(2)}) collective-permute-start(bf16[144,192]{1,0:T(8,128)(2,1)S(1)} %get-tuple-element.6), channel_id=1, source_target_pairs={{0,8},{2,10},{4,12},{6,14},{8,16},{10,18},{12,20},{14,22},{16,24},... | collective-permute-start | bytes 165896 | tf_op jit(solution)/shard_map/ppermute | solution.py:56
  91.4 1.8 %copy-start.6 = (bf16[3,3,384,384]{3,2,1,0:T(8,128)(2,1)S(1)}, bf16[3,3,384,384]{3,2,1,0:T(8,128)(2,1)}, u32[]{:S(2)}) copy-start(bf16[3,3,384,384]{3,2,1,0:T(8,128)(2,1)} %param.9) | copy-start | bytes 7962628

commit v3 on v2

--- a/solution.py
+++ b/solution.py
@@ -12,6 +12,7 @@
 SPAN = 4
 OFFSETS = list(range(-SPAN, 0)) + list(range(1, SPAN + 1))
 EXTRA = 16
+PER_STAGE = (1, 3, 2, 0)
 
 
 def turn_tables():
@@ -155,13 +156,13 @@
     row = lax.broadcasted_iota(jnp.int32, (4 * side + EXTRA, 1), 0)
     wanted = jnp.full((4 * side + EXTRA, 1), -1, jnp.int32)
     for e in range(4):
-        slot = tables_ref[e, eu_ref[own, e]]
-        start = base(et_ref[own, e]) + lax.rem(slot, 4) * side
+        slot = tables_ref[e, eu_ref[e, own]]
+        start = base(et_ref[e, own]) + lax.rem(slot, 4) * side
         along = row - e * side
         along = jnp.where(slot >= 4, side - 1 - along, along)
         wanted = jnp.where((row >= e * side) & (row < (e + 1) * side), start + along, wanted)
-        corner = tables_ref[4 + e, cu_ref[own, e]]
-        spot = base(ct_ref[own, e]) + corner_spot(corner, side)
+        corner = tables_ref[4 + e, cu_ref[e, own]]
+        spot = base(ct_ref[e, own]) + corner_spot(corner, side)
         wanted = jnp.where(row == 4 * side + e, spot, wanted)
     near = jnp.concatenate([ref[...] for ref in near_refs], axis=0)
     lane = lax.broadcasted_iota(jnp.int32, (4 * side + EXTRA, near.shape[0]), 1)
@@ -288,13 +289,13 @@
         source = lax.rem(own - offset + count, count)
         for e in range(4):
             first = index * block + e * side
-            slot = tables_ref[e, eu_ref[source, e]]
+            slot = tables_ref[e, eu_ref[e, source]]
             along = lane - first
             along = jnp.where(slot >= 4, side - 1 - along, along)
-            hit = (lane >= first) & (lane < first + side) & (et_ref[source, e] == own)
+            hit = (lane >= first) & (lane < first + side) & (et_ref[e, source] == own)
             target = jnp.where(hit, lax.rem(slot, 4) * side + along, target)
-            spot = corner_spot(tables_ref[4 + e, cu_ref[source, e]], side)
-            hit = (lane == index * block + 4 * side + e) & (ct_ref[source, e] == own)
+            spot = corner_spot(tables_ref[4 + e, cu_ref[e, source]], side)
+            hit = (lane == index * block + 4 * side + e) & (ct_ref[e, source] == own)
             target = jnp.where(hit, spot, target)
     row = lax.broadcasted_iota(jnp.int32, (4 * side, total), 0)
     place = jnp.where(row == target, 1.0, 0.0).astype(jnp.bfloat16)
@@ -340,25 +341,6 @@
     out_ref[...] = result.astype(jnp.bfloat16)
 
 
-def sum_over_tiles(partial, own_tile, count):
-    stages = mask_stages(count)
-    held = partial
-    for index, bits in enumerate(stages):
-        masks = group_masks(bits)
-        part = held.shape[0] // len(masks)
-        kind = jnp.float32 if index == 0 else jnp.bfloat16
-        pieces = [held[i * part : (i + 1) * part] for i in range(len(masks))]
-        got = [by_mask(p.astype(kind), m, count) for p, m in zip(pieces[1:], masks[1:])]
-        held = pieces[0]
-        for value in got:
-            held = held + value.astype(jnp.float32)
-    held = held.astype(jnp.bfloat16)
-    for bits in stages[:0:-1]:
-        masks = group_masks(bits)
-        held = jnp.concatenate([held] + [by_mask(held, m, count) for m in masks[1:]], axis=0)
-    return held, by_mask(held, 1, count)
-
-
 def body(features, weight, cotangent, edge_tiles, edge_turns, corner_tiles, corner_turns):
     tables = jnp.asarray(turn_tables())
     count = lax.axis_size("tile")
@@ -370,13 +352,22 @@
     flat = rows + 2 * side
     taps = weight.reshape(9, chans, chans)
     others = [(0, 1), (1, 0)]
-    smalls = (tables, edge_tiles, edge_turns, corner_tiles, corner_turns)
+    smalls = (tables, edge_tiles.T, edge_turns.T, corner_tiles.T, corner_turns.T)
 
     cot_own = cotangent[0].reshape(rows, part)
     cot_other = lax.ppermute(cot_own, "ch", others)
     (sides,) = call(functools.partial(sides_kernel, side), [vmem((4 * side, part), jnp.bfloat16)], [field])
     near = [by_offset(sides, -offset, count) for offset in OFFSETS]
     (cot_full,) = call(both_kernel, [vmem((rows, chans), jnp.bfloat16)], [cot_own, cot_other])
+
+    inner, pieces = call(
+        functools.partial(back_kernel, side, part),
+        [vmem((rows, part), jnp.float32), vmem((4 * side + EXTRA, part), jnp.bfloat16)],
+        [cot_full, taps],
+        scratch=[pltpu.VMEM((rows + 4 * side, chans), jnp.bfloat16)],
+        flops=2 * rows * 9 * part * chans,
+    )
+    near, inner, pieces = lax.optimization_barrier((near, inner, pieces))
 
     (halos,) = call(
         functools.partial(halo_kernel, side, part),
@@ -395,35 +386,54 @@
         ],
         flops=2 * rows * 9 * part * chans,
     )
-    mine, other = sum_over_tiles(local, own_tile, count)
+    packet = jnp.concatenate([field.reshape(rows, part), halos], axis=0)
+
+    stages = mask_stages(count)
+    waiting = list(OFFSETS)
+    got_pieces = []
+    other_field = lax.ppermute(packet, "ch", others)
+    held = local
+    for index, bits in enumerate(stages):
+        masks = group_masks(bits)
+        size = held.shape[0] // len(masks)
+        kind = jnp.float32 if index == 0 else jnp.bfloat16
+        cut = [held[i * size : (i + 1) * size] for i in range(len(masks))]
+        got = [by_mask(p.astype(kind), m, count) for p, m in zip(cut[1:], masks[1:])]
+        beside = [by_offset(pieces, offset, count) for offset in waiting[:PER_STAGE[min(index, 3)]]]
+        waiting = waiting[PER_STAGE[min(index, 3)]:]
+        keep, got, beside, pieces = lax.optimization_barrier((cut[0], got, beside, pieces))
+        got_pieces += beside
+        held = keep
+        for value in got:
+            held = held + value.astype(jnp.float32)
+    held = held.astype(jnp.bfloat16)
+    for index, bits in enumerate(stages[:0:-1]):
+        masks = group_masks(bits)
+        got = [by_mask(held, m, count) for m in masks[1:]]
+        if index == 0:
+            beside = [by_offset(pieces, offset, count) for offset in waiting]
+            held, got, beside, other_field = lax.optimization_barrier((held, got, beside, other_field))
+            got_pieces += beside
+        if index == len(stages) - 2:
+            (grad_features,) = call(
+                functools.partial(add_halo_kernel, side, part),
+                [vmem((rows, part), jnp.bfloat16)],
+                [*smalls, inner, *got_pieces],
+                smem=range(5),
+            )
+            (output,) = call(
+                functools.partial(output_kernel, side, part),
+                [vmem((rows, part), jnp.bfloat16)],
+                [field, halos, other_field, taps],
+                scratch=[pltpu.VMEM((3, flat, part), jnp.bfloat16)] * 2,
+                flops=2 * rows * 9 * part * chans,
+            )
+            held, got, output, grad_features = lax.optimization_barrier((held, got, output, grad_features))
+        held = jnp.concatenate([held] + got, axis=0)
     (grad_weight,) = call(
         functools.partial(unfold_kernel, part, chunk),
         [vmem((9 * part, chans), jnp.float32)],
-        [mine, other],
-    )
-
-    inner, pieces = call(
-        functools.partial(back_kernel, side, part),
-        [vmem((rows, part), jnp.float32), vmem((4 * side + EXTRA, part), jnp.bfloat16)],
-        [cot_full, taps],
-        scratch=[pltpu.VMEM((rows + 4 * side, chans), jnp.bfloat16)],
-        flops=2 * rows * 9 * part * chans,
-    )
-    got = [by_offset(pieces, offset, count) for offset in OFFSETS]
-    (grad_features,) = call(
-        functools.partial(add_halo_kernel, side, part),
-        [vmem((rows, part), jnp.bfloat16)],
-        [*smalls, inner, *got],
-        smem=range(5),
-    )
-
-    packet = jnp.concatenate([field.reshape(rows, part), halos], axis=0)
-    (output,) = call(
-        functools.partial(output_kernel, side, part),
-        [vmem((rows, part), jnp.bfloat16)],
-        [field, halos, lax.ppermute(packet, "ch", others), taps],
-        scratch=[pltpu.VMEM((3, flat, part), jnp.bfloat16)] * 2,
-        flops=2 * rows * 9 * part * chans,
+        [held, by_mask(held, 1, count)],
     )
     shape = (1, side, side, part)
     return (

time: 98.8 us -> 95 us (0.962)
  waiting for transfers between devices: 40.1 us -> 30.8 us
  local copies, waits for them, and re-layouts: 9.76 us -> 13.1 us
  other arithmetic: 0.43 us -> 2.4 us
    ppermute x10, waiting for transfers between devices: 25.9 us -> 8.42 us  [by_mask(): return lax.ppermute(value, 'tile', [(i, i ^ mask) for i in range(count)])]
    ppermute x1, waiting for transfers between devices: 0.01 us -> 6.48 us  [body(): cot_other = lax.ppermute(cot_own, 'ch', others)]
    slice x3 -> x5, local copies, waits for them, and re-layouts: 0.16 us -> 2.01 us  [body(): cut = [held[i * size:(i + 1) * size] for i in range(len(masks))]]
    ppermute x16, waiting for transfers between devices: 14.2 us -> 15.9 us  [by_offset(): lax.ppermute(value, 'tile', [(i, (i + offset) % count) for i in range(cou...]
    ppermute x10, starting transfers between devices: 9.88 us -> 8.28 us  [by_mask(): return lax.ppermute(value, 'tile', [(i, i ^ mask) for i in range(count)])]
    concatenate x1 -> x2, local copies, waits for them, and re-layouts: 0.03 us -> 1.59 us  [body(): held = jnp.concatenate([held] + got, axis=0)]
    ppermute x16, starting transfers between devices: 19.1 us -> 20.6 us  [by_offset(): lax.ppermute(value, 'tile', [(i, (i + offset) % count) for i in range(cou...]
    another operation x1, other arithmetic: 0.2 us -> 1.28 us
  transfers between devices with their start and end apart: 28 -> 28, of which waited for: 18 -> 13; matrix products, arithmetic and copies ran while one was open for 5% -> 5% of each run, Pallas kernels for 11% -> 9%
where the time goes in v3:
time: 95 us; the launch traced here: 94.6 us
  starting transfers between devices  33.4 us (35%)
  waiting for transfers between devices  30.8 us (32%)
  Pallas kernels  13.9 us (15%)
  local copies, waits for them, and re-layouts  13.1 us (14%)
  other arithmetic  2.4 us (3%)
    ppermute x16, starting transfers between devices, by_offset(): lax.ppermute(value, 'tile', [(i, (i + offset) % count) for i in range(cou...  20.6 us
    ppermute x16, waiting for transfers between devices, by_offset(): lax.ppermute(value, 'tile', [(i, (i + offset) % count) for i in range(cou...  15.9 us
    pallas_call x8, Pallas kernels, call(): pl.pallas_call(kernel, out_shape=tuple(outs), in_specs=in_specs, out_spec...  13.9 us
    unnamed x24, local copies, waits for them, and re-layouts  9.08 us
    ppermute x10, waiting for transfers between devices, by_mask(): return lax.ppermute(value, 'tile', [(i, i ^ mask) for i in range(count)])  8.42 us
    ppermute x10, starting transfers between devices, by_mask(): return lax.ppermute(value, 'tile', [(i, i ^ mask) for i in range(count)])  8.28 us
    ppermute x1, waiting for transfers between devices, body(): cot_other = lax.ppermute(cot_own, 'ch', others)  6.48 us
    ppermute x1, starting transfers between devices, body(): cot_other = lax.ppermute(cot_own, 'ch', others)  3 us
  transfers between devices with their start and end apart: 28, of which 13 were waited for; matrix products, arithmetic and copies ran while one was open for 5% of the time, Pallas kernels for 9%

profile of v3, /device:TPU:0, one launch (start us, length us, event | category | flops | bytes accessed | tf_op | source)
XLA Modules:
  0.0 94.6 jit_solution(1893336827908444470)
XLA Ops:
  0.6 3.0 %collective-permute-start.8 = (bf16[1024,192]{1,0:T(8,128)(2,1)}, bf16[1024,192]{1,0:T(8,128)(2,1)S(1)}, u32[]{:S(2)}, u32[]{:S(2)}) collective-permute-start(bf16[1024,192]{1,0:T(8,128)(2,1)} %bitcast.15), channel_id=1, source_target_pairs={{0,1},{1,0},{2,3},{3,2},{4,5},{5,4},{6,7},{7,6},{8,9},{9,8},{10,11... | collective-permute-start | bytes 1179656 | tf_op jit(solution)/shard_map/ppermute | solution.py:358
  3.6 1.0 %copy-done = bf16[1,32,32,192]{3,2,1,0:T(8,128)(2,1)S(1)} copy-done((bf16[1,32,32,192]{3,2,1,0:T(8,128)(2,1)S(1)}, bf16[1,32,32,192]{3,2,1,0:T(8,128)(2,1)}, u32[]{:S(2)}) %copy-start) | copy-done | bytes 393240
  4.7 1.6 %collective-permute-start = (bf16[128,192]{1,0:T(8,128)(2,1)S(1)}, bf16[128,192]{1,0:T(8,128)(2,1)S(1)}, u32[]{:S(2)}, u32[]{:S(2)}) collective-permute-start(bf16[128,192]{1,0:T(8,128)(2,1)S(1)} %shard_map.103), channel_id=1, source_target_pairs={{0,8},{2,10},{4,12},{6,14},{8,16},{10,18},{12,20},{14,22},{16,24},... | collective-permute-start | bytes 147464 | tf_op jit(solution)/shard_map/ppermute | solution.py:57
  6.8 1.5 %collective-permute-start.2 = (bf16[128,192]{1,0:T(8,128)(2,1)S(1)}, bf16[128,192]{1,0:T(8,128)(2,1)S(1)}, u32[]{:S(2)}, u32[]{:S(2)}) collective-permute-start(bf16[128,192]{1,0:T(8,128)(2,1)S(1)} %shard_map.103), channel_id=1, source_target_pairs={{0,4},{2,6},{4,8},{6,10},{8,12},{10,14},{12,16},{14,18},{16,20},{1... | collective-permute-start | bytes 147464 | tf_op jit(solution)/shard_map/ppermute | solution.py:57
  8.3 1.0 %collective-permute-start.3 = (bf16[128,192]{1,0:T(8,128)(2,1)S(1)}, bf16[128,192]{1,0:T(8,128)(2,1)S(1)}, u32[]{:S(2)}, u32[]{:S(2)}) collective-permute-start(bf16[128,192]{1,0:T(8,128)(2,1)S(1)} %shard_map.103), channel_id=1, source_target_pairs={{0,2},{2,4},{4,6},{6,8},{8,10},{10,12},{12,14},{14,16},{16,18},{18... | collective-permute-start | bytes 147464 | tf_op jit(solution)/shard_map/ppermute | solution.py:57
  9.3 6.5 %collective-permute-done.8.other_ref = bf16[1024,192]{1,0:T(8,128)(2,1)S(1)} collective-permute-done((bf16[1024,192]{1,0:T(8,128)(2,1)}, bf16[1024,192]{1,0:T(8,128)(2,1)S(1)}, u32[]{:S(2)}, u32[]{:S(2)}) %collective-permute-start.8) | collective-permute-done | bytes 393248 | tf_op jit(solution)/shard_map/ppermute | solution.py:358
  15.8 3.4 %collective-permute-start.4 = (bf16[128,192]{1,0:T(8,128)(2,1)S(1)}, bf16[128,192]{1,0:T(8,128)(2,1)S(1)}, u32[]{:S(2)}, u32[]{:S(2)}) collective-permute-start(bf16[128,192]{1,0:T(8,128)(2,1)S(1)} %shard_map.103), channel_id=1, source_target_pairs={{0,30},{2,0},{4,2},{6,4},{8,6},{10,8},{12,10},{14,12},{16,14},{18,... | collective-permute-start | bytes 147464 | tf_op jit(solution)/shard_map/ppermute | solution.py:57
  19.1 1.0 %copy-done.2 = bf16[1,32,32,192]{3,2,1,0:T(8,128)(2,1)S(1)} copy-done((bf16[1,32,32,192]{3,2,1,0:T(8,128)(2,1)S(1)}, bf16[1,32,32,192]{3,2,1,0:T(8,128)(2,1)}, u32[]{:S(2)}) %copy-start.2) | copy-done | bytes 393240
  20.4 1.5 %collective-permute-start.5 = (bf16[128,192]{1,0:T(8,128)(2,1)S(1)}, bf16[128,192]{1,0:T(8,128)(2,1)S(1)}, u32[]{:S(2)}, u32[]{:S(2)}) collective-permute-start(bf16[128,192]{1,0:T(8,128)(2,1)S(1)} %shard_map.103), channel_id=1, source_target_pairs={{0,28},{2,30},{4,0},{6,2},{8,4},{10,6},{12,8},{14,10},{16,12},{18,... | collective-permute-start | bytes 147464 | tf_op jit(solution)/shard_map/ppermute | solution.py:57
  22.6 1.7 %copy-done.8 = bf16[3,3,384,384]{3,2,1,0:T(8,128)(2,1)S(1)} copy-done((bf16[3,3,384,384]{3,2,1,0:T(8,128)(2,1)S(1)}, bf16[3,3,384,384]{3,2,1,0:T(8,128)(2,1)}, u32[]{:S(2)}) %copy-start.8) | copy-done | bytes 2654232
  24.4 2.8 %shard_map.105 = (f32[1024,192]{1,0:T(8,128)S(1)}, bf16[144,192]{1,0:T(8,128)(2,1)S(1)}) custom-call(bf16[1024,384]{1,0:T(8,128)(2,1)S(1)} %shard_map.104.cot_ref, bf16[9,384,384]{2,1,0:T(8,128)(2,1)S(1)} %bitcast.25), custom_call_target="tpu_custom_call" | custom-call | flops 1358954496 | bytes 4282368 | tf_op jit(solution)/shard_map/pallas_call | solution.py:104
  27.3 0.5 collective-permute-done.7.refs_7_
  27.8 1.0 %shard_map.106.halos_ref = bf16[144,192]{1,0:T(8,128)(2,1)S(1)} custom-call(s32[8,4]{1,0:T(8,128)S(1)} %copy-done.3, s32[4,16]{1,0:T(4,128)S(1)} %bitcast.17, s32[4,16]{1,0:T(4,128)S(1)} %bitcast.19, s32[4,16]{1,0:T(4,128)S(1)} %bitcast.21, s32[4,16]{1,0:T(4,128)S(1)} %bitcast.23, bf16[128,192]{1,0:T(8,128)(2,1)S(1)} %collective-permute-done.refs_0_, ...), custom_call_target="tpu_custom_call" | custom-call | bytes 449664 | tf_op jit(solution)/shard_map/pallas_call | solution.py:104
  28.8 2.4 %shard_map.107 = f32[1792,384]{1,0:T(8,128)S(1)} custom-call(bf16[32,32,192]{2,1,0:T(8,128)(2,1)S(1)} %bitcast.12, bf16[144,192]{1,0:T(8,128)(2,1)S(1)} %shard_map.106.halos_ref, bf16[1024,384]{1,0:T(8,128)(2,1)S(1)} %shard_map.104.cot_ref), custom_call_target="tpu_custom_call" | custom-call | flops 1358954496 | bytes 3987456 | tf_op jit(solution)/shard_map/pallas_call | solution.py:104
  31.4 3.3 %collective-permute-start.10 = (bf16[144,192]{1,0:T(8,128)(2,1)S(1)}, bf16[144,192]{1,0:T(8,128)(2,1)S(1)}, u32[]{:S(2)}, u32[]{:S(2)}) collective-permute-start(bf16[144,192]{1,0:T(8,128)(2,1)S(1)} %get-tuple-element.64), channel_id=1, source_target_pairs={{0,24},{2,26},{4,28},{6,30},{8,0},{10,2},{12,4},{14,6},{16,8},{18,... | collective-permute-start | bytes 165896 | tf_op jit(solution)/shard_map/ppermute | solution.py:57
  34.8 2.1 %collective-permute-done.10.refs_0_ = bf16[144,192]{1,0:T(8,128)(2,1)S(1)} collective-permute-done((bf16[144,192]{1,0:T(8,128)(2,1)S(1)}, bf16[144,192]{1,0:T(8,128)(2,1)S(1)}, u32[]{:S(2)}, u32[]{:S(2)}) %collective-permute-start.10) | collective-permute-done | bytes 55328 | tf_op jit(solution)/shard_map/ppermute | solution.py:57
  36.9 3.5 %collective-permute-start.14 = (bf16[144,192]{1,0:T(8,128)(2,1)S(1)}, bf16[144,192]{1,0:T(8,128)(2,1)S(1)}, u32[]{:S(2)}, u32[]{:S(2)}) collective-permute-start(bf16[144,192]{1,0:T(8,128)(2,1)S(1)} %get-tuple-element.64), channel_id=1, source_target_pairs={{0,26},{2,28},{4,30},{6,0},{8,2},{10,4},{12,6},{14,8},{16,10},{18,... | collective-permute-start | bytes 165896 | tf_op jit(solution)/shard_map/ppermute | solution.py:57
  40.5 1.9 %collective-permute-start.16 = (bf16[144,192]{1,0:T(8,128)(2,1)S(1)}, bf16[144,192]{1,0:T(8,128)(2,1)S(1)}, u32[]{:S(2)}, u32[]{:S(2)}) collective-permute-start(bf16[144,192]{1,0:T(8,128)(2,1)S(1)} %get-tuple-element.64), channel_id=1, source_target_pairs={{0,30},{2,0},{4,2},{6,4},{8,6},{10,8},{12,10},{14,12},{16,14},{18,... | collective-permute-start | bytes 165896 | tf_op jit(solution)/shard_map/ppermute | solution.py:57
  42.4 1.3 %fusion = (bf16[896,384]{1,0:T(8,128)(2,1)S(1)}, f32[896,384]{1,0:T(8,128)}) fusion(f32[896,384]{1,0:T(8,128)S(1)} %get-tuple-element.54, f32[896,384]{1,0:T(8,128)S(1)} %collective-permute-done.9), kind=kLoop, calls=%fused_computation.10 | loop fusion | flops 688128 | bytes 4816896 | tf_op jit(solution)/shard_map/convert.3
  43.7 0.8 fusion.2
  44.5 1.7 %collective-permute-start.11 = (bf16[224,384]{1,0:T(8,128)(2,1)}, bf16[224,384]{1,0:T(8,128)(2,1)S(1)}, u32[]{:S(2)}, u32[]{:S(2)}) collective-permute-start(bf16[224,384]{1,0:T(8,128)(2,1)} %get-tuple-element.89), channel_id=1, source_target_pairs={{0,4},{2,6},{4,0},{6,2},{8,12},{10,14},{12,8},{14,10},{16,20},{18,... | collective-permute-start | bytes 516104 | tf_op jit(solution)/shard_map/ppermute | solution.py:61
  46.2 1.8 %collective-permute-start.13 = (bf16[224,384]{1,0:T(8,128)(2,1)}, bf16[224,384]{1,0:T(8,128)(2,1)}, u32[]{:S(2)}, u32[]{:S(2)}) collective-permute-start(bf16[224,384]{1,0:T(8,128)(2,1)} %get-tuple-element.87), channel_id=1, source_target_pairs={{0,12},{2,14},{4,8},{6,10},{8,4},{10,6},{12,0},{14,2},{16,28},{18,... | collective-permute-start | bytes 516104 | tf_op jit(solution)/shard_map/ppermute | solution.py:61
  48.3 1.0 %slice.38 = f32[224,384]{1,0:T(8,128)S(1)} slice(f32[896,384]{1,0:T(8,128)} %get-tuple-element.84), slice={[0:224], [0:384]} | slice | bytes 688128 | tf_op jit(solution)/shard_map/slice | solution.py:400
  49.3 1.5 %collective-permute-start.23 = (bf16[1168,192]{0,1:T(8,128)(2,1)S(1)}, bf16[1168,192]{0,1:T(8,128)(2,1)S(1)}, u32[]{:S(2)}, u32[]{:S(2)}) collective-permute-start(bf16[1168,192]{0,1:T(8,128)(2,1)S(1)} %copy.14), channel_id=1, source_target_pairs={{0,1},{1,0},{2,3},{3,2},{4,5},{5,4},{6,7},{7,6},{8,9},{9,8},{10,11... | collective-permute-start | bytes 1345544 | tf_op jit(solution)/shard_map/ppermute | solution.py:394
  51.1 2.1 %collective-permute-done.12 = bf16[224,384]{1,0:T(8,128)(2,1)S(1)} collective-permute-done((bf16[224,384]{1,0:T(8,128)(2,1)}, bf16[224,384]{1,0:T(8,128)(2,1)S(1)}, u32[]{:S(2)}, u32[]{:S(2)}) %collective-permute-start.12) | collective-permute-done | bytes 172064 | tf_op jit(solution)/shard_map/ppermute | solution.py:61
  53.1 2.9 %collective-permute-done.13 = bf16[224,384]{1,0:T(8,128)(2,1)} collective-permute-done((bf16[224,384]{1,0:T(8,128)(2,1)}, bf16[224,384]{1,0:T(8,128)(2,1)}, u32[]{:S(2)}, u32[]{:S(2)}) %collective-permute-start.13) | collective-permute-done | bytes 172064 | tf_op jit(solution)/shard_map/ppermute | solution.py:61
  56.0 1.0 %convert_add_fusion = f32[224,384]{1,0:T(8,128)S(1)} fusion(bf16[224,384]{1,0:T(8,128)(2,1)} %collective-permute-done.13, bf16[224,384]{1,0:T(8,128)(2,1)S(1)} %collective-permute-done.12, f32[224,384]{1,0:T(8,128)S(1)} %slice.38, bf16[224,384]{1,0:T(8,128)(2,1)S(1)} %collective-permute-done.11), kind=kLoop, calls=%fused_computation.1 | loop fusion | flops 516096 | bytes 1204224 | tf_op jit(solution)/shard_map/add | solution.py:408
  57.2 0.6 collective-permute-start.19
  57.8 6.1 %collective-permute-done.18.refs_4_ = bf16[144,192]{1,0:T(8,128)(2,1)S(1)} collective-permute-done((bf16[144,192]{1,0:T(8,128)(2,1)S(1)}, bf16[144,192]{1,0:T(8,128)(2,1)S(1)}, u32[]{:S(2)}, u32[]{:S(2)}) %collective-permute-start.18) | collective-permute-done | bytes 55328 | tf_op jit(solution)/shard_map/ppermute | solution.py:57
  63.9 1.2 %collective-permute-done.19.refs_5_ = bf16[144,192]{1,0:T(8,128)(2,1)S(1)} collective-permute-done((bf16[144,192]{1,0:T(8,128)(2,1)S(1)}, bf16[144,192]{1,0:T(8,128)(2,1)S(1)}, u32[]{:S(2)}, u32[]{:S(2)}) %collective-permute-start.19) | collective-permute-done | bytes 55328 | tf_op jit(solution)/shard_map/ppermute | solution.py:57
  65.1 1.1 %collective-permute-start.20 = (bf16[112,384]{1,0:T(8,128)(2,1)S(1)}, bf16[112,384]{1,0:T(8,128)(2,1)S(1)}, u32[]{:S(2)}, u32[]{:S(2)}) collective-permute-start(bf16[112,384]{1,0:T(8,128)(2,1)S(1)} %add_convert_fusion), channel_id=1, source_target_pairs={{0,16},{2,18},{4,20},{6,22},{8,24},{10,26},{12,28},{14,30},{16,0},... | collective-permute-start | bytes 258056 | tf_op jit(solution)/shard_map/ppermute | solution.py:61
  66.2 1.0 %collective-permute-start.22 = (bf16[144,192]{1,0:T(8,128)(2,1)S(1)}, bf16[144,192]{1,0:T(8,128)(2,1)S(1)}, u32[]{:S(2)}, u32[]{:S(2)}) collective-permute-start(bf16[144,192]{1,0:T(8,128)(2,1)S(1)} %get-tuple-element.64), channel_id=1, source_target_pairs={{0,8},{2,10},{4,12},{6,14},{8,16},{10,18},{12,20},{14,22},{16,24},... | collective-permute-start | bytes 165896 | tf_op jit(solution)/shard_map/ppermute | solution.py:57
  67.1 4.9 %collective-permute-done.21.refs_6_ = bf16[144,192]{1,0:T(8,128)(2,1)S(1)} collective-permute-done((bf16[144,192]{1,0:T(8,128)(2,1)S(1)}, bf16[144,192]{1,0:T(8,128)(2,1)S(1)}, u32[]{:S(2)}, u32[]{:S(2)}) %collective-permute-start.21) | collective-permute-done | bytes 55328 | tf_op jit(solution)/shard_map/ppermute | solution.py:57
  72.1 1.1 %collective-permute-done.22.refs_7_ = bf16[144,192]{1,0:T(8,128)(2,1)S(1)} collective-permute-done((bf16[144,192]{1,0:T(8,128)(2,1)S(1)}, bf16[144,192]{1,0:T(8,128)(2,1)S(1)}, u32[]{:S(2)}, u32[]{:S(2)}) %collective-permute-start.22) | collective-permute-done | bytes 55328 | tf_op jit(solution)/shard_map/ppermute | solution.py:57
  73.2 0.8 collective-permute-done.20
  74.0 0.6 constant_dynamic-update-slice_fusion.1
  74.6 0.6 constant_dynamic-update-slice_fusion
  75.3 0.9 collective-permute-start.24
  76.2 2.6 %collective-permute-start.26 = (bf16[224,384]{1,0:T(8,128)(2,1)}, bf16[224,384]{1,0:T(8,128)(2,1)}, u32[]{:S(2)}, u32[]{:S(2)}) collective-permute-start(bf16[224,384]{1,0:T(8,128)(2,1)} %constant_dynamic-update-slice_fusion), channel_id=1, source_target_pairs={{0,12},{2,14},{4,8},{6,10},{8,4},{10,6},{12,0},{14,2},{16,28},{18,... | collective-permute-start | bytes 516104 | tf_op jit(solution)/shard_map/ppermute | solution.py:61
  79.0 2.2 %shard_map.109 = bf16[1024,192]{1,0:T(8,128)(2,1)} custom-call(s32[8,4]{1,0:T(8,128)S(1)} %copy-done.3, s32[4,16]{1,0:T(4,128)S(1)} %bitcast.18, s32[4,16]{1,0:T(4,128)S(1)} %bitcast.20, s32[4,16]{1,0:T(4,128)S(1)} %bitcast.22, s32[4,16]{1,0:T(4,128)S(1)} %bitcast.24, f32[1024,192]{1,0:T(8,128)S(1)} %get-tuple-element.68.inner_ref, ...), custom_call_target="tpu_custom_call" | custom-call | bytes 1623168 | tf_op jit(solution)/shard_map/pallas_call | solution.py:104
  81.2 1.7 %copy-done.9 = bf16[3,3,384,384]{3,2,1,0:T(8,128)(2,1)S(1)} copy-done((bf16[3,3,384,384]{3,2,1,0:T(8,128)(2,1)S(1)}, bf16[3,3,384,384]{3,2,1,0:T(8,128)(2,1)}, u32[]{:S(2)}) %copy-start.9) | copy-done | bytes 2654232
  83.0 3.5 %shard_map.108 = bf16[1024,192]{1,0:T(8,128)(2,1)} custom-call(bf16[32,32,192]{2,1,0:T(8,128)(2,1)S(1)} %bitcast.14, bf16[144,192]{1,0:T(8,128)(2,1)S(1)} %shard_map.106.halos_ref, bf16[1168,192]{1,0:T(8,128)(2,1)S(1)} %copy.15.other_ref, bf16[9,384,384]{2,1,0:T(8,128)(2,1)S(1)} %bitcast.26), custom_call_target="tpu_custom_call" | custom-call | flops 1358954496 | bytes 3944448 | tf_op jit(solution)/shard_map/pallas_call | solution.py:104
  86.8 0.9 constant_dynamic-update-slice_fusion.5
  87.7 0.9 %constant_dynamic-update-slice_fusion.4 = bf16[896,384]{1,0:T(8,128)(2,1)S(1)} fusion(bf16[896,384]{1,0:T(8,128)(2,1)S(1)} %constant_dynamic-update-slice_fusion.5, bf16[224,384]{1,0:T(8,128)(2,1)} %collective-permute-done.24), kind=kLoop, calls=%fused_computation.8 | loop fusion | bytes 344064
  88.7 0.9 %constant_dynamic-update-slice_fusion.3 = bf16[896,384]{1,0:T(8,128)(2,1)S(1)} fusion(bf16[896,384]{1,0:T(8,128)(2,1)S(1)} %constant_dynamic-update-slice_fusion.4, bf16[224,384]{1,0:T(8,128)(2,1)} %collective-permute-done.25), kind=kLoop, calls=%fused_computation.7 | loop fusion | bytes 344064
  89.6 0.9 %constant_dynamic-update-slice_fusion.2.mine_ref = bf16[896,384]{1,0:T(8,128)(2,1)S(1)} fusion(bf16[896,384]{1,0:T(8,128)(2,1)S(1)} %constant_dynamic-update-slice_fusion.3, bf16[224,384]{1,0:T(8,128)(2,1)} %collective-permute-done.26), kind=kLoop, calls=%fused_computation.6 | loop fusion | bytes 344064 | tf_op jit(solution)/shard_map/concatenate | solution.py:432
  90.7 2.1 %collective-permute-done.27.other_ref = bf16[896,384]{1,0:T(8,128)(2,1)S(1)} collective-permute-done((bf16[896,384]{1,0:T(8,128)(2,1)S(1)}, bf16[896,384]{1,0:T(8,128)(2,1)S(1)}, u32[]{:S(2)}, u32[]{:S(2)}) %collective-permute-start.27) | collective-permute-done | bytes 688160 | tf_op jit(solution)/shard_map/ppermute | solution.py:61
  92.8 1.8 %shard_map.110 = f32[1728,384]{1,0:T(8,128)} custom-call(bf16[896,384]{1,0:T(8,128)(2,1)S(1)} %constant_dynamic-update-slice_fusion.2.mine_ref, bf16[896,384]{1,0:T(8,128)(2,1)S(1)} %collective-permute-done.27.other_ref), custom_call_target="tpu_custom_call" | custom-call | bytes 4030464 | tf_op jit(solution)/shard_map/pallas_call | solution.py:104
  (53 shorter events, 3.0 us)
Async XLA Ops:
  0.6 15.1 %collective-permute-start.8 = (bf16[1024,192]{1,0:T(8,128)(2,1)}, bf16[1024,192]{1,0:T(8,128)(2,1)S(1)}, u32[]{:S(2)}, u32[]{:S(2)}) collective-permute-start(bf16[1024,192]{1,0:T(8,128)(2,1)} %bitcast.15), channel_id=1, source_target_pairs={{0,1},{1,0},{2,3},{3,2},{4,5},{5,4},{6,7},{7,6},{8,9},{9,8},{10,11... | collective-permute-start | bytes 1179656 | tf_op jit(solution)/shard_map/ppermute | solution.py:358
  3.6 1.0 %copy-start = (bf16[1,32,32,192]{3,2,1,0:T(8,128)(2,1)S(1)}, bf16[1,32,32,192]{3,2,1,0:T(8,128)(2,1)}, u32[]{:S(2)}) copy-start(bf16[1,32,32,192]{3,2,1,0:T(8,128)(2,1)} %param.8) | copy-start | bytes 1179652
  4.7 15.7 %collective-permute-start = (bf16[128,192]{1,0:T(8,128)(2,1)S(1)}, bf16[128,192]{1,0:T(8,128)(2,1)S(1)}, u32[]{:S(2)}, u32[]{:S(2)}) collective-permute-start(bf16[128,192]{1,0:T(8,128)(2,1)S(1)} %shard_map.103), channel_id=1, source_target_pairs={{0,8},{2,10},{4,12},{6,14},{8,16},{10,18},{12,20},{14,22},{16,24},... | collective-permute-start | bytes 147464 | tf_op jit(solution)/shard_map/ppermute | solution.py:57
  6.4 15.5 %collective-permute-start.1 = (bf16[128,192]{1,0:T(8,128)(2,1)S(1)}, bf16[128,192]{1,0:T(8,128)(2,1)S(1)}, u32[]{:S(2)}, u32[]{:S(2)}) collective-permute-start(bf16[128,192]{1,0:T(8,128)(2,1)S(1)} %shard_map.103), channel_id=1, source_target_pairs={{0,6},{2,8},{4,10},{6,12},{8,14},{10,16},{12,18},{14,20},{16,22},{... | collective-permute-start | bytes 147464 | tf_op jit(solution)/shard_map/ppermute | solution.py:57
  6.8 15.4 %collective-permute-start.2 = (bf16[128,192]{1,0:T(8,128)(2,1)S(1)}, bf16[128,192]{1,0:T(8,128)(2,1)S(1)}, u32[]{:S(2)}, u32[]{:S(2)}) collective-permute-start(bf16[128,192]{1,0:T(8,128)(2,1)S(1)} %shard_map.103), channel_id=1, source_target_pairs={{0,4},{2,6},{4,8},{6,10},{8,12},{10,14},{12,16},{14,18},{16,20},{1... | collective-permute-start | bytes 147464 | tf_op jit(solution)/shard_map/ppermute | solution.py:57
  8.3 18.9 %collective-permute-start.3 = (bf16[128,192]{1,0:T(8,128)(2,1)S(1)}, bf16[128,192]{1,0:T(8,128)(2,1)S(1)}, u32[]{:S(2)}, u32[]{:S(2)}) collective-permute-start(bf16[128,192]{1,0:T(8,128)(2,1)S(1)} %shard_map.103), channel_id=1, source_target_pairs={{0,2},{2,4},{4,6},{6,8},{8,10},{10,12},{12,14},{14,16},{16,18},{18... | collective-permute-start | bytes 147464 | tf_op jit(solution)/shard_map/ppermute | solution.py:57
  15.8 11.5 %collective-permute-start.4 = (bf16[128,192]{1,0:T(8,128)(2,1)S(1)}, bf16[128,192]{1,0:T(8,128)(2,1)S(1)}, u32[]{:S(2)}, u32[]{:S(2)}) collective-permute-start(bf16[128,192]{1,0:T(8,128)(2,1)S(1)} %shard_map.103), channel_id=1, source_target_pairs={{0,30},{2,0},{4,2},{6,4},{8,6},{10,8},{12,10},{14,12},{16,14},{18,... | collective-permute-start | bytes 147464 | tf_op jit(solution)/shard_map/ppermute | solution.py:57
  19.1 1.0 %copy-start.2 = (bf16[1,32,32,192]{3,2,1,0:T(8,128)(2,1)S(1)}, bf16[1,32,32,192]{3,2,1,0:T(8,128)(2,1)}, u32[]{:S(2)}) copy-start(bf16[1,32,32,192]{3,2,1,0:T(8,128)(2,1)} %param.10) | copy-start | bytes 1179652
  20.4 6.8 %collective-permute-start.5 = (bf16[128,192]{1,0:T(8,128)(2,1)S(1)}, bf16[128,192]{1,0:T(8,128)(2,1)S(1)}, u32[]{:S(2)}, u32[]{:S(2)}) collective-permute-start(bf16[128,192]{1,0:T(8,128)(2,1)S(1)} %shard_map.103), channel_id=1, source_target_pairs={{0,28},{2,30},{4,0},{6,2},{8,4},{10,6},{12,8},{14,10},{16,12},{18,... | collective-permute-start | bytes 147464 | tf_op jit(solution)/shard_map/ppermute | solution.py:57
  21.9 5.4 %collective-permute-start.6 = (bf16[128,192]{1,0:T(8,128)(2,1)S(1)}, bf16[128,192]{1,0:T(8,128)(2,1)S(1)}, u32[]{:S(2)}, u32[]{:S(2)}) collective-permute-start(bf16[128,192]{1,0:T(8,128)(2,1)S(1)} %shard_map.103), channel_id=1, source_target_pairs={{0,26},{2,28},{4,30},{6,0},{8,2},{10,4},{12,6},{14,8},{16,10},{18,... | collective-permute-start | bytes 147464 | tf_op jit(solution)/shard_map/ppermute | solution.py:57
  22.2 5.5 %collective-permute-start.7 = (bf16[128,192]{1,0:T(8,128)(2,1)S(1)}, bf16[128,192]{1,0:T(8,128)(2,1)S(1)}, u32[]{:S(2)}, u32[]{:S(2)}) collective-permute-start(bf16[128,192]{1,0:T(8,128)(2,1)S(1)} %shard_map.103), channel_id=1, source_target_pairs={{0,24},{2,26},{4,28},{6,30},{8,0},{10,2},{12,4},{14,6},{16,8},{18,... | collective-permute-start | bytes 147464 | tf_op jit(solution)/shard_map/ppermute | solution.py:57
  22.6 1.7 %copy-start.8 = (bf16[3,3,384,384]{3,2,1,0:T(8,128)(2,1)S(1)}, bf16[3,3,384,384]{3,2,1,0:T(8,128)(2,1)}, u32[]{:S(2)}) copy-start(bf16[3,3,384,384]{3,2,1,0:T(8,128)(2,1)} %param.9) | copy-start | bytes 7962628
  24.4 3.3 %copy-start.3 = (s32[8,4]{1,0:T(8,128)S(1)}, s32[8,4]{1,0:T(8,128)}, u32[]{:S(2)}) copy-start(s32[8,4]{1,0:T(8,128)} %constant.2.clone.tables_ref) | copy-start | bytes 388
  24.4 3.3 %copy-start.4 = (s32[16,4]{0,1:T(4,128)S(1)}, s32[16,4]{0,1:T(4,128)}, u32[]{:S(2)}) copy-start(s32[16,4]{0,1:T(4,128)} %param.11) | copy-start | bytes 772
  24.4 3.3 %copy-start.5 = (s32[16,4]{0,1:T(4,128)S(1)}, s32[16,4]{0,1:T(4,128)}, u32[]{:S(2)}) copy-start(s32[16,4]{0,1:T(4,128)} %param.12) | copy-start | bytes 772
  24.4 3.3 %copy-start.6 = (s32[16,4]{0,1:T(4,128)S(1)}, s32[16,4]{0,1:T(4,128)}, u32[]{:S(2)}) copy-start(s32[16,4]{0,1:T(4,128)} %param.13) | copy-start | bytes 772
  24.4 3.4 %copy-start.7 = (s32[16,4]{0,1:T(4,128)S(1)}, s32[16,4]{0,1:T(4,128)}, u32[]{:S(2)}) copy-start(s32[16,4]{0,1:T(4,128)} %param.14) | copy-start | bytes 772
  24.4 4.3 %copy-start.1 = (bf16[1,32,32,192]{3,2,1,0:T(8,128)(2,1)S(1)}, bf16[1,32,32,192]{3,2,1,0:T(8,128)(2,1)}, u32[]{:S(2)}) copy-start(bf16[1,32,32,192]{3,2,1,0:T(8,128)(2,1)} %param.8) | copy-start | bytes 1179652
  31.4 5.6 %collective-permute-start.9 = (f32[896,384]{1,0:T(8,128)S(1)}, f32[896,384]{1,0:T(8,128)S(1)}, u32[]{:S(2)}, u32[]{:S(2)}) collective-permute-start(f32[896,384]{1,0:T(8,128)S(1)} %get-tuple-element.85), channel_id=1, source_target_pairs={{0,2},{2,0},{4,6},{6,4},{8,10},{10,8},{12,14},{14,12},{16,18},{18,... | collective-permute-start | bytes 4128776 | tf_op jit(solution)/shard_map/ppermute | solution.py:61
  31.4 5.5 %collective-permute-start.10 = (bf16[144,192]{1,0:T(8,128)(2,1)S(1)}, bf16[144,192]{1,0:T(8,128)(2,1)S(1)}, u32[]{:S(2)}, u32[]{:S(2)}) collective-permute-start(bf16[144,192]{1,0:T(8,128)(2,1)S(1)} %get-tuple-element.64), channel_id=1, source_target_pairs={{0,24},{2,26},{4,28},{6,30},{8,0},{10,2},{12,4},{14,6},{16,8},{18,... | collective-permute-start | bytes 165896 | tf_op jit(solution)/shard_map/ppermute | solution.py:57
  36.9 9.3 %collective-permute-start.14 = (bf16[144,192]{1,0:T(8,128)(2,1)S(1)}, bf16[144,192]{1,0:T(8,128)(2,1)S(1)}, u32[]{:S(2)}, u32[]{:S(2)}) collective-permute-start(bf16[144,192]{1,0:T(8,128)(2,1)S(1)} %get-tuple-element.64), channel_id=1, source_target_pairs={{0,26},{2,28},{4,30},{6,0},{8,2},{10,4},{12,6},{14,8},{16,10},{18,... | collective-permute-start | bytes 165896 | tf_op jit(solution)/shard_map/ppermute | solution.py:57
  40.5 8.9 %collective-permute-start.15 = (bf16[144,192]{1,0:T(8,128)(2,1)S(1)}, bf16[144,192]{1,0:T(8,128)(2,1)S(1)}, u32[]{:S(2)}, u32[]{:S(2)}) collective-permute-start(bf16[144,192]{1,0:T(8,128)(2,1)S(1)} %get-tuple-element.64), channel_id=1, source_target_pairs={{0,28},{2,30},{4,0},{6,2},{8,4},{10,6},{12,8},{14,10},{16,12},{18,... | collective-permute-start | bytes 165896 | tf_op jit(solution)/shard_map/ppermute | solution.py:57
  40.5 10.4 %collective-permute-start.16 = (bf16[144,192]{1,0:T(8,128)(2,1)S(1)}, bf16[144,192]{1,0:T(8,128)(2,1)S(1)}, u32[]{:S(2)}, u32[]{:S(2)}) collective-permute-start(bf16[144,192]{1,0:T(8,128)(2,1)S(1)} %get-tuple-element.64), channel_id=1, source_target_pairs={{0,30},{2,0},{4,2},{6,4},{8,6},{10,8},{12,10},{14,12},{16,14},{18,... | collective-permute-start | bytes 165896 | tf_op jit(solution)/shard_map/ppermute | solution.py:57
  44.5 6.6 %collective-permute-start.11 = (bf16[224,384]{1,0:T(8,128)(2,1)}, bf16[224,384]{1,0:T(8,128)(2,1)S(1)}, u32[]{:S(2)}, u32[]{:S(2)}) collective-permute-start(bf16[224,384]{1,0:T(8,128)(2,1)} %get-tuple-element.89), channel_id=1, source_target_pairs={{0,4},{2,6},{4,0},{6,2},{8,12},{10,14},{12,8},{14,10},{16,20},{18,... | collective-permute-start | bytes 516104 | tf_op jit(solution)/shard_map/ppermute | solution.py:61
  46.2 6.9 %collective-permute-start.12 = (bf16[224,384]{1,0:T(8,128)(2,1)}, bf16[224,384]{1,0:T(8,128)(2,1)S(1)}, u32[]{:S(2)}, u32[]{:S(2)}) collective-permute-start(bf16[224,384]{1,0:T(8,128)(2,1)} %get-tuple-element.88), channel_id=1, source_target_pairs={{0,8},{2,10},{4,12},{6,14},{8,0},{10,2},{12,4},{14,6},{16,24},{18,... | collective-permute-start | bytes 516104 | tf_op jit(solution)/shard_map/ppermute | solution.py:61
  46.2 9.8 %collective-permute-start.13 = (bf16[224,384]{1,0:T(8,128)(2,1)}, bf16[224,384]{1,0:T(8,128)(2,1)}, u32[]{:S(2)}, u32[]{:S(2)}) collective-permute-start(bf16[224,384]{1,0:T(8,128)(2,1)} %get-tuple-element.87), channel_id=1, source_target_pairs={{0,12},{2,14},{4,8},{6,10},{8,4},{10,6},{12,0},{14,2},{16,28},{18,... | collective-permute-start | bytes 516104 | tf_op jit(solution)/shard_map/ppermute | solution.py:61
  49.3 17.8 %collective-permute-start.23 = (bf16[1168,192]{0,1:T(8,128)(2,1)S(1)}, bf16[1168,192]{0,1:T(8,128)(2,1)S(1)}, u32[]{:S(2)}, u32[]{:S(2)}) collective-permute-start(bf16[1168,192]{0,1:T(8,128)(2,1)S(1)} %copy.14), channel_id=1, source_target_pairs={{0,1},{1,0},{2,3},{3,2},{4,5},{5,4},{6,7},{7,6},{8,9},{9,8},{10,11... | collective-permute-start | bytes 1345544 | tf_op jit(solution)/shard_map/ppermute | solution.py:394
  57.1 8.0 %collective-permute-start.17 = (bf16[112,384]{1,0:T(8,128)(2,1)S(1)}, bf16[112,384]{1,0:T(8,128)(2,1)S(1)}, u32[]{:S(2)}, u32[]{:S(2)}) collective-permute-start(bf16[112,384]{1,0:T(8,128)(2,1)S(1)} %slice.45), channel_id=1, source_target_pairs={{0,16},{2,18},{4,20},{6,22},{8,24},{10,26},{12,28},{14,30},{16,0},... | collective-permute-start | bytes 258056 | tf_op jit(solution)/shard_map/ppermute | solution.py:61
  57.1 6.7 %collective-permute-start.18 = (bf16[144,192]{1,0:T(8,128)(2,1)S(1)}, bf16[144,192]{1,0:T(8,128)(2,1)S(1)}, u32[]{:S(2)}, u32[]{:S(2)}) collective-permute-start(bf16[144,192]{1,0:T(8,128)(2,1)S(1)} %get-tuple-element.64), channel_id=1, source_target_pairs={{0,2},{2,4},{4,6},{6,8},{8,10},{10,12},{12,14},{14,16},{16,18},{18... | collective-permute-start | bytes 165896 | tf_op jit(solution)/shard_map/ppermute | solution.py:57
  57.2 7.8 %collective-permute-start.19 = (bf16[144,192]{1,0:T(8,128)(2,1)S(1)}, bf16[144,192]{1,0:T(8,128)(2,1)S(1)}, u32[]{:S(2)}, u32[]{:S(2)}) collective-permute-start(bf16[144,192]{1,0:T(8,128)(2,1)S(1)} %get-tuple-element.64), channel_id=1, source_target_pairs={{0,4},{2,6},{4,8},{6,10},{8,12},{10,14},{12,16},{14,18},{16,20},{1... | collective-permute-start | bytes 165896 | tf_op jit(solution)/shard_map/ppermute | solution.py:57
  65.1 8.9 %collective-permute-start.20 = (bf16[112,384]{1,0:T(8,128)(2,1)S(1)}, bf16[112,384]{1,0:T(8,128)(2,1)S(1)}, u32[]{:S(2)}, u32[]{:S(2)}) collective-permute-start(bf16[112,384]{1,0:T(8,128)(2,1)S(1)} %add_convert_fusion), channel_id=1, source_target_pairs={{0,16},{2,18},{4,20},{6,22},{8,24},{10,26},{12,28},{14,30},{16,0},... | collective-permute-start | bytes 258056 | tf_op jit(solution)/shard_map/ppermute | solution.py:61
  66.2 5.9 %collective-permute-start.21 = (bf16[144,192]{1,0:T(8,128)(2,1)S(1)}, bf16[144,192]{1,0:T(8,128)(2,1)S(1)}, u32[]{:S(2)}, u32[]{:S(2)}) collective-permute-start(bf16[144,192]{1,0:T(8,128)(2,1)S(1)} %get-tuple-element.64), channel_id=1, source_target_pairs={{0,6},{2,8},{4,10},{6,12},{8,14},{10,16},{12,18},{14,20},{16,22},{... | collective-permute-start | bytes 165896 | tf_op jit(solution)/shard_map/ppermute | solution.py:57
  66.2 7.0 %collective-permute-start.22 = (bf16[144,192]{1,0:T(8,128)(2,1)S(1)}, bf16[144,192]{1,0:T(8,128)(2,1)S(1)}, u32[]{:S(2)}, u32[]{:S(2)}) collective-permute-start(bf16[144,192]{1,0:T(8,128)(2,1)S(1)} %get-tuple-element.64), channel_id=1, source_target_pairs={{0,8},{2,10},{4,12},{6,14},{8,16},{10,18},{12,20},{14,22},{16,24},... | collective-permute-start | bytes 165896 | tf_op jit(solution)/shard_map/ppermute | solution.py:57
  75.3 11.2 %collective-permute-start.24 = (bf16[224,384]{1,0:T(8,128)(2,1)}, bf16[224,384]{1,0:T(8,128)(2,1)}, u32[]{:S(2)}, u32[]{:S(2)}) collective-permute-start(bf16[224,384]{1,0:T(8,128)(2,1)} %constant_dynamic-update-slice_fusion), channel_id=1, source_target_pairs={{0,4},{2,6},{4,0},{6,2},{8,12},{10,14},{12,8},{14,10},{16,20},{18,... | collective-permute-start | bytes 516104 | tf_op jit(solution)/shard_map/ppermute | solution.py:61
  76.2 10.3 %collective-permute-start.25 = (bf16[224,384]{1,0:T(8,128)(2,1)}, bf16[224,384]{1,0:T(8,128)(2,1)}, u32[]{:S(2)}, u32[]{:S(2)}) collective-permute-start(bf16[224,384]{1,0:T(8,128)(2,1)} %constant_dynamic-update-slice_fusion), channel_id=1, source_target_pairs={{0,8},{2,10},{4,12},{6,14},{8,0},{10,2},{12,4},{14,6},{16,24},{18,... | collective-permute-start | bytes 516104 | tf_op jit(solution)/shard_map/ppermute | solution.py:61
  76.2 10.6 %collective-permute-start.26 = (bf16[224,384]{1,0:T(8,128)(2,1)}, bf16[224,384]{1,0:T(8,128)(2,1)}, u32[]{:S(2)}, u32[]{:S(2)}) collective-permute-start(bf16[224,384]{1,0:T(8,128)(2,1)} %constant_dynamic-update-slice_fusion), channel_id=1, source_target_pairs={{0,12},{2,14},{4,8},{6,10},{8,4},{10,6},{12,0},{14,2},{16,28},{18,... | collective-permute-start | bytes 516104 | tf_op jit(solution)/shard_map/ppermute | solution.py:61
  81.2 1.7 %copy-start.9 = (bf16[3,3,384,384]{3,2,1,0:T(8,128)(2,1)S(1)}, bf16[3,3,384,384]{3,2,1,0:T(8,128)(2,1)}, u32[]{:S(2)}) copy-start(bf16[3,3,384,384]{3,2,1,0:T(8,128)(2,1)} %param.9) | copy-start | bytes 7962628
  90.6 2.2 %collective-permute-start.27 = (bf16[896,384]{1,0:T(8,128)(2,1)S(1)}, bf16[896,384]{1,0:T(8,128)(2,1)S(1)}, u32[]{:S(2)}, u32[]{:S(2)}) collective-permute-start(bf16[896,384]{1,0:T(8,128)(2,1)S(1)} %constant_dynamic-update-slice_fusion.2.mine_ref), channel_id=1, source_target_pairs={{0,2},{2,0},{4,6},{6,4},{8,10},{10,8},{12,14},{14,12},{16,18},{18,... | collective-permute-start | bytes 2064392 | tf_op jit(solution)/shard_map/ppermute | solution.py:61

commit v4 on v3

--- a/solution.py
+++ b/solution.py
@@ -12,7 +12,6 @@
 SPAN = 4
 OFFSETS = list(range(-SPAN, 0)) + list(range(1, SPAN + 1))
 EXTRA = 16
-PER_STAGE = (1, 3, 2, 0)
 
 
 def turn_tables():
@@ -170,11 +169,28 @@
     halos_ref[...] = jnp.dot(pick, near, preferred_element_type=jnp.float32).astype(jnp.bfloat16)
 
 
-def grad_weight_kernel(side, part, chunk, scale, field_ref, halos_ref, cot_ref, out_ref, cols, total):
+def join_halves(own, other, out_ref):
+    part = own.shape[1]
+
+    @pl.when(lax.axis_index("ch") == 0)
+    def _():
+        out_ref[:, 0:part] = own
+        out_ref[:, part:] = other
+
+    @pl.when(lax.axis_index("ch") != 0)
+    def _():
+        out_ref[:, 0:part] = other
+        out_ref[:, part:] = own
+
+
+def grad_weight_kernel(
+    side, part, chunk, scale, field_ref, halos_ref, own_ref, other_ref, mine_ref, send_ref, cols, total, cot_ref
+):
     rows = side * side
     chans = cot_ref.shape[1]
     count = lax.axis_size("tile")
     own = lax.axis_index("tile")
+    join_halves(own_ref[...], other_ref[...], cot_ref)
     shifted_columns(side, part, field_ref, halos_ref[...], cols)
     cot = cot_ref[...]
     for a in range(3):
@@ -190,56 +206,73 @@
                 * scale
             )
     total[9 * part :, :] = jnp.zeros((chunk * count - 9 * part, chans), jnp.float32)
+    half = count * chunk // 2
     for mask in range(count):
         to = slot_of_mask(mask, count) * chunk
         start = pl.multiple_of((own ^ mask) * chunk, 16)
-        out_ref[to : to + chunk, :] = total[pl.ds(start, chunk), :]
-
-
-def unfold_kernel(part, chunk, mine_ref, other_ref, out_ref):
-    count = lax.axis_size("tile")
+        value = total[pl.ds(start, chunk), :]
+        if to < half:
+            mine_ref[to : to + chunk, :] = value
+        else:
+            send_ref[to - half : to - half + chunk, :] = value
+
+
+def sum_kernel(n_got, n_out, n_join, *refs):
+    held_ref, got_refs = refs[0], refs[1 : 1 + n_got]
+    join_refs, outs = refs[1 + n_got : 1 + n_got + n_join], refs[1 + n_got + n_join :]
+    size = held_ref.shape[0] // n_out
+    for index in range(n_out):
+        here = slice(index * size, (index + 1) * size)
+        value = held_ref[here, :]
+        for ref in got_refs:
+            value = value + ref[here, :].astype(jnp.float32)
+        outs[index][...] = value.astype(outs[index].dtype)
+    if n_join:
+        join_kernel(*join_refs, outs[n_out])
+
+
+def join_kernel(*refs):
+    row = 0
+    for ref in refs[:-1]:
+        refs[-1][row : row + ref.shape[0], :] = ref[...]
+        row += ref.shape[0]
+
+
+def unfold_kernel(whole, chunk, bit, masks, n_dep, *refs):
+    refs = refs[n_dep:]
+    n = len(masks)
+    in_refs, out_ref, wide, sems = refs[:n], refs[n], refs[n + 1], refs[n + 2]
     own = lax.axis_index("tile")
-    half = mine_ref.shape[0] // chunk
-    whole = 9 * part
-    core = lax.rem(own, 2)
-    for block in range(count):
-        size = min(chunk, whole - block * chunk)
-        if size <= 0:
-            continue
-        mask = own ^ block
-        place = 0
-        for bits in mask_stages(count)[1:]:
-            span = 1 << len(bits)
-            place = place * span + lax.rem(mask // bits[0], span)
-        start = pl.multiple_of(place * chunk, 16)
-        mine = mine_ref[pl.ds(start, size), :]
-        other = other_ref[pl.ds(start, size), :]
-        value = jnp.where(core == block % 2, mine.astype(jnp.float32), other.astype(jnp.float32))
-        out_ref[block * chunk : block * chunk + size, :] = value
-
-
-def both_kernel(own_ref, other_ref, out_ref):
-    part = own_ref.shape[1]
-
-    @pl.when(lax.axis_index("ch") == 0)
-    def _():
-        out_ref[:, 0:part] = own_ref[...]
-        out_ref[:, part:] = other_ref[...]
-
-    @pl.when(lax.axis_index("ch") != 0)
-    def _():
-        out_ref[:, 0:part] = other_ref[...]
-        out_ref[:, part:] = own_ref[...]
-
-
-def back_kernel(side, part, cot_ref, weight_ref, inner_ref, pieces_ref, tall):
+    full, rest = whole // chunk, whole % chunk
+    copies = []
+    for i, (ref, inner) in enumerate(zip(in_refs, masks)):
+        for k, mask in enumerate(inner):
+            at = i * len(inner) + k
+            wide[at] = ref[k * chunk : (k + 1) * chunk, :].astype(jnp.float32)
+            block = own ^ mask ^ bit
+            start = pl.multiple_of(block * chunk, 16)
+            copy = pltpu.make_async_copy(wide.at[at], out_ref.at[pl.ds(start, chunk), :], sems.at[at])
+            copies.append((block, copy))
+            pl.when(block < full)(copy.start)
+            if rest:
+                copy = pltpu.make_async_copy(
+                    wide.at[at, 0:rest], out_ref.at[full * chunk : whole, :], sems.at[at]
+                )
+                copies.append((None, copy))
+                pl.when(block == full)(copy.start)
+                copies[-1] = (block == full, copy)
+            copies[-1 - bool(rest)] = (block < full, copies[-1 - bool(rest)][1])
+    for going, copy in copies:
+        pl.when(going)(copy.wait)
+
+
+def back_kernel(side, part, own_ref, other_ref, weight_ref, inner_ref, pieces_ref, tall):
     rows = side * side
     flat = rows + 2 * side
     start = pl.multiple_of(lax.axis_index("ch") * part, 16)
-    chans = cot_ref.shape[1]
-    blank = jnp.zeros((2 * side, chans), jnp.bfloat16)
+    blank = jnp.zeros((2 * side, tall.shape[1]), jnp.bfloat16)
     tall[0 : 2 * side, :] = blank
-    tall[2 * side : 2 * side + rows, :] = cot_ref[...]
+    join_halves(own_ref[...], other_ref[...], tall.at[2 * side : 2 * side + rows, :])
     tall[2 * side + rows :, :] = blank
     backs = []
     for b in range(3):
@@ -278,29 +311,32 @@
 
 
 def add_halo_kernel(side, part, tables_ref, et_ref, eu_ref, ct_ref, cu_ref, inner_ref, *refs):
-    got_refs, out_ref = refs[: len(OFFSETS)], refs[len(OFFSETS)]
+    out_ref = refs[-1]
     count = lax.axis_size("tile")
     own = lax.axis_index("tile")
     block = 4 * side + EXTRA
-    total = len(OFFSETS) * block
-    lane = lax.broadcasted_iota(jnp.int32, (1, total), 1)
-    target = jnp.full((1, total), -1, jnp.int32)
-    for index, offset in enumerate(OFFSETS):
-        source = lax.rem(own - offset + count, count)
-        for e in range(4):
-            first = index * block + e * side
-            slot = tables_ref[e, eu_ref[e, source]]
-            along = lane - first
-            along = jnp.where(slot >= 4, side - 1 - along, along)
-            hit = (lane >= first) & (lane < first + side) & (et_ref[e, source] == own)
-            target = jnp.where(hit, lax.rem(slot, 4) * side + along, target)
-            spot = corner_spot(tables_ref[4 + e, cu_ref[e, source]], side)
-            hit = (lane == index * block + 4 * side + e) & (ct_ref[e, source] == own)
-            target = jnp.where(hit, spot, target)
-    row = lax.broadcasted_iota(jnp.int32, (4 * side, total), 0)
-    place = jnp.where(row == target, 1.0, 0.0).astype(jnp.bfloat16)
-    got = jnp.concatenate([ref[...] for ref in got_refs], axis=0)
-    sums = jnp.dot(place, got, preferred_element_type=jnp.float32)
+    lane = lax.broadcasted_iota(jnp.int32, (1, block), 1)
+    row = lax.broadcasted_iota(jnp.int32, (4 * side, block), 0)
+    sums = jnp.zeros((4 * side, part), jnp.float32)
+    for ref, mask in zip(refs[:-1], (0, 2, 1, 3)):
+        for index, offset in enumerate((0, SPAN, -SPAN)):
+            if mask == 0 and offset == 0:
+                continue
+            source = lax.rem((own ^ mask) + offset + count, count)
+            target = jnp.full((1, block), -1, jnp.int32)
+            for e in range(4):
+                slot = tables_ref[e, eu_ref[e, source]]
+                along = lane - e * side
+                along = jnp.where(slot >= 4, side - 1 - along, along)
+                hit = (lane >= e * side) & (lane < (e + 1) * side) & (et_ref[e, source] == own)
+                target = jnp.where(hit, lax.rem(slot, 4) * side + along, target)
+                spot = corner_spot(tables_ref[4 + e, cu_ref[e, source]], side)
+                hit = (lane == 4 * side + e) & (ct_ref[e, source] == own)
+                target = jnp.where(hit, spot, target)
+            place = jnp.where(row == target, 1.0, 0.0).astype(jnp.bfloat16)
+            sums = sums + jnp.dot(
+                place, ref[index * block : (index + 1) * block, :], preferred_element_type=jnp.float32
+            )
     rows = side * side
     spread = lambda col: jnp.broadcast_to(col[:, None, :], (side, side, part)).reshape(rows, part)
     column = lax.broadcasted_iota(jnp.int32, (rows, part), 0) % side
@@ -341,6 +377,24 @@
     out_ref[...] = result.astype(jnp.bfloat16)
 
 
+def unfold(whole, chunk, bit, masks, blocks, before):
+    n_dep = 0 if before is None else 1
+    anywhere = pl.BlockSpec(memory_space=pl.ANY)
+    n_copies = len(masks) * len(masks[0])
+    return pl.pallas_call(
+        functools.partial(unfold_kernel, whole.shape[0], chunk, bit, masks, n_dep),
+        out_shape=whole,
+        in_specs=[anywhere] * n_dep + [pl.BlockSpec(memory_space=pltpu.VMEM)] * len(blocks),
+        out_specs=anywhere,
+        scratch_shapes=[
+            pltpu.VMEM((n_copies, chunk, whole.shape[1]), jnp.float32),
+            pltpu.SemaphoreType.DMA((n_copies,)),
+        ],
+        input_output_aliases={0: 0} if n_dep else {},
+        compiler_params=pltpu.CompilerParams(vmem_limit_bytes=40 * 1024 * 1024),
+    )(*([before] if n_dep else []), *blocks)
+
+
 def body(features, weight, cotangent, edge_tiles, edge_turns, corner_tiles, corner_turns):
     tables = jnp.asarray(turn_tables())
     count = lax.axis_size("tile")
@@ -358,17 +412,6 @@
     cot_other = lax.ppermute(cot_own, "ch", others)
     (sides,) = call(functools.partial(sides_kernel, side), [vmem((4 * side, part), jnp.bfloat16)], [field])
     near = [by_offset(sides, -offset, count) for offset in OFFSETS]
-    (cot_full,) = call(both_kernel, [vmem((rows, chans), jnp.bfloat16)], [cot_own, cot_other])
-
-    inner, pieces = call(
-        functools.partial(back_kernel, side, part),
-        [vmem((rows, part), jnp.float32), vmem((4 * side + EXTRA, part), jnp.bfloat16)],
-        [cot_full, taps],
-        scratch=[pltpu.VMEM((rows + 4 * side, chans), jnp.bfloat16)],
-        flops=2 * rows * 9 * part * chans,
-    )
-    near, inner, pieces = lax.optimization_barrier((near, inner, pieces))
-
     (halos,) = call(
         functools.partial(halo_kernel, side, part),
         [vmem((4 * side + EXTRA, part), jnp.bfloat16)],
@@ -376,65 +419,93 @@
         smem=range(5),
     )
     chunk = -(-9 * part // (16 * count)) * 16
-    (local,) = call(
+    half = count * chunk // 2
+    flops = 2 * rows * 9 * part * chans
+    held, send = call(
         functools.partial(grad_weight_kernel, side, part, chunk, 1.0 / math.sqrt(count * rows)),
-        [vmem((chunk * count, chans), jnp.float32)],
-        [field, halos, cot_full],
+        [vmem((half, chans), jnp.float32)] * 2,
+        [field, halos, cot_own, cot_other],
         scratch=[
             pltpu.VMEM((3, flat, part), jnp.bfloat16),
             pltpu.VMEM((chunk * count, chans), jnp.float32),
+            pltpu.VMEM((rows, chans), jnp.bfloat16),
         ],
-        flops=2 * rows * 9 * part * chans,
+        flops=flops,
     )
     packet = jnp.concatenate([field.reshape(rows, part), halos], axis=0)
 
     stages = mask_stages(count)
-    waiting = list(OFFSETS)
-    got_pieces = []
-    other_field = lax.ppermute(packet, "ch", others)
-    held = local
-    for index, bits in enumerate(stages):
+    send, cot_other = lax.optimization_barrier((send, cot_other))
+    got = [by_mask(send, 1, count)]
+    inner, pieces = call(
+        functools.partial(back_kernel, side, part),
+        [vmem((rows, part), jnp.float32), vmem((4 * side + EXTRA, part), jnp.bfloat16)],
+        [cot_own, cot_other, taps],
+        scratch=[pltpu.VMEM((rows + 4 * side, chans), jnp.bfloat16)],
+        flops=flops,
+    )
+    got, pieces, inner = lax.optimization_barrier((got, pieces, inner))
+    joined = []
+    for index, bits in enumerate(stages[1:]):
         masks = group_masks(bits)
-        size = held.shape[0] // len(masks)
-        kind = jnp.float32 if index == 0 else jnp.bfloat16
-        cut = [held[i * size : (i + 1) * size] for i in range(len(masks))]
-        got = [by_mask(p.astype(kind), m, count) for p, m in zip(cut[1:], masks[1:])]
-        beside = [by_offset(pieces, offset, count) for offset in waiting[:PER_STAGE[min(index, 3)]]]
-        waiting = waiting[PER_STAGE[min(index, 3)]:]
-        keep, got, beside, pieces = lax.optimization_barrier((cut[0], got, beside, pieces))
-        got_pieces += beside
-        held = keep
-        for value in got:
-            held = held + value.astype(jnp.float32)
-    held = held.astype(jnp.bfloat16)
+        n_out = len(masks)
+        size = held.shape[0] // n_out
+        outs = [vmem((size, chans), jnp.float32)] + [vmem((size, chans), jnp.bfloat16)] * (n_out - 1)
+        to_join = joined if index == 1 else []
+        if to_join:
+            outs = outs + [vmem((3 * (4 * side + EXTRA), part), jnp.bfloat16)]
+        held, *send = call(
+            functools.partial(sum_kernel, len(got), n_out, len(to_join)), outs, [held, *got, *to_join]
+        )
+        if index == 0:
+            send, pieces, packet = lax.optimization_barrier((send, pieces, packet))
+            got = [by_mask(v, m, count) for v, m in zip(send, masks[1:])]
+            other_field = lax.ppermute(packet, "ch", others)
+            joined = [pieces, by_offset(pieces, -SPAN, count), by_offset(pieces, SPAN, count)]
+            got, joined = lax.optimization_barrier((got, joined))
+        elif index == 1:
+            here = send[-1]
+            got = [by_mask(v, m, count) for v, m in zip(send[:-1], masks[1:])]
+            beside = by_mask(here, 2, count)
+            got, here, beside = lax.optimization_barrier((got, here, beside))
+        else:
+            got = [by_mask(v, m, count) for v, m in zip(send, masks[1:])]
+    (held,) = call(
+        functools.partial(sum_kernel, len(got), 1, 0), [vmem(held.shape, jnp.bfloat16)], [held, *got]
+    )
+    order = [0]
     for index, bits in enumerate(stages[:0:-1]):
         masks = group_masks(bits)
         got = [by_mask(held, m, count) for m in masks[1:]]
         if index == 0:
-            beside = [by_offset(pieces, offset, count) for offset in waiting]
-            held, got, beside, other_field = lax.optimization_barrier((held, got, beside, other_field))
-            got_pieces += beside
-        if index == len(stages) - 2:
-            (grad_features,) = call(
-                functools.partial(add_halo_kernel, side, part),
-                [vmem((rows, part), jnp.bfloat16)],
-                [*smalls, inner, *got_pieces],
-                smem=range(5),
-            )
+            got_pieces = [here, beside, by_mask(here, 1, count), by_mask(beside, 1, count)]
             (output,) = call(
                 functools.partial(output_kernel, side, part),
                 [vmem((rows, part), jnp.bfloat16)],
                 [field, halos, other_field, taps],
                 scratch=[pltpu.VMEM((3, flat, part), jnp.bfloat16)] * 2,
-                flops=2 * rows * 9 * part * chans,
+                flops=2 * flops,
             )
-            held, got, output, grad_features = lax.optimization_barrier((held, got, output, grad_features))
-        held = jnp.concatenate([held] + got, axis=0)
-    (grad_weight,) = call(
-        functools.partial(unfold_kernel, part, chunk),
-        [vmem((9 * part, chans), jnp.float32)],
-        [held, by_mask(held, 1, count)],
-    )
+            held, got, output, got_pieces = lax.optimization_barrier((held, got, output, got_pieces))
+        if index < len(stages) - 2:
+            order = [m + v for m in masks for v in order]
+            (held,) = call(
+                join_kernel, [vmem((held.shape[0] * len(masks), chans), jnp.bfloat16)], [held, *got]
+            )
+            continue
+        (grad_features,) = call(
+            functools.partial(add_halo_kernel, side, part),
+            [vmem((rows, part), jnp.bfloat16)],
+            [*smalls, inner, *got_pieces],
+            smem=range(5),
+        )
+        got = [held, *got]
+        order = [[m + v for v in order] for m in masks]
+    mates = [by_mask(v, 1, count) for v in got]
+    mates, grad_features = lax.optimization_barrier((mates, grad_features))
+    whole = vmem((9 * part, chans), jnp.float32)
+    first = unfold(whole, chunk, 0, order, got, None)
+    grad_weight = unfold(whole, chunk, 1, order, mates, first)
     shape = (1, side, side, part)
     return (
         output.reshape(shape),

time: 95 us -> 84.5 us (0.89)
  starting transfers between devices: 33.4 us -> 25.4 us
  local copies, waits for them, and re-layouts: 13.1 us -> 9.8 us
  other arithmetic: 2.4 us -> 0.1 us
  waiting for transfers between devices: 30.8 us -> 32.7 us
  Pallas kernels: 13.9 us -> 15.1 us
    ppermute x16 -> x10, starting transfers between devices: 20.6 us -> 11.4 us  [by_offset(): lax.ppermute(value, 'tile', [(i, (i + offset) % count) for i in range(cou...]
    ppermute x1, waiting for transfers between devices: 6.48 us -> 0.01 us  [body(): cot_other = lax.ppermute(cot_own, 'ch', others)]
    ppermute x10 -> x16, waiting for transfers between devices: 8.42 us -> 14 us  [by_mask(): return lax.ppermute(value, 'tile', [(i, i ^ mask) for i in range(count)])]
    ppermute x16 -> x10, waiting for transfers between devices: 15.9 us -> 18.7 us  [by_offset(): lax.ppermute(value, 'tile', [(i, (i + offset) % count) for i in range(cou...]
    pallas_call x0 -> x2, Pallas kernels: none -> 2.26 us  [unfold(): pl.pallas_call(functools.partial(unfold_kernel, whole.shape[0], chunk, bi...]
    ppermute x10 -> x16, starting transfers between devices: 8.28 us -> 10.5 us  [by_mask(): return lax.ppermute(value, 'tile', [(i, i ^ mask) for i in range(count)])]
    slice x5 -> x0, local copies, waits for them, and re-layouts: 2.01 us -> none  [body(): cut = [held[i * size:(i + 1) * size] for i in range(len(masks))]]
    concatenate x3 -> x0, local copies, waits for them, and re-layouts: 1.82 us -> none  [the longest x2 1.59 us: body(): held = jnp.concatenate([held] + got, axis=0)]
  transfers between devices with their start and end apart: 28 -> 28, of which waited for: 13 -> 10; matrix products, arithmetic and copies ran while one was open for 5% -> 2% of each run, Pallas kernels for 9% -> 13%
where the time goes in v4:
time: 84.5 us; the launch traced here: 84 us
  waiting for transfers between devices  32.7 us (39%)
  starting transfers between devices  25.4 us (30%)
  Pallas kernels  15.1 us (18%)
  local copies, waits for them, and re-layouts  9.8 us (12%)
  between operations  0.88 us (1%)
    ppermute x10, waiting for transfers between devices, by_offset(): lax.ppermute(value, 'tile', [(i, (i + offset) % count) for i in range(cou...  18.7 us
    ppermute x16, waiting for transfers between devices, by_mask(): return lax.ppermute(value, 'tile', [(i, i ^ mask) for i in range(count)])  14 us
    pallas_call x10, Pallas kernels, call(): pl.pallas_call(kernel, out_shape=tuple(outs), in_specs=in_specs, out_spec...  12.9 us
    ppermute x10, starting transfers between devices, by_offset(): lax.ppermute(value, 'tile', [(i, (i + offset) % count) for i in range(cou...  11.4 us
    ppermute x16, starting transfers between devices, by_mask(): return lax.ppermute(value, 'tile', [(i, i ^ mask) for i in range(count)])  10.5 us
    unnamed x32, local copies, waits for them, and re-layouts  8.31 us
    ppermute x1, starting transfers between devices, body(): cot_other = lax.ppermute(cot_own, 'ch', others)  3 us
    pallas_call x2, Pallas kernels, unfold(): pl.pallas_call(functools.partial(unfold_kernel, whole.shape[0], chunk, bi...  2.26 us
  transfers between devices with their start and end apart: 28, of which 10 were waited for; matrix products, arithmetic and copies ran while one was open for 2% of the time, Pallas kernels for 13%

profile of v4, /device:TPU:0, one launch (start us, length us, event | category | flops | bytes accessed | tf_op | source)
XLA Modules:
  0.0 84.0 jit_solution(17332333001941927252)
XLA Ops:
  0.6 3.0 %collective-permute-start.8 = (bf16[1024,192]{1,0:T(8,128)(2,1)}, bf16[1024,192]{1,0:T(8,128)(2,1)S(1)}, u32[]{:S(2)}, u32[]{:S(2)}) collective-permute-start(bf16[1024,192]{1,0:T(8,128)(2,1)} %bitcast.25), channel_id=1, source_target_pairs={{0,1},{1,0},{2,3},{3,2},{4,5},{5,4},{6,7},{7,6},{8,9},{9,8},{10,11... | collective-permute-start | bytes 1179656 | tf_op jit(solution)/shard_map/ppermute | solution.py:412
  3.6 1.0 %copy-done = bf16[1,32,32,192]{3,2,1,0:T(8,128)(2,1)S(1)} copy-done((bf16[1,32,32,192]{3,2,1,0:T(8,128)(2,1)S(1)}, bf16[1,32,32,192]{3,2,1,0:T(8,128)(2,1)}, u32[]{:S(2)}) %copy-start) | copy-done | bytes 393240
  4.7 3.7 %collective-permute-start.7 = (bf16[128,192]{1,0:T(8,128)(2,1)S(1)}, bf16[128,192]{1,0:T(8,128)(2,1)S(1)}, u32[]{:S(2)}, u32[]{:S(2)}) collective-permute-start(bf16[128,192]{1,0:T(8,128)(2,1)S(1)} %shard_map.103), channel_id=1, source_target_pairs={{0,24},{2,26},{4,28},{6,30},{8,0},{10,2},{12,4},{14,6},{16,8},{18,... | collective-permute-start | bytes 147464 | tf_op jit(solution)/shard_map/ppermute | solution.py:56
  8.4 1.4 %collective-permute-start.5 = (bf16[128,192]{1,0:T(8,128)(2,1)S(1)}, bf16[128,192]{1,0:T(8,128)(2,1)S(1)}, u32[]{:S(2)}, u32[]{:S(2)}) collective-permute-start(bf16[128,192]{1,0:T(8,128)(2,1)S(1)} %shard_map.103), channel_id=1, source_target_pairs={{0,28},{2,30},{4,0},{6,2},{8,4},{10,6},{12,8},{14,10},{16,12},{18,... | collective-permute-start | bytes 147464 | tf_op jit(solution)/shard_map/ppermute | solution.py:56
  9.8 1.3 %collective-permute-start.4 = (bf16[128,192]{1,0:T(8,128)(2,1)S(1)}, bf16[128,192]{1,0:T(8,128)(2,1)S(1)}, u32[]{:S(2)}, u32[]{:S(2)}) collective-permute-start(bf16[128,192]{1,0:T(8,128)(2,1)S(1)} %shard_map.103), channel_id=1, source_target_pairs={{0,30},{2,0},{4,2},{6,4},{8,6},{10,8},{12,10},{14,12},{16,14},{18,... | collective-permute-start | bytes 147464 | tf_op jit(solution)/shard_map/ppermute | solution.py:56
  11.2 1.1 %collective-permute-done.6.refs_6_ = bf16[128,192]{1,0:T(8,128)(2,1)S(1)} collective-permute-done((bf16[128,192]{1,0:T(8,128)(2,1)S(1)}, bf16[128,192]{1,0:T(8,128)(2,1)S(1)}, u32[]{:S(2)}, u32[]{:S(2)}) %collective-permute-start.6) | collective-permute-done | bytes 49184 | tf_op jit(solution)/shard_map/ppermute | solution.py:56
  12.2 2.4 %collective-permute-start.2 = (bf16[128,192]{1,0:T(8,128)(2,1)S(1)}, bf16[128,192]{1,0:T(8,128)(2,1)S(1)}, u32[]{:S(2)}, u32[]{:S(2)}) collective-permute-start(bf16[128,192]{1,0:T(8,128)(2,1)S(1)} %shard_map.103), channel_id=1, source_target_pairs={{0,4},{2,6},{4,8},{6,10},{8,12},{10,14},{12,16},{14,18},{16,20},{1... | collective-permute-start | bytes 147464 | tf_op jit(solution)/shard_map/ppermute | solution.py:56
  14.6 0.9 %collective-permute-start.1 = (bf16[128,192]{1,0:T(8,128)(2,1)S(1)}, bf16[128,192]{1,0:T(8,128)(2,1)S(1)}, u32[]{:S(2)}, u32[]{:S(2)}) collective-permute-start(bf16[128,192]{1,0:T(8,128)(2,1)S(1)} %shard_map.103), channel_id=1, source_target_pairs={{0,6},{2,8},{4,10},{6,12},{8,14},{10,16},{12,18},{14,20},{16,22},{... | collective-permute-start | bytes 147464 | tf_op jit(solution)/shard_map/ppermute | solution.py:56
  15.6 2.0 %collective-permute-done.3.refs_3_ = bf16[128,192]{1,0:T(8,128)(2,1)S(1)} collective-permute-done((bf16[128,192]{1,0:T(8,128)(2,1)S(1)}, bf16[128,192]{1,0:T(8,128)(2,1)S(1)}, u32[]{:S(2)}, u32[]{:S(2)}) %collective-permute-start.3) | collective-permute-done | bytes 49184 | tf_op jit(solution)/shard_map/ppermute | solution.py:56
  17.5 1.7 %collective-permute-done.2.refs_2_ = bf16[128,192]{1,0:T(8,128)(2,1)S(1)} collective-permute-done((bf16[128,192]{1,0:T(8,128)(2,1)S(1)}, bf16[128,192]{1,0:T(8,128)(2,1)S(1)}, u32[]{:S(2)}, u32[]{:S(2)}) %collective-permute-start.2) | collective-permute-done | bytes 49184 | tf_op jit(solution)/shard_map/ppermute | solution.py:56
  19.2 0.9 %collective-permute-done.1.refs_1_ = bf16[128,192]{1,0:T(8,128)(2,1)S(1)} collective-permute-done((bf16[128,192]{1,0:T(8,128)(2,1)S(1)}, bf16[128,192]{1,0:T(8,128)(2,1)S(1)}, u32[]{:S(2)}, u32[]{:S(2)}) %collective-permute-start.1) | collective-permute-done | bytes 49184 | tf_op jit(solution)/shard_map/ppermute | solution.py:56
  20.1 1.5 %collective-permute-done.refs_0_ = bf16[128,192]{1,0:T(8,128)(2,1)S(1)} collective-permute-done((bf16[128,192]{1,0:T(8,128)(2,1)S(1)}, bf16[128,192]{1,0:T(8,128)(2,1)S(1)}, u32[]{:S(2)}, u32[]{:S(2)}) %collective-permute-start) | collective-permute-done | bytes 49184 | tf_op jit(solution)/shard_map/ppermute | solution.py:56
  21.6 0.7 copy-done.3
  22.3 0.7 copy-done.5
  23.0 0.7 copy-done.7
  23.7 0.7 copy-done.9
  24.4 0.7 copy-done.11
  25.1 1.0 %shard_map.104.halos_ref = bf16[144,192]{1,0:T(8,128)(2,1)S(1)} custom-call(s32[8,4]{1,0:T(8,128)S(1)} %copy-done.3, s32[4,16]{1,0:T(4,128)S(1)} %bitcast.15, s32[4,16]{1,0:T(4,128)S(1)} %bitcast.17, s32[4,16]{1,0:T(4,128)S(1)} %bitcast.19, s32[4,16]{1,0:T(4,128)S(1)} %bitcast.21, bf16[128,192]{1,0:T(8,128)(2,1)S(1)} %collective-permute-done.refs_0_, ...), custom_call_target="tpu_custom_call" | custom-call | bytes 449664 | tf_op jit(solution)/shard_map/pallas_call | solution.py:103
  26.1 1.0 %copy-done.1 = bf16[1,32,32,192]{3,2,1,0:T(8,128)(2,1)S(1)} copy-done((bf16[1,32,32,192]{3,2,1,0:T(8,128)(2,1)S(1)}, bf16[1,32,32,192]{3,2,1,0:T(8,128)(2,1)}, u32[]{:S(2)}) %copy-start.1) | copy-done | bytes 393240
  27.1 1.0 %copy-done.15 = bf16[1,32,32,192]{3,2,1,0:T(8,128)(2,1)S(1)} copy-done((bf16[1,32,32,192]{3,2,1,0:T(8,128)(2,1)S(1)}, bf16[1,32,32,192]{3,2,1,0:T(8,128)(2,1)}, u32[]{:S(2)}) %copy-start.15) | copy-done | bytes 393240
  28.2 2.7 %shard_map.105 = (f32[896,384]{1,0:T(8,128)S(1)}, f32[896,384]{1,0:T(8,128)S(1)}) custom-call(bf16[32,32,192]{2,1,0:T(8,128)(2,1)S(1)} %bitcast.12, bf16[144,192]{1,0:T(8,128)(2,1)S(1)} %shard_map.104.halos_ref, bf16[1024,192]{1,0:T(8,128)(2,1)S(1)} %bitcast.26, bf16[1024,192]{1,0:T(8,128)(2,1)S(1)} %collective-permute-done.8.other_ref), custom_call_target="tpu_custom_call" | custom-call | flops 1358954496 | bytes 3987456 | tf_op jit(solution)/shard_map/pallas_call | solution.py:103
  30.9 0.1 pad_maximum_fusion
  31.0 3.1 %shard_map.106 = (f32[1024,192]{1,0:T(8,128)S(1)}, bf16[144,192]{1,0:T(8,128)(2,1)S(1)}) custom-call(bf16[1024,192]{1,0:T(8,128)(2,1)S(1)} %bitcast.27, bf16[1024,192]{1,0:T(8,128)(2,1)S(1)} %collective-permute-done.8.other_ref, bf16[9,384,384]{2,1,0:T(8,128)(2,1)S(1)} %bitcast.23), custom_call_target="tpu_custom_call" | custom-call | flops 1358954496 | bytes 4282368 | tf_op jit(solution)/shard_map/pallas_call | solution.py:103
  34.1 0.1 shard_map.107
  34.3 0.2 copy.15
  34.5 0.5 collective-permute-start.18
  35.1 1.6 %collective-permute-start.10 = (bf16[224,384]{1,0:T(8,128)(2,1)S(1)}, bf16[224,384]{1,0:T(8,128)(2,1)S(1)}, u32[]{:S(2)}, u32[]{:S(2)}) collective-permute-start(bf16[224,384]{1,0:T(8,128)(2,1)S(1)} %get-tuple-element.57), channel_id=1, source_target_pairs={{0,4},{2,6},{4,0},{6,2},{8,12},{10,14},{12,8},{14,10},{16,20},{18,... | collective-permute-start | bytes 516104 | tf_op jit(solution)/shard_map/ppermute | solution.py:60
  36.7 1.9 %collective-permute-start.12 = (bf16[224,384]{1,0:T(8,128)(2,1)S(1)}, bf16[224,384]{1,0:T(8,128)(2,1)S(1)}, u32[]{:S(2)}, u32[]{:S(2)}) collective-permute-start(bf16[224,384]{1,0:T(8,128)(2,1)S(1)} %get-tuple-element.59), channel_id=1, source_target_pairs={{0,12},{2,14},{4,8},{6,10},{8,4},{10,6},{12,0},{14,2},{16,28},{18,... | collective-permute-start | bytes 516104 | tf_op jit(solution)/shard_map/ppermute | solution.py:60
  38.6 0.2 collective-permute-start.14
  38.7 8.6 %collective-permute-done.14.refs_6_ = bf16[144,192]{1,0:T(8,128)(2,1)S(1)} collective-permute-done((bf16[144,192]{1,0:T(8,128)(2,1)S(1)}, bf16[144,192]{1,0:T(8,128)(2,1)S(1)}, u32[]{:S(2)}, u32[]{:S(2)}) %collective-permute-start.14) | collective-permute-done | bytes 55328 | tf_op jit(solution)/shard_map/ppermute | solution.py:56
  47.4 1.4 %collective-permute-start.13 = (bf16[144,192]{1,0:T(8,128)(2,1)S(1)}, bf16[144,192]{1,0:T(8,128)(2,1)S(1)}, u32[]{:S(2)}, u32[]{:S(2)}) collective-permute-start(bf16[144,192]{1,0:T(8,128)(2,1)S(1)} %get-tuple-element.64.refs_4_), channel_id=1, source_target_pairs={{0,24},{2,26},{4,28},{6,30},{8,0},{10,2},{12,4},{14,6},{16,8},{18,... | collective-permute-start | bytes 165896 | tf_op jit(solution)/shard_map/ppermute | solution.py:56
  48.8 2.9 %collective-permute-done.13.refs_5_ = bf16[144,192]{1,0:T(8,128)(2,1)S(1)} collective-permute-done((bf16[144,192]{1,0:T(8,128)(2,1)S(1)}, bf16[144,192]{1,0:T(8,128)(2,1)S(1)}, u32[]{:S(2)}, u32[]{:S(2)}) %collective-permute-start.13) | collective-permute-done | bytes 55328 | tf_op jit(solution)/shard_map/ppermute | solution.py:56
  51.7 0.1 shard_map.108
  51.8 1.3 %collective-permute-start.16 = (bf16[432,192]{1,0:T(8,128)(2,1)S(1)}, bf16[432,192]{1,0:T(8,128)(2,1)S(1)}, u32[]{:S(2)}, u32[]{:S(2)}) collective-permute-start(bf16[432,192]{1,0:T(8,128)(2,1)S(1)} %get-tuple-element.78.refs_0_), channel_id=1, source_target_pairs={{0,4},{2,6},{4,0},{6,2},{8,12},{10,14},{12,8},{14,10},{16,20},{18,... | collective-permute-start | bytes 497672 | tf_op jit(solution)/shard_map/ppermute | solution.py:60
  53.1 7.2 %collective-permute-done.15.refs_1_ = bf16[112,384]{1,0:T(8,128)(2,1)S(1)} collective-permute-done((bf16[112,384]{1,0:T(8,128)(2,1)S(1)}, bf16[112,384]{1,0:T(8,128)(2,1)S(1)}, u32[]{:S(2)}, u32[]{:S(2)}) %collective-permute-start.15) | collective-permute-done | bytes 86048 | tf_op jit(solution)/shard_map/ppermute | solution.py:60
  60.5 0.5 collective-permute-start.20
  61.0 1.3 %copy.16.other_ref = bf16[1168,192]{1,0:T(8,128)(2,1)S(1)} copy(bf16[1168,192]{0,1:T(8,128)(2,1)} %collective-permute-done.18) | data formatting | bytes 897024 | tf_op jit(solution)/shard_map/ppermute | solution.py:463
  62.3 1.7 %copy-done.14 = bf16[3,3,384,384]{3,2,1,0:T(8,128)(2,1)S(1)} copy-done((bf16[3,3,384,384]{3,2,1,0:T(8,128)(2,1)S(1)}, bf16[3,3,384,384]{3,2,1,0:T(8,128)(2,1)}, u32[]{:S(2)}) %copy-start.14) | copy-done | bytes 2654232
  64.0 3.5 %shard_map.110 = bf16[1024,192]{1,0:T(8,128)(2,1)} custom-call(bf16[32,32,192]{2,1,0:T(8,128)(2,1)S(1)} %bitcast.14, bf16[144,192]{1,0:T(8,128)(2,1)S(1)} %shard_map.104.halos_ref, bf16[1168,192]{1,0:T(8,128)(2,1)S(1)} %copy.16.other_ref, bf16[9,384,384]{2,1,0:T(8,128)(2,1)S(1)} %bitcast.24), custom_call_target="tpu_custom_call" | custom-call | flops 2717908992 | bytes 3944448 | tf_op jit(solution)/shard_map/pallas_call | solution.py:103
  67.6 2.9 %collective-permute-start.26 = (bf16[224,384]{1,0:T(8,128)(2,1)S(1)}, bf16[224,384]{1,0:T(8,128)(2,1)S(1)}, u32[]{:S(2)}, u32[]{:S(2)}) collective-permute-start(bf16[224,384]{1,0:T(8,128)(2,1)S(1)} %shard_map.111.refs_0_), channel_id=1, source_target_pairs={{0,12},{2,14},{4,8},{6,10},{8,4},{10,6},{12,0},{14,2},{16,28},{18,... | collective-permute-start | bytes 516104 | tf_op jit(solution)/shard_map/ppermute | solution.py:60
  70.5 0.2 collective-permute-start.24
  70.7 1.4 %collective-permute-start.22 = (bf16[224,384]{1,0:T(8,128)(2,1)S(1)}, bf16[224,384]{1,0:T(8,128)(2,1)S(1)}, u32[]{:S(2)}, u32[]{:S(2)}) collective-permute-start(bf16[224,384]{1,0:T(8,128)(2,1)S(1)} %shard_map.111.refs_0_), channel_id=1, source_target_pairs={{0,4},{2,6},{4,0},{6,2},{8,12},{10,14},{12,8},{14,10},{16,20},{18,... | collective-permute-start | bytes 516104 | tf_op jit(solution)/shard_map/ppermute | solution.py:60
  72.1 3.7 %collective-permute-done.26.refs_3_ = bf16[224,384]{1,0:T(8,128)(2,1)S(1)} collective-permute-done((bf16[224,384]{1,0:T(8,128)(2,1)S(1)}, bf16[224,384]{1,0:T(8,128)(2,1)S(1)}, u32[]{:S(2)}, u32[]{:S(2)}) %collective-permute-start.26) | collective-permute-done | bytes 172064 | tf_op jit(solution)/shard_map/ppermute | solution.py:60
  75.8 3.1 %collective-permute-done.24.refs_2_ = bf16[224,384]{1,0:T(8,128)(2,1)S(1)} collective-permute-done((bf16[224,384]{1,0:T(8,128)(2,1)S(1)}, bf16[224,384]{1,0:T(8,128)(2,1)S(1)}, u32[]{:S(2)}, u32[]{:S(2)}) %collective-permute-start.24) | collective-permute-done | bytes 172064 | tf_op jit(solution)/shard_map/ppermute | solution.py:60
  78.9 0.5 collective-permute-start.23
  79.4 2.3 %shard_map.112 = bf16[1024,192]{1,0:T(8,128)(2,1)} custom-call(s32[8,4]{1,0:T(8,128)S(1)} %copy-done.4, s32[4,16]{1,0:T(4,128)S(1)} %bitcast.16, s32[4,16]{1,0:T(4,128)S(1)} %bitcast.18, s32[4,16]{1,0:T(4,128)S(1)} %bitcast.20, s32[4,16]{1,0:T(4,128)S(1)} %bitcast.22, f32[1024,192]{1,0:T(8,128)S(1)} %get-tuple-element.77.inner_ref, ...), custom_call_target="tpu_custom_call" | custom-call | bytes 1844352 | tf_op jit(solution)/shard_map/pallas_call | solution.py:103
  81.7 1.1 %shard_map.113.refs_0_ = f32[1728,384]{1,0:T(8,128)} custom-call(bf16[224,384]{1,0:T(8,128)(2,1)S(1)} %shard_map.111.refs_0_, bf16[224,384]{1,0:T(8,128)(2,1)S(1)} %collective-permute-done.22.refs_1_, bf16[224,384]{1,0:T(8,128)(2,1)S(1)} %collective-permute-done.24.refs_2_, bf16[224,384]{1,0:T(8,128)(2,1)S(1)} %collective-permute-done.26.refs_3_), custom_call_target="tpu_custom_call" | custom-call | tf_op jit(solution)/shard_map/pallas_call | solution.py:384
  82.9 1.1 %shard_map.114 = f32[1728,384]{1,0:T(8,128)} custom-call(f32[1728,384]{1,0:T(8,128)} %shard_map.113.refs_0_, bf16[224,384]{1,0:T(8,128)(2,1)S(1)} %collective-permute-done.21.refs_1_, bf16[224,384]{1,0:T(8,128)(2,1)S(1)} %collective-permute-done.23.refs_2_, bf16[224,384]{1,0:T(8,128)(2,1)S(1)} %collective-permute-done.25.refs_3_, ...), custom_call_target="tpu_custom_call", output_to_operand_aliasing={{}: (0, {})} | custom-call | tf_op jit(solution)/shard_map/pallas_call | solution.py:384
  (55 shorter events, 0.4 us)
Async XLA Ops:
  0.6 25.4 %collective-permute-start.8 = (bf16[1024,192]{1,0:T(8,128)(2,1)}, bf16[1024,192]{1,0:T(8,128)(2,1)S(1)}, u32[]{:S(2)}, u32[]{:S(2)}) collective-permute-start(bf16[1024,192]{1,0:T(8,128)(2,1)} %bitcast.25), channel_id=1, source_target_pairs={{0,1},{1,0},{2,3},{3,2},{4,5},{5,4},{6,7},{7,6},{8,9},{9,8},{10,11... | collective-permute-start | bytes 1179656 | tf_op jit(solution)/shard_map/ppermute | solution.py:412
  3.6 1.0 %copy-start = (bf16[1,32,32,192]{3,2,1,0:T(8,128)(2,1)S(1)}, bf16[1,32,32,192]{3,2,1,0:T(8,128)(2,1)}, u32[]{:S(2)}) copy-start(bf16[1,32,32,192]{3,2,1,0:T(8,128)(2,1)} %param.8) | copy-start | bytes 1179652
  4.7 6.4 %collective-permute-start.7 = (bf16[128,192]{1,0:T(8,128)(2,1)S(1)}, bf16[128,192]{1,0:T(8,128)(2,1)S(1)}, u32[]{:S(2)}, u32[]{:S(2)}) collective-permute-start(bf16[128,192]{1,0:T(8,128)(2,1)S(1)} %shard_map.103), channel_id=1, source_target_pairs={{0,24},{2,26},{4,28},{6,30},{8,0},{10,2},{12,4},{14,6},{16,8},{18,... | collective-permute-start | bytes 147464 | tf_op jit(solution)/shard_map/ppermute | solution.py:56
  8.4 3.8 %collective-permute-start.6 = (bf16[128,192]{1,0:T(8,128)(2,1)S(1)}, bf16[128,192]{1,0:T(8,128)(2,1)S(1)}, u32[]{:S(2)}, u32[]{:S(2)}) collective-permute-start(bf16[128,192]{1,0:T(8,128)(2,1)S(1)} %shard_map.103), channel_id=1, source_target_pairs={{0,26},{2,28},{4,30},{6,0},{8,2},{10,4},{12,6},{14,8},{16,10},{18,... | collective-permute-start | bytes 147464 | tf_op jit(solution)/shard_map/ppermute | solution.py:56
  8.4 6.3 %collective-permute-start.5 = (bf16[128,192]{1,0:T(8,128)(2,1)S(1)}, bf16[128,192]{1,0:T(8,128)(2,1)S(1)}, u32[]{:S(2)}, u32[]{:S(2)}) collective-permute-start(bf16[128,192]{1,0:T(8,128)(2,1)S(1)} %shard_map.103), channel_id=1, source_target_pairs={{0,28},{2,30},{4,0},{6,2},{8,4},{10,6},{12,8},{14,10},{16,12},{18,... | collective-permute-start | bytes 147464 | tf_op jit(solution)/shard_map/ppermute | solution.py:56
  9.8 5.8 %collective-permute-start.4 = (bf16[128,192]{1,0:T(8,128)(2,1)S(1)}, bf16[128,192]{1,0:T(8,128)(2,1)S(1)}, u32[]{:S(2)}, u32[]{:S(2)}) collective-permute-start(bf16[128,192]{1,0:T(8,128)(2,1)S(1)} %shard_map.103), channel_id=1, source_target_pairs={{0,30},{2,0},{4,2},{6,4},{8,6},{10,8},{12,10},{14,12},{16,14},{18,... | collective-permute-start | bytes 147464 | tf_op jit(solution)/shard_map/ppermute | solution.py:56
  11.1 6.4 %collective-permute-start.3 = (bf16[128,192]{1,0:T(8,128)(2,1)S(1)}, bf16[128,192]{1,0:T(8,128)(2,1)S(1)}, u32[]{:S(2)}, u32[]{:S(2)}) collective-permute-start(bf16[128,192]{1,0:T(8,128)(2,1)S(1)} %shard_map.103), channel_id=1, source_target_pairs={{0,2},{2,4},{4,6},{6,8},{8,10},{10,12},{12,14},{14,16},{16,18},{18... | collective-permute-start | bytes 147464 | tf_op jit(solution)/shard_map/ppermute | solution.py:56
  12.2 7.0 %collective-permute-start.2 = (bf16[128,192]{1,0:T(8,128)(2,1)S(1)}, bf16[128,192]{1,0:T(8,128)(2,1)S(1)}, u32[]{:S(2)}, u32[]{:S(2)}) collective-permute-start(bf16[128,192]{1,0:T(8,128)(2,1)S(1)} %shard_map.103), channel_id=1, source_target_pairs={{0,4},{2,6},{4,8},{6,10},{8,12},{10,14},{12,16},{14,18},{16,20},{1... | collective-permute-start | bytes 147464 | tf_op jit(solution)/shard_map/ppermute | solution.py:56
  14.6 5.5 %collective-permute-start.1 = (bf16[128,192]{1,0:T(8,128)(2,1)S(1)}, bf16[128,192]{1,0:T(8,128)(2,1)S(1)}, u32[]{:S(2)}, u32[]{:S(2)}) collective-permute-start(bf16[128,192]{1,0:T(8,128)(2,1)S(1)} %shard_map.103), channel_id=1, source_target_pairs={{0,6},{2,8},{4,10},{6,12},{8,14},{10,16},{12,18},{14,20},{16,22},{... | collective-permute-start | bytes 147464 | tf_op jit(solution)/shard_map/ppermute | solution.py:56
  15.6 6.1 %collective-permute-start = (bf16[128,192]{1,0:T(8,128)(2,1)S(1)}, bf16[128,192]{1,0:T(8,128)(2,1)S(1)}, u32[]{:S(2)}, u32[]{:S(2)}) collective-permute-start(bf16[128,192]{1,0:T(8,128)(2,1)S(1)} %shard_map.103), channel_id=1, source_target_pairs={{0,8},{2,10},{4,12},{6,14},{8,16},{10,18},{12,20},{14,22},{16,24},... | collective-permute-start | bytes 147464 | tf_op jit(solution)/shard_map/ppermute | solution.py:56
  21.6 0.7 copy-start.3
  22.3 0.7 copy-start.5
  23.0 0.7 copy-start.7
  23.7 0.7 copy-start.9
  24.4 0.7 copy-start.11
  26.1 1.0 %copy-start.1 = (bf16[1,32,32,192]{3,2,1,0:T(8,128)(2,1)S(1)}, bf16[1,32,32,192]{3,2,1,0:T(8,128)(2,1)}, u32[]{:S(2)}) copy-start(bf16[1,32,32,192]{3,2,1,0:T(8,128)(2,1)} %param.8) | copy-start | bytes 1179652
  27.1 1.0 %copy-start.15 = (bf16[1,32,32,192]{3,2,1,0:T(8,128)(2,1)S(1)}, bf16[1,32,32,192]{3,2,1,0:T(8,128)(2,1)}, u32[]{:S(2)}) copy-start(bf16[1,32,32,192]{3,2,1,0:T(8,128)(2,1)} %param.10) | copy-start | bytes 1179652
  28.1 2.9 %copy-start.13 = (bf16[3,3,384,384]{3,2,1,0:T(8,128)(2,1)S(1)}, bf16[3,3,384,384]{3,2,1,0:T(8,128)(2,1)}, u32[]{:S(2)}) copy-start(bf16[3,3,384,384]{3,2,1,0:T(8,128)(2,1)} %param.9) | copy-start | bytes 7962628
  30.8 3.3 %collective-permute-start.9 = (f32[896,384]{1,0:T(8,128)S(1)}, f32[896,384]{1,0:T(8,128)S(1)}, u32[]{:S(2)}, u32[]{:S(2)}) collective-permute-start(f32[896,384]{1,0:T(8,128)S(1)} %get-tuple-element.47), channel_id=1, source_target_pairs={{0,2},{2,0},{4,6},{6,4},{8,10},{10,8},{12,14},{14,12},{16,18},{18,... | collective-permute-start | bytes 4128776 | tf_op jit(solution)/shard_map/ppermute | solution.py:60
  34.5 27.7 %copy-start.2 = (bf16[1,32,32,192]{3,2,1,0:T(8,128)(2,1)S(1)}, bf16[1,32,32,192]{3,2,1,0:T(8,128)(2,1)}, u32[]{:S(2)}) copy-start(bf16[1,32,32,192]{3,2,1,0:T(8,128)(2,1)} %param.8) | copy-start | bytes 1179652
  34.5 26.4 %collective-permute-start.18 = (bf16[1168,192]{0,1:T(8,128)(2,1)S(1)}, bf16[1168,192]{0,1:T(8,128)(2,1)}, u32[]{:S(2)}, u32[]{:S(2)}) collective-permute-start(bf16[1168,192]{0,1:T(8,128)(2,1)S(1)} %copy.15), channel_id=1, source_target_pairs={{0,1},{1,0},{2,3},{3,2},{4,5},{5,4},{6,7},{7,6},{8,9},{9,8},{10,11... | collective-permute-start | bytes 1345544 | tf_op jit(solution)/shard_map/ppermute | solution.py:463
  35.1 16.7 %collective-permute-start.10 = (bf16[224,384]{1,0:T(8,128)(2,1)S(1)}, bf16[224,384]{1,0:T(8,128)(2,1)S(1)}, u32[]{:S(2)}, u32[]{:S(2)}) collective-permute-start(bf16[224,384]{1,0:T(8,128)(2,1)S(1)} %get-tuple-element.57), channel_id=1, source_target_pairs={{0,4},{2,6},{4,0},{6,2},{8,12},{10,14},{12,8},{14,10},{16,20},{18,... | collective-permute-start | bytes 516104 | tf_op jit(solution)/shard_map/ppermute | solution.py:60
  36.7 15.0 %collective-permute-start.11 = (bf16[224,384]{1,0:T(8,128)(2,1)S(1)}, bf16[224,384]{1,0:T(8,128)(2,1)S(1)}, u32[]{:S(2)}, u32[]{:S(2)}) collective-permute-start(bf16[224,384]{1,0:T(8,128)(2,1)S(1)} %get-tuple-element.58), channel_id=1, source_target_pairs={{0,8},{2,10},{4,12},{6,14},{8,0},{10,2},{12,4},{14,6},{16,24},{18,... | collective-permute-start | bytes 516104 | tf_op jit(solution)/shard_map/ppermute | solution.py:60
  36.7 15.0 %collective-permute-start.12 = (bf16[224,384]{1,0:T(8,128)(2,1)S(1)}, bf16[224,384]{1,0:T(8,128)(2,1)S(1)}, u32[]{:S(2)}, u32[]{:S(2)}) collective-permute-start(bf16[224,384]{1,0:T(8,128)(2,1)S(1)} %get-tuple-element.59), channel_id=1, source_target_pairs={{0,12},{2,14},{4,8},{6,10},{8,4},{10,6},{12,0},{14,2},{16,28},{18,... | collective-permute-start | bytes 516104 | tf_op jit(solution)/shard_map/ppermute | solution.py:60
  38.6 8.8 %collective-permute-start.14 = (bf16[144,192]{1,0:T(8,128)(2,1)S(1)}, bf16[144,192]{1,0:T(8,128)(2,1)S(1)}, u32[]{:S(2)}, u32[]{:S(2)}) collective-permute-start(bf16[144,192]{1,0:T(8,128)(2,1)S(1)} %get-tuple-element.64.refs_4_), channel_id=1, source_target_pairs={{0,8},{2,10},{4,12},{6,14},{8,16},{10,18},{12,20},{14,22},{16,24},... | collective-permute-start | bytes 165896 | tf_op jit(solution)/shard_map/ppermute | solution.py:56
  47.4 4.4 %collective-permute-start.13 = (bf16[144,192]{1,0:T(8,128)(2,1)S(1)}, bf16[144,192]{1,0:T(8,128)(2,1)S(1)}, u32[]{:S(2)}, u32[]{:S(2)}) collective-permute-start(bf16[144,192]{1,0:T(8,128)(2,1)S(1)} %get-tuple-element.64.refs_4_), channel_id=1, source_target_pairs={{0,24},{2,26},{4,28},{6,30},{8,0},{10,2},{12,4},{14,6},{16,8},{18,... | collective-permute-start | bytes 165896 | tf_op jit(solution)/shard_map/ppermute | solution.py:56
  51.8 8.4 %collective-permute-start.16 = (bf16[432,192]{1,0:T(8,128)(2,1)S(1)}, bf16[432,192]{1,0:T(8,128)(2,1)S(1)}, u32[]{:S(2)}, u32[]{:S(2)}) collective-permute-start(bf16[432,192]{1,0:T(8,128)(2,1)S(1)} %get-tuple-element.78.refs_0_), channel_id=1, source_target_pairs={{0,4},{2,6},{4,0},{6,2},{8,12},{10,14},{12,8},{14,10},{16,20},{18,... | collective-permute-start | bytes 497672 | tf_op jit(solution)/shard_map/ppermute | solution.py:60
  53.1 7.2 %collective-permute-start.15 = (bf16[112,384]{1,0:T(8,128)(2,1)S(1)}, bf16[112,384]{1,0:T(8,128)(2,1)S(1)}, u32[]{:S(2)}, u32[]{:S(2)}) collective-permute-start(bf16[112,384]{1,0:T(8,128)(2,1)S(1)} %get-tuple-element.68), channel_id=1, source_target_pairs={{0,16},{2,18},{4,20},{6,22},{8,24},{10,26},{12,28},{14,30},{16,0},... | collective-permute-start | bytes 258056 | tf_op jit(solution)/shard_map/ppermute | solution.py:60
  60.3 7.3 %collective-permute-start.17 = (bf16[112,384]{1,0:T(8,128)(2,1)S(1)}, bf16[112,384]{1,0:T(8,128)(2,1)S(1)}, u32[]{:S(2)}, u32[]{:S(2)}) collective-permute-start(bf16[112,384]{1,0:T(8,128)(2,1)S(1)} %shard_map.109.refs_0_), channel_id=1, source_target_pairs={{0,16},{2,18},{4,20},{6,22},{8,24},{10,26},{12,28},{14,30},{16,0},... | collective-permute-start | bytes 258056 | tf_op jit(solution)/shard_map/ppermute | solution.py:60
  60.4 7.2 %collective-permute-start.19 = (bf16[432,192]{1,0:T(8,128)(2,1)S(1)}, bf16[432,192]{1,0:T(8,128)(2,1)S(1)}, u32[]{:S(2)}, u32[]{:S(2)}) collective-permute-start(bf16[432,192]{1,0:T(8,128)(2,1)S(1)} %get-tuple-element.78.refs_0_), channel_id=1, source_target_pairs={{0,2},{2,0},{4,6},{6,4},{8,10},{10,8},{12,14},{14,12},{16,18},{18,... | collective-permute-start | bytes 497672 | tf_op jit(solution)/shard_map/ppermute | solution.py:60
  60.5 7.1 %collective-permute-start.20 = (bf16[432,192]{1,0:T(8,128)(2,1)S(1)}, bf16[432,192]{1,0:T(8,128)(2,1)S(1)}, u32[]{:S(2)}, u32[]{:S(2)}) collective-permute-start(bf16[432,192]{1,0:T(8,128)(2,1)S(1)} %collective-permute-done.16.refs_1_), channel_id=1, source_target_pairs={{0,2},{2,0},{4,6},{6,4},{8,10},{10,8},{12,14},{14,12},{16,18},{18,... | collective-permute-start | bytes 497672 | tf_op jit(solution)/shard_map/ppermute | solution.py:60
  62.2 1.8 %copy-start.14 = (bf16[3,3,384,384]{3,2,1,0:T(8,128)(2,1)S(1)}, bf16[3,3,384,384]{3,2,1,0:T(8,128)(2,1)}, u32[]{:S(2)}) copy-start(bf16[3,3,384,384]{3,2,1,0:T(8,128)(2,1)} %param.9) | copy-start | bytes 7962628
  64.0 15.4 %copy-start.4 = (s32[8,4]{1,0:T(8,128)S(1)}, s32[8,4]{1,0:T(8,128)}, u32[]{:S(2)}) copy-start(s32[8,4]{1,0:T(8,128)} %constant.2.clone.tables_ref) | copy-start | bytes 388
  64.0 15.4 %copy-start.6 = (s32[16,4]{0,1:T(4,128)S(1)}, s32[16,4]{0,1:T(4,128)}, u32[]{:S(2)}) copy-start(s32[16,4]{0,1:T(4,128)} %param.11) | copy-start | bytes 772
  64.0 15.4 %copy-start.8 = (s32[16,4]{0,1:T(4,128)S(1)}, s32[16,4]{0,1:T(4,128)}, u32[]{:S(2)}) copy-start(s32[16,4]{0,1:T(4,128)} %param.12) | copy-start | bytes 772
  64.0 15.4 %copy-start.10 = (s32[16,4]{0,1:T(4,128)S(1)}, s32[16,4]{0,1:T(4,128)}, u32[]{:S(2)}) copy-start(s32[16,4]{0,1:T(4,128)} %param.13) | copy-start | bytes 772
  64.0 15.4 %copy-start.12 = (s32[16,4]{0,1:T(4,128)S(1)}, s32[16,4]{0,1:T(4,128)}, u32[]{:S(2)}) copy-start(s32[16,4]{0,1:T(4,128)} %param.14) | copy-start | bytes 772
  67.6 8.2 %collective-permute-start.26 = (bf16[224,384]{1,0:T(8,128)(2,1)S(1)}, bf16[224,384]{1,0:T(8,128)(2,1)S(1)}, u32[]{:S(2)}, u32[]{:S(2)}) collective-permute-start(bf16[224,384]{1,0:T(8,128)(2,1)S(1)} %shard_map.111.refs_0_), channel_id=1, source_target_pairs={{0,12},{2,14},{4,8},{6,10},{8,4},{10,6},{12,0},{14,2},{16,28},{18,... | collective-permute-start | bytes 516104 | tf_op jit(solution)/shard_map/ppermute | solution.py:60
  70.5 8.4 %collective-permute-start.24 = (bf16[224,384]{1,0:T(8,128)(2,1)S(1)}, bf16[224,384]{1,0:T(8,128)(2,1)S(1)}, u32[]{:S(2)}, u32[]{:S(2)}) collective-permute-start(bf16[224,384]{1,0:T(8,128)(2,1)S(1)} %shard_map.111.refs_0_), channel_id=1, source_target_pairs={{0,8},{2,10},{4,12},{6,14},{8,0},{10,2},{12,4},{14,6},{16,24},{18,... | collective-permute-start | bytes 516104 | tf_op jit(solution)/shard_map/ppermute | solution.py:60
  70.7 8.2 %collective-permute-start.22 = (bf16[224,384]{1,0:T(8,128)(2,1)S(1)}, bf16[224,384]{1,0:T(8,128)(2,1)S(1)}, u32[]{:S(2)}, u32[]{:S(2)}) collective-permute-start(bf16[224,384]{1,0:T(8,128)(2,1)S(1)} %shard_map.111.refs_0_), channel_id=1, source_target_pairs={{0,4},{2,6},{4,0},{6,2},{8,12},{10,14},{12,8},{14,10},{16,20},{18,... | collective-permute-start | bytes 516104 | tf_op jit(solution)/shard_map/ppermute | solution.py:60
  72.1 10.7 %collective-permute-start.21 = (bf16[224,384]{1,0:T(8,128)(2,1)S(1)}, bf16[224,384]{1,0:T(8,128)(2,1)S(1)}, u32[]{:S(2)}, u32[]{:S(2)}) collective-permute-start(bf16[224,384]{1,0:T(8,128)(2,1)S(1)} %shard_map.111.refs_0_), channel_id=1, source_target_pairs={{0,2},{2,0},{4,6},{6,4},{8,10},{10,8},{12,14},{14,12},{16,18},{18,... | collective-permute-start | bytes 516104 | tf_op jit(solution)/shard_map/ppermute | solution.py:60
  75.8 7.1 %collective-permute-start.27 = (bf16[224,384]{1,0:T(8,128)(2,1)S(1)}, bf16[224,384]{1,0:T(8,128)(2,1)S(1)}, u32[]{:S(2)}, u32[]{:S(2)}) collective-permute-start(bf16[224,384]{1,0:T(8,128)(2,1)S(1)} %collective-permute-done.26.refs_3_), channel_id=1, source_target_pairs={{0,2},{2,0},{4,6},{6,4},{8,10},{10,8},{12,14},{14,12},{16,18},{18,... | collective-permute-start | bytes 516104 | tf_op jit(solution)/shard_map/ppermute | solution.py:60
  78.9 4.0 %collective-permute-start.25 = (bf16[224,384]{1,0:T(8,128)(2,1)S(1)}, bf16[224,384]{1,0:T(8,128)(2,1)S(1)}, u32[]{:S(2)}, u32[]{:S(2)}) collective-permute-start(bf16[224,384]{1,0:T(8,128)(2,1)S(1)} %collective-permute-done.24.refs_2_), channel_id=1, source_target_pairs={{0,2},{2,0},{4,6},{6,4},{8,10},{10,8},{12,14},{14,12},{16,18},{18,... | collective-permute-start | bytes 516104 | tf_op jit(solution)/shard_map/ppermute | solution.py:60
  78.9 4.0 %collective-permute-start.23 = (bf16[224,384]{1,0:T(8,128)(2,1)S(1)}, bf16[224,384]{1,0:T(8,128)(2,1)S(1)}, u32[]{:S(2)}, u32[]{:S(2)}) collective-permute-start(bf16[224,384]{1,0:T(8,128)(2,1)S(1)} %collective-permute-done.22.refs_1_), channel_id=1, source_target_pairs={{0,2},{2,0},{4,6},{6,4},{8,10},{10,8},{12,14},{14,12},{16,18},{18,... | collective-permute-start | bytes 516104 | tf_op jit(solution)/shard_map/ppermute | solution.py:60

commit v5 on v4

v5 whole, which is shorter than its diff:
```python
import functools
import math

import jax
import jax.numpy as jnp
import numpy as np
from jax import lax
from jax.experimental import pallas as pl
from jax.experimental.pallas import tpu as pltpu
from jax.sharding import PartitionSpec as P

SPAN = 4
EXTRA = 16


def turn_tables():
    labels = [[3 * row + col for col in range(3)] for row in range(3)]

    def turn_once(block):
        return [[block[col][2 - row] for col in range(3)] for row in range(3)]

    def sides_of(block):
        return [
            list(block[0]),
            [block[row][2] for row in range(3)],
            list(block[2]),
            [block[row][0] for row in range(3)],
        ]

    def corners_of(block):
        return [block[0][0], block[0][2], block[2][2], block[2][0]]

    base_sides = sides_of(labels)
    base_corners = corners_of(labels)
    edge_table = np.zeros((4, 4), np.int32)
    corner_table = np.zeros((4, 4), np.int32)
    for border in range(4):
        turned = labels
        for quarter in range(4):
            wanted = sides_of(turned)[(border + 2) % 4]
            for side_index in range(4):
                if base_sides[side_index] == wanted:
                    edge_table[border, quarter] = side_index
                if base_sides[side_index][::-1] == wanted:
                    edge_table[border, quarter] = side_index + 4
            corner_cell = corners_of(turned)[(border + 2) % 4]
            for corner_index in range(4):
                if base_corners[corner_index] == corner_cell:
                    corner_table[border, quarter] = corner_index
            turned = turn_once(turned)
    return np.concatenate([edge_table, corner_table], axis=0)


def by_offset(value, offset, count):
    return lax.ppermute(value, "tile", [(i, (i + offset) % count) for i in range(count)])


def by_mask(value, mask, count):
    return lax.ppermute(value, "tile", [(i, i ^ mask) for i in range(count)])


def mask_stages(count):
    bits = [1 << b for b in range(count.bit_length() - 1)]
    stages = [bits[:1]]
    rest = bits[1:]
    while rest:
        stages.append(rest[:2])
        rest = rest[2:]
    return stages


def group_masks(bits):
    masks = [0]
    for bit in bits:
        masks = masks + [m + bit for m in masks]
    return masks


def slot_of_mask(mask, count):
    place = 0
    for bits in mask_stages(count)[1:]:
        size = 1 << len(bits)
        place = place * size + (mask // bits[0]) % size
    return place


def corner_spot(slot, side):
    return jnp.where(
        slot == 0, 0, jnp.where(slot == 1, side - 1, jnp.where(slot == 2, 3 * side - 1, 2 * side))
    )


def vmem(shape, dtype):
    return jax.ShapeDtypeStruct(shape, dtype)


def call(kernel, outs, args, anywhere=(), scratch=(), flops=0):
    in_specs = [
        pl.BlockSpec(memory_space=pltpu.HBM if i in anywhere else pltpu.VMEM) for i in range(len(args))
    ]
    size = sum(math.prod(x.shape) * x.dtype.itemsize for x in list(args) + list(outs))
    return pl.pallas_call(
        kernel,
        out_shape=tuple(outs),
        in_specs=in_specs,
        out_specs=tuple(pl.BlockSpec(memory_space=pltpu.VMEM) for _ in outs),
        scratch_shapes=list(scratch),
        compiler_params=pltpu.CompilerParams(vmem_limit_bytes=40 * 1024 * 1024),
        cost_estimate=pl.CostEstimate(flops=flops, bytes_accessed=size, transcendentals=0),
    )(*args)


def packed_shape(rows, part):
    if part % 128 != 64:
        return (rows, part)
    return (rows * (part // 128) + rows // 2, 128)


def pack(value, out_ref, first=0):
    rows, part = value.shape
    if part % 128 != 64:
        out_ref[first : first + rows, :] = value
        return
    for i in range(part // 128):
        out_ref[first + i * rows : first + (i + 1) * rows, :] = value[:, i * 128 : (i + 1) * 128]
    rest = value[:, part - 64 :]
    at = first + rows * (part // 128)
    out_ref[at : at + rows // 2, :] = jnp.concatenate([rest[: rows // 2], rest[rows // 2 :]], axis=1)


def unpack(ref, out_ref, first, row, rows, part):
    if part % 128 != 64:
        out_ref[row : row + rows, :] = ref[first : first + rows, :]
        return
    for i in range(part // 128):
        out_ref[row : row + rows, i * 128 : (i + 1) * 128] = ref[first + i * rows : first + (i + 1) * rows, :]
    at = first + rows * (part // 128)
    rest = ref[at : at + rows // 2, :]
    out_ref[row : row + rows // 2, part - 64 :] = rest[:, :64]
    out_ref[row + rows // 2 : row + rows, part - 64 :] = rest[:, 64:]


def prepare_kernel(side, part, field_in, cot_in, sides_ref, cot_packed_ref, field_ref, cot_ref, sems):
    field_copy = pltpu.make_async_copy(field_in, field_ref, sems.at[0])
    cot_copy = pltpu.make_async_copy(cot_in, cot_ref, sems.at[1])
    field_copy.start()
    cot_copy.start()
    field_copy.wait()
    sides = jnp.concatenate(
        [field_ref[0], field_ref[:, side - 1, :], field_ref[side - 1], field_ref[:, 0, :]], axis=0
    )
    pack(sides, sides_ref)
    cot_copy.wait()
    pack(cot_ref[...], cot_packed_ref)


def shifted_columns(side, part, field, halos, out_ref):
    rows = side * side
    flat = rows + 2 * side
    column = lax.broadcasted_iota(jnp.int32, (flat, part), 0) % side
    if halos is None:
        none = jnp.zeros((side, part), jnp.float32)
        tall = jnp.concatenate([none, field.astype(jnp.float32), none], axis=0)
        west = east = 0.0
    else:
        edge = halos.astype(jnp.float32)
        tall = jnp.concatenate([edge[0:side], field.astype(jnp.float32), edge[2 * side : 3 * side]], axis=0)
        corner = [edge[4 * side + c : 4 * side + c + 1] for c in range(4)]
        spread = lambda col: jnp.broadcast_to(col[:, None, :], (side + 2, side, part)).reshape(flat, part)
        east = spread(jnp.concatenate([corner[1], edge[side : 2 * side], corner[2]], axis=0))
        west = spread(jnp.concatenate([corner[0], edge[3 * side : 4 * side], corner[3]], axis=0))
    out_ref[0] = jnp.where(column == 0, west, pltpu.roll(tall, 1, 0)).astype(jnp.bfloat16)
    out_ref[1] = tall.astype(jnp.bfloat16)
    out_ref[2] = jnp.where(column == side - 1, east, pltpu.roll(tall, flat - 1, 0)).astype(jnp.bfloat16)


def onehot_kernel(
    side, tables_in, et_in, eu_in, ct_in, cu_in, border_ref, halo_ref, place_ref, tables, et, eu, ct, cu, sems
):
    copies = [
        pltpu.make_async_copy(a, b, sems.at[i])
        for i, (a, b) in enumerate(
            [(tables_in, tables), (et_in, et), (eu_in, eu), (ct_in, ct), (cu_in, cu)]
        )
    ]
    for copy in copies:
        copy.start()
    for copy in copies:
        copy.wait()
    count = lax.axis_size("tile")
    own = lax.axis_index("tile")
    core = lax.rem(own, 2)
    groups = count // SPAN

    def base(source):
        slab = lax.rem(source // SPAN - own // SPAN + groups, groups)
        cross = source ^ own
        turn = lax.rem(cross // 2, 2)
        at = jnp.where(slab == 0, turn, jnp.where(slab == 1, 2, 3) + 2 * turn)
        return (6 * lax.rem(cross, 2) + at) * (4 * side)

    step = lax.broadcasted_iota(jnp.int32, (side, 1), 0)
    nothing = jnp.full((side, 1), -1, jnp.int32)

    def halo(tile, e):
        slot = tables[e, eu[e, tile]]
        start = base(et[e, tile]) + lax.rem(slot, 4) * side
        return lambda at: jnp.where(slot >= 4, start + side - 1 - at, start + at)

    def corner(tile, c):
        return base(ct[c, tile]) + corner_spot(tables[4 + c, cu[c, tile]], side)

    def onehot(wanted, width):
        lane = lax.broadcasted_iota(jnp.int32, (wanted.shape[0], width), 1)
        return jnp.where(lane == wanted, 1.0, 0.0).astype(jnp.bfloat16)

    width = 12 * 4 * side
    pieces = [[] for _ in range(4)]
    for tile in (own, own ^ 1):
        top, right, bottom, left = [halo(tile, e) for e in range(4)]
        corners = [corner(tile, c) for c in range(4)]
        low = core == 0
        row = lambda at: jnp.where(low, top(at), bottom(at))
        first = jnp.where(low, corners[0], corners[3])
        last = jnp.where(low, corners[1], corners[2])
        along = jnp.where(low, step - 1, step + 1)
        fits = (along >= 0) & (along < side)
        pieces[0] += [jnp.where(step == 0, first, row(step - 1)), jnp.where(fits, left(along), nothing)]
        pieces[1] += [row(step), nothing]
        pieces[2] += [jnp.where(step == side - 1, last, row(step + 1)), jnp.where(fits, right(along), nothing)]
        pieces[3] += [nothing, jnp.where(low, left(step), right(step))]
    border_ref[...] = onehot(jnp.concatenate(sum(pieces, []), axis=0), width)
    spots = lax.broadcasted_iota(jnp.int32, (EXTRA, 1), 0)
    ends = jnp.full((EXTRA, 1), -1, jnp.int32)
    for c in range(4):
        ends = jnp.where(spots == c, corner(own, c), ends)
    halo_ref[...] = onehot(jnp.concatenate([halo(own, e)(step) for e in range(4)] + [ends], axis=0), width)

    block = 4 * side + EXTRA
    lane = lax.broadcasted_iota(jnp.int32, (1, block), 1)
    row = lax.broadcasted_iota(jnp.int32, (4 * side, block), 0)
    places = []
    for mask in (0, 2, 1, 3):
        for offset in (0, SPAN, -SPAN):
            source = lax.rem((own ^ mask) + offset + count, count)
            target = jnp.full((1, block), -1, jnp.int32)
            for e in range(4):
                slot = tables[e, eu[e, source]]
                along = lane - e * side
                along = jnp.where(slot >= 4, side - 1 - along, along)
                hit = (lane >= e * side) & (lane < (e + 1) * side) & (et[e, source] == own)
                target = jnp.where(hit, lax.rem(slot, 4) * side + along, target)
                spot = corner_spot(tables[4 + e, cu[e, source]], side)
                hit = (lane == 4 * side + e) & (ct[e, source] == own)
                target = jnp.where(hit, spot, target)
            places.append(jnp.where(row == target, 1.0, 0.0))
    place_ref[...] = jnp.concatenate(places, axis=1).astype(jnp.bfloat16)


def inner_kernel(
    side, part, half, scale, field_ref, own_ref, other_ref, mine_ref, send_ref, cot_ref, rim_ref, cols, total
):
    rows = side * side
    chans = cot_ref.shape[1]
    first = lax.axis_index("ch") == 0
    unpack(other_ref, cols.at[0], 0, 0, rows, part)

    @pl.when(first)
    def _():
        cot_ref[:, 0:part] = own_ref[...]
        cot_ref[:, part:] = cols[0, 0:rows, :]

    @pl.when(jnp.logical_not(first))
    def _():
        cot_ref[:, 0:part] = cols[0, 0:rows, :]
        cot_ref[:, part:] = own_ref[...]

    shifted_columns(side, part, field_ref[...].reshape(rows, part), None, cols)
    cot = cot_ref[...]
    used = 9 * part // 2
    for a in range(3):
        for b in range(3):
            tap = 3 * a + b
            value = (
                lax.dot_general(
                    cols[b, a * side : a * side + rows, :],
                    cot,
                    (((0,), (0,)), ((), ())),
                    preferred_element_type=jnp.float32,
                )
                * scale
            )
            if tap < 4:
                total[tap * part : (tap + 1) * part, :] = value
            elif tap > 4:
                start = half + part // 2 + (tap - 5) * part
                total[start : start + part, :] = value
            else:
                total[4 * part : used, :] = value[: part // 2]
                total[half : half + part // 2, :] = value[part // 2 :]
    blank = jnp.zeros((half - used, chans), jnp.float32)
    total[used:half, :] = blank
    total[half + used : 2 * half, :] = blank
    core = lax.rem(lax.axis_index("tile"), 2)
    mine_ref[...] = total[pl.ds(pl.multiple_of(core * half, 16), half), :]
    send_ref[...] = total[pl.ds(pl.multiple_of((1 - core) * half, 16), half), :]
    rim_ref[...] = jnp.concatenate(
        [
            cot[0:side],
            cot[rows - side :],
            cot.reshape(side, side, chans)[:, 0, :],
            cot.reshape(side, side, chans)[:, side - 1, :],
        ],
        axis=0,
    )


def border_kernel(side, part, chunk, scale, n_near, *refs):
    near_refs = refs[:n_near]
    onehot_ref, mine_ref, got_ref, rim_ref, mate_ref = refs[n_near : n_near + 5]
    outs, near, total = refs[n_near + 5 : -2], refs[-2], refs[-1]
    count = lax.axis_size("tile")
    own = lax.axis_index("tile")
    core = lax.rem(own, 2)
    for i, ref in enumerate(near_refs):
        unpack(ref, near, 0, i * 4 * side, 4 * side, part)
    total[...] = mine_ref[...] + got_ref[...]
    left = jnp.dot(onehot_ref[...], near[...], preferred_element_type=jnp.float32).astype(jnp.bfloat16)

    def rim(ref, at):
        return ref[pl.ds(pl.multiple_of(at, 16), side), :]

    for q in range(4):
        column = (2 + q // 2) * side if q < 3 else (2 + core) * side
        right = jnp.concatenate(
            [value for ref in (rim_ref, mate_ref) for value in (rim(ref, core * side), rim(ref, column))],
            axis=0,
        )
        value = lax.dot_general(
            left[q * 4 * side : (q + 1) * 4 * side],
            right,
            (((0,), (0,)), ((), ())),
            preferred_element_type=jnp.float32,
        )
        if q < 3:
            start = q * part + core * (part // 2 + part)
        else:
            start = 3 * part - core * (3 * part - part // 2)
        here = pl.ds(pl.multiple_of(start, 16), part)
        total[here, :] = total[here, :] + value * scale
    size = outs[0].shape[0]
    for index in range(count // 2):
        to = slot_of_mask(2 * index, count) * chunk
        block = pl.multiple_of(((own // 2) ^ index) * chunk, 16)
        out = outs[to // size]
        out[to % size : to % size + chunk, :] = total[pl.ds(block, chunk), :].astype(out.dtype)


def sum_kernel(n_got, n_out, *refs):
    held_ref, got_refs, outs = refs[0], refs[1 : 1 + n_got], refs[1 + n_got :]
    size = held_ref.shape[0] // n_out
    for index in range(n_out):
        here = slice(index * size, (index + 1) * size)
        value = held_ref[here, :]
        for ref in got_refs:
            value = value + ref[here, :].astype(jnp.float32)
        outs[index][...] = value.astype(outs[index].dtype)


def join_kernel(*refs):
    row = 0
    for ref in refs[:-1]:
        refs[-1][row : row + ref.shape[0], :] = ref[...]
        row += ref.shape[0]


def unfold_kernel(used, chunk, bit, masks, n_dep, *refs):
    refs = refs[n_dep:]
    n = len(masks)
    in_refs, out_ref, wide, sems = refs[:n], refs[n], refs[n + 1], refs[n + 2]
    own = lax.axis_index("tile")
    origin = (lax.rem(own, 2) ^ bit) * used
    full, rest = used // chunk, used % chunk
    copies = []
    for i, (ref, inner) in enumerate(zip(in_refs, masks)):
        for k, mask in enumerate(inner):
            at = i * len(inner) + k
            wide[at] = ref[k * chunk : (k + 1) * chunk, :].astype(jnp.float32)
            block = (own ^ mask) // 2
            start = pl.multiple_of(origin + block * chunk, 16)
            copies.append(
                (
                    block < full,
                    pltpu.make_async_copy(wide.at[at], out_ref.at[pl.ds(start, chunk), :], sems.at[at]),
                )
            )
            if rest:
                start = pl.multiple_of(origin + full * chunk, 16)
                copies.append(
                    (
                        block == full,
                        pltpu.make_async_copy(
                            wide.at[at, 0:rest], out_ref.at[pl.ds(start, rest), :], sems.at[at]
                        ),
                    )
                )
    for going, copy in copies:
        pl.when(going)(copy.start)
    for going, copy in copies:
        pl.when(going)(copy.wait)


def unfold(whole, chunk, bit, masks, blocks, before):
    n_dep = 0 if before is None else 1
    anywhere = pl.BlockSpec(memory_space=pl.ANY)
    n_copies = len(masks) * len(masks[0])
    return pl.pallas_call(
        functools.partial(unfold_kernel, whole.shape[0] // 2, chunk, bit, masks, n_dep),
        out_shape=whole,
        in_specs=[anywhere] * n_dep + [pl.BlockSpec(memory_space=pltpu.VMEM)] * len(blocks),
        out_specs=anywhere,
        scratch_shapes=[
            pltpu.VMEM((n_copies, chunk, whole.shape[1]), jnp.float32),
            pltpu.SemaphoreType.DMA((n_copies,)),
        ],
        input_output_aliases={0: 0} if n_dep else {},
        compiler_params=pltpu.CompilerParams(vmem_limit_bytes=40 * 1024 * 1024),
    )(*([before] if n_dep else []), *blocks)


def back_kernel(side, part, cot_ref, weight_in, inner_ref, pieces_ref, tall, weight, sems):
    rows = side * side
    flat = rows + 2 * side
    start = pl.multiple_of(lax.axis_index("ch") * part, 16)
    copies = [
        pltpu.make_async_copy(weight_in.at[tap, pl.ds(start, part), :], weight.at[tap], sems.at[tap])
        for tap in range(9)
    ]
    for copy in copies:
        copy.start()
    blank = jnp.zeros((2 * side, tall.shape[1]), jnp.bfloat16)
    tall[0 : 2 * side, :] = blank
    tall[2 * side : 2 * side + rows, :] = cot_ref[...]
    tall[2 * side + rows :, :] = blank
    for copy in copies:
        copy.wait()
    backs = []
    for b in range(3):
        back = jnp.zeros((flat, part), jnp.float32)
        for a in range(3):
            back = back + lax.dot_general(
                tall[(2 - a) * side : (2 - a) * side + flat, :],
                weight[3 * a + b],
                (((1,), (1,)), ((), ())),
                preferred_element_type=jnp.float32,
            )
        backs.append(back)
    column = lax.broadcasted_iota(jnp.int32, (flat, part), 0) % side
    inner = (
        jnp.where(column == side - 1, 0.0, pltpu.roll(backs[0], flat - 1, 0))
        + backs[1]
        + jnp.where(column == 0, 0.0, pltpu.roll(backs[2], 1, 0))
    )
    inner_ref[...] = inner[side : side + rows]
    west = backs[0].reshape(side + 2, side, part)[:, 0, :]
    east = backs[2].reshape(side + 2, side, part)[:, side - 1, :]
    pieces = jnp.concatenate(
        [
            inner[0:side],
            east[1 : side + 1],
            inner[side + rows :],
            west[1 : side + 1],
            west[0:1],
            east[0:1],
            east[side + 1 :],
            west[side + 1 :],
            jnp.zeros((EXTRA - 4, part), jnp.float32),
        ],
        axis=0,
    )
    pack(pieces.astype(jnp.bfloat16), pieces_ref)


def add_halo_kernel(side, part, place_ref, inner_ref, *refs):
    got_refs, out_ref, got = refs[:-2], refs[-2], refs[-1]
    block = 4 * side + EXTRA
    size = packed_shape(block, part)[0]
    for i, ref in enumerate(got_refs):
        for k in range(3):
            unpack(ref, got, k * size, (3 * i + k) * block, block, part)
    sums = jnp.dot(place_ref[...], got[...], preferred_element_type=jnp.float32)
    rows = side * side
    spread = lambda col: jnp.broadcast_to(col[:, None, :], (side, side, part)).reshape(rows, part)
    column = lax.broadcasted_iota(jnp.int32, (rows, part), 0) % side
    inner = inner_ref[...]
    inner = inner + jnp.where(column == side - 1, spread(sums[side : 2 * side]), 0.0)
    inner = inner + jnp.where(column == 0, spread(sums[3 * side :]), 0.0)
    ends = jnp.concatenate(
        [
            inner[0:side] + sums[0:side],
            inner[side : rows - side],
            inner[rows - side :] + sums[2 * side : 3 * side],
        ],
        axis=0,
    )
    out_ref[...] = ends.astype(jnp.bfloat16)


def halo_kernel(side, part, n_near, *refs):
    near_refs, onehot_ref, field_ref = refs[:n_near], refs[n_near], refs[n_near + 1]
    halos_ref, packet_ref, near = refs[n_near + 2 :]
    rows = side * side
    for i, ref in enumerate(near_refs):
        unpack(ref, near, 0, i * 4 * side, 4 * side, part)
    halos = jnp.dot(onehot_ref[...], near[...], preferred_element_type=jnp.float32).astype(jnp.bfloat16)
    halos_ref[...] = halos
    pack(field_ref[...].reshape(rows, part), packet_ref)
    pack(halos, packet_ref, packed_shape(rows, part)[0])


def output_kernel(side, part, field_ref, halos_ref, other_ref, weight_in, out_ref, cols, other_cols, other, weight, sems):
    rows = side * side
    ch = lax.axis_index("ch")
    wide = weight.shape[2]
    lanes = pl.multiple_of(ch * (weight_in.shape[2] - wide), 128)
    copies = [
        pltpu.make_async_copy(weight_in.at[tap, :, pl.ds(lanes, wide)], weight.at[tap], sems.at[tap])
        for tap in range(9)
    ]
    for copy in copies:
        copy.start()
    unpack(other_ref, other, 0, 0, rows, part)
    unpack(other_ref, other, packed_shape(rows, part)[0], rows, 4 * side + EXTRA, part)
    shifted_columns(side, part, field_ref[...].reshape(rows, part), halos_ref[...], cols)
    shifted_columns(side, part, other[0:rows, :], other[rows:, :], other_cols)
    for copy in copies:
        copy.wait()
    starts = (pl.multiple_of(ch * part, 16), pl.multiple_of((1 - ch) * part, 16))
    total = jnp.zeros((rows, wide), jnp.float32)
    for a in range(3):
        for b in range(3):
            for ref, first in zip((cols, other_cols), starts):
                total = total + jnp.dot(
                    ref[b, a * side : a * side + rows, :],
                    weight[3 * a + b, pl.ds(first, part), :],
                    preferred_element_type=jnp.float32,
                )
    result = jnp.where(ch == 0, total[:, :part], total[:, wide - part :])
    out_ref[...] = result.astype(jnp.bfloat16)


def body(features, weight, cotangent, edge_tiles, edge_turns, corner_tiles, corner_turns):
    count = lax.axis_size("tile")
    field = features[0]
    side, part = field.shape[0], field.shape[2]
    chans = weight.shape[3]
    rows = side * side
    flat = rows + 2 * side
    block = 4 * side + EXTRA
    taps = weight.reshape(9, chans, chans)
    others = [(0, 1), (1, 0)]
    flops = 2 * rows * 9 * part * chans
    half_bytes = jnp.bfloat16
    chunk = -(-9 * part // (16 * count)) * 16
    half = count * chunk // 2
    scale = 1.0 / math.sqrt(count * rows)

    sides, cot_packed, field, cot_own = call(
        functools.partial(prepare_kernel, side, part),
        [
            vmem(packed_shape(4 * side, part), half_bytes),
            vmem(packed_shape(rows, part), half_bytes),
            vmem((side, side, part), half_bytes),
            vmem((rows, part), half_bytes),
        ],
        [field, cotangent[0].reshape(rows, part)],
        anywhere=(0, 1),
        scratch=[pltpu.SemaphoreType.DMA((2,))],
    )
    cot_other = lax.ppermute(cot_packed, "ch", others)
    near = [sides, by_mask(sides, 2, count)]
    for flip in (0, 2):
        for offset in (SPAN, -SPAN):
            pairs = [(i, ((i - offset) % count) ^ flip) for i in range(count)]
            near.append(lax.ppermute(sides, "tile", pairs))
    near, cot_other = lax.optimization_barrier((near, cot_other))
    near = near + [by_mask(v, 1, count) for v in near]

    border_pick, halo_pick, place = call(
        functools.partial(onehot_kernel, side),
        [
            vmem((16 * side, 48 * side), half_bytes),
            vmem((block, 48 * side), half_bytes),
            vmem((4 * side, 12 * block), half_bytes),
        ],
        [jnp.asarray(turn_tables()), edge_tiles.T, edge_turns.T, corner_tiles.T, corner_turns.T],
        anywhere=range(5),
        scratch=[pltpu.SMEM((8, 4), jnp.int32)]
        + [pltpu.SMEM((4, count), jnp.int32)] * 4
        + [pltpu.SemaphoreType.DMA((5,))],
    )
    mine, send, cot_full, rim = call(
        functools.partial(inner_kernel, side, part, half, scale),
        [
            vmem((half, chans), jnp.float32),
            vmem((half, chans), jnp.float32),
            vmem((rows, chans), half_bytes),
            vmem((4 * side, chans), half_bytes),
        ],
        [field, cot_own, cot_other],
        scratch=[pltpu.VMEM((3, flat, part), half_bytes), pltpu.VMEM((2 * half, chans), jnp.float32)],
        flops=flops,
    )

    stages = mask_stages(count)
    masks = group_masks(stages[1])
    size = half // len(masks)
    held, *send = call(
        functools.partial(border_kernel, side, part, chunk, scale, len(near)),
        [vmem((size, chans), jnp.float32)] + [vmem((size, chans), half_bytes)] * (len(masks) - 1),
        [*near, border_pick, mine, by_mask(send, 1, count), rim, by_mask(rim, 1, count)],
        scratch=[pltpu.VMEM((48 * side, part), half_bytes), pltpu.VMEM((half, chans), jnp.float32)],
    )
    send, near, cot_full = lax.optimization_barrier((send, near, cot_full))
    got = [by_mask(v, m, count) for v, m in zip(send, masks[1:])]
    halos, packet = call(
        functools.partial(halo_kernel, side, part, len(near)),
        [vmem((block, part), half_bytes), vmem(packed_shape(rows + block, part), half_bytes)],
        [*near, halo_pick, field],
        scratch=[pltpu.VMEM((48 * side, part), half_bytes)],
    )
    other_field = lax.ppermute(packet, "ch", others)
    inner, pieces = call(
        functools.partial(back_kernel, side, part),
        [vmem((rows, part), jnp.float32), vmem(packed_shape(block, part), half_bytes)],
        [cot_full, taps],
        anywhere=(1,),
        scratch=[
            pltpu.VMEM((rows + 4 * side, chans), half_bytes),
            pltpu.VMEM((9, part, chans), half_bytes),
            pltpu.SemaphoreType.DMA((9,)),
        ],
        flops=flops,
    )
    got, pieces, inner, halos = lax.optimization_barrier((got, pieces, inner, halos))
    for index, bits in enumerate(stages[2:]):
        masks = group_masks(bits)
        size = held.shape[0] // len(masks)
        held, *send = call(
            functools.partial(sum_kernel, len(got), len(masks)),
            [vmem((size, chans), jnp.float32)] + [vmem((size, chans), half_bytes)] * (len(masks) - 1),
            [held, *got],
        )
        send, pieces = lax.optimization_barrier((send, pieces))
        got = [by_mask(v, m, count) for v, m in zip(send, masks[1:])]
        if index == 0:
            here = [pieces, by_offset(pieces, -SPAN, count), by_offset(pieces, SPAN, count)]
            (here,) = call(join_kernel, [vmem((3 * pieces.shape[0], pieces.shape[1]), half_bytes)], here)
            got, here = lax.optimization_barrier((got, here))
    (held,) = call(functools.partial(sum_kernel, len(got), 1), [vmem(held.shape, half_bytes)], [held, *got])
    order = [0]
    for index, bits in enumerate(stages[:0:-1]):
        masks = group_masks(bits)
        if index == 0:
            held, here, other_field = lax.optimization_barrier((held, here, other_field))
            beside = by_mask(here, 2, count)
            wide = -(-part // 128) * 128
            (output,) = call(
                functools.partial(output_kernel, side, part),
                [vmem((rows, part), half_bytes)],
                [field, halos, other_field, taps],
                anywhere=(3,),
                scratch=[
                    pltpu.VMEM((3, flat, part), half_bytes),
                    pltpu.VMEM((3, flat, part), half_bytes),
                    pltpu.VMEM((rows + block, part), half_bytes),
                    pltpu.VMEM((9, chans, wide), half_bytes),
                    pltpu.SemaphoreType.DMA((9,)),
                ],
                flops=2 * flops,
            )
        got = [by_mask(held, m, count) for m in masks[1:]]
        if index == 0:
            held, got, output, beside = lax.optimization_barrier((held, got, output, beside))
        if index < len(stages) - 2:
            order = [m + v for m in masks for v in order]
            (held,) = call(
                join_kernel, [vmem((held.shape[0] * len(masks), chans), half_bytes)], [held, *got]
            )
            continue
        got_pieces = [here, beside, by_mask(here, 1, count), by_mask(beside, 1, count)]
        (grad_features,) = call(
            functools.partial(add_halo_kernel, side, part),
            [vmem((rows, part), half_bytes)],
            [place, inner, *got_pieces],
            scratch=[pltpu.VMEM((12 * block, part), half_bytes)],
        )
        got, grad_features = lax.optimization_barrier((got, grad_features))
        got = [held, *got]
        order = [[m + v for v in order] for m in masks]
    mates = [by_mask(v, 1, count) for v in got]
    whole = vmem((9 * part, chans), jnp.float32)
    first = unfold(whole, chunk, 0, order, got, None)
    grad_weight = unfold(whole, chunk, 1, order, mates, first)
    shape = (1, side, side, part)
    return (
        output.reshape(shape),
        grad_features.reshape(shape),
        grad_weight.reshape(3, 3, part, chans),
    )


def solution(mesh):
    return jax.shard_map(
        body,
        mesh=mesh,
        in_specs=(
            P("tile", None, None, "ch"),
            P(),
            P("tile", None, None, "ch"),
            P(),
            P(),
            P(),
            P(),
        ),
        out_specs=(
            P("tile", None, None, "ch"),
            P("tile", None, None, "ch"),
            P(None, None, "ch", None),
        ),
        check_vma=False,
    )
```

time: 84.5 us -> 73.2 us (0.87)
  waiting for transfers between devices: 32.7 us -> 22.4 us
  local copies, waits for them, and re-layouts: 9.8 us -> 2.11 us
  Pallas kernels: 15.1 us -> 20.6 us
  starting transfers between devices: 25.4 us -> 26.8 us
    ppermute x10 -> x2, waiting for transfers between devices: 18.7 us -> 5.95 us  [by_offset(): lax.ppermute(value, 'tile', [(i, (i + offset) % count) for i in range(cou...]
    ppermute x10 -> x2, starting transfers between devices: 11.4 us -> 2.63 us  [by_offset(): lax.ppermute(value, 'tile', [(i, (i + offset) % count) for i in range(cou...]
    ppermute x1 -> x5, starting transfers between devices: 3 us -> 10.4 us  [the longest x4 7.37 us: body(): near.append(lax.ppermute(sides, 'tile', pairs))]
    ppermute x1 -> x5, waiting for transfers between devices: 0.01 us -> 6.78 us  [the longest x4 6.78 us: body(): near.append(lax.ppermute(sides, 'tile', pairs))]
    unnamed x32 -> x16, local copies, waits for them, and re-layouts: 8.31 us -> 2.11 us
    pallas_call x10 -> x12, Pallas kernels: 12.9 us -> 18.2 us  [call(): pl.pallas_call(kernel, out_shape=tuple(outs), in_specs=in_specs, out_spec...]
    ppermute x16 -> x24, waiting for transfers between devices: 14 us -> 9.64 us  [by_mask(): return lax.ppermute(value, 'tile', [(i, i ^ mask) for i in range(count)])]
    ppermute x16 -> x24, starting transfers between devices: 10.5 us -> 13.2 us  [by_mask(): return lax.ppermute(value, 'tile', [(i, i ^ mask) for i in range(count)])]
  transfers between devices with their start and end apart: 28 -> 32, of which waited for: 10 -> 13; matrix products, arithmetic and copies ran while one was open for 2% -> 0% of each run, Pallas kernels for 13% -> 19%
where the time goes in v5:
time: 73.2 us; the launch traced here: 73 us
  starting transfers between devices  26.8 us (37%)
  waiting for transfers between devices  22.4 us (31%)
  Pallas kernels  20.6 us (28%)
  local copies, waits for them, and re-layouts  2.11 us (3%)
  between operations  1.04 us (1%)
    pallas_call x12, Pallas kernels, call(): pl.pallas_call(kernel, out_shape=tuple(outs), in_specs=in_specs, out_spec...  18.2 us
    ppermute x24, starting transfers between devices, by_mask(): return lax.ppermute(value, 'tile', [(i, i ^ mask) for i in range(count)])  13.2 us
    ppermute x24, waiting for transfers between devices, by_mask(): return lax.ppermute(value, 'tile', [(i, i ^ mask) for i in range(count)])  9.64 us
    ppermute x4, starting transfers between devices, body(): near.append(lax.ppermute(sides, 'tile', pairs))  7.37 us
    ppermute x4, waiting for transfers between devices, body(): near.append(lax.ppermute(sides, 'tile', pairs))  6.78 us
    ppermute x2, waiting for transfers between devices, by_offset(): lax.ppermute(value, 'tile', [(i, (i + offset) % count) for i in range(cou...  5.95 us
    ppermute x1, starting transfers between devices, body(): cot_other = lax.ppermute(cot_packed, 'ch', others)  3 us
    ppermute x2, starting transfers between devices, by_offset(): lax.ppermute(value, 'tile', [(i, (i + offset) % count) for i in range(cou...  2.63 us
  transfers between devices with their start and end apart: 32, of which 13 were waited for; matrix products, arithmetic and copies ran while one was open for 0% of the time, Pallas kernels for 19%

profile of v5, /device:TPU:0, one launch (start us, length us, event | category | flops | bytes accessed | tf_op | source)
XLA Modules:
  0.0 73.0 jit_solution(14083607622377180017)
XLA Ops:
  0.6 1.0 %copy-done = bf16[1,32,32,192]{3,2,1,0:T(8,128)(2,1)S(1)} copy-done((bf16[1,32,32,192]{3,2,1,0:T(8,128)(2,1)S(1)}, bf16[1,32,32,192]{3,2,1,0:T(8,128)(2,1)}, u32[]{:S(2)}) %copy-start) | copy-done | bytes 393240
  1.7 1.0 %copy-done.1 = bf16[1,32,32,192]{3,2,1,0:T(8,128)(2,1)S(1)} copy-done((bf16[1,32,32,192]{3,2,1,0:T(8,128)(2,1)S(1)}, bf16[1,32,32,192]{3,2,1,0:T(8,128)(2,1)}, u32[]{:S(2)}) %copy-start.1) | copy-done | bytes 393240
  2.7 0.3 shard_map.103
  3.0 3.0 %collective-permute-start.5 = (bf16[1536,128]{1,0:T(8,128)(2,1)S(1)}, bf16[1536,128]{1,0:T(8,128)(2,1)S(1)}, u32[]{:S(2)}, u32[]{:S(2)}) collective-permute-start(bf16[1536,128]{1,0:T(8,128)(2,1)S(1)} %get-tuple-element.69), channel_id=1, source_target_pairs={{0,1},{1,0},{2,3},{3,2},{4,5},{5,4},{6,7},{7,6},{8,9},{9,8},{10,11... | collective-permute-start | bytes 1179656 | tf_op jit(solution)/shard_map/ppermute | solution.py:580
  6.0 1.5 %collective-permute-start = (bf16[192,128]{1,0:T(8,128)(2,1)S(1)}, bf16[192,128]{1,0:T(8,128)(2,1)S(1)}, u32[]{:S(2)}, u32[]{:S(2)}) collective-permute-start(bf16[192,128]{1,0:T(8,128)(2,1)S(1)} %get-tuple-element.94.refs_0_), channel_id=1, source_target_pairs={{0,4},{2,6},{4,0},{6,2},{8,12},{10,14},{12,8},{14,10},{16,20},{18,... | collective-permute-start | bytes 147464 | tf_op jit(solution)/shard_map/ppermute | solution.py:59
  7.5 3.6 %collective-permute-start.1 = (bf16[192,128]{1,0:T(8,128)(2,1)S(1)}, bf16[192,128]{1,0:T(8,128)(2,1)S(1)}, u32[]{:S(2)}, u32[]{:S(2)}) collective-permute-start(bf16[192,128]{1,0:T(8,128)(2,1)S(1)} %get-tuple-element.94.refs_0_), channel_id=1, source_target_pairs={{0,24},{2,26},{4,28},{6,30},{8,0},{10,2},{12,4},{14,6},{16,8},{18,... | collective-permute-start | bytes 147464 | tf_op jit(solution)/shard_map/ppermute | solution.py:585
  11.2 3.8 %collective-permute-start.3 = (bf16[192,128]{1,0:T(8,128)(2,1)S(1)}, bf16[192,128]{1,0:T(8,128)(2,1)S(1)}, u32[]{:S(2)}, u32[]{:S(2)}) collective-permute-start(bf16[192,128]{1,0:T(8,128)(2,1)S(1)} %get-tuple-element.94.refs_0_), channel_id=1, source_target_pairs={{0,28},{2,30},{4,24},{6,26},{8,4},{10,6},{12,0},{14,2},{16,12},{18... | collective-permute-start | bytes 147464 | tf_op jit(solution)/shard_map/ppermute | solution.py:585
  14.9 2.1 %collective-permute-done.2.refs_3_ = bf16[192,128]{1,0:T(8,128)(2,1)S(1)} collective-permute-done((bf16[192,128]{1,0:T(8,128)(2,1)S(1)}, bf16[192,128]{1,0:T(8,128)(2,1)S(1)}, u32[]{:S(2)}, u32[]{:S(2)}) %collective-permute-start.2) | collective-permute-done | bytes 49184 | tf_op jit(solution)/shard_map/ppermute | solution.py:585
  17.0 4.7 %collective-permute-done.4.refs_5_ = bf16[192,128]{1,0:T(8,128)(2,1)S(1)} collective-permute-done((bf16[192,128]{1,0:T(8,128)(2,1)S(1)}, bf16[192,128]{1,0:T(8,128)(2,1)S(1)}, u32[]{:S(2)}, u32[]{:S(2)}) %collective-permute-start.4) | collective-permute-done | bytes 49184 | tf_op jit(solution)/shard_map/ppermute | solution.py:585
  21.7 3.3 %shard_map.105 = (f32[896,384]{1,0:T(8,128)S(1)}, f32[896,384]{1,0:T(8,128)S(1)}, bf16[1024,384]{1,0:T(8,128)(2,1)S(1)}, bf16[128,384]{1,0:T(8,128)(2,1)S(1)}) custom-call(bf16[32,32,192]{2,1,0:T(8,128)(2,1)S(1)} %get-tuple-element.77.field_ref.refs_13_, bf16[1024,192]{1,0:T(8,128)(2,1)S(1)} %get-tuple-element.78.own_ref, ...), custom_call_target="tpu_custom_call" | custom-call | flops 1358954496 | bytes 4816896 | tf_op jit(solution)/shard_map/pallas_call | solution.py:102
  25.1 0.1 collective-permute-start.12
  25.1 0.5 collective-permute-start.10
  25.6 0.1 collective-permute-start.11
  25.7 0.4 collective-permute-start.6
  26.1 0.1 collective-permute-start.13
  26.2 2.1 %collective-permute-done.10.refs_10_ = bf16[192,128]{1,0:T(8,128)(2,1)S(1)} collective-permute-done((bf16[192,128]{1,0:T(8,128)(2,1)S(1)}, bf16[192,128]{1,0:T(8,128)(2,1)S(1)}, u32[]{:S(2)}, u32[]{:S(2)}) %collective-permute-start.10) | collective-permute-done | bytes 49184 | tf_op jit(solution)/shard_map/ppermute | solution.py:59
  28.3 0.1 collective-permute-start.7
  28.5 0.4 collective-permute-start.8
  28.8 0.1 collective-permute-start.9
  29.0 2.0 %shard_map.104 = (bf16[512,1536]{1,0:T(8,128)(2,1)S(1)}, bf16[144,1536]{1,0:T(8,128)(2,1)S(1)}, bf16[128,1728]{1,0:T(8,128)(2,1)S(1)}) custom-call(s32[8,4]{1,0:T(8,128)S(1)} %copy-done.2, s32[4,16]{1,0:T(4,128)S(1)} %bitcast.12, s32[4,16]{1,0:T(4,128)S(1)} %bitcast.13, s32[4,16]{1,0:T(4,128)S(1)} %bitcast.14, s32[4,16]{1,0:T(4,128)S(1)} %bitcast.15), custom_call_target="tpu_custom_call" | custom-call | bytes 2458752 | tf_op jit(solution)/shard_map/pallas_call | solution.py:102
  31.0 1.5 %shard_map.106 = (f32[224,384]{1,0:T(8,128)S(1)}, bf16[224,384]{1,0:T(8,128)(2,1)S(1)}, bf16[224,384]{1,0:T(8,128)(2,1)S(1)}, bf16[224,384]{1,0:T(8,128)(2,1)S(1)}) custom-call(bf16[192,128]{1,0:T(8,128)(2,1)S(1)} %get-tuple-element.94.refs_0_, bf16[192,128]{1,0:T(8,128)(2,1)S(1)} %collective-permute-done.refs_1_, ...), custom_call_target="tpu_custom_call" | custom-call | bytes 5971968 | tf_op jit(solution)/shard_map/pallas_call | solution.py:102
  32.6 0.5 shard_map.108
  33.0 0.7 collective-permute-start.20
  33.7 1.5 %collective-permute-start.14 = (bf16[224,384]{1,0:T(8,128)(2,1)S(1)}, bf16[224,384]{1,0:T(8,128)(2,1)S(1)}, u32[]{:S(2)}, u32[]{:S(2)}) collective-permute-start(bf16[224,384]{1,0:T(8,128)(2,1)S(1)} %get-tuple-element.88), channel_id=1, source_target_pairs={{0,4},{2,6},{4,0},{6,2},{8,12},{10,14},{12,8},{14,10},{16,20},{18,... | collective-permute-start | bytes 516104 | tf_op jit(solution)/shard_map/ppermute | solution.py:59
  35.2 2.0 %collective-permute-start.16 = (bf16[224,384]{1,0:T(8,128)(2,1)S(1)}, bf16[224,384]{1,0:T(8,128)(2,1)S(1)}, u32[]{:S(2)}, u32[]{:S(2)}) collective-permute-start(bf16[224,384]{1,0:T(8,128)(2,1)S(1)} %get-tuple-element.90), channel_id=1, source_target_pairs={{0,12},{2,14},{4,8},{6,10},{8,4},{10,6},{12,0},{14,2},{16,28},{18,... | collective-permute-start | bytes 516104 | tf_op jit(solution)/shard_map/ppermute | solution.py:59
  37.2 4.7 %shard_map.107 = (f32[1024,192]{1,0:T(8,128)S(1)}, bf16[216,128]{1,0:T(8,128)(2,1)S(1)}) custom-call(bf16[1024,384]{1,0:T(8,128)(2,1)S(1)} %get-tuple-element.91.cot_ref, bf16[9,384,384]{2,1,0:T(8,128)(2,1)S(1)} %bitcast.16), custom_call_target="tpu_custom_call" | custom-call | flops 1358954496 | bytes 4282368 | tf_op jit(solution)/shard_map/pallas_call | solution.py:102
  41.9 0.5 collective-permute-done.15.refs_2_
  42.5 2.4 %collective-permute-done.16.refs_3_ = bf16[224,384]{1,0:T(8,128)(2,1)S(1)} collective-permute-done((bf16[224,384]{1,0:T(8,128)(2,1)S(1)}, bf16[224,384]{1,0:T(8,128)(2,1)S(1)}, u32[]{:S(2)}, u32[]{:S(2)}) %collective-permute-start.16) | collective-permute-done | bytes 172064 | tf_op jit(solution)/shard_map/ppermute | solution.py:59
  44.9 0.1 shard_map.109
  45.0 0.1 collective-permute-start.17
  45.1 2.6 %collective-permute-start.18 = (bf16[216,128]{1,0:T(8,128)(2,1)S(1)}, bf16[216,128]{1,0:T(8,128)(2,1)S(1)}, u32[]{:S(2)}, u32[]{:S(2)}) collective-permute-start(bf16[216,128]{1,0:T(8,128)(2,1)S(1)} %get-tuple-element.115.refs_0_), channel_id=1, source_target_pairs={{0,24},{2,26},{4,28},{6,30},{8,0},{10,2},{12,4},{14,6},{16,8},{18,... | collective-permute-start | bytes 165896 | tf_op jit(solution)/shard_map/ppermute | solution.py:55
  47.7 2.2 %collective-permute-done.18.refs_1_ = bf16[216,128]{1,0:T(8,128)(2,1)S(1)} collective-permute-done((bf16[216,128]{1,0:T(8,128)(2,1)S(1)}, bf16[216,128]{1,0:T(8,128)(2,1)S(1)}, u32[]{:S(2)}, u32[]{:S(2)}) %collective-permute-start.18) | collective-permute-done | bytes 55328 | tf_op jit(solution)/shard_map/ppermute | solution.py:55
  49.9 3.8 %collective-permute-done.19.refs_2_ = bf16[216,128]{1,0:T(8,128)(2,1)S(1)} collective-permute-done((bf16[216,128]{1,0:T(8,128)(2,1)S(1)}, bf16[216,128]{1,0:T(8,128)(2,1)S(1)}, u32[]{:S(2)}, u32[]{:S(2)}) %collective-permute-start.19) | collective-permute-done | bytes 55328 | tf_op jit(solution)/shard_map/ppermute | solution.py:55
  53.7 1.6 %collective-permute-start.22 = (bf16[648,128]{1,0:T(8,128)(2,1)S(1)}, bf16[648,128]{1,0:T(8,128)(2,1)S(1)}, u32[]{:S(2)}, u32[]{:S(2)}) collective-permute-start(bf16[648,128]{1,0:T(8,128)(2,1)S(1)} %shard_map.110.refs_0_), channel_id=1, source_target_pairs={{0,4},{2,6},{4,0},{6,2},{8,12},{10,14},{12,8},{14,10},{16,20},{18,... | collective-permute-start | bytes 497672 | tf_op jit(solution)/shard_map/ppermute | solution.py:59
  55.3 4.5 %shard_map.112 = bf16[1024,192]{1,0:T(8,128)(2,1)} custom-call(bf16[32,32,192]{2,1,0:T(8,128)(2,1)S(1)} %get-tuple-element.77.field_ref.refs_13_, bf16[144,192]{1,0:T(8,128)(2,1)S(1)} %get-tuple-element.120.halos_ref, bf16[1752,128]{1,0:T(8,128)(2,1)S(1)} %collective-permute-done.20.other_ref, bf16[9,384,384]{2,1,0:T(8,128)(2,1)S(1)} %bitcast.17), custom_call_target="tpu_custom_call" | custom-call | flops 2717908992 | bytes 3944448 | tf_op jit(solution)/shard_map/pallas_call | solution.py:102
  59.8 1.1 %collective-permute-done.21.refs_1_ = bf16[112,384]{1,0:T(8,128)(2,1)S(1)} collective-permute-done((bf16[112,384]{1,0:T(8,128)(2,1)S(1)}, bf16[112,384]{1,0:T(8,128)(2,1)S(1)}, u32[]{:S(2)}, u32[]{:S(2)}) %collective-permute-start.21) | collective-permute-done | bytes 86048 | tf_op jit(solution)/shard_map/ppermute | solution.py:59
  60.9 0.6 collective-permute-start.23
  61.5 3.0 %collective-permute-start.25 = (bf16[224,384]{1,0:T(8,128)(2,1)S(1)}, bf16[224,384]{1,0:T(8,128)(2,1)S(1)}, u32[]{:S(2)}, u32[]{:S(2)}) collective-permute-start(bf16[224,384]{1,0:T(8,128)(2,1)S(1)} %shard_map.113.refs_0_), channel_id=1, source_target_pairs={{0,12},{2,14},{4,8},{6,10},{8,4},{10,6},{12,0},{14,2},{16,28},{18,... | collective-permute-start | bytes 516104 | tf_op jit(solution)/shard_map/ppermute | solution.py:59
  64.5 0.5 collective-permute-start.27
  65.0 0.9 %collective-permute-done.26.refs_2_ = bf16[648,128]{1,0:T(8,128)(2,1)S(1)} collective-permute-done((bf16[648,128]{1,0:T(8,128)(2,1)S(1)}, bf16[648,128]{1,0:T(8,128)(2,1)S(1)}, u32[]{:S(2)}, u32[]{:S(2)}) %collective-permute-start.26) | collective-permute-done | bytes 165920 | tf_op jit(solution)/shard_map/ppermute | solution.py:59
  65.9 0.1 collective-permute-start.28
  66.0 0.1 collective-permute-done.27.refs_3_
  66.1 1.3 %shard_map.114 = bf16[1024,192]{1,0:T(8,128)(2,1)} custom-call(bf16[128,1728]{1,0:T(8,128)(2,1)S(1)} %get-tuple-element.126.place_ref, f32[1024,192]{1,0:T(8,128)S(1)} %get-tuple-element.127.inner_ref, bf16[648,128]{1,0:T(8,128)(2,1)S(1)} %shard_map.110.refs_0_, bf16[648,128]{1,0:T(8,128)(2,1)S(1)} %collective-permute-done.22.refs_1_, ...), custom_call_target="tpu_custom_call" | custom-call | bytes 2285568 | tf_op jit(solution)/shard_map/pallas_call | solution.py:102
  67.5 2.2 %collective-permute-done.25.refs_3_ = bf16[224,384]{1,0:T(8,128)(2,1)S(1)} collective-permute-done((bf16[224,384]{1,0:T(8,128)(2,1)S(1)}, bf16[224,384]{1,0:T(8,128)(2,1)S(1)}, u32[]{:S(2)}, u32[]{:S(2)}) %collective-permute-start.25) | collective-permute-done | bytes 172064 | tf_op jit(solution)/shard_map/ppermute | solution.py:59
  69.7 0.5 collective-permute-start.30
  70.2 1.2 %shard_map.115.refs_0_ = f32[1728,384]{1,0:T(8,128)} custom-call(bf16[224,384]{1,0:T(8,128)(2,1)S(1)} %shard_map.113.refs_0_, bf16[224,384]{1,0:T(8,128)(2,1)S(1)} %collective-permute-done.23.refs_1_, bf16[224,384]{1,0:T(8,128)(2,1)S(1)} %collective-permute-done.24.refs_2_, bf16[224,384]{1,0:T(8,128)(2,1)S(1)} %collective-permute-done.25.refs_3_), custom_call_target="tpu_custom_call" | custom-call | tf_op jit(solution)/shard_map/pallas_call | solution.py:417
  71.5 0.2 collective-permute-done.31.refs_4_
  71.6 1.2 %shard_map.116 = f32[1728,384]{1,0:T(8,128)} custom-call(f32[1728,384]{1,0:T(8,128)} %shard_map.115.refs_0_, bf16[224,384]{1,0:T(8,128)(2,1)S(1)} %collective-permute-done.28.refs_1_, bf16[224,384]{1,0:T(8,128)(2,1)S(1)} %collective-permute-done.29.refs_2_, bf16[224,384]{1,0:T(8,128)(2,1)S(1)} %collective-permute-done.30.refs_3_, ...), custom_call_target="tpu_custom_call", output_to_operand_aliasing={{}: (0, {})} | custom-call | tf_op jit(solution)/shard_map/pallas_call | solution.py:417
  (46 shorter events, 0.2 us)
Async XLA Ops:
  0.6 1.0 %copy-start = (bf16[1,32,32,192]{3,2,1,0:T(8,128)(2,1)S(1)}, bf16[1,32,32,192]{3,2,1,0:T(8,128)(2,1)}, u32[]{:S(2)}) copy-start(bf16[1,32,32,192]{3,2,1,0:T(8,128)(2,1)} %param.8) | copy-start | bytes 1179652
  1.7 1.0 %copy-start.1 = (bf16[1,32,32,192]{3,2,1,0:T(8,128)(2,1)S(1)}, bf16[1,32,32,192]{3,2,1,0:T(8,128)(2,1)}, u32[]{:S(2)}) copy-start(bf16[1,32,32,192]{3,2,1,0:T(8,128)(2,1)} %param.10) | copy-start | bytes 1179652
  3.0 18.7 %collective-permute-start.5 = (bf16[1536,128]{1,0:T(8,128)(2,1)S(1)}, bf16[1536,128]{1,0:T(8,128)(2,1)S(1)}, u32[]{:S(2)}, u32[]{:S(2)}) collective-permute-start(bf16[1536,128]{1,0:T(8,128)(2,1)S(1)} %get-tuple-element.69), channel_id=1, source_target_pairs={{0,1},{1,0},{2,3},{3,2},{4,5},{5,4},{6,7},{7,6},{8,9},{9,8},{10,11... | collective-permute-start | bytes 1179656 | tf_op jit(solution)/shard_map/ppermute | solution.py:580
  6.0 8.9 %collective-permute-start = (bf16[192,128]{1,0:T(8,128)(2,1)S(1)}, bf16[192,128]{1,0:T(8,128)(2,1)S(1)}, u32[]{:S(2)}, u32[]{:S(2)}) collective-permute-start(bf16[192,128]{1,0:T(8,128)(2,1)S(1)} %get-tuple-element.94.refs_0_), channel_id=1, source_target_pairs={{0,4},{2,6},{4,0},{6,2},{8,12},{10,14},{12,8},{14,10},{16,20},{18,... | collective-permute-start | bytes 147464 | tf_op jit(solution)/shard_map/ppermute | solution.py:59
  7.5 7.4 %collective-permute-start.1 = (bf16[192,128]{1,0:T(8,128)(2,1)S(1)}, bf16[192,128]{1,0:T(8,128)(2,1)S(1)}, u32[]{:S(2)}, u32[]{:S(2)}) collective-permute-start(bf16[192,128]{1,0:T(8,128)(2,1)S(1)} %get-tuple-element.94.refs_0_), channel_id=1, source_target_pairs={{0,24},{2,26},{4,28},{6,30},{8,0},{10,2},{12,4},{14,6},{16,8},{18,... | collective-permute-start | bytes 147464 | tf_op jit(solution)/shard_map/ppermute | solution.py:585
  11.2 5.9 %collective-permute-start.2 = (bf16[192,128]{1,0:T(8,128)(2,1)S(1)}, bf16[192,128]{1,0:T(8,128)(2,1)S(1)}, u32[]{:S(2)}, u32[]{:S(2)}) collective-permute-start(bf16[192,128]{1,0:T(8,128)(2,1)S(1)} %get-tuple-element.94.refs_0_), channel_id=1, source_target_pairs={{0,8},{2,10},{4,12},{6,14},{8,16},{10,18},{12,20},{14,22},{16,24},... | collective-permute-start | bytes 147464 | tf_op jit(solution)/shard_map/ppermute | solution.py:585
  11.2 5.9 %collective-permute-start.3 = (bf16[192,128]{1,0:T(8,128)(2,1)S(1)}, bf16[192,128]{1,0:T(8,128)(2,1)S(1)}, u32[]{:S(2)}, u32[]{:S(2)}) collective-permute-start(bf16[192,128]{1,0:T(8,128)(2,1)S(1)} %get-tuple-element.94.refs_0_), channel_id=1, source_target_pairs={{0,28},{2,30},{4,24},{6,26},{8,4},{10,6},{12,0},{14,2},{16,12},{18... | collective-permute-start | bytes 147464 | tf_op jit(solution)/shard_map/ppermute | solution.py:585
  14.9 6.8 %collective-permute-start.4 = (bf16[192,128]{1,0:T(8,128)(2,1)S(1)}, bf16[192,128]{1,0:T(8,128)(2,1)S(1)}, u32[]{:S(2)}, u32[]{:S(2)}) collective-permute-start(bf16[192,128]{1,0:T(8,128)(2,1)S(1)} %get-tuple-element.94.refs_0_), channel_id=1, source_target_pairs={{0,12},{2,14},{4,8},{6,10},{8,20},{10,22},{12,16},{14,18},{16,28},... | collective-permute-start | bytes 147464 | tf_op jit(solution)/shard_map/ppermute | solution.py:585
  21.7 7.3 %copy-start.2 = (s32[8,4]{1,0:T(8,128)S(1)}, s32[8,4]{1,0:T(8,128)}, u32[]{:S(2)}) copy-start(s32[8,4]{1,0:T(8,128)} %constant.2.clone.tables_in) | copy-start | bytes 388
  21.7 7.3 %copy-start.3 = (s32[16,4]{0,1:T(4,128)S(1)}, s32[16,4]{0,1:T(4,128)}, u32[]{:S(2)}) copy-start(s32[16,4]{0,1:T(4,128)} %param.11) | copy-start | bytes 772
  21.7 7.3 %copy-start.4 = (s32[16,4]{0,1:T(4,128)S(1)}, s32[16,4]{0,1:T(4,128)}, u32[]{:S(2)}) copy-start(s32[16,4]{0,1:T(4,128)} %param.12) | copy-start | bytes 772
  21.7 7.3 %copy-start.5 = (s32[16,4]{0,1:T(4,128)S(1)}, s32[16,4]{0,1:T(4,128)}, u32[]{:S(2)}) copy-start(s32[16,4]{0,1:T(4,128)} %param.13) | copy-start | bytes 772
  21.7 7.2 %copy-start.6 = (s32[16,4]{0,1:T(4,128)S(1)}, s32[16,4]{0,1:T(4,128)}, u32[]{:S(2)}) copy-start(s32[16,4]{0,1:T(4,128)} %param.14) | copy-start | bytes 772
  25.1 6.0 %collective-permute-start.12 = (f32[896,384]{1,0:T(8,128)S(1)}, f32[896,384]{1,0:T(8,128)S(1)}, u32[]{:S(2)}, u32[]{:S(2)}) collective-permute-start(f32[896,384]{1,0:T(8,128)S(1)} %get-tuple-element.81), channel_id=1, source_target_pairs={{0,2},{2,0},{4,6},{6,4},{8,10},{10,8},{12,14},{14,12},{16,18},{18,... | collective-permute-start | bytes 4128776 | tf_op jit(solution)/shard_map/ppermute | solution.py:59
  25.1 3.2 %collective-permute-start.10 = (bf16[192,128]{1,0:T(8,128)(2,1)S(1)}, bf16[192,128]{1,0:T(8,128)(2,1)S(1)}, u32[]{:S(2)}, u32[]{:S(2)}) collective-permute-start(bf16[192,128]{1,0:T(8,128)(2,1)S(1)} %collective-permute-done.3.refs_4_), channel_id=1, source_target_pairs={{0,2},{2,0},{4,6},{6,4},{8,10},{10,8},{12,14},{14,12},{16,18},{18,... | collective-permute-start | bytes 147464 | tf_op jit(solution)/shard_map/ppermute | solution.py:59
  25.6 2.8 %collective-permute-start.11 = (bf16[192,128]{1,0:T(8,128)(2,1)S(1)}, bf16[192,128]{1,0:T(8,128)(2,1)S(1)}, u32[]{:S(2)}, u32[]{:S(2)}) collective-permute-start(bf16[192,128]{1,0:T(8,128)(2,1)S(1)} %collective-permute-done.4.refs_5_), channel_id=1, source_target_pairs={{0,2},{2,0},{4,6},{6,4},{8,10},{10,8},{12,14},{14,12},{16,18},{18,... | collective-permute-start | bytes 147464 | tf_op jit(solution)/shard_map/ppermute | solution.py:59
  25.7 3.1 %collective-permute-start.6 = (bf16[192,128]{1,0:T(8,128)(2,1)S(1)}, bf16[192,128]{1,0:T(8,128)(2,1)S(1)}, u32[]{:S(2)}, u32[]{:S(2)}) collective-permute-start(bf16[192,128]{1,0:T(8,128)(2,1)S(1)} %get-tuple-element.94.refs_0_), channel_id=1, source_target_pairs={{0,2},{2,0},{4,6},{6,4},{8,10},{10,8},{12,14},{14,12},{16,18},{18,... | collective-permute-start | bytes 147464 | tf_op jit(solution)/shard_map/ppermute | solution.py:59
  26.1 4.9 %collective-permute-start.13 = (bf16[128,384]{1,0:T(8,128)(2,1)S(1)}, bf16[128,384]{1,0:T(8,128)(2,1)S(1)}, u32[]{:S(2)}, u32[]{:S(2)}) collective-permute-start(bf16[128,384]{1,0:T(8,128)(2,1)S(1)} %get-tuple-element.82.refs_15_), channel_id=1, source_target_pairs={{0,2},{2,0},{4,6},{6,4},{8,10},{10,8},{12,14},{14,12},{16,18},{18,... | collective-permute-start | bytes 294920 | tf_op jit(solution)/shard_map/ppermute | solution.py:59
  28.3 2.7 %collective-permute-start.7 = (bf16[192,128]{1,0:T(8,128)(2,1)S(1)}, bf16[192,128]{1,0:T(8,128)(2,1)S(1)}, u32[]{:S(2)}, u32[]{:S(2)}) collective-permute-start(bf16[192,128]{1,0:T(8,128)(2,1)S(1)} %collective-permute-done.refs_1_), channel_id=1, source_target_pairs={{0,2},{2,0},{4,6},{6,4},{8,10},{10,8},{12,14},{14,12},{16,18},{18,... | collective-permute-start | bytes 147464 | tf_op jit(solution)/shard_map/ppermute | solution.py:59
  28.5 2.5 %collective-permute-start.8 = (bf16[192,128]{1,0:T(8,128)(2,1)S(1)}, bf16[192,128]{1,0:T(8,128)(2,1)S(1)}, u32[]{:S(2)}, u32[]{:S(2)}) collective-permute-start(bf16[192,128]{1,0:T(8,128)(2,1)S(1)} %collective-permute-done.1.refs_2_), channel_id=1, source_target_pairs={{0,2},{2,0},{4,6},{6,4},{8,10},{10,8},{12,14},{14,12},{16,18},{18,... | collective-permute-start | bytes 147464 | tf_op jit(solution)/shard_map/ppermute | solution.py:59
  28.8 2.2 %collective-permute-start.9 = (bf16[192,128]{1,0:T(8,128)(2,1)S(1)}, bf16[192,128]{1,0:T(8,128)(2,1)S(1)}, u32[]{:S(2)}, u32[]{:S(2)}) collective-permute-start(bf16[192,128]{1,0:T(8,128)(2,1)S(1)} %collective-permute-done.2.refs_3_), channel_id=1, source_target_pairs={{0,2},{2,0},{4,6},{6,4},{8,10},{10,8},{12,14},{14,12},{16,18},{18,... | collective-permute-start | bytes 147464 | tf_op jit(solution)/shard_map/ppermute | solution.py:59
  31.0 6.2 %copy-start.7 = (bf16[3,3,384,384]{3,2,1,0:T(8,128)(2,1)S(1)}, bf16[3,3,384,384]{3,2,1,0:T(8,128)(2,1)}, u32[]{:S(2)}) copy-start(bf16[3,3,384,384]{3,2,1,0:T(8,128)(2,1)} %param.9) | copy-start | bytes 7962628
  33.0 20.7 %collective-permute-start.20 = (bf16[1752,128]{1,0:T(8,128)(2,1)S(1)}, bf16[1752,128]{1,0:T(8,128)(2,1)S(1)}, u32[]{:S(2)}, u32[]{:S(2)}) collective-permute-start(bf16[1752,128]{1,0:T(8,128)(2,1)S(1)} %get-tuple-element.118), channel_id=1, source_target_pairs={{0,1},{1,0},{2,3},{3,2},{4,5},{5,4},{6,7},{7,6},{8,9},{9,8},{10,11... | collective-permute-start | bytes 1345544 | tf_op jit(solution)/shard_map/ppermute | solution.py:632
  33.7 8.2 %collective-permute-start.14 = (bf16[224,384]{1,0:T(8,128)(2,1)S(1)}, bf16[224,384]{1,0:T(8,128)(2,1)S(1)}, u32[]{:S(2)}, u32[]{:S(2)}) collective-permute-start(bf16[224,384]{1,0:T(8,128)(2,1)S(1)} %get-tuple-element.88), channel_id=1, source_target_pairs={{0,4},{2,6},{4,0},{6,2},{8,12},{10,14},{12,8},{14,10},{16,20},{18,... | collective-permute-start | bytes 516104 | tf_op jit(solution)/shard_map/ppermute | solution.py:59
  35.2 7.3 %collective-permute-start.15 = (bf16[224,384]{1,0:T(8,128)(2,1)S(1)}, bf16[224,384]{1,0:T(8,128)(2,1)S(1)}, u32[]{:S(2)}, u32[]{:S(2)}) collective-permute-start(bf16[224,384]{1,0:T(8,128)(2,1)S(1)} %get-tuple-element.89), channel_id=1, source_target_pairs={{0,8},{2,10},{4,12},{6,14},{8,0},{10,2},{12,4},{14,6},{16,24},{18,... | collective-permute-start | bytes 516104 | tf_op jit(solution)/shard_map/ppermute | solution.py:59
  35.2 9.7 %collective-permute-start.16 = (bf16[224,384]{1,0:T(8,128)(2,1)S(1)}, bf16[224,384]{1,0:T(8,128)(2,1)S(1)}, u32[]{:S(2)}, u32[]{:S(2)}) collective-permute-start(bf16[224,384]{1,0:T(8,128)(2,1)S(1)} %get-tuple-element.90), channel_id=1, source_target_pairs={{0,12},{2,14},{4,8},{6,10},{8,4},{10,6},{12,0},{14,2},{16,28},{18,... | collective-permute-start | bytes 516104 | tf_op jit(solution)/shard_map/ppermute | solution.py:59
  45.0 8.7 %collective-permute-start.17 = (bf16[112,384]{1,0:T(8,128)(2,1)S(1)}, bf16[112,384]{1,0:T(8,128)(2,1)S(1)}, u32[]{:S(2)}, u32[]{:S(2)}) collective-permute-start(bf16[112,384]{1,0:T(8,128)(2,1)S(1)} %get-tuple-element.114), channel_id=1, source_target_pairs={{0,16},{2,18},{4,20},{6,22},{8,24},{10,26},{12,28},{14,30},{16,0},... | collective-permute-start | bytes 258056 | tf_op jit(solution)/shard_map/ppermute | solution.py:59
  45.1 4.8 %collective-permute-start.18 = (bf16[216,128]{1,0:T(8,128)(2,1)S(1)}, bf16[216,128]{1,0:T(8,128)(2,1)S(1)}, u32[]{:S(2)}, u32[]{:S(2)}) collective-permute-start(bf16[216,128]{1,0:T(8,128)(2,1)S(1)} %get-tuple-element.115.refs_0_), channel_id=1, source_target_pairs={{0,24},{2,26},{4,28},{6,30},{8,0},{10,2},{12,4},{14,6},{16,8},{18,... | collective-permute-start | bytes 165896 | tf_op jit(solution)/shard_map/ppermute | solution.py:55
  47.7 6.0 %collective-permute-start.19 = (bf16[216,128]{1,0:T(8,128)(2,1)S(1)}, bf16[216,128]{1,0:T(8,128)(2,1)S(1)}, u32[]{:S(2)}, u32[]{:S(2)}) collective-permute-start(bf16[216,128]{1,0:T(8,128)(2,1)S(1)} %get-tuple-element.115.refs_0_), channel_id=1, source_target_pairs={{0,8},{2,10},{4,12},{6,14},{8,16},{10,18},{12,20},{14,22},{16,24},... | collective-permute-start | bytes 165896 | tf_op jit(solution)/shard_map/ppermute | solution.py:55
  53.7 7.2 %collective-permute-start.22 = (bf16[648,128]{1,0:T(8,128)(2,1)S(1)}, bf16[648,128]{1,0:T(8,128)(2,1)S(1)}, u32[]{:S(2)}, u32[]{:S(2)}) collective-permute-start(bf16[648,128]{1,0:T(8,128)(2,1)S(1)} %shard_map.110.refs_0_), channel_id=1, source_target_pairs={{0,4},{2,6},{4,0},{6,2},{8,12},{10,14},{12,8},{14,10},{16,20},{18,... | collective-permute-start | bytes 497672 | tf_op jit(solution)/shard_map/ppermute | solution.py:59
  55.3 5.6 %collective-permute-start.21 = (bf16[112,384]{1,0:T(8,128)(2,1)S(1)}, bf16[112,384]{1,0:T(8,128)(2,1)S(1)}, u32[]{:S(2)}, u32[]{:S(2)}) collective-permute-start(bf16[112,384]{1,0:T(8,128)(2,1)S(1)} %shard_map.111.refs_0_), channel_id=1, source_target_pairs={{0,16},{2,18},{4,20},{6,22},{8,24},{10,26},{12,28},{14,30},{16,0},... | collective-permute-start | bytes 258056 | tf_op jit(solution)/shard_map/ppermute | solution.py:59
  60.9 6.6 %collective-permute-start.23 = (bf16[224,384]{1,0:T(8,128)(2,1)S(1)}, bf16[224,384]{1,0:T(8,128)(2,1)S(1)}, u32[]{:S(2)}, u32[]{:S(2)}) collective-permute-start(bf16[224,384]{1,0:T(8,128)(2,1)S(1)} %shard_map.113.refs_0_), channel_id=1, source_target_pairs={{0,4},{2,6},{4,0},{6,2},{8,12},{10,14},{12,8},{14,10},{16,20},{18,... | collective-permute-start | bytes 516104 | tf_op jit(solution)/shard_map/ppermute | solution.py:59
  61.5 6.0 %collective-permute-start.24 = (bf16[224,384]{1,0:T(8,128)(2,1)S(1)}, bf16[224,384]{1,0:T(8,128)(2,1)S(1)}, u32[]{:S(2)}, u32[]{:S(2)}) collective-permute-start(bf16[224,384]{1,0:T(8,128)(2,1)S(1)} %shard_map.113.refs_0_), channel_id=1, source_target_pairs={{0,8},{2,10},{4,12},{6,14},{8,0},{10,2},{12,4},{14,6},{16,24},{18,... | collective-permute-start | bytes 516104 | tf_op jit(solution)/shard_map/ppermute | solution.py:59
  61.5 8.2 %collective-permute-start.25 = (bf16[224,384]{1,0:T(8,128)(2,1)S(1)}, bf16[224,384]{1,0:T(8,128)(2,1)S(1)}, u32[]{:S(2)}, u32[]{:S(2)}) collective-permute-start(bf16[224,384]{1,0:T(8,128)(2,1)S(1)} %shard_map.113.refs_0_), channel_id=1, source_target_pairs={{0,12},{2,14},{4,8},{6,10},{8,4},{10,6},{12,0},{14,2},{16,28},{18,... | collective-permute-start | bytes 516104 | tf_op jit(solution)/shard_map/ppermute | solution.py:59
  64.5 1.4 %collective-permute-start.26 = (bf16[648,128]{1,0:T(8,128)(2,1)S(1)}, bf16[648,128]{1,0:T(8,128)(2,1)S(1)}, u32[]{:S(2)}, u32[]{:S(2)}) collective-permute-start(bf16[648,128]{1,0:T(8,128)(2,1)S(1)} %shard_map.110.refs_0_), channel_id=1, source_target_pairs={{0,2},{2,0},{4,6},{6,4},{8,10},{10,8},{12,14},{14,12},{16,18},{18,... | collective-permute-start | bytes 497672 | tf_op jit(solution)/shard_map/ppermute | solution.py:59
  64.5 1.6 %collective-permute-start.27 = (bf16[648,128]{1,0:T(8,128)(2,1)S(1)}, bf16[648,128]{1,0:T(8,128)(2,1)S(1)}, u32[]{:S(2)}, u32[]{:S(2)}) collective-permute-start(bf16[648,128]{1,0:T(8,128)(2,1)S(1)} %collective-permute-done.22.refs_1_), channel_id=1, source_target_pairs={{0,2},{2,0},{4,6},{6,4},{8,10},{10,8},{12,14},{14,12},{16,18},{18,... | collective-permute-start | bytes 497672 | tf_op jit(solution)/shard_map/ppermute | solution.py:59
  65.9 5.6 %collective-permute-start.28 = (bf16[224,384]{1,0:T(8,128)(2,1)S(1)}, bf16[224,384]{1,0:T(8,128)(2,1)S(1)}, u32[]{:S(2)}, u32[]{:S(2)}) collective-permute-start(bf16[224,384]{1,0:T(8,128)(2,1)S(1)} %shard_map.113.refs_0_), channel_id=1, source_target_pairs={{0,2},{2,0},{4,6},{6,4},{8,10},{10,8},{12,14},{14,12},{16,18},{18,... | collective-permute-start | bytes 516104 | tf_op jit(solution)/shard_map/ppermute | solution.py:59
  69.7 1.7 %collective-permute-start.29 = (bf16[224,384]{1,0:T(8,128)(2,1)S(1)}, bf16[224,384]{1,0:T(8,128)(2,1)S(1)}, u32[]{:S(2)}, u32[]{:S(2)}) collective-permute-start(bf16[224,384]{1,0:T(8,128)(2,1)S(1)} %collective-permute-done.23.refs_1_), channel_id=1, source_target_pairs={{0,2},{2,0},{4,6},{6,4},{8,10},{10,8},{12,14},{14,12},{16,18},{18,... | collective-permute-start | bytes 516104 | tf_op jit(solution)/shard_map/ppermute | solution.py:59
  69.7 1.7 %collective-permute-start.30 = (bf16[224,384]{1,0:T(8,128)(2,1)S(1)}, bf16[224,384]{1,0:T(8,128)(2,1)S(1)}, u32[]{:S(2)}, u32[]{:S(2)}) collective-permute-start(bf16[224,384]{1,0:T(8,128)(2,1)S(1)} %collective-permute-done.24.refs_2_), channel_id=1, source_target_pairs={{0,2},{2,0},{4,6},{6,4},{8,10},{10,8},{12,14},{14,12},{16,18},{18,... | collective-permute-start | bytes 516104 | tf_op jit(solution)/shard_map/ppermute | solution.py:59
  70.2 1.4 %collective-permute-start.31 = (bf16[224,384]{1,0:T(8,128)(2,1)S(1)}, bf16[224,384]{1,0:T(8,128)(2,1)S(1)}, u32[]{:S(2)}, u32[]{:S(2)}) collective-permute-start(bf16[224,384]{1,0:T(8,128)(2,1)S(1)} %collective-permute-done.25.refs_3_), channel_id=1, source_target_pairs={{0,2},{2,0},{4,6},{6,4},{8,10},{10,8},{12,14},{14,12},{16,18},{18,... | collective-permute-start | bytes 516104 | tf_op jit(solution)/shard_map/ppermute | solution.py:59

commit v6 on v5

--- a/solution.py
+++ b/solution.py
@@ -140,18 +140,12 @@
     out_ref[row + rows // 2 : row + rows, part - 64 :] = rest[:, 64:]
 
 
-def prepare_kernel(side, part, field_in, cot_in, sides_ref, cot_packed_ref, field_ref, cot_ref, sems):
-    field_copy = pltpu.make_async_copy(field_in, field_ref, sems.at[0])
-    cot_copy = pltpu.make_async_copy(cot_in, cot_ref, sems.at[1])
-    field_copy.start()
-    cot_copy.start()
-    field_copy.wait()
+def sides_kernel(side, field_ref, sides_ref, copy_ref):
     sides = jnp.concatenate(
         [field_ref[0], field_ref[:, side - 1, :], field_ref[side - 1], field_ref[:, 0, :]], axis=0
     )
     pack(sides, sides_ref)
-    cot_copy.wait()
-    pack(cot_ref[...], cot_packed_ref)
+    copy_ref[...] = field_ref[...]
 
 
 def shifted_columns(side, part, field, halos, out_ref):
@@ -174,19 +168,12 @@
     out_ref[2] = jnp.where(column == side - 1, east, pltpu.roll(tall, flat - 1, 0)).astype(jnp.bfloat16)
 
 
-def onehot_kernel(
-    side, tables_in, et_in, eu_in, ct_in, cu_in, border_ref, halo_ref, place_ref, tables, et, eu, ct, cu, sems
-):
-    copies = [
-        pltpu.make_async_copy(a, b, sems.at[i])
-        for i, (a, b) in enumerate(
-            [(tables_in, tables), (et_in, et), (eu_in, eu), (ct_in, ct), (cu_in, cu)]
-        )
-    ]
-    for copy in copies:
-        copy.start()
-    for copy in copies:
-        copy.wait()
+def onehot_kernel(side, tables_in, cot_in, border_ref, halo_ref, place_ref, cot_ref, tables, sem):
+    copy = pltpu.make_async_copy(tables_in, tables, sem)
+    copy.start()
+    cot_ref[...] = cot_in[...]
+    copy.wait()
+    et, eu, ct, cu = [tables.at[8 + 4 * i : 12 + 4 * i] for i in range(4)]
     count = lax.axis_size("tile")
     own = lax.axis_index("tile")
     core = lax.rem(own, 2)
@@ -196,7 +183,7 @@
         slab = lax.rem(source // SPAN - own // SPAN + groups, groups)
         cross = source ^ own
         turn = lax.rem(cross // 2, 2)
-        at = jnp.where(slab == 0, turn, jnp.where(slab == 1, 2, 3) + 2 * turn)
+        at = jnp.where(slab == 0, 0, jnp.where(slab == 1, 2, 4)) + turn
         return (6 * lax.rem(cross, 2) + at) * (4 * side)
 
     step = lax.broadcasted_iota(jnp.int32, (side, 1), 0)
@@ -257,53 +244,48 @@
     place_ref[...] = jnp.concatenate(places, axis=1).astype(jnp.bfloat16)
 
 
-def inner_kernel(
-    side, part, half, scale, field_ref, own_ref, other_ref, mine_ref, send_ref, cot_ref, rim_ref, cols, total
+def half_taps(side, part, half, scale, which, cols, cot, out_ref, middle):
+    rows = side * side
+    used = 9 * part // 2
+
+    def product(a, b):
+        value = lax.dot_general(
+            cols[b, pl.ds(pl.multiple_of(a * side, 16), rows), :],
+            cot,
+            (((0,), (0,)), ((), ())),
+            preferred_element_type=jnp.float32,
+        )
+        return value * scale
+
+    for j in range(4):
+        tap = j + 5 * which
+        start = pl.multiple_of(which * (part // 2) + j * part, 16)
+        out_ref[pl.ds(start, part), :] = product(tap // 3, lax.rem(tap, 3))
+    middle[...] = product(1, 1)
+    start = pl.multiple_of((1 - which) * 4 * part, 16)
+    out_ref[pl.ds(start, part // 2), :] = middle[pl.ds(pl.multiple_of(which * (part // 2), 16), part // 2), :]
+    out_ref[used:, :] = jnp.zeros((half - used, cot.shape[1]), jnp.float32)
+
+
+def send_kernel(
+    side, part, half, scale, field_ref, own_ref, other_ref, send_ref, cot_ref, rim_ref, cols, middle
 ):
     rows = side * side
     chans = cot_ref.shape[1]
     first = lax.axis_index("ch") == 0
-    unpack(other_ref, cols.at[0], 0, 0, rows, part)
 
     @pl.when(first)
     def _():
         cot_ref[:, 0:part] = own_ref[...]
-        cot_ref[:, part:] = cols[0, 0:rows, :]
+        cot_ref[:, part:] = other_ref[...]
 
     @pl.when(jnp.logical_not(first))
     def _():
-        cot_ref[:, 0:part] = cols[0, 0:rows, :]
+        cot_ref[:, 0:part] = other_ref[...]
         cot_ref[:, part:] = own_ref[...]
 
     shifted_columns(side, part, field_ref[...].reshape(rows, part), None, cols)
     cot = cot_ref[...]
-    used = 9 * part // 2
-    for a in range(3):
-        for b in range(3):
-            tap = 3 * a + b
-            value = (
-                lax.dot_general(
-                    cols[b, a * side : a * side + rows, :],
-                    cot,
-                    (((0,), (0,)), ((), ())),
-                    preferred_element_type=jnp.float32,
-                )
-                * scale
-            )
-            if tap < 4:
-                total[tap * part : (tap + 1) * part, :] = value
-            elif tap > 4:
-                start = half + part // 2 + (tap - 5) * part
-                total[start : start + part, :] = value
-            else:
-                total[4 * part : used, :] = value[: part // 2]
-                total[half : half + part // 2, :] = value[part // 2 :]
-    blank = jnp.zeros((half - used, chans), jnp.float32)
-    total[used:half, :] = blank
-    total[half + used : 2 * half, :] = blank
-    core = lax.rem(lax.axis_index("tile"), 2)
-    mine_ref[...] = total[pl.ds(pl.multiple_of(core * half, 16), half), :]
-    send_ref[...] = total[pl.ds(pl.multiple_of((1 - core) * half, 16), half), :]
     rim_ref[...] = jnp.concatenate(
         [
             cot[0:side],
@@ -313,6 +295,20 @@
         ],
         axis=0,
     )
+    which = 1 - lax.rem(lax.axis_index("tile"), 2)
+    half_taps(side, part, half, scale, which, cols, cot, send_ref, middle)
+
+
+def mine_kernel(side, part, half, scale, cols, cot_ref, mine_ref, middle):
+    which = lax.rem(lax.axis_index("tile"), 2)
+    half_taps(side, part, half, scale, which, cols, cot_ref[...], mine_ref, middle)
+
+
+def unpack_near(near_refs, near, side, part):
+    size = packed_shape(4 * side, part)[0]
+    for i, ref in enumerate(near_refs):
+        for k in range(2):
+            unpack(ref, near, k * size, (2 * i + k) * 4 * side, 4 * side, part)
 
 
 def border_kernel(side, part, chunk, scale, n_near, *refs):
@@ -322,8 +318,7 @@
     count = lax.axis_size("tile")
     own = lax.axis_index("tile")
     core = lax.rem(own, 2)
-    for i, ref in enumerate(near_refs):
-        unpack(ref, near, 0, i * 4 * side, 4 * side, part)
+    unpack_near(near_refs, near, side, part)
     total[...] = mine_ref[...] + got_ref[...]
     left = jnp.dot(onehot_ref[...], near[...], preferred_element_type=jnp.float32).astype(jnp.bfloat16)
 
@@ -374,15 +369,15 @@
         row += ref.shape[0]
 
 
-def unfold_kernel(used, chunk, bit, masks, n_dep, *refs):
+def unfold_kernel(used, chunk, bits, masks, n_dep, *refs):
     refs = refs[n_dep:]
     n = len(masks)
     in_refs, out_ref, wide, sems = refs[:n], refs[n], refs[n + 1], refs[n + 2]
     own = lax.axis_index("tile")
-    origin = (lax.rem(own, 2) ^ bit) * used
     full, rest = used // chunk, used % chunk
     copies = []
-    for i, (ref, inner) in enumerate(zip(in_refs, masks)):
+    for i, (ref, inner, bit) in enumerate(zip(in_refs, masks, bits)):
+        origin = (lax.rem(own, 2) ^ bit) * used
         for k, mask in enumerate(inner):
             at = i * len(inner) + k
             wide[at] = ref[k * chunk : (k + 1) * chunk, :].astype(jnp.float32)
@@ -410,12 +405,12 @@
         pl.when(going)(copy.wait)
 
 
-def unfold(whole, chunk, bit, masks, blocks, before):
+def unfold(whole, chunk, bits, masks, blocks, before):
     n_dep = 0 if before is None else 1
     anywhere = pl.BlockSpec(memory_space=pl.ANY)
     n_copies = len(masks) * len(masks[0])
     return pl.pallas_call(
-        functools.partial(unfold_kernel, whole.shape[0] // 2, chunk, bit, masks, n_dep),
+        functools.partial(unfold_kernel, whole.shape[0] // 2, chunk, bits, masks, n_dep),
         out_shape=whole,
         in_specs=[anywhere] * n_dep + [pl.BlockSpec(memory_space=pltpu.VMEM)] * len(blocks),
         out_specs=anywhere,
@@ -428,29 +423,21 @@
     )(*([before] if n_dep else []), *blocks)
 
 
-def back_kernel(side, part, cot_ref, weight_in, inner_ref, pieces_ref, tall, weight, sems):
+def back_kernel(side, part, cot_ref, weight_ref, inner_ref, pieces_ref, tall):
     rows = side * side
     flat = rows + 2 * side
     start = pl.multiple_of(lax.axis_index("ch") * part, 16)
-    copies = [
-        pltpu.make_async_copy(weight_in.at[tap, pl.ds(start, part), :], weight.at[tap], sems.at[tap])
-        for tap in range(9)
-    ]
-    for copy in copies:
-        copy.start()
     blank = jnp.zeros((2 * side, tall.shape[1]), jnp.bfloat16)
     tall[0 : 2 * side, :] = blank
     tall[2 * side : 2 * side + rows, :] = cot_ref[...]
     tall[2 * side + rows :, :] = blank
-    for copy in copies:
-        copy.wait()
     backs = []
     for b in range(3):
         back = jnp.zeros((flat, part), jnp.float32)
         for a in range(3):
             back = back + lax.dot_general(
                 tall[(2 - a) * side : (2 - a) * side + flat, :],
-                weight[3 * a + b],
+                weight_ref[3 * a + b, pl.ds(start, part), :],
                 (((1,), (1,)), ((), ())),
                 preferred_element_type=jnp.float32,
             )
@@ -510,31 +497,22 @@
     near_refs, onehot_ref, field_ref = refs[:n_near], refs[n_near], refs[n_near + 1]
     halos_ref, packet_ref, near = refs[n_near + 2 :]
     rows = side * side
-    for i, ref in enumerate(near_refs):
-        unpack(ref, near, 0, i * 4 * side, 4 * side, part)
+    unpack_near(near_refs, near, side, part)
     halos = jnp.dot(onehot_ref[...], near[...], preferred_element_type=jnp.float32).astype(jnp.bfloat16)
     halos_ref[...] = halos
     pack(field_ref[...].reshape(rows, part), packet_ref)
     pack(halos, packet_ref, packed_shape(rows, part)[0])
 
 
-def output_kernel(side, part, field_ref, halos_ref, other_ref, weight_in, out_ref, cols, other_cols, other, weight, sems):
+def output_kernel(side, part, field_ref, halos_ref, other_ref, weight_ref, out_ref, cols, other_cols, other):
     rows = side * side
     ch = lax.axis_index("ch")
-    wide = weight.shape[2]
-    lanes = pl.multiple_of(ch * (weight_in.shape[2] - wide), 128)
-    copies = [
-        pltpu.make_async_copy(weight_in.at[tap, :, pl.ds(lanes, wide)], weight.at[tap], sems.at[tap])
-        for tap in range(9)
-    ]
-    for copy in copies:
-        copy.start()
+    wide = -(-part // 128) * 128
+    lanes = pl.multiple_of(ch * (weight_ref.shape[2] - wide), 128)
     unpack(other_ref, other, 0, 0, rows, part)
     unpack(other_ref, other, packed_shape(rows, part)[0], rows, 4 * side + EXTRA, part)
     shifted_columns(side, part, field_ref[...].reshape(rows, part), halos_ref[...], cols)
     shifted_columns(side, part, other[0:rows, :], other[rows:, :], other_cols)
-    for copy in copies:
-        copy.wait()
     starts = (pl.multiple_of(ch * part, 16), pl.multiple_of((1 - ch) * part, 16))
     total = jnp.zeros((rows, wide), jnp.float32)
     for a in range(3):
@@ -542,7 +520,7 @@
             for ref, first in zip((cols, other_cols), starts):
                 total = total + jnp.dot(
                     ref[b, a * side : a * side + rows, :],
-                    weight[3 * a + b, pl.ds(first, part), :],
+                    weight_ref[3 * a + b, pl.ds(first, part), pl.ds(lanes, wide)],
                     preferred_element_type=jnp.float32,
                 )
     result = jnp.where(ch == 0, total[:, :part], total[:, wide - part :])
@@ -565,51 +543,49 @@
     half = count * chunk // 2
     scale = 1.0 / math.sqrt(count * rows)
 
-    sides, cot_packed, field, cot_own = call(
-        functools.partial(prepare_kernel, side, part),
-        [
-            vmem(packed_shape(4 * side, part), half_bytes),
-            vmem(packed_shape(rows, part), half_bytes),
-            vmem((side, side, part), half_bytes),
-            vmem((rows, part), half_bytes),
-        ],
-        [field, cotangent[0].reshape(rows, part)],
-        anywhere=(0, 1),
-        scratch=[pltpu.SemaphoreType.DMA((2,))],
-    )
-    cot_other = lax.ppermute(cot_packed, "ch", others)
-    near = [sides, by_mask(sides, 2, count)]
-    for flip in (0, 2):
-        for offset in (SPAN, -SPAN):
-            pairs = [(i, ((i - offset) % count) ^ flip) for i in range(count)]
-            near.append(lax.ppermute(sides, "tile", pairs))
-    near, cot_other = lax.optimization_barrier((near, cot_other))
-    near = near + [by_mask(v, 1, count) for v in near]
-
-    border_pick, halo_pick, place = call(
+    cot_own = cotangent[0].reshape(rows, part)
+    cot_other = lax.ppermute(cot_own, "ch", others)
+    sides, field = call(
+        functools.partial(sides_kernel, side),
+        [vmem(packed_shape(4 * side, part), half_bytes), vmem(field.shape, half_bytes)],
+        [field],
+    )
+    pair = packed_shape(8 * side, part)
+    (near,) = call(join_kernel, [vmem(pair, half_bytes)], [sides, by_mask(sides, 2, count)])
+    near = [near, by_offset(near, -SPAN, count), by_offset(near, SPAN, count)]
+    tables = jnp.pad(jnp.asarray(turn_tables()), ((0, 0), (0, count - 4)))
+    tables = jnp.concatenate([tables, edge_tiles.T, edge_turns.T, corner_tiles.T, corner_turns.T], axis=0)
+    border_pick, halo_pick, place, cot_own = call(
         functools.partial(onehot_kernel, side),
         [
             vmem((16 * side, 48 * side), half_bytes),
             vmem((block, 48 * side), half_bytes),
             vmem((4 * side, 12 * block), half_bytes),
+            vmem((rows, part), half_bytes),
         ],
-        [jnp.asarray(turn_tables()), edge_tiles.T, edge_turns.T, corner_tiles.T, corner_turns.T],
-        anywhere=range(5),
-        scratch=[pltpu.SMEM((8, 4), jnp.int32)]
-        + [pltpu.SMEM((4, count), jnp.int32)] * 4
-        + [pltpu.SemaphoreType.DMA((5,))],
-    )
-    mine, send, cot_full, rim = call(
-        functools.partial(inner_kernel, side, part, half, scale),
+        [tables, cot_own],
+        scratch=[pltpu.SMEM(tables.shape, jnp.int32), pltpu.SemaphoreType.DMA],
+    )
+    near, cot_other, border_pick = lax.optimization_barrier((near, cot_other, border_pick))
+    near = near + [by_mask(v, 1, count) for v in near]
+    send, cot_full, rim, cols = call(
+        functools.partial(send_kernel, side, part, half, scale),
         [
-            vmem((half, chans), jnp.float32),
             vmem((half, chans), jnp.float32),
             vmem((rows, chans), half_bytes),
             vmem((4 * side, chans), half_bytes),
+            vmem((3, flat, part), half_bytes),
         ],
         [field, cot_own, cot_other],
-        scratch=[pltpu.VMEM((3, flat, part), half_bytes), pltpu.VMEM((2 * half, chans), jnp.float32)],
-        flops=flops,
+        scratch=[pltpu.VMEM((part, chans), jnp.float32)],
+        flops=flops // 2,
+    )
+    (mine,) = call(
+        functools.partial(mine_kernel, side, part, half, scale),
+        [vmem((half, chans), jnp.float32)],
+        [cols, cot_full],
+        scratch=[pltpu.VMEM((part, chans), jnp.float32)],
+        flops=flops // 2,
     )
 
     stages = mask_stages(count)
@@ -621,7 +597,7 @@
         [*near, border_pick, mine, by_mask(send, 1, count), rim, by_mask(rim, 1, count)],
         scratch=[pltpu.VMEM((48 * side, part), half_bytes), pltpu.VMEM((half, chans), jnp.float32)],
     )
-    send, near, cot_full = lax.optimization_barrier((send, near, cot_full))
+    send, cot_full = lax.optimization_barrier((send, cot_full))
     got = [by_mask(v, m, count) for v, m in zip(send, masks[1:])]
     halos, packet = call(
         functools.partial(halo_kernel, side, part, len(near)),
@@ -634,12 +610,7 @@
         functools.partial(back_kernel, side, part),
         [vmem((rows, part), jnp.float32), vmem(packed_shape(block, part), half_bytes)],
         [cot_full, taps],
-        anywhere=(1,),
-        scratch=[
-            pltpu.VMEM((rows + 4 * side, chans), half_bytes),
-            pltpu.VMEM((9, part, chans), half_bytes),
-            pltpu.SemaphoreType.DMA((9,)),
-        ],
+        scratch=[pltpu.VMEM((rows + 4 * side, chans), half_bytes)],
         flops=flops,
     )
     got, pieces, inner, halos = lax.optimization_barrier((got, pieces, inner, halos))
@@ -655,27 +626,22 @@
         got = [by_mask(v, m, count) for v, m in zip(send, masks[1:])]
         if index == 0:
             here = [pieces, by_offset(pieces, -SPAN, count), by_offset(pieces, SPAN, count)]
-            (here,) = call(join_kernel, [vmem((3 * pieces.shape[0], pieces.shape[1]), half_bytes)], here)
-            got, here = lax.optimization_barrier((got, here))
     (held,) = call(functools.partial(sum_kernel, len(got), 1), [vmem(held.shape, half_bytes)], [held, *got])
     order = [0]
     for index, bits in enumerate(stages[:0:-1]):
         masks = group_masks(bits)
         if index == 0:
-            held, here, other_field = lax.optimization_barrier((held, here, other_field))
+            _, here, other_field = lax.optimization_barrier((held, here, other_field))
+            (here,) = call(join_kernel, [vmem((3 * pieces.shape[0], pieces.shape[1]), half_bytes)], here)
             beside = by_mask(here, 2, count)
-            wide = -(-part // 128) * 128
             (output,) = call(
                 functools.partial(output_kernel, side, part),
                 [vmem((rows, part), half_bytes)],
                 [field, halos, other_field, taps],
-                anywhere=(3,),
                 scratch=[
                     pltpu.VMEM((3, flat, part), half_bytes),
                     pltpu.VMEM((3, flat, part), half_bytes),
                     pltpu.VMEM((rows + block, part), half_bytes),
-                    pltpu.VMEM((9, chans, wide), half_bytes),
-                    pltpu.SemaphoreType.DMA((9,)),
                 ],
                 flops=2 * flops,
             )
@@ -700,8 +666,10 @@
         order = [[m + v for v in order] for m in masks]
     mates = [by_mask(v, 1, count) for v in got]
     whole = vmem((9 * part, chans), jnp.float32)
-    first = unfold(whole, chunk, 0, order, got, None)
-    grad_weight = unfold(whole, chunk, 1, order, mates, first)
+    early = len(got) - 1
+    bits = [0] * early + [1] * early
+    first = unfold(whole, chunk, bits, order[:-1] + order[:-1], got[:-1] + mates[:-1], None)
+    grad_weight = unfold(whole, chunk, [0, 1], order[-1:] * 2, [got[-1], mates[-1]], first)
     shape = (1, side, side, part)
     return (
         output.reshape(shape),

time: 73.2 us -> 70.6 us (0.964)
  starting transfers between devices: 26.8 us -> 24.1 us
  Pallas kernels: 20.6 us -> 18 us
  local copies, waits for them, and re-layouts: 2.11 us -> 4.2 us
    ppermute x24 -> x21, waiting for transfers between devices: 9.64 us -> 20.9 us  [by_mask(): return lax.ppermute(value, 'tile', [(i, i ^ mask) for i in range(count)])]
    ppermute x5 -> x1, starting transfers between devices: 10.4 us -> 3 us  [body(): cot_other = lax.ppermute(cot_own, 'ch', others)]
    ppermute x5 -> x1, waiting for transfers between devices: 6.78 us -> 0.01 us  [body(): cot_other = lax.ppermute(cot_own, 'ch', others)]
    ppermute x2 -> x4, waiting for transfers between devices: 5.95 us -> 2.15 us  [by_offset(): lax.ppermute(value, 'tile', [(i, (i + offset) % count) for i in range(cou...]
    ppermute x2 -> x4, starting transfers between devices: 2.63 us -> 5.68 us  [by_offset(): lax.ppermute(value, 'tile', [(i, (i + offset) % count) for i in range(cou...]
    pallas_call x12 -> x14, Pallas kernels: 18.2 us -> 15.6 us  [call(): pl.pallas_call(kernel, out_shape=tuple(outs), in_specs=in_specs, out_spec...]
    concatenate x0 -> x1, local copies, waits for them, and re-layouts: none -> 2.11 us  [body(): jnp.concatenate([tables, edge_tiles.T, edge_turns.T, corner_tiles.T, corn...]
    ppermute x24 -> x21, starting transfers between devices: 13.2 us -> 14.8 us  [by_mask(): return lax.ppermute(value, 'tile', [(i, i ^ mask) for i in range(count)])]
  transfers between devices with their start and end apart: 32 -> 27, of which waited for: 13 -> 16; matrix products, arithmetic and copies ran while one was open for 0% -> 3% of each run, Pallas kernels for 19% -> 22%
where the time goes in v6:
time: 70.6 us; the launch traced here: 70.3 us
  starting transfers between devices  24.1 us (34%)
  waiting for transfers between devices  23.1 us (33%)
  Pallas kernels  18 us (25%)
  local copies, waits for them, and re-layouts  4.2 us (6%)
  between operations  0.94 us (1%)
    ppermute x21, waiting for transfers between devices, by_mask(): return lax.ppermute(value, 'tile', [(i, i ^ mask) for i in range(count)])  20.9 us
    pallas_call x14, Pallas kernels, call(): pl.pallas_call(kernel, out_shape=tuple(outs), in_specs=in_specs, out_spec...  15.6 us
    ppermute x21, starting transfers between devices, by_mask(): return lax.ppermute(value, 'tile', [(i, i ^ mask) for i in range(count)])  14.8 us
    ppermute x4, starting transfers between devices, by_offset(): lax.ppermute(value, 'tile', [(i, (i + offset) % count) for i in range(cou...  5.68 us
    ppermute x1, starting transfers between devices, body(): cot_other = lax.ppermute(cot_own, 'ch', others)  3 us
    pallas_call x2, Pallas kernels, unfold(): pl.pallas_call(functools.partial(unfold_kernel, whole.shape[0] // 2, chun...  2.41 us
    ppermute x4, waiting for transfers between devices, by_offset(): lax.ppermute(value, 'tile', [(i, (i + offset) % count) for i in range(cou...  2.15 us
    concatenate x1, local copies, waits for them, and re-layouts, body(): jnp.concatenate([tables, edge_tiles.T, edge_turns.T, corner_tiles.T, corn...  2.11 us
  transfers between devices with their start and end apart: 27, of which 16 were waited for; matrix products, arithmetic and copies ran while one was open for 3% of the time, Pallas kernels for 22%

profile of v6, /device:TPU:0, one launch (start us, length us, event | category | flops | bytes accessed | tf_op | source)
XLA Modules:
  0.0 70.3 jit_solution(16866020294346929557)
XLA Ops:
  0.6 3.0 %collective-permute-start.3 = (bf16[1024,192]{1,0:T(8,128)(2,1)}, bf16[1024,192]{1,0:T(8,128)(2,1)S(1)}, u32[]{:S(2)}, u32[]{:S(2)}) collective-permute-start(bf16[1024,192]{1,0:T(8,128)(2,1)} %bitcast.11), channel_id=1, source_target_pairs={{0,1},{1,0},{2,3},{3,2},{4,5},{5,4},{6,7},{7,6},{8,9},{9,8},{10,11... | collective-permute-start | bytes 1179656 | tf_op jit(solution)/shard_map/ppermute | solution.py:547
  3.6 1.0 %copy-done = bf16[1,32,32,192]{3,2,1,0:T(8,128)(2,1)S(1)} copy-done((bf16[1,32,32,192]{3,2,1,0:T(8,128)(2,1)S(1)}, bf16[1,32,32,192]{3,2,1,0:T(8,128)(2,1)}, u32[]{:S(2)}) %copy-start) | copy-done | bytes 393240
  4.7 0.1 shard_map.103
  4.8 1.6 %collective-permute-start = (bf16[192,128]{1,0:T(8,128)(2,1)S(1)}, bf16[192,128]{1,0:T(8,128)(2,1)S(1)}, u32[]{:S(2)}, u32[]{:S(2)}) collective-permute-start(bf16[192,128]{1,0:T(8,128)(2,1)S(1)} %get-tuple-element.52.refs_0_), channel_id=1, source_target_pairs={{0,4},{2,6},{4,0},{6,2},{8,12},{10,14},{12,8},{14,10},{16,20},{18,... | collective-permute-start | bytes 147464 | tf_op jit(solution)/shard_map/ppermute | solution.py:59
  6.4 2.6 %collective-permute-done.refs_1_ = bf16[192,128]{1,0:T(8,128)(2,1)S(1)} collective-permute-done((bf16[192,128]{1,0:T(8,128)(2,1)S(1)}, bf16[192,128]{1,0:T(8,128)(2,1)S(1)}, u32[]{:S(2)}, u32[]{:S(2)}) %collective-permute-start) | collective-permute-done | bytes 49184 | tf_op jit(solution)/shard_map/ppermute | solution.py:59
  9.0 3.7 %collective-permute-start.1 = (bf16[384,128]{1,0:T(8,128)(2,1)S(1)}, bf16[384,128]{1,0:T(8,128)(2,1)S(1)}, u32[]{:S(2)}, u32[]{:S(2)}) collective-permute-start(bf16[384,128]{1,0:T(8,128)(2,1)S(1)} %shard_map.104.refs_0_), channel_id=1, source_target_pairs={{0,24},{2,26},{4,28},{6,30},{8,0},{10,2},{12,4},{14,6},{16,8},{18,... | collective-permute-start | bytes 294920 | tf_op jit(solution)/shard_map/ppermute | solution.py:55
  12.6 2.1 %concatenate.3.tables_in = s32[24,16]{1,0:T(8,128)S(1)} concatenate(s32[8,16]{1,0:T(8,128)} %constant.9, s32[4,16]{1,0:T(4,128)} %bitcast.17, s32[4,16]{1,0:T(4,128)} %bitcast.18, s32[4,16]{1,0:T(4,128)} %bitcast.19, s32[4,16]{1,0:T(4,128)} %bitcast.20), dimensions={0} | concatenate | bytes 3072 | tf_op jit(solution)/shard_map/concatenate | solution.py:557
  14.7 1.0 %copy-done.1 = bf16[1,32,32,192]{3,2,1,0:T(8,128)(2,1)S(1)} copy-done((bf16[1,32,32,192]{3,2,1,0:T(8,128)(2,1)S(1)}, bf16[1,32,32,192]{3,2,1,0:T(8,128)(2,1)}, u32[]{:S(2)}) %copy-start.1) | copy-done | bytes 393240
  15.8 1.9 %shard_map.105 = (bf16[512,1536]{1,0:T(8,128)(2,1)S(1)}, bf16[144,1536]{1,0:T(8,128)(2,1)S(1)}, bf16[128,1728]{1,0:T(8,128)(2,1)S(1)}, bf16[1024,192]{1,0:T(8,128)(2,1)S(1)}) custom-call(s32[24,16]{1,0:T(8,128)S(1)} %concatenate.3.tables_in, bf16[1024,192]{1,0:T(8,128)(2,1)S(1)} %bitcast.12), custom_call_target="tpu_custom_call" | custom-call | bytes 3245568 | tf_op jit(solution)/shard_map/pallas_call | solution.py:102
  17.7 1.3 %collective-permute-done.2.refs_2_ = bf16[384,128]{1,0:T(8,128)(2,1)S(1)} collective-permute-done((bf16[384,128]{1,0:T(8,128)(2,1)S(1)}, bf16[384,128]{1,0:T(8,128)(2,1)S(1)}, u32[]{:S(2)}, u32[]{:S(2)}) %collective-permute-start.2) | collective-permute-done | bytes 98336 | tf_op jit(solution)/shard_map/ppermute | solution.py:55
  19.0 2.0 %shard_map.106 = (f32[896,384]{1,0:T(8,128)S(1)}, bf16[1024,384]{1,0:T(8,128)(2,1)S(1)}, bf16[128,384]{1,0:T(8,128)(2,1)S(1)}, bf16[3,1088,192]{2,1,0:T(8,128)(2,1)S(1)}) custom-call(bf16[32,32,192]{2,1,0:T(8,128)(2,1)S(1)} %get-tuple-element.58.field_ref.refs_7_, bf16[1024,192]{1,0:T(8,128)(2,1)S(1)} %get-tuple-element.59.own_ref, ...), custom_call_target="tpu_custom_call" | custom-call | flops 679477248 | bytes 4694016 | tf_op jit(solution)/shard_map/pallas_call | solution.py:102
  21.1 0.5 collective-permute-start.4
  21.7 0.4 collective-permute-start.6
  22.1 2.2 %collective-permute-done.4.refs_3_ = bf16[384,128]{1,0:T(8,128)(2,1)S(1)} collective-permute-done((bf16[384,128]{1,0:T(8,128)(2,1)S(1)}, bf16[384,128]{1,0:T(8,128)(2,1)S(1)}, u32[]{:S(2)}, u32[]{:S(2)}) %collective-permute-start.4) | collective-permute-done | bytes 98336 | tf_op jit(solution)/shard_map/ppermute | solution.py:59
  24.3 0.1 collective-permute-done.5.refs_4_
  24.5 0.1 collective-permute-done.6.refs_5_
  24.6 0.5 shard_map.110
  25.1 0.6 collective-permute-start.16
  25.7 1.3 %shard_map.107.refs_7_ = f32[896,384]{1,0:T(8,128)S(1)} custom-call(bf16[3,1088,192]{2,1,0:T(8,128)(2,1)S(1)} %get-tuple-element.61.cols, bf16[1024,384]{1,0:T(8,128)(2,1)S(1)} %get-tuple-element.72.cot_ref), custom_call_target="tpu_custom_call" | custom-call | flops 679477248 | bytes 3416064 | tf_op jit(solution)/shard_map/pallas_call | solution.py:102
  27.0 1.5 %shard_map.108 = (f32[224,384]{1,0:T(8,128)S(1)}, bf16[224,384]{1,0:T(8,128)(2,1)S(1)}, bf16[224,384]{1,0:T(8,128)(2,1)S(1)}, bf16[224,384]{1,0:T(8,128)(2,1)S(1)}) custom-call(bf16[384,128]{1,0:T(8,128)(2,1)S(1)} %shard_map.104.refs_0_, bf16[384,128]{1,0:T(8,128)(2,1)S(1)} %collective-permute-done.1.refs_1_, ...), custom_call_target="tpu_custom_call" | custom-call | bytes 5971968 | tf_op jit(solution)/shard_map/pallas_call | solution.py:102
  28.6 1.6 %collective-permute-start.9 = (bf16[224,384]{1,0:T(8,128)(2,1)S(1)}, bf16[224,384]{1,0:T(8,128)(2,1)S(1)}, u32[]{:S(2)}, u32[]{:S(2)}) collective-permute-start(bf16[224,384]{1,0:T(8,128)(2,1)S(1)} %get-tuple-element.69), channel_id=1, source_target_pairs={{0,4},{2,6},{4,0},{6,2},{8,12},{10,14},{12,8},{14,10},{16,20},{18,... | collective-permute-start | bytes 516104 | tf_op jit(solution)/shard_map/ppermute | solution.py:59
  30.2 2.0 %collective-permute-start.11 = (bf16[224,384]{1,0:T(8,128)(2,1)S(1)}, bf16[224,384]{1,0:T(8,128)(2,1)S(1)}, u32[]{:S(2)}, u32[]{:S(2)}) collective-permute-start(bf16[224,384]{1,0:T(8,128)(2,1)S(1)} %get-tuple-element.71), channel_id=1, source_target_pairs={{0,12},{2,14},{4,8},{6,10},{8,4},{10,6},{12,0},{14,2},{16,28},{18,... | collective-permute-start | bytes 516104 | tf_op jit(solution)/shard_map/ppermute | solution.py:59
  32.1 2.9 %shard_map.109 = (f32[1024,192]{1,0:T(8,128)S(1)}, bf16[216,128]{1,0:T(8,128)(2,1)S(1)}) custom-call(bf16[1024,384]{1,0:T(8,128)(2,1)S(1)} %get-tuple-element.72.cot_ref, bf16[9,384,384]{2,1,0:T(8,128)(2,1)S(1)} %bitcast.13), custom_call_target="tpu_custom_call" | custom-call | flops 1358954496 | bytes 4282368 | tf_op jit(solution)/shard_map/pallas_call | solution.py:102
  35.0 0.4 collective-permute-done.9.refs_1_
  35.4 1.9 %collective-permute-done.10.refs_2_ = bf16[224,384]{1,0:T(8,128)(2,1)S(1)} collective-permute-done((bf16[224,384]{1,0:T(8,128)(2,1)S(1)}, bf16[224,384]{1,0:T(8,128)(2,1)S(1)}, u32[]{:S(2)}, u32[]{:S(2)}) %collective-permute-start.10) | collective-permute-done | bytes 172064 | tf_op jit(solution)/shard_map/ppermute | solution.py:59
  37.4 2.9 %collective-permute-done.11.refs_3_ = bf16[224,384]{1,0:T(8,128)(2,1)S(1)} collective-permute-done((bf16[224,384]{1,0:T(8,128)(2,1)S(1)}, bf16[224,384]{1,0:T(8,128)(2,1)S(1)}, u32[]{:S(2)}, u32[]{:S(2)}) %collective-permute-start.11) | collective-permute-done | bytes 172064 | tf_op jit(solution)/shard_map/ppermute | solution.py:59
  40.3 0.1 shard_map.111
  40.4 1.4 %collective-permute-start.12 = (bf16[112,384]{1,0:T(8,128)(2,1)S(1)}, bf16[112,384]{1,0:T(8,128)(2,1)S(1)}, u32[]{:S(2)}, u32[]{:S(2)}) collective-permute-start(bf16[112,384]{1,0:T(8,128)(2,1)S(1)} %get-tuple-element.83), channel_id=1, source_target_pairs={{0,16},{2,18},{4,20},{6,22},{8,24},{10,26},{12,28},{14,30},{16,0},... | collective-permute-start | bytes 258056 | tf_op jit(solution)/shard_map/ppermute | solution.py:59
  41.8 1.3 %collective-permute-start.14 = (bf16[216,128]{1,0:T(8,128)(2,1)S(1)}, bf16[216,128]{1,0:T(8,128)(2,1)S(1)}, u32[]{:S(2)}, u32[]{:S(2)}) collective-permute-start(bf16[216,128]{1,0:T(8,128)(2,1)S(1)} %get-tuple-element.88.refs_0_), channel_id=1, source_target_pairs={{0,24},{2,26},{4,28},{6,30},{8,0},{10,2},{12,4},{14,6},{16,8},{18,... | collective-permute-start | bytes 165896 | tf_op jit(solution)/shard_map/ppermute | solution.py:55
  43.1 0.7 %collective-permute-start.15 = (bf16[216,128]{1,0:T(8,128)(2,1)S(1)}, bf16[216,128]{1,0:T(8,128)(2,1)S(1)}, u32[]{:S(2)}, u32[]{:S(2)}) collective-permute-start(bf16[216,128]{1,0:T(8,128)(2,1)S(1)} %get-tuple-element.88.refs_0_), channel_id=1, source_target_pairs={{0,8},{2,10},{4,12},{6,14},{8,16},{10,18},{12,20},{14,22},{16,24},... | collective-permute-start | bytes 165896 | tf_op jit(solution)/shard_map/ppermute | solution.py:55
  43.8 4.4 %collective-permute-done.12.refs_1_ = bf16[112,384]{1,0:T(8,128)(2,1)S(1)} collective-permute-done((bf16[112,384]{1,0:T(8,128)(2,1)S(1)}, bf16[112,384]{1,0:T(8,128)(2,1)S(1)}, u32[]{:S(2)}, u32[]{:S(2)}) %collective-permute-start.12) | collective-permute-done | bytes 86048 | tf_op jit(solution)/shard_map/ppermute | solution.py:59
  48.3 0.8 %collective-permute-done.15.refs_2_ = bf16[216,128]{1,0:T(8,128)(2,1)S(1)} collective-permute-done((bf16[216,128]{1,0:T(8,128)(2,1)S(1)}, bf16[216,128]{1,0:T(8,128)(2,1)S(1)}, u32[]{:S(2)}, u32[]{:S(2)}) %collective-permute-start.15) | collective-permute-done | bytes 55328 | tf_op jit(solution)/shard_map/ppermute | solution.py:55
  49.2 1.6 %collective-permute-start.17 = (bf16[648,128]{1,0:T(8,128)(2,1)S(1)}, bf16[648,128]{1,0:T(8,128)(2,1)S(1)}, u32[]{:S(2)}, u32[]{:S(2)}) collective-permute-start(bf16[648,128]{1,0:T(8,128)(2,1)S(1)} %shard_map.114.refs_0_), channel_id=1, source_target_pairs={{0,4},{2,6},{4,0},{6,2},{8,12},{10,14},{12,8},{14,10},{16,20},{18,... | collective-permute-start | bytes 497672 | tf_op jit(solution)/shard_map/ppermute | solution.py:59
  50.8 3.9 %shard_map.113 = bf16[1024,192]{1,0:T(8,128)(2,1)} custom-call(bf16[32,32,192]{2,1,0:T(8,128)(2,1)S(1)} %get-tuple-element.58.field_ref.refs_7_, bf16[144,192]{1,0:T(8,128)(2,1)S(1)} %get-tuple-element.84.halos_ref, bf16[1752,128]{1,0:T(8,128)(2,1)S(1)} %collective-permute-done.16.other_ref, bf16[9,384,384]{2,1,0:T(8,128)(2,1)S(1)} %bitcast.14), custom_call_target="tpu_custom_call" | custom-call | flops 2717908992 | bytes 3944448 | tf_op jit(solution)/shard_map/pallas_call | solution.py:102
  54.7 1.6 %collective-permute-start.18 = (bf16[224,384]{1,0:T(8,128)(2,1)S(1)}, bf16[224,384]{1,0:T(8,128)(2,1)S(1)}, u32[]{:S(2)}, u32[]{:S(2)}) collective-permute-start(bf16[224,384]{1,0:T(8,128)(2,1)S(1)} %shard_map.115.refs_0_), channel_id=1, source_target_pairs={{0,4},{2,6},{4,0},{6,2},{8,12},{10,14},{12,8},{14,10},{16,20},{18,... | collective-permute-start | bytes 516104 | tf_op jit(solution)/shard_map/ppermute | solution.py:59
  56.3 2.8 %collective-permute-start.19 = (bf16[224,384]{1,0:T(8,128)(2,1)S(1)}, bf16[224,384]{1,0:T(8,128)(2,1)S(1)}, u32[]{:S(2)}, u32[]{:S(2)}) collective-permute-start(bf16[224,384]{1,0:T(8,128)(2,1)S(1)} %shard_map.115.refs_0_), channel_id=1, source_target_pairs={{0,8},{2,10},{4,12},{6,14},{8,0},{10,2},{12,4},{14,6},{16,24},{18,... | collective-permute-start | bytes 516104 | tf_op jit(solution)/shard_map/ppermute | solution.py:59
  59.0 0.5 collective-permute-start.22
  59.5 0.9 %collective-permute-done.21.refs_2_ = bf16[648,128]{1,0:T(8,128)(2,1)S(1)} collective-permute-done((bf16[648,128]{1,0:T(8,128)(2,1)S(1)}, bf16[648,128]{1,0:T(8,128)(2,1)S(1)}, u32[]{:S(2)}, u32[]{:S(2)}) %collective-permute-start.21) | collective-permute-done | bytes 165920 | tf_op jit(solution)/shard_map/ppermute | solution.py:59
  60.4 0.1 collective-permute-start.23
  60.6 0.1 collective-permute-done.22.refs_3_
  60.7 1.3 %shard_map.116 = bf16[1024,192]{1,0:T(8,128)(2,1)} custom-call(bf16[128,1728]{1,0:T(8,128)(2,1)S(1)} %get-tuple-element.94.place_ref, f32[1024,192]{1,0:T(8,128)S(1)} %get-tuple-element.95.inner_ref, bf16[648,128]{1,0:T(8,128)(2,1)S(1)} %shard_map.114.refs_0_, bf16[648,128]{1,0:T(8,128)(2,1)S(1)} %collective-permute-done.17.refs_1_, ...), custom_call_target="tpu_custom_call" | custom-call | bytes 2285568 | tf_op jit(solution)/shard_map/pallas_call | solution.py:102
  62.0 1.8 %collective-permute-done.19.refs_2_ = bf16[224,384]{1,0:T(8,128)(2,1)S(1)} collective-permute-done((bf16[224,384]{1,0:T(8,128)(2,1)S(1)}, bf16[224,384]{1,0:T(8,128)(2,1)S(1)}, u32[]{:S(2)}, u32[]{:S(2)}) %collective-permute-start.19) | collective-permute-done | bytes 172064 | tf_op jit(solution)/shard_map/ppermute | solution.py:59
  63.8 2.3 %collective-permute-done.20.refs_1_ = bf16[224,384]{1,0:T(8,128)(2,1)S(1)} collective-permute-done((bf16[224,384]{1,0:T(8,128)(2,1)S(1)}, bf16[224,384]{1,0:T(8,128)(2,1)S(1)}, u32[]{:S(2)}, u32[]{:S(2)}) %collective-permute-start.20) | collective-permute-done | bytes 172064 | tf_op jit(solution)/shard_map/ppermute | solution.py:59
  66.0 0.5 collective-permute-start.25
  66.6 0.9 %collective-permute-done.24.refs_4_ = bf16[224,384]{1,0:T(8,128)(2,1)S(1)} collective-permute-done((bf16[224,384]{1,0:T(8,128)(2,1)S(1)}, bf16[224,384]{1,0:T(8,128)(2,1)S(1)}, u32[]{:S(2)}, u32[]{:S(2)}) %collective-permute-start.24) | collective-permute-done | bytes 172064 | tf_op jit(solution)/shard_map/ppermute | solution.py:59
  67.4 0.2 collective-permute-done.25.refs_5_
  67.7 1.5 %shard_map.117.refs_0_ = f32[1728,384]{1,0:T(8,128)} custom-call(bf16[224,384]{1,0:T(8,128)(2,1)S(1)} %shard_map.115.refs_0_, bf16[224,384]{1,0:T(8,128)(2,1)S(1)} %collective-permute-done.18.refs_1_, bf16[224,384]{1,0:T(8,128)(2,1)S(1)} %collective-permute-done.19.refs_2_, bf16[224,384]{1,0:T(8,128)(2,1)S(1)} %collective-permute-done.23.refs_3_, ...), custom_call_target="tpu_custom_call" | custom-call | tf_op jit(solution)/shard_map/pallas_call | solution.py:412
  69.2 0.9 %shard_map.118 = f32[1728,384]{1,0:T(8,128)} custom-call(f32[1728,384]{1,0:T(8,128)} %shard_map.117.refs_0_, bf16[224,384]{1,0:T(8,128)(2,1)S(1)} %collective-permute-done.20.refs_1_, bf16[224,384]{1,0:T(8,128)(2,1)S(1)} %collective-permute-done.26.refs_2_), custom_call_target="tpu_custom_call", output_to_operand_aliasing={{}: (0, {})} | custom-call | tf_op jit(solution)/shard_map/pallas_call | solution.py:412
  (29 shorter events, 0.3 us)
Async XLA Ops:
  0.6 18.4 %collective-permute-start.3 = (bf16[1024,192]{1,0:T(8,128)(2,1)}, bf16[1024,192]{1,0:T(8,128)(2,1)S(1)}, u32[]{:S(2)}, u32[]{:S(2)}) collective-permute-start(bf16[1024,192]{1,0:T(8,128)(2,1)} %bitcast.11), channel_id=1, source_target_pairs={{0,1},{1,0},{2,3},{3,2},{4,5},{5,4},{6,7},{7,6},{8,9},{9,8},{10,11... | collective-permute-start | bytes 1179656 | tf_op jit(solution)/shard_map/ppermute | solution.py:547
  3.6 1.0 %copy-start = (bf16[1,32,32,192]{3,2,1,0:T(8,128)(2,1)S(1)}, bf16[1,32,32,192]{3,2,1,0:T(8,128)(2,1)}, u32[]{:S(2)}) copy-start(bf16[1,32,32,192]{3,2,1,0:T(8,128)(2,1)} %param.8) | copy-start | bytes 1179652
  4.8 4.2 %collective-permute-start = (bf16[192,128]{1,0:T(8,128)(2,1)S(1)}, bf16[192,128]{1,0:T(8,128)(2,1)S(1)}, u32[]{:S(2)}, u32[]{:S(2)}) collective-permute-start(bf16[192,128]{1,0:T(8,128)(2,1)S(1)} %get-tuple-element.52.refs_0_), channel_id=1, source_target_pairs={{0,4},{2,6},{4,0},{6,2},{8,12},{10,14},{12,8},{14,10},{16,20},{18,... | collective-permute-start | bytes 147464 | tf_op jit(solution)/shard_map/ppermute | solution.py:59
  9.0 8.8 %collective-permute-start.1 = (bf16[384,128]{1,0:T(8,128)(2,1)S(1)}, bf16[384,128]{1,0:T(8,128)(2,1)S(1)}, u32[]{:S(2)}, u32[]{:S(2)}) collective-permute-start(bf16[384,128]{1,0:T(8,128)(2,1)S(1)} %shard_map.104.refs_0_), channel_id=1, source_target_pairs={{0,24},{2,26},{4,28},{6,30},{8,0},{10,2},{12,4},{14,6},{16,8},{18,... | collective-permute-start | bytes 294920 | tf_op jit(solution)/shard_map/ppermute | solution.py:55
  12.6 6.4 %collective-permute-start.2 = (bf16[384,128]{1,0:T(8,128)(2,1)S(1)}, bf16[384,128]{1,0:T(8,128)(2,1)S(1)}, u32[]{:S(2)}, u32[]{:S(2)}) collective-permute-start(bf16[384,128]{1,0:T(8,128)(2,1)S(1)} %shard_map.104.refs_0_), channel_id=1, source_target_pairs={{0,8},{2,10},{4,12},{6,14},{8,16},{10,18},{12,20},{14,22},{16,24},... | collective-permute-start | bytes 294920 | tf_op jit(solution)/shard_map/ppermute | solution.py:55
  14.7 1.0 %copy-start.1 = (bf16[1,32,32,192]{3,2,1,0:T(8,128)(2,1)S(1)}, bf16[1,32,32,192]{3,2,1,0:T(8,128)(2,1)}, u32[]{:S(2)}) copy-start(bf16[1,32,32,192]{3,2,1,0:T(8,128)(2,1)} %param.10) | copy-start | bytes 1179652
  21.0 6.0 %collective-permute-start.7 = (f32[896,384]{1,0:T(8,128)S(1)}, f32[896,384]{1,0:T(8,128)S(1)}, u32[]{:S(2)}, u32[]{:S(2)}) collective-permute-start(f32[896,384]{1,0:T(8,128)S(1)} %get-tuple-element.63), channel_id=1, source_target_pairs={{0,2},{2,0},{4,6},{6,4},{8,10},{10,8},{12,14},{14,12},{16,18},{18,... | collective-permute-start | bytes 4128776 | tf_op jit(solution)/shard_map/ppermute | solution.py:59
  21.1 3.3 %collective-permute-start.4 = (bf16[384,128]{1,0:T(8,128)(2,1)S(1)}, bf16[384,128]{1,0:T(8,128)(2,1)S(1)}, u32[]{:S(2)}, u32[]{:S(2)}) collective-permute-start(bf16[384,128]{1,0:T(8,128)(2,1)S(1)} %shard_map.104.refs_0_), channel_id=1, source_target_pairs={{0,2},{2,0},{4,6},{6,4},{8,10},{10,8},{12,14},{14,12},{16,18},{18,... | collective-permute-start | bytes 294920 | tf_op jit(solution)/shard_map/ppermute | solution.py:59
  21.6 2.9 %collective-permute-start.5 = (bf16[384,128]{1,0:T(8,128)(2,1)S(1)}, bf16[384,128]{1,0:T(8,128)(2,1)S(1)}, u32[]{:S(2)}, u32[]{:S(2)}) collective-permute-start(bf16[384,128]{1,0:T(8,128)(2,1)S(1)} %collective-permute-done.1.refs_1_), channel_id=1, source_target_pairs={{0,2},{2,0},{4,6},{6,4},{8,10},{10,8},{12,14},{14,12},{16,18},{18,... | collective-permute-start | bytes 294920 | tf_op jit(solution)/shard_map/ppermute | solution.py:59
  21.7 3.0 %collective-permute-start.6 = (bf16[384,128]{1,0:T(8,128)(2,1)S(1)}, bf16[384,128]{1,0:T(8,128)(2,1)S(1)}, u32[]{:S(2)}, u32[]{:S(2)}) collective-permute-start(bf16[384,128]{1,0:T(8,128)(2,1)S(1)} %collective-permute-done.2.refs_2_), channel_id=1, source_target_pairs={{0,2},{2,0},{4,6},{6,4},{8,10},{10,8},{12,14},{14,12},{16,18},{18,... | collective-permute-start | bytes 294920 | tf_op jit(solution)/shard_map/ppermute | solution.py:59
  25.1 23.2 %collective-permute-start.16 = (bf16[1752,128]{1,0:T(8,128)(2,1)S(1)}, bf16[1752,128]{1,0:T(8,128)(2,1)S(1)}, u32[]{:S(2)}, u32[]{:S(2)}) collective-permute-start(bf16[1752,128]{1,0:T(8,128)(2,1)S(1)} %get-tuple-element.86), channel_id=1, source_target_pairs={{0,1},{1,0},{2,3},{3,2},{4,5},{5,4},{6,7},{7,6},{8,9},{9,8},{10,11... | collective-permute-start | bytes 1345544 | tf_op jit(solution)/shard_map/ppermute | solution.py:608
  25.7 1.4 %collective-permute-start.8 = (bf16[128,384]{1,0:T(8,128)(2,1)S(1)}, bf16[128,384]{1,0:T(8,128)(2,1)S(1)}, u32[]{:S(2)}, u32[]{:S(2)}) collective-permute-start(bf16[128,384]{1,0:T(8,128)(2,1)S(1)} %get-tuple-element.64.refs_9_), channel_id=1, source_target_pairs={{0,2},{2,0},{4,6},{6,4},{8,10},{10,8},{12,14},{14,12},{16,18},{18,... | collective-permute-start | bytes 294920 | tf_op jit(solution)/shard_map/ppermute | solution.py:59
  27.0 5.1 %copy-start.2 = (bf16[3,3,384,384]{3,2,1,0:T(8,128)(2,1)S(1)}, bf16[3,3,384,384]{3,2,1,0:T(8,128)(2,1)}, u32[]{:S(2)}) copy-start(bf16[3,3,384,384]{3,2,1,0:T(8,128)(2,1)} %param.9) | copy-start | bytes 7962628
  28.6 6.9 %collective-permute-start.9 = (bf16[224,384]{1,0:T(8,128)(2,1)S(1)}, bf16[224,384]{1,0:T(8,128)(2,1)S(1)}, u32[]{:S(2)}, u32[]{:S(2)}) collective-permute-start(bf16[224,384]{1,0:T(8,128)(2,1)S(1)} %get-tuple-element.69), channel_id=1, source_target_pairs={{0,4},{2,6},{4,0},{6,2},{8,12},{10,14},{12,8},{14,10},{16,20},{18,... | collective-permute-start | bytes 516104 | tf_op jit(solution)/shard_map/ppermute | solution.py:59
  30.2 7.2 %collective-permute-start.10 = (bf16[224,384]{1,0:T(8,128)(2,1)S(1)}, bf16[224,384]{1,0:T(8,128)(2,1)S(1)}, u32[]{:S(2)}, u32[]{:S(2)}) collective-permute-start(bf16[224,384]{1,0:T(8,128)(2,1)S(1)} %get-tuple-element.70), channel_id=1, source_target_pairs={{0,8},{2,10},{4,12},{6,14},{8,0},{10,2},{12,4},{14,6},{16,24},{18,... | collective-permute-start | bytes 516104 | tf_op jit(solution)/shard_map/ppermute | solution.py:59
  30.2 10.1 %collective-permute-start.11 = (bf16[224,384]{1,0:T(8,128)(2,1)S(1)}, bf16[224,384]{1,0:T(8,128)(2,1)S(1)}, u32[]{:S(2)}, u32[]{:S(2)}) collective-permute-start(bf16[224,384]{1,0:T(8,128)(2,1)S(1)} %get-tuple-element.71), channel_id=1, source_target_pairs={{0,12},{2,14},{4,8},{6,10},{8,4},{10,6},{12,0},{14,2},{16,28},{18,... | collective-permute-start | bytes 516104 | tf_op jit(solution)/shard_map/ppermute | solution.py:59
  40.4 7.8 %collective-permute-start.12 = (bf16[112,384]{1,0:T(8,128)(2,1)S(1)}, bf16[112,384]{1,0:T(8,128)(2,1)S(1)}, u32[]{:S(2)}, u32[]{:S(2)}) collective-permute-start(bf16[112,384]{1,0:T(8,128)(2,1)S(1)} %get-tuple-element.83), channel_id=1, source_target_pairs={{0,16},{2,18},{4,20},{6,22},{8,24},{10,26},{12,28},{14,30},{16,0},... | collective-permute-start | bytes 258056 | tf_op jit(solution)/shard_map/ppermute | solution.py:59
  41.8 6.5 %collective-permute-start.14 = (bf16[216,128]{1,0:T(8,128)(2,1)S(1)}, bf16[216,128]{1,0:T(8,128)(2,1)S(1)}, u32[]{:S(2)}, u32[]{:S(2)}) collective-permute-start(bf16[216,128]{1,0:T(8,128)(2,1)S(1)} %get-tuple-element.88.refs_0_), channel_id=1, source_target_pairs={{0,24},{2,26},{4,28},{6,30},{8,0},{10,2},{12,4},{14,6},{16,8},{18,... | collective-permute-start | bytes 165896 | tf_op jit(solution)/shard_map/ppermute | solution.py:55
  43.1 6.1 %collective-permute-start.15 = (bf16[216,128]{1,0:T(8,128)(2,1)S(1)}, bf16[216,128]{1,0:T(8,128)(2,1)S(1)}, u32[]{:S(2)}, u32[]{:S(2)}) collective-permute-start(bf16[216,128]{1,0:T(8,128)(2,1)S(1)} %get-tuple-element.88.refs_0_), channel_id=1, source_target_pairs={{0,8},{2,10},{4,12},{6,14},{8,16},{10,18},{12,20},{14,22},{16,24},... | collective-permute-start | bytes 165896 | tf_op jit(solution)/shard_map/ppermute | solution.py:55
  48.2 6.5 %collective-permute-start.13 = (bf16[112,384]{1,0:T(8,128)(2,1)S(1)}, bf16[112,384]{1,0:T(8,128)(2,1)S(1)}, u32[]{:S(2)}, u32[]{:S(2)}) collective-permute-start(bf16[112,384]{1,0:T(8,128)(2,1)S(1)} %shard_map.112.refs_0_), channel_id=1, source_target_pairs={{0,16},{2,18},{4,20},{6,22},{8,24},{10,26},{12,28},{14,30},{16,0},... | collective-permute-start | bytes 258056 | tf_op jit(solution)/shard_map/ppermute | solution.py:59
  49.2 5.5 %collective-permute-start.17 = (bf16[648,128]{1,0:T(8,128)(2,1)S(1)}, bf16[648,128]{1,0:T(8,128)(2,1)S(1)}, u32[]{:S(2)}, u32[]{:S(2)}) collective-permute-start(bf16[648,128]{1,0:T(8,128)(2,1)S(1)} %shard_map.114.refs_0_), channel_id=1, source_target_pairs={{0,4},{2,6},{4,0},{6,2},{8,12},{10,14},{12,8},{14,10},{16,20},{18,... | collective-permute-start | bytes 497672 | tf_op jit(solution)/shard_map/ppermute | solution.py:59
  54.7 7.3 %collective-permute-start.18 = (bf16[224,384]{1,0:T(8,128)(2,1)S(1)}, bf16[224,384]{1,0:T(8,128)(2,1)S(1)}, u32[]{:S(2)}, u32[]{:S(2)}) collective-permute-start(bf16[224,384]{1,0:T(8,128)(2,1)S(1)} %shard_map.115.refs_0_), channel_id=1, source_target_pairs={{0,4},{2,6},{4,0},{6,2},{8,12},{10,14},{12,8},{14,10},{16,20},{18,... | collective-permute-start | bytes 516104 | tf_op jit(solution)/shard_map/ppermute | solution.py:59
  56.3 7.5 %collective-permute-start.19 = (bf16[224,384]{1,0:T(8,128)(2,1)S(1)}, bf16[224,384]{1,0:T(8,128)(2,1)S(1)}, u32[]{:S(2)}, u32[]{:S(2)}) collective-permute-start(bf16[224,384]{1,0:T(8,128)(2,1)S(1)} %shard_map.115.refs_0_), channel_id=1, source_target_pairs={{0,8},{2,10},{4,12},{6,14},{8,0},{10,2},{12,4},{14,6},{16,24},{18,... | collective-permute-start | bytes 516104 | tf_op jit(solution)/shard_map/ppermute | solution.py:59
  59.0 7.0 %collective-permute-start.20 = (bf16[224,384]{1,0:T(8,128)(2,1)S(1)}, bf16[224,384]{1,0:T(8,128)(2,1)S(1)}, u32[]{:S(2)}, u32[]{:S(2)}) collective-permute-start(bf16[224,384]{1,0:T(8,128)(2,1)S(1)} %shard_map.115.refs_0_), channel_id=1, source_target_pairs={{0,12},{2,14},{4,8},{6,10},{8,4},{10,6},{12,0},{14,2},{16,28},{18,... | collective-permute-start | bytes 516104 | tf_op jit(solution)/shard_map/ppermute | solution.py:59
  59.0 1.4 %collective-permute-start.21 = (bf16[648,128]{1,0:T(8,128)(2,1)S(1)}, bf16[648,128]{1,0:T(8,128)(2,1)S(1)}, u32[]{:S(2)}, u32[]{:S(2)}) collective-permute-start(bf16[648,128]{1,0:T(8,128)(2,1)S(1)} %shard_map.114.refs_0_), channel_id=1, source_target_pairs={{0,2},{2,0},{4,6},{6,4},{8,10},{10,8},{12,14},{14,12},{16,18},{18,... | collective-permute-start | bytes 497672 | tf_op jit(solution)/shard_map/ppermute | solution.py:59
  59.0 1.6 %collective-permute-start.22 = (bf16[648,128]{1,0:T(8,128)(2,1)S(1)}, bf16[648,128]{1,0:T(8,128)(2,1)S(1)}, u32[]{:S(2)}, u32[]{:S(2)}) collective-permute-start(bf16[648,128]{1,0:T(8,128)(2,1)S(1)} %collective-permute-done.17.refs_1_), channel_id=1, source_target_pairs={{0,2},{2,0},{4,6},{6,4},{8,10},{10,8},{12,14},{14,12},{16,18},{18,... | collective-permute-start | bytes 497672 | tf_op jit(solution)/shard_map/ppermute | solution.py:59
  60.4 6.1 %collective-permute-start.23 = (bf16[224,384]{1,0:T(8,128)(2,1)S(1)}, bf16[224,384]{1,0:T(8,128)(2,1)S(1)}, u32[]{:S(2)}, u32[]{:S(2)}) collective-permute-start(bf16[224,384]{1,0:T(8,128)(2,1)S(1)} %shard_map.115.refs_0_), channel_id=1, source_target_pairs={{0,2},{2,0},{4,6},{6,4},{8,10},{10,8},{12,14},{14,12},{16,18},{18,... | collective-permute-start | bytes 516104 | tf_op jit(solution)/shard_map/ppermute | solution.py:59
  66.0 1.4 %collective-permute-start.24 = (bf16[224,384]{1,0:T(8,128)(2,1)S(1)}, bf16[224,384]{1,0:T(8,128)(2,1)S(1)}, u32[]{:S(2)}, u32[]{:S(2)}) collective-permute-start(bf16[224,384]{1,0:T(8,128)(2,1)S(1)} %collective-permute-done.18.refs_1_), channel_id=1, source_target_pairs={{0,2},{2,0},{4,6},{6,4},{8,10},{10,8},{12,14},{14,12},{16,18},{18,... | collective-permute-start | bytes 516104 | tf_op jit(solution)/shard_map/ppermute | solution.py:59
  66.0 1.6 %collective-permute-start.25 = (bf16[224,384]{1,0:T(8,128)(2,1)S(1)}, bf16[224,384]{1,0:T(8,128)(2,1)S(1)}, u32[]{:S(2)}, u32[]{:S(2)}) collective-permute-start(bf16[224,384]{1,0:T(8,128)(2,1)S(1)} %collective-permute-done.19.refs_2_), channel_id=1, source_target_pairs={{0,2},{2,0},{4,6},{6,4},{8,10},{10,8},{12,14},{14,12},{16,18},{18,... | collective-permute-start | bytes 516104 | tf_op jit(solution)/shard_map/ppermute | solution.py:59
  66.5 2.7 %collective-permute-start.26 = (bf16[224,384]{1,0:T(8,128)(2,1)S(1)}, bf16[224,384]{1,0:T(8,128)(2,1)S(1)}, u32[]{:S(2)}, u32[]{:S(2)}) collective-permute-start(bf16[224,384]{1,0:T(8,128)(2,1)S(1)} %collective-permute-done.20.refs_1_), channel_id=1, source_target_pairs={{0,2},{2,0},{4,6},{6,4},{8,10},{10,8},{12,14},{14,12},{16,18},{18,... | collective-permute-start | bytes 516104 | tf_op jit(solution)/shard_map/ppermute | solution.py:59

commit v7 on v6

--- a/solution.py
+++ b/solution.py
@@ -11,6 +11,7 @@
 
 SPAN = 4
 EXTRA = 16
+CUTS = 2
 
 
 def turn_tables():
@@ -48,7 +49,8 @@
                 if base_corners[corner_index] == corner_cell:
                     corner_table[border, quarter] = corner_index
             turned = turn_once(turned)
-    return np.concatenate([edge_table, corner_table], axis=0)
+    tables = np.concatenate([edge_table, corner_table], axis=0)
+    return [sum(int(slot) << (3 * quarter) for quarter, slot in enumerate(row)) for row in tables]
 
 
 def by_offset(value, offset, count):
@@ -82,6 +84,10 @@
         size = 1 << len(bits)
         place = place * size + (mask // bits[0]) % size
     return place
+
+
+def slot_in(row, quarter):
+    return (row >> (3 * quarter)) & 7
 
 
 def corner_spot(slot, side):
@@ -173,7 +179,8 @@
     copy.start()
     cot_ref[...] = cot_in[...]
     copy.wait()
-    et, eu, ct, cu = [tables.at[8 + 4 * i : 12 + 4 * i] for i in range(4)]
+    et, eu, ct, cu = [tables.at[4 * i : 4 * i + 4] for i in range(4)]
+    digits = turn_tables()
     count = lax.axis_size("tile")
     own = lax.axis_index("tile")
     core = lax.rem(own, 2)
@@ -183,19 +190,19 @@
         slab = lax.rem(source // SPAN - own // SPAN + groups, groups)
         cross = source ^ own
         turn = lax.rem(cross // 2, 2)
-        at = jnp.where(slab == 0, 0, jnp.where(slab == 1, 2, 4)) + turn
+        at = jnp.where(slab == 0, turn, jnp.where(slab == 1, 2, 3) + 2 * turn)
         return (6 * lax.rem(cross, 2) + at) * (4 * side)
 
     step = lax.broadcasted_iota(jnp.int32, (side, 1), 0)
     nothing = jnp.full((side, 1), -1, jnp.int32)
 
     def halo(tile, e):
-        slot = tables[e, eu[e, tile]]
+        slot = slot_in(digits[e], eu[e, tile])
         start = base(et[e, tile]) + lax.rem(slot, 4) * side
         return lambda at: jnp.where(slot >= 4, start + side - 1 - at, start + at)
 
     def corner(tile, c):
-        return base(ct[c, tile]) + corner_spot(tables[4 + c, cu[c, tile]], side)
+        return base(ct[c, tile]) + corner_spot(slot_in(digits[4 + c], cu[c, tile]), side)
 
     def onehot(wanted, width):
         lane = lax.broadcasted_iota(jnp.int32, (wanted.shape[0], width), 1)
@@ -232,12 +239,12 @@
             source = lax.rem((own ^ mask) + offset + count, count)
             target = jnp.full((1, block), -1, jnp.int32)
             for e in range(4):
-                slot = tables[e, eu[e, source]]
+                slot = slot_in(digits[e], eu[e, source])
                 along = lane - e * side
                 along = jnp.where(slot >= 4, side - 1 - along, along)
                 hit = (lane >= e * side) & (lane < (e + 1) * side) & (et[e, source] == own)
                 target = jnp.where(hit, lax.rem(slot, 4) * side + along, target)
-                spot = corner_spot(tables[4 + e, cu[e, source]], side)
+                spot = corner_spot(slot_in(digits[4 + e], cu[e, source]), side)
                 hit = (lane == 4 * side + e) & (ct[e, source] == own)
                 target = jnp.where(hit, spot, target)
             places.append(jnp.where(row == target, 1.0, 0.0))
@@ -267,9 +274,8 @@
     out_ref[used:, :] = jnp.zeros((half - used, cot.shape[1]), jnp.float32)
 
 
-def send_kernel(
-    side, part, half, scale, field_ref, own_ref, other_ref, send_ref, cot_ref, rim_ref, cols, middle
-):
+def send_kernel(side, part, half, scale, field_ref, own_ref, other_ref, *refs):
+    send_refs, (cot_ref, rim_ref, cols, middle, send) = refs[:CUTS], refs[CUTS:]
     rows = side * side
     chans = cot_ref.shape[1]
     first = lax.axis_index("ch") == 0
@@ -296,7 +302,9 @@
         axis=0,
     )
     which = 1 - lax.rem(lax.axis_index("tile"), 2)
-    half_taps(side, part, half, scale, which, cols, cot, send_ref, middle)
+    half_taps(side, part, half, scale, which, cols, cot, send, middle)
+    for i, ref in enumerate(send_refs):
+        ref[...] = send[i * (half // CUTS) : (i + 1) * (half // CUTS), :]
 
 
 def mine_kernel(side, part, half, scale, cols, cot_ref, mine_ref, middle):
@@ -306,20 +314,25 @@
 
 def unpack_near(near_refs, near, side, part):
     size = packed_shape(4 * side, part)[0]
-    for i, ref in enumerate(near_refs):
-        for k in range(2):
-            unpack(ref, near, k * size, (2 * i + k) * 4 * side, 4 * side, part)
+    row = 0
+    for ref in near_refs:
+        for k in range(ref.shape[0] // size):
+            unpack(ref, near, k * size, row, 4 * side, part)
+            row += 4 * side
 
 
 def border_kernel(side, part, chunk, scale, n_near, *refs):
     near_refs = refs[:n_near]
-    onehot_ref, mine_ref, got_ref, rim_ref, mate_ref = refs[n_near : n_near + 5]
-    outs, near, total = refs[n_near + 5 : -2], refs[-2], refs[-1]
+    onehot_ref, mine_ref, rim_ref, mate_ref = refs[n_near : n_near + 4]
+    got_refs = refs[n_near + 4 : n_near + 4 + CUTS]
+    outs, near, total = refs[n_near + 4 + CUTS : -2], refs[-2], refs[-1]
     count = lax.axis_size("tile")
     own = lax.axis_index("tile")
     core = lax.rem(own, 2)
     unpack_near(near_refs, near, side, part)
-    total[...] = mine_ref[...] + got_ref[...]
+    for i, ref in enumerate(got_refs):
+        here = slice(i * ref.shape[0], (i + 1) * ref.shape[0])
+        total[here, :] = mine_ref[here, :] + ref[...]
     left = jnp.dot(onehot_ref[...], near[...], preferred_element_type=jnp.float32).astype(jnp.bfloat16)
 
     def rim(ref, at):
@@ -550,11 +563,9 @@
         [vmem(packed_shape(4 * side, part), half_bytes), vmem(field.shape, half_bytes)],
         [field],
     )
-    pair = packed_shape(8 * side, part)
-    (near,) = call(join_kernel, [vmem(pair, half_bytes)], [sides, by_mask(sides, 2, count)])
-    near = [near, by_offset(near, -SPAN, count), by_offset(near, SPAN, count)]
-    tables = jnp.pad(jnp.asarray(turn_tables()), ((0, 0), (0, count - 4)))
-    tables = jnp.concatenate([tables, edge_tiles.T, edge_turns.T, corner_tiles.T, corner_turns.T], axis=0)
+    ahead, behind = by_offset(sides, -SPAN, count), by_offset(sides, SPAN, count)
+    across = by_mask(sides, 2, count)
+    tables = jnp.concatenate([edge_tiles.T, edge_turns.T, corner_tiles.T, corner_turns.T], axis=0)
     border_pick, halo_pick, place, cot_own = call(
         functools.partial(onehot_kernel, side),
         [
@@ -566,18 +577,22 @@
         [tables, cot_own],
         scratch=[pltpu.SMEM(tables.shape, jnp.int32), pltpu.SemaphoreType.DMA],
     )
+    pair = packed_shape(8 * side, part)
+    (beyond,) = call(join_kernel, [vmem(pair, half_bytes)], [ahead, behind])
+    near = [sides, across, ahead, behind, by_mask(beyond, 2, count)]
     near, cot_other, border_pick = lax.optimization_barrier((near, cot_other, border_pick))
-    near = near + [by_mask(v, 1, count) for v in near]
-    send, cot_full, rim, cols = call(
+    (near,) = call(join_kernel, [vmem(packed_shape(24 * side, part), half_bytes)], near)
+    mates = by_mask(near, 1, count)
+    *send, cot_full, rim, cols = call(
         functools.partial(send_kernel, side, part, half, scale),
         [
-            vmem((half, chans), jnp.float32),
+            *[vmem((half // CUTS, chans), jnp.float32)] * CUTS,
             vmem((rows, chans), half_bytes),
             vmem((4 * side, chans), half_bytes),
             vmem((3, flat, part), half_bytes),
         ],
         [field, cot_own, cot_other],
-        scratch=[pltpu.VMEM((part, chans), jnp.float32)],
+        scratch=[pltpu.VMEM((part, chans), jnp.float32), pltpu.VMEM((half, chans), jnp.float32)],
         flops=flops // 2,
     )
     (mine,) = call(
@@ -588,13 +603,16 @@
         flops=flops // 2,
     )
 
+    mates, mine, rim_mate = lax.optimization_barrier((mates, mine, by_mask(rim, 1, count)))
+    near = [near, mates]
+
     stages = mask_stages(count)
     masks = group_masks(stages[1])
     size = half // len(masks)
     held, *send = call(
         functools.partial(border_kernel, side, part, chunk, scale, len(near)),
         [vmem((size, chans), jnp.float32)] + [vmem((size, chans), half_bytes)] * (len(masks) - 1),
-        [*near, border_pick, mine, by_mask(send, 1, count), rim, by_mask(rim, 1, count)],
+        [*near, border_pick, mine, rim, rim_mate, *[by_mask(v, 1, count) for v in send]],
         scratch=[pltpu.VMEM((48 * side, part), half_bytes), pltpu.VMEM((half, chans), jnp.float32)],
     )
     send, cot_full = lax.optimization_barrier((send, cot_full))

time: 70.6 us -> 69 us (0.977)
  waiting for transfers between devices: 23.1 us -> 12.7 us
  starting transfers between devices: 24.1 us -> 33.9 us
  local copies, waits for them, and re-layouts: 4.2 us -> 2.08 us
  other arithmetic: 0 us -> 0.74 us
    ppermute x21, waiting for transfers between devices: 20.9 us -> 10.9 us  [by_mask(): return lax.ppermute(value, 'tile', [(i, i ^ mask) for i in range(count)])]
    ppermute x21, starting transfers between devices: 14.8 us -> 22 us  [by_mask(): return lax.ppermute(value, 'tile', [(i, i ^ mask) for i in range(count)])]
    concatenate x1 -> x0, local copies, waits for them, and re-layouts: 2.11 us -> none  [body(): jnp.concatenate([tables, edge_tiles.T, edge_turns.T, corner_tiles.T, corn...]
    ppermute x4, starting transfers between devices: 5.68 us -> 7.7 us  [by_offset(): lax.ppermute(value, 'tile', [(i, (i + offset) % count) for i in range(cou...]
    concatenate x0 -> x1, other arithmetic: none -> 0.74 us  [body(): jnp.concatenate([edge_tiles.T, edge_turns.T, corner_tiles.T, corner_turns...]
    pallas_call x14 -> x15, Pallas kernels: 15.6 us -> 16 us  [call(): pl.pallas_call(kernel, out_shape=tuple(outs), in_specs=in_specs, out_spec...]
  transfers between devices with their start and end apart: 27 -> 27, of which waited for: 16 -> 11; matrix products, arithmetic and copies ran while one was open for 3% -> 1% of each run, Pallas kernels for 22% -> 22%
where the time goes in v7:
time: 69 us; the launch traced here: 68.8 us
  starting transfers between devices  33.9 us (49%)
  Pallas kernels  18.4 us (27%)
  waiting for transfers between devices  12.7 us (18%)
  local copies, waits for them, and re-layouts  2.08 us (3%)
  between operations  0.93 us (1%)
  other arithmetic  0.74 us (1%)
    ppermute x21, starting transfers between devices, by_mask(): return lax.ppermute(value, 'tile', [(i, i ^ mask) for i in range(count)])  22 us
    pallas_call x15, Pallas kernels, call(): pl.pallas_call(kernel, out_shape=tuple(outs), in_specs=in_specs, out_spec...  16 us
    ppermute x21, waiting for transfers between devices, by_mask(): return lax.ppermute(value, 'tile', [(i, i ^ mask) for i in range(count)])  10.9 us
    ppermute x4, starting transfers between devices, by_offset(): lax.ppermute(value, 'tile', [(i, (i + offset) % count) for i in range(cou...  7.7 us
    ppermute x1, starting transfers between devices, body(): cot_other = lax.ppermute(cot_own, 'ch', others)  3 us
    pallas_call x2, Pallas kernels, unfold(): pl.pallas_call(functools.partial(unfold_kernel, whole.shape[0] // 2, chun...  2.41 us
    unnamed x6, local copies, waits for them, and re-layouts  2.08 us
    ppermute x4, waiting for transfers between devices, by_offset(): lax.ppermute(value, 'tile', [(i, (i + offset) % count) for i in range(cou...  1.8 us
  transfers between devices with their start and end apart: 27, of which 11 were waited for; matrix products, arithmetic and copies ran while one was open for 1% of the time, Pallas kernels for 22%

profile of v7, /device:TPU:0, one launch (start us, length us, event | category | flops | bytes accessed | tf_op | source)
XLA Modules:
  0.0 68.8 jit_solution(3015405417344234114)
XLA Ops:
  0.6 3.0 %collective-permute-start.4 = (bf16[1024,192]{1,0:T(8,128)(2,1)}, bf16[1024,192]{1,0:T(8,128)(2,1)S(1)}, u32[]{:S(2)}, u32[]{:S(2)}) collective-permute-start(bf16[1024,192]{1,0:T(8,128)(2,1)} %bitcast.11), channel_id=1, source_target_pairs={{0,1},{1,0},{2,3},{3,2},{4,5},{5,4},{6,7},{7,6},{8,9},{9,8},{10,11... | collective-permute-start | bytes 1179656 | tf_op jit(solution)/shard_map/ppermute | solution.py:560
  3.6 1.0 %copy-done = bf16[1,32,32,192]{3,2,1,0:T(8,128)(2,1)S(1)} copy-done((bf16[1,32,32,192]{3,2,1,0:T(8,128)(2,1)S(1)}, bf16[1,32,32,192]{3,2,1,0:T(8,128)(2,1)}, u32[]{:S(2)}) %copy-start) | copy-done | bytes 393240
  4.7 0.1 shard_map.94
  4.8 1.6 %collective-permute-start.2 = (bf16[192,128]{1,0:T(8,128)(2,1)S(1)}, bf16[192,128]{1,0:T(8,128)(2,1)S(1)}, u32[]{:S(2)}, u32[]{:S(2)}) collective-permute-start(bf16[192,128]{1,0:T(8,128)(2,1)S(1)} %get-tuple-element.60.refs_0_), channel_id=1, source_target_pairs={{0,8},{2,10},{4,12},{6,14},{8,16},{10,18},{12,20},{14,22},{16,24},... | collective-permute-start | bytes 147464 | tf_op jit(solution)/shard_map/ppermute | solution.py:57
  6.4 2.2 %collective-permute-start.1 = (bf16[192,128]{1,0:T(8,128)(2,1)S(1)}, bf16[192,128]{1,0:T(8,128)(2,1)S(1)}, u32[]{:S(2)}, u32[]{:S(2)}) collective-permute-start(bf16[192,128]{1,0:T(8,128)(2,1)S(1)} %get-tuple-element.60.refs_0_), channel_id=1, source_target_pairs={{0,24},{2,26},{4,28},{6,30},{8,0},{10,2},{12,4},{14,6},{16,8},{18,... | collective-permute-start | bytes 147464 | tf_op jit(solution)/shard_map/ppermute | solution.py:57
  8.7 1.5 %collective-permute-start = (bf16[192,128]{1,0:T(8,128)(2,1)S(1)}, bf16[192,128]{1,0:T(8,128)(2,1)S(1)}, u32[]{:S(2)}, u32[]{:S(2)}) collective-permute-start(bf16[192,128]{1,0:T(8,128)(2,1)S(1)} %get-tuple-element.60.refs_0_), channel_id=1, source_target_pairs={{0,4},{2,6},{4,0},{6,2},{8,12},{10,14},{12,8},{14,10},{16,20},{18,... | collective-permute-start | bytes 147464 | tf_op jit(solution)/shard_map/ppermute | solution.py:61
  10.2 1.0 %collective-permute-done.2.refs_1_.refs_3_ = bf16[192,128]{1,0:T(8,128)(2,1)S(1)} collective-permute-done((bf16[192,128]{1,0:T(8,128)(2,1)S(1)}, bf16[192,128]{1,0:T(8,128)(2,1)S(1)}, u32[]{:S(2)}, u32[]{:S(2)}) %collective-permute-start.2) | collective-permute-done | bytes 49184 | tf_op jit(solution)/shard_map/ppermute | solution.py:57
  11.2 1.6 %collective-permute-start.3 = (bf16[384,128]{1,0:T(8,128)(2,1)S(1)}, bf16[384,128]{1,0:T(8,128)(2,1)S(1)}, u32[]{:S(2)}, u32[]{:S(2)}) collective-permute-start(bf16[384,128]{1,0:T(8,128)(2,1)S(1)} %shard_map.95), channel_id=1, source_target_pairs={{0,4},{2,6},{4,0},{6,2},{8,12},{10,14},{12,8},{14,10},{16,20},{18,... | collective-permute-start | bytes 294920 | tf_op jit(solution)/shard_map/ppermute | solution.py:61
  12.7 0.7 %pad_add_fusion.tables_in = s32[16,16]{1,0:T(8,128)S(1)} fusion(s32[4,16]{1,0:T(4,128)} %bitcast.17, s32[4,16]{1,0:T(4,128)} %bitcast.18, s32[4,16]{1,0:T(4,128)} %bitcast.19, s32[4,16]{1,0:T(4,128)} %bitcast.20), kind=kLoop, calls=%fused_computation | loop fusion | flops 768 | bytes 2048 | tf_op jit(solution)/shard_map/concatenate | solution.py:568
  13.5 1.0 %copy-done.1 = bf16[1,32,32,192]{3,2,1,0:T(8,128)(2,1)S(1)} copy-done((bf16[1,32,32,192]{3,2,1,0:T(8,128)(2,1)S(1)}, bf16[1,32,32,192]{3,2,1,0:T(8,128)(2,1)}, u32[]{:S(2)}) %copy-start.1) | copy-done | bytes 393240
  14.5 1.8 %shard_map.96 = (bf16[512,1536]{1,0:T(8,128)(2,1)S(1)}, bf16[144,1536]{1,0:T(8,128)(2,1)S(1)}, bf16[128,1728]{1,0:T(8,128)(2,1)S(1)}, bf16[1024,192]{1,0:T(8,128)(2,1)S(1)}) custom-call(s32[16,16]{1,0:T(8,128)S(1)} %pad_add_fusion.tables_in, bf16[1024,192]{1,0:T(8,128)(2,1)S(1)} %bitcast.12), custom_call_target="tpu_custom_call" | custom-call | bytes 3245056 | tf_op jit(solution)/shard_map/pallas_call | solution.py:108
  16.4 2.5 %shard_map.98 = (f32[448,384]{1,0:T(8,128)S(1)}, f32[448,384]{1,0:T(8,128)S(1)}, bf16[1024,384]{1,0:T(8,128)(2,1)S(1)}, bf16[128,384]{1,0:T(8,128)(2,1)S(1)}, bf16[3,1088,192]{2,1,0:T(8,128)(2,1)S(1)}) custom-call(bf16[32,32,192]{2,1,0:T(8,128)(2,1)S(1)} %get-tuple-element.65.field_ref.refs_3_, bf16[1024,192]{1,0:T(8,128)(2,1)S(1)} %get-tuple-element.66.own_ref, ...), custom_call_target="tpu_custom_call" | custom-call | flops 679477248 | bytes 4694016 | tf_op jit(solution)/shard_map/pallas_call | solution.py:108
  19.0 0.5 collective-permute-start.8
  19.5 0.1 collective-permute-start.5
  19.6 0.4 collective-permute-start.6
  20.1 1.3 %shard_map.99.refs_3_ = f32[896,384]{1,0:T(8,128)S(1)} custom-call(bf16[3,1088,192]{2,1,0:T(8,128)(2,1)S(1)} %get-tuple-element.68.cols, bf16[1024,384]{1,0:T(8,128)(2,1)S(1)} %get-tuple-element.84.cot_ref), custom_call_target="tpu_custom_call" | custom-call | flops 679477248 | bytes 3416064 | tf_op jit(solution)/shard_map/pallas_call | solution.py:108
  21.4 1.2 %collective-permute-done.6.refs_5_ = bf16[128,384]{1,0:T(8,128)(2,1)S(1)} collective-permute-done((bf16[128,384]{1,0:T(8,128)(2,1)S(1)}, bf16[128,384]{1,0:T(8,128)(2,1)S(1)}, u32[]{:S(2)}, u32[]{:S(2)}) %collective-permute-start.6) | collective-permute-done | bytes 98336 | tf_op jit(solution)/shard_map/ppermute | solution.py:61
  22.6 0.5 shard_map.102
  23.1 1.2 %collective-permute-start.16 = (bf16[1752,128]{1,0:T(8,128)(2,1)S(1)}, bf16[1752,128]{1,0:T(8,128)(2,1)S(1)}, u32[]{:S(2)}, u32[]{:S(2)}) collective-permute-start(bf16[1752,128]{1,0:T(8,128)(2,1)S(1)} %get-tuple-element.98), channel_id=1, source_target_pairs={{0,1},{1,0},{2,3},{3,2},{4,5},{5,4},{6,7},{7,6},{8,9},{9,8},{10,11... | collective-permute-start | bytes 1345544 | tf_op jit(solution)/shard_map/ppermute | solution.py:626
  24.3 1.5 %shard_map.100 = (f32[224,384]{1,0:T(8,128)S(1)}, bf16[224,384]{1,0:T(8,128)(2,1)S(1)}, bf16[224,384]{1,0:T(8,128)(2,1)S(1)}, bf16[224,384]{1,0:T(8,128)(2,1)S(1)}) custom-call(bf16[1152,128]{1,0:T(8,128)(2,1)S(1)} %shard_map.97.refs_0_, bf16[1152,128]{1,0:T(8,128)(2,1)S(1)} %collective-permute-done.5.refs_1_, ...), custom_call_target="tpu_custom_call" | custom-call | bytes 5971968 | tf_op jit(solution)/shard_map/pallas_call | solution.py:108
  25.8 1.6 %collective-permute-start.9 = (bf16[224,384]{1,0:T(8,128)(2,1)S(1)}, bf16[224,384]{1,0:T(8,128)(2,1)S(1)}, u32[]{:S(2)}, u32[]{:S(2)}) collective-permute-start(bf16[224,384]{1,0:T(8,128)(2,1)S(1)} %get-tuple-element.81), channel_id=1, source_target_pairs={{0,4},{2,6},{4,0},{6,2},{8,12},{10,14},{12,8},{14,10},{16,20},{18,... | collective-permute-start | bytes 516104 | tf_op jit(solution)/shard_map/ppermute | solution.py:61
  27.4 1.6 %collective-permute-start.10 = (bf16[224,384]{1,0:T(8,128)(2,1)S(1)}, bf16[224,384]{1,0:T(8,128)(2,1)S(1)}, u32[]{:S(2)}, u32[]{:S(2)}) collective-permute-start(bf16[224,384]{1,0:T(8,128)(2,1)S(1)} %get-tuple-element.82), channel_id=1, source_target_pairs={{0,8},{2,10},{4,12},{6,14},{8,0},{10,2},{12,4},{14,6},{16,24},{18,... | collective-permute-start | bytes 516104 | tf_op jit(solution)/shard_map/ppermute | solution.py:61
  29.0 0.4 collective-permute-start.11
  29.4 2.9 %shard_map.101 = (f32[1024,192]{1,0:T(8,128)S(1)}, bf16[216,128]{1,0:T(8,128)(2,1)S(1)}) custom-call(bf16[1024,384]{1,0:T(8,128)(2,1)S(1)} %get-tuple-element.84.cot_ref, bf16[9,384,384]{2,1,0:T(8,128)(2,1)S(1)} %bitcast.13), custom_call_target="tpu_custom_call" | custom-call | flops 1358954496 | bytes 4282368 | tf_op jit(solution)/shard_map/pallas_call | solution.py:108
  32.3 2.4 %collective-permute-done.10.refs_2_ = bf16[224,384]{1,0:T(8,128)(2,1)S(1)} collective-permute-done((bf16[224,384]{1,0:T(8,128)(2,1)S(1)}, bf16[224,384]{1,0:T(8,128)(2,1)S(1)}, u32[]{:S(2)}, u32[]{:S(2)}) %collective-permute-start.10) | collective-permute-done | bytes 172064 | tf_op jit(solution)/shard_map/ppermute | solution.py:61
  34.7 2.2 %collective-permute-done.11.refs_3_ = bf16[224,384]{1,0:T(8,128)(2,1)S(1)} collective-permute-done((bf16[224,384]{1,0:T(8,128)(2,1)S(1)}, bf16[224,384]{1,0:T(8,128)(2,1)S(1)}, u32[]{:S(2)}, u32[]{:S(2)}) %collective-permute-start.11) | collective-permute-done | bytes 172064 | tf_op jit(solution)/shard_map/ppermute | solution.py:61
  36.9 0.1 shard_map.103
  37.0 2.7 %collective-permute-start.12 = (bf16[112,384]{1,0:T(8,128)(2,1)S(1)}, bf16[112,384]{1,0:T(8,128)(2,1)S(1)}, u32[]{:S(2)}, u32[]{:S(2)}) collective-permute-start(bf16[112,384]{1,0:T(8,128)(2,1)S(1)} %get-tuple-element.95), channel_id=1, source_target_pairs={{0,16},{2,18},{4,20},{6,22},{8,24},{10,26},{12,28},{14,30},{16,0},... | collective-permute-start | bytes 258056 | tf_op jit(solution)/shard_map/ppermute | solution.py:61
  39.7 1.6 %collective-permute-start.15 = (bf16[216,128]{1,0:T(8,128)(2,1)S(1)}, bf16[216,128]{1,0:T(8,128)(2,1)S(1)}, u32[]{:S(2)}, u32[]{:S(2)}) collective-permute-start(bf16[216,128]{1,0:T(8,128)(2,1)S(1)} %get-tuple-element.100.refs_0_), channel_id=1, source_target_pairs={{0,8},{2,10},{4,12},{6,14},{8,16},{10,18},{12,20},{14,22},{16,24},... | collective-permute-start | bytes 165896 | tf_op jit(solution)/shard_map/ppermute | solution.py:57
  41.2 2.2 %collective-permute-start.14 = (bf16[216,128]{1,0:T(8,128)(2,1)S(1)}, bf16[216,128]{1,0:T(8,128)(2,1)S(1)}, u32[]{:S(2)}, u32[]{:S(2)}) collective-permute-start(bf16[216,128]{1,0:T(8,128)(2,1)S(1)} %get-tuple-element.100.refs_0_), channel_id=1, source_target_pairs={{0,24},{2,26},{4,28},{6,30},{8,0},{10,2},{12,4},{14,6},{16,8},{18,... | collective-permute-start | bytes 165896 | tf_op jit(solution)/shard_map/ppermute | solution.py:57
  43.5 1.1 %collective-permute-done.12.refs_1_ = bf16[112,384]{1,0:T(8,128)(2,1)S(1)} collective-permute-done((bf16[112,384]{1,0:T(8,128)(2,1)S(1)}, bf16[112,384]{1,0:T(8,128)(2,1)S(1)}, u32[]{:S(2)}, u32[]{:S(2)}) %collective-permute-start.12) | collective-permute-done | bytes 86048 | tf_op jit(solution)/shard_map/ppermute | solution.py:61
  44.6 0.7 collective-permute-start.13
  45.2 0.8 %collective-permute-done.15.refs_2_ = bf16[216,128]{1,0:T(8,128)(2,1)S(1)} collective-permute-done((bf16[216,128]{1,0:T(8,128)(2,1)S(1)}, bf16[216,128]{1,0:T(8,128)(2,1)S(1)}, u32[]{:S(2)}, u32[]{:S(2)}) %collective-permute-start.15) | collective-permute-done | bytes 55328 | tf_op jit(solution)/shard_map/ppermute | solution.py:57
  46.1 1.6 %collective-permute-start.17 = (bf16[648,128]{1,0:T(8,128)(2,1)S(1)}, bf16[648,128]{1,0:T(8,128)(2,1)S(1)}, u32[]{:S(2)}, u32[]{:S(2)}) collective-permute-start(bf16[648,128]{1,0:T(8,128)(2,1)S(1)} %shard_map.106.refs_0_), channel_id=1, source_target_pairs={{0,4},{2,6},{4,0},{6,2},{8,12},{10,14},{12,8},{14,10},{16,20},{18,... | collective-permute-start | bytes 497672 | tf_op jit(solution)/shard_map/ppermute | solution.py:61
  47.7 3.9 %shard_map.105 = bf16[1024,192]{1,0:T(8,128)(2,1)} custom-call(bf16[32,32,192]{2,1,0:T(8,128)(2,1)S(1)} %get-tuple-element.65.field_ref.refs_3_, bf16[144,192]{1,0:T(8,128)(2,1)S(1)} %get-tuple-element.96.halos_ref, bf16[1752,128]{1,0:T(8,128)(2,1)S(1)} %collective-permute-done.16.other_ref, bf16[9,384,384]{2,1,0:T(8,128)(2,1)S(1)} %bitcast.14), custom_call_target="tpu_custom_call" | custom-call | flops 2717908992 | bytes 3944448 | tf_op jit(solution)/shard_map/pallas_call | solution.py:108
  51.6 7.5 %collective-permute-start.20 = (bf16[224,384]{1,0:T(8,128)(2,1)S(1)}, bf16[224,384]{1,0:T(8,128)(2,1)S(1)}, u32[]{:S(2)}, u32[]{:S(2)}) collective-permute-start(bf16[224,384]{1,0:T(8,128)(2,1)S(1)} %shard_map.107.refs_0_), channel_id=1, source_target_pairs={{0,12},{2,14},{4,8},{6,10},{8,4},{10,6},{12,0},{14,2},{16,28},{18,... | collective-permute-start | bytes 516104 | tf_op jit(solution)/shard_map/ppermute | solution.py:61
  59.1 0.6 collective-permute-start.18
  59.8 0.5 collective-permute-start.22
  60.3 0.9 %collective-permute-done.21.refs_2_ = bf16[648,128]{1,0:T(8,128)(2,1)S(1)} collective-permute-done((bf16[648,128]{1,0:T(8,128)(2,1)S(1)}, bf16[648,128]{1,0:T(8,128)(2,1)S(1)}, u32[]{:S(2)}, u32[]{:S(2)}) %collective-permute-start.21) | collective-permute-done | bytes 165920 | tf_op jit(solution)/shard_map/ppermute | solution.py:61
  61.2 0.1 collective-permute-start.23
  61.3 0.1 collective-permute-done.22.refs_3_
  61.4 1.3 %shard_map.108 = bf16[1024,192]{1,0:T(8,128)(2,1)} custom-call(bf16[128,1728]{1,0:T(8,128)(2,1)S(1)} %get-tuple-element.106.place_ref, f32[1024,192]{1,0:T(8,128)S(1)} %get-tuple-element.107.inner_ref, bf16[648,128]{1,0:T(8,128)(2,1)S(1)} %shard_map.106.refs_0_, bf16[648,128]{1,0:T(8,128)(2,1)S(1)} %collective-permute-done.17.refs_1_, ...), custom_call_target="tpu_custom_call" | custom-call | bytes 2285568 | tf_op jit(solution)/shard_map/pallas_call | solution.py:108
  62.7 1.8 %collective-permute-done.19.refs_2_ = bf16[224,384]{1,0:T(8,128)(2,1)S(1)} collective-permute-done((bf16[224,384]{1,0:T(8,128)(2,1)S(1)}, bf16[224,384]{1,0:T(8,128)(2,1)S(1)}, u32[]{:S(2)}, u32[]{:S(2)}) %collective-permute-start.19) | collective-permute-done | bytes 172064 | tf_op jit(solution)/shard_map/ppermute | solution.py:61
  64.5 0.5 collective-permute-start.25
  65.1 0.9 %collective-permute-done.24.refs_4_ = bf16[224,384]{1,0:T(8,128)(2,1)S(1)} collective-permute-done((bf16[224,384]{1,0:T(8,128)(2,1)S(1)}, bf16[224,384]{1,0:T(8,128)(2,1)S(1)}, u32[]{:S(2)}, u32[]{:S(2)}) %collective-permute-start.24) | collective-permute-done | bytes 172064 | tf_op jit(solution)/shard_map/ppermute | solution.py:61
  66.0 0.2 collective-permute-done.25.refs_5_
  66.2 1.5 %shard_map.109.refs_0_ = f32[1728,384]{1,0:T(8,128)} custom-call(bf16[224,384]{1,0:T(8,128)(2,1)S(1)} %shard_map.107.refs_0_, bf16[224,384]{1,0:T(8,128)(2,1)S(1)} %collective-permute-done.18.refs_1_, bf16[224,384]{1,0:T(8,128)(2,1)S(1)} %collective-permute-done.19.refs_2_, bf16[224,384]{1,0:T(8,128)(2,1)S(1)} %collective-permute-done.23.refs_3_, ...), custom_call_target="tpu_custom_call" | custom-call | tf_op jit(solution)/shard_map/pallas_call | solution.py:425
  67.7 0.9 %shard_map.110 = f32[1728,384]{1,0:T(8,128)} custom-call(f32[1728,384]{1,0:T(8,128)} %shard_map.109.refs_0_, bf16[224,384]{1,0:T(8,128)(2,1)S(1)} %collective-permute-done.20.refs_1_, bf16[224,384]{1,0:T(8,128)(2,1)S(1)} %collective-permute-done.26.refs_2_), custom_call_target="tpu_custom_call", output_to_operand_aliasing={{}: (0, {})} | custom-call | tf_op jit(solution)/shard_map/pallas_call | solution.py:425
  (30 shorter events, 0.3 us)
Async XLA Ops:
  0.6 15.7 %collective-permute-start.4 = (bf16[1024,192]{1,0:T(8,128)(2,1)}, bf16[1024,192]{1,0:T(8,128)(2,1)S(1)}, u32[]{:S(2)}, u32[]{:S(2)}) collective-permute-start(bf16[1024,192]{1,0:T(8,128)(2,1)} %bitcast.11), channel_id=1, source_target_pairs={{0,1},{1,0},{2,3},{3,2},{4,5},{5,4},{6,7},{7,6},{8,9},{9,8},{10,11... | collective-permute-start | bytes 1179656 | tf_op jit(solution)/shard_map/ppermute | solution.py:560
  3.6 1.0 %copy-start = (bf16[1,32,32,192]{3,2,1,0:T(8,128)(2,1)S(1)}, bf16[1,32,32,192]{3,2,1,0:T(8,128)(2,1)}, u32[]{:S(2)}) copy-start(bf16[1,32,32,192]{3,2,1,0:T(8,128)(2,1)} %param.7) | copy-start | bytes 1179652
  4.8 6.4 %collective-permute-start.2 = (bf16[192,128]{1,0:T(8,128)(2,1)S(1)}, bf16[192,128]{1,0:T(8,128)(2,1)S(1)}, u32[]{:S(2)}, u32[]{:S(2)}) collective-permute-start(bf16[192,128]{1,0:T(8,128)(2,1)S(1)} %get-tuple-element.60.refs_0_), channel_id=1, source_target_pairs={{0,8},{2,10},{4,12},{6,14},{8,16},{10,18},{12,20},{14,22},{16,24},... | collective-permute-start | bytes 147464 | tf_op jit(solution)/shard_map/ppermute | solution.py:57
  6.4 4.7 %collective-permute-start.1 = (bf16[192,128]{1,0:T(8,128)(2,1)S(1)}, bf16[192,128]{1,0:T(8,128)(2,1)S(1)}, u32[]{:S(2)}, u32[]{:S(2)}) collective-permute-start(bf16[192,128]{1,0:T(8,128)(2,1)S(1)} %get-tuple-element.60.refs_0_), channel_id=1, source_target_pairs={{0,24},{2,26},{4,28},{6,30},{8,0},{10,2},{12,4},{14,6},{16,8},{18,... | collective-permute-start | bytes 147464 | tf_op jit(solution)/shard_map/ppermute | solution.py:57
  8.7 7.7 %collective-permute-start = (bf16[192,128]{1,0:T(8,128)(2,1)S(1)}, bf16[192,128]{1,0:T(8,128)(2,1)S(1)}, u32[]{:S(2)}, u32[]{:S(2)}) collective-permute-start(bf16[192,128]{1,0:T(8,128)(2,1)S(1)} %get-tuple-element.60.refs_0_), channel_id=1, source_target_pairs={{0,4},{2,6},{4,0},{6,2},{8,12},{10,14},{12,8},{14,10},{16,20},{18,... | collective-permute-start | bytes 147464 | tf_op jit(solution)/shard_map/ppermute | solution.py:61
  11.2 5.2 %collective-permute-start.3 = (bf16[384,128]{1,0:T(8,128)(2,1)S(1)}, bf16[384,128]{1,0:T(8,128)(2,1)S(1)}, u32[]{:S(2)}, u32[]{:S(2)}) collective-permute-start(bf16[384,128]{1,0:T(8,128)(2,1)S(1)} %shard_map.95), channel_id=1, source_target_pairs={{0,4},{2,6},{4,0},{6,2},{8,12},{10,14},{12,8},{14,10},{16,20},{18,... | collective-permute-start | bytes 294920 | tf_op jit(solution)/shard_map/ppermute | solution.py:61
  13.5 1.0 %copy-start.1 = (bf16[1,32,32,192]{3,2,1,0:T(8,128)(2,1)S(1)}, bf16[1,32,32,192]{3,2,1,0:T(8,128)(2,1)}, u32[]{:S(2)}) copy-start(bf16[1,32,32,192]{3,2,1,0:T(8,128)(2,1)} %param.9) | copy-start | bytes 1179652
  18.9 5.4 %collective-permute-start.7 = (f32[448,384]{1,0:T(8,128)S(1)}, f32[448,384]{1,0:T(8,128)S(1)}, u32[]{:S(2)}, u32[]{:S(2)}) collective-permute-start(f32[448,384]{1,0:T(8,128)S(1)} %get-tuple-element.75), channel_id=1, source_target_pairs={{0,2},{2,0},{4,6},{6,4},{8,10},{10,8},{12,14},{14,12},{16,18},{18,... | collective-permute-start | bytes 2064392 | tf_op jit(solution)/shard_map/ppermute | solution.py:61
  19.0 5.4 %collective-permute-start.8 = (f32[448,384]{1,0:T(8,128)S(1)}, f32[448,384]{1,0:T(8,128)S(1)}, u32[]{:S(2)}, u32[]{:S(2)}) collective-permute-start(f32[448,384]{1,0:T(8,128)S(1)} %get-tuple-element.76), channel_id=1, source_target_pairs={{0,2},{2,0},{4,6},{6,4},{8,10},{10,8},{12,14},{14,12},{16,18},{18,... | collective-permute-start | bytes 2064392 | tf_op jit(solution)/shard_map/ppermute | solution.py:61
  19.5 3.2 %collective-permute-start.5 = (bf16[1152,128]{1,0:T(8,128)(2,1)S(1)}, bf16[1152,128]{1,0:T(8,128)(2,1)S(1)}, u32[]{:S(2)}, u32[]{:S(2)}) collective-permute-start(bf16[1152,128]{1,0:T(8,128)(2,1)S(1)} %shard_map.97.refs_0_), channel_id=1, source_target_pairs={{0,2},{2,0},{4,6},{6,4},{8,10},{10,8},{12,14},{14,12},{16,18},{18,... | collective-permute-start | bytes 884744 | tf_op jit(solution)/shard_map/ppermute | solution.py:61
  19.6 3.0 %collective-permute-start.6 = (bf16[128,384]{1,0:T(8,128)(2,1)S(1)}, bf16[128,384]{1,0:T(8,128)(2,1)S(1)}, u32[]{:S(2)}, u32[]{:S(2)}) collective-permute-start(bf16[128,384]{1,0:T(8,128)(2,1)S(1)} %get-tuple-element.70.refs_4_), channel_id=1, source_target_pairs={{0,2},{2,0},{4,6},{6,4},{8,10},{10,8},{12,14},{14,12},{16,18},{18,... | collective-permute-start | bytes 294920 | tf_op jit(solution)/shard_map/ppermute | solution.py:61
  23.1 6.3 %copy-start.2 = (bf16[3,3,384,384]{3,2,1,0:T(8,128)(2,1)S(1)}, bf16[3,3,384,384]{3,2,1,0:T(8,128)(2,1)}, u32[]{:S(2)}) copy-start(bf16[3,3,384,384]{3,2,1,0:T(8,128)(2,1)} %param.8) | copy-start | bytes 7962628
  23.1 22.1 %collective-permute-start.16 = (bf16[1752,128]{1,0:T(8,128)(2,1)S(1)}, bf16[1752,128]{1,0:T(8,128)(2,1)S(1)}, u32[]{:S(2)}, u32[]{:S(2)}) collective-permute-start(bf16[1752,128]{1,0:T(8,128)(2,1)S(1)} %get-tuple-element.98), channel_id=1, source_target_pairs={{0,1},{1,0},{2,3},{3,2},{4,5},{5,4},{6,7},{7,6},{8,9},{9,8},{10,11... | collective-permute-start | bytes 1345544 | tf_op jit(solution)/shard_map/ppermute | solution.py:626
  25.8 6.5 %collective-permute-start.9 = (bf16[224,384]{1,0:T(8,128)(2,1)S(1)}, bf16[224,384]{1,0:T(8,128)(2,1)S(1)}, u32[]{:S(2)}, u32[]{:S(2)}) collective-permute-start(bf16[224,384]{1,0:T(8,128)(2,1)S(1)} %get-tuple-element.81), channel_id=1, source_target_pairs={{0,4},{2,6},{4,0},{6,2},{8,12},{10,14},{12,8},{14,10},{16,20},{18,... | collective-permute-start | bytes 516104 | tf_op jit(solution)/shard_map/ppermute | solution.py:61
  27.4 7.3 %collective-permute-start.10 = (bf16[224,384]{1,0:T(8,128)(2,1)S(1)}, bf16[224,384]{1,0:T(8,128)(2,1)S(1)}, u32[]{:S(2)}, u32[]{:S(2)}) collective-permute-start(bf16[224,384]{1,0:T(8,128)(2,1)S(1)} %get-tuple-element.82), channel_id=1, source_target_pairs={{0,8},{2,10},{4,12},{6,14},{8,0},{10,2},{12,4},{14,6},{16,24},{18,... | collective-permute-start | bytes 516104 | tf_op jit(solution)/shard_map/ppermute | solution.py:61
  29.0 7.9 %collective-permute-start.11 = (bf16[224,384]{1,0:T(8,128)(2,1)S(1)}, bf16[224,384]{1,0:T(8,128)(2,1)S(1)}, u32[]{:S(2)}, u32[]{:S(2)}) collective-permute-start(bf16[224,384]{1,0:T(8,128)(2,1)S(1)} %get-tuple-element.83), channel_id=1, source_target_pairs={{0,12},{2,14},{4,8},{6,10},{8,4},{10,6},{12,0},{14,2},{16,28},{18,... | collective-permute-start | bytes 516104 | tf_op jit(solution)/shard_map/ppermute | solution.py:61
  37.0 7.6 %collective-permute-start.12 = (bf16[112,384]{1,0:T(8,128)(2,1)S(1)}, bf16[112,384]{1,0:T(8,128)(2,1)S(1)}, u32[]{:S(2)}, u32[]{:S(2)}) collective-permute-start(bf16[112,384]{1,0:T(8,128)(2,1)S(1)} %get-tuple-element.95), channel_id=1, source_target_pairs={{0,16},{2,18},{4,20},{6,22},{8,24},{10,26},{12,28},{14,30},{16,0},... | collective-permute-start | bytes 258056 | tf_op jit(solution)/shard_map/ppermute | solution.py:61
  39.7 6.4 %collective-permute-start.15 = (bf16[216,128]{1,0:T(8,128)(2,1)S(1)}, bf16[216,128]{1,0:T(8,128)(2,1)S(1)}, u32[]{:S(2)}, u32[]{:S(2)}) collective-permute-start(bf16[216,128]{1,0:T(8,128)(2,1)S(1)} %get-tuple-element.100.refs_0_), channel_id=1, source_target_pairs={{0,8},{2,10},{4,12},{6,14},{8,16},{10,18},{12,20},{14,22},{16,24},... | collective-permute-start | bytes 165896 | tf_op jit(solution)/shard_map/ppermute | solution.py:57
  41.2 4.8 %collective-permute-start.14 = (bf16[216,128]{1,0:T(8,128)(2,1)S(1)}, bf16[216,128]{1,0:T(8,128)(2,1)S(1)}, u32[]{:S(2)}, u32[]{:S(2)}) collective-permute-start(bf16[216,128]{1,0:T(8,128)(2,1)S(1)} %get-tuple-element.100.refs_0_), channel_id=1, source_target_pairs={{0,24},{2,26},{4,28},{6,30},{8,0},{10,2},{12,4},{14,6},{16,8},{18,... | collective-permute-start | bytes 165896 | tf_op jit(solution)/shard_map/ppermute | solution.py:57
  44.6 7.0 %collective-permute-start.13 = (bf16[112,384]{1,0:T(8,128)(2,1)S(1)}, bf16[112,384]{1,0:T(8,128)(2,1)S(1)}, u32[]{:S(2)}, u32[]{:S(2)}) collective-permute-start(bf16[112,384]{1,0:T(8,128)(2,1)S(1)} %shard_map.104.refs_0_), channel_id=1, source_target_pairs={{0,16},{2,18},{4,20},{6,22},{8,24},{10,26},{12,28},{14,30},{16,0},... | collective-permute-start | bytes 258056 | tf_op jit(solution)/shard_map/ppermute | solution.py:61
  46.1 5.5 %collective-permute-start.17 = (bf16[648,128]{1,0:T(8,128)(2,1)S(1)}, bf16[648,128]{1,0:T(8,128)(2,1)S(1)}, u32[]{:S(2)}, u32[]{:S(2)}) collective-permute-start(bf16[648,128]{1,0:T(8,128)(2,1)S(1)} %shard_map.106.refs_0_), channel_id=1, source_target_pairs={{0,4},{2,6},{4,0},{6,2},{8,12},{10,14},{12,8},{14,10},{16,20},{18,... | collective-permute-start | bytes 497672 | tf_op jit(solution)/shard_map/ppermute | solution.py:61
  51.6 11.1 %collective-permute-start.20 = (bf16[224,384]{1,0:T(8,128)(2,1)S(1)}, bf16[224,384]{1,0:T(8,128)(2,1)S(1)}, u32[]{:S(2)}, u32[]{:S(2)}) collective-permute-start(bf16[224,384]{1,0:T(8,128)(2,1)S(1)} %shard_map.107.refs_0_), channel_id=1, source_target_pairs={{0,12},{2,14},{4,8},{6,10},{8,4},{10,6},{12,0},{14,2},{16,28},{18,... | collective-permute-start | bytes 516104 | tf_op jit(solution)/shard_map/ppermute | solution.py:61
  59.1 5.4 %collective-permute-start.19 = (bf16[224,384]{1,0:T(8,128)(2,1)S(1)}, bf16[224,384]{1,0:T(8,128)(2,1)S(1)}, u32[]{:S(2)}, u32[]{:S(2)}) collective-permute-start(bf16[224,384]{1,0:T(8,128)(2,1)S(1)} %shard_map.107.refs_0_), channel_id=1, source_target_pairs={{0,8},{2,10},{4,12},{6,14},{8,0},{10,2},{12,4},{14,6},{16,24},{18,... | collective-permute-start | bytes 516104 | tf_op jit(solution)/shard_map/ppermute | solution.py:61
  59.1 5.4 %collective-permute-start.18 = (bf16[224,384]{1,0:T(8,128)(2,1)S(1)}, bf16[224,384]{1,0:T(8,128)(2,1)S(1)}, u32[]{:S(2)}, u32[]{:S(2)}) collective-permute-start(bf16[224,384]{1,0:T(8,128)(2,1)S(1)} %shard_map.107.refs_0_), channel_id=1, source_target_pairs={{0,4},{2,6},{4,0},{6,2},{8,12},{10,14},{12,8},{14,10},{16,20},{18,... | collective-permute-start | bytes 516104 | tf_op jit(solution)/shard_map/ppermute | solution.py:61
  59.8 1.4 %collective-permute-start.21 = (bf16[648,128]{1,0:T(8,128)(2,1)S(1)}, bf16[648,128]{1,0:T(8,128)(2,1)S(1)}, u32[]{:S(2)}, u32[]{:S(2)}) collective-permute-start(bf16[648,128]{1,0:T(8,128)(2,1)S(1)} %shard_map.106.refs_0_), channel_id=1, source_target_pairs={{0,2},{2,0},{4,6},{6,4},{8,10},{10,8},{12,14},{14,12},{16,18},{18,... | collective-permute-start | bytes 497672 | tf_op jit(solution)/shard_map/ppermute | solution.py:61
  59.8 1.6 %collective-permute-start.22 = (bf16[648,128]{1,0:T(8,128)(2,1)S(1)}, bf16[648,128]{1,0:T(8,128)(2,1)S(1)}, u32[]{:S(2)}, u32[]{:S(2)}) collective-permute-start(bf16[648,128]{1,0:T(8,128)(2,1)S(1)} %collective-permute-done.17.refs_1_), channel_id=1, source_target_pairs={{0,2},{2,0},{4,6},{6,4},{8,10},{10,8},{12,14},{14,12},{16,18},{18,... | collective-permute-start | bytes 497672 | tf_op jit(solution)/shard_map/ppermute | solution.py:61
  61.2 3.9 %collective-permute-start.23 = (bf16[224,384]{1,0:T(8,128)(2,1)S(1)}, bf16[224,384]{1,0:T(8,128)(2,1)S(1)}, u32[]{:S(2)}, u32[]{:S(2)}) collective-permute-start(bf16[224,384]{1,0:T(8,128)(2,1)S(1)} %shard_map.107.refs_0_), channel_id=1, source_target_pairs={{0,2},{2,0},{4,6},{6,4},{8,10},{10,8},{12,14},{14,12},{16,18},{18,... | collective-permute-start | bytes 516104 | tf_op jit(solution)/shard_map/ppermute | solution.py:61
  64.5 1.4 %collective-permute-start.24 = (bf16[224,384]{1,0:T(8,128)(2,1)S(1)}, bf16[224,384]{1,0:T(8,128)(2,1)S(1)}, u32[]{:S(2)}, u32[]{:S(2)}) collective-permute-start(bf16[224,384]{1,0:T(8,128)(2,1)S(1)} %collective-permute-done.18.refs_1_), channel_id=1, source_target_pairs={{0,2},{2,0},{4,6},{6,4},{8,10},{10,8},{12,14},{14,12},{16,18},{18,... | collective-permute-start | bytes 516104 | tf_op jit(solution)/shard_map/ppermute | solution.py:61
  64.5 1.7 %collective-permute-start.25 = (bf16[224,384]{1,0:T(8,128)(2,1)S(1)}, bf16[224,384]{1,0:T(8,128)(2,1)S(1)}, u32[]{:S(2)}, u32[]{:S(2)}) collective-permute-start(bf16[224,384]{1,0:T(8,128)(2,1)S(1)} %collective-permute-done.19.refs_2_), channel_id=1, source_target_pairs={{0,2},{2,0},{4,6},{6,4},{8,10},{10,8},{12,14},{14,12},{16,18},{18,... | collective-permute-start | bytes 516104 | tf_op jit(solution)/shard_map/ppermute | solution.py:61
  65.1 2.7 %collective-permute-start.26 = (bf16[224,384]{1,0:T(8,128)(2,1)S(1)}, bf16[224,384]{1,0:T(8,128)(2,1)S(1)}, u32[]{:S(2)}, u32[]{:S(2)}) collective-permute-start(bf16[224,384]{1,0:T(8,128)(2,1)S(1)} %collective-permute-done.20.refs_1_), channel_id=1, source_target_pairs={{0,2},{2,0},{4,6},{6,4},{8,10},{10,8},{12,14},{14,12},{16,18},{18,... | collective-permute-start | bytes 516104 | tf_op jit(solution)/shard_map/ppermute | solution.py:61

commit v8 on v7

--- a/solution.py
+++ b/solution.py
@@ -174,78 +174,98 @@
     out_ref[2] = jnp.where(column == side - 1, east, pltpu.roll(tall, flat - 1, 0)).astype(jnp.bfloat16)
 
 
-def onehot_kernel(side, tables_in, cot_in, border_ref, halo_ref, place_ref, cot_ref, tables, sem):
+class Neighbours:
+    def __init__(self, side, tables):
+        self.side = side
+        self.et, self.eu, self.ct, self.cu = [tables.at[4 * i : 4 * i + 4] for i in range(4)]
+        self.digits = turn_tables()
+        self.count = lax.axis_size("tile")
+        self.own = lax.axis_index("tile")
+
+    def block(self, source):
+        groups = self.count // SPAN
+        slab = lax.rem(source // SPAN - self.own // SPAN + groups, groups)
+        cross = source ^ self.own
+        turn = lax.rem(cross // 2, 2)
+        at = jnp.where(slab == 0, turn, jnp.where(slab == 1, 2, 3) + 2 * turn)
+        return 6 * lax.rem(cross, 2) + at
+
+    def edge(self, tile, e):
+        slot = slot_in(self.digits[e], self.eu[e, tile])
+        start = lax.rem(slot, 4) * self.side
+        end = start + self.side - 1
+        return self.block(self.et[e, tile]), lambda at: jnp.where(slot >= 4, end - at, start + at)
+
+    def corner(self, tile, c):
+        slot = slot_in(self.digits[4 + c], self.cu[c, tile])
+        return self.block(self.ct[c, tile]), corner_spot(slot, self.side)
+
+
+def onehot(wanted, width):
+    lane = lax.broadcasted_iota(jnp.int32, (wanted.shape[0], width), 1)
+    return jnp.where(lane == wanted, 1.0, 0.0).astype(jnp.bfloat16)
+
+
+def border_onehot_kernel(side, tables_in, cot_in, border_ref, cot_ref, tables, sem):
     copy = pltpu.make_async_copy(tables_in, tables, sem)
     copy.start()
     cot_ref[...] = cot_in[...]
+    border_ref[...] = jnp.zeros_like(border_ref)
     copy.wait()
-    et, eu, ct, cu = [tables.at[4 * i : 4 * i + 4] for i in range(4)]
-    digits = turn_tables()
-    count = lax.axis_size("tile")
-    own = lax.axis_index("tile")
-    core = lax.rem(own, 2)
-    groups = count // SPAN
-
-    def base(source):
-        slab = lax.rem(source // SPAN - own // SPAN + groups, groups)
-        cross = source ^ own
-        turn = lax.rem(cross // 2, 2)
-        at = jnp.where(slab == 0, turn, jnp.where(slab == 1, 2, 3) + 2 * turn)
-        return (6 * lax.rem(cross, 2) + at) * (4 * side)
-
+    near = Neighbours(side, tables)
+    low = lax.rem(near.own, 2) == 0
+    width = 4 * side
     step = lax.broadcasted_iota(jnp.int32, (side, 1), 0)
-    nothing = jnp.full((side, 1), -1, jnp.int32)
-
-    def halo(tile, e):
-        slot = slot_in(digits[e], eu[e, tile])
-        start = base(et[e, tile]) + lax.rem(slot, 4) * side
-        return lambda at: jnp.where(slot >= 4, start + side - 1 - at, start + at)
-
-    def corner(tile, c):
-        return base(ct[c, tile]) + corner_spot(slot_in(digits[4 + c], cu[c, tile]), side)
-
-    def onehot(wanted, width):
-        lane = lax.broadcasted_iota(jnp.int32, (wanted.shape[0], width), 1)
-        return jnp.where(lane == wanted, 1.0, 0.0).astype(jnp.bfloat16)
-
-    width = 12 * 4 * side
-    pieces = [[] for _ in range(4)]
-    for tile in (own, own ^ 1):
-        top, right, bottom, left = [halo(tile, e) for e in range(4)]
-        corners = [corner(tile, c) for c in range(4)]
-        low = core == 0
-        row = lambda at: jnp.where(low, top(at), bottom(at))
-        first = jnp.where(low, corners[0], corners[3])
-        last = jnp.where(low, corners[1], corners[2])
+
+    def put(row, block, wanted, add=False):
+        here = (slice(row, row + side), pl.ds(pl.multiple_of(block * width, 128), width))
+        value = onehot(wanted, width)
+        border_ref[here] = border_ref[here] + value if add else value
+
+    for m, tile in enumerate((near.own, near.own ^ 1)):
+        first = 2 * m * side
+        flat = [near.edge(tile, e) for e in range(4)]
+        corners = [near.corner(tile, c) for c in range(4)]
+        pick = lambda a, b: (jnp.where(low, a[0], b[0]), lambda at: jnp.where(low, a[1](at), b[1](at)))
+        block, at = pick(flat[0], flat[2])
+        left, right = [
+            (jnp.where(low, corners[a][0], corners[b][0]), jnp.where(low, corners[a][1], corners[b][1]))
+            for a, b in ((0, 3), (1, 2))
+        ]
         along = jnp.where(low, step - 1, step + 1)
         fits = (along >= 0) & (along < side)
-        pieces[0] += [jnp.where(step == 0, first, row(step - 1)), jnp.where(fits, left(along), nothing)]
-        pieces[1] += [row(step), nothing]
-        pieces[2] += [jnp.where(step == side - 1, last, row(step + 1)), jnp.where(fits, right(along), nothing)]
-        pieces[3] += [nothing, jnp.where(low, left(step), right(step))]
-    border_ref[...] = onehot(jnp.concatenate(sum(pieces, []), axis=0), width)
-    spots = lax.broadcasted_iota(jnp.int32, (EXTRA, 1), 0)
-    ends = jnp.full((EXTRA, 1), -1, jnp.int32)
-    for c in range(4):
-        ends = jnp.where(spots == c, corner(own, c), ends)
-    halo_ref[...] = onehot(jnp.concatenate([halo(own, e)(step) for e in range(4)] + [ends], axis=0), width)
-
+        put(first, block, jnp.where(step == 0, -1, at(step - 1)))
+        put(first, left[0], jnp.where(step == 0, left[1], -1), add=True)
+        put(first + side, flat[3][0], jnp.where(fits, flat[3][1](along), -1))
+        put(first + 4 * side, block, at(step))
+        put(first + 8 * side, block, jnp.where(step == side - 1, -1, at(step + 1)))
+        put(first + 8 * side, right[0], jnp.where(step == side - 1, right[1], -1), add=True)
+        put(first + 9 * side, flat[1][0], jnp.where(fits, flat[1][1](along), -1))
+        block, at = pick(flat[3], flat[1])
+        put(first + 13 * side, block, at(step))
+
+
+def place_kernel(side, tables_in, place_ref, tables, sem):
+    copy = pltpu.make_async_copy(tables_in, tables, sem)
+    copy.start()
+    copy.wait()
+    near = Neighbours(side, tables)
     block = 4 * side + EXTRA
     lane = lax.broadcasted_iota(jnp.int32, (1, block), 1)
     row = lax.broadcasted_iota(jnp.int32, (4 * side, block), 0)
     places = []
     for mask in (0, 2, 1, 3):
         for offset in (0, SPAN, -SPAN):
-            source = lax.rem((own ^ mask) + offset + count, count)
+            source = lax.rem((near.own ^ mask) + offset + near.count, near.count)
             target = jnp.full((1, block), -1, jnp.int32)
             for e in range(4):
-                slot = slot_in(digits[e], eu[e, source])
+                slot = slot_in(near.digits[e], near.eu[e, source])
                 along = lane - e * side
                 along = jnp.where(slot >= 4, side - 1 - along, along)
-                hit = (lane >= e * side) & (lane < (e + 1) * side) & (et[e, source] == own)
+                hit = (lane >= e * side) & (lane < (e + 1) * side) & (near.et[e, source] == near.own)
                 target = jnp.where(hit, lax.rem(slot, 4) * side + along, target)
-                spot = corner_spot(slot_in(digits[4 + e], cu[e, source]), side)
-                hit = (lane == 4 * side + e) & (ct[e, source] == own)
+                spot = corner_spot(slot_in(near.digits[4 + e], near.cu[e, source]), side)
+                hit = (lane == 4 * side + e) & (near.ct[e, source] == near.own)
                 target = jnp.where(hit, spot, target)
             places.append(jnp.where(row == target, 1.0, 0.0))
     place_ref[...] = jnp.concatenate(places, axis=1).astype(jnp.bfloat16)
@@ -507,13 +527,28 @@
 
 
 def halo_kernel(side, part, n_near, *refs):
-    near_refs, onehot_ref, field_ref = refs[:n_near], refs[n_near], refs[n_near + 1]
-    halos_ref, packet_ref, near = refs[n_near + 2 :]
+    near_refs, tables_in, field_ref = refs[:n_near], refs[n_near], refs[n_near + 1]
+    halos_ref, packet_ref, near, tables, sem = refs[n_near + 2 :]
+    copy = pltpu.make_async_copy(tables_in, tables, sem)
+    copy.start()
     rows = side * side
     unpack_near(near_refs, near, side, part)
-    halos = jnp.dot(onehot_ref[...], near[...], preferred_element_type=jnp.float32).astype(jnp.bfloat16)
+    pack(field_ref[...].reshape(rows, part), packet_ref)
+    copy.wait()
+    index = Neighbours(side, tables)
+    step = lax.broadcasted_iota(jnp.int32, (side, 1), 0)
+    wanted = []
+    for e in range(4):
+        block, at = index.edge(index.own, e)
+        wanted.append(block * (4 * side) + at(step))
+    spots = lax.broadcasted_iota(jnp.int32, (EXTRA, 1), 0)
+    ends = jnp.full((EXTRA, 1), -1, jnp.int32)
+    for c in range(4):
+        block, spot = index.corner(index.own, c)
+        ends = jnp.where(spots == c, block * (4 * side) + spot, ends)
+    pick = onehot(jnp.concatenate(wanted + [ends], axis=0), near.shape[0])
+    halos = jnp.dot(pick, near[...], preferred_element_type=jnp.float32).astype(jnp.bfloat16)
     halos_ref[...] = halos
-    pack(field_ref[...].reshape(rows, part), packet_ref)
     pack(halos, packet_ref, packed_shape(rows, part)[0])
 
 
@@ -566,16 +601,12 @@
     ahead, behind = by_offset(sides, -SPAN, count), by_offset(sides, SPAN, count)
     across = by_mask(sides, 2, count)
     tables = jnp.concatenate([edge_tiles.T, edge_turns.T, corner_tiles.T, corner_turns.T], axis=0)
-    border_pick, halo_pick, place, cot_own = call(
-        functools.partial(onehot_kernel, side),
-        [
-            vmem((16 * side, 48 * side), half_bytes),
-            vmem((block, 48 * side), half_bytes),
-            vmem((4 * side, 12 * block), half_bytes),
-            vmem((rows, part), half_bytes),
-        ],
+    table_scratch = [pltpu.SMEM(tables.shape, jnp.int32), pltpu.SemaphoreType.DMA]
+    border_pick, cot_own = call(
+        functools.partial(border_onehot_kernel, side),
+        [vmem((16 * side, 48 * side), half_bytes), vmem((rows, part), half_bytes)],
         [tables, cot_own],
-        scratch=[pltpu.SMEM(tables.shape, jnp.int32), pltpu.SemaphoreType.DMA],
+        scratch=table_scratch,
     )
     pair = packed_shape(8 * side, part)
     (beyond,) = call(join_kernel, [vmem(pair, half_bytes)], [ahead, behind])
@@ -615,15 +646,8 @@
         [*near, border_pick, mine, rim, rim_mate, *[by_mask(v, 1, count) for v in send]],
         scratch=[pltpu.VMEM((48 * side, part), half_bytes), pltpu.VMEM((half, chans), jnp.float32)],
     )
-    send, cot_full = lax.optimization_barrier((send, cot_full))
+    send, cot_full, near = lax.optimization_barrier((send, cot_full, near))
     got = [by_mask(v, m, count) for v, m in zip(send, masks[1:])]
-    halos, packet = call(
-        functools.partial(halo_kernel, side, part, len(near)),
-        [vmem((block, part), half_bytes), vmem(packed_shape(rows + block, part), half_bytes)],
-        [*near, halo_pick, field],
-        scratch=[pltpu.VMEM((48 * side, part), half_bytes)],
-    )
-    other_field = lax.ppermute(packet, "ch", others)
     inner, pieces = call(
         functools.partial(back_kernel, side, part),
         [vmem((rows, part), jnp.float32), vmem(packed_shape(block, part), half_bytes)],
@@ -631,7 +655,20 @@
         scratch=[pltpu.VMEM((rows + 4 * side, chans), half_bytes)],
         flops=flops,
     )
-    got, pieces, inner, halos = lax.optimization_barrier((got, pieces, inner, halos))
+    here = [pieces, by_offset(pieces, -SPAN, count), by_offset(pieces, SPAN, count)]
+    (place,) = call(
+        functools.partial(place_kernel, side),
+        [vmem((4 * side, 12 * block), half_bytes)],
+        [tables],
+        scratch=table_scratch,
+    )
+    halos, packet = call(
+        functools.partial(halo_kernel, side, part, len(near)),
+        [vmem((block, part), half_bytes), vmem(packed_shape(rows + block, part), half_bytes)],
+        [*near, tables, field],
+        scratch=[pltpu.VMEM((48 * side, part), half_bytes), *table_scratch],
+    )
+    got, here, inner, halos, packet = lax.optimization_barrier((got, here, inner, halos, packet))
     for index, bits in enumerate(stages[2:]):
         masks = group_masks(bits)
         size = held.shape[0] // len(masks)
@@ -640,32 +677,21 @@
             [vmem((size, chans), jnp.float32)] + [vmem((size, chans), half_bytes)] * (len(masks) - 1),
             [held, *got],
         )
-        send, pieces = lax.optimization_barrier((send, pieces))
+        if index == 0:
+            send, here, packet = lax.optimization_barrier((send, here, packet))
         got = [by_mask(v, m, count) for v, m in zip(send, masks[1:])]
         if index == 0:
-            here = [pieces, by_offset(pieces, -SPAN, count), by_offset(pieces, SPAN, count)]
+            (here,) = call(join_kernel, [vmem((3 * pieces.shape[0], pieces.shape[1]), half_bytes)], here)
+            beside = by_mask(here, 2, count)
+            other_field = lax.ppermute(packet, "ch", others)
+            got, here = lax.optimization_barrier((got, here))
     (held,) = call(functools.partial(sum_kernel, len(got), 1), [vmem(held.shape, half_bytes)], [held, *got])
     order = [0]
     for index, bits in enumerate(stages[:0:-1]):
         masks = group_masks(bits)
-        if index == 0:
-            _, here, other_field = lax.optimization_barrier((held, here, other_field))
-            (here,) = call(join_kernel, [vmem((3 * pieces.shape[0], pieces.shape[1]), half_bytes)], here)
-            beside = by_mask(here, 2, count)
-            (output,) = call(
-                functools.partial(output_kernel, side, part),
-                [vmem((rows, part), half_bytes)],
-                [field, halos, other_field, taps],
-                scratch=[
-                    pltpu.VMEM((3, flat, part), half_bytes),
-                    pltpu.VMEM((3, flat, part), half_bytes),
-                    pltpu.VMEM((rows + block, part), half_bytes),
-                ],
-                flops=2 * flops,
-            )
         got = [by_mask(held, m, count) for m in masks[1:]]
         if index == 0:
-            held, got, output, beside = lax.optimization_barrier((held, got, output, beside))
+            held, got, beside = lax.optimization_barrier((held, got, beside))
         if index < len(stages) - 2:
             order = [m + v for m in masks for v in order]
             (held,) = call(
@@ -679,7 +705,18 @@
             [place, inner, *got_pieces],
             scratch=[pltpu.VMEM((12 * block, part), half_bytes)],
         )
-        got, grad_features = lax.optimization_barrier((got, grad_features))
+        (output,) = call(
+            functools.partial(output_kernel, side, part),
+            [vmem((rows, part), half_bytes)],
+            [field, halos, other_field, taps],
+            scratch=[
+                pltpu.VMEM((3, flat, part), half_bytes),
+                pltpu.VMEM((3, flat, part), half_bytes),
+                pltpu.VMEM((rows + block, part), half_bytes),
+            ],
+            flops=2 * flops,
+        )
+        got, grad_features, output = lax.optimization_barrier((got, grad_features, output))
         got = [held, *got]
         order = [[m + v for v in order] for m in masks]
     mates = [by_mask(v, 1, count) for v in got]

time: 69 us -> 69.8 us (1.012)
  starting transfers between devices: 33.9 us -> 23.9 us
  waiting for transfers between devices: 12.7 us -> 22.3 us
  Pallas kernels: 18.4 us -> 19.7 us
    ppermute x21, starting transfers between devices: 22 us -> 13.6 us  [by_mask(): return lax.ppermute(value, 'tile', [(i, i ^ mask) for i in range(count)])]
    ppermute x4, waiting for transfers between devices: 1.8 us -> 7.63 us  [by_offset(): lax.ppermute(value, 'tile', [(i, (i + offset) % count) for i in range(cou...]
    ppermute x21, waiting for transfers between devices: 10.9 us -> 14.7 us  [by_mask(): return lax.ppermute(value, 'tile', [(i, i ^ mask) for i in range(count)])]
    ppermute x4, starting transfers between devices: 7.7 us -> 5.69 us  [by_offset(): lax.ppermute(value, 'tile', [(i, (i + offset) % count) for i in range(cou...]
    pallas_call x15 -> x16, Pallas kernels: 16 us -> 17.2 us  [call(): pl.pallas_call(kernel, out_shape=tuple(outs), in_specs=in_specs, out_spec...]
  transfers between devices with their start and end apart: 27 -> 27, of which waited for: 11 -> 11; matrix products, arithmetic and copies ran while one was open for 1% -> 1% of each run, Pallas kernels for 22% -> 21%
where the time goes in v8:
time: 69.8 us; the launch traced here: 69.6 us
  starting transfers between devices  23.9 us (34%)
  waiting for transfers between devices  22.3 us (32%)
  Pallas kernels  19.7 us (28%)
  local copies, waits for them, and re-layouts  2.09 us (3%)
  between operations  0.94 us (1%)
  other arithmetic  0.74 us (1%)
    pallas_call x16, Pallas kernels, call(): pl.pallas_call(kernel, out_shape=tuple(outs), in_specs=in_specs, out_spec...  17.2 us
    ppermute x21, waiting for transfers between devices, by_mask(): return lax.ppermute(value, 'tile', [(i, i ^ mask) for i in range(count)])  14.7 us
    ppermute x21, starting transfers between devices, by_mask(): return lax.ppermute(value, 'tile', [(i, i ^ mask) for i in range(count)])  13.6 us
    ppermute x4, waiting for transfers between devices, by_offset(): lax.ppermute(value, 'tile', [(i, (i + offset) % count) for i in range(cou...  7.63 us
    ppermute x4, starting transfers between devices, by_offset(): lax.ppermute(value, 'tile', [(i, (i + offset) % count) for i in range(cou...  5.69 us
    ppermute x1, starting transfers between devices, body(): cot_other = lax.ppermute(cot_own, 'ch', others)  3 us
    pallas_call x2, Pallas kernels, unfold(): pl.pallas_call(functools.partial(unfold_kernel, whole.shape[0] // 2, chun...  2.41 us
    unnamed x6, local copies, waits for them, and re-layouts  2.09 us
  transfers between devices with their start and end apart: 27, of which 11 were waited for; matrix products, arithmetic and copies ran while one was open for 1% of the time, Pallas kernels for 21%

profile of v8, /device:TPU:0, one launch (start us, length us, event | category | flops | bytes accessed | tf_op | source)
XLA Modules:
  0.0 69.6 jit_solution(2273300125057552318)
XLA Ops:
  0.6 3.0 %collective-permute-start.4 = (bf16[1024,192]{1,0:T(8,128)(2,1)}, bf16[1024,192]{1,0:T(8,128)(2,1)S(1)}, u32[]{:S(2)}, u32[]{:S(2)}) collective-permute-start(bf16[1024,192]{1,0:T(8,128)(2,1)} %bitcast.11), channel_id=1, source_target_pairs={{0,1},{1,0},{2,3},{3,2},{4,5},{5,4},{6,7},{7,6},{8,9},{9,8},{10,11... | collective-permute-start | bytes 1179656 | tf_op jit(solution)/shard_map/ppermute | solution.py:595
  3.6 1.0 %copy-done = bf16[1,32,32,192]{3,2,1,0:T(8,128)(2,1)S(1)} copy-done((bf16[1,32,32,192]{3,2,1,0:T(8,128)(2,1)S(1)}, bf16[1,32,32,192]{3,2,1,0:T(8,128)(2,1)}, u32[]{:S(2)}) %copy-start) | copy-done | bytes 393240
  4.7 0.1 shard_map.94
  4.8 3.7 %collective-permute-start.1 = (bf16[192,128]{1,0:T(8,128)(2,1)S(1)}, bf16[192,128]{1,0:T(8,128)(2,1)S(1)}, u32[]{:S(2)}, u32[]{:S(2)}) collective-permute-start(bf16[192,128]{1,0:T(8,128)(2,1)S(1)} %get-tuple-element.64.refs_0_), channel_id=1, source_target_pairs={{0,24},{2,26},{4,28},{6,30},{8,0},{10,2},{12,4},{14,6},{16,8},{18,... | collective-permute-start | bytes 147464 | tf_op jit(solution)/shard_map/ppermute | solution.py:57
  8.4 1.5 %collective-permute-start = (bf16[192,128]{1,0:T(8,128)(2,1)S(1)}, bf16[192,128]{1,0:T(8,128)(2,1)S(1)}, u32[]{:S(2)}, u32[]{:S(2)}) collective-permute-start(bf16[192,128]{1,0:T(8,128)(2,1)S(1)} %get-tuple-element.64.refs_0_), channel_id=1, source_target_pairs={{0,4},{2,6},{4,0},{6,2},{8,12},{10,14},{12,8},{14,10},{16,20},{18,... | collective-permute-start | bytes 147464 | tf_op jit(solution)/shard_map/ppermute | solution.py:61
  10.0 0.2 collective-permute-done.1.refs_0_.refs_2_
  10.2 4.1 %collective-permute-done.2.refs_1_.refs_3_ = bf16[192,128]{1,0:T(8,128)(2,1)S(1)} collective-permute-done((bf16[192,128]{1,0:T(8,128)(2,1)S(1)}, bf16[192,128]{1,0:T(8,128)(2,1)S(1)}, u32[]{:S(2)}, u32[]{:S(2)}) %collective-permute-start.2) | collective-permute-done | bytes 49184 | tf_op jit(solution)/shard_map/ppermute | solution.py:57
  14.3 1.6 %collective-permute-start.3 = (bf16[384,128]{1,0:T(8,128)(2,1)S(1)}, bf16[384,128]{1,0:T(8,128)(2,1)S(1)}, u32[]{:S(2)}, u32[]{:S(2)}) collective-permute-start(bf16[384,128]{1,0:T(8,128)(2,1)S(1)} %shard_map.95), channel_id=1, source_target_pairs={{0,4},{2,6},{4,0},{6,2},{8,12},{10,14},{12,8},{14,10},{16,20},{18,... | collective-permute-start | bytes 294920 | tf_op jit(solution)/shard_map/ppermute | solution.py:61
  15.9 0.7 %pad_add_fusion.tables_in.refs_2_ = s32[16,16]{1,0:T(8,128)S(1)} fusion(s32[4,16]{1,0:T(4,128)} %bitcast.17, s32[4,16]{1,0:T(4,128)} %bitcast.18, s32[4,16]{1,0:T(4,128)} %bitcast.19, s32[4,16]{1,0:T(4,128)} %bitcast.20), kind=kLoop, calls=%fused_computation | loop fusion | flops 768 | bytes 2048 | tf_op jit(solution)/shard_map/concatenate | solution.py:603
  16.7 1.0 %copy-done.1 = bf16[1,32,32,192]{3,2,1,0:T(8,128)(2,1)S(1)} copy-done((bf16[1,32,32,192]{3,2,1,0:T(8,128)(2,1)S(1)}, bf16[1,32,32,192]{3,2,1,0:T(8,128)(2,1)}, u32[]{:S(2)}) %copy-start.1) | copy-done | bytes 393240
  17.7 1.0 %shard_map.96 = (bf16[512,1536]{1,0:T(8,128)(2,1)S(1)}, bf16[1024,192]{1,0:T(8,128)(2,1)S(1)}) custom-call(s32[16,16]{1,0:T(8,128)S(1)} %pad_add_fusion.tables_in.refs_2_, bf16[1024,192]{1,0:T(8,128)(2,1)S(1)} %bitcast.12), custom_call_target="tpu_custom_call" | custom-call | bytes 2360320 | tf_op jit(solution)/shard_map/pallas_call | solution.py:108
  18.8 0.3 collective-permute-done.3.refs_4_
  19.0 2.5 %shard_map.98 = (f32[448,384]{1,0:T(8,128)S(1)}, f32[448,384]{1,0:T(8,128)S(1)}, bf16[1024,384]{1,0:T(8,128)(2,1)S(1)}, bf16[128,384]{1,0:T(8,128)(2,1)S(1)}, bf16[3,1088,192]{2,1,0:T(8,128)(2,1)S(1)}) custom-call(bf16[32,32,192]{2,1,0:T(8,128)(2,1)S(1)} %get-tuple-element.69.field_ref.refs_3_, bf16[1024,192]{1,0:T(8,128)(2,1)S(1)} %get-tuple-element.70.own_ref, ...), custom_call_target="tpu_custom_call" | custom-call | flops 679477248 | bytes 4694016 | tf_op jit(solution)/shard_map/pallas_call | solution.py:108
  21.6 0.1 collective-permute-start.7
  21.6 0.5 collective-permute-start.8
  22.1 0.1 collective-permute-start.5
  22.3 0.4 collective-permute-start.6
  22.7 1.3 %shard_map.99.refs_3_ = f32[896,384]{1,0:T(8,128)S(1)} custom-call(bf16[3,1088,192]{2,1,0:T(8,128)(2,1)S(1)} %get-tuple-element.72.cols, bf16[1024,384]{1,0:T(8,128)(2,1)S(1)} %get-tuple-element.88.cot_ref), custom_call_target="tpu_custom_call" | custom-call | flops 679477248 | bytes 3416064 | tf_op jit(solution)/shard_map/pallas_call | solution.py:108
  24.1 0.0 copy-start.2
  24.1 1.2 %collective-permute-done.6.refs_5_ = bf16[128,384]{1,0:T(8,128)(2,1)S(1)} collective-permute-done((bf16[128,384]{1,0:T(8,128)(2,1)S(1)}, bf16[128,384]{1,0:T(8,128)(2,1)S(1)}, u32[]{:S(2)}, u32[]{:S(2)}) %collective-permute-start.6) | collective-permute-done | bytes 98336 | tf_op jit(solution)/shard_map/ppermute | solution.py:61
  25.3 1.5 %shard_map.100 = (f32[224,384]{1,0:T(8,128)S(1)}, bf16[224,384]{1,0:T(8,128)(2,1)S(1)}, bf16[224,384]{1,0:T(8,128)(2,1)S(1)}, bf16[224,384]{1,0:T(8,128)(2,1)S(1)}) custom-call(bf16[1152,128]{1,0:T(8,128)(2,1)S(1)} %shard_map.97.refs_0_, bf16[1152,128]{1,0:T(8,128)(2,1)S(1)} %collective-permute-done.5.refs_1_, ...), custom_call_target="tpu_custom_call" | custom-call | bytes 5971968 | tf_op jit(solution)/shard_map/pallas_call | solution.py:108
  26.9 0.1 collective-permute-start.10
  26.9 3.0 %collective-permute-start.11 = (bf16[224,384]{1,0:T(8,128)(2,1)S(1)}, bf16[224,384]{1,0:T(8,128)(2,1)S(1)}, u32[]{:S(2)}, u32[]{:S(2)}) collective-permute-start(bf16[224,384]{1,0:T(8,128)(2,1)S(1)} %get-tuple-element.87), channel_id=1, source_target_pairs={{0,12},{2,14},{4,8},{6,10},{8,4},{10,6},{12,0},{14,2},{16,28},{18,... | collective-permute-start | bytes 516104 | tf_op jit(solution)/shard_map/ppermute | solution.py:61
  29.9 0.5 collective-permute-start.9
  30.4 2.9 %shard_map.101 = (f32[1024,192]{1,0:T(8,128)S(1)}, bf16[216,128]{1,0:T(8,128)(2,1)S(1)}) custom-call(bf16[1024,384]{1,0:T(8,128)(2,1)S(1)} %get-tuple-element.88.cot_ref, bf16[9,384,384]{2,1,0:T(8,128)(2,1)S(1)} %bitcast.13), custom_call_target="tpu_custom_call" | custom-call | flops 1358954496 | bytes 4282368 | tf_op jit(solution)/shard_map/pallas_call | solution.py:108
  33.3 0.6 collective-permute-start.12
  33.9 1.4 %collective-permute-start.13 = (bf16[216,128]{1,0:T(8,128)(2,1)S(1)}, bf16[216,128]{1,0:T(8,128)(2,1)S(1)}, u32[]{:S(2)}, u32[]{:S(2)}) collective-permute-start(bf16[216,128]{1,0:T(8,128)(2,1)S(1)} %get-tuple-element.105.refs_0_), channel_id=1, source_target_pairs={{0,8},{2,10},{4,12},{6,14},{8,16},{10,18},{12,20},{14,22},{16,24},... | collective-permute-start | bytes 165896 | tf_op jit(solution)/shard_map/ppermute | solution.py:57
  35.3 1.2 %shard_map.102 = (bf16[144,192]{1,0:T(8,128)(2,1)S(1)}, bf16[1752,128]{1,0:T(8,128)(2,1)S(1)}) custom-call(bf16[1152,128]{1,0:T(8,128)(2,1)S(1)} %shard_map.97.refs_0_, bf16[1152,128]{1,0:T(8,128)(2,1)S(1)} %collective-permute-done.5.refs_1_, s32[16,16]{1,0:T(8,128)S(1)} %pad_add_fusion.tables_in.refs_2_, ...), custom_call_target="tpu_custom_call" | custom-call | bytes 1487872 | tf_op jit(solution)/shard_map/pallas_call | solution.py:108
  36.6 2.3 %collective-permute-done.12.refs_1_ = bf16[216,128]{1,0:T(8,128)(2,1)S(1)} collective-permute-done((bf16[216,128]{1,0:T(8,128)(2,1)S(1)}, bf16[216,128]{1,0:T(8,128)(2,1)S(1)}, u32[]{:S(2)}, u32[]{:S(2)}) %collective-permute-start.12) | collective-permute-done | bytes 55328 | tf_op jit(solution)/shard_map/ppermute | solution.py:57
  38.9 1.0 %collective-permute-done.13.refs_2_ = bf16[216,128]{1,0:T(8,128)(2,1)S(1)} collective-permute-done((bf16[216,128]{1,0:T(8,128)(2,1)S(1)}, bf16[216,128]{1,0:T(8,128)(2,1)S(1)}, u32[]{:S(2)}, u32[]{:S(2)}) %collective-permute-start.13) | collective-permute-done | bytes 55328 | tf_op jit(solution)/shard_map/ppermute | solution.py:57
  39.9 0.1 shard_map.103
  40.0 1.6 %collective-permute-start.22 = (bf16[1752,128]{1,0:T(8,128)(2,1)S(1)}, bf16[1752,128]{1,0:T(8,128)(2,1)S(1)}, u32[]{:S(2)}, u32[]{:S(2)}) collective-permute-start(bf16[1752,128]{1,0:T(8,128)(2,1)S(1)} %get-tuple-element.115), channel_id=1, source_target_pairs={{0,1},{1,0},{2,3},{3,2},{4,5},{5,4},{6,7},{7,6},{8,9},{9,8},{10,11... | collective-permute-start | bytes 1345544 | tf_op jit(solution)/shard_map/ppermute | solution.py:686
  41.5 1.6 %collective-permute-start.16 = (bf16[648,128]{1,0:T(8,128)(2,1)S(1)}, bf16[648,128]{1,0:T(8,128)(2,1)S(1)}, u32[]{:S(2)}, u32[]{:S(2)}) collective-permute-start(bf16[648,128]{1,0:T(8,128)(2,1)S(1)} %shard_map.104.refs_0_), channel_id=1, source_target_pairs={{0,4},{2,6},{4,0},{6,2},{8,12},{10,14},{12,8},{14,10},{16,20},{18,... | collective-permute-start | bytes 497672 | tf_op jit(solution)/shard_map/ppermute | solution.py:61
  43.1 3.8 %collective-permute-done.14.refs_1_ = bf16[112,384]{1,0:T(8,128)(2,1)S(1)} collective-permute-done((bf16[112,384]{1,0:T(8,128)(2,1)S(1)}, bf16[112,384]{1,0:T(8,128)(2,1)S(1)}, u32[]{:S(2)}, u32[]{:S(2)}) %collective-permute-start.14) | collective-permute-done | bytes 86048 | tf_op jit(solution)/shard_map/ppermute | solution.py:61
  46.9 0.2 collective-permute-start.15
  47.1 5.3 %collective-permute-done.15.refs_1_ = bf16[112,384]{1,0:T(8,128)(2,1)S(1)} collective-permute-done((bf16[112,384]{1,0:T(8,128)(2,1)S(1)}, bf16[112,384]{1,0:T(8,128)(2,1)S(1)}, u32[]{:S(2)}, u32[]{:S(2)}) %collective-permute-start.15) | collective-permute-done | bytes 86048 | tf_op jit(solution)/shard_map/ppermute | solution.py:61
  52.4 1.2 %shard_map.107.place_ref = bf16[128,1728]{1,0:T(8,128)(2,1)S(1)} custom-call(s32[16,16]{1,0:T(8,128)S(1)} %pad_add_fusion.tables_in.refs_2_), custom_call_target="tpu_custom_call" | custom-call | bytes 443392 | tf_op jit(solution)/shard_map/pallas_call | solution.py:108
  53.6 1.6 %collective-permute-start.17 = (bf16[224,384]{1,0:T(8,128)(2,1)S(1)}, bf16[224,384]{1,0:T(8,128)(2,1)S(1)}, u32[]{:S(2)}, u32[]{:S(2)}) collective-permute-start(bf16[224,384]{1,0:T(8,128)(2,1)S(1)} %shard_map.106.refs_0_), channel_id=1, source_target_pairs={{0,4},{2,6},{4,0},{6,2},{8,12},{10,14},{12,8},{14,10},{16,20},{18,... | collective-permute-start | bytes 516104 | tf_op jit(solution)/shard_map/ppermute | solution.py:61
  55.2 2.0 %collective-permute-start.19 = (bf16[224,384]{1,0:T(8,128)(2,1)S(1)}, bf16[224,384]{1,0:T(8,128)(2,1)S(1)}, u32[]{:S(2)}, u32[]{:S(2)}) collective-permute-start(bf16[224,384]{1,0:T(8,128)(2,1)S(1)} %shard_map.106.refs_0_), channel_id=1, source_target_pairs={{0,12},{2,14},{4,8},{6,10},{8,4},{10,6},{12,0},{14,2},{16,28},{18,... | collective-permute-start | bytes 516104 | tf_op jit(solution)/shard_map/ppermute | solution.py:61
  57.2 1.3 %shard_map.108 = bf16[1024,192]{1,0:T(8,128)(2,1)} custom-call(bf16[128,1728]{1,0:T(8,128)(2,1)S(1)} %shard_map.107.place_ref, f32[1024,192]{1,0:T(8,128)S(1)} %get-tuple-element.111.inner_ref, bf16[648,128]{1,0:T(8,128)(2,1)S(1)} %shard_map.104.refs_0_, bf16[648,128]{1,0:T(8,128)(2,1)S(1)} %collective-permute-done.16.refs_1_, ...), custom_call_target="tpu_custom_call" | custom-call | bytes 2285568 | tf_op jit(solution)/shard_map/pallas_call | solution.py:108
  58.5 3.9 %shard_map.109 = bf16[1024,192]{1,0:T(8,128)(2,1)} custom-call(bf16[32,32,192]{2,1,0:T(8,128)(2,1)S(1)} %get-tuple-element.69.field_ref.refs_3_, bf16[144,192]{1,0:T(8,128)(2,1)S(1)} %get-tuple-element.114.halos_ref, bf16[1752,128]{1,0:T(8,128)(2,1)S(1)} %collective-permute-done.22.other_ref, bf16[9,384,384]{2,1,0:T(8,128)(2,1)S(1)} %bitcast.14), custom_call_target="tpu_custom_call" | custom-call | flops 2717908992 | bytes 3944448 | tf_op jit(solution)/shard_map/pallas_call | solution.py:108
  62.4 0.0 collective-permute-done.18.refs_2_
  62.4 2.9 %collective-permute-done.19.refs_1_ = bf16[224,384]{1,0:T(8,128)(2,1)S(1)} collective-permute-done((bf16[224,384]{1,0:T(8,128)(2,1)S(1)}, bf16[224,384]{1,0:T(8,128)(2,1)S(1)}, u32[]{:S(2)}, u32[]{:S(2)}) %collective-permute-start.19) | collective-permute-done | bytes 172064 | tf_op jit(solution)/shard_map/ppermute | solution.py:61
  65.3 0.5 collective-permute-start.25
  65.8 0.9 %collective-permute-done.24.refs_4_ = bf16[224,384]{1,0:T(8,128)(2,1)S(1)} collective-permute-done((bf16[224,384]{1,0:T(8,128)(2,1)S(1)}, bf16[224,384]{1,0:T(8,128)(2,1)S(1)}, u32[]{:S(2)}, u32[]{:S(2)}) %collective-permute-start.24) | collective-permute-done | bytes 172064 | tf_op jit(solution)/shard_map/ppermute | solution.py:61
  66.7 0.2 collective-permute-done.25.refs_5_
  67.0 1.5 %shard_map.110.refs_0_ = f32[1728,384]{1,0:T(8,128)} custom-call(bf16[224,384]{1,0:T(8,128)(2,1)S(1)} %shard_map.106.refs_0_, bf16[224,384]{1,0:T(8,128)(2,1)S(1)} %collective-permute-done.17.refs_1_, bf16[224,384]{1,0:T(8,128)(2,1)S(1)} %collective-permute-done.18.refs_2_, bf16[224,384]{1,0:T(8,128)(2,1)S(1)} %collective-permute-done.23.refs_3_, ...), custom_call_target="tpu_custom_call" | custom-call | tf_op jit(solution)/shard_map/pallas_call | solution.py:445
  68.5 0.9 %shard_map.111 = f32[1728,384]{1,0:T(8,128)} custom-call(f32[1728,384]{1,0:T(8,128)} %shard_map.110.refs_0_, bf16[224,384]{1,0:T(8,128)(2,1)S(1)} %collective-permute-done.19.refs_1_, bf16[224,384]{1,0:T(8,128)(2,1)S(1)} %collective-permute-done.26.refs_2_), custom_call_target="tpu_custom_call", output_to_operand_aliasing={{}: (0, {})} | custom-call | tf_op jit(solution)/shard_map/pallas_call | solution.py:445
  (31 shorter events, 0.1 us)
Async XLA Ops:
  0.6 18.4 %collective-permute-start.4 = (bf16[1024,192]{1,0:T(8,128)(2,1)}, bf16[1024,192]{1,0:T(8,128)(2,1)S(1)}, u32[]{:S(2)}, u32[]{:S(2)}) collective-permute-start(bf16[1024,192]{1,0:T(8,128)(2,1)} %bitcast.11), channel_id=1, source_target_pairs={{0,1},{1,0},{2,3},{3,2},{4,5},{5,4},{6,7},{7,6},{8,9},{9,8},{10,11... | collective-permute-start | bytes 1179656 | tf_op jit(solution)/shard_map/ppermute | solution.py:595
  3.6 1.0 %copy-start = (bf16[1,32,32,192]{3,2,1,0:T(8,128)(2,1)S(1)}, bf16[1,32,32,192]{3,2,1,0:T(8,128)(2,1)}, u32[]{:S(2)}) copy-start(bf16[1,32,32,192]{3,2,1,0:T(8,128)(2,1)} %param.7) | copy-start | bytes 1179652
  4.8 5.4 %collective-permute-start.1 = (bf16[192,128]{1,0:T(8,128)(2,1)S(1)}, bf16[192,128]{1,0:T(8,128)(2,1)S(1)}, u32[]{:S(2)}, u32[]{:S(2)}) collective-permute-start(bf16[192,128]{1,0:T(8,128)(2,1)S(1)} %get-tuple-element.64.refs_0_), channel_id=1, source_target_pairs={{0,24},{2,26},{4,28},{6,30},{8,0},{10,2},{12,4},{14,6},{16,8},{18,... | collective-permute-start | bytes 147464 | tf_op jit(solution)/shard_map/ppermute | solution.py:57
  8.4 5.9 %collective-permute-start.2 = (bf16[192,128]{1,0:T(8,128)(2,1)S(1)}, bf16[192,128]{1,0:T(8,128)(2,1)S(1)}, u32[]{:S(2)}, u32[]{:S(2)}) collective-permute-start(bf16[192,128]{1,0:T(8,128)(2,1)S(1)} %get-tuple-element.64.refs_0_), channel_id=1, source_target_pairs={{0,8},{2,10},{4,12},{6,14},{8,16},{10,18},{12,20},{14,22},{16,24},... | collective-permute-start | bytes 147464 | tf_op jit(solution)/shard_map/ppermute | solution.py:57
  8.4 10.3 %collective-permute-start = (bf16[192,128]{1,0:T(8,128)(2,1)S(1)}, bf16[192,128]{1,0:T(8,128)(2,1)S(1)}, u32[]{:S(2)}, u32[]{:S(2)}) collective-permute-start(bf16[192,128]{1,0:T(8,128)(2,1)S(1)} %get-tuple-element.64.refs_0_), channel_id=1, source_target_pairs={{0,4},{2,6},{4,0},{6,2},{8,12},{10,14},{12,8},{14,10},{16,20},{18,... | collective-permute-start | bytes 147464 | tf_op jit(solution)/shard_map/ppermute | solution.py:61
  14.3 4.7 %collective-permute-start.3 = (bf16[384,128]{1,0:T(8,128)(2,1)S(1)}, bf16[384,128]{1,0:T(8,128)(2,1)S(1)}, u32[]{:S(2)}, u32[]{:S(2)}) collective-permute-start(bf16[384,128]{1,0:T(8,128)(2,1)S(1)} %shard_map.95), channel_id=1, source_target_pairs={{0,4},{2,6},{4,0},{6,2},{8,12},{10,14},{12,8},{14,10},{16,20},{18,... | collective-permute-start | bytes 294920 | tf_op jit(solution)/shard_map/ppermute | solution.py:61
  16.7 1.0 %copy-start.1 = (bf16[1,32,32,192]{3,2,1,0:T(8,128)(2,1)S(1)}, bf16[1,32,32,192]{3,2,1,0:T(8,128)(2,1)}, u32[]{:S(2)}) copy-start(bf16[1,32,32,192]{3,2,1,0:T(8,128)(2,1)} %param.9) | copy-start | bytes 1179652
  21.6 3.8 %collective-permute-start.7 = (f32[448,384]{1,0:T(8,128)S(1)}, f32[448,384]{1,0:T(8,128)S(1)}, u32[]{:S(2)}, u32[]{:S(2)}) collective-permute-start(f32[448,384]{1,0:T(8,128)S(1)} %get-tuple-element.79), channel_id=1, source_target_pairs={{0,2},{2,0},{4,6},{6,4},{8,10},{10,8},{12,14},{14,12},{16,18},{18,... | collective-permute-start | bytes 2064392 | tf_op jit(solution)/shard_map/ppermute | solution.py:61
  21.6 3.7 %collective-permute-start.8 = (f32[448,384]{1,0:T(8,128)S(1)}, f32[448,384]{1,0:T(8,128)S(1)}, u32[]{:S(2)}, u32[]{:S(2)}) collective-permute-start(f32[448,384]{1,0:T(8,128)S(1)} %get-tuple-element.80), channel_id=1, source_target_pairs={{0,2},{2,0},{4,6},{6,4},{8,10},{10,8},{12,14},{14,12},{16,18},{18,... | collective-permute-start | bytes 2064392 | tf_op jit(solution)/shard_map/ppermute | solution.py:61
  22.1 3.2 %collective-permute-start.5 = (bf16[1152,128]{1,0:T(8,128)(2,1)S(1)}, bf16[1152,128]{1,0:T(8,128)(2,1)S(1)}, u32[]{:S(2)}, u32[]{:S(2)}) collective-permute-start(bf16[1152,128]{1,0:T(8,128)(2,1)S(1)} %shard_map.97.refs_0_), channel_id=1, source_target_pairs={{0,2},{2,0},{4,6},{6,4},{8,10},{10,8},{12,14},{14,12},{16,18},{18,... | collective-permute-start | bytes 884744 | tf_op jit(solution)/shard_map/ppermute | solution.py:61
  22.3 3.0 %collective-permute-start.6 = (bf16[128,384]{1,0:T(8,128)(2,1)S(1)}, bf16[128,384]{1,0:T(8,128)(2,1)S(1)}, u32[]{:S(2)}, u32[]{:S(2)}) collective-permute-start(bf16[128,384]{1,0:T(8,128)(2,1)S(1)} %get-tuple-element.74.refs_4_), channel_id=1, source_target_pairs={{0,2},{2,0},{4,6},{6,4},{8,10},{10,8},{12,14},{14,12},{16,18},{18,... | collective-permute-start | bytes 294920 | tf_op jit(solution)/shard_map/ppermute | solution.py:61
  24.1 6.4 %copy-start.2 = (bf16[3,3,384,384]{3,2,1,0:T(8,128)(2,1)S(1)}, bf16[3,3,384,384]{3,2,1,0:T(8,128)(2,1)}, u32[]{:S(2)}) copy-start(bf16[3,3,384,384]{3,2,1,0:T(8,128)(2,1)} %param.8) | copy-start | bytes 7962628
  26.9 13.0 %collective-permute-start.10 = (bf16[224,384]{1,0:T(8,128)(2,1)S(1)}, bf16[224,384]{1,0:T(8,128)(2,1)S(1)}, u32[]{:S(2)}, u32[]{:S(2)}) collective-permute-start(bf16[224,384]{1,0:T(8,128)(2,1)S(1)} %get-tuple-element.86), channel_id=1, source_target_pairs={{0,8},{2,10},{4,12},{6,14},{8,0},{10,2},{12,4},{14,6},{16,24},{18,... | collective-permute-start | bytes 516104 | tf_op jit(solution)/shard_map/ppermute | solution.py:61
  26.9 12.9 %collective-permute-start.11 = (bf16[224,384]{1,0:T(8,128)(2,1)S(1)}, bf16[224,384]{1,0:T(8,128)(2,1)S(1)}, u32[]{:S(2)}, u32[]{:S(2)}) collective-permute-start(bf16[224,384]{1,0:T(8,128)(2,1)S(1)} %get-tuple-element.87), channel_id=1, source_target_pairs={{0,12},{2,14},{4,8},{6,10},{8,4},{10,6},{12,0},{14,2},{16,28},{18,... | collective-permute-start | bytes 516104 | tf_op jit(solution)/shard_map/ppermute | solution.py:61
  29.9 10.0 %collective-permute-start.9 = (bf16[224,384]{1,0:T(8,128)(2,1)S(1)}, bf16[224,384]{1,0:T(8,128)(2,1)S(1)}, u32[]{:S(2)}, u32[]{:S(2)}) collective-permute-start(bf16[224,384]{1,0:T(8,128)(2,1)S(1)} %get-tuple-element.85), channel_id=1, source_target_pairs={{0,4},{2,6},{4,0},{6,2},{8,12},{10,14},{12,8},{14,10},{16,20},{18,... | collective-permute-start | bytes 516104 | tf_op jit(solution)/shard_map/ppermute | solution.py:61
  33.3 5.6 %collective-permute-start.12 = (bf16[216,128]{1,0:T(8,128)(2,1)S(1)}, bf16[216,128]{1,0:T(8,128)(2,1)S(1)}, u32[]{:S(2)}, u32[]{:S(2)}) collective-permute-start(bf16[216,128]{1,0:T(8,128)(2,1)S(1)} %get-tuple-element.105.refs_0_), channel_id=1, source_target_pairs={{0,24},{2,26},{4,28},{6,30},{8,0},{10,2},{12,4},{14,6},{16,8},{18,... | collective-permute-start | bytes 165896 | tf_op jit(solution)/shard_map/ppermute | solution.py:57
  33.9 6.0 %collective-permute-start.13 = (bf16[216,128]{1,0:T(8,128)(2,1)S(1)}, bf16[216,128]{1,0:T(8,128)(2,1)S(1)}, u32[]{:S(2)}, u32[]{:S(2)}) collective-permute-start(bf16[216,128]{1,0:T(8,128)(2,1)S(1)} %get-tuple-element.105.refs_0_), channel_id=1, source_target_pairs={{0,8},{2,10},{4,12},{6,14},{8,16},{10,18},{12,20},{14,22},{16,24},... | collective-permute-start | bytes 165896 | tf_op jit(solution)/shard_map/ppermute | solution.py:57
  40.0 18.5 %collective-permute-start.22 = (bf16[1752,128]{1,0:T(8,128)(2,1)S(1)}, bf16[1752,128]{1,0:T(8,128)(2,1)S(1)}, u32[]{:S(2)}, u32[]{:S(2)}) collective-permute-start(bf16[1752,128]{1,0:T(8,128)(2,1)S(1)} %get-tuple-element.115), channel_id=1, source_target_pairs={{0,1},{1,0},{2,3},{3,2},{4,5},{5,4},{6,7},{7,6},{8,9},{9,8},{10,11... | collective-permute-start | bytes 1345544 | tf_op jit(solution)/shard_map/ppermute | solution.py:686
  41.5 5.4 %collective-permute-start.14 = (bf16[112,384]{1,0:T(8,128)(2,1)S(1)}, bf16[112,384]{1,0:T(8,128)(2,1)S(1)}, u32[]{:S(2)}, u32[]{:S(2)}) collective-permute-start(bf16[112,384]{1,0:T(8,128)(2,1)S(1)} %get-tuple-element.104), channel_id=1, source_target_pairs={{0,16},{2,18},{4,20},{6,22},{8,24},{10,26},{12,28},{14,30},{16,0},... | collective-permute-start | bytes 258056 | tf_op jit(solution)/shard_map/ppermute | solution.py:61
  41.5 5.6 %collective-permute-start.16 = (bf16[648,128]{1,0:T(8,128)(2,1)S(1)}, bf16[648,128]{1,0:T(8,128)(2,1)S(1)}, u32[]{:S(2)}, u32[]{:S(2)}) collective-permute-start(bf16[648,128]{1,0:T(8,128)(2,1)S(1)} %shard_map.104.refs_0_), channel_id=1, source_target_pairs={{0,4},{2,6},{4,0},{6,2},{8,12},{10,14},{12,8},{14,10},{16,20},{18,... | collective-permute-start | bytes 497672 | tf_op jit(solution)/shard_map/ppermute | solution.py:61
  46.9 5.4 %collective-permute-start.15 = (bf16[112,384]{1,0:T(8,128)(2,1)S(1)}, bf16[112,384]{1,0:T(8,128)(2,1)S(1)}, u32[]{:S(2)}, u32[]{:S(2)}) collective-permute-start(bf16[112,384]{1,0:T(8,128)(2,1)S(1)} %shard_map.105.refs_0_), channel_id=1, source_target_pairs={{0,16},{2,18},{4,20},{6,22},{8,24},{10,26},{12,28},{14,30},{16,0},... | collective-permute-start | bytes 258056 | tf_op jit(solution)/shard_map/ppermute | solution.py:61
  47.1 8.1 %collective-permute-start.20 = (bf16[648,128]{1,0:T(8,128)(2,1)S(1)}, bf16[648,128]{1,0:T(8,128)(2,1)S(1)}, u32[]{:S(2)}, u32[]{:S(2)}) collective-permute-start(bf16[648,128]{1,0:T(8,128)(2,1)S(1)} %shard_map.104.refs_0_), channel_id=1, source_target_pairs={{0,2},{2,0},{4,6},{6,4},{8,10},{10,8},{12,14},{14,12},{16,18},{18,... | collective-permute-start | bytes 497672 | tf_op jit(solution)/shard_map/ppermute | solution.py:61
  52.4 4.8 %collective-permute-start.21 = (bf16[648,128]{1,0:T(8,128)(2,1)S(1)}, bf16[648,128]{1,0:T(8,128)(2,1)S(1)}, u32[]{:S(2)}, u32[]{:S(2)}) collective-permute-start(bf16[648,128]{1,0:T(8,128)(2,1)S(1)} %collective-permute-done.16.refs_1_), channel_id=1, source_target_pairs={{0,2},{2,0},{4,6},{6,4},{8,10},{10,8},{12,14},{14,12},{16,18},{18,... | collective-permute-start | bytes 497672 | tf_op jit(solution)/shard_map/ppermute | solution.py:61
  53.6 8.8 %collective-permute-start.17 = (bf16[224,384]{1,0:T(8,128)(2,1)S(1)}, bf16[224,384]{1,0:T(8,128)(2,1)S(1)}, u32[]{:S(2)}, u32[]{:S(2)}) collective-permute-start(bf16[224,384]{1,0:T(8,128)(2,1)S(1)} %shard_map.106.refs_0_), channel_id=1, source_target_pairs={{0,4},{2,6},{4,0},{6,2},{8,12},{10,14},{12,8},{14,10},{16,20},{18,... | collective-permute-start | bytes 516104 | tf_op jit(solution)/shard_map/ppermute | solution.py:61
  55.2 7.2 %collective-permute-start.18 = (bf16[224,384]{1,0:T(8,128)(2,1)S(1)}, bf16[224,384]{1,0:T(8,128)(2,1)S(1)}, u32[]{:S(2)}, u32[]{:S(2)}) collective-permute-start(bf16[224,384]{1,0:T(8,128)(2,1)S(1)} %shard_map.106.refs_0_), channel_id=1, source_target_pairs={{0,8},{2,10},{4,12},{6,14},{8,0},{10,2},{12,4},{14,6},{16,24},{18,... | collective-permute-start | bytes 516104 | tf_op jit(solution)/shard_map/ppermute | solution.py:61
  55.2 10.1 %collective-permute-start.19 = (bf16[224,384]{1,0:T(8,128)(2,1)S(1)}, bf16[224,384]{1,0:T(8,128)(2,1)S(1)}, u32[]{:S(2)}, u32[]{:S(2)}) collective-permute-start(bf16[224,384]{1,0:T(8,128)(2,1)S(1)} %shard_map.106.refs_0_), channel_id=1, source_target_pairs={{0,12},{2,14},{4,8},{6,10},{8,4},{10,6},{12,0},{14,2},{16,28},{18,... | collective-permute-start | bytes 516104 | tf_op jit(solution)/shard_map/ppermute | solution.py:61
  57.2 8.7 %collective-permute-start.23 = (bf16[224,384]{1,0:T(8,128)(2,1)S(1)}, bf16[224,384]{1,0:T(8,128)(2,1)S(1)}, u32[]{:S(2)}, u32[]{:S(2)}) collective-permute-start(bf16[224,384]{1,0:T(8,128)(2,1)S(1)} %shard_map.106.refs_0_), channel_id=1, source_target_pairs={{0,2},{2,0},{4,6},{6,4},{8,10},{10,8},{12,14},{14,12},{16,18},{18,... | collective-permute-start | bytes 516104 | tf_op jit(solution)/shard_map/ppermute | solution.py:61
  65.3 1.4 %collective-permute-start.24 = (bf16[224,384]{1,0:T(8,128)(2,1)S(1)}, bf16[224,384]{1,0:T(8,128)(2,1)S(1)}, u32[]{:S(2)}, u32[]{:S(2)}) collective-permute-start(bf16[224,384]{1,0:T(8,128)(2,1)S(1)} %collective-permute-done.17.refs_1_), channel_id=1, source_target_pairs={{0,2},{2,0},{4,6},{6,4},{8,10},{10,8},{12,14},{14,12},{16,18},{18,... | collective-permute-start | bytes 516104 | tf_op jit(solution)/shard_map/ppermute | solution.py:61
  65.3 1.6 %collective-permute-start.25 = (bf16[224,384]{1,0:T(8,128)(2,1)S(1)}, bf16[224,384]{1,0:T(8,128)(2,1)S(1)}, u32[]{:S(2)}, u32[]{:S(2)}) collective-permute-start(bf16[224,384]{1,0:T(8,128)(2,1)S(1)} %collective-permute-done.18.refs_2_), channel_id=1, source_target_pairs={{0,2},{2,0},{4,6},{6,4},{8,10},{10,8},{12,14},{14,12},{16,18},{18,... | collective-permute-start | bytes 516104 | tf_op jit(solution)/shard_map/ppermute | solution.py:61
  65.8 2.7 %collective-permute-start.26 = (bf16[224,384]{1,0:T(8,128)(2,1)S(1)}, bf16[224,384]{1,0:T(8,128)(2,1)S(1)}, u32[]{:S(2)}, u32[]{:S(2)}) collective-permute-start(bf16[224,384]{1,0:T(8,128)(2,1)S(1)} %collective-permute-done.19.refs_1_), channel_id=1, source_target_pairs={{0,2},{2,0},{4,6},{6,4},{8,10},{10,8},{12,14},{14,12},{16,18},{18,... | collective-permute-start | bytes 516104 | tf_op jit(solution)/shard_map/ppermute | solution.py:61

commit v9 on v8

--- a/solution.py
+++ b/solution.py
@@ -53,8 +53,11 @@
     return [sum(int(slot) << (3 * quarter) for quarter, slot in enumerate(row)) for row in tables]
 
 
-def by_offset(value, offset, count):
-    return lax.ppermute(value, "tile", [(i, (i + offset) % count) for i in range(count)])
+def by_swap(value, odd, count):
+    pairs = [
+        (i, (i + (SPAN if (i // SPAN) % 2 == odd else -SPAN)) % count) for i in range(count)
+    ]
+    return lax.ppermute(value, "tile", pairs)
 
 
 def by_mask(value, mask, count):
@@ -187,7 +190,8 @@
         slab = lax.rem(source // SPAN - self.own // SPAN + groups, groups)
         cross = source ^ self.own
         turn = lax.rem(cross // 2, 2)
-        at = jnp.where(slab == 0, turn, jnp.where(slab == 1, 2, 3) + 2 * turn)
+        even = lax.rem(self.own // SPAN, 2) == 0
+        at = jnp.where(slab == 0, turn, jnp.where((slab == 1) == even, 2, 3) + 2 * turn)
         return 6 * lax.rem(cross, 2) + at
 
     def edge(self, tile, e):
@@ -254,8 +258,9 @@
     lane = lax.broadcasted_iota(jnp.int32, (1, block), 1)
     row = lax.broadcasted_iota(jnp.int32, (4 * side, block), 0)
     places = []
+    swap = jnp.where(lax.rem(near.own // SPAN, 2) == 0, SPAN, -SPAN)
     for mask in (0, 2, 1, 3):
-        for offset in (0, SPAN, -SPAN):
+        for offset in (0, swap, -swap):
             source = lax.rem((near.own ^ mask) + offset + near.count, near.count)
             target = jnp.full((1, block), -1, jnp.int32)
             for e in range(4):
@@ -598,7 +603,7 @@
         [vmem(packed_shape(4 * side, part), half_bytes), vmem(field.shape, half_bytes)],
         [field],
     )
-    ahead, behind = by_offset(sides, -SPAN, count), by_offset(sides, SPAN, count)
+    swaps = [by_swap(sides, odd, count) for odd in (0, 1)]
     across = by_mask(sides, 2, count)
     tables = jnp.concatenate([edge_tiles.T, edge_turns.T, corner_tiles.T, corner_turns.T], axis=0)
     table_scratch = [pltpu.SMEM(tables.shape, jnp.int32), pltpu.SemaphoreType.DMA]
@@ -609,8 +614,8 @@
         scratch=table_scratch,
     )
     pair = packed_shape(8 * side, part)
-    (beyond,) = call(join_kernel, [vmem(pair, half_bytes)], [ahead, behind])
-    near = [sides, across, ahead, behind, by_mask(beyond, 2, count)]
+    (beyond,) = call(join_kernel, [vmem(pair, half_bytes)], swaps)
+    near = [sides, across, *swaps, by_mask(beyond, 2, count)]
     near, cot_other, border_pick = lax.optimization_barrier((near, cot_other, border_pick))
     (near,) = call(join_kernel, [vmem(packed_shape(24 * side, part), half_bytes)], near)
     mates = by_mask(near, 1, count)
@@ -655,7 +660,8 @@
         scratch=[pltpu.VMEM((rows + 4 * side, chans), half_bytes)],
         flops=flops,
     )
-    here = [pieces, by_offset(pieces, -SPAN, count), by_offset(pieces, SPAN, count)]
+    pieces, near = lax.optimization_barrier((pieces, near))
+    here = [pieces, *[by_swap(pieces, odd, count) for odd in (0, 1)]]
     (place,) = call(
         functools.partial(place_kernel, side),
         [vmem((4 * side, 12 * block), half_bytes)],
@@ -668,7 +674,9 @@
         [*near, tables, field],
         scratch=[pltpu.VMEM((48 * side, part), half_bytes), *table_scratch],
     )
-    got, here, inner, halos, packet = lax.optimization_barrier((got, here, inner, halos, packet))
+    got, here, inner, halos, packet, place = lax.optimization_barrier(
+        (got, here, inner, halos, packet, place)
+    )
     for index, bits in enumerate(stages[2:]):
         masks = group_masks(bits)
         size = held.shape[0] // len(masks)
@@ -678,7 +686,7 @@
             [held, *got],
         )
         if index == 0:
-            send, here, packet = lax.optimization_barrier((send, here, packet))
+            send, here = lax.optimization_barrier((send, here))
         got = [by_mask(v, m, count) for v, m in zip(send, masks[1:])]
         if index == 0:
             (here,) = call(join_kernel, [vmem((3 * pieces.shape[0], pieces.shape[1]), half_bytes)], here)
@@ -721,10 +729,9 @@
         order = [[m + v for v in order] for m in masks]
     mates = [by_mask(v, 1, count) for v in got]
     whole = vmem((9 * part, chans), jnp.float32)
-    early = len(got) - 1
-    bits = [0] * early + [1] * early
-    first = unfold(whole, chunk, bits, order[:-1] + order[:-1], got[:-1] + mates[:-1], None)
-    grad_weight = unfold(whole, chunk, [0, 1], order[-1:] * 2, [got[-1], mates[-1]], first)
+    own = len(got)
+    first = unfold(whole, chunk, [0] * own + [1], order + order[:1], got + mates[:1], None)
+    grad_weight = unfold(whole, chunk, [1] * (own - 1), order[1:], mates[1:], first)
     shape = (1, side, side, part)
     return (
         output.reshape(shape),

time: 69.8 us -> 66.4 us (0.951)
  waiting for transfers between devices: 22.3 us -> 16.7 us
  starting transfers between devices: 23.9 us -> 26.1 us
    ppermute x4, waiting for transfers between devices: 7.63 us -> 3.52 us  [by_swap(): return lax.ppermute(value, 'tile', pairs)]
    ppermute x4, starting transfers between devices: 5.69 us -> 7.17 us  [by_swap(): return lax.ppermute(value, 'tile', pairs)]
    ppermute x21, waiting for transfers between devices: 14.7 us -> 13.2 us  [by_mask(): return lax.ppermute(value, 'tile', [(i, i ^ mask) for i in range(count)])]
    ppermute x21, starting transfers between devices: 13.6 us -> 14.3 us  [by_mask(): return lax.ppermute(value, 'tile', [(i, i ^ mask) for i in range(count)])]
  transfers between devices with their start and end apart: 27 -> 27, of which waited for: 11 -> 7; matrix products, arithmetic and copies ran while one was open for 1% -> 1% of each run, Pallas kernels for 21% -> 22%
where the time goes in v9:
time: 66.4 us; the launch traced here: 66.1 us
  starting transfers between devices  26.1 us (39%)
  Pallas kernels  19.7 us (30%)
  waiting for transfers between devices  16.7 us (25%)
  local copies, waits for them, and re-layouts  2.09 us (3%)
  between operations  0.78 us (1%)
  other arithmetic  0.74 us (1%)
    pallas_call x16, Pallas kernels, call(): pl.pallas_call(kernel, out_shape=tuple(outs), in_specs=in_specs, out_spec...  17.3 us
    ppermute x21, starting transfers between devices, by_mask(): return lax.ppermute(value, 'tile', [(i, i ^ mask) for i in range(count)])  14.3 us
    ppermute x21, waiting for transfers between devices, by_mask(): return lax.ppermute(value, 'tile', [(i, i ^ mask) for i in range(count)])  13.2 us
    ppermute x4, starting transfers between devices, by_swap(): return lax.ppermute(value, 'tile', pairs)  7.17 us
    ppermute x4, waiting for transfers between devices, by_swap(): return lax.ppermute(value, 'tile', pairs)  3.52 us
    ppermute x1, starting transfers between devices, body(): cot_other = lax.ppermute(cot_own, 'ch', others)  3 us
    pallas_call x2, Pallas kernels, unfold(): pl.pallas_call(functools.partial(unfold_kernel, whole.shape[0] // 2, chun...  2.41 us
    unnamed x6, local copies, waits for them, and re-layouts  2.09 us
  transfers between devices with their start and end apart: 27, of which 7 were waited for; matrix products, arithmetic and copies ran while one was open for 1% of the time, Pallas kernels for 22%

profile of v9, /device:TPU:0, one launch (start us, length us, event | category | flops | bytes accessed | tf_op | source)
XLA Modules:
  0.0 66.1 jit_solution(15154865021321224259)
XLA Ops:
  0.6 3.0 %collective-permute-start.4 = (bf16[1024,192]{1,0:T(8,128)(2,1)}, bf16[1024,192]{1,0:T(8,128)(2,1)S(1)}, u32[]{:S(2)}, u32[]{:S(2)}) collective-permute-start(bf16[1024,192]{1,0:T(8,128)(2,1)} %bitcast.11), channel_id=1, source_target_pairs={{0,1},{1,0},{2,3},{3,2},{4,5},{5,4},{6,7},{7,6},{8,9},{9,8},{10,11... | collective-permute-start | bytes 1179656 | tf_op jit(solution)/shard_map/ppermute | solution.py:600
  3.6 1.0 %copy-done = bf16[1,32,32,192]{3,2,1,0:T(8,128)(2,1)S(1)} copy-done((bf16[1,32,32,192]{3,2,1,0:T(8,128)(2,1)S(1)}, bf16[1,32,32,192]{3,2,1,0:T(8,128)(2,1)}, u32[]{:S(2)}) %copy-start) | copy-done | bytes 393240
  4.7 0.1 shard_map.94
  4.8 1.6 %collective-permute-start.1 = (bf16[192,128]{1,0:T(8,128)(2,1)S(1)}, bf16[192,128]{1,0:T(8,128)(2,1)S(1)}, u32[]{:S(2)}, u32[]{:S(2)}) collective-permute-start(bf16[192,128]{1,0:T(8,128)(2,1)S(1)} %get-tuple-element.67.refs_0_), channel_id=1, source_target_pairs={{0,8},{2,10},{4,12},{6,14},{8,0},{10,2},{12,4},{14,6},{16,24},{18,... | collective-permute-start | bytes 147464 | tf_op jit(solution)/shard_map/ppermute | solution.py:60
  6.4 2.5 %collective-permute-start.2 = (bf16[192,128]{1,0:T(8,128)(2,1)S(1)}, bf16[192,128]{1,0:T(8,128)(2,1)S(1)}, u32[]{:S(2)}, u32[]{:S(2)}) collective-permute-start(bf16[192,128]{1,0:T(8,128)(2,1)S(1)} %get-tuple-element.67.refs_0_), channel_id=1, source_target_pairs={{0,24},{2,26},{4,28},{6,30},{8,16},{10,18},{12,20},{14,22},{16,8},... | collective-permute-start | bytes 147464 | tf_op jit(solution)/shard_map/ppermute | solution.py:60
  8.9 1.5 %collective-permute-start = (bf16[192,128]{1,0:T(8,128)(2,1)S(1)}, bf16[192,128]{1,0:T(8,128)(2,1)S(1)}, u32[]{:S(2)}, u32[]{:S(2)}) collective-permute-start(bf16[192,128]{1,0:T(8,128)(2,1)S(1)} %get-tuple-element.67.refs_0_), channel_id=1, source_target_pairs={{0,4},{2,6},{4,0},{6,2},{8,12},{10,14},{12,8},{14,10},{16,20},{18,... | collective-permute-start | bytes 147464 | tf_op jit(solution)/shard_map/ppermute | solution.py:64
  10.4 1.9 %collective-permute-done.2.refs_1_.refs_3_ = bf16[192,128]{1,0:T(8,128)(2,1)S(1)} collective-permute-done((bf16[192,128]{1,0:T(8,128)(2,1)S(1)}, bf16[192,128]{1,0:T(8,128)(2,1)S(1)}, u32[]{:S(2)}, u32[]{:S(2)}) %collective-permute-start.2) | collective-permute-done | bytes 49184 | tf_op jit(solution)/shard_map/ppermute | solution.py:60
  12.3 1.6 %collective-permute-start.3 = (bf16[384,128]{1,0:T(8,128)(2,1)S(1)}, bf16[384,128]{1,0:T(8,128)(2,1)S(1)}, u32[]{:S(2)}, u32[]{:S(2)}) collective-permute-start(bf16[384,128]{1,0:T(8,128)(2,1)S(1)} %shard_map.95), channel_id=1, source_target_pairs={{0,4},{2,6},{4,0},{6,2},{8,12},{10,14},{12,8},{14,10},{16,20},{18,... | collective-permute-start | bytes 294920 | tf_op jit(solution)/shard_map/ppermute | solution.py:64
  13.9 0.7 %pad_add_fusion.tables_in.refs_2_ = s32[16,16]{1,0:T(8,128)S(1)} fusion(s32[4,16]{1,0:T(4,128)} %bitcast.17, s32[4,16]{1,0:T(4,128)} %bitcast.18, s32[4,16]{1,0:T(4,128)} %bitcast.19, s32[4,16]{1,0:T(4,128)} %bitcast.20), kind=kLoop, calls=%fused_computation | loop fusion | flops 768 | bytes 2048 | tf_op jit(solution)/shard_map/concatenate | solution.py:608
  14.7 1.0 %copy-done.1 = bf16[1,32,32,192]{3,2,1,0:T(8,128)(2,1)S(1)} copy-done((bf16[1,32,32,192]{3,2,1,0:T(8,128)(2,1)S(1)}, bf16[1,32,32,192]{3,2,1,0:T(8,128)(2,1)}, u32[]{:S(2)}) %copy-start.1) | copy-done | bytes 393240
  15.7 1.1 %shard_map.96 = (bf16[512,1536]{1,0:T(8,128)(2,1)S(1)}, bf16[1024,192]{1,0:T(8,128)(2,1)S(1)}) custom-call(s32[16,16]{1,0:T(8,128)S(1)} %pad_add_fusion.tables_in.refs_2_, bf16[1024,192]{1,0:T(8,128)(2,1)S(1)} %bitcast.12), custom_call_target="tpu_custom_call" | custom-call | bytes 2360320 | tf_op jit(solution)/shard_map/pallas_call | solution.py:111
  16.8 0.0 collective-permute-done.refs_1_
  16.8 0.2 collective-permute-done.3.refs_4_
  17.0 2.5 %shard_map.98 = (f32[448,384]{1,0:T(8,128)S(1)}, f32[448,384]{1,0:T(8,128)S(1)}, bf16[1024,384]{1,0:T(8,128)(2,1)S(1)}, bf16[128,384]{1,0:T(8,128)(2,1)S(1)}, bf16[3,1088,192]{2,1,0:T(8,128)(2,1)S(1)}) custom-call(bf16[32,32,192]{2,1,0:T(8,128)(2,1)S(1)} %get-tuple-element.72.field_ref.refs_3_, bf16[1024,192]{1,0:T(8,128)(2,1)S(1)} %get-tuple-element.73.own_ref, ...), custom_call_target="tpu_custom_call" | custom-call | flops 679477248 | bytes 4694016 | tf_op jit(solution)/shard_map/pallas_call | solution.py:111
  19.5 0.1 collective-permute-start.7
  19.6 0.5 collective-permute-start.8
  20.1 0.1 collective-permute-start.5
  20.3 0.4 collective-permute-start.6
  20.7 1.3 %shard_map.99.refs_3_ = f32[896,384]{1,0:T(8,128)S(1)} custom-call(bf16[3,1088,192]{2,1,0:T(8,128)(2,1)S(1)} %get-tuple-element.75.cols, bf16[1024,384]{1,0:T(8,128)(2,1)S(1)} %get-tuple-element.91.cot_ref), custom_call_target="tpu_custom_call" | custom-call | flops 679477248 | bytes 3416064 | tf_op jit(solution)/shard_map/pallas_call | solution.py:111
  22.0 0.0 copy-start.2
  22.1 1.2 %collective-permute-done.6.refs_5_ = bf16[128,384]{1,0:T(8,128)(2,1)S(1)} collective-permute-done((bf16[128,384]{1,0:T(8,128)(2,1)S(1)}, bf16[128,384]{1,0:T(8,128)(2,1)S(1)}, u32[]{:S(2)}, u32[]{:S(2)}) %collective-permute-start.6) | collective-permute-done | bytes 98336 | tf_op jit(solution)/shard_map/ppermute | solution.py:64
  23.3 1.5 %shard_map.100 = (f32[224,384]{1,0:T(8,128)S(1)}, bf16[224,384]{1,0:T(8,128)(2,1)S(1)}, bf16[224,384]{1,0:T(8,128)(2,1)S(1)}, bf16[224,384]{1,0:T(8,128)(2,1)S(1)}) custom-call(bf16[1152,128]{1,0:T(8,128)(2,1)S(1)} %shard_map.97.refs_0_, bf16[1152,128]{1,0:T(8,128)(2,1)S(1)} %collective-permute-done.5.refs_1_, ...), custom_call_target="tpu_custom_call" | custom-call | bytes 5971968 | tf_op jit(solution)/shard_map/pallas_call | solution.py:111
  24.9 0.6 collective-permute-start.10
  25.5 2.4 %collective-permute-start.11 = (bf16[224,384]{1,0:T(8,128)(2,1)S(1)}, bf16[224,384]{1,0:T(8,128)(2,1)S(1)}, u32[]{:S(2)}, u32[]{:S(2)}) collective-permute-start(bf16[224,384]{1,0:T(8,128)(2,1)S(1)} %get-tuple-element.90), channel_id=1, source_target_pairs={{0,12},{2,14},{4,8},{6,10},{8,4},{10,6},{12,0},{14,2},{16,28},{18,... | collective-permute-start | bytes 516104 | tf_op jit(solution)/shard_map/ppermute | solution.py:64
  27.9 0.5 collective-permute-start.9
  28.4 2.9 %shard_map.101 = (f32[1024,192]{1,0:T(8,128)S(1)}, bf16[216,128]{1,0:T(8,128)(2,1)S(1)}) custom-call(bf16[1024,384]{1,0:T(8,128)(2,1)S(1)} %get-tuple-element.91.cot_ref, bf16[9,384,384]{2,1,0:T(8,128)(2,1)S(1)} %bitcast.13), custom_call_target="tpu_custom_call" | custom-call | flops 1358954496 | bytes 4282368 | tf_op jit(solution)/shard_map/pallas_call | solution.py:111
  31.3 0.6 collective-permute-start.12
  31.9 2.5 %collective-permute-start.13 = (bf16[216,128]{1,0:T(8,128)(2,1)S(1)}, bf16[216,128]{1,0:T(8,128)(2,1)S(1)}, u32[]{:S(2)}, u32[]{:S(2)}) collective-permute-start(bf16[216,128]{1,0:T(8,128)(2,1)S(1)} %get-tuple-element.110.refs_0_), channel_id=1, source_target_pairs={{0,24},{2,26},{4,28},{6,30},{8,16},{10,18},{12,20},{14,22},{16,8},... | collective-permute-start | bytes 165896 | tf_op jit(solution)/shard_map/ppermute | solution.py:60
  34.3 1.2 %shard_map.103.place_ref = bf16[128,1728]{1,0:T(8,128)(2,1)S(1)} custom-call(s32[16,16]{1,0:T(8,128)S(1)} %pad_add_fusion.tables_in.refs_2_), custom_call_target="tpu_custom_call" | custom-call | bytes 443392 | tf_op jit(solution)/shard_map/pallas_call | solution.py:111
  35.6 1.3 %shard_map.102 = (bf16[144,192]{1,0:T(8,128)(2,1)S(1)}, bf16[1752,128]{1,0:T(8,128)(2,1)S(1)}) custom-call(bf16[1152,128]{1,0:T(8,128)(2,1)S(1)} %shard_map.97.refs_0_, bf16[1152,128]{1,0:T(8,128)(2,1)S(1)} %collective-permute-done.5.refs_1_, s32[16,16]{1,0:T(8,128)S(1)} %pad_add_fusion.tables_in.refs_2_, ...), custom_call_target="tpu_custom_call" | custom-call | bytes 1487872 | tf_op jit(solution)/shard_map/pallas_call | solution.py:111
  36.8 1.6 %collective-permute-done.13.refs_2_ = bf16[216,128]{1,0:T(8,128)(2,1)S(1)} collective-permute-done((bf16[216,128]{1,0:T(8,128)(2,1)S(1)}, bf16[216,128]{1,0:T(8,128)(2,1)S(1)}, u32[]{:S(2)}, u32[]{:S(2)}) %collective-permute-start.13) | collective-permute-done | bytes 55328 | tf_op jit(solution)/shard_map/ppermute | solution.py:60
  38.5 1.6 %collective-permute-start.22 = (bf16[1752,128]{1,0:T(8,128)(2,1)S(1)}, bf16[1752,128]{1,0:T(8,128)(2,1)S(1)}, u32[]{:S(2)}, u32[]{:S(2)}) collective-permute-start(bf16[1752,128]{1,0:T(8,128)(2,1)S(1)} %get-tuple-element.121), channel_id=1, source_target_pairs={{0,1},{1,0},{2,3},{3,2},{4,5},{5,4},{6,7},{7,6},{8,9},{9,8},{10,11... | collective-permute-start | bytes 1345544 | tf_op jit(solution)/shard_map/ppermute | solution.py:694
  40.0 0.1 shard_map.104
  40.1 0.6 collective-permute-start.14
  40.7 1.3 %collective-permute-start.16 = (bf16[648,128]{1,0:T(8,128)(2,1)S(1)}, bf16[648,128]{1,0:T(8,128)(2,1)S(1)}, u32[]{:S(2)}, u32[]{:S(2)}) collective-permute-start(bf16[648,128]{1,0:T(8,128)(2,1)S(1)} %shard_map.105.refs_0_), channel_id=1, source_target_pairs={{0,4},{2,6},{4,0},{6,2},{8,12},{10,14},{12,8},{14,10},{16,20},{18,... | collective-permute-start | bytes 497672 | tf_op jit(solution)/shard_map/ppermute | solution.py:64
  42.0 3.6 %collective-permute-done.14.refs_1_ = bf16[112,384]{1,0:T(8,128)(2,1)S(1)} collective-permute-done((bf16[112,384]{1,0:T(8,128)(2,1)S(1)}, bf16[112,384]{1,0:T(8,128)(2,1)S(1)}, u32[]{:S(2)}, u32[]{:S(2)}) %collective-permute-start.14) | collective-permute-done | bytes 86048 | tf_op jit(solution)/shard_map/ppermute | solution.py:64
  45.6 0.6 collective-permute-start.15
  46.2 5.2 %collective-permute-done.15.refs_1_ = bf16[112,384]{1,0:T(8,128)(2,1)S(1)} collective-permute-done((bf16[112,384]{1,0:T(8,128)(2,1)S(1)}, bf16[112,384]{1,0:T(8,128)(2,1)S(1)}, u32[]{:S(2)}, u32[]{:S(2)}) %collective-permute-start.15) | collective-permute-done | bytes 86048 | tf_op jit(solution)/shard_map/ppermute | solution.py:64
  51.4 1.3 %collective-permute-start.17 = (bf16[224,384]{1,0:T(8,128)(2,1)S(1)}, bf16[224,384]{1,0:T(8,128)(2,1)S(1)}, u32[]{:S(2)}, u32[]{:S(2)}) collective-permute-start(bf16[224,384]{1,0:T(8,128)(2,1)S(1)} %shard_map.107.refs_0_), channel_id=1, source_target_pairs={{0,4},{2,6},{4,0},{6,2},{8,12},{10,14},{12,8},{14,10},{16,20},{18,... | collective-permute-start | bytes 516104 | tf_op jit(solution)/shard_map/ppermute | solution.py:64
  52.7 2.3 %collective-permute-start.19 = (bf16[224,384]{1,0:T(8,128)(2,1)S(1)}, bf16[224,384]{1,0:T(8,128)(2,1)S(1)}, u32[]{:S(2)}, u32[]{:S(2)}) collective-permute-start(bf16[224,384]{1,0:T(8,128)(2,1)S(1)} %shard_map.107.refs_0_), channel_id=1, source_target_pairs={{0,12},{2,14},{4,8},{6,10},{8,4},{10,6},{12,0},{14,2},{16,28},{18,... | collective-permute-start | bytes 516104 | tf_op jit(solution)/shard_map/ppermute | solution.py:64
  55.0 1.3 %shard_map.108 = bf16[1024,192]{1,0:T(8,128)(2,1)} custom-call(bf16[128,1728]{1,0:T(8,128)(2,1)S(1)} %shard_map.103.place_ref, f32[1024,192]{1,0:T(8,128)S(1)} %get-tuple-element.117.inner_ref, bf16[648,128]{1,0:T(8,128)(2,1)S(1)} %shard_map.105.refs_0_, bf16[648,128]{1,0:T(8,128)(2,1)S(1)} %collective-permute-done.16.refs_1_, ...), custom_call_target="tpu_custom_call" | custom-call | bytes 2285568 | tf_op jit(solution)/shard_map/pallas_call | solution.py:111
  56.3 3.9 %shard_map.109 = bf16[1024,192]{1,0:T(8,128)(2,1)} custom-call(bf16[32,32,192]{2,1,0:T(8,128)(2,1)S(1)} %get-tuple-element.72.field_ref.refs_3_, bf16[144,192]{1,0:T(8,128)(2,1)S(1)} %get-tuple-element.120.halos_ref, bf16[1752,128]{1,0:T(8,128)(2,1)S(1)} %collective-permute-done.22.other_ref, bf16[9,384,384]{2,1,0:T(8,128)(2,1)S(1)} %bitcast.14), custom_call_target="tpu_custom_call" | custom-call | flops 2717908992 | bytes 3944448 | tf_op jit(solution)/shard_map/pallas_call | solution.py:111
  60.2 2.9 %collective-permute-done.19.refs_3_ = bf16[224,384]{1,0:T(8,128)(2,1)S(1)} collective-permute-done((bf16[224,384]{1,0:T(8,128)(2,1)S(1)}, bf16[224,384]{1,0:T(8,128)(2,1)S(1)}, u32[]{:S(2)}, u32[]{:S(2)}) %collective-permute-start.19) | collective-permute-done | bytes 172064 | tf_op jit(solution)/shard_map/ppermute | solution.py:64
  63.1 0.5 collective-permute-start.25
  63.6 0.0 collective-permute-start.26
  63.6 1.4 %shard_map.110.refs_0_ = f32[1728,384]{1,0:T(8,128)} custom-call(bf16[224,384]{1,0:T(8,128)(2,1)S(1)} %shard_map.107.refs_0_, bf16[224,384]{1,0:T(8,128)(2,1)S(1)} %collective-permute-done.17.refs_1_, bf16[224,384]{1,0:T(8,128)(2,1)S(1)} %collective-permute-done.18.refs_2_, bf16[224,384]{1,0:T(8,128)(2,1)S(1)} %collective-permute-done.19.refs_3_, ...), custom_call_target="tpu_custom_call" | custom-call | tf_op jit(solution)/shard_map/pallas_call | solution.py:450
  65.0 0.0 collective-permute-done.26.refs_3_
  65.0 1.1 %shard_map.111 = f32[1728,384]{1,0:T(8,128)} custom-call(f32[1728,384]{1,0:T(8,128)} %shard_map.110.refs_0_, bf16[224,384]{1,0:T(8,128)(2,1)S(1)} %collective-permute-done.24.refs_1_, bf16[224,384]{1,0:T(8,128)(2,1)S(1)} %collective-permute-done.25.refs_2_, bf16[224,384]{1,0:T(8,128)(2,1)S(1)} %collective-permute-done.26.refs_3_), custom_call_target="tpu_custom_call", output_to_operand_aliasing={{}: (0, {})} | custom-call | tf_op jit(solution)/shard_map/pallas_call | solution.py:450
  (31 shorter events, 0.1 us)
Async XLA Ops:
  0.6 16.4 %collective-permute-start.4 = (bf16[1024,192]{1,0:T(8,128)(2,1)}, bf16[1024,192]{1,0:T(8,128)(2,1)S(1)}, u32[]{:S(2)}, u32[]{:S(2)}) collective-permute-start(bf16[1024,192]{1,0:T(8,128)(2,1)} %bitcast.11), channel_id=1, source_target_pairs={{0,1},{1,0},{2,3},{3,2},{4,5},{5,4},{6,7},{7,6},{8,9},{9,8},{10,11... | collective-permute-start | bytes 1179656 | tf_op jit(solution)/shard_map/ppermute | solution.py:600
  3.6 1.0 %copy-start = (bf16[1,32,32,192]{3,2,1,0:T(8,128)(2,1)S(1)}, bf16[1,32,32,192]{3,2,1,0:T(8,128)(2,1)}, u32[]{:S(2)}) copy-start(bf16[1,32,32,192]{3,2,1,0:T(8,128)(2,1)} %param.7) | copy-start | bytes 1179652
  4.8 5.6 %collective-permute-start.1 = (bf16[192,128]{1,0:T(8,128)(2,1)S(1)}, bf16[192,128]{1,0:T(8,128)(2,1)S(1)}, u32[]{:S(2)}, u32[]{:S(2)}) collective-permute-start(bf16[192,128]{1,0:T(8,128)(2,1)S(1)} %get-tuple-element.67.refs_0_), channel_id=1, source_target_pairs={{0,8},{2,10},{4,12},{6,14},{8,0},{10,2},{12,4},{14,6},{16,24},{18,... | collective-permute-start | bytes 147464 | tf_op jit(solution)/shard_map/ppermute | solution.py:60
  6.4 5.9 %collective-permute-start.2 = (bf16[192,128]{1,0:T(8,128)(2,1)S(1)}, bf16[192,128]{1,0:T(8,128)(2,1)S(1)}, u32[]{:S(2)}, u32[]{:S(2)}) collective-permute-start(bf16[192,128]{1,0:T(8,128)(2,1)S(1)} %get-tuple-element.67.refs_0_), channel_id=1, source_target_pairs={{0,24},{2,26},{4,28},{6,30},{8,16},{10,18},{12,20},{14,22},{16,8},... | collective-permute-start | bytes 147464 | tf_op jit(solution)/shard_map/ppermute | solution.py:60
  8.9 7.9 %collective-permute-start = (bf16[192,128]{1,0:T(8,128)(2,1)S(1)}, bf16[192,128]{1,0:T(8,128)(2,1)S(1)}, u32[]{:S(2)}, u32[]{:S(2)}) collective-permute-start(bf16[192,128]{1,0:T(8,128)(2,1)S(1)} %get-tuple-element.67.refs_0_), channel_id=1, source_target_pairs={{0,4},{2,6},{4,0},{6,2},{8,12},{10,14},{12,8},{14,10},{16,20},{18,... | collective-permute-start | bytes 147464 | tf_op jit(solution)/shard_map/ppermute | solution.py:64
  12.3 4.7 %collective-permute-start.3 = (bf16[384,128]{1,0:T(8,128)(2,1)S(1)}, bf16[384,128]{1,0:T(8,128)(2,1)S(1)}, u32[]{:S(2)}, u32[]{:S(2)}) collective-permute-start(bf16[384,128]{1,0:T(8,128)(2,1)S(1)} %shard_map.95), channel_id=1, source_target_pairs={{0,4},{2,6},{4,0},{6,2},{8,12},{10,14},{12,8},{14,10},{16,20},{18,... | collective-permute-start | bytes 294920 | tf_op jit(solution)/shard_map/ppermute | solution.py:64
  14.7 1.0 %copy-start.1 = (bf16[1,32,32,192]{3,2,1,0:T(8,128)(2,1)S(1)}, bf16[1,32,32,192]{3,2,1,0:T(8,128)(2,1)}, u32[]{:S(2)}) copy-start(bf16[1,32,32,192]{3,2,1,0:T(8,128)(2,1)} %param.9) | copy-start | bytes 1179652
  19.5 3.8 %collective-permute-start.7 = (f32[448,384]{1,0:T(8,128)S(1)}, f32[448,384]{1,0:T(8,128)S(1)}, u32[]{:S(2)}, u32[]{:S(2)}) collective-permute-start(f32[448,384]{1,0:T(8,128)S(1)} %get-tuple-element.82), channel_id=1, source_target_pairs={{0,2},{2,0},{4,6},{6,4},{8,10},{10,8},{12,14},{14,12},{16,18},{18,... | collective-permute-start | bytes 2064392 | tf_op jit(solution)/shard_map/ppermute | solution.py:64
  19.6 3.7 %collective-permute-start.8 = (f32[448,384]{1,0:T(8,128)S(1)}, f32[448,384]{1,0:T(8,128)S(1)}, u32[]{:S(2)}, u32[]{:S(2)}) collective-permute-start(f32[448,384]{1,0:T(8,128)S(1)} %get-tuple-element.83), channel_id=1, source_target_pairs={{0,2},{2,0},{4,6},{6,4},{8,10},{10,8},{12,14},{14,12},{16,18},{18,... | collective-permute-start | bytes 2064392 | tf_op jit(solution)/shard_map/ppermute | solution.py:64
  20.1 3.2 %collective-permute-start.5 = (bf16[1152,128]{1,0:T(8,128)(2,1)S(1)}, bf16[1152,128]{1,0:T(8,128)(2,1)S(1)}, u32[]{:S(2)}, u32[]{:S(2)}) collective-permute-start(bf16[1152,128]{1,0:T(8,128)(2,1)S(1)} %shard_map.97.refs_0_), channel_id=1, source_target_pairs={{0,2},{2,0},{4,6},{6,4},{8,10},{10,8},{12,14},{14,12},{16,18},{18,... | collective-permute-start | bytes 884744 | tf_op jit(solution)/shard_map/ppermute | solution.py:64
  20.3 3.0 %collective-permute-start.6 = (bf16[128,384]{1,0:T(8,128)(2,1)S(1)}, bf16[128,384]{1,0:T(8,128)(2,1)S(1)}, u32[]{:S(2)}, u32[]{:S(2)}) collective-permute-start(bf16[128,384]{1,0:T(8,128)(2,1)S(1)} %get-tuple-element.77.refs_4_), channel_id=1, source_target_pairs={{0,2},{2,0},{4,6},{6,4},{8,10},{10,8},{12,14},{14,12},{16,18},{18,... | collective-permute-start | bytes 294920 | tf_op jit(solution)/shard_map/ppermute | solution.py:64
  22.0 6.4 %copy-start.2 = (bf16[3,3,384,384]{3,2,1,0:T(8,128)(2,1)S(1)}, bf16[3,3,384,384]{3,2,1,0:T(8,128)(2,1)}, u32[]{:S(2)}) copy-start(bf16[3,3,384,384]{3,2,1,0:T(8,128)(2,1)} %param.8) | copy-start | bytes 7962628
  24.9 13.6 %collective-permute-start.10 = (bf16[224,384]{1,0:T(8,128)(2,1)S(1)}, bf16[224,384]{1,0:T(8,128)(2,1)S(1)}, u32[]{:S(2)}, u32[]{:S(2)}) collective-permute-start(bf16[224,384]{1,0:T(8,128)(2,1)S(1)} %get-tuple-element.89), channel_id=1, source_target_pairs={{0,8},{2,10},{4,12},{6,14},{8,0},{10,2},{12,4},{14,6},{16,24},{18,... | collective-permute-start | bytes 516104 | tf_op jit(solution)/shard_map/ppermute | solution.py:64
  25.5 13.0 %collective-permute-start.11 = (bf16[224,384]{1,0:T(8,128)(2,1)S(1)}, bf16[224,384]{1,0:T(8,128)(2,1)S(1)}, u32[]{:S(2)}, u32[]{:S(2)}) collective-permute-start(bf16[224,384]{1,0:T(8,128)(2,1)S(1)} %get-tuple-element.90), channel_id=1, source_target_pairs={{0,12},{2,14},{4,8},{6,10},{8,4},{10,6},{12,0},{14,2},{16,28},{18,... | collective-permute-start | bytes 516104 | tf_op jit(solution)/shard_map/ppermute | solution.py:64
  27.9 10.6 %collective-permute-start.9 = (bf16[224,384]{1,0:T(8,128)(2,1)S(1)}, bf16[224,384]{1,0:T(8,128)(2,1)S(1)}, u32[]{:S(2)}, u32[]{:S(2)}) collective-permute-start(bf16[224,384]{1,0:T(8,128)(2,1)S(1)} %get-tuple-element.88), channel_id=1, source_target_pairs={{0,4},{2,6},{4,0},{6,2},{8,12},{10,14},{12,8},{14,10},{16,20},{18,... | collective-permute-start | bytes 516104 | tf_op jit(solution)/shard_map/ppermute | solution.py:64
  31.3 5.5 %collective-permute-start.12 = (bf16[216,128]{1,0:T(8,128)(2,1)S(1)}, bf16[216,128]{1,0:T(8,128)(2,1)S(1)}, u32[]{:S(2)}, u32[]{:S(2)}) collective-permute-start(bf16[216,128]{1,0:T(8,128)(2,1)S(1)} %get-tuple-element.110.refs_0_), channel_id=1, source_target_pairs={{0,8},{2,10},{4,12},{6,14},{8,0},{10,2},{12,4},{14,6},{16,24},{18,... | collective-permute-start | bytes 165896 | tf_op jit(solution)/shard_map/ppermute | solution.py:60
  31.9 6.6 %collective-permute-start.13 = (bf16[216,128]{1,0:T(8,128)(2,1)S(1)}, bf16[216,128]{1,0:T(8,128)(2,1)S(1)}, u32[]{:S(2)}, u32[]{:S(2)}) collective-permute-start(bf16[216,128]{1,0:T(8,128)(2,1)S(1)} %get-tuple-element.110.refs_0_), channel_id=1, source_target_pairs={{0,24},{2,26},{4,28},{6,30},{8,16},{10,18},{12,20},{14,22},{16,8},... | collective-permute-start | bytes 165896 | tf_op jit(solution)/shard_map/ppermute | solution.py:60
  38.5 17.8 %collective-permute-start.22 = (bf16[1752,128]{1,0:T(8,128)(2,1)S(1)}, bf16[1752,128]{1,0:T(8,128)(2,1)S(1)}, u32[]{:S(2)}, u32[]{:S(2)}) collective-permute-start(bf16[1752,128]{1,0:T(8,128)(2,1)S(1)} %get-tuple-element.121), channel_id=1, source_target_pairs={{0,1},{1,0},{2,3},{3,2},{4,5},{5,4},{6,7},{7,6},{8,9},{9,8},{10,11... | collective-permute-start | bytes 1345544 | tf_op jit(solution)/shard_map/ppermute | solution.py:694
  40.1 5.4 %collective-permute-start.14 = (bf16[112,384]{1,0:T(8,128)(2,1)S(1)}, bf16[112,384]{1,0:T(8,128)(2,1)S(1)}, u32[]{:S(2)}, u32[]{:S(2)}) collective-permute-start(bf16[112,384]{1,0:T(8,128)(2,1)S(1)} %get-tuple-element.109), channel_id=1, source_target_pairs={{0,16},{2,18},{4,20},{6,22},{8,24},{10,26},{12,28},{14,30},{16,0},... | collective-permute-start | bytes 258056 | tf_op jit(solution)/shard_map/ppermute | solution.py:64
  40.7 5.5 %collective-permute-start.16 = (bf16[648,128]{1,0:T(8,128)(2,1)S(1)}, bf16[648,128]{1,0:T(8,128)(2,1)S(1)}, u32[]{:S(2)}, u32[]{:S(2)}) collective-permute-start(bf16[648,128]{1,0:T(8,128)(2,1)S(1)} %shard_map.105.refs_0_), channel_id=1, source_target_pairs={{0,4},{2,6},{4,0},{6,2},{8,12},{10,14},{12,8},{14,10},{16,20},{18,... | collective-permute-start | bytes 497672 | tf_op jit(solution)/shard_map/ppermute | solution.py:64
  45.6 5.8 %collective-permute-start.15 = (bf16[112,384]{1,0:T(8,128)(2,1)S(1)}, bf16[112,384]{1,0:T(8,128)(2,1)S(1)}, u32[]{:S(2)}, u32[]{:S(2)}) collective-permute-start(bf16[112,384]{1,0:T(8,128)(2,1)S(1)} %shard_map.106.refs_0_), channel_id=1, source_target_pairs={{0,16},{2,18},{4,20},{6,22},{8,24},{10,26},{12,28},{14,30},{16,0},... | collective-permute-start | bytes 258056 | tf_op jit(solution)/shard_map/ppermute | solution.py:64
  46.2 6.5 %collective-permute-start.20 = (bf16[648,128]{1,0:T(8,128)(2,1)S(1)}, bf16[648,128]{1,0:T(8,128)(2,1)S(1)}, u32[]{:S(2)}, u32[]{:S(2)}) collective-permute-start(bf16[648,128]{1,0:T(8,128)(2,1)S(1)} %shard_map.105.refs_0_), channel_id=1, source_target_pairs={{0,2},{2,0},{4,6},{6,4},{8,10},{10,8},{12,14},{14,12},{16,18},{18,... | collective-permute-start | bytes 497672 | tf_op jit(solution)/shard_map/ppermute | solution.py:64
  51.4 3.6 %collective-permute-start.21 = (bf16[648,128]{1,0:T(8,128)(2,1)S(1)}, bf16[648,128]{1,0:T(8,128)(2,1)S(1)}, u32[]{:S(2)}, u32[]{:S(2)}) collective-permute-start(bf16[648,128]{1,0:T(8,128)(2,1)S(1)} %collective-permute-done.16.refs_1_), channel_id=1, source_target_pairs={{0,2},{2,0},{4,6},{6,4},{8,10},{10,8},{12,14},{14,12},{16,18},{18,... | collective-permute-start | bytes 497672 | tf_op jit(solution)/shard_map/ppermute | solution.py:64
  51.4 8.8 %collective-permute-start.17 = (bf16[224,384]{1,0:T(8,128)(2,1)S(1)}, bf16[224,384]{1,0:T(8,128)(2,1)S(1)}, u32[]{:S(2)}, u32[]{:S(2)}) collective-permute-start(bf16[224,384]{1,0:T(8,128)(2,1)S(1)} %shard_map.107.refs_0_), channel_id=1, source_target_pairs={{0,4},{2,6},{4,0},{6,2},{8,12},{10,14},{12,8},{14,10},{16,20},{18,... | collective-permute-start | bytes 516104 | tf_op jit(solution)/shard_map/ppermute | solution.py:64
  52.7 7.5 %collective-permute-start.18 = (bf16[224,384]{1,0:T(8,128)(2,1)S(1)}, bf16[224,384]{1,0:T(8,128)(2,1)S(1)}, u32[]{:S(2)}, u32[]{:S(2)}) collective-permute-start(bf16[224,384]{1,0:T(8,128)(2,1)S(1)} %shard_map.107.refs_0_), channel_id=1, source_target_pairs={{0,8},{2,10},{4,12},{6,14},{8,0},{10,2},{12,4},{14,6},{16,24},{18,... | collective-permute-start | bytes 516104 | tf_op jit(solution)/shard_map/ppermute | solution.py:64
  52.7 10.4 %collective-permute-start.19 = (bf16[224,384]{1,0:T(8,128)(2,1)S(1)}, bf16[224,384]{1,0:T(8,128)(2,1)S(1)}, u32[]{:S(2)}, u32[]{:S(2)}) collective-permute-start(bf16[224,384]{1,0:T(8,128)(2,1)S(1)} %shard_map.107.refs_0_), channel_id=1, source_target_pairs={{0,12},{2,14},{4,8},{6,10},{8,4},{10,6},{12,0},{14,2},{16,28},{18,... | collective-permute-start | bytes 516104 | tf_op jit(solution)/shard_map/ppermute | solution.py:64
  54.9 8.7 %collective-permute-start.23 = (bf16[224,384]{1,0:T(8,128)(2,1)S(1)}, bf16[224,384]{1,0:T(8,128)(2,1)S(1)}, u32[]{:S(2)}, u32[]{:S(2)}) collective-permute-start(bf16[224,384]{1,0:T(8,128)(2,1)S(1)} %shard_map.107.refs_0_), channel_id=1, source_target_pairs={{0,2},{2,0},{4,6},{6,4},{8,10},{10,8},{12,14},{14,12},{16,18},{18,... | collective-permute-start | bytes 516104 | tf_op jit(solution)/shard_map/ppermute | solution.py:64
  63.1 1.9 %collective-permute-start.24 = (bf16[224,384]{1,0:T(8,128)(2,1)S(1)}, bf16[224,384]{1,0:T(8,128)(2,1)S(1)}, u32[]{:S(2)}, u32[]{:S(2)}) collective-permute-start(bf16[224,384]{1,0:T(8,128)(2,1)S(1)} %collective-permute-done.17.refs_1_), channel_id=1, source_target_pairs={{0,2},{2,0},{4,6},{6,4},{8,10},{10,8},{12,14},{14,12},{16,18},{18,... | collective-permute-start | bytes 516104 | tf_op jit(solution)/shard_map/ppermute | solution.py:64
  63.1 1.9 %collective-permute-start.25 = (bf16[224,384]{1,0:T(8,128)(2,1)S(1)}, bf16[224,384]{1,0:T(8,128)(2,1)S(1)}, u32[]{:S(2)}, u32[]{:S(2)}) collective-permute-start(bf16[224,384]{1,0:T(8,128)(2,1)S(1)} %collective-permute-done.18.refs_2_), channel_id=1, source_target_pairs={{0,2},{2,0},{4,6},{6,4},{8,10},{10,8},{12,14},{14,12},{16,18},{18,... | collective-permute-start | bytes 516104 | tf_op jit(solution)/shard_map/ppermute | solution.py:64
  63.6 1.4 %collective-permute-start.26 = (bf16[224,384]{1,0:T(8,128)(2,1)S(1)}, bf16[224,384]{1,0:T(8,128)(2,1)S(1)}, u32[]{:S(2)}, u32[]{:S(2)}) collective-permute-start(bf16[224,384]{1,0:T(8,128)(2,1)S(1)} %collective-permute-done.19.refs_3_), channel_id=1, source_target_pairs={{0,2},{2,0},{4,6},{6,4},{8,10},{10,8},{12,14},{14,12},{16,18},{18,... | collective-permute-start | bytes 516104 | tf_op jit(solution)/shard_map/ppermute | solution.py:64

commit v10 on v9

--- a/solution.py
+++ b/solution.py
@@ -11,7 +11,6 @@
 
 SPAN = 4
 EXTRA = 16
-CUTS = 2
 
 
 def turn_tables():
@@ -103,11 +102,11 @@
     return jax.ShapeDtypeStruct(shape, dtype)
 
 
-def call(kernel, outs, args, anywhere=(), scratch=(), flops=0):
+def call(kernel, outs, args, anywhere=(), scratch=(), flops=0, costed=True):
     in_specs = [
         pl.BlockSpec(memory_space=pltpu.HBM if i in anywhere else pltpu.VMEM) for i in range(len(args))
     ]
-    size = sum(math.prod(x.shape) * x.dtype.itemsize for x in list(args) + list(outs))
+    size = costed * sum(math.prod(x.shape) * x.dtype.itemsize for x in list(args) + list(outs))
     return pl.pallas_call(
         kernel,
         out_shape=tuple(outs),
@@ -276,65 +275,55 @@
     place_ref[...] = jnp.concatenate(places, axis=1).astype(jnp.bfloat16)
 
 
-def half_taps(side, part, half, scale, which, cols, cot, out_ref, middle):
+def tap_product(side, scale, tap, cols, tall):
     rows = side * side
-    used = 9 * part // 2
-
-    def product(a, b):
-        value = lax.dot_general(
-            cols[b, pl.ds(pl.multiple_of(a * side, 16), rows), :],
-            cot,
-            (((0,), (0,)), ((), ())),
-            preferred_element_type=jnp.float32,
-        )
-        return value * scale
-
-    for j in range(4):
-        tap = j + 5 * which
-        start = pl.multiple_of(which * (part // 2) + j * part, 16)
-        out_ref[pl.ds(start, part), :] = product(tap // 3, lax.rem(tap, 3))
-    middle[...] = product(1, 1)
-    start = pl.multiple_of((1 - which) * 4 * part, 16)
-    out_ref[pl.ds(start, part // 2), :] = middle[pl.ds(pl.multiple_of(which * (part // 2), 16), part // 2), :]
-    out_ref[used:, :] = jnp.zeros((half - used, cot.shape[1]), jnp.float32)
-
-
-def send_kernel(side, part, half, scale, field_ref, own_ref, other_ref, *refs):
-    send_refs, (cot_ref, rim_ref, cols, middle, send) = refs[:CUTS], refs[CUTS:]
+    start = pl.multiple_of((3 - tap // 3) * side, 16)
+    value = jnp.dot(
+        cols[lax.rem(tap, 3)], tall[pl.ds(start, rows), :], preferred_element_type=jnp.float32
+    )
+    return value * scale
+
+
+def send_kernel(
+    side, part, scale, field_ref, own_ref, other_ref, send_ref, tall_ref, rim_ref, cols_ref
+):
     rows = side * side
-    chans = cot_ref.shape[1]
     first = lax.axis_index("ch") == 0
+    here = slice(2 * side, 2 * side + rows)
+    blank = jnp.zeros((2 * side, tall_ref.shape[1]), jnp.bfloat16)
+    tall_ref[0 : 2 * side, :] = blank
+    tall_ref[2 * side + rows :, :] = blank
 
     @pl.when(first)
     def _():
-        cot_ref[:, 0:part] = own_ref[...]
-        cot_ref[:, part:] = other_ref[...]
+        tall_ref[here, 0:part] = own_ref[...]
+        tall_ref[here, part:] = other_ref[...]
 
     @pl.when(jnp.logical_not(first))
     def _():
-        cot_ref[:, 0:part] = other_ref[...]
-        cot_ref[:, part:] = own_ref[...]
-
-    shifted_columns(side, part, field_ref[...].reshape(rows, part), None, cols)
-    cot = cot_ref[...]
-    rim_ref[...] = jnp.concatenate(
-        [
-            cot[0:side],
-            cot[rows - side :],
-            cot.reshape(side, side, chans)[:, 0, :],
-            cot.reshape(side, side, chans)[:, side - 1, :],
-        ],
-        axis=0,
-    )
+        tall_ref[here, 0:part] = other_ref[...]
+        tall_ref[here, part:] = own_ref[...]
+
+    cot = tall_ref[here, :]
+    column = lax.broadcasted_iota(jnp.int32, (rows, part), 0) % side
+    field = field_ref[...].reshape(rows, part).astype(jnp.float32)
+    cols_ref[0] = jnp.where(column == 0, 0.0, pltpu.roll(field, 1, 0)).astype(jnp.bfloat16).T
+    cols_ref[1] = field.astype(jnp.bfloat16).T
+    cols_ref[2] = jnp.where(column == side - 1, 0.0, pltpu.roll(field, rows - 1, 0)).astype(jnp.bfloat16).T
     which = 1 - lax.rem(lax.axis_index("tile"), 2)
-    half_taps(side, part, half, scale, which, cols, cot, send, middle)
-    for i, ref in enumerate(send_refs):
-        ref[...] = send[i * (half // CUTS) : (i + 1) * (half // CUTS), :]
-
-
-def mine_kernel(side, part, half, scale, cols, cot_ref, mine_ref, middle):
-    which = lax.rem(lax.axis_index("tile"), 2)
-    half_taps(side, part, half, scale, which, cols, cot_ref[...], mine_ref, middle)
+    for j in range(2):
+        send_ref[j * part : (j + 1) * part, :] = tap_product(side, scale, j + 5 * which, cols_ref, tall_ref)
+    rim = cot.reshape(side, side, cot.shape[1])
+    rim_ref[...] = jnp.concatenate([cot[0:side], cot[rows - side :], rim[:, 0, :], rim[:, side - 1, :]], axis=0)
+
+
+def half_kernel(side, part, scale, mate, taps, cols, tall, out_ref, middle):
+    which = lax.rem(lax.axis_index("tile") + mate, 2)
+    for at, j in enumerate(taps):
+        out_ref[at * part : (at + 1) * part, :] = tap_product(side, scale, j + 5 * which, cols, tall)
+    middle[...] = tap_product(side, scale, 4, cols, tall)
+    start = pl.multiple_of(which * (part // 2), 16)
+    out_ref[len(taps) * part :, :] = middle[pl.ds(start, part // 2), :]
 
 
 def unpack_near(near_refs, near, side, part):
@@ -348,16 +337,22 @@
 
 def border_kernel(side, part, chunk, scale, n_near, *refs):
     near_refs = refs[:n_near]
-    onehot_ref, mine_ref, rim_ref, mate_ref = refs[n_near : n_near + 4]
-    got_refs = refs[n_near + 4 : n_near + 4 + CUTS]
-    outs, near, total = refs[n_near + 4 + CUTS : -2], refs[-2], refs[-1]
+    onehot_ref, mine_ref, rim_ref, mate_ref, first_ref, second_ref = refs[n_near : n_near + 6]
+    outs, near, total = refs[n_near + 6 : -2], refs[-2], refs[-1]
     count = lax.axis_size("tile")
     own = lax.axis_index("tile")
     core = lax.rem(own, 2)
     unpack_near(near_refs, near, side, part)
-    for i, ref in enumerate(got_refs):
-        here = slice(i * ref.shape[0], (i + 1) * ref.shape[0])
-        total[here, :] = mine_ref[here, :] + ref[...]
+    half = part // 2
+    used = 9 * half
+
+    def place(start, value):
+        total[pl.ds(pl.multiple_of(start, 16), value.shape[0]), :] = value
+
+    place(core * half, mine_ref[0 : 2 * part, :] + first_ref[...])
+    place(core * half + 2 * part, mine_ref[2 * part : 4 * part, :] + second_ref[0 : 2 * part, :])
+    place((1 - core) * 4 * part, mine_ref[4 * part :, :] + second_ref[2 * part :, :])
+    total[used:, :] = jnp.zeros((total.shape[0] - used, total.shape[1]), jnp.float32)
     left = jnp.dot(onehot_ref[...], near[...], preferred_element_type=jnp.float32).astype(jnp.bfloat16)
 
     def rim(ref, at):
@@ -461,14 +456,10 @@
     )(*([before] if n_dep else []), *blocks)
 
 
-def back_kernel(side, part, cot_ref, weight_ref, inner_ref, pieces_ref, tall):
+def back_kernel(side, part, tall, weight_ref, inner_ref, pieces_ref):
     rows = side * side
     flat = rows + 2 * side
     start = pl.multiple_of(lax.axis_index("ch") * part, 16)
-    blank = jnp.zeros((2 * side, tall.shape[1]), jnp.bfloat16)
-    tall[0 : 2 * side, :] = blank
-    tall[2 * side : 2 * side + rows, :] = cot_ref[...]
-    tall[2 * side + rows :, :] = blank
     backs = []
     for b in range(3):
         back = jnp.zeros((flat, part), jnp.float32)
@@ -619,26 +610,32 @@
     near, cot_other, border_pick = lax.optimization_barrier((near, cot_other, border_pick))
     (near,) = call(join_kernel, [vmem(packed_shape(24 * side, part), half_bytes)], near)
     mates = by_mask(near, 1, count)
-    *send, cot_full, rim, cols = call(
-        functools.partial(send_kernel, side, part, half, scale),
+    first, tall, rim, cols = call(
+        functools.partial(send_kernel, side, part, scale),
         [
-            *[vmem((half // CUTS, chans), jnp.float32)] * CUTS,
-            vmem((rows, chans), half_bytes),
+            vmem((2 * part, chans), jnp.float32),
+            vmem((rows + 4 * side, chans), half_bytes),
             vmem((4 * side, chans), half_bytes),
-            vmem((3, flat, part), half_bytes),
+            vmem((3, part, rows), half_bytes),
         ],
         [field, cot_own, cot_other],
-        scratch=[pltpu.VMEM((part, chans), jnp.float32), pltpu.VMEM((half, chans), jnp.float32)],
-        flops=flops // 2,
-    )
+        flops=flops // 4,
+    )
+    (second,) = call(
+        functools.partial(half_kernel, side, part, scale, 1, (2, 3)),
+        [vmem((5 * part // 2, chans), jnp.float32)],
+        [cols, tall],
+        scratch=[pltpu.VMEM((part, chans), jnp.float32)],
+        flops=flops,
+    )
+    tall, second = lax.optimization_barrier((tall, second))
     (mine,) = call(
-        functools.partial(mine_kernel, side, part, half, scale),
-        [vmem((half, chans), jnp.float32)],
-        [cols, cot_full],
+        functools.partial(half_kernel, side, part, scale, 0, (0, 1, 2, 3)),
+        [vmem((9 * part // 2, chans), jnp.float32)],
+        [cols, tall],
         scratch=[pltpu.VMEM((part, chans), jnp.float32)],
-        flops=flops // 2,
-    )
-
+        costed=False,
+    )
     mates, mine, rim_mate = lax.optimization_barrier((mates, mine, by_mask(rim, 1, count)))
     near = [near, mates]
 
@@ -648,16 +645,15 @@
     held, *send = call(
         functools.partial(border_kernel, side, part, chunk, scale, len(near)),
         [vmem((size, chans), jnp.float32)] + [vmem((size, chans), half_bytes)] * (len(masks) - 1),
-        [*near, border_pick, mine, rim, rim_mate, *[by_mask(v, 1, count) for v in send]],
+        [*near, border_pick, mine, rim, rim_mate, by_mask(first, 1, count), by_mask(second, 1, count)],
         scratch=[pltpu.VMEM((48 * side, part), half_bytes), pltpu.VMEM((half, chans), jnp.float32)],
     )
-    send, cot_full, near = lax.optimization_barrier((send, cot_full, near))
+    send, tall, near = lax.optimization_barrier((send, tall, near))
     got = [by_mask(v, m, count) for v, m in zip(send, masks[1:])]
     inner, pieces = call(
         functools.partial(back_kernel, side, part),
         [vmem((rows, part), jnp.float32), vmem(packed_shape(block, part), half_bytes)],
-        [cot_full, taps],
-        scratch=[pltpu.VMEM((rows + 4 * side, chans), half_bytes)],
+        [tall, taps],
         flops=flops,
     )
     pieces, near = lax.optimization_barrier((pieces, near))

time: 66.4 us -> 65.9 us (level)
    pallas_call x16 -> x17, Pallas kernels: 17.3 us -> 16.8 us  [call(): pl.pallas_call(kernel, out_shape=tuple(outs), in_specs=in_specs, out_spec...]
where the time goes in v10:
time: 65.9 us; the launch traced here: 65.6 us
  starting transfers between devices  26.1 us (40%)
  Pallas kernels  19.2 us (29%)
  waiting for transfers between devices  16.8 us (25%)
  local copies, waits for them, and re-layouts  2.09 us (3%)
  between operations  0.79 us (1%)
  other arithmetic  0.74 us (1%)
    pallas_call x17, Pallas kernels, call(): pl.pallas_call(kernel, out_shape=tuple(outs), in_specs=in_specs, out_spec...  16.8 us
    ppermute x21, starting transfers between devices, by_mask(): return lax.ppermute(value, 'tile', [(i, i ^ mask) for i in range(count)])  14.3 us
    ppermute x21, waiting for transfers between devices, by_mask(): return lax.ppermute(value, 'tile', [(i, i ^ mask) for i in range(count)])  13.2 us
    ppermute x4, starting transfers between devices, by_swap(): return lax.ppermute(value, 'tile', pairs)  7.17 us
    ppermute x4, waiting for transfers between devices, by_swap(): return lax.ppermute(value, 'tile', pairs)  3.53 us
    ppermute x1, starting transfers between devices, body(): cot_other = lax.ppermute(cot_own, 'ch', others)  3 us
    pallas_call x2, Pallas kernels, unfold(): pl.pallas_call(functools.partial(unfold_kernel, whole.shape[0] // 2, chun...  2.41 us
    unnamed x6, local copies, waits for them, and re-layouts  2.09 us
  transfers between devices with their start and end apart: 27, of which 7 were waited for; matrix products, arithmetic and copies ran while one was open for 1% of the time, Pallas kernels for 22%

profile of v10, /device:TPU:0, one launch (start us, length us, event | category | flops | bytes accessed | tf_op | source)
XLA Modules:
  0.0 65.6 jit_solution(16080875791122062809)
XLA Ops:
  0.6 3.0 %collective-permute-start.4 = (bf16[1024,192]{1,0:T(8,128)(2,1)}, bf16[1024,192]{1,0:T(8,128)(2,1)S(1)}, u32[]{:S(2)}, u32[]{:S(2)}) collective-permute-start(bf16[1024,192]{1,0:T(8,128)(2,1)} %bitcast.11), channel_id=1, source_target_pairs={{0,1},{1,0},{2,3},{3,2},{4,5},{5,4},{6,7},{7,6},{8,9},{9,8},{10,11... | collective-permute-start | bytes 1179656 | tf_op jit(solution)/shard_map/ppermute | solution.py:591
  3.6 1.0 %copy-done = bf16[1,32,32,192]{3,2,1,0:T(8,128)(2,1)S(1)} copy-done((bf16[1,32,32,192]{3,2,1,0:T(8,128)(2,1)S(1)}, bf16[1,32,32,192]{3,2,1,0:T(8,128)(2,1)}, u32[]{:S(2)}) %copy-start) | copy-done | bytes 393240
  4.7 0.1 shard_map.94
  4.8 1.6 %collective-permute-start.1 = (bf16[192,128]{1,0:T(8,128)(2,1)S(1)}, bf16[192,128]{1,0:T(8,128)(2,1)S(1)}, u32[]{:S(2)}, u32[]{:S(2)}) collective-permute-start(bf16[192,128]{1,0:T(8,128)(2,1)S(1)} %get-tuple-element.68.refs_0_), channel_id=1, source_target_pairs={{0,8},{2,10},{4,12},{6,14},{8,0},{10,2},{12,4},{14,6},{16,24},{18,... | collective-permute-start | bytes 147464 | tf_op jit(solution)/shard_map/ppermute | solution.py:59
  6.4 2.5 %collective-permute-start.2 = (bf16[192,128]{1,0:T(8,128)(2,1)S(1)}, bf16[192,128]{1,0:T(8,128)(2,1)S(1)}, u32[]{:S(2)}, u32[]{:S(2)}) collective-permute-start(bf16[192,128]{1,0:T(8,128)(2,1)S(1)} %get-tuple-element.68.refs_0_), channel_id=1, source_target_pairs={{0,24},{2,26},{4,28},{6,30},{8,16},{10,18},{12,20},{14,22},{16,8},... | collective-permute-start | bytes 147464 | tf_op jit(solution)/shard_map/ppermute | solution.py:59
  8.9 1.5 %collective-permute-start = (bf16[192,128]{1,0:T(8,128)(2,1)S(1)}, bf16[192,128]{1,0:T(8,128)(2,1)S(1)}, u32[]{:S(2)}, u32[]{:S(2)}) collective-permute-start(bf16[192,128]{1,0:T(8,128)(2,1)S(1)} %get-tuple-element.68.refs_0_), channel_id=1, source_target_pairs={{0,4},{2,6},{4,0},{6,2},{8,12},{10,14},{12,8},{14,10},{16,20},{18,... | collective-permute-start | bytes 147464 | tf_op jit(solution)/shard_map/ppermute | solution.py:63
  10.4 1.9 %collective-permute-done.2.refs_1_.refs_3_ = bf16[192,128]{1,0:T(8,128)(2,1)S(1)} collective-permute-done((bf16[192,128]{1,0:T(8,128)(2,1)S(1)}, bf16[192,128]{1,0:T(8,128)(2,1)S(1)}, u32[]{:S(2)}, u32[]{:S(2)}) %collective-permute-start.2) | collective-permute-done | bytes 49184 | tf_op jit(solution)/shard_map/ppermute | solution.py:59
  12.3 1.6 %collective-permute-start.3 = (bf16[384,128]{1,0:T(8,128)(2,1)S(1)}, bf16[384,128]{1,0:T(8,128)(2,1)S(1)}, u32[]{:S(2)}, u32[]{:S(2)}) collective-permute-start(bf16[384,128]{1,0:T(8,128)(2,1)S(1)} %shard_map.95), channel_id=1, source_target_pairs={{0,4},{2,6},{4,0},{6,2},{8,12},{10,14},{12,8},{14,10},{16,20},{18,... | collective-permute-start | bytes 294920 | tf_op jit(solution)/shard_map/ppermute | solution.py:63
  13.9 0.7 %pad_add_fusion.tables_in.refs_2_ = s32[16,16]{1,0:T(8,128)S(1)} fusion(s32[4,16]{1,0:T(4,128)} %bitcast.17, s32[4,16]{1,0:T(4,128)} %bitcast.18, s32[4,16]{1,0:T(4,128)} %bitcast.19, s32[4,16]{1,0:T(4,128)} %bitcast.20), kind=kLoop, calls=%fused_computation | loop fusion | flops 768 | bytes 2048 | tf_op jit(solution)/shard_map/concatenate | solution.py:599
  14.7 1.0 %copy-done.1 = bf16[1,32,32,192]{3,2,1,0:T(8,128)(2,1)S(1)} copy-done((bf16[1,32,32,192]{3,2,1,0:T(8,128)(2,1)S(1)}, bf16[1,32,32,192]{3,2,1,0:T(8,128)(2,1)}, u32[]{:S(2)}) %copy-start.1) | copy-done | bytes 393240
  15.7 1.1 %shard_map.96 = (bf16[512,1536]{1,0:T(8,128)(2,1)S(1)}, bf16[1024,192]{1,0:T(8,128)(2,1)S(1)}) custom-call(s32[16,16]{1,0:T(8,128)S(1)} %pad_add_fusion.tables_in.refs_2_, bf16[1024,192]{1,0:T(8,128)(2,1)S(1)} %bitcast.12), custom_call_target="tpu_custom_call" | custom-call | bytes 2360320 | tf_op jit(solution)/shard_map/pallas_call | solution.py:110
  16.8 0.2 collective-permute-done.3.refs_4_
  17.0 1.3 %shard_map.98 = (f32[384,384]{1,0:T(8,128)S(1)}, bf16[1152,384]{1,0:T(8,128)(2,1)S(1)}, bf16[128,384]{1,0:T(8,128)(2,1)S(1)}, bf16[3,192,1024]{2,1,0:T(8,128)(2,1)S(1)}) custom-call(bf16[32,32,192]{2,1,0:T(8,128)(2,1)S(1)} %get-tuple-element.73.field_ref.refs_3_, bf16[1024,192]{1,0:T(8,128)(2,1)S(1)} %get-tuple-element.74.own_ref, ...), custom_call_target="tpu_custom_call" | custom-call | flops 339738624 | bytes 3932160 | tf_op jit(solution)/shard_map/pallas_call | solution.py:110
  18.4 0.8 %shard_map.99 = f32[480,384]{1,0:T(8,128)S(1)} custom-call(bf16[3,192,1024]{2,1,0:T(8,128)(2,1)S(1)} %get-tuple-element.76.cols, bf16[1152,384]{1,0:T(8,128)(2,1)S(1)} %get-tuple-element.93.tall), custom_call_target="tpu_custom_call" | custom-call | flops 1358954496 | bytes 2801664 | tf_op jit(solution)/shard_map/pallas_call | solution.py:110
  19.2 0.1 collective-permute-start.8
  19.3 0.5 collective-permute-start.7
  19.8 0.1 collective-permute-start.5
  19.9 0.4 collective-permute-start.6
  20.4 1.2 %shard_map.100.refs_3_ = f32[864,384]{1,0:T(8,128)S(1)} custom-call(bf16[3,192,1024]{2,1,0:T(8,128)(2,1)S(1)} %get-tuple-element.76.cols, bf16[1152,384]{1,0:T(8,128)(2,1)S(1)} %get-tuple-element.93.tall), custom_call_target="tpu_custom_call" | custom-call | tf_op jit(solution)/shard_map/pallas_call | solution.py:110
  21.6 0.0 copy-start.2
  21.6 1.3 %collective-permute-done.6.refs_5_ = bf16[128,384]{1,0:T(8,128)(2,1)S(1)} collective-permute-done((bf16[128,384]{1,0:T(8,128)(2,1)S(1)}, bf16[128,384]{1,0:T(8,128)(2,1)S(1)}, u32[]{:S(2)}, u32[]{:S(2)}) %collective-permute-start.6) | collective-permute-done | bytes 98336 | tf_op jit(solution)/shard_map/ppermute | solution.py:63
  22.9 1.5 %shard_map.101 = (f32[224,384]{1,0:T(8,128)S(1)}, bf16[224,384]{1,0:T(8,128)(2,1)S(1)}, bf16[224,384]{1,0:T(8,128)(2,1)S(1)}, bf16[224,384]{1,0:T(8,128)(2,1)S(1)}) custom-call(bf16[1152,128]{1,0:T(8,128)(2,1)S(1)} %shard_map.97.refs_0_, bf16[1152,128]{1,0:T(8,128)(2,1)S(1)} %collective-permute-done.5.refs_1_, ...), custom_call_target="tpu_custom_call" | custom-call | bytes 5873664 | tf_op jit(solution)/shard_map/pallas_call | solution.py:110
  24.4 0.6 collective-permute-start.10
  25.1 2.4 %collective-permute-start.11 = (bf16[224,384]{1,0:T(8,128)(2,1)S(1)}, bf16[224,384]{1,0:T(8,128)(2,1)S(1)}, u32[]{:S(2)}, u32[]{:S(2)}) collective-permute-start(bf16[224,384]{1,0:T(8,128)(2,1)S(1)} %get-tuple-element.92), channel_id=1, source_target_pairs={{0,12},{2,14},{4,8},{6,10},{8,4},{10,6},{12,0},{14,2},{16,28},{18,... | collective-permute-start | bytes 516104 | tf_op jit(solution)/shard_map/ppermute | solution.py:63
  27.5 0.5 collective-permute-start.9
  28.0 2.9 %shard_map.102 = (f32[1024,192]{1,0:T(8,128)S(1)}, bf16[216,128]{1,0:T(8,128)(2,1)S(1)}) custom-call(bf16[1152,384]{1,0:T(8,128)(2,1)S(1)} %get-tuple-element.93.tall, bf16[9,384,384]{2,1,0:T(8,128)(2,1)S(1)} %bitcast.13), custom_call_target="tpu_custom_call" | custom-call | flops 1358954496 | bytes 4380672 | tf_op jit(solution)/shard_map/pallas_call | solution.py:110
  30.8 0.6 collective-permute-start.12
  31.4 2.5 %collective-permute-start.13 = (bf16[216,128]{1,0:T(8,128)(2,1)S(1)}, bf16[216,128]{1,0:T(8,128)(2,1)S(1)}, u32[]{:S(2)}, u32[]{:S(2)}) collective-permute-start(bf16[216,128]{1,0:T(8,128)(2,1)S(1)} %get-tuple-element.112.refs_0_), channel_id=1, source_target_pairs={{0,24},{2,26},{4,28},{6,30},{8,16},{10,18},{12,20},{14,22},{16,8},... | collective-permute-start | bytes 165896 | tf_op jit(solution)/shard_map/ppermute | solution.py:59
  33.9 1.2 %shard_map.104.place_ref = bf16[128,1728]{1,0:T(8,128)(2,1)S(1)} custom-call(s32[16,16]{1,0:T(8,128)S(1)} %pad_add_fusion.tables_in.refs_2_), custom_call_target="tpu_custom_call" | custom-call | bytes 443392 | tf_op jit(solution)/shard_map/pallas_call | solution.py:110
  35.1 1.3 %shard_map.103 = (bf16[144,192]{1,0:T(8,128)(2,1)S(1)}, bf16[1752,128]{1,0:T(8,128)(2,1)S(1)}) custom-call(bf16[1152,128]{1,0:T(8,128)(2,1)S(1)} %shard_map.97.refs_0_, bf16[1152,128]{1,0:T(8,128)(2,1)S(1)} %collective-permute-done.5.refs_1_, s32[16,16]{1,0:T(8,128)S(1)} %pad_add_fusion.tables_in.refs_2_, ...), custom_call_target="tpu_custom_call" | custom-call | bytes 1487872 | tf_op jit(solution)/shard_map/pallas_call | solution.py:110
  36.4 1.6 %collective-permute-done.13.refs_2_ = bf16[216,128]{1,0:T(8,128)(2,1)S(1)} collective-permute-done((bf16[216,128]{1,0:T(8,128)(2,1)S(1)}, bf16[216,128]{1,0:T(8,128)(2,1)S(1)}, u32[]{:S(2)}, u32[]{:S(2)}) %collective-permute-start.13) | collective-permute-done | bytes 55328 | tf_op jit(solution)/shard_map/ppermute | solution.py:59
  38.0 1.6 %collective-permute-start.22 = (bf16[1752,128]{1,0:T(8,128)(2,1)S(1)}, bf16[1752,128]{1,0:T(8,128)(2,1)S(1)}, u32[]{:S(2)}, u32[]{:S(2)}) collective-permute-start(bf16[1752,128]{1,0:T(8,128)(2,1)S(1)} %get-tuple-element.123), channel_id=1, source_target_pairs={{0,1},{1,0},{2,3},{3,2},{4,5},{5,4},{6,7},{7,6},{8,9},{9,8},{10,11... | collective-permute-start | bytes 1345544 | tf_op jit(solution)/shard_map/ppermute | solution.py:690
  39.6 0.1 shard_map.105
  39.7 0.6 collective-permute-start.14
  40.3 1.3 %collective-permute-start.16 = (bf16[648,128]{1,0:T(8,128)(2,1)S(1)}, bf16[648,128]{1,0:T(8,128)(2,1)S(1)}, u32[]{:S(2)}, u32[]{:S(2)}) collective-permute-start(bf16[648,128]{1,0:T(8,128)(2,1)S(1)} %shard_map.106.refs_0_), channel_id=1, source_target_pairs={{0,4},{2,6},{4,0},{6,2},{8,12},{10,14},{12,8},{14,10},{16,20},{18,... | collective-permute-start | bytes 497672 | tf_op jit(solution)/shard_map/ppermute | solution.py:63
  41.5 3.6 %collective-permute-done.14.refs_1_ = bf16[112,384]{1,0:T(8,128)(2,1)S(1)} collective-permute-done((bf16[112,384]{1,0:T(8,128)(2,1)S(1)}, bf16[112,384]{1,0:T(8,128)(2,1)S(1)}, u32[]{:S(2)}, u32[]{:S(2)}) %collective-permute-start.14) | collective-permute-done | bytes 86048 | tf_op jit(solution)/shard_map/ppermute | solution.py:63
  45.2 0.6 collective-permute-start.15
  45.8 5.2 %collective-permute-done.15.refs_1_ = bf16[112,384]{1,0:T(8,128)(2,1)S(1)} collective-permute-done((bf16[112,384]{1,0:T(8,128)(2,1)S(1)}, bf16[112,384]{1,0:T(8,128)(2,1)S(1)}, u32[]{:S(2)}, u32[]{:S(2)}) %collective-permute-start.15) | collective-permute-done | bytes 86048 | tf_op jit(solution)/shard_map/ppermute | solution.py:63
  50.9 1.3 %collective-permute-start.17 = (bf16[224,384]{1,0:T(8,128)(2,1)S(1)}, bf16[224,384]{1,0:T(8,128)(2,1)S(1)}, u32[]{:S(2)}, u32[]{:S(2)}) collective-permute-start(bf16[224,384]{1,0:T(8,128)(2,1)S(1)} %shard_map.108.refs_0_), channel_id=1, source_target_pairs={{0,4},{2,6},{4,0},{6,2},{8,12},{10,14},{12,8},{14,10},{16,20},{18,... | collective-permute-start | bytes 516104 | tf_op jit(solution)/shard_map/ppermute | solution.py:63
  52.2 2.3 %collective-permute-start.19 = (bf16[224,384]{1,0:T(8,128)(2,1)S(1)}, bf16[224,384]{1,0:T(8,128)(2,1)S(1)}, u32[]{:S(2)}, u32[]{:S(2)}) collective-permute-start(bf16[224,384]{1,0:T(8,128)(2,1)S(1)} %shard_map.108.refs_0_), channel_id=1, source_target_pairs={{0,12},{2,14},{4,8},{6,10},{8,4},{10,6},{12,0},{14,2},{16,28},{18,... | collective-permute-start | bytes 516104 | tf_op jit(solution)/shard_map/ppermute | solution.py:63
  54.5 1.3 %shard_map.109 = bf16[1024,192]{1,0:T(8,128)(2,1)} custom-call(bf16[128,1728]{1,0:T(8,128)(2,1)S(1)} %shard_map.104.place_ref, f32[1024,192]{1,0:T(8,128)S(1)} %get-tuple-element.119.inner_ref, bf16[648,128]{1,0:T(8,128)(2,1)S(1)} %shard_map.106.refs_0_, bf16[648,128]{1,0:T(8,128)(2,1)S(1)} %collective-permute-done.16.refs_1_, ...), custom_call_target="tpu_custom_call" | custom-call | bytes 2285568 | tf_op jit(solution)/shard_map/pallas_call | solution.py:110
  55.8 3.9 %shard_map.110 = bf16[1024,192]{1,0:T(8,128)(2,1)} custom-call(bf16[32,32,192]{2,1,0:T(8,128)(2,1)S(1)} %get-tuple-element.73.field_ref.refs_3_, bf16[144,192]{1,0:T(8,128)(2,1)S(1)} %get-tuple-element.122.halos_ref, bf16[1752,128]{1,0:T(8,128)(2,1)S(1)} %collective-permute-done.22.other_ref, bf16[9,384,384]{2,1,0:T(8,128)(2,1)S(1)} %bitcast.14), custom_call_target="tpu_custom_call" | custom-call | flops 2717908992 | bytes 3944448 | tf_op jit(solution)/shard_map/pallas_call | solution.py:110
  59.7 2.9 %collective-permute-done.19.refs_3_ = bf16[224,384]{1,0:T(8,128)(2,1)S(1)} collective-permute-done((bf16[224,384]{1,0:T(8,128)(2,1)S(1)}, bf16[224,384]{1,0:T(8,128)(2,1)S(1)}, u32[]{:S(2)}, u32[]{:S(2)}) %collective-permute-start.19) | collective-permute-done | bytes 172064 | tf_op jit(solution)/shard_map/ppermute | solution.py:63
  62.7 0.5 collective-permute-start.25
  63.2 0.0 collective-permute-start.26
  63.2 1.4 %shard_map.111.refs_0_ = f32[1728,384]{1,0:T(8,128)} custom-call(bf16[224,384]{1,0:T(8,128)(2,1)S(1)} %shard_map.108.refs_0_, bf16[224,384]{1,0:T(8,128)(2,1)S(1)} %collective-permute-done.17.refs_1_, bf16[224,384]{1,0:T(8,128)(2,1)S(1)} %collective-permute-done.18.refs_2_, bf16[224,384]{1,0:T(8,128)(2,1)S(1)} %collective-permute-done.19.refs_3_, ...), custom_call_target="tpu_custom_call" | custom-call | tf_op jit(solution)/shard_map/pallas_call | solution.py:445
  64.6 0.0 collective-permute-done.26.refs_3_
  64.6 1.1 %shard_map.112 = f32[1728,384]{1,0:T(8,128)} custom-call(f32[1728,384]{1,0:T(8,128)} %shard_map.111.refs_0_, bf16[224,384]{1,0:T(8,128)(2,1)S(1)} %collective-permute-done.24.refs_1_, bf16[224,384]{1,0:T(8,128)(2,1)S(1)} %collective-permute-done.25.refs_2_, bf16[224,384]{1,0:T(8,128)(2,1)S(1)} %collective-permute-done.26.refs_3_), custom_call_target="tpu_custom_call", output_to_operand_aliasing={{}: (0, {})} | custom-call | tf_op jit(solution)/shard_map/pallas_call | solution.py:445
  (32 shorter events, 0.1 us)
Async XLA Ops:
  0.6 16.4 %collective-permute-start.4 = (bf16[1024,192]{1,0:T(8,128)(2,1)}, bf16[1024,192]{1,0:T(8,128)(2,1)S(1)}, u32[]{:S(2)}, u32[]{:S(2)}) collective-permute-start(bf16[1024,192]{1,0:T(8,128)(2,1)} %bitcast.11), channel_id=1, source_target_pairs={{0,1},{1,0},{2,3},{3,2},{4,5},{5,4},{6,7},{7,6},{8,9},{9,8},{10,11... | collective-permute-start | bytes 1179656 | tf_op jit(solution)/shard_map/ppermute | solution.py:591
  3.6 1.0 %copy-start = (bf16[1,32,32,192]{3,2,1,0:T(8,128)(2,1)S(1)}, bf16[1,32,32,192]{3,2,1,0:T(8,128)(2,1)}, u32[]{:S(2)}) copy-start(bf16[1,32,32,192]{3,2,1,0:T(8,128)(2,1)} %param.7) | copy-start | bytes 1179652
  4.8 5.6 %collective-permute-start.1 = (bf16[192,128]{1,0:T(8,128)(2,1)S(1)}, bf16[192,128]{1,0:T(8,128)(2,1)S(1)}, u32[]{:S(2)}, u32[]{:S(2)}) collective-permute-start(bf16[192,128]{1,0:T(8,128)(2,1)S(1)} %get-tuple-element.68.refs_0_), channel_id=1, source_target_pairs={{0,8},{2,10},{4,12},{6,14},{8,0},{10,2},{12,4},{14,6},{16,24},{18,... | collective-permute-start | bytes 147464 | tf_op jit(solution)/shard_map/ppermute | solution.py:59
  6.4 5.9 %collective-permute-start.2 = (bf16[192,128]{1,0:T(8,128)(2,1)S(1)}, bf16[192,128]{1,0:T(8,128)(2,1)S(1)}, u32[]{:S(2)}, u32[]{:S(2)}) collective-permute-start(bf16[192,128]{1,0:T(8,128)(2,1)S(1)} %get-tuple-element.68.refs_0_), channel_id=1, source_target_pairs={{0,24},{2,26},{4,28},{6,30},{8,16},{10,18},{12,20},{14,22},{16,8},... | collective-permute-start | bytes 147464 | tf_op jit(solution)/shard_map/ppermute | solution.py:59
  8.9 7.9 %collective-permute-start = (bf16[192,128]{1,0:T(8,128)(2,1)S(1)}, bf16[192,128]{1,0:T(8,128)(2,1)S(1)}, u32[]{:S(2)}, u32[]{:S(2)}) collective-permute-start(bf16[192,128]{1,0:T(8,128)(2,1)S(1)} %get-tuple-element.68.refs_0_), channel_id=1, source_target_pairs={{0,4},{2,6},{4,0},{6,2},{8,12},{10,14},{12,8},{14,10},{16,20},{18,... | collective-permute-start | bytes 147464 | tf_op jit(solution)/shard_map/ppermute | solution.py:63
  12.3 4.7 %collective-permute-start.3 = (bf16[384,128]{1,0:T(8,128)(2,1)S(1)}, bf16[384,128]{1,0:T(8,128)(2,1)S(1)}, u32[]{:S(2)}, u32[]{:S(2)}) collective-permute-start(bf16[384,128]{1,0:T(8,128)(2,1)S(1)} %shard_map.95), channel_id=1, source_target_pairs={{0,4},{2,6},{4,0},{6,2},{8,12},{10,14},{12,8},{14,10},{16,20},{18,... | collective-permute-start | bytes 294920 | tf_op jit(solution)/shard_map/ppermute | solution.py:63
  14.7 1.0 %copy-start.1 = (bf16[1,32,32,192]{3,2,1,0:T(8,128)(2,1)S(1)}, bf16[1,32,32,192]{3,2,1,0:T(8,128)(2,1)}, u32[]{:S(2)}) copy-start(bf16[1,32,32,192]{3,2,1,0:T(8,128)(2,1)} %param.9) | copy-start | bytes 1179652
  19.2 3.7 %collective-permute-start.8 = (f32[480,384]{1,0:T(8,128)S(1)}, f32[480,384]{1,0:T(8,128)S(1)}, u32[]{:S(2)}, u32[]{:S(2)}) collective-permute-start(f32[480,384]{1,0:T(8,128)S(1)} %shard_map.99), channel_id=1, source_target_pairs={{0,2},{2,0},{4,6},{6,4},{8,10},{10,8},{12,14},{14,12},{16,18},{18,... | collective-permute-start | bytes 2211848 | tf_op jit(solution)/shard_map/ppermute | solution.py:63
  19.3 3.6 %collective-permute-start.7 = (f32[384,384]{1,0:T(8,128)S(1)}, f32[384,384]{1,0:T(8,128)S(1)}, u32[]{:S(2)}, u32[]{:S(2)}) collective-permute-start(f32[384,384]{1,0:T(8,128)S(1)} %get-tuple-element.84), channel_id=1, source_target_pairs={{0,2},{2,0},{4,6},{6,4},{8,10},{10,8},{12,14},{14,12},{16,18},{18,... | collective-permute-start | bytes 1769480 | tf_op jit(solution)/shard_map/ppermute | solution.py:63
  19.8 3.1 %collective-permute-start.5 = (bf16[1152,128]{1,0:T(8,128)(2,1)S(1)}, bf16[1152,128]{1,0:T(8,128)(2,1)S(1)}, u32[]{:S(2)}, u32[]{:S(2)}) collective-permute-start(bf16[1152,128]{1,0:T(8,128)(2,1)S(1)} %shard_map.97.refs_0_), channel_id=1, source_target_pairs={{0,2},{2,0},{4,6},{6,4},{8,10},{10,8},{12,14},{14,12},{16,18},{18,... | collective-permute-start | bytes 884744 | tf_op jit(solution)/shard_map/ppermute | solution.py:63
  19.9 2.9 %collective-permute-start.6 = (bf16[128,384]{1,0:T(8,128)(2,1)S(1)}, bf16[128,384]{1,0:T(8,128)(2,1)S(1)}, u32[]{:S(2)}, u32[]{:S(2)}) collective-permute-start(bf16[128,384]{1,0:T(8,128)(2,1)S(1)} %get-tuple-element.79.refs_4_), channel_id=1, source_target_pairs={{0,2},{2,0},{4,6},{6,4},{8,10},{10,8},{12,14},{14,12},{16,18},{18,... | collective-permute-start | bytes 294920 | tf_op jit(solution)/shard_map/ppermute | solution.py:63
  21.6 6.4 %copy-start.2 = (bf16[3,3,384,384]{3,2,1,0:T(8,128)(2,1)S(1)}, bf16[3,3,384,384]{3,2,1,0:T(8,128)(2,1)}, u32[]{:S(2)}) copy-start(bf16[3,3,384,384]{3,2,1,0:T(8,128)(2,1)} %param.8) | copy-start | bytes 7962628
  24.4 13.6 %collective-permute-start.10 = (bf16[224,384]{1,0:T(8,128)(2,1)S(1)}, bf16[224,384]{1,0:T(8,128)(2,1)S(1)}, u32[]{:S(2)}, u32[]{:S(2)}) collective-permute-start(bf16[224,384]{1,0:T(8,128)(2,1)S(1)} %get-tuple-element.91), channel_id=1, source_target_pairs={{0,8},{2,10},{4,12},{6,14},{8,0},{10,2},{12,4},{14,6},{16,24},{18,... | collective-permute-start | bytes 516104 | tf_op jit(solution)/shard_map/ppermute | solution.py:63
  25.1 13.0 %collective-permute-start.11 = (bf16[224,384]{1,0:T(8,128)(2,1)S(1)}, bf16[224,384]{1,0:T(8,128)(2,1)S(1)}, u32[]{:S(2)}, u32[]{:S(2)}) collective-permute-start(bf16[224,384]{1,0:T(8,128)(2,1)S(1)} %get-tuple-element.92), channel_id=1, source_target_pairs={{0,12},{2,14},{4,8},{6,10},{8,4},{10,6},{12,0},{14,2},{16,28},{18,... | collective-permute-start | bytes 516104 | tf_op jit(solution)/shard_map/ppermute | solution.py:63
  27.5 10.6 %collective-permute-start.9 = (bf16[224,384]{1,0:T(8,128)(2,1)S(1)}, bf16[224,384]{1,0:T(8,128)(2,1)S(1)}, u32[]{:S(2)}, u32[]{:S(2)}) collective-permute-start(bf16[224,384]{1,0:T(8,128)(2,1)S(1)} %get-tuple-element.90), channel_id=1, source_target_pairs={{0,4},{2,6},{4,0},{6,2},{8,12},{10,14},{12,8},{14,10},{16,20},{18,... | collective-permute-start | bytes 516104 | tf_op jit(solution)/shard_map/ppermute | solution.py:63
  30.8 5.5 %collective-permute-start.12 = (bf16[216,128]{1,0:T(8,128)(2,1)S(1)}, bf16[216,128]{1,0:T(8,128)(2,1)S(1)}, u32[]{:S(2)}, u32[]{:S(2)}) collective-permute-start(bf16[216,128]{1,0:T(8,128)(2,1)S(1)} %get-tuple-element.112.refs_0_), channel_id=1, source_target_pairs={{0,8},{2,10},{4,12},{6,14},{8,0},{10,2},{12,4},{14,6},{16,24},{18,... | collective-permute-start | bytes 165896 | tf_op jit(solution)/shard_map/ppermute | solution.py:59
  31.4 6.6 %collective-permute-start.13 = (bf16[216,128]{1,0:T(8,128)(2,1)S(1)}, bf16[216,128]{1,0:T(8,128)(2,1)S(1)}, u32[]{:S(2)}, u32[]{:S(2)}) collective-permute-start(bf16[216,128]{1,0:T(8,128)(2,1)S(1)} %get-tuple-element.112.refs_0_), channel_id=1, source_target_pairs={{0,24},{2,26},{4,28},{6,30},{8,16},{10,18},{12,20},{14,22},{16,8},... | collective-permute-start | bytes 165896 | tf_op jit(solution)/shard_map/ppermute | solution.py:59
  38.0 17.8 %collective-permute-start.22 = (bf16[1752,128]{1,0:T(8,128)(2,1)S(1)}, bf16[1752,128]{1,0:T(8,128)(2,1)S(1)}, u32[]{:S(2)}, u32[]{:S(2)}) collective-permute-start(bf16[1752,128]{1,0:T(8,128)(2,1)S(1)} %get-tuple-element.123), channel_id=1, source_target_pairs={{0,1},{1,0},{2,3},{3,2},{4,5},{5,4},{6,7},{7,6},{8,9},{9,8},{10,11... | collective-permute-start | bytes 1345544 | tf_op jit(solution)/shard_map/ppermute | solution.py:690
  39.7 5.4 %collective-permute-start.14 = (bf16[112,384]{1,0:T(8,128)(2,1)S(1)}, bf16[112,384]{1,0:T(8,128)(2,1)S(1)}, u32[]{:S(2)}, u32[]{:S(2)}) collective-permute-start(bf16[112,384]{1,0:T(8,128)(2,1)S(1)} %get-tuple-element.111), channel_id=1, source_target_pairs={{0,16},{2,18},{4,20},{6,22},{8,24},{10,26},{12,28},{14,30},{16,0},... | collective-permute-start | bytes 258056 | tf_op jit(solution)/shard_map/ppermute | solution.py:63
  40.3 5.5 %collective-permute-start.16 = (bf16[648,128]{1,0:T(8,128)(2,1)S(1)}, bf16[648,128]{1,0:T(8,128)(2,1)S(1)}, u32[]{:S(2)}, u32[]{:S(2)}) collective-permute-start(bf16[648,128]{1,0:T(8,128)(2,1)S(1)} %shard_map.106.refs_0_), channel_id=1, source_target_pairs={{0,4},{2,6},{4,0},{6,2},{8,12},{10,14},{12,8},{14,10},{16,20},{18,... | collective-permute-start | bytes 497672 | tf_op jit(solution)/shard_map/ppermute | solution.py:63
  45.2 5.8 %collective-permute-start.15 = (bf16[112,384]{1,0:T(8,128)(2,1)S(1)}, bf16[112,384]{1,0:T(8,128)(2,1)S(1)}, u32[]{:S(2)}, u32[]{:S(2)}) collective-permute-start(bf16[112,384]{1,0:T(8,128)(2,1)S(1)} %shard_map.107.refs_0_), channel_id=1, source_target_pairs={{0,16},{2,18},{4,20},{6,22},{8,24},{10,26},{12,28},{14,30},{16,0},... | collective-permute-start | bytes 258056 | tf_op jit(solution)/shard_map/ppermute | solution.py:63
  45.8 6.5 %collective-permute-start.20 = (bf16[648,128]{1,0:T(8,128)(2,1)S(1)}, bf16[648,128]{1,0:T(8,128)(2,1)S(1)}, u32[]{:S(2)}, u32[]{:S(2)}) collective-permute-start(bf16[648,128]{1,0:T(8,128)(2,1)S(1)} %shard_map.106.refs_0_), channel_id=1, source_target_pairs={{0,2},{2,0},{4,6},{6,4},{8,10},{10,8},{12,14},{14,12},{16,18},{18,... | collective-permute-start | bytes 497672 | tf_op jit(solution)/shard_map/ppermute | solution.py:63
  50.9 3.6 %collective-permute-start.21 = (bf16[648,128]{1,0:T(8,128)(2,1)S(1)}, bf16[648,128]{1,0:T(8,128)(2,1)S(1)}, u32[]{:S(2)}, u32[]{:S(2)}) collective-permute-start(bf16[648,128]{1,0:T(8,128)(2,1)S(1)} %collective-permute-done.16.refs_1_), channel_id=1, source_target_pairs={{0,2},{2,0},{4,6},{6,4},{8,10},{10,8},{12,14},{14,12},{16,18},{18,... | collective-permute-start | bytes 497672 | tf_op jit(solution)/shard_map/ppermute | solution.py:63
  50.9 8.8 %collective-permute-start.17 = (bf16[224,384]{1,0:T(8,128)(2,1)S(1)}, bf16[224,384]{1,0:T(8,128)(2,1)S(1)}, u32[]{:S(2)}, u32[]{:S(2)}) collective-permute-start(bf16[224,384]{1,0:T(8,128)(2,1)S(1)} %shard_map.108.refs_0_), channel_id=1, source_target_pairs={{0,4},{2,6},{4,0},{6,2},{8,12},{10,14},{12,8},{14,10},{16,20},{18,... | collective-permute-start | bytes 516104 | tf_op jit(solution)/shard_map/ppermute | solution.py:63
  52.2 7.5 %collective-permute-start.18 = (bf16[224,384]{1,0:T(8,128)(2,1)S(1)}, bf16[224,384]{1,0:T(8,128)(2,1)S(1)}, u32[]{:S(2)}, u32[]{:S(2)}) collective-permute-start(bf16[224,384]{1,0:T(8,128)(2,1)S(1)} %shard_map.108.refs_0_), channel_id=1, source_target_pairs={{0,8},{2,10},{4,12},{6,14},{8,0},{10,2},{12,4},{14,6},{16,24},{18,... | collective-permute-start | bytes 516104 | tf_op jit(solution)/shard_map/ppermute | solution.py:63
  52.2 10.4 %collective-permute-start.19 = (bf16[224,384]{1,0:T(8,128)(2,1)S(1)}, bf16[224,384]{1,0:T(8,128)(2,1)S(1)}, u32[]{:S(2)}, u32[]{:S(2)}) collective-permute-start(bf16[224,384]{1,0:T(8,128)(2,1)S(1)} %shard_map.108.refs_0_), channel_id=1, source_target_pairs={{0,12},{2,14},{4,8},{6,10},{8,4},{10,6},{12,0},{14,2},{16,28},{18,... | collective-permute-start | bytes 516104 | tf_op jit(solution)/shard_map/ppermute | solution.py:63
  54.5 8.7 %collective-permute-start.23 = (bf16[224,384]{1,0:T(8,128)(2,1)S(1)}, bf16[224,384]{1,0:T(8,128)(2,1)S(1)}, u32[]{:S(2)}, u32[]{:S(2)}) collective-permute-start(bf16[224,384]{1,0:T(8,128)(2,1)S(1)} %shard_map.108.refs_0_), channel_id=1, source_target_pairs={{0,2},{2,0},{4,6},{6,4},{8,10},{10,8},{12,14},{14,12},{16,18},{18,... | collective-permute-start | bytes 516104 | tf_op jit(solution)/shard_map/ppermute | solution.py:63
  62.7 1.9 %collective-permute-start.24 = (bf16[224,384]{1,0:T(8,128)(2,1)S(1)}, bf16[224,384]{1,0:T(8,128)(2,1)S(1)}, u32[]{:S(2)}, u32[]{:S(2)}) collective-permute-start(bf16[224,384]{1,0:T(8,128)(2,1)S(1)} %collective-permute-done.17.refs_1_), channel_id=1, source_target_pairs={{0,2},{2,0},{4,6},{6,4},{8,10},{10,8},{12,14},{14,12},{16,18},{18,... | collective-permute-start | bytes 516104 | tf_op jit(solution)/shard_map/ppermute | solution.py:63
  62.7 1.9 %collective-permute-start.25 = (bf16[224,384]{1,0:T(8,128)(2,1)S(1)}, bf16[224,384]{1,0:T(8,128)(2,1)S(1)}, u32[]{:S(2)}, u32[]{:S(2)}) collective-permute-start(bf16[224,384]{1,0:T(8,128)(2,1)S(1)} %collective-permute-done.18.refs_2_), channel_id=1, source_target_pairs={{0,2},{2,0},{4,6},{6,4},{8,10},{10,8},{12,14},{14,12},{16,18},{18,... | collective-permute-start | bytes 516104 | tf_op jit(solution)/shard_map/ppermute | solution.py:63
  63.2 1.4 %collective-permute-start.26 = (bf16[224,384]{1,0:T(8,128)(2,1)S(1)}, bf16[224,384]{1,0:T(8,128)(2,1)S(1)}, u32[]{:S(2)}, u32[]{:S(2)}) collective-permute-start(bf16[224,384]{1,0:T(8,128)(2,1)S(1)} %collective-permute-done.19.refs_3_), channel_id=1, source_target_pairs={{0,2},{2,0},{4,6},{6,4},{8,10},{10,8},{12,14},{14,12},{16,18},{18,... | collective-permute-start | bytes 516104 | tf_op jit(solution)/shard_map/ppermute | solution.py:63

commit v11 on v10

--- a/solution.py
+++ b/solution.py
@@ -393,6 +393,13 @@
         for ref in got_refs:
             value = value + ref[here, :].astype(jnp.float32)
         outs[index][...] = value.astype(outs[index].dtype)
+
+
+def exchange_kernel(held_ref, got_ref, out_ref):
+    half = held_ref.shape[0] // 2
+    for a, b in ((0, half), (half, 0)):
+        value = held_ref[a : a + half, :].astype(jnp.float32) + got_ref[b : b + half, :].astype(jnp.float32)
+        out_ref[a : a + half, :] = value.astype(out_ref.dtype)
 
 
 def join_kernel(*refs):
@@ -673,7 +680,16 @@
     got, here, inner, halos, packet, place = lax.optimization_barrier(
         (got, here, inner, halos, packet, place)
     )
-    for index, bits in enumerate(stages[2:]):
+    swap = len(stages[-1]) == 1 and len(stages) > 2
+    rs_stages = stages[2:-1] if swap else stages[2:]
+    aside = [here, packet]
+
+    def start_aside(send, aside):
+        send, here, packet = lax.optimization_barrier((send, *aside))
+        (here,) = call(join_kernel, [vmem((3 * pieces.shape[0], pieces.shape[1]), half_bytes)], here)
+        return send, here, by_mask(here, 2, count), lax.ppermute(packet, "ch", others)
+
+    for index, bits in enumerate(rs_stages):
         masks = group_masks(bits)
         size = held.shape[0] // len(masks)
         held, *send = call(
@@ -682,47 +698,50 @@
             [held, *got],
         )
         if index == 0:
-            send, here = lax.optimization_barrier((send, here))
+            send, here, beside, other_field = start_aside(send, aside)
         got = [by_mask(v, m, count) for v, m in zip(send, masks[1:])]
-        if index == 0:
-            (here,) = call(join_kernel, [vmem((3 * pieces.shape[0], pieces.shape[1]), half_bytes)], here)
-            beside = by_mask(here, 2, count)
-            other_field = lax.ppermute(packet, "ch", others)
-            got, here = lax.optimization_barrier((got, here))
     (held,) = call(functools.partial(sum_kernel, len(got), 1), [vmem(held.shape, half_bytes)], [held, *got])
-    order = [0]
-    for index, bits in enumerate(stages[:0:-1]):
+    def add_halos(here, beside):
+        got_pieces = [here, beside, by_mask(here, 1, count), by_mask(beside, 1, count)]
+        return call(
+            functools.partial(add_halo_kernel, side, part),
+            [vmem((rows, part), half_bytes)],
+            [place, inner, *got_pieces],
+            scratch=[pltpu.VMEM((12 * block, part), half_bytes)],
+        )[0]
+
+    if swap:
+        if not rs_stages:
+            held, here, beside, other_field = start_aside(held, aside)
+        got = by_mask(held, stages[-1][0], count)
+        got, grad_features = lax.optimization_barrier((got, add_halos(here, beside)))
+        (held,) = call(exchange_kernel, [vmem(held.shape, half_bytes)], [held, got])
+    else:
+        grad_features = add_halos(here, beside)
+    order = [0] if not swap else [0, stages[-1][0]]
+    ag_stages = stages[-2:0:-1] if swap else stages[:0:-1]
+    for index, bits in enumerate(ag_stages):
         masks = group_masks(bits)
         got = [by_mask(held, m, count) for m in masks[1:]]
-        if index == 0:
-            held, got, beside = lax.optimization_barrier((held, got, beside))
-        if index < len(stages) - 2:
+        if index < len(ag_stages) - 1:
             order = [m + v for m in masks for v in order]
             (held,) = call(
                 join_kernel, [vmem((held.shape[0] * len(masks), chans), half_bytes)], [held, *got]
             )
-            continue
-        got_pieces = [here, beside, by_mask(here, 1, count), by_mask(beside, 1, count)]
-        (grad_features,) = call(
-            functools.partial(add_halo_kernel, side, part),
-            [vmem((rows, part), half_bytes)],
-            [place, inner, *got_pieces],
-            scratch=[pltpu.VMEM((12 * block, part), half_bytes)],
-        )
-        (output,) = call(
-            functools.partial(output_kernel, side, part),
-            [vmem((rows, part), half_bytes)],
-            [field, halos, other_field, taps],
-            scratch=[
-                pltpu.VMEM((3, flat, part), half_bytes),
-                pltpu.VMEM((3, flat, part), half_bytes),
-                pltpu.VMEM((rows + block, part), half_bytes),
-            ],
-            flops=2 * flops,
-        )
-        got, grad_features, output = lax.optimization_barrier((got, grad_features, output))
-        got = [held, *got]
-        order = [[m + v for v in order] for m in masks]
+    order = [[m + v for v in order] for m in masks]
+    (output,) = call(
+        functools.partial(output_kernel, side, part),
+        [vmem((rows, part), half_bytes)],
+        [field, halos, other_field, taps],
+        scratch=[
+            pltpu.VMEM((3, flat, part), half_bytes),
+            pltpu.VMEM((3, flat, part), half_bytes),
+            pltpu.VMEM((rows + block, part), half_bytes),
+        ],
+        flops=2 * flops,
+    )
+    got, grad_features, output = lax.optimization_barrier((got, grad_features, output))
+    got = [held, *got]
     mates = [by_mask(v, 1, count) for v in got]
     whole = vmem((9 * part, chans), jnp.float32)
     own = len(got)

time: 65.9 us -> 62.9 us (0.954)
  waiting for transfers between devices: 16.8 us -> 14.4 us
  starting transfers between devices: 26.1 us -> 25.4 us
    ppermute x21 -> x20, waiting for transfers between devices: 13.2 us -> 10.9 us  [by_mask(): return lax.ppermute(value, 'tile', [(i, i ^ mask) for i in range(count)])]
    ppermute x21 -> x20, starting transfers between devices: 14.3 us -> 13.6 us  [by_mask(): return lax.ppermute(value, 'tile', [(i, i ^ mask) for i in range(count)])]
    pallas_call x17 -> x16, Pallas kernels: 16.8 us -> 16.8 us  [call(): pl.pallas_call(kernel, out_shape=tuple(outs), in_specs=in_specs, out_spec...]
  transfers between devices with their start and end apart: 27 -> 26, of which waited for: 7 -> 9; matrix products, arithmetic and copies ran while one was open for 1% -> 1% of each run, Pallas kernels for 22% -> 23%
where the time goes in v11:
time: 62.9 us; the launch traced here: 62.7 us
  starting transfers between devices  25.4 us (40%)
  Pallas kernels  19.2 us (31%)
  waiting for transfers between devices  14.4 us (23%)
  local copies, waits for them, and re-layouts  2.09 us (3%)
  between operations  0.79 us (1%)
  other arithmetic  0.74 us (1%)
    pallas_call x16, Pallas kernels, call(): pl.pallas_call(kernel, out_shape=tuple(outs), in_specs=in_specs, out_spec...  16.8 us
    ppermute x20, starting transfers between devices, by_mask(): return lax.ppermute(value, 'tile', [(i, i ^ mask) for i in range(count)])  13.6 us
    ppermute x20, waiting for transfers between devices, by_mask(): return lax.ppermute(value, 'tile', [(i, i ^ mask) for i in range(count)])  10.9 us
    ppermute x4, starting transfers between devices, by_swap(): return lax.ppermute(value, 'tile', pairs)  7.17 us
    ppermute x4, waiting for transfers between devices, by_swap(): return lax.ppermute(value, 'tile', pairs)  3.53 us
    ppermute x1, starting transfers between devices, body(): cot_other = lax.ppermute(cot_own, 'ch', others)  3 us
    pallas_call x2, Pallas kernels, unfold(): pl.pallas_call(functools.partial(unfold_kernel, whole.shape[0] // 2, chun...  2.41 us
    unnamed x6, local copies, waits for them, and re-layouts  2.09 us
  transfers between devices with their start and end apart: 26, of which 9 were waited for; matrix products, arithmetic and copies ran while one was open for 1% of the time, Pallas kernels for 23%

profile of v11, /device:TPU:0, one launch (start us, length us, event | category | flops | bytes accessed | tf_op | source)
XLA Modules:
  0.0 62.7 jit_solution(13784762836919176986)
XLA Ops:
  0.6 3.0 %collective-permute-start.4 = (bf16[1024,192]{1,0:T(8,128)(2,1)}, bf16[1024,192]{1,0:T(8,128)(2,1)S(1)}, u32[]{:S(2)}, u32[]{:S(2)}) collective-permute-start(bf16[1024,192]{1,0:T(8,128)(2,1)} %bitcast.11), channel_id=1, source_target_pairs={{0,1},{1,0},{2,3},{3,2},{4,5},{5,4},{6,7},{7,6},{8,9},{9,8},{10,11... | collective-permute-start | bytes 1179656 | tf_op jit(solution)/shard_map/ppermute | solution.py:598
  3.6 1.0 %copy-done = bf16[1,32,32,192]{3,2,1,0:T(8,128)(2,1)S(1)} copy-done((bf16[1,32,32,192]{3,2,1,0:T(8,128)(2,1)S(1)}, bf16[1,32,32,192]{3,2,1,0:T(8,128)(2,1)}, u32[]{:S(2)}) %copy-start) | copy-done | bytes 393240
  4.7 0.1 shard_map.94
  4.8 1.6 %collective-permute-start.1 = (bf16[192,128]{1,0:T(8,128)(2,1)S(1)}, bf16[192,128]{1,0:T(8,128)(2,1)S(1)}, u32[]{:S(2)}, u32[]{:S(2)}) collective-permute-start(bf16[192,128]{1,0:T(8,128)(2,1)S(1)} %get-tuple-element.64.refs_0_), channel_id=1, source_target_pairs={{0,8},{2,10},{4,12},{6,14},{8,0},{10,2},{12,4},{14,6},{16,24},{18,... | collective-permute-start | bytes 147464 | tf_op jit(solution)/shard_map/ppermute | solution.py:59
  6.4 2.5 %collective-permute-start.2 = (bf16[192,128]{1,0:T(8,128)(2,1)S(1)}, bf16[192,128]{1,0:T(8,128)(2,1)S(1)}, u32[]{:S(2)}, u32[]{:S(2)}) collective-permute-start(bf16[192,128]{1,0:T(8,128)(2,1)S(1)} %get-tuple-element.64.refs_0_), channel_id=1, source_target_pairs={{0,24},{2,26},{4,28},{6,30},{8,16},{10,18},{12,20},{14,22},{16,8},... | collective-permute-start | bytes 147464 | tf_op jit(solution)/shard_map/ppermute | solution.py:59
  8.9 1.5 %collective-permute-start = (bf16[192,128]{1,0:T(8,128)(2,1)S(1)}, bf16[192,128]{1,0:T(8,128)(2,1)S(1)}, u32[]{:S(2)}, u32[]{:S(2)}) collective-permute-start(bf16[192,128]{1,0:T(8,128)(2,1)S(1)} %get-tuple-element.64.refs_0_), channel_id=1, source_target_pairs={{0,4},{2,6},{4,0},{6,2},{8,12},{10,14},{12,8},{14,10},{16,20},{18,... | collective-permute-start | bytes 147464 | tf_op jit(solution)/shard_map/ppermute | solution.py:63
  10.4 1.9 %collective-permute-done.2.refs_1_.refs_3_ = bf16[192,128]{1,0:T(8,128)(2,1)S(1)} collective-permute-done((bf16[192,128]{1,0:T(8,128)(2,1)S(1)}, bf16[192,128]{1,0:T(8,128)(2,1)S(1)}, u32[]{:S(2)}, u32[]{:S(2)}) %collective-permute-start.2) | collective-permute-done | bytes 49184 | tf_op jit(solution)/shard_map/ppermute | solution.py:59
  12.3 1.6 %collective-permute-start.3 = (bf16[384,128]{1,0:T(8,128)(2,1)S(1)}, bf16[384,128]{1,0:T(8,128)(2,1)S(1)}, u32[]{:S(2)}, u32[]{:S(2)}) collective-permute-start(bf16[384,128]{1,0:T(8,128)(2,1)S(1)} %shard_map.95), channel_id=1, source_target_pairs={{0,4},{2,6},{4,0},{6,2},{8,12},{10,14},{12,8},{14,10},{16,20},{18,... | collective-permute-start | bytes 294920 | tf_op jit(solution)/shard_map/ppermute | solution.py:63
  13.9 0.7 %pad_add_fusion.tables_in.refs_2_ = s32[16,16]{1,0:T(8,128)S(1)} fusion(s32[4,16]{1,0:T(4,128)} %bitcast.17, s32[4,16]{1,0:T(4,128)} %bitcast.18, s32[4,16]{1,0:T(4,128)} %bitcast.19, s32[4,16]{1,0:T(4,128)} %bitcast.20), kind=kLoop, calls=%fused_computation | loop fusion | flops 768 | bytes 2048 | tf_op jit(solution)/shard_map/concatenate | solution.py:606
  14.7 1.0 %copy-done.1 = bf16[1,32,32,192]{3,2,1,0:T(8,128)(2,1)S(1)} copy-done((bf16[1,32,32,192]{3,2,1,0:T(8,128)(2,1)S(1)}, bf16[1,32,32,192]{3,2,1,0:T(8,128)(2,1)}, u32[]{:S(2)}) %copy-start.1) | copy-done | bytes 393240
  15.7 1.1 %shard_map.96 = (bf16[512,1536]{1,0:T(8,128)(2,1)S(1)}, bf16[1024,192]{1,0:T(8,128)(2,1)S(1)}) custom-call(s32[16,16]{1,0:T(8,128)S(1)} %pad_add_fusion.tables_in.refs_2_, bf16[1024,192]{1,0:T(8,128)(2,1)S(1)} %bitcast.12), custom_call_target="tpu_custom_call" | custom-call | bytes 2360320 | tf_op jit(solution)/shard_map/pallas_call | solution.py:110
  16.8 0.2 collective-permute-done.3.refs_4_
  17.0 1.3 %shard_map.98 = (f32[384,384]{1,0:T(8,128)S(1)}, bf16[1152,384]{1,0:T(8,128)(2,1)S(1)}, bf16[128,384]{1,0:T(8,128)(2,1)S(1)}, bf16[3,192,1024]{2,1,0:T(8,128)(2,1)S(1)}) custom-call(bf16[32,32,192]{2,1,0:T(8,128)(2,1)S(1)} %get-tuple-element.69.field_ref.refs_3_, bf16[1024,192]{1,0:T(8,128)(2,1)S(1)} %get-tuple-element.70.own_ref, ...), custom_call_target="tpu_custom_call" | custom-call | flops 339738624 | bytes 3932160 | tf_op jit(solution)/shard_map/pallas_call | solution.py:110
  18.4 0.8 %shard_map.99 = f32[480,384]{1,0:T(8,128)S(1)} custom-call(bf16[3,192,1024]{2,1,0:T(8,128)(2,1)S(1)} %get-tuple-element.72.cols, bf16[1152,384]{1,0:T(8,128)(2,1)S(1)} %get-tuple-element.89.tall), custom_call_target="tpu_custom_call" | custom-call | flops 1358954496 | bytes 2801664 | tf_op jit(solution)/shard_map/pallas_call | solution.py:110
  19.2 0.1 collective-permute-start.8
  19.3 0.5 collective-permute-start.7
  19.8 0.1 collective-permute-start.5
  19.9 0.4 collective-permute-start.6
  20.4 1.2 %shard_map.100.refs_3_ = f32[864,384]{1,0:T(8,128)S(1)} custom-call(bf16[3,192,1024]{2,1,0:T(8,128)(2,1)S(1)} %get-tuple-element.72.cols, bf16[1152,384]{1,0:T(8,128)(2,1)S(1)} %get-tuple-element.89.tall), custom_call_target="tpu_custom_call" | custom-call | tf_op jit(solution)/shard_map/pallas_call | solution.py:110
  21.6 0.0 copy-start.2
  21.6 1.3 %collective-permute-done.6.refs_5_ = bf16[128,384]{1,0:T(8,128)(2,1)S(1)} collective-permute-done((bf16[128,384]{1,0:T(8,128)(2,1)S(1)}, bf16[128,384]{1,0:T(8,128)(2,1)S(1)}, u32[]{:S(2)}, u32[]{:S(2)}) %collective-permute-start.6) | collective-permute-done | bytes 98336 | tf_op jit(solution)/shard_map/ppermute | solution.py:63
  22.9 1.5 %shard_map.101 = (f32[224,384]{1,0:T(8,128)S(1)}, bf16[224,384]{1,0:T(8,128)(2,1)S(1)}, bf16[224,384]{1,0:T(8,128)(2,1)S(1)}, bf16[224,384]{1,0:T(8,128)(2,1)S(1)}) custom-call(bf16[1152,128]{1,0:T(8,128)(2,1)S(1)} %shard_map.97.refs_0_, bf16[1152,128]{1,0:T(8,128)(2,1)S(1)} %collective-permute-done.5.refs_1_, ...), custom_call_target="tpu_custom_call" | custom-call | bytes 5873664 | tf_op jit(solution)/shard_map/pallas_call | solution.py:110
  24.4 0.6 %collective-permute-start.10 = (bf16[224,384]{1,0:T(8,128)(2,1)S(1)}, bf16[224,384]{1,0:T(8,128)(2,1)S(1)}, u32[]{:S(2)}, u32[]{:S(2)}) collective-permute-start(bf16[224,384]{1,0:T(8,128)(2,1)S(1)} %get-tuple-element.87), channel_id=1, source_target_pairs={{0,8},{2,10},{4,12},{6,14},{8,0},{10,2},{12,4},{14,6},{16,24},{18,... | collective-permute-start | bytes 516104 | tf_op jit(solution)/shard_map/ppermute | solution.py:63
  25.1 2.4 %collective-permute-start.11 = (bf16[224,384]{1,0:T(8,128)(2,1)S(1)}, bf16[224,384]{1,0:T(8,128)(2,1)S(1)}, u32[]{:S(2)}, u32[]{:S(2)}) collective-permute-start(bf16[224,384]{1,0:T(8,128)(2,1)S(1)} %get-tuple-element.88), channel_id=1, source_target_pairs={{0,12},{2,14},{4,8},{6,10},{8,4},{10,6},{12,0},{14,2},{16,28},{18,... | collective-permute-start | bytes 516104 | tf_op jit(solution)/shard_map/ppermute | solution.py:63
  27.5 0.5 collective-permute-start.9
  28.0 2.9 %shard_map.102 = (f32[1024,192]{1,0:T(8,128)S(1)}, bf16[216,128]{1,0:T(8,128)(2,1)S(1)}) custom-call(bf16[1152,384]{1,0:T(8,128)(2,1)S(1)} %get-tuple-element.89.tall, bf16[9,384,384]{2,1,0:T(8,128)(2,1)S(1)} %bitcast.13), custom_call_target="tpu_custom_call" | custom-call | flops 1358954496 | bytes 4380672 | tf_op jit(solution)/shard_map/pallas_call | solution.py:110
  30.8 0.6 collective-permute-start.12
  31.4 2.5 %collective-permute-start.13 = (bf16[216,128]{1,0:T(8,128)(2,1)S(1)}, bf16[216,128]{1,0:T(8,128)(2,1)S(1)}, u32[]{:S(2)}, u32[]{:S(2)}) collective-permute-start(bf16[216,128]{1,0:T(8,128)(2,1)S(1)} %get-tuple-element.109.refs_0_), channel_id=1, source_target_pairs={{0,24},{2,26},{4,28},{6,30},{8,16},{10,18},{12,20},{14,22},{16,8},... | collective-permute-start | bytes 165896 | tf_op jit(solution)/shard_map/ppermute | solution.py:59
  33.9 1.2 %shard_map.104.place_ref = bf16[128,1728]{1,0:T(8,128)(2,1)S(1)} custom-call(s32[16,16]{1,0:T(8,128)S(1)} %pad_add_fusion.tables_in.refs_2_), custom_call_target="tpu_custom_call" | custom-call | bytes 443392 | tf_op jit(solution)/shard_map/pallas_call | solution.py:110
  35.1 1.3 %shard_map.103 = (bf16[144,192]{1,0:T(8,128)(2,1)S(1)}, bf16[1752,128]{1,0:T(8,128)(2,1)S(1)}) custom-call(bf16[1152,128]{1,0:T(8,128)(2,1)S(1)} %shard_map.97.refs_0_, bf16[1152,128]{1,0:T(8,128)(2,1)S(1)} %collective-permute-done.5.refs_1_, s32[16,16]{1,0:T(8,128)S(1)} %pad_add_fusion.tables_in.refs_2_, ...), custom_call_target="tpu_custom_call" | custom-call | bytes 1487872 | tf_op jit(solution)/shard_map/pallas_call | solution.py:110
  36.4 1.6 %collective-permute-done.13.refs_2_ = bf16[216,128]{1,0:T(8,128)(2,1)S(1)} collective-permute-done((bf16[216,128]{1,0:T(8,128)(2,1)S(1)}, bf16[216,128]{1,0:T(8,128)(2,1)S(1)}, u32[]{:S(2)}, u32[]{:S(2)}) %collective-permute-start.13) | collective-permute-done | bytes 55328 | tf_op jit(solution)/shard_map/ppermute | solution.py:59
  38.0 0.1 shard_map.105.held_ref
  38.1 1.6 %collective-permute-start.21 = (bf16[1752,128]{1,0:T(8,128)(2,1)S(1)}, bf16[1752,128]{1,0:T(8,128)(2,1)S(1)}, u32[]{:S(2)}, u32[]{:S(2)}) collective-permute-start(bf16[1752,128]{1,0:T(8,128)(2,1)S(1)} %get-tuple-element.115), channel_id=1, source_target_pairs={{0,1},{1,0},{2,3},{3,2},{4,5},{5,4},{6,7},{7,6},{8,9},{9,8},{10,11... | collective-permute-start | bytes 1345544 | tf_op jit(solution)/shard_map/ppermute | solution.py:690
  39.7 1.6 %collective-permute-start.15 = (bf16[648,128]{1,0:T(8,128)(2,1)S(1)}, bf16[648,128]{1,0:T(8,128)(2,1)S(1)}, u32[]{:S(2)}, u32[]{:S(2)}) collective-permute-start(bf16[648,128]{1,0:T(8,128)(2,1)S(1)} %shard_map.106.refs_0_), channel_id=1, source_target_pairs={{0,4},{2,6},{4,0},{6,2},{8,12},{10,14},{12,8},{14,10},{16,20},{18,... | collective-permute-start | bytes 497672 | tf_op jit(solution)/shard_map/ppermute | solution.py:63
  41.3 0.2 collective-permute-start.14
  41.5 3.6 %collective-permute-done.15.refs_1_ = bf16[648,128]{1,0:T(8,128)(2,1)S(1)} collective-permute-done((bf16[648,128]{1,0:T(8,128)(2,1)S(1)}, bf16[648,128]{1,0:T(8,128)(2,1)S(1)}, u32[]{:S(2)}, u32[]{:S(2)}) %collective-permute-start.15) | collective-permute-done | bytes 165920 | tf_op jit(solution)/shard_map/ppermute | solution.py:63
  45.1 1.4 %collective-permute-done.17.refs_3_ = bf16[648,128]{1,0:T(8,128)(2,1)S(1)} collective-permute-done((bf16[648,128]{1,0:T(8,128)(2,1)S(1)}, bf16[648,128]{1,0:T(8,128)(2,1)S(1)}, u32[]{:S(2)}, u32[]{:S(2)}) %collective-permute-start.17) | collective-permute-done | bytes 165920 | tf_op jit(solution)/shard_map/ppermute | solution.py:63
  46.5 1.3 %shard_map.107 = bf16[1024,192]{1,0:T(8,128)(2,1)} custom-call(bf16[128,1728]{1,0:T(8,128)(2,1)S(1)} %shard_map.104.place_ref, f32[1024,192]{1,0:T(8,128)S(1)} %get-tuple-element.108.inner_ref, bf16[648,128]{1,0:T(8,128)(2,1)S(1)} %shard_map.106.refs_0_, bf16[648,128]{1,0:T(8,128)(2,1)S(1)} %collective-permute-done.15.refs_1_, ...), custom_call_target="tpu_custom_call" | custom-call | bytes 2285568 | tf_op jit(solution)/shard_map/pallas_call | solution.py:110
  47.8 1.5 %collective-permute-done.14.got_ref = bf16[224,384]{1,0:T(8,128)(2,1)S(1)} collective-permute-done((bf16[224,384]{1,0:T(8,128)(2,1)S(1)}, bf16[224,384]{1,0:T(8,128)(2,1)S(1)}, u32[]{:S(2)}, u32[]{:S(2)}) %collective-permute-start.14) | collective-permute-done | bytes 172064 | tf_op jit(solution)/shard_map/ppermute | solution.py:63
  49.4 0.6 collective-permute-start.18
  50.0 3.0 %collective-permute-start.20 = (bf16[224,384]{1,0:T(8,128)(2,1)S(1)}, bf16[224,384]{1,0:T(8,128)(2,1)S(1)}, u32[]{:S(2)}, u32[]{:S(2)}) collective-permute-start(bf16[224,384]{1,0:T(8,128)(2,1)S(1)} %shard_map.108.refs_0_), channel_id=1, source_target_pairs={{0,12},{2,14},{4,8},{6,10},{8,4},{10,6},{12,0},{14,2},{16,28},{18,... | collective-permute-start | bytes 516104 | tf_op jit(solution)/shard_map/ppermute | solution.py:63
  52.9 3.9 %shard_map.109 = bf16[1024,192]{1,0:T(8,128)(2,1)} custom-call(bf16[32,32,192]{2,1,0:T(8,128)(2,1)S(1)} %get-tuple-element.69.field_ref.refs_3_, bf16[144,192]{1,0:T(8,128)(2,1)S(1)} %get-tuple-element.114.halos_ref, bf16[1752,128]{1,0:T(8,128)(2,1)S(1)} %collective-permute-done.21.other_ref, bf16[9,384,384]{2,1,0:T(8,128)(2,1)S(1)} %bitcast.14), custom_call_target="tpu_custom_call" | custom-call | flops 2717908992 | bytes 3944448 | tf_op jit(solution)/shard_map/pallas_call | solution.py:110
  56.8 0.4 collective-permute-done.19.refs_2_
  57.3 2.4 %collective-permute-done.20.refs_3_ = bf16[224,384]{1,0:T(8,128)(2,1)S(1)} collective-permute-done((bf16[224,384]{1,0:T(8,128)(2,1)S(1)}, bf16[224,384]{1,0:T(8,128)(2,1)S(1)}, u32[]{:S(2)}, u32[]{:S(2)}) %collective-permute-start.20) | collective-permute-done | bytes 172064 | tf_op jit(solution)/shard_map/ppermute | solution.py:63
  59.7 0.5 collective-permute-start.24
  60.2 1.4 %shard_map.110.refs_0_ = f32[1728,384]{1,0:T(8,128)} custom-call(bf16[224,384]{1,0:T(8,128)(2,1)S(1)} %shard_map.108.refs_0_, bf16[224,384]{1,0:T(8,128)(2,1)S(1)} %collective-permute-done.18.refs_1_, bf16[224,384]{1,0:T(8,128)(2,1)S(1)} %collective-permute-done.19.refs_2_, bf16[224,384]{1,0:T(8,128)(2,1)S(1)} %collective-permute-done.20.refs_3_, ...), custom_call_target="tpu_custom_call" | custom-call | tf_op jit(solution)/shard_map/pallas_call | solution.py:452
  61.6 0.0 collective-permute-done.25.refs_3_
  61.6 1.1 %shard_map.111 = f32[1728,384]{1,0:T(8,128)} custom-call(f32[1728,384]{1,0:T(8,128)} %shard_map.110.refs_0_, bf16[224,384]{1,0:T(8,128)(2,1)S(1)} %collective-permute-done.23.refs_1_, bf16[224,384]{1,0:T(8,128)(2,1)S(1)} %collective-permute-done.24.refs_2_, bf16[224,384]{1,0:T(8,128)(2,1)S(1)} %collective-permute-done.25.refs_3_), custom_call_target="tpu_custom_call", output_to_operand_aliasing={{}: (0, {})} | custom-call | tf_op jit(solution)/shard_map/pallas_call | solution.py:452
  (29 shorter events, 0.1 us)
Async XLA Ops:
  0.6 16.4 %collective-permute-start.4 = (bf16[1024,192]{1,0:T(8,128)(2,1)}, bf16[1024,192]{1,0:T(8,128)(2,1)S(1)}, u32[]{:S(2)}, u32[]{:S(2)}) collective-permute-start(bf16[1024,192]{1,0:T(8,128)(2,1)} %bitcast.11), channel_id=1, source_target_pairs={{0,1},{1,0},{2,3},{3,2},{4,5},{5,4},{6,7},{7,6},{8,9},{9,8},{10,11... | collective-permute-start | bytes 1179656 | tf_op jit(solution)/shard_map/ppermute | solution.py:598
  3.6 1.0 %copy-start = (bf16[1,32,32,192]{3,2,1,0:T(8,128)(2,1)S(1)}, bf16[1,32,32,192]{3,2,1,0:T(8,128)(2,1)}, u32[]{:S(2)}) copy-start(bf16[1,32,32,192]{3,2,1,0:T(8,128)(2,1)} %param.7) | copy-start | bytes 1179652
  4.8 5.6 %collective-permute-start.1 = (bf16[192,128]{1,0:T(8,128)(2,1)S(1)}, bf16[192,128]{1,0:T(8,128)(2,1)S(1)}, u32[]{:S(2)}, u32[]{:S(2)}) collective-permute-start(bf16[192,128]{1,0:T(8,128)(2,1)S(1)} %get-tuple-element.64.refs_0_), channel_id=1, source_target_pairs={{0,8},{2,10},{4,12},{6,14},{8,0},{10,2},{12,4},{14,6},{16,24},{18,... | collective-permute-start | bytes 147464 | tf_op jit(solution)/shard_map/ppermute | solution.py:59
  6.4 5.9 %collective-permute-start.2 = (bf16[192,128]{1,0:T(8,128)(2,1)S(1)}, bf16[192,128]{1,0:T(8,128)(2,1)S(1)}, u32[]{:S(2)}, u32[]{:S(2)}) collective-permute-start(bf16[192,128]{1,0:T(8,128)(2,1)S(1)} %get-tuple-element.64.refs_0_), channel_id=1, source_target_pairs={{0,24},{2,26},{4,28},{6,30},{8,16},{10,18},{12,20},{14,22},{16,8},... | collective-permute-start | bytes 147464 | tf_op jit(solution)/shard_map/ppermute | solution.py:59
  8.9 7.9 %collective-permute-start = (bf16[192,128]{1,0:T(8,128)(2,1)S(1)}, bf16[192,128]{1,0:T(8,128)(2,1)S(1)}, u32[]{:S(2)}, u32[]{:S(2)}) collective-permute-start(bf16[192,128]{1,0:T(8,128)(2,1)S(1)} %get-tuple-element.64.refs_0_), channel_id=1, source_target_pairs={{0,4},{2,6},{4,0},{6,2},{8,12},{10,14},{12,8},{14,10},{16,20},{18,... | collective-permute-start | bytes 147464 | tf_op jit(solution)/shard_map/ppermute | solution.py:63
  12.3 4.7 %collective-permute-start.3 = (bf16[384,128]{1,0:T(8,128)(2,1)S(1)}, bf16[384,128]{1,0:T(8,128)(2,1)S(1)}, u32[]{:S(2)}, u32[]{:S(2)}) collective-permute-start(bf16[384,128]{1,0:T(8,128)(2,1)S(1)} %shard_map.95), channel_id=1, source_target_pairs={{0,4},{2,6},{4,0},{6,2},{8,12},{10,14},{12,8},{14,10},{16,20},{18,... | collective-permute-start | bytes 294920 | tf_op jit(solution)/shard_map/ppermute | solution.py:63
  14.7 1.0 %copy-start.1 = (bf16[1,32,32,192]{3,2,1,0:T(8,128)(2,1)S(1)}, bf16[1,32,32,192]{3,2,1,0:T(8,128)(2,1)}, u32[]{:S(2)}) copy-start(bf16[1,32,32,192]{3,2,1,0:T(8,128)(2,1)} %param.9) | copy-start | bytes 1179652
  19.2 3.7 %collective-permute-start.8 = (f32[480,384]{1,0:T(8,128)S(1)}, f32[480,384]{1,0:T(8,128)S(1)}, u32[]{:S(2)}, u32[]{:S(2)}) collective-permute-start(f32[480,384]{1,0:T(8,128)S(1)} %shard_map.99), channel_id=1, source_target_pairs={{0,2},{2,0},{4,6},{6,4},{8,10},{10,8},{12,14},{14,12},{16,18},{18,... | collective-permute-start | bytes 2211848 | tf_op jit(solution)/shard_map/ppermute | solution.py:63
  19.3 3.6 %collective-permute-start.7 = (f32[384,384]{1,0:T(8,128)S(1)}, f32[384,384]{1,0:T(8,128)S(1)}, u32[]{:S(2)}, u32[]{:S(2)}) collective-permute-start(f32[384,384]{1,0:T(8,128)S(1)} %get-tuple-element.80), channel_id=1, source_target_pairs={{0,2},{2,0},{4,6},{6,4},{8,10},{10,8},{12,14},{14,12},{16,18},{18,... | collective-permute-start | bytes 1769480 | tf_op jit(solution)/shard_map/ppermute | solution.py:63
  19.8 3.1 %collective-permute-start.5 = (bf16[1152,128]{1,0:T(8,128)(2,1)S(1)}, bf16[1152,128]{1,0:T(8,128)(2,1)S(1)}, u32[]{:S(2)}, u32[]{:S(2)}) collective-permute-start(bf16[1152,128]{1,0:T(8,128)(2,1)S(1)} %shard_map.97.refs_0_), channel_id=1, source_target_pairs={{0,2},{2,0},{4,6},{6,4},{8,10},{10,8},{12,14},{14,12},{16,18},{18,... | collective-permute-start | bytes 884744 | tf_op jit(solution)/shard_map/ppermute | solution.py:63
  19.9 2.9 %collective-permute-start.6 = (bf16[128,384]{1,0:T(8,128)(2,1)S(1)}, bf16[128,384]{1,0:T(8,128)(2,1)S(1)}, u32[]{:S(2)}, u32[]{:S(2)}) collective-permute-start(bf16[128,384]{1,0:T(8,128)(2,1)S(1)} %get-tuple-element.75.refs_4_), channel_id=1, source_target_pairs={{0,2},{2,0},{4,6},{6,4},{8,10},{10,8},{12,14},{14,12},{16,18},{18,... | collective-permute-start | bytes 294920 | tf_op jit(solution)/shard_map/ppermute | solution.py:63
  21.6 6.4 %copy-start.2 = (bf16[3,3,384,384]{3,2,1,0:T(8,128)(2,1)S(1)}, bf16[3,3,384,384]{3,2,1,0:T(8,128)(2,1)}, u32[]{:S(2)}) copy-start(bf16[3,3,384,384]{3,2,1,0:T(8,128)(2,1)} %param.8) | copy-start | bytes 7962628
  24.4 13.6 %collective-permute-start.10 = (bf16[224,384]{1,0:T(8,128)(2,1)S(1)}, bf16[224,384]{1,0:T(8,128)(2,1)S(1)}, u32[]{:S(2)}, u32[]{:S(2)}) collective-permute-start(bf16[224,384]{1,0:T(8,128)(2,1)S(1)} %get-tuple-element.87), channel_id=1, source_target_pairs={{0,8},{2,10},{4,12},{6,14},{8,0},{10,2},{12,4},{14,6},{16,24},{18,... | collective-permute-start | bytes 516104 | tf_op jit(solution)/shard_map/ppermute | solution.py:63
  25.1 13.0 %collective-permute-start.11 = (bf16[224,384]{1,0:T(8,128)(2,1)S(1)}, bf16[224,384]{1,0:T(8,128)(2,1)S(1)}, u32[]{:S(2)}, u32[]{:S(2)}) collective-permute-start(bf16[224,384]{1,0:T(8,128)(2,1)S(1)} %get-tuple-element.88), channel_id=1, source_target_pairs={{0,12},{2,14},{4,8},{6,10},{8,4},{10,6},{12,0},{14,2},{16,28},{18,... | collective-permute-start | bytes 516104 | tf_op jit(solution)/shard_map/ppermute | solution.py:63
  27.5 10.6 %collective-permute-start.9 = (bf16[224,384]{1,0:T(8,128)(2,1)S(1)}, bf16[224,384]{1,0:T(8,128)(2,1)S(1)}, u32[]{:S(2)}, u32[]{:S(2)}) collective-permute-start(bf16[224,384]{1,0:T(8,128)(2,1)S(1)} %get-tuple-element.86), channel_id=1, source_target_pairs={{0,4},{2,6},{4,0},{6,2},{8,12},{10,14},{12,8},{14,10},{16,20},{18,... | collective-permute-start | bytes 516104 | tf_op jit(solution)/shard_map/ppermute | solution.py:63
  30.8 5.5 %collective-permute-start.12 = (bf16[216,128]{1,0:T(8,128)(2,1)S(1)}, bf16[216,128]{1,0:T(8,128)(2,1)S(1)}, u32[]{:S(2)}, u32[]{:S(2)}) collective-permute-start(bf16[216,128]{1,0:T(8,128)(2,1)S(1)} %get-tuple-element.109.refs_0_), channel_id=1, source_target_pairs={{0,8},{2,10},{4,12},{6,14},{8,0},{10,2},{12,4},{14,6},{16,24},{18,... | collective-permute-start | bytes 165896 | tf_op jit(solution)/shard_map/ppermute | solution.py:59
  31.4 6.6 %collective-permute-start.13 = (bf16[216,128]{1,0:T(8,128)(2,1)S(1)}, bf16[216,128]{1,0:T(8,128)(2,1)S(1)}, u32[]{:S(2)}, u32[]{:S(2)}) collective-permute-start(bf16[216,128]{1,0:T(8,128)(2,1)S(1)} %get-tuple-element.109.refs_0_), channel_id=1, source_target_pairs={{0,24},{2,26},{4,28},{6,30},{8,16},{10,18},{12,20},{14,22},{16,8},... | collective-permute-start | bytes 165896 | tf_op jit(solution)/shard_map/ppermute | solution.py:59
  38.1 14.8 %collective-permute-start.21 = (bf16[1752,128]{1,0:T(8,128)(2,1)S(1)}, bf16[1752,128]{1,0:T(8,128)(2,1)S(1)}, u32[]{:S(2)}, u32[]{:S(2)}) collective-permute-start(bf16[1752,128]{1,0:T(8,128)(2,1)S(1)} %get-tuple-element.115), channel_id=1, source_target_pairs={{0,1},{1,0},{2,3},{3,2},{4,5},{5,4},{6,7},{7,6},{8,9},{9,8},{10,11... | collective-permute-start | bytes 1345544 | tf_op jit(solution)/shard_map/ppermute | solution.py:690
  39.7 5.4 %collective-permute-start.15 = (bf16[648,128]{1,0:T(8,128)(2,1)S(1)}, bf16[648,128]{1,0:T(8,128)(2,1)S(1)}, u32[]{:S(2)}, u32[]{:S(2)}) collective-permute-start(bf16[648,128]{1,0:T(8,128)(2,1)S(1)} %shard_map.106.refs_0_), channel_id=1, source_target_pairs={{0,4},{2,6},{4,0},{6,2},{8,12},{10,14},{12,8},{14,10},{16,20},{18,... | collective-permute-start | bytes 497672 | tf_op jit(solution)/shard_map/ppermute | solution.py:63
  41.3 8.0 %collective-permute-start.14 = (bf16[224,384]{1,0:T(8,128)(2,1)S(1)}, bf16[224,384]{1,0:T(8,128)(2,1)S(1)}, u32[]{:S(2)}, u32[]{:S(2)}) collective-permute-start(bf16[224,384]{1,0:T(8,128)(2,1)S(1)} %shard_map.105.held_ref), channel_id=1, source_target_pairs={{0,16},{2,18},{4,20},{6,22},{8,24},{10,26},{12,28},{14,30},{16,0},... | collective-permute-start | bytes 516104 | tf_op jit(solution)/shard_map/ppermute | solution.py:63
  41.5 3.6 %collective-permute-start.16 = (bf16[648,128]{1,0:T(8,128)(2,1)S(1)}, bf16[648,128]{1,0:T(8,128)(2,1)S(1)}, u32[]{:S(2)}, u32[]{:S(2)}) collective-permute-start(bf16[648,128]{1,0:T(8,128)(2,1)S(1)} %shard_map.106.refs_0_), channel_id=1, source_target_pairs={{0,2},{2,0},{4,6},{6,4},{8,10},{10,8},{12,14},{14,12},{16,18},{18,... | collective-permute-start | bytes 497672 | tf_op jit(solution)/shard_map/ppermute | solution.py:63
  45.1 1.4 %collective-permute-start.17 = (bf16[648,128]{1,0:T(8,128)(2,1)S(1)}, bf16[648,128]{1,0:T(8,128)(2,1)S(1)}, u32[]{:S(2)}, u32[]{:S(2)}) collective-permute-start(bf16[648,128]{1,0:T(8,128)(2,1)S(1)} %collective-permute-done.15.refs_1_), channel_id=1, source_target_pairs={{0,2},{2,0},{4,6},{6,4},{8,10},{10,8},{12,14},{14,12},{16,18},{18,... | collective-permute-start | bytes 497672 | tf_op jit(solution)/shard_map/ppermute | solution.py:63
  49.4 7.5 %collective-permute-start.18 = (bf16[224,384]{1,0:T(8,128)(2,1)S(1)}, bf16[224,384]{1,0:T(8,128)(2,1)S(1)}, u32[]{:S(2)}, u32[]{:S(2)}) collective-permute-start(bf16[224,384]{1,0:T(8,128)(2,1)S(1)} %shard_map.108.refs_0_), channel_id=1, source_target_pairs={{0,4},{2,6},{4,0},{6,2},{8,12},{10,14},{12,8},{14,10},{16,20},{18,... | collective-permute-start | bytes 516104 | tf_op jit(solution)/shard_map/ppermute | solution.py:63
  50.0 7.3 %collective-permute-start.19 = (bf16[224,384]{1,0:T(8,128)(2,1)S(1)}, bf16[224,384]{1,0:T(8,128)(2,1)S(1)}, u32[]{:S(2)}, u32[]{:S(2)}) collective-permute-start(bf16[224,384]{1,0:T(8,128)(2,1)S(1)} %shard_map.108.refs_0_), channel_id=1, source_target_pairs={{0,8},{2,10},{4,12},{6,14},{8,0},{10,2},{12,4},{14,6},{16,24},{18,... | collective-permute-start | bytes 516104 | tf_op jit(solution)/shard_map/ppermute | solution.py:63
  50.0 9.7 %collective-permute-start.20 = (bf16[224,384]{1,0:T(8,128)(2,1)S(1)}, bf16[224,384]{1,0:T(8,128)(2,1)S(1)}, u32[]{:S(2)}, u32[]{:S(2)}) collective-permute-start(bf16[224,384]{1,0:T(8,128)(2,1)S(1)} %shard_map.108.refs_0_), channel_id=1, source_target_pairs={{0,12},{2,14},{4,8},{6,10},{8,4},{10,6},{12,0},{14,2},{16,28},{18,... | collective-permute-start | bytes 516104 | tf_op jit(solution)/shard_map/ppermute | solution.py:63
  52.9 7.3 %collective-permute-start.22 = (bf16[224,384]{1,0:T(8,128)(2,1)S(1)}, bf16[224,384]{1,0:T(8,128)(2,1)S(1)}, u32[]{:S(2)}, u32[]{:S(2)}) collective-permute-start(bf16[224,384]{1,0:T(8,128)(2,1)S(1)} %shard_map.108.refs_0_), channel_id=1, source_target_pairs={{0,2},{2,0},{4,6},{6,4},{8,10},{10,8},{12,14},{14,12},{16,18},{18,... | collective-permute-start | bytes 516104 | tf_op jit(solution)/shard_map/ppermute | solution.py:63
  59.7 1.9 %collective-permute-start.23 = (bf16[224,384]{1,0:T(8,128)(2,1)S(1)}, bf16[224,384]{1,0:T(8,128)(2,1)S(1)}, u32[]{:S(2)}, u32[]{:S(2)}) collective-permute-start(bf16[224,384]{1,0:T(8,128)(2,1)S(1)} %collective-permute-done.18.refs_1_), channel_id=1, source_target_pairs={{0,2},{2,0},{4,6},{6,4},{8,10},{10,8},{12,14},{14,12},{16,18},{18,... | collective-permute-start | bytes 516104 | tf_op jit(solution)/shard_map/ppermute | solution.py:63
  59.7 1.9 %collective-permute-start.24 = (bf16[224,384]{1,0:T(8,128)(2,1)S(1)}, bf16[224,384]{1,0:T(8,128)(2,1)S(1)}, u32[]{:S(2)}, u32[]{:S(2)}) collective-permute-start(bf16[224,384]{1,0:T(8,128)(2,1)S(1)} %collective-permute-done.19.refs_2_), channel_id=1, source_target_pairs={{0,2},{2,0},{4,6},{6,4},{8,10},{10,8},{12,14},{14,12},{16,18},{18,... | collective-permute-start | bytes 516104 | tf_op jit(solution)/shard_map/ppermute | solution.py:63
  60.2 1.4 %collective-permute-start.25 = (bf16[224,384]{1,0:T(8,128)(2,1)S(1)}, bf16[224,384]{1,0:T(8,128)(2,1)S(1)}, u32[]{:S(2)}, u32[]{:S(2)}) collective-permute-start(bf16[224,384]{1,0:T(8,128)(2,1)S(1)} %collective-permute-done.20.refs_3_), channel_id=1, source_target_pairs={{0,2},{2,0},{4,6},{6,4},{8,10},{10,8},{12,14},{14,12},{16,18},{18,... | collective-permute-start | bytes 516104 | tf_op jit(solution)/shard_map/ppermute | solution.py:63

commit v12 on v11

--- a/solution.py
+++ b/solution.py
@@ -11,6 +11,7 @@
 
 SPAN = 4
 EXTRA = 16
+PARTS = 3
 
 
 def turn_tables():
@@ -529,14 +530,23 @@
     out_ref[...] = ends.astype(jnp.bfloat16)
 
 
+def parts_of(rows):
+    size = -(-rows // (32 * PARTS)) * 32
+    return [min(size, rows - first) for first in range(0, rows, size)]
+
+
 def halo_kernel(side, part, n_near, *refs):
     near_refs, tables_in, field_ref = refs[:n_near], refs[n_near], refs[n_near + 1]
-    halos_ref, packet_ref, near, tables, sem = refs[n_near + 2 :]
+    halos_ref, *packet_refs = refs[n_near + 2 : -3]
+    near, tables, sem = refs[-3:]
     copy = pltpu.make_async_copy(tables_in, tables, sem)
     copy.start()
     rows = side * side
     unpack_near(near_refs, near, side, part)
-    pack(field_ref[...].reshape(rows, part), packet_ref)
+    field = field_ref[...].reshape(rows, part)
+    sizes = parts_of(rows)
+    for k, ref in enumerate(packet_refs):
+        pack(field[sum(sizes[:k]) : sum(sizes[: k + 1])], ref)
     copy.wait()
     index = Neighbours(side, tables)
     step = lax.broadcasted_iota(jnp.int32, (side, 1), 0)
@@ -552,16 +562,19 @@
     pick = onehot(jnp.concatenate(wanted + [ends], axis=0), near.shape[0])
     halos = jnp.dot(pick, near[...], preferred_element_type=jnp.float32).astype(jnp.bfloat16)
     halos_ref[...] = halos
-    pack(halos, packet_ref, packed_shape(rows, part)[0])
-
-
-def output_kernel(side, part, field_ref, halos_ref, other_ref, weight_ref, out_ref, cols, other_cols, other):
+    pack(halos, packet_refs[-1], packed_shape(sizes[-1], part)[0])
+
+
+def output_kernel(side, part, field_ref, halos_ref, weight_ref, *refs):
     rows = side * side
     ch = lax.axis_index("ch")
+    other_refs, (out_ref, cols, other_cols, other) = refs[:PARTS], refs[PARTS:]
     wide = -(-part // 128) * 128
     lanes = pl.multiple_of(ch * (weight_ref.shape[2] - wide), 128)
-    unpack(other_ref, other, 0, 0, rows, part)
-    unpack(other_ref, other, packed_shape(rows, part)[0], rows, 4 * side + EXTRA, part)
+    sizes = parts_of(rows)
+    for k, ref in enumerate(other_refs):
+        unpack(ref, other, 0, sum(sizes[:k]), sizes[k], part)
+    unpack(other_refs[-1], other, packed_shape(sizes[-1], part)[0], rows, 4 * side + EXTRA, part)
     shifted_columns(side, part, field_ref[...].reshape(rows, part), halos_ref[...], cols)
     shifted_columns(side, part, other[0:rows, :], other[rows:, :], other_cols)
     starts = (pl.multiple_of(ch * part, 16), pl.multiple_of((1 - ch) * part, 16))
@@ -671,9 +684,11 @@
         [tables],
         scratch=table_scratch,
     )
-    halos, packet = call(
+    halos, *packet = call(
         functools.partial(halo_kernel, side, part, len(near)),
-        [vmem((block, part), half_bytes), vmem(packed_shape(rows + block, part), half_bytes)],
+        [vmem((block, part), half_bytes)]
+        + [vmem(packed_shape(size, part), half_bytes) for size in parts_of(rows)[:-1]]
+        + [vmem(packed_shape(parts_of(rows)[-1] + block, part), half_bytes)],
         [*near, tables, field],
         scratch=[pltpu.VMEM((48 * side, part), half_bytes), *table_scratch],
     )
@@ -687,7 +702,7 @@
     def start_aside(send, aside):
         send, here, packet = lax.optimization_barrier((send, *aside))
         (here,) = call(join_kernel, [vmem((3 * pieces.shape[0], pieces.shape[1]), half_bytes)], here)
-        return send, here, by_mask(here, 2, count), lax.ppermute(packet, "ch", others)
+        return send, here, by_mask(here, 2, count), [lax.ppermute(v, "ch", others) for v in packet]
 
     for index, bits in enumerate(rs_stages):
         masks = group_masks(bits)
@@ -701,23 +716,12 @@
             send, here, beside, other_field = start_aside(send, aside)
         got = [by_mask(v, m, count) for v, m in zip(send, masks[1:])]
     (held,) = call(functools.partial(sum_kernel, len(got), 1), [vmem(held.shape, half_bytes)], [held, *got])
-    def add_halos(here, beside):
-        got_pieces = [here, beside, by_mask(here, 1, count), by_mask(beside, 1, count)]
-        return call(
-            functools.partial(add_halo_kernel, side, part),
-            [vmem((rows, part), half_bytes)],
-            [place, inner, *got_pieces],
-            scratch=[pltpu.VMEM((12 * block, part), half_bytes)],
-        )[0]
-
     if swap:
         if not rs_stages:
             held, here, beside, other_field = start_aside(held, aside)
         got = by_mask(held, stages[-1][0], count)
-        got, grad_features = lax.optimization_barrier((got, add_halos(here, beside)))
+        got, here, beside = lax.optimization_barrier((got, here, beside))
         (held,) = call(exchange_kernel, [vmem(held.shape, half_bytes)], [held, got])
-    else:
-        grad_features = add_halos(here, beside)
     order = [0] if not swap else [0, stages[-1][0]]
     ag_stages = stages[-2:0:-1] if swap else stages[:0:-1]
     for index, bits in enumerate(ag_stages):
@@ -729,10 +733,17 @@
                 join_kernel, [vmem((held.shape[0] * len(masks), chans), half_bytes)], [held, *got]
             )
     order = [[m + v for v in order] for m in masks]
+    got_pieces = [here, beside, by_mask(here, 1, count), by_mask(beside, 1, count)]
+    (grad_features,) = call(
+        functools.partial(add_halo_kernel, side, part),
+        [vmem((rows, part), half_bytes)],
+        [place, inner, *got_pieces],
+        scratch=[pltpu.VMEM((12 * block, part), half_bytes)],
+    )
     (output,) = call(
         functools.partial(output_kernel, side, part),
         [vmem((rows, part), half_bytes)],
-        [field, halos, other_field, taps],
+        [field, halos, taps, *other_field],
         scratch=[
             pltpu.VMEM((3, flat, part), half_bytes),
             pltpu.VMEM((3, flat, part), half_bytes),

time: 62.9 us -> 61.8 us (0.983)
  waiting for transfers between devices: 14.4 us -> 10.7 us
  starting transfers between devices: 25.4 us -> 28 us
    ppermute x20, waiting for transfers between devices: 10.9 us -> 7.18 us  [by_mask(): return lax.ppermute(value, 'tile', [(i, i ^ mask) for i in range(count)])]
    ppermute x1 -> x3, starting transfers between devices: 1.56 us -> 3.58 us  [start_aside(): lax.ppermute(v, 'ch', others)]
  transfers between devices with their start and end apart: 26 -> 28, of which waited for: 9 -> 7; matrix products, arithmetic and copies ran while one was open for 1% -> 1% of each run, Pallas kernels for 23% -> 23%
where the time goes in v12:
time: 61.8 us; the launch traced here: 61.5 us
  starting transfers between devices  28 us (45%)
  Pallas kernels  19.2 us (31%)
  waiting for transfers between devices  10.7 us (17%)
  local copies, waits for them, and re-layouts  2.09 us (3%)
  between operations  0.79 us (1%)
  other arithmetic  0.74 us (1%)
    pallas_call x16, Pallas kernels, call(): pl.pallas_call(kernel, out_shape=tuple(outs), in_specs=in_specs, out_spec...  16.8 us
    ppermute x20, starting transfers between devices, by_mask(): return lax.ppermute(value, 'tile', [(i, i ^ mask) for i in range(count)])  14.2 us
    ppermute x20, waiting for transfers between devices, by_mask(): return lax.ppermute(value, 'tile', [(i, i ^ mask) for i in range(count)])  7.18 us
    ppermute x4, starting transfers between devices, by_swap(): return lax.ppermute(value, 'tile', pairs)  7.17 us
    ppermute x3, starting transfers between devices, start_aside(): lax.ppermute(v, 'ch', others)  3.58 us
    ppermute x4, waiting for transfers between devices, by_swap(): return lax.ppermute(value, 'tile', pairs)  3.53 us
    ppermute x1, starting transfers between devices, body(): cot_other = lax.ppermute(cot_own, 'ch', others)  3 us
    pallas_call x2, Pallas kernels, unfold(): pl.pallas_call(functools.partial(unfold_kernel, whole.shape[0] // 2, chun...  2.41 us
  transfers between devices with their start and end apart: 28, of which 7 were waited for; matrix products, arithmetic and copies ran while one was open for 1% of the time, Pallas kernels for 23%

profile of v12, /device:TPU:0, one launch (start us, length us, event | category | flops | bytes accessed | tf_op | source)
XLA Modules:
  0.0 61.5 jit_solution(6734740814563936382)
XLA Ops:
  0.6 3.0 %collective-permute-start.4 = (bf16[1024,192]{1,0:T(8,128)(2,1)}, bf16[1024,192]{1,0:T(8,128)(2,1)S(1)}, u32[]{:S(2)}, u32[]{:S(2)}) collective-permute-start(bf16[1024,192]{1,0:T(8,128)(2,1)} %bitcast.11), channel_id=1, source_target_pairs={{0,1},{1,0},{2,3},{3,2},{4,5},{5,4},{6,7},{7,6},{8,9},{9,8},{10,11... | collective-permute-start | bytes 1179656 | tf_op jit(solution)/shard_map/ppermute | solution.py:611
  3.6 1.0 %copy-done = bf16[1,32,32,192]{3,2,1,0:T(8,128)(2,1)S(1)} copy-done((bf16[1,32,32,192]{3,2,1,0:T(8,128)(2,1)S(1)}, bf16[1,32,32,192]{3,2,1,0:T(8,128)(2,1)}, u32[]{:S(2)}) %copy-start) | copy-done | bytes 393240
  4.7 0.1 shard_map.94
  4.8 1.6 %collective-permute-start.1 = (bf16[192,128]{1,0:T(8,128)(2,1)S(1)}, bf16[192,128]{1,0:T(8,128)(2,1)S(1)}, u32[]{:S(2)}, u32[]{:S(2)}) collective-permute-start(bf16[192,128]{1,0:T(8,128)(2,1)S(1)} %get-tuple-element.71.refs_0_), channel_id=1, source_target_pairs={{0,8},{2,10},{4,12},{6,14},{8,0},{10,2},{12,4},{14,6},{16,24},{18,... | collective-permute-start | bytes 147464 | tf_op jit(solution)/shard_map/ppermute | solution.py:60
  6.4 2.5 %collective-permute-start.2 = (bf16[192,128]{1,0:T(8,128)(2,1)S(1)}, bf16[192,128]{1,0:T(8,128)(2,1)S(1)}, u32[]{:S(2)}, u32[]{:S(2)}) collective-permute-start(bf16[192,128]{1,0:T(8,128)(2,1)S(1)} %get-tuple-element.71.refs_0_), channel_id=1, source_target_pairs={{0,24},{2,26},{4,28},{6,30},{8,16},{10,18},{12,20},{14,22},{16,8},... | collective-permute-start | bytes 147464 | tf_op jit(solution)/shard_map/ppermute | solution.py:60
  8.9 1.5 %collective-permute-start = (bf16[192,128]{1,0:T(8,128)(2,1)S(1)}, bf16[192,128]{1,0:T(8,128)(2,1)S(1)}, u32[]{:S(2)}, u32[]{:S(2)}) collective-permute-start(bf16[192,128]{1,0:T(8,128)(2,1)S(1)} %get-tuple-element.71.refs_0_), channel_id=1, source_target_pairs={{0,4},{2,6},{4,0},{6,2},{8,12},{10,14},{12,8},{14,10},{16,20},{18,... | collective-permute-start | bytes 147464 | tf_op jit(solution)/shard_map/ppermute | solution.py:64
  10.4 1.9 %collective-permute-done.2.refs_1_.refs_3_ = bf16[192,128]{1,0:T(8,128)(2,1)S(1)} collective-permute-done((bf16[192,128]{1,0:T(8,128)(2,1)S(1)}, bf16[192,128]{1,0:T(8,128)(2,1)S(1)}, u32[]{:S(2)}, u32[]{:S(2)}) %collective-permute-start.2) | collective-permute-done | bytes 49184 | tf_op jit(solution)/shard_map/ppermute | solution.py:60
  12.3 1.6 %collective-permute-start.3 = (bf16[384,128]{1,0:T(8,128)(2,1)S(1)}, bf16[384,128]{1,0:T(8,128)(2,1)S(1)}, u32[]{:S(2)}, u32[]{:S(2)}) collective-permute-start(bf16[384,128]{1,0:T(8,128)(2,1)S(1)} %shard_map.95), channel_id=1, source_target_pairs={{0,4},{2,6},{4,0},{6,2},{8,12},{10,14},{12,8},{14,10},{16,20},{18,... | collective-permute-start | bytes 294920 | tf_op jit(solution)/shard_map/ppermute | solution.py:64
  13.9 0.7 %pad_add_fusion.tables_in.refs_2_ = s32[16,16]{1,0:T(8,128)S(1)} fusion(s32[4,16]{1,0:T(4,128)} %bitcast.17, s32[4,16]{1,0:T(4,128)} %bitcast.18, s32[4,16]{1,0:T(4,128)} %bitcast.19, s32[4,16]{1,0:T(4,128)} %bitcast.20), kind=kLoop, calls=%fused_computation | loop fusion | flops 768 | bytes 2048 | tf_op jit(solution)/shard_map/concatenate | solution.py:619
  14.7 1.0 %copy-done.1 = bf16[1,32,32,192]{3,2,1,0:T(8,128)(2,1)S(1)} copy-done((bf16[1,32,32,192]{3,2,1,0:T(8,128)(2,1)S(1)}, bf16[1,32,32,192]{3,2,1,0:T(8,128)(2,1)}, u32[]{:S(2)}) %copy-start.1) | copy-done | bytes 393240
  15.7 1.1 %shard_map.96 = (bf16[512,1536]{1,0:T(8,128)(2,1)S(1)}, bf16[1024,192]{1,0:T(8,128)(2,1)S(1)}) custom-call(s32[16,16]{1,0:T(8,128)S(1)} %pad_add_fusion.tables_in.refs_2_, bf16[1024,192]{1,0:T(8,128)(2,1)S(1)} %bitcast.12), custom_call_target="tpu_custom_call" | custom-call | bytes 2360320 | tf_op jit(solution)/shard_map/pallas_call | solution.py:111
  16.8 0.2 collective-permute-done.3.refs_4_
  17.0 1.3 %shard_map.98 = (f32[384,384]{1,0:T(8,128)S(1)}, bf16[1152,384]{1,0:T(8,128)(2,1)S(1)}, bf16[128,384]{1,0:T(8,128)(2,1)S(1)}, bf16[3,192,1024]{2,1,0:T(8,128)(2,1)S(1)}) custom-call(bf16[32,32,192]{2,1,0:T(8,128)(2,1)S(1)} %get-tuple-element.76.field_ref.refs_3_, bf16[1024,192]{1,0:T(8,128)(2,1)S(1)} %get-tuple-element.77.own_ref, ...), custom_call_target="tpu_custom_call" | custom-call | flops 339738624 | bytes 3932160 | tf_op jit(solution)/shard_map/pallas_call | solution.py:111
  18.4 0.8 %shard_map.99 = f32[480,384]{1,0:T(8,128)S(1)} custom-call(bf16[3,192,1024]{2,1,0:T(8,128)(2,1)S(1)} %get-tuple-element.79.cols, bf16[1152,384]{1,0:T(8,128)(2,1)S(1)} %get-tuple-element.96.tall), custom_call_target="tpu_custom_call" | custom-call | flops 1358954496 | bytes 2801664 | tf_op jit(solution)/shard_map/pallas_call | solution.py:111
  19.2 0.1 collective-permute-start.8
  19.3 0.5 collective-permute-start.7
  19.8 0.1 collective-permute-start.5
  19.9 0.4 collective-permute-start.6
  20.4 1.2 %shard_map.100.refs_3_ = f32[864,384]{1,0:T(8,128)S(1)} custom-call(bf16[3,192,1024]{2,1,0:T(8,128)(2,1)S(1)} %get-tuple-element.79.cols, bf16[1152,384]{1,0:T(8,128)(2,1)S(1)} %get-tuple-element.96.tall), custom_call_target="tpu_custom_call" | custom-call | tf_op jit(solution)/shard_map/pallas_call | solution.py:111
  21.6 1.3 %collective-permute-done.6.refs_5_ = bf16[128,384]{1,0:T(8,128)(2,1)S(1)} collective-permute-done((bf16[128,384]{1,0:T(8,128)(2,1)S(1)}, bf16[128,384]{1,0:T(8,128)(2,1)S(1)}, u32[]{:S(2)}, u32[]{:S(2)}) %collective-permute-start.6) | collective-permute-done | bytes 98336 | tf_op jit(solution)/shard_map/ppermute | solution.py:64
  22.9 1.5 %shard_map.101 = (f32[224,384]{1,0:T(8,128)S(1)}, bf16[224,384]{1,0:T(8,128)(2,1)S(1)}, bf16[224,384]{1,0:T(8,128)(2,1)S(1)}, bf16[224,384]{1,0:T(8,128)(2,1)S(1)}) custom-call(bf16[1152,128]{1,0:T(8,128)(2,1)S(1)} %shard_map.97.refs_0_, bf16[1152,128]{1,0:T(8,128)(2,1)S(1)} %collective-permute-done.5.refs_1_, ...), custom_call_target="tpu_custom_call" | custom-call | bytes 5873664 | tf_op jit(solution)/shard_map/pallas_call | solution.py:111
  24.4 0.6 %collective-permute-start.10 = (bf16[224,384]{1,0:T(8,128)(2,1)S(1)}, bf16[224,384]{1,0:T(8,128)(2,1)S(1)}, u32[]{:S(2)}, u32[]{:S(2)}) collective-permute-start(bf16[224,384]{1,0:T(8,128)(2,1)S(1)} %get-tuple-element.94), channel_id=1, source_target_pairs={{0,8},{2,10},{4,12},{6,14},{8,0},{10,2},{12,4},{14,6},{16,24},{18,... | collective-permute-start | bytes 516104 | tf_op jit(solution)/shard_map/ppermute | solution.py:64
  25.1 2.4 %collective-permute-start.11 = (bf16[224,384]{1,0:T(8,128)(2,1)S(1)}, bf16[224,384]{1,0:T(8,128)(2,1)S(1)}, u32[]{:S(2)}, u32[]{:S(2)}) collective-permute-start(bf16[224,384]{1,0:T(8,128)(2,1)S(1)} %get-tuple-element.95), channel_id=1, source_target_pairs={{0,12},{2,14},{4,8},{6,10},{8,4},{10,6},{12,0},{14,2},{16,28},{18,... | collective-permute-start | bytes 516104 | tf_op jit(solution)/shard_map/ppermute | solution.py:64
  27.5 0.5 collective-permute-start.9
  28.0 2.9 %shard_map.102 = (f32[1024,192]{1,0:T(8,128)S(1)}, bf16[216,128]{1,0:T(8,128)(2,1)S(1)}) custom-call(bf16[1152,384]{1,0:T(8,128)(2,1)S(1)} %get-tuple-element.96.tall, bf16[9,384,384]{2,1,0:T(8,128)(2,1)S(1)} %bitcast.13), custom_call_target="tpu_custom_call" | custom-call | flops 1358954496 | bytes 4380672 | tf_op jit(solution)/shard_map/pallas_call | solution.py:111
  30.8 0.6 collective-permute-start.12
  31.4 2.5 %collective-permute-start.13 = (bf16[216,128]{1,0:T(8,128)(2,1)S(1)}, bf16[216,128]{1,0:T(8,128)(2,1)S(1)}, u32[]{:S(2)}, u32[]{:S(2)}) collective-permute-start(bf16[216,128]{1,0:T(8,128)(2,1)S(1)} %get-tuple-element.118.refs_0_), channel_id=1, source_target_pairs={{0,24},{2,26},{4,28},{6,30},{8,16},{10,18},{12,20},{14,22},{16,8},... | collective-permute-start | bytes 165896 | tf_op jit(solution)/shard_map/ppermute | solution.py:60
  33.9 1.2 %shard_map.104.place_ref = bf16[128,1728]{1,0:T(8,128)(2,1)S(1)} custom-call(s32[16,16]{1,0:T(8,128)S(1)} %pad_add_fusion.tables_in.refs_2_), custom_call_target="tpu_custom_call" | custom-call | bytes 443392 | tf_op jit(solution)/shard_map/pallas_call | solution.py:111
  35.1 1.3 %shard_map.103 = (bf16[144,192]{1,0:T(8,128)(2,1)S(1)}, bf16[528,128]{1,0:T(8,128)(2,1)S(1)}, bf16[528,128]{1,0:T(8,128)(2,1)S(1)}, bf16[696,128]{1,0:T(8,128)(2,1)S(1)}) custom-call(bf16[1152,128]{1,0:T(8,128)(2,1)S(1)} %shard_map.97.refs_0_, bf16[1152,128]{1,0:T(8,128)(2,1)S(1)} %collective-permute-done.5.refs_1_, ...), custom_call_target="tpu_custom_call" | custom-call | bytes 1487872 | tf_op jit(solution)/shard_map/pallas_call | solution.py:111
  36.4 1.6 %collective-permute-done.13.refs_2_ = bf16[216,128]{1,0:T(8,128)(2,1)S(1)} collective-permute-done((bf16[216,128]{1,0:T(8,128)(2,1)S(1)}, bf16[216,128]{1,0:T(8,128)(2,1)S(1)}, u32[]{:S(2)}, u32[]{:S(2)}) %collective-permute-start.13) | collective-permute-done | bytes 55328 | tf_op jit(solution)/shard_map/ppermute | solution.py:60
  38.0 0.1 shard_map.105.held_ref
  38.1 1.6 %collective-permute-start.23 = (bf16[696,128]{1,0:T(8,128)(2,1)S(1)}, bf16[696,128]{1,0:T(8,128)(2,1)S(1)}, u32[]{:S(2)}, u32[]{:S(2)}) collective-permute-start(bf16[696,128]{1,0:T(8,128)(2,1)S(1)} %get-tuple-element.129), channel_id=1, source_target_pairs={{0,1},{1,0},{2,3},{3,2},{4,5},{5,4},{6,7},{7,6},{8,9},{9,8},{10,11... | collective-permute-start | bytes 534536 | tf_op jit(solution)/shard_map/ppermute | solution.py:705
  39.7 0.6 collective-permute-start.14
  40.3 1.2 %collective-permute-start.15 = (bf16[648,128]{1,0:T(8,128)(2,1)S(1)}, bf16[648,128]{1,0:T(8,128)(2,1)S(1)}, u32[]{:S(2)}, u32[]{:S(2)}) collective-permute-start(bf16[648,128]{1,0:T(8,128)(2,1)S(1)} %shard_map.106.refs_0_), channel_id=1, source_target_pairs={{0,4},{2,6},{4,0},{6,2},{8,12},{10,14},{12,8},{14,10},{16,20},{18,... | collective-permute-start | bytes 497672 | tf_op jit(solution)/shard_map/ppermute | solution.py:64
  41.5 0.5 collective-permute-start.21
  42.0 1.5 %collective-permute-start.22 = (bf16[528,128]{1,0:T(8,128)(2,1)S(1)}, bf16[528,128]{1,0:T(8,128)(2,1)S(1)}, u32[]{:S(2)}, u32[]{:S(2)}) collective-permute-start(bf16[528,128]{1,0:T(8,128)(2,1)S(1)} %get-tuple-element.128), channel_id=1, source_target_pairs={{0,1},{1,0},{2,3},{3,2},{4,5},{5,4},{6,7},{7,6},{8,9},{9,8},{10,11... | collective-permute-start | bytes 405512 | tf_op jit(solution)/shard_map/ppermute | solution.py:705
  43.5 2.2 %collective-permute-done.15.refs_1_ = bf16[648,128]{1,0:T(8,128)(2,1)S(1)} collective-permute-done((bf16[648,128]{1,0:T(8,128)(2,1)S(1)}, bf16[648,128]{1,0:T(8,128)(2,1)S(1)}, u32[]{:S(2)}, u32[]{:S(2)}) %collective-permute-start.15) | collective-permute-done | bytes 165920 | tf_op jit(solution)/shard_map/ppermute | solution.py:64
  45.7 2.3 %collective-permute-done.14.got_ref = bf16[224,384]{1,0:T(8,128)(2,1)S(1)} collective-permute-done((bf16[224,384]{1,0:T(8,128)(2,1)S(1)}, bf16[224,384]{1,0:T(8,128)(2,1)S(1)}, u32[]{:S(2)}, u32[]{:S(2)}) %collective-permute-start.14) | collective-permute-done | bytes 172064 | tf_op jit(solution)/shard_map/ppermute | solution.py:64
  48.1 1.6 %collective-permute-start.16 = (bf16[224,384]{1,0:T(8,128)(2,1)S(1)}, bf16[224,384]{1,0:T(8,128)(2,1)S(1)}, u32[]{:S(2)}, u32[]{:S(2)}) collective-permute-start(bf16[224,384]{1,0:T(8,128)(2,1)S(1)} %shard_map.107.refs_0_), channel_id=1, source_target_pairs={{0,4},{2,6},{4,0},{6,2},{8,12},{10,14},{12,8},{14,10},{16,20},{18,... | collective-permute-start | bytes 516104 | tf_op jit(solution)/shard_map/ppermute | solution.py:64
  49.6 2.0 %collective-permute-start.18 = (bf16[224,384]{1,0:T(8,128)(2,1)S(1)}, bf16[224,384]{1,0:T(8,128)(2,1)S(1)}, u32[]{:S(2)}, u32[]{:S(2)}) collective-permute-start(bf16[224,384]{1,0:T(8,128)(2,1)S(1)} %shard_map.107.refs_0_), channel_id=1, source_target_pairs={{0,12},{2,14},{4,8},{6,10},{8,4},{10,6},{12,0},{14,2},{16,28},{18,... | collective-permute-start | bytes 516104 | tf_op jit(solution)/shard_map/ppermute | solution.py:64
  51.6 0.5 collective-permute-start.20
  52.1 3.9 %shard_map.109 = bf16[1024,192]{1,0:T(8,128)(2,1)} custom-call(bf16[32,32,192]{2,1,0:T(8,128)(2,1)S(1)} %get-tuple-element.76.field_ref.refs_3_, bf16[144,192]{1,0:T(8,128)(2,1)S(1)} %get-tuple-element.126.halos_ref, bf16[9,384,384]{2,1,0:T(8,128)(2,1)S(1)} %bitcast.14, bf16[528,128]{1,0:T(8,128)(2,1)S(1)} %collective-permute-done.21.refs_0_, ...), custom_call_target="tpu_custom_call" | custom-call | flops 2717908992 | bytes 3944448 | tf_op jit(solution)/shard_map/pallas_call | solution.py:111
  56.0 0.1 collective-permute-start.24
  56.1 1.3 %shard_map.108 = bf16[1024,192]{1,0:T(8,128)(2,1)} custom-call(bf16[128,1728]{1,0:T(8,128)(2,1)S(1)} %shard_map.104.place_ref, f32[1024,192]{1,0:T(8,128)S(1)} %get-tuple-element.123.inner_ref, bf16[648,128]{1,0:T(8,128)(2,1)S(1)} %shard_map.106.refs_0_, bf16[648,128]{1,0:T(8,128)(2,1)S(1)} %collective-permute-done.15.refs_1_, ...), custom_call_target="tpu_custom_call" | custom-call | bytes 2285568 | tf_op jit(solution)/shard_map/pallas_call | solution.py:111
  57.4 1.1 %collective-permute-done.18.refs_3_ = bf16[224,384]{1,0:T(8,128)(2,1)S(1)} collective-permute-done((bf16[224,384]{1,0:T(8,128)(2,1)S(1)}, bf16[224,384]{1,0:T(8,128)(2,1)S(1)}, u32[]{:S(2)}, u32[]{:S(2)}) %collective-permute-start.18) | collective-permute-done | bytes 172064 | tf_op jit(solution)/shard_map/ppermute | solution.py:64
  58.6 0.5 collective-permute-start.26
  59.1 1.4 %shard_map.110.refs_0_ = f32[1728,384]{1,0:T(8,128)} custom-call(bf16[224,384]{1,0:T(8,128)(2,1)S(1)} %shard_map.107.refs_0_, bf16[224,384]{1,0:T(8,128)(2,1)S(1)} %collective-permute-done.16.refs_1_, bf16[224,384]{1,0:T(8,128)(2,1)S(1)} %collective-permute-done.17.refs_2_, bf16[224,384]{1,0:T(8,128)(2,1)S(1)} %collective-permute-done.18.refs_3_, ...), custom_call_target="tpu_custom_call" | custom-call | tf_op jit(solution)/shard_map/pallas_call | solution.py:453
  60.5 1.1 %shard_map.111 = f32[1728,384]{1,0:T(8,128)} custom-call(f32[1728,384]{1,0:T(8,128)} %shard_map.110.refs_0_, bf16[224,384]{1,0:T(8,128)(2,1)S(1)} %collective-permute-done.25.refs_1_, bf16[224,384]{1,0:T(8,128)(2,1)S(1)} %collective-permute-done.26.refs_2_, bf16[224,384]{1,0:T(8,128)(2,1)S(1)} %collective-permute-done.27.refs_3_), custom_call_target="tpu_custom_call", output_to_operand_aliasing={{}: (0, {})} | custom-call | tf_op jit(solution)/shard_map/pallas_call | solution.py:453
  (33 shorter events, 0.2 us)
Async XLA Ops:
  0.6 16.4 %collective-permute-start.4 = (bf16[1024,192]{1,0:T(8,128)(2,1)}, bf16[1024,192]{1,0:T(8,128)(2,1)S(1)}, u32[]{:S(2)}, u32[]{:S(2)}) collective-permute-start(bf16[1024,192]{1,0:T(8,128)(2,1)} %bitcast.11), channel_id=1, source_target_pairs={{0,1},{1,0},{2,3},{3,2},{4,5},{5,4},{6,7},{7,6},{8,9},{9,8},{10,11... | collective-permute-start | bytes 1179656 | tf_op jit(solution)/shard_map/ppermute | solution.py:611
  3.6 1.0 %copy-start = (bf16[1,32,32,192]{3,2,1,0:T(8,128)(2,1)S(1)}, bf16[1,32,32,192]{3,2,1,0:T(8,128)(2,1)}, u32[]{:S(2)}) copy-start(bf16[1,32,32,192]{3,2,1,0:T(8,128)(2,1)} %param.7) | copy-start | bytes 1179652
  4.8 5.6 %collective-permute-start.1 = (bf16[192,128]{1,0:T(8,128)(2,1)S(1)}, bf16[192,128]{1,0:T(8,128)(2,1)S(1)}, u32[]{:S(2)}, u32[]{:S(2)}) collective-permute-start(bf16[192,128]{1,0:T(8,128)(2,1)S(1)} %get-tuple-element.71.refs_0_), channel_id=1, source_target_pairs={{0,8},{2,10},{4,12},{6,14},{8,0},{10,2},{12,4},{14,6},{16,24},{18,... | collective-permute-start | bytes 147464 | tf_op jit(solution)/shard_map/ppermute | solution.py:60
  6.4 5.9 %collective-permute-start.2 = (bf16[192,128]{1,0:T(8,128)(2,1)S(1)}, bf16[192,128]{1,0:T(8,128)(2,1)S(1)}, u32[]{:S(2)}, u32[]{:S(2)}) collective-permute-start(bf16[192,128]{1,0:T(8,128)(2,1)S(1)} %get-tuple-element.71.refs_0_), channel_id=1, source_target_pairs={{0,24},{2,26},{4,28},{6,30},{8,16},{10,18},{12,20},{14,22},{16,8},... | collective-permute-start | bytes 147464 | tf_op jit(solution)/shard_map/ppermute | solution.py:60
  8.9 7.9 %collective-permute-start = (bf16[192,128]{1,0:T(8,128)(2,1)S(1)}, bf16[192,128]{1,0:T(8,128)(2,1)S(1)}, u32[]{:S(2)}, u32[]{:S(2)}) collective-permute-start(bf16[192,128]{1,0:T(8,128)(2,1)S(1)} %get-tuple-element.71.refs_0_), channel_id=1, source_target_pairs={{0,4},{2,6},{4,0},{6,2},{8,12},{10,14},{12,8},{14,10},{16,20},{18,... | collective-permute-start | bytes 147464 | tf_op jit(solution)/shard_map/ppermute | solution.py:64
  12.3 4.7 %collective-permute-start.3 = (bf16[384,128]{1,0:T(8,128)(2,1)S(1)}, bf16[384,128]{1,0:T(8,128)(2,1)S(1)}, u32[]{:S(2)}, u32[]{:S(2)}) collective-permute-start(bf16[384,128]{1,0:T(8,128)(2,1)S(1)} %shard_map.95), channel_id=1, source_target_pairs={{0,4},{2,6},{4,0},{6,2},{8,12},{10,14},{12,8},{14,10},{16,20},{18,... | collective-permute-start | bytes 294920 | tf_op jit(solution)/shard_map/ppermute | solution.py:64
  14.7 1.0 %copy-start.1 = (bf16[1,32,32,192]{3,2,1,0:T(8,128)(2,1)S(1)}, bf16[1,32,32,192]{3,2,1,0:T(8,128)(2,1)}, u32[]{:S(2)}) copy-start(bf16[1,32,32,192]{3,2,1,0:T(8,128)(2,1)} %param.9) | copy-start | bytes 1179652
  19.2 3.7 %collective-permute-start.8 = (f32[480,384]{1,0:T(8,128)S(1)}, f32[480,384]{1,0:T(8,128)S(1)}, u32[]{:S(2)}, u32[]{:S(2)}) collective-permute-start(f32[480,384]{1,0:T(8,128)S(1)} %shard_map.99), channel_id=1, source_target_pairs={{0,2},{2,0},{4,6},{6,4},{8,10},{10,8},{12,14},{14,12},{16,18},{18,... | collective-permute-start | bytes 2211848 | tf_op jit(solution)/shard_map/ppermute | solution.py:64
  19.3 3.6 %collective-permute-start.7 = (f32[384,384]{1,0:T(8,128)S(1)}, f32[384,384]{1,0:T(8,128)S(1)}, u32[]{:S(2)}, u32[]{:S(2)}) collective-permute-start(f32[384,384]{1,0:T(8,128)S(1)} %get-tuple-element.87), channel_id=1, source_target_pairs={{0,2},{2,0},{4,6},{6,4},{8,10},{10,8},{12,14},{14,12},{16,18},{18,... | collective-permute-start | bytes 1769480 | tf_op jit(solution)/shard_map/ppermute | solution.py:64
  19.8 3.1 %collective-permute-start.5 = (bf16[1152,128]{1,0:T(8,128)(2,1)S(1)}, bf16[1152,128]{1,0:T(8,128)(2,1)S(1)}, u32[]{:S(2)}, u32[]{:S(2)}) collective-permute-start(bf16[1152,128]{1,0:T(8,128)(2,1)S(1)} %shard_map.97.refs_0_), channel_id=1, source_target_pairs={{0,2},{2,0},{4,6},{6,4},{8,10},{10,8},{12,14},{14,12},{16,18},{18,... | collective-permute-start | bytes 884744 | tf_op jit(solution)/shard_map/ppermute | solution.py:64
  19.9 2.9 %collective-permute-start.6 = (bf16[128,384]{1,0:T(8,128)(2,1)S(1)}, bf16[128,384]{1,0:T(8,128)(2,1)S(1)}, u32[]{:S(2)}, u32[]{:S(2)}) collective-permute-start(bf16[128,384]{1,0:T(8,128)(2,1)S(1)} %get-tuple-element.82.refs_4_), channel_id=1, source_target_pairs={{0,2},{2,0},{4,6},{6,4},{8,10},{10,8},{12,14},{14,12},{16,18},{18,... | collective-permute-start | bytes 294920 | tf_op jit(solution)/shard_map/ppermute | solution.py:64
  21.6 6.4 %copy-start.2 = (bf16[3,3,384,384]{3,2,1,0:T(8,128)(2,1)S(1)}, bf16[3,3,384,384]{3,2,1,0:T(8,128)(2,1)}, u32[]{:S(2)}) copy-start(bf16[3,3,384,384]{3,2,1,0:T(8,128)(2,1)} %param.8) | copy-start | bytes 7962628
  24.4 13.6 %collective-permute-start.10 = (bf16[224,384]{1,0:T(8,128)(2,1)S(1)}, bf16[224,384]{1,0:T(8,128)(2,1)S(1)}, u32[]{:S(2)}, u32[]{:S(2)}) collective-permute-start(bf16[224,384]{1,0:T(8,128)(2,1)S(1)} %get-tuple-element.94), channel_id=1, source_target_pairs={{0,8},{2,10},{4,12},{6,14},{8,0},{10,2},{12,4},{14,6},{16,24},{18,... | collective-permute-start | bytes 516104 | tf_op jit(solution)/shard_map/ppermute | solution.py:64
  25.1 13.0 %collective-permute-start.11 = (bf16[224,384]{1,0:T(8,128)(2,1)S(1)}, bf16[224,384]{1,0:T(8,128)(2,1)S(1)}, u32[]{:S(2)}, u32[]{:S(2)}) collective-permute-start(bf16[224,384]{1,0:T(8,128)(2,1)S(1)} %get-tuple-element.95), channel_id=1, source_target_pairs={{0,12},{2,14},{4,8},{6,10},{8,4},{10,6},{12,0},{14,2},{16,28},{18,... | collective-permute-start | bytes 516104 | tf_op jit(solution)/shard_map/ppermute | solution.py:64
  27.5 10.6 %collective-permute-start.9 = (bf16[224,384]{1,0:T(8,128)(2,1)S(1)}, bf16[224,384]{1,0:T(8,128)(2,1)S(1)}, u32[]{:S(2)}, u32[]{:S(2)}) collective-permute-start(bf16[224,384]{1,0:T(8,128)(2,1)S(1)} %get-tuple-element.93), channel_id=1, source_target_pairs={{0,4},{2,6},{4,0},{6,2},{8,12},{10,14},{12,8},{14,10},{16,20},{18,... | collective-permute-start | bytes 516104 | tf_op jit(solution)/shard_map/ppermute | solution.py:64
  30.8 5.5 %collective-permute-start.12 = (bf16[216,128]{1,0:T(8,128)(2,1)S(1)}, bf16[216,128]{1,0:T(8,128)(2,1)S(1)}, u32[]{:S(2)}, u32[]{:S(2)}) collective-permute-start(bf16[216,128]{1,0:T(8,128)(2,1)S(1)} %get-tuple-element.118.refs_0_), channel_id=1, source_target_pairs={{0,8},{2,10},{4,12},{6,14},{8,0},{10,2},{12,4},{14,6},{16,24},{18,... | collective-permute-start | bytes 165896 | tf_op jit(solution)/shard_map/ppermute | solution.py:60
  31.4 6.6 %collective-permute-start.13 = (bf16[216,128]{1,0:T(8,128)(2,1)S(1)}, bf16[216,128]{1,0:T(8,128)(2,1)S(1)}, u32[]{:S(2)}, u32[]{:S(2)}) collective-permute-start(bf16[216,128]{1,0:T(8,128)(2,1)S(1)} %get-tuple-element.118.refs_0_), channel_id=1, source_target_pairs={{0,24},{2,26},{4,28},{6,30},{8,16},{10,18},{12,20},{14,22},{16,8},... | collective-permute-start | bytes 165896 | tf_op jit(solution)/shard_map/ppermute | solution.py:60
  38.1 13.5 %collective-permute-start.23 = (bf16[696,128]{1,0:T(8,128)(2,1)S(1)}, bf16[696,128]{1,0:T(8,128)(2,1)S(1)}, u32[]{:S(2)}, u32[]{:S(2)}) collective-permute-start(bf16[696,128]{1,0:T(8,128)(2,1)S(1)} %get-tuple-element.129), channel_id=1, source_target_pairs={{0,1},{1,0},{2,3},{3,2},{4,5},{5,4},{6,7},{7,6},{8,9},{9,8},{10,11... | collective-permute-start | bytes 534536 | tf_op jit(solution)/shard_map/ppermute | solution.py:705
  39.7 8.3 %collective-permute-start.14 = (bf16[224,384]{1,0:T(8,128)(2,1)S(1)}, bf16[224,384]{1,0:T(8,128)(2,1)S(1)}, u32[]{:S(2)}, u32[]{:S(2)}) collective-permute-start(bf16[224,384]{1,0:T(8,128)(2,1)S(1)} %shard_map.105.held_ref), channel_id=1, source_target_pairs={{0,16},{2,18},{4,20},{6,22},{8,24},{10,26},{12,28},{14,30},{16,0},... | collective-permute-start | bytes 516104 | tf_op jit(solution)/shard_map/ppermute | solution.py:64
  40.3 5.4 %collective-permute-start.15 = (bf16[648,128]{1,0:T(8,128)(2,1)S(1)}, bf16[648,128]{1,0:T(8,128)(2,1)S(1)}, u32[]{:S(2)}, u32[]{:S(2)}) collective-permute-start(bf16[648,128]{1,0:T(8,128)(2,1)S(1)} %shard_map.106.refs_0_), channel_id=1, source_target_pairs={{0,4},{2,6},{4,0},{6,2},{8,12},{10,14},{12,8},{14,10},{16,20},{18,... | collective-permute-start | bytes 497672 | tf_op jit(solution)/shard_map/ppermute | solution.py:64
  41.5 8.2 %collective-permute-start.21 = (bf16[528,128]{1,0:T(8,128)(2,1)S(1)}, bf16[528,128]{1,0:T(8,128)(2,1)S(1)}, u32[]{:S(2)}, u32[]{:S(2)}) collective-permute-start(bf16[528,128]{1,0:T(8,128)(2,1)S(1)} %get-tuple-element.127), channel_id=1, source_target_pairs={{0,1},{1,0},{2,3},{3,2},{4,5},{5,4},{6,7},{7,6},{8,9},{9,8},{10,11... | collective-permute-start | bytes 405512 | tf_op jit(solution)/shard_map/ppermute | solution.py:705
  42.0 9.6 %collective-permute-start.22 = (bf16[528,128]{1,0:T(8,128)(2,1)S(1)}, bf16[528,128]{1,0:T(8,128)(2,1)S(1)}, u32[]{:S(2)}, u32[]{:S(2)}) collective-permute-start(bf16[528,128]{1,0:T(8,128)(2,1)S(1)} %get-tuple-element.128), channel_id=1, source_target_pairs={{0,1},{1,0},{2,3},{3,2},{4,5},{5,4},{6,7},{7,6},{8,9},{9,8},{10,11... | collective-permute-start | bytes 405512 | tf_op jit(solution)/shard_map/ppermute | solution.py:705
  48.1 9.4 %collective-permute-start.16 = (bf16[224,384]{1,0:T(8,128)(2,1)S(1)}, bf16[224,384]{1,0:T(8,128)(2,1)S(1)}, u32[]{:S(2)}, u32[]{:S(2)}) collective-permute-start(bf16[224,384]{1,0:T(8,128)(2,1)S(1)} %shard_map.107.refs_0_), channel_id=1, source_target_pairs={{0,4},{2,6},{4,0},{6,2},{8,12},{10,14},{12,8},{14,10},{16,20},{18,... | collective-permute-start | bytes 516104 | tf_op jit(solution)/shard_map/ppermute | solution.py:64
  49.6 7.8 %collective-permute-start.17 = (bf16[224,384]{1,0:T(8,128)(2,1)S(1)}, bf16[224,384]{1,0:T(8,128)(2,1)S(1)}, u32[]{:S(2)}, u32[]{:S(2)}) collective-permute-start(bf16[224,384]{1,0:T(8,128)(2,1)S(1)} %shard_map.107.refs_0_), channel_id=1, source_target_pairs={{0,8},{2,10},{4,12},{6,14},{8,0},{10,2},{12,4},{14,6},{16,24},{18,... | collective-permute-start | bytes 516104 | tf_op jit(solution)/shard_map/ppermute | solution.py:64
  49.6 8.9 %collective-permute-start.18 = (bf16[224,384]{1,0:T(8,128)(2,1)S(1)}, bf16[224,384]{1,0:T(8,128)(2,1)S(1)}, u32[]{:S(2)}, u32[]{:S(2)}) collective-permute-start(bf16[224,384]{1,0:T(8,128)(2,1)S(1)} %shard_map.107.refs_0_), channel_id=1, source_target_pairs={{0,12},{2,14},{4,8},{6,10},{8,4},{10,6},{12,0},{14,2},{16,28},{18,... | collective-permute-start | bytes 516104 | tf_op jit(solution)/shard_map/ppermute | solution.py:64
  51.6 4.4 %collective-permute-start.19 = (bf16[648,128]{1,0:T(8,128)(2,1)S(1)}, bf16[648,128]{1,0:T(8,128)(2,1)S(1)}, u32[]{:S(2)}, u32[]{:S(2)}) collective-permute-start(bf16[648,128]{1,0:T(8,128)(2,1)S(1)} %shard_map.106.refs_0_), channel_id=1, source_target_pairs={{0,2},{2,0},{4,6},{6,4},{8,10},{10,8},{12,14},{14,12},{16,18},{18,... | collective-permute-start | bytes 497672 | tf_op jit(solution)/shard_map/ppermute | solution.py:64
  51.6 4.5 %collective-permute-start.20 = (bf16[648,128]{1,0:T(8,128)(2,1)S(1)}, bf16[648,128]{1,0:T(8,128)(2,1)S(1)}, u32[]{:S(2)}, u32[]{:S(2)}) collective-permute-start(bf16[648,128]{1,0:T(8,128)(2,1)S(1)} %collective-permute-done.15.refs_1_), channel_id=1, source_target_pairs={{0,2},{2,0},{4,6},{6,4},{8,10},{10,8},{12,14},{14,12},{16,18},{18,... | collective-permute-start | bytes 497672 | tf_op jit(solution)/shard_map/ppermute | solution.py:64
  56.0 3.1 %collective-permute-start.24 = (bf16[224,384]{1,0:T(8,128)(2,1)S(1)}, bf16[224,384]{1,0:T(8,128)(2,1)S(1)}, u32[]{:S(2)}, u32[]{:S(2)}) collective-permute-start(bf16[224,384]{1,0:T(8,128)(2,1)S(1)} %shard_map.107.refs_0_), channel_id=1, source_target_pairs={{0,2},{2,0},{4,6},{6,4},{8,10},{10,8},{12,14},{14,12},{16,18},{18,... | collective-permute-start | bytes 516104 | tf_op jit(solution)/shard_map/ppermute | solution.py:64
  58.6 1.9 %collective-permute-start.25 = (bf16[224,384]{1,0:T(8,128)(2,1)S(1)}, bf16[224,384]{1,0:T(8,128)(2,1)S(1)}, u32[]{:S(2)}, u32[]{:S(2)}) collective-permute-start(bf16[224,384]{1,0:T(8,128)(2,1)S(1)} %collective-permute-done.16.refs_1_), channel_id=1, source_target_pairs={{0,2},{2,0},{4,6},{6,4},{8,10},{10,8},{12,14},{14,12},{16,18},{18,... | collective-permute-start | bytes 516104 | tf_op jit(solution)/shard_map/ppermute | solution.py:64
  58.6 1.9 %collective-permute-start.26 = (bf16[224,384]{1,0:T(8,128)(2,1)S(1)}, bf16[224,384]{1,0:T(8,128)(2,1)S(1)}, u32[]{:S(2)}, u32[]{:S(2)}) collective-permute-start(bf16[224,384]{1,0:T(8,128)(2,1)S(1)} %collective-permute-done.17.refs_2_), channel_id=1, source_target_pairs={{0,2},{2,0},{4,6},{6,4},{8,10},{10,8},{12,14},{14,12},{16,18},{18,... | collective-permute-start | bytes 516104 | tf_op jit(solution)/shard_map/ppermute | solution.py:64
  59.1 1.4 %collective-permute-start.27 = (bf16[224,384]{1,0:T(8,128)(2,1)S(1)}, bf16[224,384]{1,0:T(8,128)(2,1)S(1)}, u32[]{:S(2)}, u32[]{:S(2)}) collective-permute-start(bf16[224,384]{1,0:T(8,128)(2,1)S(1)} %collective-permute-done.18.refs_3_), channel_id=1, source_target_pairs={{0,2},{2,0},{4,6},{6,4},{8,10},{10,8},{12,14},{14,12},{16,18},{18,... | collective-permute-start | bytes 516104 | tf_op jit(solution)/shard_map/ppermute | solution.py:64

commit v13 on v12

--- a/solution.py
+++ b/solution.py
@@ -530,9 +530,9 @@
     out_ref[...] = ends.astype(jnp.bfloat16)
 
 
-def parts_of(rows):
-    size = -(-rows // (32 * PARTS)) * 32
-    return [min(size, rows - first) for first in range(0, rows, size)]
+def parts_of(rows, extra):
+    size = (rows + extra) // (32 * PARTS) * 32
+    return [size] * (PARTS - 1) + [rows - size * (PARTS - 1)]
 
 
 def halo_kernel(side, part, n_near, *refs):
@@ -544,7 +544,7 @@
     rows = side * side
     unpack_near(near_refs, near, side, part)
     field = field_ref[...].reshape(rows, part)
-    sizes = parts_of(rows)
+    sizes = parts_of(rows, 4 * side + EXTRA)
     for k, ref in enumerate(packet_refs):
         pack(field[sum(sizes[:k]) : sum(sizes[: k + 1])], ref)
     copy.wait()
@@ -571,7 +571,7 @@
     other_refs, (out_ref, cols, other_cols, other) = refs[:PARTS], refs[PARTS:]
     wide = -(-part // 128) * 128
     lanes = pl.multiple_of(ch * (weight_ref.shape[2] - wide), 128)
-    sizes = parts_of(rows)
+    sizes = parts_of(rows, 4 * side + EXTRA)
     for k, ref in enumerate(other_refs):
         unpack(ref, other, 0, sum(sizes[:k]), sizes[k], part)
     unpack(other_refs[-1], other, packed_shape(sizes[-1], part)[0], rows, 4 * side + EXTRA, part)
@@ -687,8 +687,8 @@
     halos, *packet = call(
         functools.partial(halo_kernel, side, part, len(near)),
         [vmem((block, part), half_bytes)]
-        + [vmem(packed_shape(size, part), half_bytes) for size in parts_of(rows)[:-1]]
-        + [vmem(packed_shape(parts_of(rows)[-1] + block, part), half_bytes)],
+        + [vmem(packed_shape(size, part), half_bytes) for size in parts_of(rows, block)[:-1]]
+        + [vmem(packed_shape(parts_of(rows, block)[-1] + block, part), half_bytes)],
         [*near, tables, field],
         scratch=[pltpu.VMEM((48 * side, part), half_bytes), *table_scratch],
     )

time: 61.8 us -> 61 us (0.987)
    ppermute x20, waiting for transfers between devices: 7.18 us -> 6.02 us  [by_mask(): return lax.ppermute(value, 'tile', [(i, i ^ mask) for i in range(count)])]
    ppermute x3, waiting for transfers between devices: 0.01 us -> 0.77 us  [start_aside(): lax.ppermute(v, 'ch', others)]
  transfers between devices with their start and end apart: 28 -> 28, of which waited for: 7 -> 8; matrix products, arithmetic and copies ran while one was open for 1% -> 1% of each run, Pallas kernels for 23% -> 24%
where the time goes in v13:
time: 61 us; the launch traced here: 60.7 us
  starting transfers between devices  27.6 us (45%)
  Pallas kernels  19.2 us (31%)
  waiting for transfers between devices  10.3 us (17%)
  local copies, waits for them, and re-layouts  2.09 us (3%)
  between operations  0.79 us (1%)
  other arithmetic  0.74 us (1%)
    pallas_call x16, Pallas kernels, call(): pl.pallas_call(kernel, out_shape=tuple(outs), in_specs=in_specs, out_spec...  16.8 us
    ppermute x20, starting transfers between devices, by_mask(): return lax.ppermute(value, 'tile', [(i, i ^ mask) for i in range(count)])  13.9 us
    ppermute x4, starting transfers between devices, by_swap(): return lax.ppermute(value, 'tile', pairs)  7.17 us
    ppermute x20, waiting for transfers between devices, by_mask(): return lax.ppermute(value, 'tile', [(i, i ^ mask) for i in range(count)])  6.02 us
    ppermute x4, waiting for transfers between devices, by_swap(): return lax.ppermute(value, 'tile', pairs)  3.53 us
    ppermute x3, starting transfers between devices, start_aside(): lax.ppermute(v, 'ch', others)  3.52 us
    ppermute x1, starting transfers between devices, body(): cot_other = lax.ppermute(cot_own, 'ch', others)  3 us
    pallas_call x2, Pallas kernels, unfold(): pl.pallas_call(functools.partial(unfold_kernel, whole.shape[0] // 2, chun...  2.41 us
  transfers between devices with their start and end apart: 28, of which 8 were waited for; matrix products, arithmetic and copies ran while one was open for 1% of the time, Pallas kernels for 24%

profile of v13, /device:TPU:0, one launch (start us, length us, event | category | flops | bytes accessed | tf_op | source)
XLA Modules:
  0.0 60.7 jit_solution(559568079098000610)
XLA Ops:
  0.6 3.0 %collective-permute-start.4 = (bf16[1024,192]{1,0:T(8,128)(2,1)}, bf16[1024,192]{1,0:T(8,128)(2,1)S(1)}, u32[]{:S(2)}, u32[]{:S(2)}) collective-permute-start(bf16[1024,192]{1,0:T(8,128)(2,1)} %bitcast.11), channel_id=1, source_target_pairs={{0,1},{1,0},{2,3},{3,2},{4,5},{5,4},{6,7},{7,6},{8,9},{9,8},{10,11... | collective-permute-start | bytes 1179656 | tf_op jit(solution)/shard_map/ppermute | solution.py:611
  3.6 1.0 %copy-done = bf16[1,32,32,192]{3,2,1,0:T(8,128)(2,1)S(1)} copy-done((bf16[1,32,32,192]{3,2,1,0:T(8,128)(2,1)S(1)}, bf16[1,32,32,192]{3,2,1,0:T(8,128)(2,1)}, u32[]{:S(2)}) %copy-start) | copy-done | bytes 393240
  4.7 0.1 shard_map.94
  4.8 1.6 %collective-permute-start.1 = (bf16[192,128]{1,0:T(8,128)(2,1)S(1)}, bf16[192,128]{1,0:T(8,128)(2,1)S(1)}, u32[]{:S(2)}, u32[]{:S(2)}) collective-permute-start(bf16[192,128]{1,0:T(8,128)(2,1)S(1)} %get-tuple-element.71.refs_0_), channel_id=1, source_target_pairs={{0,8},{2,10},{4,12},{6,14},{8,0},{10,2},{12,4},{14,6},{16,24},{18,... | collective-permute-start | bytes 147464 | tf_op jit(solution)/shard_map/ppermute | solution.py:60
  6.4 2.5 %collective-permute-start.2 = (bf16[192,128]{1,0:T(8,128)(2,1)S(1)}, bf16[192,128]{1,0:T(8,128)(2,1)S(1)}, u32[]{:S(2)}, u32[]{:S(2)}) collective-permute-start(bf16[192,128]{1,0:T(8,128)(2,1)S(1)} %get-tuple-element.71.refs_0_), channel_id=1, source_target_pairs={{0,24},{2,26},{4,28},{6,30},{8,16},{10,18},{12,20},{14,22},{16,8},... | collective-permute-start | bytes 147464 | tf_op jit(solution)/shard_map/ppermute | solution.py:60
  8.9 1.5 %collective-permute-start = (bf16[192,128]{1,0:T(8,128)(2,1)S(1)}, bf16[192,128]{1,0:T(8,128)(2,1)S(1)}, u32[]{:S(2)}, u32[]{:S(2)}) collective-permute-start(bf16[192,128]{1,0:T(8,128)(2,1)S(1)} %get-tuple-element.71.refs_0_), channel_id=1, source_target_pairs={{0,4},{2,6},{4,0},{6,2},{8,12},{10,14},{12,8},{14,10},{16,20},{18,... | collective-permute-start | bytes 147464 | tf_op jit(solution)/shard_map/ppermute | solution.py:64
  10.4 1.9 %collective-permute-done.2.refs_1_.refs_3_ = bf16[192,128]{1,0:T(8,128)(2,1)S(1)} collective-permute-done((bf16[192,128]{1,0:T(8,128)(2,1)S(1)}, bf16[192,128]{1,0:T(8,128)(2,1)S(1)}, u32[]{:S(2)}, u32[]{:S(2)}) %collective-permute-start.2) | collective-permute-done | bytes 49184 | tf_op jit(solution)/shard_map/ppermute | solution.py:60
  12.3 1.6 %collective-permute-start.3 = (bf16[384,128]{1,0:T(8,128)(2,1)S(1)}, bf16[384,128]{1,0:T(8,128)(2,1)S(1)}, u32[]{:S(2)}, u32[]{:S(2)}) collective-permute-start(bf16[384,128]{1,0:T(8,128)(2,1)S(1)} %shard_map.95), channel_id=1, source_target_pairs={{0,4},{2,6},{4,0},{6,2},{8,12},{10,14},{12,8},{14,10},{16,20},{18,... | collective-permute-start | bytes 294920 | tf_op jit(solution)/shard_map/ppermute | solution.py:64
  13.9 0.7 %pad_add_fusion.tables_in.refs_2_ = s32[16,16]{1,0:T(8,128)S(1)} fusion(s32[4,16]{1,0:T(4,128)} %bitcast.17, s32[4,16]{1,0:T(4,128)} %bitcast.18, s32[4,16]{1,0:T(4,128)} %bitcast.19, s32[4,16]{1,0:T(4,128)} %bitcast.20), kind=kLoop, calls=%fused_computation | loop fusion | flops 768 | bytes 2048 | tf_op jit(solution)/shard_map/concatenate | solution.py:619
  14.7 1.0 %copy-done.1 = bf16[1,32,32,192]{3,2,1,0:T(8,128)(2,1)S(1)} copy-done((bf16[1,32,32,192]{3,2,1,0:T(8,128)(2,1)S(1)}, bf16[1,32,32,192]{3,2,1,0:T(8,128)(2,1)}, u32[]{:S(2)}) %copy-start.1) | copy-done | bytes 393240
  15.7 1.1 %shard_map.96 = (bf16[512,1536]{1,0:T(8,128)(2,1)S(1)}, bf16[1024,192]{1,0:T(8,128)(2,1)S(1)}) custom-call(s32[16,16]{1,0:T(8,128)S(1)} %pad_add_fusion.tables_in.refs_2_, bf16[1024,192]{1,0:T(8,128)(2,1)S(1)} %bitcast.12), custom_call_target="tpu_custom_call" | custom-call | bytes 2360320 | tf_op jit(solution)/shard_map/pallas_call | solution.py:111
  16.8 0.2 collective-permute-done.3.refs_4_
  17.0 1.3 %shard_map.98 = (f32[384,384]{1,0:T(8,128)S(1)}, bf16[1152,384]{1,0:T(8,128)(2,1)S(1)}, bf16[128,384]{1,0:T(8,128)(2,1)S(1)}, bf16[3,192,1024]{2,1,0:T(8,128)(2,1)S(1)}) custom-call(bf16[32,32,192]{2,1,0:T(8,128)(2,1)S(1)} %get-tuple-element.76.field_ref.refs_3_, bf16[1024,192]{1,0:T(8,128)(2,1)S(1)} %get-tuple-element.77.own_ref, ...), custom_call_target="tpu_custom_call" | custom-call | flops 339738624 | bytes 3932160 | tf_op jit(solution)/shard_map/pallas_call | solution.py:111
  18.4 0.8 %shard_map.99 = f32[480,384]{1,0:T(8,128)S(1)} custom-call(bf16[3,192,1024]{2,1,0:T(8,128)(2,1)S(1)} %get-tuple-element.79.cols, bf16[1152,384]{1,0:T(8,128)(2,1)S(1)} %get-tuple-element.96.tall), custom_call_target="tpu_custom_call" | custom-call | flops 1358954496 | bytes 2801664 | tf_op jit(solution)/shard_map/pallas_call | solution.py:111
  19.2 0.1 collective-permute-start.8
  19.3 0.5 collective-permute-start.7
  19.8 0.1 collective-permute-start.5
  19.9 0.4 collective-permute-start.6
  20.4 1.2 %shard_map.100.refs_3_ = f32[864,384]{1,0:T(8,128)S(1)} custom-call(bf16[3,192,1024]{2,1,0:T(8,128)(2,1)S(1)} %get-tuple-element.79.cols, bf16[1152,384]{1,0:T(8,128)(2,1)S(1)} %get-tuple-element.96.tall), custom_call_target="tpu_custom_call" | custom-call | tf_op jit(solution)/shard_map/pallas_call | solution.py:111
  21.6 1.3 %collective-permute-done.6.refs_5_ = bf16[128,384]{1,0:T(8,128)(2,1)S(1)} collective-permute-done((bf16[128,384]{1,0:T(8,128)(2,1)S(1)}, bf16[128,384]{1,0:T(8,128)(2,1)S(1)}, u32[]{:S(2)}, u32[]{:S(2)}) %collective-permute-start.6) | collective-permute-done | bytes 98336 | tf_op jit(solution)/shard_map/ppermute | solution.py:64
  22.9 1.5 %shard_map.101 = (f32[224,384]{1,0:T(8,128)S(1)}, bf16[224,384]{1,0:T(8,128)(2,1)S(1)}, bf16[224,384]{1,0:T(8,128)(2,1)S(1)}, bf16[224,384]{1,0:T(8,128)(2,1)S(1)}) custom-call(bf16[1152,128]{1,0:T(8,128)(2,1)S(1)} %shard_map.97.refs_0_, bf16[1152,128]{1,0:T(8,128)(2,1)S(1)} %collective-permute-done.5.refs_1_, ...), custom_call_target="tpu_custom_call" | custom-call | bytes 5873664 | tf_op jit(solution)/shard_map/pallas_call | solution.py:111
  24.4 0.6 %collective-permute-start.10 = (bf16[224,384]{1,0:T(8,128)(2,1)S(1)}, bf16[224,384]{1,0:T(8,128)(2,1)S(1)}, u32[]{:S(2)}, u32[]{:S(2)}) collective-permute-start(bf16[224,384]{1,0:T(8,128)(2,1)S(1)} %get-tuple-element.94), channel_id=1, source_target_pairs={{0,8},{2,10},{4,12},{6,14},{8,0},{10,2},{12,4},{14,6},{16,24},{18,... | collective-permute-start | bytes 516104 | tf_op jit(solution)/shard_map/ppermute | solution.py:64
  25.1 2.4 %collective-permute-start.11 = (bf16[224,384]{1,0:T(8,128)(2,1)S(1)}, bf16[224,384]{1,0:T(8,128)(2,1)S(1)}, u32[]{:S(2)}, u32[]{:S(2)}) collective-permute-start(bf16[224,384]{1,0:T(8,128)(2,1)S(1)} %get-tuple-element.95), channel_id=1, source_target_pairs={{0,12},{2,14},{4,8},{6,10},{8,4},{10,6},{12,0},{14,2},{16,28},{18,... | collective-permute-start | bytes 516104 | tf_op jit(solution)/shard_map/ppermute | solution.py:64
  27.5 0.5 collective-permute-start.9
  28.0 2.9 %shard_map.102 = (f32[1024,192]{1,0:T(8,128)S(1)}, bf16[216,128]{1,0:T(8,128)(2,1)S(1)}) custom-call(bf16[1152,384]{1,0:T(8,128)(2,1)S(1)} %get-tuple-element.96.tall, bf16[9,384,384]{2,1,0:T(8,128)(2,1)S(1)} %bitcast.13), custom_call_target="tpu_custom_call" | custom-call | flops 1358954496 | bytes 4380672 | tf_op jit(solution)/shard_map/pallas_call | solution.py:111
  30.8 0.6 collective-permute-start.12
  31.4 2.5 %collective-permute-start.13 = (bf16[216,128]{1,0:T(8,128)(2,1)S(1)}, bf16[216,128]{1,0:T(8,128)(2,1)S(1)}, u32[]{:S(2)}, u32[]{:S(2)}) collective-permute-start(bf16[216,128]{1,0:T(8,128)(2,1)S(1)} %get-tuple-element.118.refs_0_), channel_id=1, source_target_pairs={{0,24},{2,26},{4,28},{6,30},{8,16},{10,18},{12,20},{14,22},{16,8},... | collective-permute-start | bytes 165896 | tf_op jit(solution)/shard_map/ppermute | solution.py:60
  33.9 1.2 %shard_map.104.place_ref = bf16[128,1728]{1,0:T(8,128)(2,1)S(1)} custom-call(s32[16,16]{1,0:T(8,128)S(1)} %pad_add_fusion.tables_in.refs_2_), custom_call_target="tpu_custom_call" | custom-call | bytes 443392 | tf_op jit(solution)/shard_map/pallas_call | solution.py:111
  35.1 1.3 %shard_map.103 = (bf16[144,192]{1,0:T(8,128)(2,1)S(1)}, bf16[576,128]{1,0:T(8,128)(2,1)S(1)}, bf16[576,128]{1,0:T(8,128)(2,1)S(1)}, bf16[600,128]{1,0:T(8,128)(2,1)S(1)}) custom-call(bf16[1152,128]{1,0:T(8,128)(2,1)S(1)} %shard_map.97.refs_0_, bf16[1152,128]{1,0:T(8,128)(2,1)S(1)} %collective-permute-done.5.refs_1_, ...), custom_call_target="tpu_custom_call" | custom-call | bytes 1487872 | tf_op jit(solution)/shard_map/pallas_call | solution.py:111
  36.4 1.6 %collective-permute-done.13.refs_2_ = bf16[216,128]{1,0:T(8,128)(2,1)S(1)} collective-permute-done((bf16[216,128]{1,0:T(8,128)(2,1)S(1)}, bf16[216,128]{1,0:T(8,128)(2,1)S(1)}, u32[]{:S(2)}, u32[]{:S(2)}) %collective-permute-start.13) | collective-permute-done | bytes 55328 | tf_op jit(solution)/shard_map/ppermute | solution.py:60
  38.0 0.1 shard_map.105.held_ref
  38.1 0.6 %collective-permute-start.14 = (bf16[224,384]{1,0:T(8,128)(2,1)S(1)}, bf16[224,384]{1,0:T(8,128)(2,1)S(1)}, u32[]{:S(2)}, u32[]{:S(2)}) collective-permute-start(bf16[224,384]{1,0:T(8,128)(2,1)S(1)} %shard_map.105.held_ref), channel_id=1, source_target_pairs={{0,16},{2,18},{4,20},{6,22},{8,24},{10,26},{12,28},{14,30},{16,0},... | collective-permute-start | bytes 516104 | tf_op jit(solution)/shard_map/ppermute | solution.py:64
  38.8 1.2 %collective-permute-start.15 = (bf16[648,128]{1,0:T(8,128)(2,1)S(1)}, bf16[648,128]{1,0:T(8,128)(2,1)S(1)}, u32[]{:S(2)}, u32[]{:S(2)}) collective-permute-start(bf16[648,128]{1,0:T(8,128)(2,1)S(1)} %shard_map.106.refs_0_), channel_id=1, source_target_pairs={{0,4},{2,6},{4,0},{6,2},{8,12},{10,14},{12,8},{14,10},{16,20},{18,... | collective-permute-start | bytes 497672 | tf_op jit(solution)/shard_map/ppermute | solution.py:64
  40.0 1.5 %collective-permute-start.23 = (bf16[600,128]{1,0:T(8,128)(2,1)S(1)}, bf16[600,128]{1,0:T(8,128)(2,1)S(1)}, u32[]{:S(2)}, u32[]{:S(2)}) collective-permute-start(bf16[600,128]{1,0:T(8,128)(2,1)S(1)} %get-tuple-element.129), channel_id=1, source_target_pairs={{0,1},{1,0},{2,3},{3,2},{4,5},{5,4},{6,7},{7,6},{8,9},{9,8},{10,11... | collective-permute-start | bytes 460808 | tf_op jit(solution)/shard_map/ppermute | solution.py:705
  41.5 0.5 collective-permute-start.21
  42.0 1.5 %collective-permute-start.22 = (bf16[576,128]{1,0:T(8,128)(2,1)S(1)}, bf16[576,128]{1,0:T(8,128)(2,1)S(1)}, u32[]{:S(2)}, u32[]{:S(2)}) collective-permute-start(bf16[576,128]{1,0:T(8,128)(2,1)S(1)} %get-tuple-element.128), channel_id=1, source_target_pairs={{0,1},{1,0},{2,3},{3,2},{4,5},{5,4},{6,7},{7,6},{8,9},{9,8},{10,11... | collective-permute-start | bytes 442376 | tf_op jit(solution)/shard_map/ppermute | solution.py:705
  43.5 0.7 %collective-permute-done.15.refs_1_ = bf16[648,128]{1,0:T(8,128)(2,1)S(1)} collective-permute-done((bf16[648,128]{1,0:T(8,128)(2,1)S(1)}, bf16[648,128]{1,0:T(8,128)(2,1)S(1)}, u32[]{:S(2)}, u32[]{:S(2)}) %collective-permute-start.15) | collective-permute-done | bytes 165920 | tf_op jit(solution)/shard_map/ppermute | solution.py:64
  44.2 2.6 %collective-permute-done.14.got_ref = bf16[224,384]{1,0:T(8,128)(2,1)S(1)} collective-permute-done((bf16[224,384]{1,0:T(8,128)(2,1)S(1)}, bf16[224,384]{1,0:T(8,128)(2,1)S(1)}, u32[]{:S(2)}, u32[]{:S(2)}) %collective-permute-start.14) | collective-permute-done | bytes 172064 | tf_op jit(solution)/shard_map/ppermute | solution.py:64
  46.9 1.6 %collective-permute-start.16 = (bf16[224,384]{1,0:T(8,128)(2,1)S(1)}, bf16[224,384]{1,0:T(8,128)(2,1)S(1)}, u32[]{:S(2)}, u32[]{:S(2)}) collective-permute-start(bf16[224,384]{1,0:T(8,128)(2,1)S(1)} %shard_map.107.refs_0_), channel_id=1, source_target_pairs={{0,4},{2,6},{4,0},{6,2},{8,12},{10,14},{12,8},{14,10},{16,20},{18,... | collective-permute-start | bytes 516104 | tf_op jit(solution)/shard_map/ppermute | solution.py:64
  48.4 0.7 %collective-permute-done.21.refs_0_ = bf16[576,128]{1,0:T(8,128)(2,1)S(1)} collective-permute-done((bf16[576,128]{1,0:T(8,128)(2,1)S(1)}, bf16[576,128]{1,0:T(8,128)(2,1)S(1)}, u32[]{:S(2)}, u32[]{:S(2)}) %collective-permute-start.21) | collective-permute-done | bytes 147488 | tf_op jit(solution)/shard_map/ppermute | solution.py:705
  49.2 1.6 %collective-permute-start.18 = (bf16[224,384]{1,0:T(8,128)(2,1)S(1)}, bf16[224,384]{1,0:T(8,128)(2,1)S(1)}, u32[]{:S(2)}, u32[]{:S(2)}) collective-permute-start(bf16[224,384]{1,0:T(8,128)(2,1)S(1)} %shard_map.107.refs_0_), channel_id=1, source_target_pairs={{0,12},{2,14},{4,8},{6,10},{8,4},{10,6},{12,0},{14,2},{16,28},{18,... | collective-permute-start | bytes 516104 | tf_op jit(solution)/shard_map/ppermute | solution.py:64
  50.8 0.5 collective-permute-start.20
  51.3 3.9 %shard_map.109 = bf16[1024,192]{1,0:T(8,128)(2,1)} custom-call(bf16[32,32,192]{2,1,0:T(8,128)(2,1)S(1)} %get-tuple-element.76.field_ref.refs_3_, bf16[144,192]{1,0:T(8,128)(2,1)S(1)} %get-tuple-element.126.halos_ref, bf16[9,384,384]{2,1,0:T(8,128)(2,1)S(1)} %bitcast.14, bf16[576,128]{1,0:T(8,128)(2,1)S(1)} %collective-permute-done.21.refs_0_, ...), custom_call_target="tpu_custom_call" | custom-call | flops 2717908992 | bytes 3944448 | tf_op jit(solution)/shard_map/pallas_call | solution.py:111
  55.2 1.3 %shard_map.108 = bf16[1024,192]{1,0:T(8,128)(2,1)} custom-call(bf16[128,1728]{1,0:T(8,128)(2,1)S(1)} %shard_map.104.place_ref, f32[1024,192]{1,0:T(8,128)S(1)} %get-tuple-element.123.inner_ref, bf16[648,128]{1,0:T(8,128)(2,1)S(1)} %shard_map.106.refs_0_, bf16[648,128]{1,0:T(8,128)(2,1)S(1)} %collective-permute-done.15.refs_1_, ...), custom_call_target="tpu_custom_call" | custom-call | bytes 2285568 | tf_op jit(solution)/shard_map/pallas_call | solution.py:111
  56.6 1.2 %collective-permute-done.18.refs_3_ = bf16[224,384]{1,0:T(8,128)(2,1)S(1)} collective-permute-done((bf16[224,384]{1,0:T(8,128)(2,1)S(1)}, bf16[224,384]{1,0:T(8,128)(2,1)S(1)}, u32[]{:S(2)}, u32[]{:S(2)}) %collective-permute-start.18) | collective-permute-done | bytes 172064 | tf_op jit(solution)/shard_map/ppermute | solution.py:64
  57.7 0.5 collective-permute-start.26
  58.3 1.4 %shard_map.110.refs_0_ = f32[1728,384]{1,0:T(8,128)} custom-call(bf16[224,384]{1,0:T(8,128)(2,1)S(1)} %shard_map.107.refs_0_, bf16[224,384]{1,0:T(8,128)(2,1)S(1)} %collective-permute-done.16.refs_1_, bf16[224,384]{1,0:T(8,128)(2,1)S(1)} %collective-permute-done.17.refs_2_, bf16[224,384]{1,0:T(8,128)(2,1)S(1)} %collective-permute-done.18.refs_3_, ...), custom_call_target="tpu_custom_call" | custom-call | tf_op jit(solution)/shard_map/pallas_call | solution.py:453
  59.7 1.1 %shard_map.111 = f32[1728,384]{1,0:T(8,128)} custom-call(f32[1728,384]{1,0:T(8,128)} %shard_map.110.refs_0_, bf16[224,384]{1,0:T(8,128)(2,1)S(1)} %collective-permute-done.25.refs_1_, bf16[224,384]{1,0:T(8,128)(2,1)S(1)} %collective-permute-done.26.refs_2_, bf16[224,384]{1,0:T(8,128)(2,1)S(1)} %collective-permute-done.27.refs_3_), custom_call_target="tpu_custom_call", output_to_operand_aliasing={{}: (0, {})} | custom-call | tf_op jit(solution)/shard_map/pallas_call | solution.py:453
  (33 shorter events, 0.2 us)
Async XLA Ops:
  0.6 16.4 %collective-permute-start.4 = (bf16[1024,192]{1,0:T(8,128)(2,1)}, bf16[1024,192]{1,0:T(8,128)(2,1)S(1)}, u32[]{:S(2)}, u32[]{:S(2)}) collective-permute-start(bf16[1024,192]{1,0:T(8,128)(2,1)} %bitcast.11), channel_id=1, source_target_pairs={{0,1},{1,0},{2,3},{3,2},{4,5},{5,4},{6,7},{7,6},{8,9},{9,8},{10,11... | collective-permute-start | bytes 1179656 | tf_op jit(solution)/shard_map/ppermute | solution.py:611
  3.6 1.0 %copy-start = (bf16[1,32,32,192]{3,2,1,0:T(8,128)(2,1)S(1)}, bf16[1,32,32,192]{3,2,1,0:T(8,128)(2,1)}, u32[]{:S(2)}) copy-start(bf16[1,32,32,192]{3,2,1,0:T(8,128)(2,1)} %param.7) | copy-start | bytes 1179652
  4.8 5.6 %collective-permute-start.1 = (bf16[192,128]{1,0:T(8,128)(2,1)S(1)}, bf16[192,128]{1,0:T(8,128)(2,1)S(1)}, u32[]{:S(2)}, u32[]{:S(2)}) collective-permute-start(bf16[192,128]{1,0:T(8,128)(2,1)S(1)} %get-tuple-element.71.refs_0_), channel_id=1, source_target_pairs={{0,8},{2,10},{4,12},{6,14},{8,0},{10,2},{12,4},{14,6},{16,24},{18,... | collective-permute-start | bytes 147464 | tf_op jit(solution)/shard_map/ppermute | solution.py:60
  6.4 5.9 %collective-permute-start.2 = (bf16[192,128]{1,0:T(8,128)(2,1)S(1)}, bf16[192,128]{1,0:T(8,128)(2,1)S(1)}, u32[]{:S(2)}, u32[]{:S(2)}) collective-permute-start(bf16[192,128]{1,0:T(8,128)(2,1)S(1)} %get-tuple-element.71.refs_0_), channel_id=1, source_target_pairs={{0,24},{2,26},{4,28},{6,30},{8,16},{10,18},{12,20},{14,22},{16,8},... | collective-permute-start | bytes 147464 | tf_op jit(solution)/shard_map/ppermute | solution.py:60
  8.9 7.9 %collective-permute-start = (bf16[192,128]{1,0:T(8,128)(2,1)S(1)}, bf16[192,128]{1,0:T(8,128)(2,1)S(1)}, u32[]{:S(2)}, u32[]{:S(2)}) collective-permute-start(bf16[192,128]{1,0:T(8,128)(2,1)S(1)} %get-tuple-element.71.refs_0_), channel_id=1, source_target_pairs={{0,4},{2,6},{4,0},{6,2},{8,12},{10,14},{12,8},{14,10},{16,20},{18,... | collective-permute-start | bytes 147464 | tf_op jit(solution)/shard_map/ppermute | solution.py:64
  12.3 4.7 %collective-permute-start.3 = (bf16[384,128]{1,0:T(8,128)(2,1)S(1)}, bf16[384,128]{1,0:T(8,128)(2,1)S(1)}, u32[]{:S(2)}, u32[]{:S(2)}) collective-permute-start(bf16[384,128]{1,0:T(8,128)(2,1)S(1)} %shard_map.95), channel_id=1, source_target_pairs={{0,4},{2,6},{4,0},{6,2},{8,12},{10,14},{12,8},{14,10},{16,20},{18,... | collective-permute-start | bytes 294920 | tf_op jit(solution)/shard_map/ppermute | solution.py:64
  14.7 1.0 %copy-start.1 = (bf16[1,32,32,192]{3,2,1,0:T(8,128)(2,1)S(1)}, bf16[1,32,32,192]{3,2,1,0:T(8,128)(2,1)}, u32[]{:S(2)}) copy-start(bf16[1,32,32,192]{3,2,1,0:T(8,128)(2,1)} %param.9) | copy-start | bytes 1179652
  19.2 3.7 %collective-permute-start.8 = (f32[480,384]{1,0:T(8,128)S(1)}, f32[480,384]{1,0:T(8,128)S(1)}, u32[]{:S(2)}, u32[]{:S(2)}) collective-permute-start(f32[480,384]{1,0:T(8,128)S(1)} %shard_map.99), channel_id=1, source_target_pairs={{0,2},{2,0},{4,6},{6,4},{8,10},{10,8},{12,14},{14,12},{16,18},{18,... | collective-permute-start | bytes 2211848 | tf_op jit(solution)/shard_map/ppermute | solution.py:64
  19.3 3.6 %collective-permute-start.7 = (f32[384,384]{1,0:T(8,128)S(1)}, f32[384,384]{1,0:T(8,128)S(1)}, u32[]{:S(2)}, u32[]{:S(2)}) collective-permute-start(f32[384,384]{1,0:T(8,128)S(1)} %get-tuple-element.87), channel_id=1, source_target_pairs={{0,2},{2,0},{4,6},{6,4},{8,10},{10,8},{12,14},{14,12},{16,18},{18,... | collective-permute-start | bytes 1769480 | tf_op jit(solution)/shard_map/ppermute | solution.py:64
  19.8 3.1 %collective-permute-start.5 = (bf16[1152,128]{1,0:T(8,128)(2,1)S(1)}, bf16[1152,128]{1,0:T(8,128)(2,1)S(1)}, u32[]{:S(2)}, u32[]{:S(2)}) collective-permute-start(bf16[1152,128]{1,0:T(8,128)(2,1)S(1)} %shard_map.97.refs_0_), channel_id=1, source_target_pairs={{0,2},{2,0},{4,6},{6,4},{8,10},{10,8},{12,14},{14,12},{16,18},{18,... | collective-permute-start | bytes 884744 | tf_op jit(solution)/shard_map/ppermute | solution.py:64
  19.9 2.9 %collective-permute-start.6 = (bf16[128,384]{1,0:T(8,128)(2,1)S(1)}, bf16[128,384]{1,0:T(8,128)(2,1)S(1)}, u32[]{:S(2)}, u32[]{:S(2)}) collective-permute-start(bf16[128,384]{1,0:T(8,128)(2,1)S(1)} %get-tuple-element.82.refs_4_), channel_id=1, source_target_pairs={{0,2},{2,0},{4,6},{6,4},{8,10},{10,8},{12,14},{14,12},{16,18},{18,... | collective-permute-start | bytes 294920 | tf_op jit(solution)/shard_map/ppermute | solution.py:64
  21.6 6.4 %copy-start.2 = (bf16[3,3,384,384]{3,2,1,0:T(8,128)(2,1)S(1)}, bf16[3,3,384,384]{3,2,1,0:T(8,128)(2,1)}, u32[]{:S(2)}) copy-start(bf16[3,3,384,384]{3,2,1,0:T(8,128)(2,1)} %param.8) | copy-start | bytes 7962628
  24.4 13.6 %collective-permute-start.10 = (bf16[224,384]{1,0:T(8,128)(2,1)S(1)}, bf16[224,384]{1,0:T(8,128)(2,1)S(1)}, u32[]{:S(2)}, u32[]{:S(2)}) collective-permute-start(bf16[224,384]{1,0:T(8,128)(2,1)S(1)} %get-tuple-element.94), channel_id=1, source_target_pairs={{0,8},{2,10},{4,12},{6,14},{8,0},{10,2},{12,4},{14,6},{16,24},{18,... | collective-permute-start | bytes 516104 | tf_op jit(solution)/shard_map/ppermute | solution.py:64
  25.1 13.0 %collective-permute-start.11 = (bf16[224,384]{1,0:T(8,128)(2,1)S(1)}, bf16[224,384]{1,0:T(8,128)(2,1)S(1)}, u32[]{:S(2)}, u32[]{:S(2)}) collective-permute-start(bf16[224,384]{1,0:T(8,128)(2,1)S(1)} %get-tuple-element.95), channel_id=1, source_target_pairs={{0,12},{2,14},{4,8},{6,10},{8,4},{10,6},{12,0},{14,2},{16,28},{18,... | collective-permute-start | bytes 516104 | tf_op jit(solution)/shard_map/ppermute | solution.py:64
  27.5 10.6 %collective-permute-start.9 = (bf16[224,384]{1,0:T(8,128)(2,1)S(1)}, bf16[224,384]{1,0:T(8,128)(2,1)S(1)}, u32[]{:S(2)}, u32[]{:S(2)}) collective-permute-start(bf16[224,384]{1,0:T(8,128)(2,1)S(1)} %get-tuple-element.93), channel_id=1, source_target_pairs={{0,4},{2,6},{4,0},{6,2},{8,12},{10,14},{12,8},{14,10},{16,20},{18,... | collective-permute-start | bytes 516104 | tf_op jit(solution)/shard_map/ppermute | solution.py:64
  30.8 5.5 %collective-permute-start.12 = (bf16[216,128]{1,0:T(8,128)(2,1)S(1)}, bf16[216,128]{1,0:T(8,128)(2,1)S(1)}, u32[]{:S(2)}, u32[]{:S(2)}) collective-permute-start(bf16[216,128]{1,0:T(8,128)(2,1)S(1)} %get-tuple-element.118.refs_0_), channel_id=1, source_target_pairs={{0,8},{2,10},{4,12},{6,14},{8,0},{10,2},{12,4},{14,6},{16,24},{18,... | collective-permute-start | bytes 165896 | tf_op jit(solution)/shard_map/ppermute | solution.py:60
  31.4 6.6 %collective-permute-start.13 = (bf16[216,128]{1,0:T(8,128)(2,1)S(1)}, bf16[216,128]{1,0:T(8,128)(2,1)S(1)}, u32[]{:S(2)}, u32[]{:S(2)}) collective-permute-start(bf16[216,128]{1,0:T(8,128)(2,1)S(1)} %get-tuple-element.118.refs_0_), channel_id=1, source_target_pairs={{0,24},{2,26},{4,28},{6,30},{8,16},{10,18},{12,20},{14,22},{16,8},... | collective-permute-start | bytes 165896 | tf_op jit(solution)/shard_map/ppermute | solution.py:60
  38.1 8.7 %collective-permute-start.14 = (bf16[224,384]{1,0:T(8,128)(2,1)S(1)}, bf16[224,384]{1,0:T(8,128)(2,1)S(1)}, u32[]{:S(2)}, u32[]{:S(2)}) collective-permute-start(bf16[224,384]{1,0:T(8,128)(2,1)S(1)} %shard_map.105.held_ref), channel_id=1, source_target_pairs={{0,16},{2,18},{4,20},{6,22},{8,24},{10,26},{12,28},{14,30},{16,0},... | collective-permute-start | bytes 516104 | tf_op jit(solution)/shard_map/ppermute | solution.py:64
  38.8 5.4 %collective-permute-start.15 = (bf16[648,128]{1,0:T(8,128)(2,1)S(1)}, bf16[648,128]{1,0:T(8,128)(2,1)S(1)}, u32[]{:S(2)}, u32[]{:S(2)}) collective-permute-start(bf16[648,128]{1,0:T(8,128)(2,1)S(1)} %shard_map.106.refs_0_), channel_id=1, source_target_pairs={{0,4},{2,6},{4,0},{6,2},{8,12},{10,14},{12,8},{14,10},{16,20},{18,... | collective-permute-start | bytes 497672 | tf_op jit(solution)/shard_map/ppermute | solution.py:64
  40.0 10.8 %collective-permute-start.23 = (bf16[600,128]{1,0:T(8,128)(2,1)S(1)}, bf16[600,128]{1,0:T(8,128)(2,1)S(1)}, u32[]{:S(2)}, u32[]{:S(2)}) collective-permute-start(bf16[600,128]{1,0:T(8,128)(2,1)S(1)} %get-tuple-element.129), channel_id=1, source_target_pairs={{0,1},{1,0},{2,3},{3,2},{4,5},{5,4},{6,7},{7,6},{8,9},{9,8},{10,11... | collective-permute-start | bytes 460808 | tf_op jit(solution)/shard_map/ppermute | solution.py:705
  41.5 7.7 %collective-permute-start.21 = (bf16[576,128]{1,0:T(8,128)(2,1)S(1)}, bf16[576,128]{1,0:T(8,128)(2,1)S(1)}, u32[]{:S(2)}, u32[]{:S(2)}) collective-permute-start(bf16[576,128]{1,0:T(8,128)(2,1)S(1)} %get-tuple-element.127), channel_id=1, source_target_pairs={{0,1},{1,0},{2,3},{3,2},{4,5},{5,4},{6,7},{7,6},{8,9},{9,8},{10,11... | collective-permute-start | bytes 442376 | tf_op jit(solution)/shard_map/ppermute | solution.py:705
  42.0 8.7 %collective-permute-start.22 = (bf16[576,128]{1,0:T(8,128)(2,1)S(1)}, bf16[576,128]{1,0:T(8,128)(2,1)S(1)}, u32[]{:S(2)}, u32[]{:S(2)}) collective-permute-start(bf16[576,128]{1,0:T(8,128)(2,1)S(1)} %get-tuple-element.128), channel_id=1, source_target_pairs={{0,1},{1,0},{2,3},{3,2},{4,5},{5,4},{6,7},{7,6},{8,9},{9,8},{10,11... | collective-permute-start | bytes 442376 | tf_op jit(solution)/shard_map/ppermute | solution.py:705
  46.9 9.7 %collective-permute-start.16 = (bf16[224,384]{1,0:T(8,128)(2,1)S(1)}, bf16[224,384]{1,0:T(8,128)(2,1)S(1)}, u32[]{:S(2)}, u32[]{:S(2)}) collective-permute-start(bf16[224,384]{1,0:T(8,128)(2,1)S(1)} %shard_map.107.refs_0_), channel_id=1, source_target_pairs={{0,4},{2,6},{4,0},{6,2},{8,12},{10,14},{12,8},{14,10},{16,20},{18,... | collective-permute-start | bytes 516104 | tf_op jit(solution)/shard_map/ppermute | solution.py:64
  48.4 8.1 %collective-permute-start.17 = (bf16[224,384]{1,0:T(8,128)(2,1)S(1)}, bf16[224,384]{1,0:T(8,128)(2,1)S(1)}, u32[]{:S(2)}, u32[]{:S(2)}) collective-permute-start(bf16[224,384]{1,0:T(8,128)(2,1)S(1)} %shard_map.107.refs_0_), channel_id=1, source_target_pairs={{0,8},{2,10},{4,12},{6,14},{8,0},{10,2},{12,4},{14,6},{16,24},{18,... | collective-permute-start | bytes 516104 | tf_op jit(solution)/shard_map/ppermute | solution.py:64
  49.2 8.6 %collective-permute-start.18 = (bf16[224,384]{1,0:T(8,128)(2,1)S(1)}, bf16[224,384]{1,0:T(8,128)(2,1)S(1)}, u32[]{:S(2)}, u32[]{:S(2)}) collective-permute-start(bf16[224,384]{1,0:T(8,128)(2,1)S(1)} %shard_map.107.refs_0_), channel_id=1, source_target_pairs={{0,12},{2,14},{4,8},{6,10},{8,4},{10,6},{12,0},{14,2},{16,28},{18,... | collective-permute-start | bytes 516104 | tf_op jit(solution)/shard_map/ppermute | solution.py:64
  50.8 4.4 %collective-permute-start.19 = (bf16[648,128]{1,0:T(8,128)(2,1)S(1)}, bf16[648,128]{1,0:T(8,128)(2,1)S(1)}, u32[]{:S(2)}, u32[]{:S(2)}) collective-permute-start(bf16[648,128]{1,0:T(8,128)(2,1)S(1)} %shard_map.106.refs_0_), channel_id=1, source_target_pairs={{0,2},{2,0},{4,6},{6,4},{8,10},{10,8},{12,14},{14,12},{16,18},{18,... | collective-permute-start | bytes 497672 | tf_op jit(solution)/shard_map/ppermute | solution.py:64
  50.8 4.5 %collective-permute-start.20 = (bf16[648,128]{1,0:T(8,128)(2,1)S(1)}, bf16[648,128]{1,0:T(8,128)(2,1)S(1)}, u32[]{:S(2)}, u32[]{:S(2)}) collective-permute-start(bf16[648,128]{1,0:T(8,128)(2,1)S(1)} %collective-permute-done.15.refs_1_), channel_id=1, source_target_pairs={{0,2},{2,0},{4,6},{6,4},{8,10},{10,8},{12,14},{14,12},{16,18},{18,... | collective-permute-start | bytes 497672 | tf_op jit(solution)/shard_map/ppermute | solution.py:64
  55.2 3.1 %collective-permute-start.24 = (bf16[224,384]{1,0:T(8,128)(2,1)S(1)}, bf16[224,384]{1,0:T(8,128)(2,1)S(1)}, u32[]{:S(2)}, u32[]{:S(2)}) collective-permute-start(bf16[224,384]{1,0:T(8,128)(2,1)S(1)} %shard_map.107.refs_0_), channel_id=1, source_target_pairs={{0,2},{2,0},{4,6},{6,4},{8,10},{10,8},{12,14},{14,12},{16,18},{18,... | collective-permute-start | bytes 516104 | tf_op jit(solution)/shard_map/ppermute | solution.py:64
  57.7 1.9 %collective-permute-start.25 = (bf16[224,384]{1,0:T(8,128)(2,1)S(1)}, bf16[224,384]{1,0:T(8,128)(2,1)S(1)}, u32[]{:S(2)}, u32[]{:S(2)}) collective-permute-start(bf16[224,384]{1,0:T(8,128)(2,1)S(1)} %collective-permute-done.16.refs_1_), channel_id=1, source_target_pairs={{0,2},{2,0},{4,6},{6,4},{8,10},{10,8},{12,14},{14,12},{16,18},{18,... | collective-permute-start | bytes 516104 | tf_op jit(solution)/shard_map/ppermute | solution.py:64
  57.7 1.9 %collective-permute-start.26 = (bf16[224,384]{1,0:T(8,128)(2,1)S(1)}, bf16[224,384]{1,0:T(8,128)(2,1)S(1)}, u32[]{:S(2)}, u32[]{:S(2)}) collective-permute-start(bf16[224,384]{1,0:T(8,128)(2,1)S(1)} %collective-permute-done.17.refs_2_), channel_id=1, source_target_pairs={{0,2},{2,0},{4,6},{6,4},{8,10},{10,8},{12,14},{14,12},{16,18},{18,... | collective-permute-start | bytes 516104 | tf_op jit(solution)/shard_map/ppermute | solution.py:64
  58.3 1.4 %collective-permute-start.27 = (bf16[224,384]{1,0:T(8,128)(2,1)S(1)}, bf16[224,384]{1,0:T(8,128)(2,1)S(1)}, u32[]{:S(2)}, u32[]{:S(2)}) collective-permute-start(bf16[224,384]{1,0:T(8,128)(2,1)S(1)} %collective-permute-done.18.refs_3_), channel_id=1, source_target_pairs={{0,2},{2,0},{4,6},{6,4},{8,10},{10,8},{12,14},{14,12},{16,18},{18,... | collective-permute-start | bytes 516104 | tf_op jit(solution)/shard_map/ppermute | solution.py:64

commit v14 on v13

--- a/solution.py
+++ b/solution.py
@@ -312,7 +312,7 @@
     cols_ref[1] = field.astype(jnp.bfloat16).T
     cols_ref[2] = jnp.where(column == side - 1, 0.0, pltpu.roll(field, rows - 1, 0)).astype(jnp.bfloat16).T
     which = 1 - lax.rem(lax.axis_index("tile"), 2)
-    for j in range(2):
+    for j in range(3):
         send_ref[j * part : (j + 1) * part, :] = tap_product(side, scale, j + 5 * which, cols_ref, tall_ref)
     rim = cot.reshape(side, side, cot.shape[1])
     rim_ref[...] = jnp.concatenate([cot[0:side], cot[rows - side :], rim[:, 0, :], rim[:, side - 1, :]], axis=0)
@@ -350,9 +350,11 @@
     def place(start, value):
         total[pl.ds(pl.multiple_of(start, 16), value.shape[0]), :] = value
 
-    place(core * half, mine_ref[0 : 2 * part, :] + first_ref[...])
-    place(core * half + 2 * part, mine_ref[2 * part : 4 * part, :] + second_ref[0 : 2 * part, :])
-    place((1 - core) * 4 * part, mine_ref[4 * part :, :] + second_ref[2 * part :, :])
+    cut = first_ref.shape[0]
+    place(core * half, mine_ref[0:cut, :] + first_ref[...])
+    if cut < 4 * part:
+        place(core * half + cut, mine_ref[cut : 4 * part, :] + second_ref[0 : 4 * part - cut, :])
+    place((1 - core) * 4 * part, mine_ref[4 * part :, :] + second_ref[4 * part - cut :, :])
     total[used:, :] = jnp.zeros((total.shape[0] - used, total.shape[1]), jnp.float32)
     left = jnp.dot(onehot_ref[...], near[...], preferred_element_type=jnp.float32).astype(jnp.bfloat16)
 
@@ -633,7 +635,7 @@
     first, tall, rim, cols = call(
         functools.partial(send_kernel, side, part, scale),
         [
-            vmem((2 * part, chans), jnp.float32),
+            vmem((3 * part, chans), jnp.float32),
             vmem((rows + 4 * side, chans), half_bytes),
             vmem((4 * side, chans), half_bytes),
             vmem((3, part, rows), half_bytes),
@@ -642,8 +644,8 @@
         flops=flops // 4,
     )
     (second,) = call(
-        functools.partial(half_kernel, side, part, scale, 1, (2, 3)),
-        [vmem((5 * part // 2, chans), jnp.float32)],
+        functools.partial(half_kernel, side, part, scale, 1, (3,)),
+        [vmem((3 * part // 2, chans), jnp.float32)],
         [cols, tall],
         scratch=[pltpu.VMEM((part, chans), jnp.float32)],
         flops=flops,
@@ -677,7 +679,7 @@
         flops=flops,
     )
     pieces, near = lax.optimization_barrier((pieces, near))
-    here = [pieces, *[by_swap(pieces, odd, count) for odd in (0, 1)]]
+    here = [pieces, *[by_swap(pieces, odd, count) for odd in (1, 0)][::-1]]
     (place,) = call(
         functools.partial(place_kernel, side),
         [vmem((4 * side, 12 * block), half_bytes)],

time: 61 us -> 60.4 us (level)
  waiting for transfers between devices: 10.3 us -> 9.67 us
    ppermute x20, waiting for transfers between devices: 6.02 us -> 5.35 us  [by_mask(): return lax.ppermute(value, 'tile', [(i, i ^ mask) for i in range(count)])]
  transfers between devices with their start and end apart: 28 -> 28, of which waited for: 8 -> 8; matrix products, arithmetic and copies ran while one was open for 1% -> 1% of each run, Pallas kernels for 24% -> 25%
where the time goes in v14:
time: 60.4 us; the launch traced here: 60.1 us
  starting transfers between devices  27.6 us (46%)
  Pallas kernels  19.2 us (32%)
  waiting for transfers between devices  9.67 us (16%)
  local copies, waits for them, and re-layouts  2.09 us (3%)
  between operations  0.79 us (1%)
  other arithmetic  0.74 us (1%)
    pallas_call x16, Pallas kernels, call(): pl.pallas_call(kernel, out_shape=tuple(outs), in_specs=in_specs, out_spec...  16.8 us
    ppermute x20, starting transfers between devices, by_mask(): return lax.ppermute(value, 'tile', [(i, i ^ mask) for i in range(count)])  13.9 us
    ppermute x4, starting transfers between devices, by_swap(): return lax.ppermute(value, 'tile', pairs)  7.17 us
    ppermute x20, waiting for transfers between devices, by_mask(): return lax.ppermute(value, 'tile', [(i, i ^ mask) for i in range(count)])  5.35 us
    ppermute x4, waiting for transfers between devices, by_swap(): return lax.ppermute(value, 'tile', pairs)  3.53 us
    ppermute x3, starting transfers between devices, start_aside(): lax.ppermute(v, 'ch', others)  3.52 us
    ppermute x1, starting transfers between devices, body(): cot_other = lax.ppermute(cot_own, 'ch', others)  3 us
    pallas_call x2, Pallas kernels, unfold(): pl.pallas_call(functools.partial(unfold_kernel, whole.shape[0] // 2, chun...  2.41 us
  transfers between devices with their start and end apart: 28, of which 8 were waited for; matrix products, arithmetic and copies ran while one was open for 1% of the time, Pallas kernels for 25%

profile of v14, /device:TPU:0, one launch (start us, length us, event | category | flops | bytes accessed | tf_op | source)
XLA Modules:
  0.0 60.1 jit_solution(1554887718225738638)
XLA Ops:
  0.6 3.0 %collective-permute-start.4 = (bf16[1024,192]{1,0:T(8,128)(2,1)}, bf16[1024,192]{1,0:T(8,128)(2,1)S(1)}, u32[]{:S(2)}, u32[]{:S(2)}) collective-permute-start(bf16[1024,192]{1,0:T(8,128)(2,1)} %bitcast.11), channel_id=1, source_target_pairs={{0,1},{1,0},{2,3},{3,2},{4,5},{5,4},{6,7},{7,6},{8,9},{9,8},{10,11... | collective-permute-start | bytes 1179656 | tf_op jit(solution)/shard_map/ppermute | solution.py:613
  3.6 1.0 %copy-done = bf16[1,32,32,192]{3,2,1,0:T(8,128)(2,1)S(1)} copy-done((bf16[1,32,32,192]{3,2,1,0:T(8,128)(2,1)S(1)}, bf16[1,32,32,192]{3,2,1,0:T(8,128)(2,1)}, u32[]{:S(2)}) %copy-start) | copy-done | bytes 393240
  4.7 0.1 shard_map.94
  4.8 1.6 %collective-permute-start.1 = (bf16[192,128]{1,0:T(8,128)(2,1)S(1)}, bf16[192,128]{1,0:T(8,128)(2,1)S(1)}, u32[]{:S(2)}, u32[]{:S(2)}) collective-permute-start(bf16[192,128]{1,0:T(8,128)(2,1)S(1)} %get-tuple-element.71.refs_0_), channel_id=1, source_target_pairs={{0,8},{2,10},{4,12},{6,14},{8,0},{10,2},{12,4},{14,6},{16,24},{18,... | collective-permute-start | bytes 147464 | tf_op jit(solution)/shard_map/ppermute | solution.py:60
  6.4 2.5 %collective-permute-start.2 = (bf16[192,128]{1,0:T(8,128)(2,1)S(1)}, bf16[192,128]{1,0:T(8,128)(2,1)S(1)}, u32[]{:S(2)}, u32[]{:S(2)}) collective-permute-start(bf16[192,128]{1,0:T(8,128)(2,1)S(1)} %get-tuple-element.71.refs_0_), channel_id=1, source_target_pairs={{0,24},{2,26},{4,28},{6,30},{8,16},{10,18},{12,20},{14,22},{16,8},... | collective-permute-start | bytes 147464 | tf_op jit(solution)/shard_map/ppermute | solution.py:60
  8.9 1.5 %collective-permute-start = (bf16[192,128]{1,0:T(8,128)(2,1)S(1)}, bf16[192,128]{1,0:T(8,128)(2,1)S(1)}, u32[]{:S(2)}, u32[]{:S(2)}) collective-permute-start(bf16[192,128]{1,0:T(8,128)(2,1)S(1)} %get-tuple-element.71.refs_0_), channel_id=1, source_target_pairs={{0,4},{2,6},{4,0},{6,2},{8,12},{10,14},{12,8},{14,10},{16,20},{18,... | collective-permute-start | bytes 147464 | tf_op jit(solution)/shard_map/ppermute | solution.py:64
  10.4 1.9 %collective-permute-done.2.refs_1_.refs_3_ = bf16[192,128]{1,0:T(8,128)(2,1)S(1)} collective-permute-done((bf16[192,128]{1,0:T(8,128)(2,1)S(1)}, bf16[192,128]{1,0:T(8,128)(2,1)S(1)}, u32[]{:S(2)}, u32[]{:S(2)}) %collective-permute-start.2) | collective-permute-done | bytes 49184 | tf_op jit(solution)/shard_map/ppermute | solution.py:60
  12.3 1.6 %collective-permute-start.3 = (bf16[384,128]{1,0:T(8,128)(2,1)S(1)}, bf16[384,128]{1,0:T(8,128)(2,1)S(1)}, u32[]{:S(2)}, u32[]{:S(2)}) collective-permute-start(bf16[384,128]{1,0:T(8,128)(2,1)S(1)} %shard_map.95), channel_id=1, source_target_pairs={{0,4},{2,6},{4,0},{6,2},{8,12},{10,14},{12,8},{14,10},{16,20},{18,... | collective-permute-start | bytes 294920 | tf_op jit(solution)/shard_map/ppermute | solution.py:64
  13.9 0.7 %pad_add_fusion.tables_in.refs_2_ = s32[16,16]{1,0:T(8,128)S(1)} fusion(s32[4,16]{1,0:T(4,128)} %bitcast.17, s32[4,16]{1,0:T(4,128)} %bitcast.18, s32[4,16]{1,0:T(4,128)} %bitcast.19, s32[4,16]{1,0:T(4,128)} %bitcast.20), kind=kLoop, calls=%fused_computation | loop fusion | flops 768 | bytes 2048 | tf_op jit(solution)/shard_map/concatenate | solution.py:621
  14.7 1.0 %copy-done.1 = bf16[1,32,32,192]{3,2,1,0:T(8,128)(2,1)S(1)} copy-done((bf16[1,32,32,192]{3,2,1,0:T(8,128)(2,1)S(1)}, bf16[1,32,32,192]{3,2,1,0:T(8,128)(2,1)}, u32[]{:S(2)}) %copy-start.1) | copy-done | bytes 393240
  15.7 1.1 %shard_map.96 = (bf16[512,1536]{1,0:T(8,128)(2,1)S(1)}, bf16[1024,192]{1,0:T(8,128)(2,1)S(1)}) custom-call(s32[16,16]{1,0:T(8,128)S(1)} %pad_add_fusion.tables_in.refs_2_, bf16[1024,192]{1,0:T(8,128)(2,1)S(1)} %bitcast.12), custom_call_target="tpu_custom_call" | custom-call | bytes 2360320 | tf_op jit(solution)/shard_map/pallas_call | solution.py:111
  16.8 0.2 collective-permute-done.3.refs_4_
  17.0 1.5 %shard_map.98 = (f32[576,384]{1,0:T(8,128)S(1)}, bf16[1152,384]{1,0:T(8,128)(2,1)S(1)}, bf16[128,384]{1,0:T(8,128)(2,1)S(1)}, bf16[3,192,1024]{2,1,0:T(8,128)(2,1)S(1)}) custom-call(bf16[32,32,192]{2,1,0:T(8,128)(2,1)S(1)} %get-tuple-element.76.field_ref.refs_3_, bf16[1024,192]{1,0:T(8,128)(2,1)S(1)} %get-tuple-element.77.own_ref, ...), custom_call_target="tpu_custom_call" | custom-call | flops 339738624 | bytes 4227072 | tf_op jit(solution)/shard_map/pallas_call | solution.py:111
  18.6 0.1 collective-permute-start.7
  18.6 0.6 %shard_map.99 = f32[288,384]{1,0:T(8,128)S(1)} custom-call(bf16[3,192,1024]{2,1,0:T(8,128)(2,1)S(1)} %get-tuple-element.79.cols, bf16[1152,384]{1,0:T(8,128)(2,1)S(1)} %get-tuple-element.96.tall), custom_call_target="tpu_custom_call" | custom-call | flops 1358954496 | bytes 2506752 | tf_op jit(solution)/shard_map/pallas_call | solution.py:111
  19.3 0.5 collective-permute-start.8
  19.8 0.1 collective-permute-start.5
  19.9 0.5 collective-permute-start.6
  20.4 1.2 %shard_map.100.refs_3_ = f32[864,384]{1,0:T(8,128)S(1)} custom-call(bf16[3,192,1024]{2,1,0:T(8,128)(2,1)S(1)} %get-tuple-element.79.cols, bf16[1152,384]{1,0:T(8,128)(2,1)S(1)} %get-tuple-element.96.tall), custom_call_target="tpu_custom_call" | custom-call | tf_op jit(solution)/shard_map/pallas_call | solution.py:111
  21.7 0.6 collective-permute-done.6.refs_5_
  22.3 1.5 %shard_map.101 = (f32[224,384]{1,0:T(8,128)S(1)}, bf16[224,384]{1,0:T(8,128)(2,1)S(1)}, bf16[224,384]{1,0:T(8,128)(2,1)S(1)}, bf16[224,384]{1,0:T(8,128)(2,1)S(1)}) custom-call(bf16[1152,128]{1,0:T(8,128)(2,1)S(1)} %shard_map.97.refs_0_, bf16[1152,128]{1,0:T(8,128)(2,1)S(1)} %collective-permute-done.5.refs_1_, ...), custom_call_target="tpu_custom_call" | custom-call | bytes 5873664 | tf_op jit(solution)/shard_map/pallas_call | solution.py:111
  23.8 0.6 %collective-permute-start.10 = (bf16[224,384]{1,0:T(8,128)(2,1)S(1)}, bf16[224,384]{1,0:T(8,128)(2,1)S(1)}, u32[]{:S(2)}, u32[]{:S(2)}) collective-permute-start(bf16[224,384]{1,0:T(8,128)(2,1)S(1)} %get-tuple-element.94), channel_id=1, source_target_pairs={{0,8},{2,10},{4,12},{6,14},{8,0},{10,2},{12,4},{14,6},{16,24},{18,... | collective-permute-start | bytes 516104 | tf_op jit(solution)/shard_map/ppermute | solution.py:64
  24.4 2.4 %collective-permute-start.11 = (bf16[224,384]{1,0:T(8,128)(2,1)S(1)}, bf16[224,384]{1,0:T(8,128)(2,1)S(1)}, u32[]{:S(2)}, u32[]{:S(2)}) collective-permute-start(bf16[224,384]{1,0:T(8,128)(2,1)S(1)} %get-tuple-element.95), channel_id=1, source_target_pairs={{0,12},{2,14},{4,8},{6,10},{8,4},{10,6},{12,0},{14,2},{16,28},{18,... | collective-permute-start | bytes 516104 | tf_op jit(solution)/shard_map/ppermute | solution.py:64
  26.8 0.5 collective-permute-start.9
  27.3 2.9 %shard_map.102 = (f32[1024,192]{1,0:T(8,128)S(1)}, bf16[216,128]{1,0:T(8,128)(2,1)S(1)}) custom-call(bf16[1152,384]{1,0:T(8,128)(2,1)S(1)} %get-tuple-element.96.tall, bf16[9,384,384]{2,1,0:T(8,128)(2,1)S(1)} %bitcast.13), custom_call_target="tpu_custom_call" | custom-call | flops 1358954496 | bytes 4380672 | tf_op jit(solution)/shard_map/pallas_call | solution.py:111
  30.2 0.6 collective-permute-start.12
  30.8 2.5 %collective-permute-start.13 = (bf16[216,128]{1,0:T(8,128)(2,1)S(1)}, bf16[216,128]{1,0:T(8,128)(2,1)S(1)}, u32[]{:S(2)}, u32[]{:S(2)}) collective-permute-start(bf16[216,128]{1,0:T(8,128)(2,1)S(1)} %get-tuple-element.118.refs_0_), channel_id=1, source_target_pairs={{0,24},{2,26},{4,28},{6,30},{8,16},{10,18},{12,20},{14,22},{16,8},... | collective-permute-start | bytes 165896 | tf_op jit(solution)/shard_map/ppermute | solution.py:60
  33.3 1.2 %shard_map.104.place_ref = bf16[128,1728]{1,0:T(8,128)(2,1)S(1)} custom-call(s32[16,16]{1,0:T(8,128)S(1)} %pad_add_fusion.tables_in.refs_2_), custom_call_target="tpu_custom_call" | custom-call | bytes 443392 | tf_op jit(solution)/shard_map/pallas_call | solution.py:111
  34.5 1.3 %shard_map.103 = (bf16[144,192]{1,0:T(8,128)(2,1)S(1)}, bf16[576,128]{1,0:T(8,128)(2,1)S(1)}, bf16[576,128]{1,0:T(8,128)(2,1)S(1)}, bf16[600,128]{1,0:T(8,128)(2,1)S(1)}) custom-call(bf16[1152,128]{1,0:T(8,128)(2,1)S(1)} %shard_map.97.refs_0_, bf16[1152,128]{1,0:T(8,128)(2,1)S(1)} %collective-permute-done.5.refs_1_, ...), custom_call_target="tpu_custom_call" | custom-call | bytes 1487872 | tf_op jit(solution)/shard_map/pallas_call | solution.py:111
  35.8 1.6 %collective-permute-done.13.refs_2_ = bf16[216,128]{1,0:T(8,128)(2,1)S(1)} collective-permute-done((bf16[216,128]{1,0:T(8,128)(2,1)S(1)}, bf16[216,128]{1,0:T(8,128)(2,1)S(1)}, u32[]{:S(2)}, u32[]{:S(2)}) %collective-permute-start.13) | collective-permute-done | bytes 55328 | tf_op jit(solution)/shard_map/ppermute | solution.py:60
  37.4 0.1 shard_map.105.held_ref
  37.5 0.6 %collective-permute-start.14 = (bf16[224,384]{1,0:T(8,128)(2,1)S(1)}, bf16[224,384]{1,0:T(8,128)(2,1)S(1)}, u32[]{:S(2)}, u32[]{:S(2)}) collective-permute-start(bf16[224,384]{1,0:T(8,128)(2,1)S(1)} %shard_map.105.held_ref), channel_id=1, source_target_pairs={{0,16},{2,18},{4,20},{6,22},{8,24},{10,26},{12,28},{14,30},{16,0},... | collective-permute-start | bytes 516104 | tf_op jit(solution)/shard_map/ppermute | solution.py:64
  38.1 1.2 %collective-permute-start.15 = (bf16[648,128]{1,0:T(8,128)(2,1)S(1)}, bf16[648,128]{1,0:T(8,128)(2,1)S(1)}, u32[]{:S(2)}, u32[]{:S(2)}) collective-permute-start(bf16[648,128]{1,0:T(8,128)(2,1)S(1)} %shard_map.106.refs_0_), channel_id=1, source_target_pairs={{0,4},{2,6},{4,0},{6,2},{8,12},{10,14},{12,8},{14,10},{16,20},{18,... | collective-permute-start | bytes 497672 | tf_op jit(solution)/shard_map/ppermute | solution.py:64
  39.4 1.5 %collective-permute-start.23 = (bf16[600,128]{1,0:T(8,128)(2,1)S(1)}, bf16[600,128]{1,0:T(8,128)(2,1)S(1)}, u32[]{:S(2)}, u32[]{:S(2)}) collective-permute-start(bf16[600,128]{1,0:T(8,128)(2,1)S(1)} %get-tuple-element.129), channel_id=1, source_target_pairs={{0,1},{1,0},{2,3},{3,2},{4,5},{5,4},{6,7},{7,6},{8,9},{9,8},{10,11... | collective-permute-start | bytes 460808 | tf_op jit(solution)/shard_map/ppermute | solution.py:707
  40.9 0.5 collective-permute-start.21
  41.4 1.5 %collective-permute-start.22 = (bf16[576,128]{1,0:T(8,128)(2,1)S(1)}, bf16[576,128]{1,0:T(8,128)(2,1)S(1)}, u32[]{:S(2)}, u32[]{:S(2)}) collective-permute-start(bf16[576,128]{1,0:T(8,128)(2,1)S(1)} %get-tuple-element.128), channel_id=1, source_target_pairs={{0,1},{1,0},{2,3},{3,2},{4,5},{5,4},{6,7},{7,6},{8,9},{9,8},{10,11... | collective-permute-start | bytes 442376 | tf_op jit(solution)/shard_map/ppermute | solution.py:707
  42.9 0.7 %collective-permute-done.15.refs_1_ = bf16[648,128]{1,0:T(8,128)(2,1)S(1)} collective-permute-done((bf16[648,128]{1,0:T(8,128)(2,1)S(1)}, bf16[648,128]{1,0:T(8,128)(2,1)S(1)}, u32[]{:S(2)}, u32[]{:S(2)}) %collective-permute-start.15) | collective-permute-done | bytes 165920 | tf_op jit(solution)/shard_map/ppermute | solution.py:64
  43.6 2.6 %collective-permute-done.14.got_ref = bf16[224,384]{1,0:T(8,128)(2,1)S(1)} collective-permute-done((bf16[224,384]{1,0:T(8,128)(2,1)S(1)}, bf16[224,384]{1,0:T(8,128)(2,1)S(1)}, u32[]{:S(2)}, u32[]{:S(2)}) %collective-permute-start.14) | collective-permute-done | bytes 172064 | tf_op jit(solution)/shard_map/ppermute | solution.py:64
  46.2 1.6 %collective-permute-start.16 = (bf16[224,384]{1,0:T(8,128)(2,1)S(1)}, bf16[224,384]{1,0:T(8,128)(2,1)S(1)}, u32[]{:S(2)}, u32[]{:S(2)}) collective-permute-start(bf16[224,384]{1,0:T(8,128)(2,1)S(1)} %shard_map.107.refs_0_), channel_id=1, source_target_pairs={{0,4},{2,6},{4,0},{6,2},{8,12},{10,14},{12,8},{14,10},{16,20},{18,... | collective-permute-start | bytes 516104 | tf_op jit(solution)/shard_map/ppermute | solution.py:64
  47.8 0.8 %collective-permute-done.21.refs_0_ = bf16[576,128]{1,0:T(8,128)(2,1)S(1)} collective-permute-done((bf16[576,128]{1,0:T(8,128)(2,1)S(1)}, bf16[576,128]{1,0:T(8,128)(2,1)S(1)}, u32[]{:S(2)}, u32[]{:S(2)}) %collective-permute-start.21) | collective-permute-done | bytes 147488 | tf_op jit(solution)/shard_map/ppermute | solution.py:707
  48.6 1.6 %collective-permute-start.18 = (bf16[224,384]{1,0:T(8,128)(2,1)S(1)}, bf16[224,384]{1,0:T(8,128)(2,1)S(1)}, u32[]{:S(2)}, u32[]{:S(2)}) collective-permute-start(bf16[224,384]{1,0:T(8,128)(2,1)S(1)} %shard_map.107.refs_0_), channel_id=1, source_target_pairs={{0,12},{2,14},{4,8},{6,10},{8,4},{10,6},{12,0},{14,2},{16,28},{18,... | collective-permute-start | bytes 516104 | tf_op jit(solution)/shard_map/ppermute | solution.py:64
  50.1 0.5 collective-permute-start.20
  50.7 3.9 %shard_map.109 = bf16[1024,192]{1,0:T(8,128)(2,1)} custom-call(bf16[32,32,192]{2,1,0:T(8,128)(2,1)S(1)} %get-tuple-element.76.field_ref.refs_3_, bf16[144,192]{1,0:T(8,128)(2,1)S(1)} %get-tuple-element.126.halos_ref, bf16[9,384,384]{2,1,0:T(8,128)(2,1)S(1)} %bitcast.14, bf16[576,128]{1,0:T(8,128)(2,1)S(1)} %collective-permute-done.21.refs_0_, ...), custom_call_target="tpu_custom_call" | custom-call | flops 2717908992 | bytes 3944448 | tf_op jit(solution)/shard_map/pallas_call | solution.py:111
  54.6 1.3 %shard_map.108 = bf16[1024,192]{1,0:T(8,128)(2,1)} custom-call(bf16[128,1728]{1,0:T(8,128)(2,1)S(1)} %shard_map.104.place_ref, f32[1024,192]{1,0:T(8,128)S(1)} %get-tuple-element.123.inner_ref, bf16[648,128]{1,0:T(8,128)(2,1)S(1)} %shard_map.106.refs_0_, bf16[648,128]{1,0:T(8,128)(2,1)S(1)} %collective-permute-done.15.refs_1_, ...), custom_call_target="tpu_custom_call" | custom-call | bytes 2285568 | tf_op jit(solution)/shard_map/pallas_call | solution.py:111
  55.9 1.2 %collective-permute-done.18.refs_3_ = bf16[224,384]{1,0:T(8,128)(2,1)S(1)} collective-permute-done((bf16[224,384]{1,0:T(8,128)(2,1)S(1)}, bf16[224,384]{1,0:T(8,128)(2,1)S(1)}, u32[]{:S(2)}, u32[]{:S(2)}) %collective-permute-start.18) | collective-permute-done | bytes 172064 | tf_op jit(solution)/shard_map/ppermute | solution.py:64
  57.1 0.5 collective-permute-start.26
  57.6 1.4 %shard_map.110.refs_0_ = f32[1728,384]{1,0:T(8,128)} custom-call(bf16[224,384]{1,0:T(8,128)(2,1)S(1)} %shard_map.107.refs_0_, bf16[224,384]{1,0:T(8,128)(2,1)S(1)} %collective-permute-done.16.refs_1_, bf16[224,384]{1,0:T(8,128)(2,1)S(1)} %collective-permute-done.17.refs_2_, bf16[224,384]{1,0:T(8,128)(2,1)S(1)} %collective-permute-done.18.refs_3_, ...), custom_call_target="tpu_custom_call" | custom-call | tf_op jit(solution)/shard_map/pallas_call | solution.py:455
  59.0 1.1 %shard_map.111 = f32[1728,384]{1,0:T(8,128)} custom-call(f32[1728,384]{1,0:T(8,128)} %shard_map.110.refs_0_, bf16[224,384]{1,0:T(8,128)(2,1)S(1)} %collective-permute-done.25.refs_1_, bf16[224,384]{1,0:T(8,128)(2,1)S(1)} %collective-permute-done.26.refs_2_, bf16[224,384]{1,0:T(8,128)(2,1)S(1)} %collective-permute-done.27.refs_3_), custom_call_target="tpu_custom_call", output_to_operand_aliasing={{}: (0, {})} | custom-call | tf_op jit(solution)/shard_map/pallas_call | solution.py:455
  (33 shorter events, 0.2 us)
Async XLA Ops:
  0.6 16.4 %collective-permute-start.4 = (bf16[1024,192]{1,0:T(8,128)(2,1)}, bf16[1024,192]{1,0:T(8,128)(2,1)S(1)}, u32[]{:S(2)}, u32[]{:S(2)}) collective-permute-start(bf16[1024,192]{1,0:T(8,128)(2,1)} %bitcast.11), channel_id=1, source_target_pairs={{0,1},{1,0},{2,3},{3,2},{4,5},{5,4},{6,7},{7,6},{8,9},{9,8},{10,11... | collective-permute-start | bytes 1179656 | tf_op jit(solution)/shard_map/ppermute | solution.py:613
  3.6 1.0 %copy-start = (bf16[1,32,32,192]{3,2,1,0:T(8,128)(2,1)S(1)}, bf16[1,32,32,192]{3,2,1,0:T(8,128)(2,1)}, u32[]{:S(2)}) copy-start(bf16[1,32,32,192]{3,2,1,0:T(8,128)(2,1)} %param.7) | copy-start | bytes 1179652
  4.8 5.6 %collective-permute-start.1 = (bf16[192,128]{1,0:T(8,128)(2,1)S(1)}, bf16[192,128]{1,0:T(8,128)(2,1)S(1)}, u32[]{:S(2)}, u32[]{:S(2)}) collective-permute-start(bf16[192,128]{1,0:T(8,128)(2,1)S(1)} %get-tuple-element.71.refs_0_), channel_id=1, source_target_pairs={{0,8},{2,10},{4,12},{6,14},{8,0},{10,2},{12,4},{14,6},{16,24},{18,... | collective-permute-start | bytes 147464 | tf_op jit(solution)/shard_map/ppermute | solution.py:60
  6.4 5.9 %collective-permute-start.2 = (bf16[192,128]{1,0:T(8,128)(2,1)S(1)}, bf16[192,128]{1,0:T(8,128)(2,1)S(1)}, u32[]{:S(2)}, u32[]{:S(2)}) collective-permute-start(bf16[192,128]{1,0:T(8,128)(2,1)S(1)} %get-tuple-element.71.refs_0_), channel_id=1, source_target_pairs={{0,24},{2,26},{4,28},{6,30},{8,16},{10,18},{12,20},{14,22},{16,8},... | collective-permute-start | bytes 147464 | tf_op jit(solution)/shard_map/ppermute | solution.py:60
  8.9 7.9 %collective-permute-start = (bf16[192,128]{1,0:T(8,128)(2,1)S(1)}, bf16[192,128]{1,0:T(8,128)(2,1)S(1)}, u32[]{:S(2)}, u32[]{:S(2)}) collective-permute-start(bf16[192,128]{1,0:T(8,128)(2,1)S(1)} %get-tuple-element.71.refs_0_), channel_id=1, source_target_pairs={{0,4},{2,6},{4,0},{6,2},{8,12},{10,14},{12,8},{14,10},{16,20},{18,... | collective-permute-start | bytes 147464 | tf_op jit(solution)/shard_map/ppermute | solution.py:64
  12.3 4.7 %collective-permute-start.3 = (bf16[384,128]{1,0:T(8,128)(2,1)S(1)}, bf16[384,128]{1,0:T(8,128)(2,1)S(1)}, u32[]{:S(2)}, u32[]{:S(2)}) collective-permute-start(bf16[384,128]{1,0:T(8,128)(2,1)S(1)} %shard_map.95), channel_id=1, source_target_pairs={{0,4},{2,6},{4,0},{6,2},{8,12},{10,14},{12,8},{14,10},{16,20},{18,... | collective-permute-start | bytes 294920 | tf_op jit(solution)/shard_map/ppermute | solution.py:64
  14.7 1.0 %copy-start.1 = (bf16[1,32,32,192]{3,2,1,0:T(8,128)(2,1)S(1)}, bf16[1,32,32,192]{3,2,1,0:T(8,128)(2,1)}, u32[]{:S(2)}) copy-start(bf16[1,32,32,192]{3,2,1,0:T(8,128)(2,1)} %param.9) | copy-start | bytes 1179652
  18.6 3.7 %collective-permute-start.7 = (f32[576,384]{1,0:T(8,128)S(1)}, f32[576,384]{1,0:T(8,128)S(1)}, u32[]{:S(2)}, u32[]{:S(2)}) collective-permute-start(f32[576,384]{1,0:T(8,128)S(1)} %get-tuple-element.87), channel_id=1, source_target_pairs={{0,2},{2,0},{4,6},{6,4},{8,10},{10,8},{12,14},{14,12},{16,18},{18,... | collective-permute-start | bytes 2654216 | tf_op jit(solution)/shard_map/ppermute | solution.py:64
  19.3 3.0 %collective-permute-start.8 = (f32[288,384]{1,0:T(8,128)S(1)}, f32[288,384]{1,0:T(8,128)S(1)}, u32[]{:S(2)}, u32[]{:S(2)}) collective-permute-start(f32[288,384]{1,0:T(8,128)S(1)} %shard_map.99), channel_id=1, source_target_pairs={{0,2},{2,0},{4,6},{6,4},{8,10},{10,8},{12,14},{14,12},{16,18},{18,... | collective-permute-start | bytes 1327112 | tf_op jit(solution)/shard_map/ppermute | solution.py:64
  19.8 2.4 %collective-permute-start.5 = (bf16[1152,128]{1,0:T(8,128)(2,1)S(1)}, bf16[1152,128]{1,0:T(8,128)(2,1)S(1)}, u32[]{:S(2)}, u32[]{:S(2)}) collective-permute-start(bf16[1152,128]{1,0:T(8,128)(2,1)S(1)} %shard_map.97.refs_0_), channel_id=1, source_target_pairs={{0,2},{2,0},{4,6},{6,4},{8,10},{10,8},{12,14},{14,12},{16,18},{18,... | collective-permute-start | bytes 884744 | tf_op jit(solution)/shard_map/ppermute | solution.py:64
  19.9 2.3 %collective-permute-start.6 = (bf16[128,384]{1,0:T(8,128)(2,1)S(1)}, bf16[128,384]{1,0:T(8,128)(2,1)S(1)}, u32[]{:S(2)}, u32[]{:S(2)}) collective-permute-start(bf16[128,384]{1,0:T(8,128)(2,1)S(1)} %get-tuple-element.82.refs_4_), channel_id=1, source_target_pairs={{0,2},{2,0},{4,6},{6,4},{8,10},{10,8},{12,14},{14,12},{16,18},{18,... | collective-permute-start | bytes 294920 | tf_op jit(solution)/shard_map/ppermute | solution.py:64
  21.7 5.7 %copy-start.2 = (bf16[3,3,384,384]{3,2,1,0:T(8,128)(2,1)S(1)}, bf16[3,3,384,384]{3,2,1,0:T(8,128)(2,1)}, u32[]{:S(2)}) copy-start(bf16[3,3,384,384]{3,2,1,0:T(8,128)(2,1)} %param.8) | copy-start | bytes 7962628
  23.8 13.6 %collective-permute-start.10 = (bf16[224,384]{1,0:T(8,128)(2,1)S(1)}, bf16[224,384]{1,0:T(8,128)(2,1)S(1)}, u32[]{:S(2)}, u32[]{:S(2)}) collective-permute-start(bf16[224,384]{1,0:T(8,128)(2,1)S(1)} %get-tuple-element.94), channel_id=1, source_target_pairs={{0,8},{2,10},{4,12},{6,14},{8,0},{10,2},{12,4},{14,6},{16,24},{18,... | collective-permute-start | bytes 516104 | tf_op jit(solution)/shard_map/ppermute | solution.py:64
  24.4 13.0 %collective-permute-start.11 = (bf16[224,384]{1,0:T(8,128)(2,1)S(1)}, bf16[224,384]{1,0:T(8,128)(2,1)S(1)}, u32[]{:S(2)}, u32[]{:S(2)}) collective-permute-start(bf16[224,384]{1,0:T(8,128)(2,1)S(1)} %get-tuple-element.95), channel_id=1, source_target_pairs={{0,12},{2,14},{4,8},{6,10},{8,4},{10,6},{12,0},{14,2},{16,28},{18,... | collective-permute-start | bytes 516104 | tf_op jit(solution)/shard_map/ppermute | solution.py:64
  26.8 10.6 %collective-permute-start.9 = (bf16[224,384]{1,0:T(8,128)(2,1)S(1)}, bf16[224,384]{1,0:T(8,128)(2,1)S(1)}, u32[]{:S(2)}, u32[]{:S(2)}) collective-permute-start(bf16[224,384]{1,0:T(8,128)(2,1)S(1)} %get-tuple-element.93), channel_id=1, source_target_pairs={{0,4},{2,6},{4,0},{6,2},{8,12},{10,14},{12,8},{14,10},{16,20},{18,... | collective-permute-start | bytes 516104 | tf_op jit(solution)/shard_map/ppermute | solution.py:64
  30.2 5.5 %collective-permute-start.12 = (bf16[216,128]{1,0:T(8,128)(2,1)S(1)}, bf16[216,128]{1,0:T(8,128)(2,1)S(1)}, u32[]{:S(2)}, u32[]{:S(2)}) collective-permute-start(bf16[216,128]{1,0:T(8,128)(2,1)S(1)} %get-tuple-element.118.refs_0_), channel_id=1, source_target_pairs={{0,8},{2,10},{4,12},{6,14},{8,0},{10,2},{12,4},{14,6},{16,24},{18,... | collective-permute-start | bytes 165896 | tf_op jit(solution)/shard_map/ppermute | solution.py:60
  30.8 6.6 %collective-permute-start.13 = (bf16[216,128]{1,0:T(8,128)(2,1)S(1)}, bf16[216,128]{1,0:T(8,128)(2,1)S(1)}, u32[]{:S(2)}, u32[]{:S(2)}) collective-permute-start(bf16[216,128]{1,0:T(8,128)(2,1)S(1)} %get-tuple-element.118.refs_0_), channel_id=1, source_target_pairs={{0,24},{2,26},{4,28},{6,30},{8,16},{10,18},{12,20},{14,22},{16,8},... | collective-permute-start | bytes 165896 | tf_op jit(solution)/shard_map/ppermute | solution.py:60
  37.5 8.7 %collective-permute-start.14 = (bf16[224,384]{1,0:T(8,128)(2,1)S(1)}, bf16[224,384]{1,0:T(8,128)(2,1)S(1)}, u32[]{:S(2)}, u32[]{:S(2)}) collective-permute-start(bf16[224,384]{1,0:T(8,128)(2,1)S(1)} %shard_map.105.held_ref), channel_id=1, source_target_pairs={{0,16},{2,18},{4,20},{6,22},{8,24},{10,26},{12,28},{14,30},{16,0},... | collective-permute-start | bytes 516104 | tf_op jit(solution)/shard_map/ppermute | solution.py:64
  38.1 5.4 %collective-permute-start.15 = (bf16[648,128]{1,0:T(8,128)(2,1)S(1)}, bf16[648,128]{1,0:T(8,128)(2,1)S(1)}, u32[]{:S(2)}, u32[]{:S(2)}) collective-permute-start(bf16[648,128]{1,0:T(8,128)(2,1)S(1)} %shard_map.106.refs_0_), channel_id=1, source_target_pairs={{0,4},{2,6},{4,0},{6,2},{8,12},{10,14},{12,8},{14,10},{16,20},{18,... | collective-permute-start | bytes 497672 | tf_op jit(solution)/shard_map/ppermute | solution.py:64
  39.4 10.8 %collective-permute-start.23 = (bf16[600,128]{1,0:T(8,128)(2,1)S(1)}, bf16[600,128]{1,0:T(8,128)(2,1)S(1)}, u32[]{:S(2)}, u32[]{:S(2)}) collective-permute-start(bf16[600,128]{1,0:T(8,128)(2,1)S(1)} %get-tuple-element.129), channel_id=1, source_target_pairs={{0,1},{1,0},{2,3},{3,2},{4,5},{5,4},{6,7},{7,6},{8,9},{9,8},{10,11... | collective-permute-start | bytes 460808 | tf_op jit(solution)/shard_map/ppermute | solution.py:707
  40.9 7.7 %collective-permute-start.21 = (bf16[576,128]{1,0:T(8,128)(2,1)S(1)}, bf16[576,128]{1,0:T(8,128)(2,1)S(1)}, u32[]{:S(2)}, u32[]{:S(2)}) collective-permute-start(bf16[576,128]{1,0:T(8,128)(2,1)S(1)} %get-tuple-element.127), channel_id=1, source_target_pairs={{0,1},{1,0},{2,3},{3,2},{4,5},{5,4},{6,7},{7,6},{8,9},{9,8},{10,11... | collective-permute-start | bytes 442376 | tf_op jit(solution)/shard_map/ppermute | solution.py:707
  41.4 8.8 %collective-permute-start.22 = (bf16[576,128]{1,0:T(8,128)(2,1)S(1)}, bf16[576,128]{1,0:T(8,128)(2,1)S(1)}, u32[]{:S(2)}, u32[]{:S(2)}) collective-permute-start(bf16[576,128]{1,0:T(8,128)(2,1)S(1)} %get-tuple-element.128), channel_id=1, source_target_pairs={{0,1},{1,0},{2,3},{3,2},{4,5},{5,4},{6,7},{7,6},{8,9},{9,8},{10,11... | collective-permute-start | bytes 442376 | tf_op jit(solution)/shard_map/ppermute | solution.py:707
  46.2 9.7 %collective-permute-start.16 = (bf16[224,384]{1,0:T(8,128)(2,1)S(1)}, bf16[224,384]{1,0:T(8,128)(2,1)S(1)}, u32[]{:S(2)}, u32[]{:S(2)}) collective-permute-start(bf16[224,384]{1,0:T(8,128)(2,1)S(1)} %shard_map.107.refs_0_), channel_id=1, source_target_pairs={{0,4},{2,6},{4,0},{6,2},{8,12},{10,14},{12,8},{14,10},{16,20},{18,... | collective-permute-start | bytes 516104 | tf_op jit(solution)/shard_map/ppermute | solution.py:64
  47.8 8.1 %collective-permute-start.17 = (bf16[224,384]{1,0:T(8,128)(2,1)S(1)}, bf16[224,384]{1,0:T(8,128)(2,1)S(1)}, u32[]{:S(2)}, u32[]{:S(2)}) collective-permute-start(bf16[224,384]{1,0:T(8,128)(2,1)S(1)} %shard_map.107.refs_0_), channel_id=1, source_target_pairs={{0,8},{2,10},{4,12},{6,14},{8,0},{10,2},{12,4},{14,6},{16,24},{18,... | collective-permute-start | bytes 516104 | tf_op jit(solution)/shard_map/ppermute | solution.py:64
  48.6 8.6 %collective-permute-start.18 = (bf16[224,384]{1,0:T(8,128)(2,1)S(1)}, bf16[224,384]{1,0:T(8,128)(2,1)S(1)}, u32[]{:S(2)}, u32[]{:S(2)}) collective-permute-start(bf16[224,384]{1,0:T(8,128)(2,1)S(1)} %shard_map.107.refs_0_), channel_id=1, source_target_pairs={{0,12},{2,14},{4,8},{6,10},{8,4},{10,6},{12,0},{14,2},{16,28},{18,... | collective-permute-start | bytes 516104 | tf_op jit(solution)/shard_map/ppermute | solution.py:64
  50.1 4.4 %collective-permute-start.19 = (bf16[648,128]{1,0:T(8,128)(2,1)S(1)}, bf16[648,128]{1,0:T(8,128)(2,1)S(1)}, u32[]{:S(2)}, u32[]{:S(2)}) collective-permute-start(bf16[648,128]{1,0:T(8,128)(2,1)S(1)} %shard_map.106.refs_0_), channel_id=1, source_target_pairs={{0,2},{2,0},{4,6},{6,4},{8,10},{10,8},{12,14},{14,12},{16,18},{18,... | collective-permute-start | bytes 497672 | tf_op jit(solution)/shard_map/ppermute | solution.py:64
  50.1 4.5 %collective-permute-start.20 = (bf16[648,128]{1,0:T(8,128)(2,1)S(1)}, bf16[648,128]{1,0:T(8,128)(2,1)S(1)}, u32[]{:S(2)}, u32[]{:S(2)}) collective-permute-start(bf16[648,128]{1,0:T(8,128)(2,1)S(1)} %collective-permute-done.15.refs_1_), channel_id=1, source_target_pairs={{0,2},{2,0},{4,6},{6,4},{8,10},{10,8},{12,14},{14,12},{16,18},{18,... | collective-permute-start | bytes 497672 | tf_op jit(solution)/shard_map/ppermute | solution.py:64
  54.5 3.1 %collective-permute-start.24 = (bf16[224,384]{1,0:T(8,128)(2,1)S(1)}, bf16[224,384]{1,0:T(8,128)(2,1)S(1)}, u32[]{:S(2)}, u32[]{:S(2)}) collective-permute-start(bf16[224,384]{1,0:T(8,128)(2,1)S(1)} %shard_map.107.refs_0_), channel_id=1, source_target_pairs={{0,2},{2,0},{4,6},{6,4},{8,10},{10,8},{12,14},{14,12},{16,18},{18,... | collective-permute-start | bytes 516104 | tf_op jit(solution)/shard_map/ppermute | solution.py:64
  57.1 1.9 %collective-permute-start.25 = (bf16[224,384]{1,0:T(8,128)(2,1)S(1)}, bf16[224,384]{1,0:T(8,128)(2,1)S(1)}, u32[]{:S(2)}, u32[]{:S(2)}) collective-permute-start(bf16[224,384]{1,0:T(8,128)(2,1)S(1)} %collective-permute-done.16.refs_1_), channel_id=1, source_target_pairs={{0,2},{2,0},{4,6},{6,4},{8,10},{10,8},{12,14},{14,12},{16,18},{18,... | collective-permute-start | bytes 516104 | tf_op jit(solution)/shard_map/ppermute | solution.py:64
  57.1 1.9 %collective-permute-start.26 = (bf16[224,384]{1,0:T(8,128)(2,1)S(1)}, bf16[224,384]{1,0:T(8,128)(2,1)S(1)}, u32[]{:S(2)}, u32[]{:S(2)}) collective-permute-start(bf16[224,384]{1,0:T(8,128)(2,1)S(1)} %collective-permute-done.17.refs_2_), channel_id=1, source_target_pairs={{0,2},{2,0},{4,6},{6,4},{8,10},{10,8},{12,14},{14,12},{16,18},{18,... | collective-permute-start | bytes 516104 | tf_op jit(solution)/shard_map/ppermute | solution.py:64
  57.6 1.4 %collective-permute-start.27 = (bf16[224,384]{1,0:T(8,128)(2,1)S(1)}, bf16[224,384]{1,0:T(8,128)(2,1)S(1)}, u32[]{:S(2)}, u32[]{:S(2)}) collective-permute-start(bf16[224,384]{1,0:T(8,128)(2,1)S(1)} %collective-permute-done.18.refs_3_), channel_id=1, source_target_pairs={{0,2},{2,0},{4,6},{6,4},{8,10},{10,8},{12,14},{14,12},{16,18},{18,... | collective-permute-start | bytes 516104 | tf_op jit(solution)/shard_map/ppermute | solution.py:64

commit v15 on v14

--- a/solution.py
+++ b/solution.py
@@ -694,15 +694,16 @@
         [*near, tables, field],
         scratch=[pltpu.VMEM((48 * side, part), half_bytes), *table_scratch],
     )
-    got, here, inner, halos, packet, place = lax.optimization_barrier(
-        (got, here, inner, halos, packet, place)
+    got, here[:2], inner, halos, packet, place = lax.optimization_barrier(
+        (got, here[:2], inner, halos, packet, place)
     )
     swap = len(stages[-1]) == 1 and len(stages) > 2
     rs_stages = stages[2:-1] if swap else stages[2:]
     aside = [here, packet]
 
     def start_aside(send, aside):
-        send, here, packet = lax.optimization_barrier((send, *aside))
+        here = aside[0]
+        send, here[0], packet = lax.optimization_barrier((send, here[0], aside[1]))
         (here,) = call(join_kernel, [vmem((3 * pieces.shape[0], pieces.shape[1]), half_bytes)], here)
         return send, here, by_mask(here, 2, count), [lax.ppermute(v, "ch", others) for v in packet]
 

time: 60.4 us -> 59.6 us (0.987)
  waiting for transfers between devices: 9.67 us -> 8.37 us
    ppermute x4, waiting for transfers between devices: 3.53 us -> 1.9 us  [by_swap(): return lax.ppermute(value, 'tile', pairs)]
    ppermute x3, waiting for transfers between devices: 0.79 us -> 1.44 us  [start_aside(): lax.ppermute(v, 'ch', others)]
  transfers between devices with their start and end apart: 28 -> 28, of which waited for: 8 -> 9; matrix products, arithmetic and copies ran while one was open for 1% -> 1% of each run, Pallas kernels for 25% -> 25%
where the time goes in v15:
time: 59.6 us; the launch traced here: 59.3 us
  starting transfers between devices  28.1 us (47%)
  Pallas kernels  19.2 us (32%)
  waiting for transfers between devices  8.37 us (14%)
  local copies, waits for them, and re-layouts  2.09 us (4%)
  between operations  0.81 us (1%)
  other arithmetic  0.74 us (1%)
    pallas_call x16, Pallas kernels, call(): pl.pallas_call(kernel, out_shape=tuple(outs), in_specs=in_specs, out_spec...  16.8 us
    ppermute x20, starting transfers between devices, by_mask(): return lax.ppermute(value, 'tile', [(i, i ^ mask) for i in range(count)])  14.4 us
    ppermute x4, starting transfers between devices, by_swap(): return lax.ppermute(value, 'tile', pairs)  7.17 us
    ppermute x20, waiting for transfers between devices, by_mask(): return lax.ppermute(value, 'tile', [(i, i ^ mask) for i in range(count)])  5.03 us
    ppermute x3, starting transfers between devices, start_aside(): lax.ppermute(v, 'ch', others)  3.51 us
    ppermute x1, starting transfers between devices, body(): cot_other = lax.ppermute(cot_own, 'ch', others)  3 us
    pallas_call x2, Pallas kernels, unfold(): pl.pallas_call(functools.partial(unfold_kernel, whole.shape[0] // 2, chun...  2.41 us
    unnamed x6, local copies, waits for them, and re-layouts  2.09 us
  transfers between devices with their start and end apart: 28, of which 9 were waited for; matrix products, arithmetic and copies ran while one was open for 1% of the time, Pallas kernels for 25%

profile of v15, /device:TPU:0, one launch (start us, length us, event | category | flops | bytes accessed | tf_op | source)
XLA Modules:
  0.0 59.3 jit_solution(15067512823580316607)
XLA Ops:
  0.6 3.0 %collective-permute-start.4 = (bf16[1024,192]{1,0:T(8,128)(2,1)}, bf16[1024,192]{1,0:T(8,128)(2,1)S(1)}, u32[]{:S(2)}, u32[]{:S(2)}) collective-permute-start(bf16[1024,192]{1,0:T(8,128)(2,1)} %bitcast.11), channel_id=1, source_target_pairs={{0,1},{1,0},{2,3},{3,2},{4,5},{5,4},{6,7},{7,6},{8,9},{9,8},{10,11... | collective-permute-start | bytes 1179656 | tf_op jit(solution)/shard_map/ppermute | solution.py:613
  3.6 1.0 %copy-done = bf16[1,32,32,192]{3,2,1,0:T(8,128)(2,1)S(1)} copy-done((bf16[1,32,32,192]{3,2,1,0:T(8,128)(2,1)S(1)}, bf16[1,32,32,192]{3,2,1,0:T(8,128)(2,1)}, u32[]{:S(2)}) %copy-start) | copy-done | bytes 393240
  4.7 0.1 shard_map.94
  4.8 1.6 %collective-permute-start.1 = (bf16[192,128]{1,0:T(8,128)(2,1)S(1)}, bf16[192,128]{1,0:T(8,128)(2,1)S(1)}, u32[]{:S(2)}, u32[]{:S(2)}) collective-permute-start(bf16[192,128]{1,0:T(8,128)(2,1)S(1)} %get-tuple-element.68.refs_0_), channel_id=1, source_target_pairs={{0,8},{2,10},{4,12},{6,14},{8,0},{10,2},{12,4},{14,6},{16,24},{18,... | collective-permute-start | bytes 147464 | tf_op jit(solution)/shard_map/ppermute | solution.py:60
  6.4 2.5 %collective-permute-start.2 = (bf16[192,128]{1,0:T(8,128)(2,1)S(1)}, bf16[192,128]{1,0:T(8,128)(2,1)S(1)}, u32[]{:S(2)}, u32[]{:S(2)}) collective-permute-start(bf16[192,128]{1,0:T(8,128)(2,1)S(1)} %get-tuple-element.68.refs_0_), channel_id=1, source_target_pairs={{0,24},{2,26},{4,28},{6,30},{8,16},{10,18},{12,20},{14,22},{16,8},... | collective-permute-start | bytes 147464 | tf_op jit(solution)/shard_map/ppermute | solution.py:60
  8.9 1.5 %collective-permute-start = (bf16[192,128]{1,0:T(8,128)(2,1)S(1)}, bf16[192,128]{1,0:T(8,128)(2,1)S(1)}, u32[]{:S(2)}, u32[]{:S(2)}) collective-permute-start(bf16[192,128]{1,0:T(8,128)(2,1)S(1)} %get-tuple-element.68.refs_0_), channel_id=1, source_target_pairs={{0,4},{2,6},{4,0},{6,2},{8,12},{10,14},{12,8},{14,10},{16,20},{18,... | collective-permute-start | bytes 147464 | tf_op jit(solution)/shard_map/ppermute | solution.py:64
  10.4 1.9 %collective-permute-done.2.refs_1_.refs_3_ = bf16[192,128]{1,0:T(8,128)(2,1)S(1)} collective-permute-done((bf16[192,128]{1,0:T(8,128)(2,1)S(1)}, bf16[192,128]{1,0:T(8,128)(2,1)S(1)}, u32[]{:S(2)}, u32[]{:S(2)}) %collective-permute-start.2) | collective-permute-done | bytes 49184 | tf_op jit(solution)/shard_map/ppermute | solution.py:60
  12.3 1.6 %collective-permute-start.3 = (bf16[384,128]{1,0:T(8,128)(2,1)S(1)}, bf16[384,128]{1,0:T(8,128)(2,1)S(1)}, u32[]{:S(2)}, u32[]{:S(2)}) collective-permute-start(bf16[384,128]{1,0:T(8,128)(2,1)S(1)} %shard_map.95), channel_id=1, source_target_pairs={{0,4},{2,6},{4,0},{6,2},{8,12},{10,14},{12,8},{14,10},{16,20},{18,... | collective-permute-start | bytes 294920 | tf_op jit(solution)/shard_map/ppermute | solution.py:64
  13.9 0.7 %pad_add_fusion.tables_in.refs_2_ = s32[16,16]{1,0:T(8,128)S(1)} fusion(s32[4,16]{1,0:T(4,128)} %bitcast.17, s32[4,16]{1,0:T(4,128)} %bitcast.18, s32[4,16]{1,0:T(4,128)} %bitcast.19, s32[4,16]{1,0:T(4,128)} %bitcast.20), kind=kLoop, calls=%fused_computation | loop fusion | flops 768 | bytes 2048 | tf_op jit(solution)/shard_map/concatenate | solution.py:621
  14.7 1.0 %copy-done.1 = bf16[1,32,32,192]{3,2,1,0:T(8,128)(2,1)S(1)} copy-done((bf16[1,32,32,192]{3,2,1,0:T(8,128)(2,1)S(1)}, bf16[1,32,32,192]{3,2,1,0:T(8,128)(2,1)}, u32[]{:S(2)}) %copy-start.1) | copy-done | bytes 393240
  15.7 1.1 %shard_map.96 = (bf16[512,1536]{1,0:T(8,128)(2,1)S(1)}, bf16[1024,192]{1,0:T(8,128)(2,1)S(1)}) custom-call(s32[16,16]{1,0:T(8,128)S(1)} %pad_add_fusion.tables_in.refs_2_, bf16[1024,192]{1,0:T(8,128)(2,1)S(1)} %bitcast.12), custom_call_target="tpu_custom_call" | custom-call | bytes 2360320 | tf_op jit(solution)/shard_map/pallas_call | solution.py:111
  16.8 0.2 collective-permute-done.3.refs_4_
  17.0 1.5 %shard_map.98 = (f32[576,384]{1,0:T(8,128)S(1)}, bf16[1152,384]{1,0:T(8,128)(2,1)S(1)}, bf16[128,384]{1,0:T(8,128)(2,1)S(1)}, bf16[3,192,1024]{2,1,0:T(8,128)(2,1)S(1)}) custom-call(bf16[32,32,192]{2,1,0:T(8,128)(2,1)S(1)} %get-tuple-element.73.field_ref.refs_3_, bf16[1024,192]{1,0:T(8,128)(2,1)S(1)} %get-tuple-element.74.own_ref, ...), custom_call_target="tpu_custom_call" | custom-call | flops 339738624 | bytes 4227072 | tf_op jit(solution)/shard_map/pallas_call | solution.py:111
  18.6 0.6 %shard_map.99 = f32[288,384]{1,0:T(8,128)S(1)} custom-call(bf16[3,192,1024]{2,1,0:T(8,128)(2,1)S(1)} %get-tuple-element.76.cols, bf16[1152,384]{1,0:T(8,128)(2,1)S(1)} %get-tuple-element.93.tall), custom_call_target="tpu_custom_call" | custom-call | flops 1358954496 | bytes 2506752 | tf_op jit(solution)/shard_map/pallas_call | solution.py:111
  19.3 0.5 collective-permute-start.8
  19.8 0.1 collective-permute-start.5
  19.9 0.5 collective-permute-start.6
  20.4 1.2 %shard_map.100.refs_3_ = f32[864,384]{1,0:T(8,128)S(1)} custom-call(bf16[3,192,1024]{2,1,0:T(8,128)(2,1)S(1)} %get-tuple-element.76.cols, bf16[1152,384]{1,0:T(8,128)(2,1)S(1)} %get-tuple-element.93.tall), custom_call_target="tpu_custom_call" | custom-call | tf_op jit(solution)/shard_map/pallas_call | solution.py:111
  21.7 0.6 collective-permute-done.6.refs_5_
  22.3 1.5 %shard_map.101 = (f32[224,384]{1,0:T(8,128)S(1)}, bf16[224,384]{1,0:T(8,128)(2,1)S(1)}, bf16[224,384]{1,0:T(8,128)(2,1)S(1)}, bf16[224,384]{1,0:T(8,128)(2,1)S(1)}) custom-call(bf16[1152,128]{1,0:T(8,128)(2,1)S(1)} %shard_map.97.refs_0_, bf16[1152,128]{1,0:T(8,128)(2,1)S(1)} %collective-permute-done.5.refs_1_, ...), custom_call_target="tpu_custom_call" | custom-call | bytes 5873664 | tf_op jit(solution)/shard_map/pallas_call | solution.py:111
  23.8 0.6 %collective-permute-start.10 = (bf16[224,384]{1,0:T(8,128)(2,1)S(1)}, bf16[224,384]{1,0:T(8,128)(2,1)S(1)}, u32[]{:S(2)}, u32[]{:S(2)}) collective-permute-start(bf16[224,384]{1,0:T(8,128)(2,1)S(1)} %get-tuple-element.91), channel_id=1, source_target_pairs={{0,8},{2,10},{4,12},{6,14},{8,0},{10,2},{12,4},{14,6},{16,24},{18,... | collective-permute-start | bytes 516104 | tf_op jit(solution)/shard_map/ppermute | solution.py:64
  24.4 2.4 %collective-permute-start.11 = (bf16[224,384]{1,0:T(8,128)(2,1)S(1)}, bf16[224,384]{1,0:T(8,128)(2,1)S(1)}, u32[]{:S(2)}, u32[]{:S(2)}) collective-permute-start(bf16[224,384]{1,0:T(8,128)(2,1)S(1)} %get-tuple-element.92), channel_id=1, source_target_pairs={{0,12},{2,14},{4,8},{6,10},{8,4},{10,6},{12,0},{14,2},{16,28},{18,... | collective-permute-start | bytes 516104 | tf_op jit(solution)/shard_map/ppermute | solution.py:64
  26.8 0.5 collective-permute-start.9
  27.3 2.9 %shard_map.102 = (f32[1024,192]{1,0:T(8,128)S(1)}, bf16[216,128]{1,0:T(8,128)(2,1)S(1)}) custom-call(bf16[1152,384]{1,0:T(8,128)(2,1)S(1)} %get-tuple-element.93.tall, bf16[9,384,384]{2,1,0:T(8,128)(2,1)S(1)} %bitcast.13), custom_call_target="tpu_custom_call" | custom-call | flops 1358954496 | bytes 4380672 | tf_op jit(solution)/shard_map/pallas_call | solution.py:111
  30.2 0.6 collective-permute-start.12
  30.8 2.5 %collective-permute-start.14 = (bf16[216,128]{1,0:T(8,128)(2,1)S(1)}, bf16[216,128]{1,0:T(8,128)(2,1)S(1)}, u32[]{:S(2)}, u32[]{:S(2)}) collective-permute-start(bf16[216,128]{1,0:T(8,128)(2,1)S(1)} %get-tuple-element.113.refs_0_), channel_id=1, source_target_pairs={{0,24},{2,26},{4,28},{6,30},{8,16},{10,18},{12,20},{14,22},{16,8},... | collective-permute-start | bytes 165896 | tf_op jit(solution)/shard_map/ppermute | solution.py:60
  33.3 1.2 %shard_map.104.place_ref = bf16[128,1728]{1,0:T(8,128)(2,1)S(1)} custom-call(s32[16,16]{1,0:T(8,128)S(1)} %pad_add_fusion.tables_in.refs_2_), custom_call_target="tpu_custom_call" | custom-call | bytes 443392 | tf_op jit(solution)/shard_map/pallas_call | solution.py:111
  34.5 1.3 %shard_map.103 = (bf16[144,192]{1,0:T(8,128)(2,1)S(1)}, bf16[576,128]{1,0:T(8,128)(2,1)S(1)}, bf16[576,128]{1,0:T(8,128)(2,1)S(1)}, bf16[600,128]{1,0:T(8,128)(2,1)S(1)}) custom-call(bf16[1152,128]{1,0:T(8,128)(2,1)S(1)} %shard_map.97.refs_0_, bf16[1152,128]{1,0:T(8,128)(2,1)S(1)} %collective-permute-done.5.refs_1_, ...), custom_call_target="tpu_custom_call" | custom-call | bytes 1487872 | tf_op jit(solution)/shard_map/pallas_call | solution.py:111
  35.8 0.6 collective-permute-done.9.refs_1_
  36.4 0.1 shard_map.105.held_ref
  36.5 1.7 %collective-permute-start.13 = (bf16[224,384]{1,0:T(8,128)(2,1)S(1)}, bf16[224,384]{1,0:T(8,128)(2,1)S(1)}, u32[]{:S(2)}, u32[]{:S(2)}) collective-permute-start(bf16[224,384]{1,0:T(8,128)(2,1)S(1)} %shard_map.105.held_ref), channel_id=1, source_target_pairs={{0,16},{2,18},{4,20},{6,22},{8,24},{10,26},{12,28},{14,30},{16,0},... | collective-permute-start | bytes 516104 | tf_op jit(solution)/shard_map/ppermute | solution.py:64
  38.2 1.0 %collective-permute-start.15 = (bf16[648,128]{1,0:T(8,128)(2,1)S(1)}, bf16[648,128]{1,0:T(8,128)(2,1)S(1)}, u32[]{:S(2)}, u32[]{:S(2)}) collective-permute-start(bf16[648,128]{1,0:T(8,128)(2,1)S(1)} %shard_map.106.refs_0_), channel_id=1, source_target_pairs={{0,4},{2,6},{4,0},{6,2},{8,12},{10,14},{12,8},{14,10},{16,20},{18,... | collective-permute-start | bytes 497672 | tf_op jit(solution)/shard_map/ppermute | solution.py:64
  39.2 1.5 %collective-permute-start.23 = (bf16[600,128]{1,0:T(8,128)(2,1)S(1)}, bf16[600,128]{1,0:T(8,128)(2,1)S(1)}, u32[]{:S(2)}, u32[]{:S(2)}) collective-permute-start(bf16[600,128]{1,0:T(8,128)(2,1)S(1)} %get-tuple-element.123), channel_id=1, source_target_pairs={{0,1},{1,0},{2,3},{3,2},{4,5},{5,4},{6,7},{7,6},{8,9},{9,8},{10,11... | collective-permute-start | bytes 460808 | tf_op jit(solution)/shard_map/ppermute | solution.py:708
  40.6 0.5 collective-permute-start.21
  41.2 1.5 %collective-permute-start.22 = (bf16[576,128]{1,0:T(8,128)(2,1)S(1)}, bf16[576,128]{1,0:T(8,128)(2,1)S(1)}, u32[]{:S(2)}, u32[]{:S(2)}) collective-permute-start(bf16[576,128]{1,0:T(8,128)(2,1)S(1)} %get-tuple-element.122), channel_id=1, source_target_pairs={{0,1},{1,0},{2,3},{3,2},{4,5},{5,4},{6,7},{7,6},{8,9},{9,8},{10,11... | collective-permute-start | bytes 442376 | tf_op jit(solution)/shard_map/ppermute | solution.py:708
  42.7 0.9 %collective-permute-done.15.refs_1_ = bf16[648,128]{1,0:T(8,128)(2,1)S(1)} collective-permute-done((bf16[648,128]{1,0:T(8,128)(2,1)S(1)}, bf16[648,128]{1,0:T(8,128)(2,1)S(1)}, u32[]{:S(2)}, u32[]{:S(2)}) %collective-permute-start.15) | collective-permute-done | bytes 165920 | tf_op jit(solution)/shard_map/ppermute | solution.py:64
  43.6 2.0 %collective-permute-done.13.got_ref = bf16[224,384]{1,0:T(8,128)(2,1)S(1)} collective-permute-done((bf16[224,384]{1,0:T(8,128)(2,1)S(1)}, bf16[224,384]{1,0:T(8,128)(2,1)S(1)}, u32[]{:S(2)}, u32[]{:S(2)}) %collective-permute-start.13) | collective-permute-done | bytes 172064 | tf_op jit(solution)/shard_map/ppermute | solution.py:64
  45.6 1.6 %collective-permute-start.16 = (bf16[224,384]{1,0:T(8,128)(2,1)S(1)}, bf16[224,384]{1,0:T(8,128)(2,1)S(1)}, u32[]{:S(2)}, u32[]{:S(2)}) collective-permute-start(bf16[224,384]{1,0:T(8,128)(2,1)S(1)} %shard_map.107.refs_0_), channel_id=1, source_target_pairs={{0,4},{2,6},{4,0},{6,2},{8,12},{10,14},{12,8},{14,10},{16,20},{18,... | collective-permute-start | bytes 516104 | tf_op jit(solution)/shard_map/ppermute | solution.py:64
  47.2 1.2 %collective-permute-done.21.refs_0_ = bf16[576,128]{1,0:T(8,128)(2,1)S(1)} collective-permute-done((bf16[576,128]{1,0:T(8,128)(2,1)S(1)}, bf16[576,128]{1,0:T(8,128)(2,1)S(1)}, u32[]{:S(2)}, u32[]{:S(2)}) %collective-permute-start.21) | collective-permute-done | bytes 147488 | tf_op jit(solution)/shard_map/ppermute | solution.py:708
  48.4 1.3 %collective-permute-start.18 = (bf16[224,384]{1,0:T(8,128)(2,1)S(1)}, bf16[224,384]{1,0:T(8,128)(2,1)S(1)}, u32[]{:S(2)}, u32[]{:S(2)}) collective-permute-start(bf16[224,384]{1,0:T(8,128)(2,1)S(1)} %shard_map.107.refs_0_), channel_id=1, source_target_pairs={{0,12},{2,14},{4,8},{6,10},{8,4},{10,6},{12,0},{14,2},{16,28},{18,... | collective-permute-start | bytes 516104 | tf_op jit(solution)/shard_map/ppermute | solution.py:64
  49.7 0.3 collective-permute-done.22.refs_1_
  50.0 0.5 collective-permute-start.20
  50.5 3.9 %shard_map.109 = bf16[1024,192]{1,0:T(8,128)(2,1)} custom-call(bf16[32,32,192]{2,1,0:T(8,128)(2,1)S(1)} %get-tuple-element.73.field_ref.refs_3_, bf16[144,192]{1,0:T(8,128)(2,1)S(1)} %get-tuple-element.120.halos_ref, bf16[9,384,384]{2,1,0:T(8,128)(2,1)S(1)} %bitcast.14, bf16[576,128]{1,0:T(8,128)(2,1)S(1)} %collective-permute-done.21.refs_0_, ...), custom_call_target="tpu_custom_call" | custom-call | flops 2717908992 | bytes 3944448 | tf_op jit(solution)/shard_map/pallas_call | solution.py:111
  54.4 1.3 %shard_map.108 = bf16[1024,192]{1,0:T(8,128)(2,1)} custom-call(bf16[128,1728]{1,0:T(8,128)(2,1)S(1)} %shard_map.104.place_ref, f32[1024,192]{1,0:T(8,128)S(1)} %get-tuple-element.117.inner_ref, bf16[648,128]{1,0:T(8,128)(2,1)S(1)} %shard_map.106.refs_0_, bf16[648,128]{1,0:T(8,128)(2,1)S(1)} %collective-permute-done.15.refs_1_, ...), custom_call_target="tpu_custom_call" | custom-call | bytes 2285568 | tf_op jit(solution)/shard_map/pallas_call | solution.py:111
  55.7 0.7 %collective-permute-done.18.refs_3_ = bf16[224,384]{1,0:T(8,128)(2,1)S(1)} collective-permute-done((bf16[224,384]{1,0:T(8,128)(2,1)S(1)}, bf16[224,384]{1,0:T(8,128)(2,1)S(1)}, u32[]{:S(2)}, u32[]{:S(2)}) %collective-permute-start.18) | collective-permute-done | bytes 172064 | tf_op jit(solution)/shard_map/ppermute | solution.py:64
  56.4 0.5 collective-permute-start.26
  56.9 1.4 %shard_map.110.refs_0_ = f32[1728,384]{1,0:T(8,128)} custom-call(bf16[224,384]{1,0:T(8,128)(2,1)S(1)} %shard_map.107.refs_0_, bf16[224,384]{1,0:T(8,128)(2,1)S(1)} %collective-permute-done.16.refs_1_, bf16[224,384]{1,0:T(8,128)(2,1)S(1)} %collective-permute-done.17.refs_2_, bf16[224,384]{1,0:T(8,128)(2,1)S(1)} %collective-permute-done.18.refs_3_, ...), custom_call_target="tpu_custom_call" | custom-call | tf_op jit(solution)/shard_map/pallas_call | solution.py:455
  58.3 1.1 %shard_map.111 = f32[1728,384]{1,0:T(8,128)} custom-call(f32[1728,384]{1,0:T(8,128)} %shard_map.110.refs_0_, bf16[224,384]{1,0:T(8,128)(2,1)S(1)} %collective-permute-done.25.refs_1_, bf16[224,384]{1,0:T(8,128)(2,1)S(1)} %collective-permute-done.26.refs_2_, bf16[224,384]{1,0:T(8,128)(2,1)S(1)} %collective-permute-done.27.refs_3_), custom_call_target="tpu_custom_call", output_to_operand_aliasing={{}: (0, {})} | custom-call | tf_op jit(solution)/shard_map/pallas_call | solution.py:455
  (33 shorter events, 0.2 us)
Async XLA Ops:
  0.6 16.4 %collective-permute-start.4 = (bf16[1024,192]{1,0:T(8,128)(2,1)}, bf16[1024,192]{1,0:T(8,128)(2,1)S(1)}, u32[]{:S(2)}, u32[]{:S(2)}) collective-permute-start(bf16[1024,192]{1,0:T(8,128)(2,1)} %bitcast.11), channel_id=1, source_target_pairs={{0,1},{1,0},{2,3},{3,2},{4,5},{5,4},{6,7},{7,6},{8,9},{9,8},{10,11... | collective-permute-start | bytes 1179656 | tf_op jit(solution)/shard_map/ppermute | solution.py:613
  3.6 1.0 %copy-start = (bf16[1,32,32,192]{3,2,1,0:T(8,128)(2,1)S(1)}, bf16[1,32,32,192]{3,2,1,0:T(8,128)(2,1)}, u32[]{:S(2)}) copy-start(bf16[1,32,32,192]{3,2,1,0:T(8,128)(2,1)} %param.7) | copy-start | bytes 1179652
  4.8 5.6 %collective-permute-start.1 = (bf16[192,128]{1,0:T(8,128)(2,1)S(1)}, bf16[192,128]{1,0:T(8,128)(2,1)S(1)}, u32[]{:S(2)}, u32[]{:S(2)}) collective-permute-start(bf16[192,128]{1,0:T(8,128)(2,1)S(1)} %get-tuple-element.68.refs_0_), channel_id=1, source_target_pairs={{0,8},{2,10},{4,12},{6,14},{8,0},{10,2},{12,4},{14,6},{16,24},{18,... | collective-permute-start | bytes 147464 | tf_op jit(solution)/shard_map/ppermute | solution.py:60
  6.4 5.9 %collective-permute-start.2 = (bf16[192,128]{1,0:T(8,128)(2,1)S(1)}, bf16[192,128]{1,0:T(8,128)(2,1)S(1)}, u32[]{:S(2)}, u32[]{:S(2)}) collective-permute-start(bf16[192,128]{1,0:T(8,128)(2,1)S(1)} %get-tuple-element.68.refs_0_), channel_id=1, source_target_pairs={{0,24},{2,26},{4,28},{6,30},{8,16},{10,18},{12,20},{14,22},{16,8},... | collective-permute-start | bytes 147464 | tf_op jit(solution)/shard_map/ppermute | solution.py:60
  8.9 7.9 %collective-permute-start = (bf16[192,128]{1,0:T(8,128)(2,1)S(1)}, bf16[192,128]{1,0:T(8,128)(2,1)S(1)}, u32[]{:S(2)}, u32[]{:S(2)}) collective-permute-start(bf16[192,128]{1,0:T(8,128)(2,1)S(1)} %get-tuple-element.68.refs_0_), channel_id=1, source_target_pairs={{0,4},{2,6},{4,0},{6,2},{8,12},{10,14},{12,8},{14,10},{16,20},{18,... | collective-permute-start | bytes 147464 | tf_op jit(solution)/shard_map/ppermute | solution.py:64
  12.3 4.7 %collective-permute-start.3 = (bf16[384,128]{1,0:T(8,128)(2,1)S(1)}, bf16[384,128]{1,0:T(8,128)(2,1)S(1)}, u32[]{:S(2)}, u32[]{:S(2)}) collective-permute-start(bf16[384,128]{1,0:T(8,128)(2,1)S(1)} %shard_map.95), channel_id=1, source_target_pairs={{0,4},{2,6},{4,0},{6,2},{8,12},{10,14},{12,8},{14,10},{16,20},{18,... | collective-permute-start | bytes 294920 | tf_op jit(solution)/shard_map/ppermute | solution.py:64
  14.7 1.0 %copy-start.1 = (bf16[1,32,32,192]{3,2,1,0:T(8,128)(2,1)S(1)}, bf16[1,32,32,192]{3,2,1,0:T(8,128)(2,1)}, u32[]{:S(2)}) copy-start(bf16[1,32,32,192]{3,2,1,0:T(8,128)(2,1)} %param.9) | copy-start | bytes 1179652
  18.6 3.7 %collective-permute-start.7 = (f32[576,384]{1,0:T(8,128)S(1)}, f32[576,384]{1,0:T(8,128)S(1)}, u32[]{:S(2)}, u32[]{:S(2)}) collective-permute-start(f32[576,384]{1,0:T(8,128)S(1)} %get-tuple-element.84), channel_id=1, source_target_pairs={{0,2},{2,0},{4,6},{6,4},{8,10},{10,8},{12,14},{14,12},{16,18},{18,... | collective-permute-start | bytes 2654216 | tf_op jit(solution)/shard_map/ppermute | solution.py:64
  19.3 3.0 %collective-permute-start.8 = (f32[288,384]{1,0:T(8,128)S(1)}, f32[288,384]{1,0:T(8,128)S(1)}, u32[]{:S(2)}, u32[]{:S(2)}) collective-permute-start(f32[288,384]{1,0:T(8,128)S(1)} %shard_map.99), channel_id=1, source_target_pairs={{0,2},{2,0},{4,6},{6,4},{8,10},{10,8},{12,14},{14,12},{16,18},{18,... | collective-permute-start | bytes 1327112 | tf_op jit(solution)/shard_map/ppermute | solution.py:64
  19.8 2.4 %collective-permute-start.5 = (bf16[1152,128]{1,0:T(8,128)(2,1)S(1)}, bf16[1152,128]{1,0:T(8,128)(2,1)S(1)}, u32[]{:S(2)}, u32[]{:S(2)}) collective-permute-start(bf16[1152,128]{1,0:T(8,128)(2,1)S(1)} %shard_map.97.refs_0_), channel_id=1, source_target_pairs={{0,2},{2,0},{4,6},{6,4},{8,10},{10,8},{12,14},{14,12},{16,18},{18,... | collective-permute-start | bytes 884744 | tf_op jit(solution)/shard_map/ppermute | solution.py:64
  19.9 2.3 %collective-permute-start.6 = (bf16[128,384]{1,0:T(8,128)(2,1)S(1)}, bf16[128,384]{1,0:T(8,128)(2,1)S(1)}, u32[]{:S(2)}, u32[]{:S(2)}) collective-permute-start(bf16[128,384]{1,0:T(8,128)(2,1)S(1)} %get-tuple-element.79.refs_4_), channel_id=1, source_target_pairs={{0,2},{2,0},{4,6},{6,4},{8,10},{10,8},{12,14},{14,12},{16,18},{18,... | collective-permute-start | bytes 294920 | tf_op jit(solution)/shard_map/ppermute | solution.py:64
  21.7 5.7 %copy-start.2 = (bf16[3,3,384,384]{3,2,1,0:T(8,128)(2,1)S(1)}, bf16[3,3,384,384]{3,2,1,0:T(8,128)(2,1)}, u32[]{:S(2)}) copy-start(bf16[3,3,384,384]{3,2,1,0:T(8,128)(2,1)} %param.8) | copy-start | bytes 7962628
  23.8 12.0 %collective-permute-start.10 = (bf16[224,384]{1,0:T(8,128)(2,1)S(1)}, bf16[224,384]{1,0:T(8,128)(2,1)S(1)}, u32[]{:S(2)}, u32[]{:S(2)}) collective-permute-start(bf16[224,384]{1,0:T(8,128)(2,1)S(1)} %get-tuple-element.91), channel_id=1, source_target_pairs={{0,8},{2,10},{4,12},{6,14},{8,0},{10,2},{12,4},{14,6},{16,24},{18,... | collective-permute-start | bytes 516104 | tf_op jit(solution)/shard_map/ppermute | solution.py:64
  24.4 11.3 %collective-permute-start.11 = (bf16[224,384]{1,0:T(8,128)(2,1)S(1)}, bf16[224,384]{1,0:T(8,128)(2,1)S(1)}, u32[]{:S(2)}, u32[]{:S(2)}) collective-permute-start(bf16[224,384]{1,0:T(8,128)(2,1)S(1)} %get-tuple-element.92), channel_id=1, source_target_pairs={{0,12},{2,14},{4,8},{6,10},{8,4},{10,6},{12,0},{14,2},{16,28},{18,... | collective-permute-start | bytes 516104 | tf_op jit(solution)/shard_map/ppermute | solution.py:64
  26.8 9.6 %collective-permute-start.9 = (bf16[224,384]{1,0:T(8,128)(2,1)S(1)}, bf16[224,384]{1,0:T(8,128)(2,1)S(1)}, u32[]{:S(2)}, u32[]{:S(2)}) collective-permute-start(bf16[224,384]{1,0:T(8,128)(2,1)S(1)} %get-tuple-element.90), channel_id=1, source_target_pairs={{0,4},{2,6},{4,0},{6,2},{8,12},{10,14},{12,8},{14,10},{16,20},{18,... | collective-permute-start | bytes 516104 | tf_op jit(solution)/shard_map/ppermute | solution.py:64
  30.2 5.5 %collective-permute-start.12 = (bf16[216,128]{1,0:T(8,128)(2,1)S(1)}, bf16[216,128]{1,0:T(8,128)(2,1)S(1)}, u32[]{:S(2)}, u32[]{:S(2)}) collective-permute-start(bf16[216,128]{1,0:T(8,128)(2,1)S(1)} %get-tuple-element.113.refs_0_), channel_id=1, source_target_pairs={{0,8},{2,10},{4,12},{6,14},{8,0},{10,2},{12,4},{14,6},{16,24},{18,... | collective-permute-start | bytes 165896 | tf_op jit(solution)/shard_map/ppermute | solution.py:60
  30.8 7.3 %collective-permute-start.14 = (bf16[216,128]{1,0:T(8,128)(2,1)S(1)}, bf16[216,128]{1,0:T(8,128)(2,1)S(1)}, u32[]{:S(2)}, u32[]{:S(2)}) collective-permute-start(bf16[216,128]{1,0:T(8,128)(2,1)S(1)} %get-tuple-element.113.refs_0_), channel_id=1, source_target_pairs={{0,24},{2,26},{4,28},{6,30},{8,16},{10,18},{12,20},{14,22},{16,8},... | collective-permute-start | bytes 165896 | tf_op jit(solution)/shard_map/ppermute | solution.py:60
  36.5 9.1 %collective-permute-start.13 = (bf16[224,384]{1,0:T(8,128)(2,1)S(1)}, bf16[224,384]{1,0:T(8,128)(2,1)S(1)}, u32[]{:S(2)}, u32[]{:S(2)}) collective-permute-start(bf16[224,384]{1,0:T(8,128)(2,1)S(1)} %shard_map.105.held_ref), channel_id=1, source_target_pairs={{0,16},{2,18},{4,20},{6,22},{8,24},{10,26},{12,28},{14,30},{16,0},... | collective-permute-start | bytes 516104 | tf_op jit(solution)/shard_map/ppermute | solution.py:64
  38.2 5.4 %collective-permute-start.15 = (bf16[648,128]{1,0:T(8,128)(2,1)S(1)}, bf16[648,128]{1,0:T(8,128)(2,1)S(1)}, u32[]{:S(2)}, u32[]{:S(2)}) collective-permute-start(bf16[648,128]{1,0:T(8,128)(2,1)S(1)} %shard_map.106.refs_0_), channel_id=1, source_target_pairs={{0,4},{2,6},{4,0},{6,2},{8,12},{10,14},{12,8},{14,10},{16,20},{18,... | collective-permute-start | bytes 497672 | tf_op jit(solution)/shard_map/ppermute | solution.py:64
  39.2 10.8 %collective-permute-start.23 = (bf16[600,128]{1,0:T(8,128)(2,1)S(1)}, bf16[600,128]{1,0:T(8,128)(2,1)S(1)}, u32[]{:S(2)}, u32[]{:S(2)}) collective-permute-start(bf16[600,128]{1,0:T(8,128)(2,1)S(1)} %get-tuple-element.123), channel_id=1, source_target_pairs={{0,1},{1,0},{2,3},{3,2},{4,5},{5,4},{6,7},{7,6},{8,9},{9,8},{10,11... | collective-permute-start | bytes 460808 | tf_op jit(solution)/shard_map/ppermute | solution.py:708
  40.6 7.7 %collective-permute-start.21 = (bf16[576,128]{1,0:T(8,128)(2,1)S(1)}, bf16[576,128]{1,0:T(8,128)(2,1)S(1)}, u32[]{:S(2)}, u32[]{:S(2)}) collective-permute-start(bf16[576,128]{1,0:T(8,128)(2,1)S(1)} %get-tuple-element.121), channel_id=1, source_target_pairs={{0,1},{1,0},{2,3},{3,2},{4,5},{5,4},{6,7},{7,6},{8,9},{9,8},{10,11... | collective-permute-start | bytes 442376 | tf_op jit(solution)/shard_map/ppermute | solution.py:708
  41.2 8.8 %collective-permute-start.22 = (bf16[576,128]{1,0:T(8,128)(2,1)S(1)}, bf16[576,128]{1,0:T(8,128)(2,1)S(1)}, u32[]{:S(2)}, u32[]{:S(2)}) collective-permute-start(bf16[576,128]{1,0:T(8,128)(2,1)S(1)} %get-tuple-element.122), channel_id=1, source_target_pairs={{0,1},{1,0},{2,3},{3,2},{4,5},{5,4},{6,7},{7,6},{8,9},{9,8},{10,11... | collective-permute-start | bytes 442376 | tf_op jit(solution)/shard_map/ppermute | solution.py:708
  45.6 10.1 %collective-permute-start.16 = (bf16[224,384]{1,0:T(8,128)(2,1)S(1)}, bf16[224,384]{1,0:T(8,128)(2,1)S(1)}, u32[]{:S(2)}, u32[]{:S(2)}) collective-permute-start(bf16[224,384]{1,0:T(8,128)(2,1)S(1)} %shard_map.107.refs_0_), channel_id=1, source_target_pairs={{0,4},{2,6},{4,0},{6,2},{8,12},{10,14},{12,8},{14,10},{16,20},{18,... | collective-permute-start | bytes 516104 | tf_op jit(solution)/shard_map/ppermute | solution.py:64
  47.2 8.5 %collective-permute-start.17 = (bf16[224,384]{1,0:T(8,128)(2,1)S(1)}, bf16[224,384]{1,0:T(8,128)(2,1)S(1)}, u32[]{:S(2)}, u32[]{:S(2)}) collective-permute-start(bf16[224,384]{1,0:T(8,128)(2,1)S(1)} %shard_map.107.refs_0_), channel_id=1, source_target_pairs={{0,8},{2,10},{4,12},{6,14},{8,0},{10,2},{12,4},{14,6},{16,24},{18,... | collective-permute-start | bytes 516104 | tf_op jit(solution)/shard_map/ppermute | solution.py:64
  48.4 8.0 %collective-permute-start.18 = (bf16[224,384]{1,0:T(8,128)(2,1)S(1)}, bf16[224,384]{1,0:T(8,128)(2,1)S(1)}, u32[]{:S(2)}, u32[]{:S(2)}) collective-permute-start(bf16[224,384]{1,0:T(8,128)(2,1)S(1)} %shard_map.107.refs_0_), channel_id=1, source_target_pairs={{0,12},{2,14},{4,8},{6,10},{8,4},{10,6},{12,0},{14,2},{16,28},{18,... | collective-permute-start | bytes 516104 | tf_op jit(solution)/shard_map/ppermute | solution.py:64
  49.9 4.4 %collective-permute-start.19 = (bf16[648,128]{1,0:T(8,128)(2,1)S(1)}, bf16[648,128]{1,0:T(8,128)(2,1)S(1)}, u32[]{:S(2)}, u32[]{:S(2)}) collective-permute-start(bf16[648,128]{1,0:T(8,128)(2,1)S(1)} %shard_map.106.refs_0_), channel_id=1, source_target_pairs={{0,2},{2,0},{4,6},{6,4},{8,10},{10,8},{12,14},{14,12},{16,18},{18,... | collective-permute-start | bytes 497672 | tf_op jit(solution)/shard_map/ppermute | solution.py:64
  50.0 4.4 %collective-permute-start.20 = (bf16[648,128]{1,0:T(8,128)(2,1)S(1)}, bf16[648,128]{1,0:T(8,128)(2,1)S(1)}, u32[]{:S(2)}, u32[]{:S(2)}) collective-permute-start(bf16[648,128]{1,0:T(8,128)(2,1)S(1)} %collective-permute-done.15.refs_1_), channel_id=1, source_target_pairs={{0,2},{2,0},{4,6},{6,4},{8,10},{10,8},{12,14},{14,12},{16,18},{18,... | collective-permute-start | bytes 497672 | tf_op jit(solution)/shard_map/ppermute | solution.py:64
  54.3 2.5 %collective-permute-start.24 = (bf16[224,384]{1,0:T(8,128)(2,1)S(1)}, bf16[224,384]{1,0:T(8,128)(2,1)S(1)}, u32[]{:S(2)}, u32[]{:S(2)}) collective-permute-start(bf16[224,384]{1,0:T(8,128)(2,1)S(1)} %shard_map.107.refs_0_), channel_id=1, source_target_pairs={{0,2},{2,0},{4,6},{6,4},{8,10},{10,8},{12,14},{14,12},{16,18},{18,... | collective-permute-start | bytes 516104 | tf_op jit(solution)/shard_map/ppermute | solution.py:64
  56.4 1.9 %collective-permute-start.25 = (bf16[224,384]{1,0:T(8,128)(2,1)S(1)}, bf16[224,384]{1,0:T(8,128)(2,1)S(1)}, u32[]{:S(2)}, u32[]{:S(2)}) collective-permute-start(bf16[224,384]{1,0:T(8,128)(2,1)S(1)} %collective-permute-done.16.refs_1_), channel_id=1, source_target_pairs={{0,2},{2,0},{4,6},{6,4},{8,10},{10,8},{12,14},{14,12},{16,18},{18,... | collective-permute-start | bytes 516104 | tf_op jit(solution)/shard_map/ppermute | solution.py:64
  56.4 1.9 %collective-permute-start.26 = (bf16[224,384]{1,0:T(8,128)(2,1)S(1)}, bf16[224,384]{1,0:T(8,128)(2,1)S(1)}, u32[]{:S(2)}, u32[]{:S(2)}) collective-permute-start(bf16[224,384]{1,0:T(8,128)(2,1)S(1)} %collective-permute-done.17.refs_2_), channel_id=1, source_target_pairs={{0,2},{2,0},{4,6},{6,4},{8,10},{10,8},{12,14},{14,12},{16,18},{18,... | collective-permute-start | bytes 516104 | tf_op jit(solution)/shard_map/ppermute | solution.py:64
  56.9 1.4 %collective-permute-start.27 = (bf16[224,384]{1,0:T(8,128)(2,1)S(1)}, bf16[224,384]{1,0:T(8,128)(2,1)S(1)}, u32[]{:S(2)}, u32[]{:S(2)}) collective-permute-start(bf16[224,384]{1,0:T(8,128)(2,1)S(1)} %collective-permute-done.18.refs_3_), channel_id=1, source_target_pairs={{0,2},{2,0},{4,6},{6,4},{8,10},{10,8},{12,14},{14,12},{16,18},{18,... | collective-permute-start | bytes 516104 | tf_op jit(solution)/shard_map/ppermute | solution.py:64

commit v16 on v15

--- a/solution.py
+++ b/solution.py
@@ -10,7 +10,7 @@
 from jax.sharding import PartitionSpec as P
 
 SPAN = 4
-EXTRA = 16
+EXTRA = 32
 PARTS = 3
 
 

time: 59.6 us -> 61.7 us (1.035)
  waiting for transfers between devices: 8.37 us -> 11.2 us
  starting transfers between devices: 28.1 us -> 27.3 us
    ppermute x20, waiting for transfers between devices: 5.03 us -> 7.56 us  [by_mask(): return lax.ppermute(value, 'tile', [(i, i ^ mask) for i in range(count)])]
    ppermute x4, waiting for transfers between devices: 1.9 us -> 3.08 us  [by_swap(): return lax.ppermute(value, 'tile', pairs)]
    ppermute x3, waiting for transfers between devices: 1.44 us -> 0.56 us  [start_aside(): lax.ppermute(v, 'ch', others)]
    ppermute x20, starting transfers between devices: 14.4 us -> 13.6 us  [by_mask(): return lax.ppermute(value, 'tile', [(i, i ^ mask) for i in range(count)])]
  transfers between devices with their start and end apart: 28 -> 28, of which waited for: 9 -> 8; matrix products, arithmetic and copies ran while one was open for 1% -> 1% of each run, Pallas kernels for 25% -> 25%
where the time goes in v16:
time: 61.7 us; the launch traced here: 61.4 us
  starting transfers between devices  27.3 us (44%)
  Pallas kernels  19.2 us (31%)
  waiting for transfers between devices  11.2 us (18%)
  local copies, waits for them, and re-layouts  2.09 us (3%)
  between operations  0.81 us (1%)
  other arithmetic  0.74 us (1%)
    pallas_call x16, Pallas kernels, call(): pl.pallas_call(kernel, out_shape=tuple(outs), in_specs=in_specs, out_spec...  16.8 us
    ppermute x20, starting transfers between devices, by_mask(): return lax.ppermute(value, 'tile', [(i, i ^ mask) for i in range(count)])  13.6 us
    ppermute x20, waiting for transfers between devices, by_mask(): return lax.ppermute(value, 'tile', [(i, i ^ mask) for i in range(count)])  7.56 us
    ppermute x4, starting transfers between devices, by_swap(): return lax.ppermute(value, 'tile', pairs)  7.17 us
    ppermute x3, starting transfers between devices, start_aside(): lax.ppermute(v, 'ch', others)  3.52 us
    ppermute x4, waiting for transfers between devices, by_swap(): return lax.ppermute(value, 'tile', pairs)  3.08 us
    ppermute x1, starting transfers between devices, body(): cot_other = lax.ppermute(cot_own, 'ch', others)  3 us
    pallas_call x2, Pallas kernels, unfold(): pl.pallas_call(functools.partial(unfold_kernel, whole.shape[0] // 2, chun...  2.41 us
  transfers between devices with their start and end apart: 28, of which 8 were waited for; matrix products, arithmetic and copies ran while one was open for 1% of the time, Pallas kernels for 25%

profile of v16, /device:TPU:0, one launch (start us, length us, event | category | flops | bytes accessed | tf_op | source)
XLA Modules:
  0.0 61.4 jit_solution(2538494854992487908)
XLA Ops:
  0.6 3.0 %collective-permute-start.4 = (bf16[1024,192]{1,0:T(8,128)(2,1)}, bf16[1024,192]{1,0:T(8,128)(2,1)S(1)}, u32[]{:S(2)}, u32[]{:S(2)}) collective-permute-start(bf16[1024,192]{1,0:T(8,128)(2,1)} %bitcast.11), channel_id=1, source_target_pairs={{0,1},{1,0},{2,3},{3,2},{4,5},{5,4},{6,7},{7,6},{8,9},{9,8},{10,11... | collective-permute-start | bytes 1179656 | tf_op jit(solution)/shard_map/ppermute | solution.py:613
  3.6 1.0 %copy-done = bf16[1,32,32,192]{3,2,1,0:T(8,128)(2,1)S(1)} copy-done((bf16[1,32,32,192]{3,2,1,0:T(8,128)(2,1)S(1)}, bf16[1,32,32,192]{3,2,1,0:T(8,128)(2,1)}, u32[]{:S(2)}) %copy-start) | copy-done | bytes 393240
  4.7 0.1 shard_map.94
  4.8 1.6 %collective-permute-start.1 = (bf16[192,128]{1,0:T(8,128)(2,1)S(1)}, bf16[192,128]{1,0:T(8,128)(2,1)S(1)}, u32[]{:S(2)}, u32[]{:S(2)}) collective-permute-start(bf16[192,128]{1,0:T(8,128)(2,1)S(1)} %get-tuple-element.68.refs_0_), channel_id=1, source_target_pairs={{0,8},{2,10},{4,12},{6,14},{8,0},{10,2},{12,4},{14,6},{16,24},{18,... | collective-permute-start | bytes 147464 | tf_op jit(solution)/shard_map/ppermute | solution.py:60
  6.4 2.5 %collective-permute-start.2 = (bf16[192,128]{1,0:T(8,128)(2,1)S(1)}, bf16[192,128]{1,0:T(8,128)(2,1)S(1)}, u32[]{:S(2)}, u32[]{:S(2)}) collective-permute-start(bf16[192,128]{1,0:T(8,128)(2,1)S(1)} %get-tuple-element.68.refs_0_), channel_id=1, source_target_pairs={{0,24},{2,26},{4,28},{6,30},{8,16},{10,18},{12,20},{14,22},{16,8},... | collective-permute-start | bytes 147464 | tf_op jit(solution)/shard_map/ppermute | solution.py:60
  8.9 1.5 %collective-permute-start = (bf16[192,128]{1,0:T(8,128)(2,1)S(1)}, bf16[192,128]{1,0:T(8,128)(2,1)S(1)}, u32[]{:S(2)}, u32[]{:S(2)}) collective-permute-start(bf16[192,128]{1,0:T(8,128)(2,1)S(1)} %get-tuple-element.68.refs_0_), channel_id=1, source_target_pairs={{0,4},{2,6},{4,0},{6,2},{8,12},{10,14},{12,8},{14,10},{16,20},{18,... | collective-permute-start | bytes 147464 | tf_op jit(solution)/shard_map/ppermute | solution.py:64
  10.4 1.9 %collective-permute-done.2.refs_1_.refs_3_ = bf16[192,128]{1,0:T(8,128)(2,1)S(1)} collective-permute-done((bf16[192,128]{1,0:T(8,128)(2,1)S(1)}, bf16[192,128]{1,0:T(8,128)(2,1)S(1)}, u32[]{:S(2)}, u32[]{:S(2)}) %collective-permute-start.2) | collective-permute-done | bytes 49184 | tf_op jit(solution)/shard_map/ppermute | solution.py:60
  12.3 1.6 %collective-permute-start.3 = (bf16[384,128]{1,0:T(8,128)(2,1)S(1)}, bf16[384,128]{1,0:T(8,128)(2,1)S(1)}, u32[]{:S(2)}, u32[]{:S(2)}) collective-permute-start(bf16[384,128]{1,0:T(8,128)(2,1)S(1)} %shard_map.95), channel_id=1, source_target_pairs={{0,4},{2,6},{4,0},{6,2},{8,12},{10,14},{12,8},{14,10},{16,20},{18,... | collective-permute-start | bytes 294920 | tf_op jit(solution)/shard_map/ppermute | solution.py:64
  13.9 0.7 %pad_add_fusion.tables_in.refs_2_ = s32[16,16]{1,0:T(8,128)S(1)} fusion(s32[4,16]{1,0:T(4,128)} %bitcast.17, s32[4,16]{1,0:T(4,128)} %bitcast.18, s32[4,16]{1,0:T(4,128)} %bitcast.19, s32[4,16]{1,0:T(4,128)} %bitcast.20), kind=kLoop, calls=%fused_computation | loop fusion | flops 768 | bytes 2048 | tf_op jit(solution)/shard_map/concatenate | solution.py:621
  14.7 1.0 %copy-done.1 = bf16[1,32,32,192]{3,2,1,0:T(8,128)(2,1)S(1)} copy-done((bf16[1,32,32,192]{3,2,1,0:T(8,128)(2,1)S(1)}, bf16[1,32,32,192]{3,2,1,0:T(8,128)(2,1)}, u32[]{:S(2)}) %copy-start.1) | copy-done | bytes 393240
  15.7 1.1 %shard_map.96 = (bf16[512,1536]{1,0:T(8,128)(2,1)S(1)}, bf16[1024,192]{1,0:T(8,128)(2,1)S(1)}) custom-call(s32[16,16]{1,0:T(8,128)S(1)} %pad_add_fusion.tables_in.refs_2_, bf16[1024,192]{1,0:T(8,128)(2,1)S(1)} %bitcast.12), custom_call_target="tpu_custom_call" | custom-call | bytes 2360320 | tf_op jit(solution)/shard_map/pallas_call | solution.py:111
  16.8 0.2 collective-permute-done.3.refs_4_
  17.0 1.5 %shard_map.98 = (f32[576,384]{1,0:T(8,128)S(1)}, bf16[1152,384]{1,0:T(8,128)(2,1)S(1)}, bf16[128,384]{1,0:T(8,128)(2,1)S(1)}, bf16[3,192,1024]{2,1,0:T(8,128)(2,1)S(1)}) custom-call(bf16[32,32,192]{2,1,0:T(8,128)(2,1)S(1)} %get-tuple-element.73.field_ref.refs_3_, bf16[1024,192]{1,0:T(8,128)(2,1)S(1)} %get-tuple-element.74.own_ref, ...), custom_call_target="tpu_custom_call" | custom-call | flops 339738624 | bytes 4227072 | tf_op jit(solution)/shard_map/pallas_call | solution.py:111
  18.6 0.1 collective-permute-start.7
  18.6 0.6 %shard_map.99 = f32[288,384]{1,0:T(8,128)S(1)} custom-call(bf16[3,192,1024]{2,1,0:T(8,128)(2,1)S(1)} %get-tuple-element.76.cols, bf16[1152,384]{1,0:T(8,128)(2,1)S(1)} %get-tuple-element.93.tall), custom_call_target="tpu_custom_call" | custom-call | flops 1358954496 | bytes 2506752 | tf_op jit(solution)/shard_map/pallas_call | solution.py:111
  19.3 0.5 collective-permute-start.8
  19.8 0.1 collective-permute-start.5
  19.9 0.5 collective-permute-start.6
  20.4 1.2 %shard_map.100.refs_3_ = f32[864,384]{1,0:T(8,128)S(1)} custom-call(bf16[3,192,1024]{2,1,0:T(8,128)(2,1)S(1)} %get-tuple-element.76.cols, bf16[1152,384]{1,0:T(8,128)(2,1)S(1)} %get-tuple-element.93.tall), custom_call_target="tpu_custom_call" | custom-call | tf_op jit(solution)/shard_map/pallas_call | solution.py:111
  21.7 0.6 collective-permute-done.6.refs_5_
  22.3 1.5 %shard_map.101 = (f32[224,384]{1,0:T(8,128)S(1)}, bf16[224,384]{1,0:T(8,128)(2,1)S(1)}, bf16[224,384]{1,0:T(8,128)(2,1)S(1)}, bf16[224,384]{1,0:T(8,128)(2,1)S(1)}) custom-call(bf16[1152,128]{1,0:T(8,128)(2,1)S(1)} %shard_map.97.refs_0_, bf16[1152,128]{1,0:T(8,128)(2,1)S(1)} %collective-permute-done.5.refs_1_, ...), custom_call_target="tpu_custom_call" | custom-call | bytes 5873664 | tf_op jit(solution)/shard_map/pallas_call | solution.py:111
  23.8 0.6 %collective-permute-start.10 = (bf16[224,384]{1,0:T(8,128)(2,1)S(1)}, bf16[224,384]{1,0:T(8,128)(2,1)S(1)}, u32[]{:S(2)}, u32[]{:S(2)}) collective-permute-start(bf16[224,384]{1,0:T(8,128)(2,1)S(1)} %get-tuple-element.91), channel_id=1, source_target_pairs={{0,8},{2,10},{4,12},{6,14},{8,0},{10,2},{12,4},{14,6},{16,24},{18,... | collective-permute-start | bytes 516104 | tf_op jit(solution)/shard_map/ppermute | solution.py:64
  24.4 2.4 %collective-permute-start.11 = (bf16[224,384]{1,0:T(8,128)(2,1)S(1)}, bf16[224,384]{1,0:T(8,128)(2,1)S(1)}, u32[]{:S(2)}, u32[]{:S(2)}) collective-permute-start(bf16[224,384]{1,0:T(8,128)(2,1)S(1)} %get-tuple-element.92), channel_id=1, source_target_pairs={{0,12},{2,14},{4,8},{6,10},{8,4},{10,6},{12,0},{14,2},{16,28},{18,... | collective-permute-start | bytes 516104 | tf_op jit(solution)/shard_map/ppermute | solution.py:64
  26.8 0.5 collective-permute-start.9
  27.3 2.9 %shard_map.102 = (f32[1024,192]{1,0:T(8,128)S(1)}, bf16[240,128]{1,0:T(8,128)(2,1)S(1)}) custom-call(bf16[1152,384]{1,0:T(8,128)(2,1)S(1)} %get-tuple-element.93.tall, bf16[9,384,384]{2,1,0:T(8,128)(2,1)S(1)} %bitcast.13), custom_call_target="tpu_custom_call" | custom-call | flops 1358954496 | bytes 4386816 | tf_op jit(solution)/shard_map/pallas_call | solution.py:111
  30.2 0.6 collective-permute-start.12
  30.8 2.5 %collective-permute-start.14 = (bf16[240,128]{1,0:T(8,128)(2,1)S(1)}, bf16[240,128]{1,0:T(8,128)(2,1)S(1)}, u32[]{:S(2)}, u32[]{:S(2)}) collective-permute-start(bf16[240,128]{1,0:T(8,128)(2,1)S(1)} %get-tuple-element.113.refs_0_), channel_id=1, source_target_pairs={{0,24},{2,26},{4,28},{6,30},{8,16},{10,18},{12,20},{14,22},{16,8},... | collective-permute-start | bytes 184328 | tf_op jit(solution)/shard_map/ppermute | solution.py:60
  33.3 1.2 %shard_map.104.place_ref = bf16[128,1920]{1,0:T(8,128)(2,1)S(1)} custom-call(s32[16,16]{1,0:T(8,128)S(1)} %pad_add_fusion.tables_in.refs_2_), custom_call_target="tpu_custom_call" | custom-call | bytes 492544 | tf_op jit(solution)/shard_map/pallas_call | solution.py:111
  34.5 1.3 %shard_map.103 = (bf16[160,192]{1,0:T(8,128)(2,1)S(1)}, bf16[576,128]{1,0:T(8,128)(2,1)S(1)}, bf16[576,128]{1,0:T(8,128)(2,1)S(1)}, bf16[624,128]{1,0:T(8,128)(2,1)S(1)}) custom-call(bf16[1152,128]{1,0:T(8,128)(2,1)S(1)} %shard_map.97.refs_0_, bf16[1152,128]{1,0:T(8,128)(2,1)S(1)} %collective-permute-done.5.refs_1_, ...), custom_call_target="tpu_custom_call" | custom-call | bytes 1500160 | tf_op jit(solution)/shard_map/pallas_call | solution.py:111
  35.8 0.6 collective-permute-done.9.refs_1_
  36.4 0.1 shard_map.105.held_ref
  36.5 1.2 %collective-permute-done.14.refs_2_ = bf16[240,128]{1,0:T(8,128)(2,1)S(1)} collective-permute-done((bf16[240,128]{1,0:T(8,128)(2,1)S(1)}, bf16[240,128]{1,0:T(8,128)(2,1)S(1)}, u32[]{:S(2)}, u32[]{:S(2)}) %collective-permute-start.14) | collective-permute-done | bytes 61472 | tf_op jit(solution)/shard_map/ppermute | solution.py:60
  37.7 1.6 %collective-permute-start.15 = (bf16[720,128]{1,0:T(8,128)(2,1)S(1)}, bf16[720,128]{1,0:T(8,128)(2,1)S(1)}, u32[]{:S(2)}, u32[]{:S(2)}) collective-permute-start(bf16[720,128]{1,0:T(8,128)(2,1)S(1)} %shard_map.106.refs_0_), channel_id=1, source_target_pairs={{0,4},{2,6},{4,0},{6,2},{8,12},{10,14},{12,8},{14,10},{16,20},{18,... | collective-permute-start | bytes 552968 | tf_op jit(solution)/shard_map/ppermute | solution.py:64
  39.3 0.1 collective-permute-start.13
  39.4 1.5 %collective-permute-start.23 = (bf16[624,128]{1,0:T(8,128)(2,1)S(1)}, bf16[624,128]{1,0:T(8,128)(2,1)S(1)}, u32[]{:S(2)}, u32[]{:S(2)}) collective-permute-start(bf16[624,128]{1,0:T(8,128)(2,1)S(1)} %get-tuple-element.123), channel_id=1, source_target_pairs={{0,1},{1,0},{2,3},{3,2},{4,5},{5,4},{6,7},{7,6},{8,9},{9,8},{10,11... | collective-permute-start | bytes 479240 | tf_op jit(solution)/shard_map/ppermute | solution.py:708
  40.9 0.5 collective-permute-start.21
  41.4 1.5 %collective-permute-start.22 = (bf16[576,128]{1,0:T(8,128)(2,1)S(1)}, bf16[576,128]{1,0:T(8,128)(2,1)S(1)}, u32[]{:S(2)}, u32[]{:S(2)}) collective-permute-start(bf16[576,128]{1,0:T(8,128)(2,1)S(1)} %get-tuple-element.122), channel_id=1, source_target_pairs={{0,1},{1,0},{2,3},{3,2},{4,5},{5,4},{6,7},{7,6},{8,9},{9,8},{10,11... | collective-permute-start | bytes 442376 | tf_op jit(solution)/shard_map/ppermute | solution.py:708
  42.9 4.7 %collective-permute-done.13.got_ref = bf16[224,384]{1,0:T(8,128)(2,1)S(1)} collective-permute-done((bf16[224,384]{1,0:T(8,128)(2,1)S(1)}, bf16[224,384]{1,0:T(8,128)(2,1)S(1)}, u32[]{:S(2)}, u32[]{:S(2)}) %collective-permute-start.13) | collective-permute-done | bytes 172064 | tf_op jit(solution)/shard_map/ppermute | solution.py:64
  47.6 0.6 collective-permute-start.16
  48.2 0.6 collective-permute-done.21.refs_0_
  48.8 2.4 %collective-permute-start.18 = (bf16[224,384]{1,0:T(8,128)(2,1)S(1)}, bf16[224,384]{1,0:T(8,128)(2,1)S(1)}, u32[]{:S(2)}, u32[]{:S(2)}) collective-permute-start(bf16[224,384]{1,0:T(8,128)(2,1)S(1)} %shard_map.107.refs_0_), channel_id=1, source_target_pairs={{0,12},{2,14},{4,8},{6,10},{8,4},{10,6},{12,0},{14,2},{16,28},{18,... | collective-permute-start | bytes 516104 | tf_op jit(solution)/shard_map/ppermute | solution.py:64
  51.2 0.5 collective-permute-start.20
  51.7 3.9 %shard_map.109 = bf16[1024,192]{1,0:T(8,128)(2,1)} custom-call(bf16[32,32,192]{2,1,0:T(8,128)(2,1)S(1)} %get-tuple-element.73.field_ref.refs_3_, bf16[160,192]{1,0:T(8,128)(2,1)S(1)} %get-tuple-element.120.halos_ref, bf16[9,384,384]{2,1,0:T(8,128)(2,1)S(1)} %bitcast.14, bf16[576,128]{1,0:T(8,128)(2,1)S(1)} %collective-permute-done.21.refs_0_, ...), custom_call_target="tpu_custom_call" | custom-call | flops 2717908992 | bytes 3956736 | tf_op jit(solution)/shard_map/pallas_call | solution.py:111
  55.7 1.3 %shard_map.108 = bf16[1024,192]{1,0:T(8,128)(2,1)} custom-call(bf16[128,1920]{1,0:T(8,128)(2,1)S(1)} %shard_map.104.place_ref, f32[1024,192]{1,0:T(8,128)S(1)} %get-tuple-element.117.inner_ref, bf16[720,128]{1,0:T(8,128)(2,1)S(1)} %shard_map.106.refs_0_, bf16[720,128]{1,0:T(8,128)(2,1)S(1)} %collective-permute-done.15.refs_1_, ...), custom_call_target="tpu_custom_call" | custom-call | bytes 2408448 | tf_op jit(solution)/shard_map/pallas_call | solution.py:111
  57.0 1.5 %collective-permute-done.18.refs_3_ = bf16[224,384]{1,0:T(8,128)(2,1)S(1)} collective-permute-done((bf16[224,384]{1,0:T(8,128)(2,1)S(1)}, bf16[224,384]{1,0:T(8,128)(2,1)S(1)}, u32[]{:S(2)}, u32[]{:S(2)}) %collective-permute-start.18) | collective-permute-done | bytes 172064 | tf_op jit(solution)/shard_map/ppermute | solution.py:64
  58.4 0.5 collective-permute-start.26
  59.0 1.4 %shard_map.110.refs_0_ = f32[1728,384]{1,0:T(8,128)} custom-call(bf16[224,384]{1,0:T(8,128)(2,1)S(1)} %shard_map.107.refs_0_, bf16[224,384]{1,0:T(8,128)(2,1)S(1)} %collective-permute-done.16.refs_1_, bf16[224,384]{1,0:T(8,128)(2,1)S(1)} %collective-permute-done.17.refs_2_, bf16[224,384]{1,0:T(8,128)(2,1)S(1)} %collective-permute-done.18.refs_3_, ...), custom_call_target="tpu_custom_call" | custom-call | tf_op jit(solution)/shard_map/pallas_call | solution.py:455
  60.4 1.1 %shard_map.111 = f32[1728,384]{1,0:T(8,128)} custom-call(f32[1728,384]{1,0:T(8,128)} %shard_map.110.refs_0_, bf16[224,384]{1,0:T(8,128)(2,1)S(1)} %collective-permute-done.25.refs_1_, bf16[224,384]{1,0:T(8,128)(2,1)S(1)} %collective-permute-done.26.refs_2_, bf16[224,384]{1,0:T(8,128)(2,1)S(1)} %collective-permute-done.27.refs_3_), custom_call_target="tpu_custom_call", output_to_operand_aliasing={{}: (0, {})} | custom-call | tf_op jit(solution)/shard_map/pallas_call | solution.py:455
  (33 shorter events, 0.2 us)
Async XLA Ops:
  0.6 16.4 %collective-permute-start.4 = (bf16[1024,192]{1,0:T(8,128)(2,1)}, bf16[1024,192]{1,0:T(8,128)(2,1)S(1)}, u32[]{:S(2)}, u32[]{:S(2)}) collective-permute-start(bf16[1024,192]{1,0:T(8,128)(2,1)} %bitcast.11), channel_id=1, source_target_pairs={{0,1},{1,0},{2,3},{3,2},{4,5},{5,4},{6,7},{7,6},{8,9},{9,8},{10,11... | collective-permute-start | bytes 1179656 | tf_op jit(solution)/shard_map/ppermute | solution.py:613
  3.6 1.0 %copy-start = (bf16[1,32,32,192]{3,2,1,0:T(8,128)(2,1)S(1)}, bf16[1,32,32,192]{3,2,1,0:T(8,128)(2,1)}, u32[]{:S(2)}) copy-start(bf16[1,32,32,192]{3,2,1,0:T(8,128)(2,1)} %param.7) | copy-start | bytes 1179652
  4.8 5.6 %collective-permute-start.1 = (bf16[192,128]{1,0:T(8,128)(2,1)S(1)}, bf16[192,128]{1,0:T(8,128)(2,1)S(1)}, u32[]{:S(2)}, u32[]{:S(2)}) collective-permute-start(bf16[192,128]{1,0:T(8,128)(2,1)S(1)} %get-tuple-element.68.refs_0_), channel_id=1, source_target_pairs={{0,8},{2,10},{4,12},{6,14},{8,0},{10,2},{12,4},{14,6},{16,24},{18,... | collective-permute-start | bytes 147464 | tf_op jit(solution)/shard_map/ppermute | solution.py:60
  6.4 5.9 %collective-permute-start.2 = (bf16[192,128]{1,0:T(8,128)(2,1)S(1)}, bf16[192,128]{1,0:T(8,128)(2,1)S(1)}, u32[]{:S(2)}, u32[]{:S(2)}) collective-permute-start(bf16[192,128]{1,0:T(8,128)(2,1)S(1)} %get-tuple-element.68.refs_0_), channel_id=1, source_target_pairs={{0,24},{2,26},{4,28},{6,30},{8,16},{10,18},{12,20},{14,22},{16,8},... | collective-permute-start | bytes 147464 | tf_op jit(solution)/shard_map/ppermute | solution.py:60
  8.9 7.9 %collective-permute-start = (bf16[192,128]{1,0:T(8,128)(2,1)S(1)}, bf16[192,128]{1,0:T(8,128)(2,1)S(1)}, u32[]{:S(2)}, u32[]{:S(2)}) collective-permute-start(bf16[192,128]{1,0:T(8,128)(2,1)S(1)} %get-tuple-element.68.refs_0_), channel_id=1, source_target_pairs={{0,4},{2,6},{4,0},{6,2},{8,12},{10,14},{12,8},{14,10},{16,20},{18,... | collective-permute-start | bytes 147464 | tf_op jit(solution)/shard_map/ppermute | solution.py:64
  12.3 4.7 %collective-permute-start.3 = (bf16[384,128]{1,0:T(8,128)(2,1)S(1)}, bf16[384,128]{1,0:T(8,128)(2,1)S(1)}, u32[]{:S(2)}, u32[]{:S(2)}) collective-permute-start(bf16[384,128]{1,0:T(8,128)(2,1)S(1)} %shard_map.95), channel_id=1, source_target_pairs={{0,4},{2,6},{4,0},{6,2},{8,12},{10,14},{12,8},{14,10},{16,20},{18,... | collective-permute-start | bytes 294920 | tf_op jit(solution)/shard_map/ppermute | solution.py:64
  14.7 1.0 %copy-start.1 = (bf16[1,32,32,192]{3,2,1,0:T(8,128)(2,1)S(1)}, bf16[1,32,32,192]{3,2,1,0:T(8,128)(2,1)}, u32[]{:S(2)}) copy-start(bf16[1,32,32,192]{3,2,1,0:T(8,128)(2,1)} %param.9) | copy-start | bytes 1179652
  18.6 3.7 %collective-permute-start.7 = (f32[576,384]{1,0:T(8,128)S(1)}, f32[576,384]{1,0:T(8,128)S(1)}, u32[]{:S(2)}, u32[]{:S(2)}) collective-permute-start(f32[576,384]{1,0:T(8,128)S(1)} %get-tuple-element.84), channel_id=1, source_target_pairs={{0,2},{2,0},{4,6},{6,4},{8,10},{10,8},{12,14},{14,12},{16,18},{18,... | collective-permute-start | bytes 2654216 | tf_op jit(solution)/shard_map/ppermute | solution.py:64
  19.3 3.0 %collective-permute-start.8 = (f32[288,384]{1,0:T(8,128)S(1)}, f32[288,384]{1,0:T(8,128)S(1)}, u32[]{:S(2)}, u32[]{:S(2)}) collective-permute-start(f32[288,384]{1,0:T(8,128)S(1)} %shard_map.99), channel_id=1, source_target_pairs={{0,2},{2,0},{4,6},{6,4},{8,10},{10,8},{12,14},{14,12},{16,18},{18,... | collective-permute-start | bytes 1327112 | tf_op jit(solution)/shard_map/ppermute | solution.py:64
  19.8 2.4 %collective-permute-start.5 = (bf16[1152,128]{1,0:T(8,128)(2,1)S(1)}, bf16[1152,128]{1,0:T(8,128)(2,1)S(1)}, u32[]{:S(2)}, u32[]{:S(2)}) collective-permute-start(bf16[1152,128]{1,0:T(8,128)(2,1)S(1)} %shard_map.97.refs_0_), channel_id=1, source_target_pairs={{0,2},{2,0},{4,6},{6,4},{8,10},{10,8},{12,14},{14,12},{16,18},{18,... | collective-permute-start | bytes 884744 | tf_op jit(solution)/shard_map/ppermute | solution.py:64
  19.9 2.3 %collective-permute-start.6 = (bf16[128,384]{1,0:T(8,128)(2,1)S(1)}, bf16[128,384]{1,0:T(8,128)(2,1)S(1)}, u32[]{:S(2)}, u32[]{:S(2)}) collective-permute-start(bf16[128,384]{1,0:T(8,128)(2,1)S(1)} %get-tuple-element.79.refs_4_), channel_id=1, source_target_pairs={{0,2},{2,0},{4,6},{6,4},{8,10},{10,8},{12,14},{14,12},{16,18},{18,... | collective-permute-start | bytes 294920 | tf_op jit(solution)/shard_map/ppermute | solution.py:64
  21.7 5.7 %copy-start.2 = (bf16[3,3,384,384]{3,2,1,0:T(8,128)(2,1)S(1)}, bf16[3,3,384,384]{3,2,1,0:T(8,128)(2,1)}, u32[]{:S(2)}) copy-start(bf16[3,3,384,384]{3,2,1,0:T(8,128)(2,1)} %param.8) | copy-start | bytes 7962628
  23.8 12.0 %collective-permute-start.10 = (bf16[224,384]{1,0:T(8,128)(2,1)S(1)}, bf16[224,384]{1,0:T(8,128)(2,1)S(1)}, u32[]{:S(2)}, u32[]{:S(2)}) collective-permute-start(bf16[224,384]{1,0:T(8,128)(2,1)S(1)} %get-tuple-element.91), channel_id=1, source_target_pairs={{0,8},{2,10},{4,12},{6,14},{8,0},{10,2},{12,4},{14,6},{16,24},{18,... | collective-permute-start | bytes 516104 | tf_op jit(solution)/shard_map/ppermute | solution.py:64
  24.4 11.4 %collective-permute-start.11 = (bf16[224,384]{1,0:T(8,128)(2,1)S(1)}, bf16[224,384]{1,0:T(8,128)(2,1)S(1)}, u32[]{:S(2)}, u32[]{:S(2)}) collective-permute-start(bf16[224,384]{1,0:T(8,128)(2,1)S(1)} %get-tuple-element.92), channel_id=1, source_target_pairs={{0,12},{2,14},{4,8},{6,10},{8,4},{10,6},{12,0},{14,2},{16,28},{18,... | collective-permute-start | bytes 516104 | tf_op jit(solution)/shard_map/ppermute | solution.py:64
  26.8 9.6 %collective-permute-start.9 = (bf16[224,384]{1,0:T(8,128)(2,1)S(1)}, bf16[224,384]{1,0:T(8,128)(2,1)S(1)}, u32[]{:S(2)}, u32[]{:S(2)}) collective-permute-start(bf16[224,384]{1,0:T(8,128)(2,1)S(1)} %get-tuple-element.90), channel_id=1, source_target_pairs={{0,4},{2,6},{4,0},{6,2},{8,12},{10,14},{12,8},{14,10},{16,20},{18,... | collective-permute-start | bytes 516104 | tf_op jit(solution)/shard_map/ppermute | solution.py:64
  30.2 5.5 %collective-permute-start.12 = (bf16[240,128]{1,0:T(8,128)(2,1)S(1)}, bf16[240,128]{1,0:T(8,128)(2,1)S(1)}, u32[]{:S(2)}, u32[]{:S(2)}) collective-permute-start(bf16[240,128]{1,0:T(8,128)(2,1)S(1)} %get-tuple-element.113.refs_0_), channel_id=1, source_target_pairs={{0,8},{2,10},{4,12},{6,14},{8,0},{10,2},{12,4},{14,6},{16,24},{18,... | collective-permute-start | bytes 184328 | tf_op jit(solution)/shard_map/ppermute | solution.py:60
  30.8 6.9 %collective-permute-start.14 = (bf16[240,128]{1,0:T(8,128)(2,1)S(1)}, bf16[240,128]{1,0:T(8,128)(2,1)S(1)}, u32[]{:S(2)}, u32[]{:S(2)}) collective-permute-start(bf16[240,128]{1,0:T(8,128)(2,1)S(1)} %get-tuple-element.113.refs_0_), channel_id=1, source_target_pairs={{0,24},{2,26},{4,28},{6,30},{8,16},{10,18},{12,20},{14,22},{16,8},... | collective-permute-start | bytes 184328 | tf_op jit(solution)/shard_map/ppermute | solution.py:60
  37.7 9.9 %collective-permute-start.15 = (bf16[720,128]{1,0:T(8,128)(2,1)S(1)}, bf16[720,128]{1,0:T(8,128)(2,1)S(1)}, u32[]{:S(2)}, u32[]{:S(2)}) collective-permute-start(bf16[720,128]{1,0:T(8,128)(2,1)S(1)} %shard_map.106.refs_0_), channel_id=1, source_target_pairs={{0,4},{2,6},{4,0},{6,2},{8,12},{10,14},{12,8},{14,10},{16,20},{18,... | collective-permute-start | bytes 552968 | tf_op jit(solution)/shard_map/ppermute | solution.py:64
  39.3 8.3 %collective-permute-start.13 = (bf16[224,384]{1,0:T(8,128)(2,1)S(1)}, bf16[224,384]{1,0:T(8,128)(2,1)S(1)}, u32[]{:S(2)}, u32[]{:S(2)}) collective-permute-start(bf16[224,384]{1,0:T(8,128)(2,1)S(1)} %shard_map.105.held_ref), channel_id=1, source_target_pairs={{0,16},{2,18},{4,20},{6,22},{8,24},{10,26},{12,28},{14,30},{16,0},... | collective-permute-start | bytes 516104 | tf_op jit(solution)/shard_map/ppermute | solution.py:64
  39.4 11.8 %collective-permute-start.23 = (bf16[624,128]{1,0:T(8,128)(2,1)S(1)}, bf16[624,128]{1,0:T(8,128)(2,1)S(1)}, u32[]{:S(2)}, u32[]{:S(2)}) collective-permute-start(bf16[624,128]{1,0:T(8,128)(2,1)S(1)} %get-tuple-element.123), channel_id=1, source_target_pairs={{0,1},{1,0},{2,3},{3,2},{4,5},{5,4},{6,7},{7,6},{8,9},{9,8},{10,11... | collective-permute-start | bytes 479240 | tf_op jit(solution)/shard_map/ppermute | solution.py:708
  40.9 7.9 %collective-permute-start.21 = (bf16[576,128]{1,0:T(8,128)(2,1)S(1)}, bf16[576,128]{1,0:T(8,128)(2,1)S(1)}, u32[]{:S(2)}, u32[]{:S(2)}) collective-permute-start(bf16[576,128]{1,0:T(8,128)(2,1)S(1)} %get-tuple-element.121), channel_id=1, source_target_pairs={{0,1},{1,0},{2,3},{3,2},{4,5},{5,4},{6,7},{7,6},{8,9},{9,8},{10,11... | collective-permute-start | bytes 442376 | tf_op jit(solution)/shard_map/ppermute | solution.py:708
  41.4 9.8 %collective-permute-start.22 = (bf16[576,128]{1,0:T(8,128)(2,1)S(1)}, bf16[576,128]{1,0:T(8,128)(2,1)S(1)}, u32[]{:S(2)}, u32[]{:S(2)}) collective-permute-start(bf16[576,128]{1,0:T(8,128)(2,1)S(1)} %get-tuple-element.122), channel_id=1, source_target_pairs={{0,1},{1,0},{2,3},{3,2},{4,5},{5,4},{6,7},{7,6},{8,9},{9,8},{10,11... | collective-permute-start | bytes 442376 | tf_op jit(solution)/shard_map/ppermute | solution.py:708
  47.6 9.4 %collective-permute-start.16 = (bf16[224,384]{1,0:T(8,128)(2,1)S(1)}, bf16[224,384]{1,0:T(8,128)(2,1)S(1)}, u32[]{:S(2)}, u32[]{:S(2)}) collective-permute-start(bf16[224,384]{1,0:T(8,128)(2,1)S(1)} %shard_map.107.refs_0_), channel_id=1, source_target_pairs={{0,4},{2,6},{4,0},{6,2},{8,12},{10,14},{12,8},{14,10},{16,20},{18,... | collective-permute-start | bytes 516104 | tf_op jit(solution)/shard_map/ppermute | solution.py:64
  48.2 8.8 %collective-permute-start.17 = (bf16[224,384]{1,0:T(8,128)(2,1)S(1)}, bf16[224,384]{1,0:T(8,128)(2,1)S(1)}, u32[]{:S(2)}, u32[]{:S(2)}) collective-permute-start(bf16[224,384]{1,0:T(8,128)(2,1)S(1)} %shard_map.107.refs_0_), channel_id=1, source_target_pairs={{0,8},{2,10},{4,12},{6,14},{8,0},{10,2},{12,4},{14,6},{16,24},{18,... | collective-permute-start | bytes 516104 | tf_op jit(solution)/shard_map/ppermute | solution.py:64
  48.8 9.7 %collective-permute-start.18 = (bf16[224,384]{1,0:T(8,128)(2,1)S(1)}, bf16[224,384]{1,0:T(8,128)(2,1)S(1)}, u32[]{:S(2)}, u32[]{:S(2)}) collective-permute-start(bf16[224,384]{1,0:T(8,128)(2,1)S(1)} %shard_map.107.refs_0_), channel_id=1, source_target_pairs={{0,12},{2,14},{4,8},{6,10},{8,4},{10,6},{12,0},{14,2},{16,28},{18,... | collective-permute-start | bytes 516104 | tf_op jit(solution)/shard_map/ppermute | solution.py:64
  51.2 4.4 %collective-permute-start.19 = (bf16[720,128]{1,0:T(8,128)(2,1)S(1)}, bf16[720,128]{1,0:T(8,128)(2,1)S(1)}, u32[]{:S(2)}, u32[]{:S(2)}) collective-permute-start(bf16[720,128]{1,0:T(8,128)(2,1)S(1)} %shard_map.106.refs_0_), channel_id=1, source_target_pairs={{0,2},{2,0},{4,6},{6,4},{8,10},{10,8},{12,14},{14,12},{16,18},{18,... | collective-permute-start | bytes 552968 | tf_op jit(solution)/shard_map/ppermute | solution.py:64
  51.2 4.5 %collective-permute-start.20 = (bf16[720,128]{1,0:T(8,128)(2,1)S(1)}, bf16[720,128]{1,0:T(8,128)(2,1)S(1)}, u32[]{:S(2)}, u32[]{:S(2)}) collective-permute-start(bf16[720,128]{1,0:T(8,128)(2,1)S(1)} %collective-permute-done.15.refs_1_), channel_id=1, source_target_pairs={{0,2},{2,0},{4,6},{6,4},{8,10},{10,8},{12,14},{14,12},{16,18},{18,... | collective-permute-start | bytes 552968 | tf_op jit(solution)/shard_map/ppermute | solution.py:64
  55.6 3.4 %collective-permute-start.24 = (bf16[224,384]{1,0:T(8,128)(2,1)S(1)}, bf16[224,384]{1,0:T(8,128)(2,1)S(1)}, u32[]{:S(2)}, u32[]{:S(2)}) collective-permute-start(bf16[224,384]{1,0:T(8,128)(2,1)S(1)} %shard_map.107.refs_0_), channel_id=1, source_target_pairs={{0,2},{2,0},{4,6},{6,4},{8,10},{10,8},{12,14},{14,12},{16,18},{18,... | collective-permute-start | bytes 516104 | tf_op jit(solution)/shard_map/ppermute | solution.py:64
  58.4 1.9 %collective-permute-start.25 = (bf16[224,384]{1,0:T(8,128)(2,1)S(1)}, bf16[224,384]{1,0:T(8,128)(2,1)S(1)}, u32[]{:S(2)}, u32[]{:S(2)}) collective-permute-start(bf16[224,384]{1,0:T(8,128)(2,1)S(1)} %collective-permute-done.16.refs_1_), channel_id=1, source_target_pairs={{0,2},{2,0},{4,6},{6,4},{8,10},{10,8},{12,14},{14,12},{16,18},{18,... | collective-permute-start | bytes 516104 | tf_op jit(solution)/shard_map/ppermute | solution.py:64
  58.4 1.9 %collective-permute-start.26 = (bf16[224,384]{1,0:T(8,128)(2,1)S(1)}, bf16[224,384]{1,0:T(8,128)(2,1)S(1)}, u32[]{:S(2)}, u32[]{:S(2)}) collective-permute-start(bf16[224,384]{1,0:T(8,128)(2,1)S(1)} %collective-permute-done.17.refs_2_), channel_id=1, source_target_pairs={{0,2},{2,0},{4,6},{6,4},{8,10},{10,8},{12,14},{14,12},{16,18},{18,... | collective-permute-start | bytes 516104 | tf_op jit(solution)/shard_map/ppermute | solution.py:64
  59.0 1.4 %collective-permute-start.27 = (bf16[224,384]{1,0:T(8,128)(2,1)S(1)}, bf16[224,384]{1,0:T(8,128)(2,1)S(1)}, u32[]{:S(2)}, u32[]{:S(2)}) collective-permute-start(bf16[224,384]{1,0:T(8,128)(2,1)S(1)} %collective-permute-done.18.refs_3_), channel_id=1, source_target_pairs={{0,2},{2,0},{4,6},{6,4},{8,10},{10,8},{12,14},{14,12},{16,18},{18,... | collective-permute-start | bytes 516104 | tf_op jit(solution)/shard_map/ppermute | solution.py:64

commit v17 on v15

--- a/solution.py
+++ b/solution.py
@@ -122,7 +122,11 @@
 def packed_shape(rows, part):
     if part % 128 != 64:
         return (rows, part)
-    return (rows * (part // 128) + rows // 2, 128)
+    return (rows * (part // 128) + upper_half(rows), 128)
+
+
+def upper_half(rows):
+    return -(-rows // 32) * 16
 
 
 def pack(value, out_ref, first=0):
@@ -134,7 +138,11 @@
         out_ref[first + i * rows : first + (i + 1) * rows, :] = value[:, i * 128 : (i + 1) * 128]
     rest = value[:, part - 64 :]
     at = first + rows * (part // 128)
-    out_ref[at : at + rows // 2, :] = jnp.concatenate([rest[: rows // 2], rest[rows // 2 :]], axis=1)
+    cut = upper_half(rows)
+    out_ref[at : at + cut, 0:64] = rest[:cut]
+    out_ref[at : at + rows - cut, 64:128] = rest[cut:]
+    if rows < 2 * cut:
+        out_ref[at + rows - cut : at + cut, 64:128] = jnp.zeros((2 * cut - rows, 64), out_ref.dtype)
 
 
 def unpack(ref, out_ref, first, row, rows, part):
@@ -144,9 +152,9 @@
     for i in range(part // 128):
         out_ref[row : row + rows, i * 128 : (i + 1) * 128] = ref[first + i * rows : first + (i + 1) * rows, :]
     at = first + rows * (part // 128)
-    rest = ref[at : at + rows // 2, :]
-    out_ref[row : row + rows // 2, part - 64 :] = rest[:, :64]
-    out_ref[row + rows // 2 : row + rows, part - 64 :] = rest[:, 64:]
+    cut = upper_half(rows)
+    out_ref[row : row + cut, part - 64 :] = ref[at : at + cut, :][:, :64]
+    out_ref[row + cut : row + rows, part - 64 :] = ref[at : at + rows - cut, :][:, 64:]
 
 
 def sides_kernel(side, field_ref, sides_ref, copy_ref):
@@ -704,8 +712,12 @@
     def start_aside(send, aside):
         here = aside[0]
         send, here[0], packet = lax.optimization_barrier((send, here[0], aside[1]))
-        (here,) = call(join_kernel, [vmem((3 * pieces.shape[0], pieces.shape[1]), half_bytes)], here)
-        return send, here, by_mask(here, 2, count), [lax.ppermute(v, "ch", others) for v in packet]
+        lines, lanes = pieces.shape
+        (swapped,) = call(join_kernel, [vmem((2 * lines, lanes), half_bytes)], here[1:])
+        parts = [by_mask(v, 2, count) for v in (here[0], swapped)]
+        (here,) = call(join_kernel, [vmem((3 * lines, lanes), half_bytes)], [here[0], swapped])
+        (beside,) = call(join_kernel, [vmem((3 * lines, lanes), half_bytes)], parts)
+        return send, here, beside, [lax.ppermute(v, "ch", others) for v in packet]
 
     for index, bits in enumerate(rs_stages):
         masks = group_masks(bits)

time: 59.6 us -> 60.9 us (1.022)
  starting transfers between devices: 28.1 us -> 30.3 us
  waiting for transfers between devices: 8.37 us -> 7.58 us
    ppermute x20 -> x21, starting transfers between devices: 14.4 us -> 16.6 us  [by_mask(): return lax.ppermute(value, 'tile', [(i, i ^ mask) for i in range(count)])]
    ppermute x3, waiting for transfers between devices: 1.44 us -> 0.01 us  [start_aside(): return (send, here, beside, [lax.ppermute(v, 'ch', others) for v in packet])]
    ppermute x20 -> x21, waiting for transfers between devices: 5.03 us -> 5.67 us  [by_mask(): return lax.ppermute(value, 'tile', [(i, i ^ mask) for i in range(count)])]
    pallas_call x16 -> x18, Pallas kernels: 16.8 us -> 16.8 us  [call(): pl.pallas_call(kernel, out_shape=tuple(outs), in_specs=in_specs, out_spec...]
  transfers between devices with their start and end apart: 28 -> 29, of which waited for: 9 -> 6; matrix products, arithmetic and copies ran while one was open for 1% -> 1% of each run, Pallas kernels for 25% -> 25%
where the time goes in v17:
time: 60.9 us; the launch traced here: 60.7 us
  starting transfers between devices  30.3 us (50%)
  Pallas kernels  19.2 us (32%)
  waiting for transfers between devices  7.58 us (12%)
  local copies, waits for them, and re-layouts  2.09 us (3%)
  between operations  0.86 us (1%)
  other arithmetic  0.74 us (1%)
    pallas_call x18, Pallas kernels, call(): pl.pallas_call(kernel, out_shape=tuple(outs), in_specs=in_specs, out_spec...  16.8 us
    ppermute x21, starting transfers between devices, by_mask(): return lax.ppermute(value, 'tile', [(i, i ^ mask) for i in range(count)])  16.6 us
    ppermute x4, starting transfers between devices, by_swap(): return lax.ppermute(value, 'tile', pairs)  7.18 us
    ppermute x21, waiting for transfers between devices, by_mask(): return lax.ppermute(value, 'tile', [(i, i ^ mask) for i in range(count)])  5.67 us
    ppermute x3, starting transfers between devices, start_aside(): return (send, here, beside, [lax.ppermute(v, 'ch', others) for v in packet])  3.51 us
    ppermute x1, starting transfers between devices, body(): cot_other = lax.ppermute(cot_own, 'ch', others)  3 us
    pallas_call x2, Pallas kernels, unfold(): pl.pallas_call(functools.partial(unfold_kernel, whole.shape[0] // 2, chun...  2.41 us
    unnamed x6, local copies, waits for them, and re-layouts  2.09 us
  transfers between devices with their start and end apart: 29, of which 6 were waited for; matrix products, arithmetic and copies ran while one was open for 1% of the time, Pallas kernels for 25%

profile of v17, /device:TPU:0, one launch (start us, length us, event | category | flops | bytes accessed | tf_op | source)
XLA Modules:
  0.0 60.7 jit_solution(6590135794892548261)
XLA Ops:
  0.6 3.0 %collective-permute-start.4 = (bf16[1024,192]{1,0:T(8,128)(2,1)}, bf16[1024,192]{1,0:T(8,128)(2,1)S(1)}, u32[]{:S(2)}, u32[]{:S(2)}) collective-permute-start(bf16[1024,192]{1,0:T(8,128)(2,1)} %bitcast.11), channel_id=1, source_target_pairs={{0,1},{1,0},{2,3},{3,2},{4,5},{5,4},{6,7},{7,6},{8,9},{9,8},{10,11... | collective-permute-start | bytes 1179656 | tf_op jit(solution)/shard_map/ppermute | solution.py:621
  3.6 1.0 %copy-done = bf16[1,32,32,192]{3,2,1,0:T(8,128)(2,1)S(1)} copy-done((bf16[1,32,32,192]{3,2,1,0:T(8,128)(2,1)S(1)}, bf16[1,32,32,192]{3,2,1,0:T(8,128)(2,1)}, u32[]{:S(2)}) %copy-start) | copy-done | bytes 393240
  4.7 0.1 shard_map.94
  4.8 1.6 %collective-permute-start.1 = (bf16[192,128]{1,0:T(8,128)(2,1)S(1)}, bf16[192,128]{1,0:T(8,128)(2,1)S(1)}, u32[]{:S(2)}, u32[]{:S(2)}) collective-permute-start(bf16[192,128]{1,0:T(8,128)(2,1)S(1)} %get-tuple-element.68.refs_0_), channel_id=1, source_target_pairs={{0,8},{2,10},{4,12},{6,14},{8,0},{10,2},{12,4},{14,6},{16,24},{18,... | collective-permute-start | bytes 147464 | tf_op jit(solution)/shard_map/ppermute | solution.py:60
  6.4 2.5 %collective-permute-start.2 = (bf16[192,128]{1,0:T(8,128)(2,1)S(1)}, bf16[192,128]{1,0:T(8,128)(2,1)S(1)}, u32[]{:S(2)}, u32[]{:S(2)}) collective-permute-start(bf16[192,128]{1,0:T(8,128)(2,1)S(1)} %get-tuple-element.68.refs_0_), channel_id=1, source_target_pairs={{0,24},{2,26},{4,28},{6,30},{8,16},{10,18},{12,20},{14,22},{16,8},... | collective-permute-start | bytes 147464 | tf_op jit(solution)/shard_map/ppermute | solution.py:60
  8.9 1.5 %collective-permute-start = (bf16[192,128]{1,0:T(8,128)(2,1)S(1)}, bf16[192,128]{1,0:T(8,128)(2,1)S(1)}, u32[]{:S(2)}, u32[]{:S(2)}) collective-permute-start(bf16[192,128]{1,0:T(8,128)(2,1)S(1)} %get-tuple-element.68.refs_0_), channel_id=1, source_target_pairs={{0,4},{2,6},{4,0},{6,2},{8,12},{10,14},{12,8},{14,10},{16,20},{18,... | collective-permute-start | bytes 147464 | tf_op jit(solution)/shard_map/ppermute | solution.py:64
  10.4 1.9 %collective-permute-done.2.refs_1_.refs_3_ = bf16[192,128]{1,0:T(8,128)(2,1)S(1)} collective-permute-done((bf16[192,128]{1,0:T(8,128)(2,1)S(1)}, bf16[192,128]{1,0:T(8,128)(2,1)S(1)}, u32[]{:S(2)}, u32[]{:S(2)}) %collective-permute-start.2) | collective-permute-done | bytes 49184 | tf_op jit(solution)/shard_map/ppermute | solution.py:60
  12.3 1.6 %collective-permute-start.3 = (bf16[384,128]{1,0:T(8,128)(2,1)S(1)}, bf16[384,128]{1,0:T(8,128)(2,1)S(1)}, u32[]{:S(2)}, u32[]{:S(2)}) collective-permute-start(bf16[384,128]{1,0:T(8,128)(2,1)S(1)} %shard_map.95), channel_id=1, source_target_pairs={{0,4},{2,6},{4,0},{6,2},{8,12},{10,14},{12,8},{14,10},{16,20},{18,... | collective-permute-start | bytes 294920 | tf_op jit(solution)/shard_map/ppermute | solution.py:64
  13.9 0.7 %pad_add_fusion.tables_in.refs_2_ = s32[16,16]{1,0:T(8,128)S(1)} fusion(s32[4,16]{1,0:T(4,128)} %bitcast.17, s32[4,16]{1,0:T(4,128)} %bitcast.18, s32[4,16]{1,0:T(4,128)} %bitcast.19, s32[4,16]{1,0:T(4,128)} %bitcast.20), kind=kLoop, calls=%fused_computation | loop fusion | flops 768 | bytes 2048 | tf_op jit(solution)/shard_map/concatenate | solution.py:629
  14.7 1.0 %copy-done.1 = bf16[1,32,32,192]{3,2,1,0:T(8,128)(2,1)S(1)} copy-done((bf16[1,32,32,192]{3,2,1,0:T(8,128)(2,1)S(1)}, bf16[1,32,32,192]{3,2,1,0:T(8,128)(2,1)}, u32[]{:S(2)}) %copy-start.1) | copy-done | bytes 393240
  15.7 1.1 %shard_map.96 = (bf16[512,1536]{1,0:T(8,128)(2,1)S(1)}, bf16[1024,192]{1,0:T(8,128)(2,1)S(1)}) custom-call(s32[16,16]{1,0:T(8,128)S(1)} %pad_add_fusion.tables_in.refs_2_, bf16[1024,192]{1,0:T(8,128)(2,1)S(1)} %bitcast.12), custom_call_target="tpu_custom_call" | custom-call | bytes 2360320 | tf_op jit(solution)/shard_map/pallas_call | solution.py:111
  16.8 0.2 collective-permute-done.3.refs_4_
  17.0 1.5 %shard_map.98 = (f32[576,384]{1,0:T(8,128)S(1)}, bf16[1152,384]{1,0:T(8,128)(2,1)S(1)}, bf16[128,384]{1,0:T(8,128)(2,1)S(1)}, bf16[3,192,1024]{2,1,0:T(8,128)(2,1)S(1)}) custom-call(bf16[32,32,192]{2,1,0:T(8,128)(2,1)S(1)} %get-tuple-element.73.field_ref.refs_3_, bf16[1024,192]{1,0:T(8,128)(2,1)S(1)} %get-tuple-element.74.own_ref, ...), custom_call_target="tpu_custom_call" | custom-call | flops 339738624 | bytes 4227072 | tf_op jit(solution)/shard_map/pallas_call | solution.py:111
  18.6 0.1 collective-permute-start.7
  18.6 0.6 %shard_map.99 = f32[288,384]{1,0:T(8,128)S(1)} custom-call(bf16[3,192,1024]{2,1,0:T(8,128)(2,1)S(1)} %get-tuple-element.76.cols, bf16[1152,384]{1,0:T(8,128)(2,1)S(1)} %get-tuple-element.93.tall), custom_call_target="tpu_custom_call" | custom-call | flops 1358954496 | bytes 2506752 | tf_op jit(solution)/shard_map/pallas_call | solution.py:111
  19.3 0.5 collective-permute-start.8
  19.8 0.1 collective-permute-start.5
  19.9 0.5 collective-permute-start.6
  20.4 1.2 %shard_map.100.refs_3_ = f32[864,384]{1,0:T(8,128)S(1)} custom-call(bf16[3,192,1024]{2,1,0:T(8,128)(2,1)S(1)} %get-tuple-element.76.cols, bf16[1152,384]{1,0:T(8,128)(2,1)S(1)} %get-tuple-element.93.tall), custom_call_target="tpu_custom_call" | custom-call | tf_op jit(solution)/shard_map/pallas_call | solution.py:111
  21.7 0.6 collective-permute-done.6.refs_5_
  22.3 1.5 %shard_map.101 = (f32[224,384]{1,0:T(8,128)S(1)}, bf16[224,384]{1,0:T(8,128)(2,1)S(1)}, bf16[224,384]{1,0:T(8,128)(2,1)S(1)}, bf16[224,384]{1,0:T(8,128)(2,1)S(1)}) custom-call(bf16[1152,128]{1,0:T(8,128)(2,1)S(1)} %shard_map.97.refs_0_, bf16[1152,128]{1,0:T(8,128)(2,1)S(1)} %collective-permute-done.5.refs_1_, ...), custom_call_target="tpu_custom_call" | custom-call | bytes 5873664 | tf_op jit(solution)/shard_map/pallas_call | solution.py:111
  23.8 0.6 %collective-permute-start.10 = (bf16[224,384]{1,0:T(8,128)(2,1)S(1)}, bf16[224,384]{1,0:T(8,128)(2,1)S(1)}, u32[]{:S(2)}, u32[]{:S(2)}) collective-permute-start(bf16[224,384]{1,0:T(8,128)(2,1)S(1)} %get-tuple-element.91), channel_id=1, source_target_pairs={{0,8},{2,10},{4,12},{6,14},{8,0},{10,2},{12,4},{14,6},{16,24},{18,... | collective-permute-start | bytes 516104 | tf_op jit(solution)/shard_map/ppermute | solution.py:64
  24.4 2.4 %collective-permute-start.11 = (bf16[224,384]{1,0:T(8,128)(2,1)S(1)}, bf16[224,384]{1,0:T(8,128)(2,1)S(1)}, u32[]{:S(2)}, u32[]{:S(2)}) collective-permute-start(bf16[224,384]{1,0:T(8,128)(2,1)S(1)} %get-tuple-element.92), channel_id=1, source_target_pairs={{0,12},{2,14},{4,8},{6,10},{8,4},{10,6},{12,0},{14,2},{16,28},{18,... | collective-permute-start | bytes 516104 | tf_op jit(solution)/shard_map/ppermute | solution.py:64
  26.8 0.5 collective-permute-start.9
  27.3 2.9 %shard_map.102 = (f32[1024,192]{1,0:T(8,128)S(1)}, bf16[224,128]{1,0:T(8,128)(2,1)S(1)}) custom-call(bf16[1152,384]{1,0:T(8,128)(2,1)S(1)} %get-tuple-element.93.tall, bf16[9,384,384]{2,1,0:T(8,128)(2,1)S(1)} %bitcast.13), custom_call_target="tpu_custom_call" | custom-call | flops 1358954496 | bytes 4382720 | tf_op jit(solution)/shard_map/pallas_call | solution.py:111
  30.2 0.6 collective-permute-start.12
  30.8 2.5 %collective-permute-start.14 = (bf16[224,128]{1,0:T(8,128)(2,1)S(1)}, bf16[224,128]{1,0:T(8,128)(2,1)S(1)}, u32[]{:S(2)}, u32[]{:S(2)}) collective-permute-start(bf16[224,128]{1,0:T(8,128)(2,1)S(1)} %get-tuple-element.113.refs_0_), channel_id=1, source_target_pairs={{0,24},{2,26},{4,28},{6,30},{8,16},{10,18},{12,20},{14,22},{16,8},... | collective-permute-start | bytes 172040 | tf_op jit(solution)/shard_map/ppermute | solution.py:60
  33.2 1.2 %shard_map.104.place_ref = bf16[128,1728]{1,0:T(8,128)(2,1)S(1)} custom-call(s32[16,16]{1,0:T(8,128)S(1)} %pad_add_fusion.tables_in.refs_2_), custom_call_target="tpu_custom_call" | custom-call | bytes 443392 | tf_op jit(solution)/shard_map/pallas_call | solution.py:111
  34.5 1.2 %shard_map.103 = (bf16[144,192]{1,0:T(8,128)(2,1)S(1)}, bf16[576,128]{1,0:T(8,128)(2,1)S(1)}, bf16[576,128]{1,0:T(8,128)(2,1)S(1)}, bf16[608,128]{1,0:T(8,128)(2,1)S(1)}) custom-call(bf16[1152,128]{1,0:T(8,128)(2,1)S(1)} %shard_map.97.refs_0_, bf16[1152,128]{1,0:T(8,128)(2,1)S(1)} %collective-permute-done.5.refs_1_, ...), custom_call_target="tpu_custom_call" | custom-call | bytes 1489920 | tf_op jit(solution)/shard_map/pallas_call | solution.py:111
  35.7 0.6 %collective-permute-done.9.refs_1_ = bf16[224,384]{1,0:T(8,128)(2,1)S(1)} collective-permute-done((bf16[224,384]{1,0:T(8,128)(2,1)S(1)}, bf16[224,384]{1,0:T(8,128)(2,1)S(1)}, u32[]{:S(2)}, u32[]{:S(2)}) %collective-permute-start.9) | collective-permute-done | bytes 172064 | tf_op jit(solution)/shard_map/ppermute | solution.py:64
  36.4 0.1 shard_map.105.held_ref
  36.5 1.0 %collective-permute-start.15 = (bf16[224,128]{1,0:T(8,128)(2,1)S(1)}, bf16[224,128]{1,0:T(8,128)(2,1)S(1)}, u32[]{:S(2)}, u32[]{:S(2)}) collective-permute-start(bf16[224,128]{1,0:T(8,128)(2,1)S(1)} %get-tuple-element.113.refs_0_), channel_id=1, source_target_pairs={{0,4},{2,6},{4,0},{6,2},{8,12},{10,14},{12,8},{14,10},{16,20},{18,... | collective-permute-start | bytes 172040 | tf_op jit(solution)/shard_map/ppermute | solution.py:64
  37.4 1.7 %collective-permute-start.13 = (bf16[224,384]{1,0:T(8,128)(2,1)S(1)}, bf16[224,384]{1,0:T(8,128)(2,1)S(1)}, u32[]{:S(2)}, u32[]{:S(2)}) collective-permute-start(bf16[224,384]{1,0:T(8,128)(2,1)S(1)} %shard_map.105.held_ref), channel_id=1, source_target_pairs={{0,16},{2,18},{4,20},{6,22},{8,24},{10,26},{12,28},{14,30},{16,0},... | collective-permute-start | bytes 516104 | tf_op jit(solution)/shard_map/ppermute | solution.py:64
  39.1 1.5 %collective-permute-start.24 = (bf16[608,128]{1,0:T(8,128)(2,1)S(1)}, bf16[608,128]{1,0:T(8,128)(2,1)S(1)}, u32[]{:S(2)}, u32[]{:S(2)}) collective-permute-start(bf16[608,128]{1,0:T(8,128)(2,1)S(1)} %get-tuple-element.123), channel_id=1, source_target_pairs={{0,1},{1,0},{2,3},{3,2},{4,5},{5,4},{6,7},{7,6},{8,9},{9,8},{10,11... | collective-permute-start | bytes 466952 | tf_op jit(solution)/shard_map/ppermute | solution.py:720
  40.6 0.5 collective-permute-start.22
  41.1 1.5 %collective-permute-start.23 = (bf16[576,128]{1,0:T(8,128)(2,1)S(1)}, bf16[576,128]{1,0:T(8,128)(2,1)S(1)}, u32[]{:S(2)}, u32[]{:S(2)}) collective-permute-start(bf16[576,128]{1,0:T(8,128)(2,1)S(1)} %get-tuple-element.122), channel_id=1, source_target_pairs={{0,1},{1,0},{2,3},{3,2},{4,5},{5,4},{6,7},{7,6},{8,9},{9,8},{10,11... | collective-permute-start | bytes 442376 | tf_op jit(solution)/shard_map/ppermute | solution.py:720
  42.7 1.1 %collective-permute-start.16 = (bf16[448,128]{1,0:T(8,128)(2,1)S(1)}, bf16[448,128]{1,0:T(8,128)(2,1)S(1)}, u32[]{:S(2)}, u32[]{:S(2)}) collective-permute-start(bf16[448,128]{1,0:T(8,128)(2,1)S(1)} %shard_map.106.refs_1_), channel_id=1, source_target_pairs={{0,4},{2,6},{4,0},{6,2},{8,12},{10,14},{12,8},{14,10},{16,20},{18,... | collective-permute-start | bytes 344072 | tf_op jit(solution)/shard_map/ppermute | solution.py:64
  43.8 3.8 %collective-permute-done.16.refs_1_ = bf16[448,128]{1,0:T(8,128)(2,1)S(1)} collective-permute-done((bf16[448,128]{1,0:T(8,128)(2,1)S(1)}, bf16[448,128]{1,0:T(8,128)(2,1)S(1)}, u32[]{:S(2)}, u32[]{:S(2)}) %collective-permute-start.16) | collective-permute-done | bytes 114720 | tf_op jit(solution)/shard_map/ppermute | solution.py:64
  47.6 1.1 %collective-permute-start.17 = (bf16[224,384]{1,0:T(8,128)(2,1)S(1)}, bf16[224,384]{1,0:T(8,128)(2,1)S(1)}, u32[]{:S(2)}, u32[]{:S(2)}) collective-permute-start(bf16[224,384]{1,0:T(8,128)(2,1)S(1)} %shard_map.109.refs_0_), channel_id=1, source_target_pairs={{0,4},{2,6},{4,0},{6,2},{8,12},{10,14},{12,8},{14,10},{16,20},{18,... | collective-permute-start | bytes 516104 | tf_op jit(solution)/shard_map/ppermute | solution.py:64
  48.7 2.7 %collective-permute-start.18 = (bf16[224,384]{1,0:T(8,128)(2,1)S(1)}, bf16[224,384]{1,0:T(8,128)(2,1)S(1)}, u32[]{:S(2)}, u32[]{:S(2)}) collective-permute-start(bf16[224,384]{1,0:T(8,128)(2,1)S(1)} %shard_map.109.refs_0_), channel_id=1, source_target_pairs={{0,8},{2,10},{4,12},{6,14},{8,0},{10,2},{12,4},{14,6},{16,24},{18,... | collective-permute-start | bytes 516104 | tf_op jit(solution)/shard_map/ppermute | solution.py:64
  51.5 0.5 collective-permute-start.21
  52.0 3.9 %shard_map.111 = bf16[1024,192]{1,0:T(8,128)(2,1)} custom-call(bf16[32,32,192]{2,1,0:T(8,128)(2,1)S(1)} %get-tuple-element.73.field_ref.refs_3_, bf16[144,192]{1,0:T(8,128)(2,1)S(1)} %get-tuple-element.120.halos_ref, bf16[9,384,384]{2,1,0:T(8,128)(2,1)S(1)} %bitcast.14, bf16[576,128]{1,0:T(8,128)(2,1)S(1)} %collective-permute-done.22.refs_0_, ...), custom_call_target="tpu_custom_call" | custom-call | flops 2717908992 | bytes 3946496 | tf_op jit(solution)/shard_map/pallas_call | solution.py:111
  55.8 0.1 collective-permute-start.25
  55.9 1.3 %shard_map.110 = bf16[1024,192]{1,0:T(8,128)(2,1)} custom-call(bf16[128,1728]{1,0:T(8,128)(2,1)S(1)} %shard_map.104.place_ref, f32[1024,192]{1,0:T(8,128)S(1)} %get-tuple-element.117.inner_ref, bf16[672,128]{1,0:T(8,128)(2,1)S(1)} %shard_map.107.refs_0_, bf16[672,128]{1,0:T(8,128)(2,1)S(1)} %shard_map.108.refs_1_, ...), custom_call_target="tpu_custom_call" | custom-call | bytes 2310144 | tf_op jit(solution)/shard_map/pallas_call | solution.py:111
  57.2 0.4 collective-permute-done.19.refs_3_
  57.7 0.5 collective-permute-start.27
  58.2 1.4 %shard_map.112.refs_0_ = f32[1728,384]{1,0:T(8,128)} custom-call(bf16[224,384]{1,0:T(8,128)(2,1)S(1)} %shard_map.109.refs_0_, bf16[224,384]{1,0:T(8,128)(2,1)S(1)} %collective-permute-done.17.refs_1_, bf16[224,384]{1,0:T(8,128)(2,1)S(1)} %collective-permute-done.18.refs_2_, bf16[224,384]{1,0:T(8,128)(2,1)S(1)} %collective-permute-done.19.refs_3_, ...), custom_call_target="tpu_custom_call" | custom-call | tf_op jit(solution)/shard_map/pallas_call | solution.py:463
  59.6 1.1 %shard_map.113 = f32[1728,384]{1,0:T(8,128)} custom-call(f32[1728,384]{1,0:T(8,128)} %shard_map.112.refs_0_, bf16[224,384]{1,0:T(8,128)(2,1)S(1)} %collective-permute-done.26.refs_1_, bf16[224,384]{1,0:T(8,128)(2,1)S(1)} %collective-permute-done.27.refs_2_, bf16[224,384]{1,0:T(8,128)(2,1)S(1)} %collective-permute-done.28.refs_3_), custom_call_target="tpu_custom_call", output_to_operand_aliasing={{}: (0, {})} | custom-call | tf_op jit(solution)/shard_map/pallas_call | solution.py:463
  (37 shorter events, 0.3 us)
Async XLA Ops:
  0.6 16.4 %collective-permute-start.4 = (bf16[1024,192]{1,0:T(8,128)(2,1)}, bf16[1024,192]{1,0:T(8,128)(2,1)S(1)}, u32[]{:S(2)}, u32[]{:S(2)}) collective-permute-start(bf16[1024,192]{1,0:T(8,128)(2,1)} %bitcast.11), channel_id=1, source_target_pairs={{0,1},{1,0},{2,3},{3,2},{4,5},{5,4},{6,7},{7,6},{8,9},{9,8},{10,11... | collective-permute-start | bytes 1179656 | tf_op jit(solution)/shard_map/ppermute | solution.py:621
  3.6 1.0 %copy-start = (bf16[1,32,32,192]{3,2,1,0:T(8,128)(2,1)S(1)}, bf16[1,32,32,192]{3,2,1,0:T(8,128)(2,1)}, u32[]{:S(2)}) copy-start(bf16[1,32,32,192]{3,2,1,0:T(8,128)(2,1)} %param.7) | copy-start | bytes 1179652
  4.8 5.6 %collective-permute-start.1 = (bf16[192,128]{1,0:T(8,128)(2,1)S(1)}, bf16[192,128]{1,0:T(8,128)(2,1)S(1)}, u32[]{:S(2)}, u32[]{:S(2)}) collective-permute-start(bf16[192,128]{1,0:T(8,128)(2,1)S(1)} %get-tuple-element.68.refs_0_), channel_id=1, source_target_pairs={{0,8},{2,10},{4,12},{6,14},{8,0},{10,2},{12,4},{14,6},{16,24},{18,... | collective-permute-start | bytes 147464 | tf_op jit(solution)/shard_map/ppermute | solution.py:60
  6.4 5.9 %collective-permute-start.2 = (bf16[192,128]{1,0:T(8,128)(2,1)S(1)}, bf16[192,128]{1,0:T(8,128)(2,1)S(1)}, u32[]{:S(2)}, u32[]{:S(2)}) collective-permute-start(bf16[192,128]{1,0:T(8,128)(2,1)S(1)} %get-tuple-element.68.refs_0_), channel_id=1, source_target_pairs={{0,24},{2,26},{4,28},{6,30},{8,16},{10,18},{12,20},{14,22},{16,8},... | collective-permute-start | bytes 147464 | tf_op jit(solution)/shard_map/ppermute | solution.py:60
  8.9 7.9 %collective-permute-start = (bf16[192,128]{1,0:T(8,128)(2,1)S(1)}, bf16[192,128]{1,0:T(8,128)(2,1)S(1)}, u32[]{:S(2)}, u32[]{:S(2)}) collective-permute-start(bf16[192,128]{1,0:T(8,128)(2,1)S(1)} %get-tuple-element.68.refs_0_), channel_id=1, source_target_pairs={{0,4},{2,6},{4,0},{6,2},{8,12},{10,14},{12,8},{14,10},{16,20},{18,... | collective-permute-start | bytes 147464 | tf_op jit(solution)/shard_map/ppermute | solution.py:64
  12.3 4.7 %collective-permute-start.3 = (bf16[384,128]{1,0:T(8,128)(2,1)S(1)}, bf16[384,128]{1,0:T(8,128)(2,1)S(1)}, u32[]{:S(2)}, u32[]{:S(2)}) collective-permute-start(bf16[384,128]{1,0:T(8,128)(2,1)S(1)} %shard_map.95), channel_id=1, source_target_pairs={{0,4},{2,6},{4,0},{6,2},{8,12},{10,14},{12,8},{14,10},{16,20},{18,... | collective-permute-start | bytes 294920 | tf_op jit(solution)/shard_map/ppermute | solution.py:64
  14.7 1.0 %copy-start.1 = (bf16[1,32,32,192]{3,2,1,0:T(8,128)(2,1)S(1)}, bf16[1,32,32,192]{3,2,1,0:T(8,128)(2,1)}, u32[]{:S(2)}) copy-start(bf16[1,32,32,192]{3,2,1,0:T(8,128)(2,1)} %param.9) | copy-start | bytes 1179652
  18.6 3.7 %collective-permute-start.7 = (f32[576,384]{1,0:T(8,128)S(1)}, f32[576,384]{1,0:T(8,128)S(1)}, u32[]{:S(2)}, u32[]{:S(2)}) collective-permute-start(f32[576,384]{1,0:T(8,128)S(1)} %get-tuple-element.84), channel_id=1, source_target_pairs={{0,2},{2,0},{4,6},{6,4},{8,10},{10,8},{12,14},{14,12},{16,18},{18,... | collective-permute-start | bytes 2654216 | tf_op jit(solution)/shard_map/ppermute | solution.py:64
  19.3 3.0 %collective-permute-start.8 = (f32[288,384]{1,0:T(8,128)S(1)}, f32[288,384]{1,0:T(8,128)S(1)}, u32[]{:S(2)}, u32[]{:S(2)}) collective-permute-start(f32[288,384]{1,0:T(8,128)S(1)} %shard_map.99), channel_id=1, source_target_pairs={{0,2},{2,0},{4,6},{6,4},{8,10},{10,8},{12,14},{14,12},{16,18},{18,... | collective-permute-start | bytes 1327112 | tf_op jit(solution)/shard_map/ppermute | solution.py:64
  19.8 2.4 %collective-permute-start.5 = (bf16[1152,128]{1,0:T(8,128)(2,1)S(1)}, bf16[1152,128]{1,0:T(8,128)(2,1)S(1)}, u32[]{:S(2)}, u32[]{:S(2)}) collective-permute-start(bf16[1152,128]{1,0:T(8,128)(2,1)S(1)} %shard_map.97.refs_0_), channel_id=1, source_target_pairs={{0,2},{2,0},{4,6},{6,4},{8,10},{10,8},{12,14},{14,12},{16,18},{18,... | collective-permute-start | bytes 884744 | tf_op jit(solution)/shard_map/ppermute | solution.py:64
  19.9 2.3 %collective-permute-start.6 = (bf16[128,384]{1,0:T(8,128)(2,1)S(1)}, bf16[128,384]{1,0:T(8,128)(2,1)S(1)}, u32[]{:S(2)}, u32[]{:S(2)}) collective-permute-start(bf16[128,384]{1,0:T(8,128)(2,1)S(1)} %get-tuple-element.79.refs_4_), channel_id=1, source_target_pairs={{0,2},{2,0},{4,6},{6,4},{8,10},{10,8},{12,14},{14,12},{16,18},{18,... | collective-permute-start | bytes 294920 | tf_op jit(solution)/shard_map/ppermute | solution.py:64
  21.7 5.7 %copy-start.2 = (bf16[3,3,384,384]{3,2,1,0:T(8,128)(2,1)S(1)}, bf16[3,3,384,384]{3,2,1,0:T(8,128)(2,1)}, u32[]{:S(2)}) copy-start(bf16[3,3,384,384]{3,2,1,0:T(8,128)(2,1)} %param.8) | copy-start | bytes 7962628
  23.8 12.0 %collective-permute-start.10 = (bf16[224,384]{1,0:T(8,128)(2,1)S(1)}, bf16[224,384]{1,0:T(8,128)(2,1)S(1)}, u32[]{:S(2)}, u32[]{:S(2)}) collective-permute-start(bf16[224,384]{1,0:T(8,128)(2,1)S(1)} %get-tuple-element.91), channel_id=1, source_target_pairs={{0,8},{2,10},{4,12},{6,14},{8,0},{10,2},{12,4},{14,6},{16,24},{18,... | collective-permute-start | bytes 516104 | tf_op jit(solution)/shard_map/ppermute | solution.py:64
  24.4 11.3 %collective-permute-start.11 = (bf16[224,384]{1,0:T(8,128)(2,1)S(1)}, bf16[224,384]{1,0:T(8,128)(2,1)S(1)}, u32[]{:S(2)}, u32[]{:S(2)}) collective-permute-start(bf16[224,384]{1,0:T(8,128)(2,1)S(1)} %get-tuple-element.92), channel_id=1, source_target_pairs={{0,12},{2,14},{4,8},{6,10},{8,4},{10,6},{12,0},{14,2},{16,28},{18,... | collective-permute-start | bytes 516104 | tf_op jit(solution)/shard_map/ppermute | solution.py:64
  26.8 9.6 %collective-permute-start.9 = (bf16[224,384]{1,0:T(8,128)(2,1)S(1)}, bf16[224,384]{1,0:T(8,128)(2,1)S(1)}, u32[]{:S(2)}, u32[]{:S(2)}) collective-permute-start(bf16[224,384]{1,0:T(8,128)(2,1)S(1)} %get-tuple-element.90), channel_id=1, source_target_pairs={{0,4},{2,6},{4,0},{6,2},{8,12},{10,14},{12,8},{14,10},{16,20},{18,... | collective-permute-start | bytes 516104 | tf_op jit(solution)/shard_map/ppermute | solution.py:64
  30.2 5.5 %collective-permute-start.12 = (bf16[224,128]{1,0:T(8,128)(2,1)S(1)}, bf16[224,128]{1,0:T(8,128)(2,1)S(1)}, u32[]{:S(2)}, u32[]{:S(2)}) collective-permute-start(bf16[224,128]{1,0:T(8,128)(2,1)S(1)} %get-tuple-element.113.refs_0_), channel_id=1, source_target_pairs={{0,8},{2,10},{4,12},{6,14},{8,0},{10,2},{12,4},{14,6},{16,24},{18,... | collective-permute-start | bytes 172040 | tf_op jit(solution)/shard_map/ppermute | solution.py:60
  30.8 10.4 %collective-permute-start.14 = (bf16[224,128]{1,0:T(8,128)(2,1)S(1)}, bf16[224,128]{1,0:T(8,128)(2,1)S(1)}, u32[]{:S(2)}, u32[]{:S(2)}) collective-permute-start(bf16[224,128]{1,0:T(8,128)(2,1)S(1)} %get-tuple-element.113.refs_0_), channel_id=1, source_target_pairs={{0,24},{2,26},{4,28},{6,30},{8,16},{10,18},{12,20},{14,22},{16,8},... | collective-permute-start | bytes 172040 | tf_op jit(solution)/shard_map/ppermute | solution.py:60
  36.5 6.2 %collective-permute-start.15 = (bf16[224,128]{1,0:T(8,128)(2,1)S(1)}, bf16[224,128]{1,0:T(8,128)(2,1)S(1)}, u32[]{:S(2)}, u32[]{:S(2)}) collective-permute-start(bf16[224,128]{1,0:T(8,128)(2,1)S(1)} %get-tuple-element.113.refs_0_), channel_id=1, source_target_pairs={{0,4},{2,6},{4,0},{6,2},{8,12},{10,14},{12,8},{14,10},{16,20},{18,... | collective-permute-start | bytes 172040 | tf_op jit(solution)/shard_map/ppermute | solution.py:64
  37.4 10.1 %collective-permute-start.13 = (bf16[224,384]{1,0:T(8,128)(2,1)S(1)}, bf16[224,384]{1,0:T(8,128)(2,1)S(1)}, u32[]{:S(2)}, u32[]{:S(2)}) collective-permute-start(bf16[224,384]{1,0:T(8,128)(2,1)S(1)} %shard_map.105.held_ref), channel_id=1, source_target_pairs={{0,16},{2,18},{4,20},{6,22},{8,24},{10,26},{12,28},{14,30},{16,0},... | collective-permute-start | bytes 516104 | tf_op jit(solution)/shard_map/ppermute | solution.py:64
  39.1 12.3 %collective-permute-start.24 = (bf16[608,128]{1,0:T(8,128)(2,1)S(1)}, bf16[608,128]{1,0:T(8,128)(2,1)S(1)}, u32[]{:S(2)}, u32[]{:S(2)}) collective-permute-start(bf16[608,128]{1,0:T(8,128)(2,1)S(1)} %get-tuple-element.123), channel_id=1, source_target_pairs={{0,1},{1,0},{2,3},{3,2},{4,5},{5,4},{6,7},{7,6},{8,9},{9,8},{10,11... | collective-permute-start | bytes 466952 | tf_op jit(solution)/shard_map/ppermute | solution.py:720
  40.6 10.8 %collective-permute-start.22 = (bf16[576,128]{1,0:T(8,128)(2,1)S(1)}, bf16[576,128]{1,0:T(8,128)(2,1)S(1)}, u32[]{:S(2)}, u32[]{:S(2)}) collective-permute-start(bf16[576,128]{1,0:T(8,128)(2,1)S(1)} %get-tuple-element.121), channel_id=1, source_target_pairs={{0,1},{1,0},{2,3},{3,2},{4,5},{5,4},{6,7},{7,6},{8,9},{9,8},{10,11... | collective-permute-start | bytes 442376 | tf_op jit(solution)/shard_map/ppermute | solution.py:720
  41.1 10.2 %collective-permute-start.23 = (bf16[576,128]{1,0:T(8,128)(2,1)S(1)}, bf16[576,128]{1,0:T(8,128)(2,1)S(1)}, u32[]{:S(2)}, u32[]{:S(2)}) collective-permute-start(bf16[576,128]{1,0:T(8,128)(2,1)S(1)} %get-tuple-element.122), channel_id=1, source_target_pairs={{0,1},{1,0},{2,3},{3,2},{4,5},{5,4},{6,7},{7,6},{8,9},{9,8},{10,11... | collective-permute-start | bytes 442376 | tf_op jit(solution)/shard_map/ppermute | solution.py:720
  42.7 4.9 %collective-permute-start.16 = (bf16[448,128]{1,0:T(8,128)(2,1)S(1)}, bf16[448,128]{1,0:T(8,128)(2,1)S(1)}, u32[]{:S(2)}, u32[]{:S(2)}) collective-permute-start(bf16[448,128]{1,0:T(8,128)(2,1)S(1)} %shard_map.106.refs_1_), channel_id=1, source_target_pairs={{0,4},{2,6},{4,0},{6,2},{8,12},{10,14},{12,8},{14,10},{16,20},{18,... | collective-permute-start | bytes 344072 | tf_op jit(solution)/shard_map/ppermute | solution.py:64
  47.6 9.6 %collective-permute-start.17 = (bf16[224,384]{1,0:T(8,128)(2,1)S(1)}, bf16[224,384]{1,0:T(8,128)(2,1)S(1)}, u32[]{:S(2)}, u32[]{:S(2)}) collective-permute-start(bf16[224,384]{1,0:T(8,128)(2,1)S(1)} %shard_map.109.refs_0_), channel_id=1, source_target_pairs={{0,4},{2,6},{4,0},{6,2},{8,12},{10,14},{12,8},{14,10},{16,20},{18,... | collective-permute-start | bytes 516104 | tf_op jit(solution)/shard_map/ppermute | solution.py:64
  48.7 8.6 %collective-permute-start.18 = (bf16[224,384]{1,0:T(8,128)(2,1)S(1)}, bf16[224,384]{1,0:T(8,128)(2,1)S(1)}, u32[]{:S(2)}, u32[]{:S(2)}) collective-permute-start(bf16[224,384]{1,0:T(8,128)(2,1)S(1)} %shard_map.109.refs_0_), channel_id=1, source_target_pairs={{0,8},{2,10},{4,12},{6,14},{8,0},{10,2},{12,4},{14,6},{16,24},{18,... | collective-permute-start | bytes 516104 | tf_op jit(solution)/shard_map/ppermute | solution.py:64
  51.4 6.3 %collective-permute-start.19 = (bf16[224,384]{1,0:T(8,128)(2,1)S(1)}, bf16[224,384]{1,0:T(8,128)(2,1)S(1)}, u32[]{:S(2)}, u32[]{:S(2)}) collective-permute-start(bf16[224,384]{1,0:T(8,128)(2,1)S(1)} %shard_map.109.refs_0_), channel_id=1, source_target_pairs={{0,12},{2,14},{4,8},{6,10},{8,4},{10,6},{12,0},{14,2},{16,28},{18,... | collective-permute-start | bytes 516104 | tf_op jit(solution)/shard_map/ppermute | solution.py:64
  51.4 4.5 %collective-permute-start.20 = (bf16[672,128]{1,0:T(8,128)(2,1)S(1)}, bf16[672,128]{1,0:T(8,128)(2,1)S(1)}, u32[]{:S(2)}, u32[]{:S(2)}) collective-permute-start(bf16[672,128]{1,0:T(8,128)(2,1)S(1)} %shard_map.107.refs_0_), channel_id=1, source_target_pairs={{0,2},{2,0},{4,6},{6,4},{8,10},{10,8},{12,14},{14,12},{16,18},{18,... | collective-permute-start | bytes 516104 | tf_op jit(solution)/shard_map/ppermute | solution.py:64
  51.5 4.5 %collective-permute-start.21 = (bf16[672,128]{1,0:T(8,128)(2,1)S(1)}, bf16[672,128]{1,0:T(8,128)(2,1)S(1)}, u32[]{:S(2)}, u32[]{:S(2)}) collective-permute-start(bf16[672,128]{1,0:T(8,128)(2,1)S(1)} %shard_map.108.refs_1_), channel_id=1, source_target_pairs={{0,2},{2,0},{4,6},{6,4},{8,10},{10,8},{12,14},{14,12},{16,18},{18,... | collective-permute-start | bytes 516104 | tf_op jit(solution)/shard_map/ppermute | solution.py:64
  55.8 2.4 %collective-permute-start.25 = (bf16[224,384]{1,0:T(8,128)(2,1)S(1)}, bf16[224,384]{1,0:T(8,128)(2,1)S(1)}, u32[]{:S(2)}, u32[]{:S(2)}) collective-permute-start(bf16[224,384]{1,0:T(8,128)(2,1)S(1)} %shard_map.109.refs_0_), channel_id=1, source_target_pairs={{0,2},{2,0},{4,6},{6,4},{8,10},{10,8},{12,14},{14,12},{16,18},{18,... | collective-permute-start | bytes 516104 | tf_op jit(solution)/shard_map/ppermute | solution.py:64
  57.7 1.9 %collective-permute-start.26 = (bf16[224,384]{1,0:T(8,128)(2,1)S(1)}, bf16[224,384]{1,0:T(8,128)(2,1)S(1)}, u32[]{:S(2)}, u32[]{:S(2)}) collective-permute-start(bf16[224,384]{1,0:T(8,128)(2,1)S(1)} %collective-permute-done.17.refs_1_), channel_id=1, source_target_pairs={{0,2},{2,0},{4,6},{6,4},{8,10},{10,8},{12,14},{14,12},{16,18},{18,... | collective-permute-start | bytes 516104 | tf_op jit(solution)/shard_map/ppermute | solution.py:64
  57.7 1.9 %collective-permute-start.27 = (bf16[224,384]{1,0:T(8,128)(2,1)S(1)}, bf16[224,384]{1,0:T(8,128)(2,1)S(1)}, u32[]{:S(2)}, u32[]{:S(2)}) collective-permute-start(bf16[224,384]{1,0:T(8,128)(2,1)S(1)} %collective-permute-done.18.refs_2_), channel_id=1, source_target_pairs={{0,2},{2,0},{4,6},{6,4},{8,10},{10,8},{12,14},{14,12},{16,18},{18,... | collective-permute-start | bytes 516104 | tf_op jit(solution)/shard_map/ppermute | solution.py:64
  58.2 1.4 %collective-permute-start.28 = (bf16[224,384]{1,0:T(8,128)(2,1)S(1)}, bf16[224,384]{1,0:T(8,128)(2,1)S(1)}, u32[]{:S(2)}, u32[]{:S(2)}) collective-permute-start(bf16[224,384]{1,0:T(8,128)(2,1)S(1)} %collective-permute-done.19.refs_3_), channel_id=1, source_target_pairs={{0,2},{2,0},{4,6},{6,4},{8,10},{10,8},{12,14},{14,12},{16,18},{18,... | collective-permute-start | bytes 516104 | tf_op jit(solution)/shard_map/ppermute | solution.py:64
